TPU v7x, 32 devices: a whole 2x2x4 slice. The times are simulated.
32 devices in a mesh: grp: 4 (over y, x), dom: 8 (over z, core).
Axes of the slice: x: 2, y: 2, z: 4, core: 2. Of those that a mesh axis runs over, the one named last changes fastest.
Arguments:
- features: bfloat16 [16384, 1024], P(('grp', 'dom')), may hold values from -6 to 6
- node_order: int32 [16384], P(('grp', 'dom')), may hold values from 0 to 16383, as said below
- block_cols: int32 [128, 16], P(('grp', 'dom')), may hold values from 0 to 31
- block_count: int32 [128], P(('grp', 'dom')), may hold values from 1 to 16, as said below
- block_vals: bfloat16 [128, 16, 128, 128], P(('grp', 'dom')), may hold values from -0.1875 to 0.1875
- weight: bfloat16 [1024, 512], replicated, may hold values from -0.1875 to 0.1875
- cotangent: bfloat16 [16384, 512], P(('grp', 'dom')), may hold values from -12 to 12
Outputs:
- hidden: bfloat16 [16384, 512], P(('grp', 'dom'))
- grad_weight: float32 [1024, 512], replicated
Inputs may be any that keep to these rules, and one draw needn't show every extreme that they name: `node_order`: A permutation of the crawl rows; the positions of one device's block of 512 take exactly 16 crawl rows from each device's block of 512 crawl rows. `block_count`: some row of blocks holds exactly 16 live blocks.
All inputs are finite; a program needn't handle non-finite values.
Results may differ from a plain program's by a relative error of at most 0.014.
Values may be sent and summed in bfloat16 or wider, within the bound.
No kernel may reach another device: no remote copies, remote signals or barrier semaphores. Data moves between devices by JAX's collectives and lax.ppermute only.
A program may use at most 128 MiB of HBM per device.

v0:
```python
import jax
import jax.numpy as jnp
from jax import lax
from jax.sharding import PartitionSpec as P


def silu_slope(values):
    sig = jax.nn.sigmoid(values)
    return sig * (1.0 + values * (1.0 - sig))


def shards(features, node_order, block_cols, block_count, block_vals, weight, cotangent):
    row_count = features.shape[0]
    width_in = features.shape[1]
    hidden_units = weight.shape[1]
    tiles_dev = block_vals.shape[0]
    blocks = block_vals.shape[1]
    tile_size = block_vals.shape[-1]
    devices = lax.axis_size("grp") * lax.axis_size("dom")
    per_pair = row_count // devices
    source_device = node_order // row_count
    source_row = node_order % row_count
    ordering = jnp.argsort(source_device, stable=True)
    requests = source_row[ordering].reshape(devices, per_pair)
    asked_rows = lax.all_to_all(requests, ("grp", "dom"), split_axis=0, concat_axis=0, tiled=True)
    outgoing = features[asked_rows.reshape(-1)].reshape(devices, per_pair, width_in)
    arrived = lax.all_to_all(outgoing, ("grp", "dom"), split_axis=0, concat_axis=0, tiled=True)
    arrived = arrived.reshape(row_count, width_in)
    inverse = jnp.argsort(ordering)
    ordered = arrived[inverse]
    gathered = jnp.dot(
        lax.all_gather(ordered, "dom", axis=0, tiled=True),
        weight,
        preferred_element_type=jnp.float32,
    ).astype(jnp.bfloat16)
    panel_tiles = gathered.reshape(-1, tile_size, hidden_units)
    live_mask = lax.broadcasted_iota(jnp.int32, (tiles_dev, blocks), 1) < block_count[:, None]
    masked_vals = jnp.where(live_mask[:, :, None, None], block_vals, jnp.zeros((), jnp.bfloat16))
    selected = panel_tiles[block_cols]
    aggregate = jnp.einsum(
        "tkij,tkjh->tih", masked_vals, selected, preferred_element_type=jnp.float32
    )
    hidden = jax.nn.silu(aggregate).astype(jnp.bfloat16)
    cot_tiles = cotangent.reshape(tiles_dev, tile_size, hidden_units).astype(jnp.float32)
    grad_agg = (cot_tiles * silu_slope(aggregate)).astype(jnp.bfloat16)
    contrib = jnp.einsum(
        "tkij,tih->tkjh", masked_vals, grad_agg, preferred_element_type=jnp.float32
    )
    partial_value = jnp.zeros((panel_tiles.shape[0], tile_size, hidden_units), jnp.float32)
    partial_value = partial_value.at[block_cols.reshape(-1)].add(
        contrib.reshape(-1, tile_size, hidden_units)
    )
    partial_value = partial_value.reshape(-1, hidden_units).astype(jnp.bfloat16)
    grad_rows = lax.psum_scatter(
        partial_value.astype(jnp.float32).astype(jnp.bfloat16),
        "dom",
        scatter_dimension=0,
        tiled=True,
    ).astype(jnp.float32)
    local_grad = jnp.dot(ordered.astype(jnp.float32).T, grad_rows, precision=lax.Precision.HIGHEST)
    grad_weight = lax.psum(local_grad, ("grp", "dom"))
    return (hidden.reshape(row_count, hidden_units), grad_weight)


def solution(mesh):
    placed = (
        P(("grp", "dom"), None),
        P(("grp", "dom")),
        P(("grp", "dom"), None),
        P(("grp", "dom")),
        P(("grp", "dom"), None, None, None),
        P(),
        P(("grp", "dom"), None),
    )
    return jax.shard_map(
        shards,
        mesh=mesh,
        in_specs=placed,
        out_specs=(P(("grp", "dom"), None), P()),
        check_vma=False,
    )
```

profile of v0, /device:TPU:0, one launch (start us, length us, event | category | flops | bytes accessed | tf_op | source)
XLA Modules:
  0.0 423.2 jit_solution(17844784017499621041)
XLA Ops:
  7.2 0.0 copy-start
  7.2 0.8 add_select_fusion
  8.0 3.8 sort.34
  11.7 3.5 gather_fusion
  15.2 0.1 all_to_all.9
  15.3 14.2 %all_to_all.14 = s32[32,1,16]{2,1,0:T(1,128)S(1)} all-to-all(s32[32,1,16]{2,1,0:T(1,128)S(1)} %bitcast.32), channel_id=1, replica_groups=mesh['grp'=4,'dom'=8] {'grp','dom'}, dimensions={0} | all-to-all | bytes 4096 | tf_op jit(solution)/shard_map/all_to_all | solution.py:25
  29.6 0.5 broadcast.90
  30.1 0.7 reduce.3
  30.8 0.1 reshape.110
  30.9 4.8 %gather_fusion.1 = bf16[512,1024]{1,0:T(8,128)(2,1)} fusion(bf16[512,1024]{1,0:T(8,128)(2,1)} %param.7, s32[1024]{0:T(1024)S(1)} %pad_clamp_fusion.2), kind=kCustom, calls=%fused_computation.1 | custom fusion | bytes 2099200 | tf_op jit(solution)/shard_map/gather | solution.py:26
  35.7 0.0 copy-start.4
  35.7 0.0 copy-start.5
  35.7 2.8 all-to-all-start.1
  38.5 0.0 all-gather.3.cloned.1.call-start
  38.5 3.8 sort.35
  42.3 23.7 %all-to-all-done.1 = bf16[32,16,1024]{2,1,0:T(8,128)(2,1)S(1)} async-done(((bf16[32,16,1024]{2,1,0:T(8,128)(2,1)}), bf16[32,16,1024]{2,1,0:T(8,128)(2,1)S(1)}, u32[]{:S(2)}, u32[]{:S(2)}) %all-to-all-start.1) | async-done | bytes 1048608 | tf_op jit(solution)/shard_map/all_to_all | solution.py:27
  66.1 2.8 gather_fusion.2
  68.8 0.0 all-gather.3.cloned.1.call-update
  68.9 0.2 reduce-scatter.2.cloned.1.call-start
  69.1 0.0 copy-done.4
  69.1 0.1 reshape.115
  69.2 0.1 reshape.144
  69.3 0.0 copy-done.5
  69.3 0.1 iota_compare_fusion
  69.4 79.2 %all-gather.3.cloned.1.call-done = bf16[4096,1024]{1,0:T(8,128)(2,1)} async-done(((bf16[512,1024]{1,0:T(8,128)(2,1)}), bf16[4096,1024]{1,0:T(8,128)(2,1)}) %all-gather.3.cloned.1.call-update) | async-done | bytes 8388624 | tf_op jit(solution)/shard_map/all_gather | solution.py:32
  148.6 0.0 copy-done
  148.6 9.4 %convolution_convert_fusion = bf16[4096,512]{1,0:T(8,128)(2,1)} fusion(bf16[4096,1024]{1,0:T(8,128)(2,1)} %all-gather.3.cloned.1.call-done, bf16[1024,512]{1,0:T(8,128)(2,1)S(1)} %copy-done), kind=kOutput, calls=%fused_computation.5 | convolution fusion | flops 4297064448 | bytes 13631488 | tf_op jit(solution)/shard_map/dot_general | solution.py:31
  158.1 0.0 copy-start.2
  158.1 7.9 %gather_fusion.3 = bf16[64,128,512]{2,1,0:T(8,128)(2,1)} fusion(bf16[32,128,512]{2,1,0:T(8,128)(2,1)} %bitcast.29, s32[1024]{0:T(1024)S(1)} %pad_clamp_fusion), kind=kCustom, calls=%fused_computation.3 | custom fusion | bytes 16777472 | tf_op jit(solution)/shard_map/gather | solution.py:39
  165.9 0.0 copy-start.3
  165.9 0.0 copy-done.2
  165.9 5.7 %multiply_convert_fusion = (bf16[4,128,512]{2,1,0:T(8,128)(2,1)}, f32[4,128,512]{2,1,0:T(8,128)S(1)}) fusion(bf16[4,16,128,512]{3,2,1,0:T(8,128)(2,1)} %bitcast.30, bf16[4,16,128,128]{3,2,1,0:T(8,128)(2,1)S(1)} %copy-done.2, pred[4,16]{1,0:T(4,128)(4,1)S(1)} %iota_compare_fusion), kind=kOutput, calls=%fused_computation.12 | convolution fusion | flops 1076101120 | bytes 12058688 | tf_op jit(solution)/shard_map/tkij,tkjh->tih/dot_general | solution.py:40
  171.6 0.0 copy-done.3
  171.6 8.2 %fusion = f32[4,16,128,512]{3,2,1,0:T(8,128)} fusion(bf16[4,16,128,128]{3,2,1,0:T(8,128)(2,1)S(1)} %copy-done.2, pred[4,16]{1,0:T(4,128)(4,1)S(1)} %iota_compare_fusion, bf16[4,128,512]{2,1,0:T(8,128)(2,1)S(1)} %bitcast.31, f32[4,128,512]{2,1,0:T(8,128)S(1)} %get-tuple-element.9), kind=kOutput, calls=%fused_computation.7 | convolution fusion | flops 1077411840 | bytes 20447296 | tf_op jit(solution)/shard_map/tkij,tih->tkjh/dot_general | solution.py:46
  179.8 4.3 %broadcast_in_dim.33 = f32[32,128,512]{2,1,0:T(8,128)} broadcast(f32[]{:T(128)} %constant.42.clone.1), dimensions={} | broadcast | bytes 8388612 | tf_op jit(solution)/shard_map/broadcast_in_dim | solution.py:49
  184.1 36.8 %scatter_fusion = f32[32,128,512]{2,1,0:T(8,128)} fusion(f32[32,128,512]{2,1,0:T(8,128)} %broadcast_in_dim.33, s32[64]{0:T(128)S(1)} %fusion.9, f32[64,128,512]{2,1,0:T(8,128)} %bitcast.27), kind=kCustom, calls=%fused_computation.4 | custom fusion | flops 4194304 | bytes 50331904 | tf_op jit(solution)/shard_map/scatter-add | solution.py:50
  220.9 0.0 copy-start.1
  220.9 6.0 %convert_element_type.30 = bf16[32,128,512]{2,1,0:T(8,128)(2,1)} convert(f32[32,128,512]{2,1,0:T(8,128)} %scatter_fusion) | non-fusion elementwise | flops 2097152 | bytes 12582912 | tf_op jit(solution)/shard_map/convert_element_type | solution.py:53
  226.9 0.0 reduce-scatter.2.cloned.1.call-update
  227.0 0.0 all-reduce.2.cloned.1.call-start
  227.0 48.7 %reduce-scatter.2.cloned.1.call-done = bf16[512,512]{1,0:T(8,128)(2,1)} async-done(((bf16[4096,512]{1,0:T(8,128)(2,1)}), bf16[512,512]{1,0:T(8,128)(2,1)}) %reduce-scatter.2.cloned.1.call-update) | async-done | bytes 524304 | tf_op jit(solution)/shard_map/reduce_scatter | solution.py:54
  275.7 0.0 copy-done.1
  275.7 3.1 fusion.13
  278.9 0.0 all-reduce.2.cloned.1.call-update
  278.9 134.7 %all-reduce.2.cloned.1.call-done = f32[1024,512]{1,0:T(8,128)} async-done(((f32[1024,512]{1,0:T(8,128)}), f32[1024,512]{1,0:T(8,128)}) %all-reduce.2.cloned.1.call-update) | async-done | bytes 2097168 | tf_op jit(solution)/shard_map/psum | solution.py:61
  413.5 3.1 copy.18
  (11 shorter events, 0.1 us)
Async XLA Ops:
  7.2 141.4 %copy-start = (bf16[1024,512]{1,0:T(8,128)(2,1)S(1)}, bf16[1024,512]{1,0:T(8,128)(2,1)}, u32[]{:S(2)}) copy-start(bf16[1024,512]{1,0:T(8,128)(2,1)} %param.12) | copy-start | bytes 3145732
  35.7 33.4 %copy-start.4 = (s32[4,16]{1,0:T(4,128)S(1)}, s32[4,16]{1,0:T(4,128)}, u32[]{:S(2)}) copy-start(s32[4,16]{1,0:T(4,128)} %param.9) | copy-start | bytes 772
  35.7 33.6 %copy-start.5 = (s32[4]{0:T(128)S(1)}, s32[4]{0:T(128)}, u32[]{:S(2)}) copy-start(s32[4]{0:T(128)} %param.10) | copy-start | bytes 52
  35.7 30.4 %all-to-all-start.1 = ((bf16[32,16,1024]{2,1,0:T(8,128)(2,1)}), bf16[32,16,1024]{2,1,0:T(8,128)(2,1)S(1)}, u32[]{:S(2)}, u32[]{:S(2)}) async-start(bf16[32,16,1024]{2,1,0:T(8,128)(2,1)} %bitcast.2), calls=%async_computation.1 | async-start | bytes 2097152 | tf_op jit(solution)/shard_map/all_to_all | solution.py:27
  38.5 110.1 %all-gather.3.cloned.1.call-start = ((), (), s32[]{:S(2)}) async-start(), calls=%async_computation.5 | async-start | bytes 9437184 | tf_op jit(solution)/shard_map/all_gather | solution.py:32
  68.9 206.9 %reduce-scatter.2.cloned.1.call-start = ((), (), s32[]{:S(2)}) async-start(), calls=%async_computation.3 | async-start | bytes 4718592 | tf_op jit(solution)/shard_map/reduce_scatter | solution.py:54
  158.1 7.9 %copy-start.2 = (bf16[4,16,128,128]{3,2,1,0:T(8,128)(2,1)S(1)}, bf16[4,16,128,128]{3,2,1,0:T(8,128)(2,1)}, u32[]{:S(2)}) copy-start(bf16[4,16,128,128]{3,2,1,0:T(8,128)(2,1)} %param.11) | copy-start | bytes 6291460
  165.9 5.7 %copy-start.3 = (bf16[512,512]{1,0:T(8,128)(2,1)S(1)}, bf16[512,512]{1,0:T(8,128)(2,1)}, u32[]{:S(2)}) copy-start(bf16[512,512]{1,0:T(8,128)(2,1)} %param.13) | copy-start | bytes 1572868
  220.9 54.8 %copy-start.1 = (bf16[512,1024]{1,0:T(8,128)(2,1)S(1)}, bf16[512,1024]{1,0:T(8,128)(2,1)}, u32[]{:S(2)}) copy-start(bf16[512,1024]{1,0:T(8,128)(2,1)} %gather_fusion.2) | copy-start | bytes 3145732
  227.0 186.6 %all-reduce.2.cloned.1.call-start = ((), (), s32[]{:S(2)}) async-start(), calls=%async_computation.4 | async-start | bytes 4194304 | tf_op jit(solution)/shard_map/psum | solution.py:61
Sparse Core Ops, SparseCore 0:
  69.0 79.5 all-gather.2
  227.1 48.6 reduce-scatter.1
  281.7 131.8 all-reduce.1
where the time goes:
time: 424 us; the launch traced here: 423 us
  waiting for transfers between devices  286 us (67%)
  other arithmetic  51.9 us (12%)
  local copies, waits for them, and re-layouts  27.2 us (6%)
  matrix products  26.5 us (6%)
  blocking collectives  14.2 us (3%)
  between operations  13.8 us (3%)
    psum x1, waiting for transfers between devices, shards(): grad_weight = lax.psum(local_grad, ('grp', 'dom'))  135 us
    all_gather x1, waiting for transfers between devices, shards(): lax.all_gather(ordered, 'dom', axis=0, tiled=True)  79.2 us
    reduce_scatter x1, waiting for transfers between devices, shards(): lax.psum_scatter(partial_value.astype(jnp.float32).astype(jnp.bfloat16),...  48.7 us
    scatter-add x1, other arithmetic, shards(): partial_value.at[block_cols.reshape(-1)]  36.8 us
    all_to_all x1, waiting for transfers between devices, shards(): lax.all_to_all(outgoing, ('grp', 'dom'), split_axis=0, concat_axis=0, til...  23.7 us
    all_to_all x1, blocking collectives, shards(): lax.all_to_all(requests, ('grp', 'dom'), split_axis=0, concat_axis=0, til...  14.2 us
    dot_general x1, matrix products, shards(): jnp.dot(lax.all_gather(ordered, 'dom', axis=0, tiled=True), weight, prefe...  9.44 us
  transfers between devices with their start and end apart: 4, of which 4 were waited for; matrix products, arithmetic and copies ran while one was open for 1% of the time, Pallas kernels for 0%

commit v1 on v0

v1 whole, which is shorter than its diff:
```python
import jax
import jax.numpy as jnp
from jax import lax
from jax.experimental import pallas as pl
from jax.experimental.pallas import tpu as pltpu
from jax.sharding import Mesh, PartitionSpec as P

BF16 = jnp.bfloat16
F32 = jnp.float32
I32 = jnp.int32


def log2(n):
    assert n & (n - 1) == 0
    return n.bit_length() - 1


def iota(shape, dim):
    return lax.broadcasted_iota(I32, shape, dim)


def one_hot(mask):
    return jnp.where(mask, 1.0, 0.0).astype(BF16)


def dot(a, b):
    return jnp.dot(a, b, preferred_element_type=F32)


def dot_rows(a, b):
    return lax.dot_general(a, b, (((0,), (0,)), ((), ())), preferred_element_type=F32)


def call(body, outs, ins, name, mib, scratch=()):
    smem = pl.BlockSpec(memory_space=pltpu.SMEM)
    vmem = pl.BlockSpec(memory_space=pltpu.VMEM)
    return pl.pallas_call(
        body,
        out_shape=tuple(jax.ShapeDtypeStruct(s, d) for s, d in outs),
        in_specs=[smem if where == "s" else vmem for where, _ in ins],
        out_specs=tuple(vmem for _ in outs),
        scratch_shapes=list(scratch),
        compiler_params=pltpu.CompilerParams(vmem_limit_bytes=mib << 20),
        name=name,
    )(*(value for _, value in ins))


class Sizes:
    def __init__(self, rows, tiles):
        self.grp, self.zz = lax.axis_size("grp"), lax.axis_size("zz")
        self.dom = 2 * self.zz
        self.rows, self.tiles = rows, tiles
        self.pair = rows // (self.grp * self.dom)
        self.piece = self.grp * self.pair
        self.per_grp = self.dom * self.pair


def index_kernel(z, me_ref, order_ref, *outs):
    want_refs, slot_ref = outs[:-1], outs[-1]
    rows = z.rows
    shift = log2(rows)
    flip = me_ref[0] * z.dom
    order_r = order_ref[...]
    down, across = iota((rows, rows), 0), iota((rows, rows), 1)
    order_c = jnp.sum(
        jnp.where(down == across, order_r.astype(F32), 0.0), axis=1, keepdims=True
    ).astype(I32)
    source_r, source_c = order_r >> shift, order_c >> shift
    row_c = order_c & (rows - 1)
    same = jnp.where(source_c == source_r, 1.0, 0.0)
    rank_c = jnp.sum(jnp.where(across < down, same, 0.0), axis=1, keepdims=True).astype(I32)
    rank_r = jnp.sum(jnp.where(down < across, same, 0.0), axis=0, keepdims=True).astype(I32)
    owner = one_hot(iota((z.grp * z.dom, rows), 0) == (source_r ^ flip))
    at_rank = iota((rows, z.pair), 1) == rank_c
    high = jnp.where(at_rank, (row_c >> 4).astype(F32), 0.0).astype(BF16)
    low = jnp.where(at_rank, (row_c & 15).astype(F32), 0.0).astype(BF16)
    want = (dot(owner, high) * 16.0 + dot(owner, low)).astype(I32)
    for s in range(z.grp):
        want_refs[s][...] = want[s * z.dom:(s + 1) * z.dom, :]
    across_grp = (source_r >> log2(z.dom)) ^ me_ref[0]
    inner = source_r & (z.dom - 1)
    slot_ref[...] = (inner * z.grp + across_grp) * z.pair + rank_r


def product_kernel(z, me_ref, features_ref, weight_ref, own_ref, other_ref):
    half = own_ref.shape[1]
    for flip, out in ((0, own_ref), (1, other_ref)):
        at = pl.multiple_of((me_ref[2] ^ flip) * half, half)
        out[...] = dot(features_ref[...], weight_ref[:, pl.ds(at, half)]).astype(BF16)


def picks(z, at_zz, table, source):
    shape = (z.rows, table.shape[0])
    row = iota(shape, 0)
    s, n = row >> log2(z.per_grp), (row >> log2(z.pair)) & (z.dom - 1)
    held_at = ((at_zz - (n >> 1)) & (z.zz - 1)) * 2 + (n & 1)
    spread = one_hot(iota(shape, 1) == (held_at * z.grp + s) * z.dom + source)
    high = dot(spread, (table >> 4).astype(F32).astype(BF16))
    low = dot(spread, (table & 15).astype(F32).astype(BF16))
    mine = iota((z.rows, z.pair), 1) == (iota((z.rows, z.pair), 0) & (z.pair - 1))
    wanted = jnp.sum(jnp.where(mine, high * 16.0 + low, 0.0), axis=1, keepdims=True).astype(I32)
    return one_hot(iota((z.rows, z.rows), 1) == wanted)


def select_kernel(z, k, me_ref, table_ref, *refs):
    ins, outs = refs[:2 if k else 3], refs[2 if k else 3:]
    table = table_ref[...]
    at_zz = (me_ref[1] - k) & (z.zz - 1)
    for rel in range(2):
        pick = picks(z, me_ref[1], table, at_zz * 2 + (me_ref[2] ^ rel))
        got = dot(pick, ins[rel][...]).astype(BF16)
        for s in range(z.grp):
            outs[s][rel] = got[s * z.per_grp:(s + 1) * z.per_grp, :]
        if k == 0 and rel == 0:
            for s in range(z.grp):
                part = pick[s * z.per_grp:(s + 1) * z.per_grp, :]
                outs[z.grp + s][...] = dot(part, ins[2][...]).astype(BF16)


def layer_kernel(z, packed, me_ref, cols_ref, slot_ref, *refs):
    count = 1 if packed else z.zz * z.grp
    y_refs, refs = refs[:count], refs[count:]
    vals_a, vals_b, cot_a, cot_b, hidden_a, hidden_b = refs[:6]
    partial_refs, (panel, total) = refs[6:-2], refs[-2:]
    rows, tile = z.rows, vals_a.shape[2]
    blocks = vals_a.shape[1]
    half = cot_a.shape[1]

    def pick_of(n):
        held_at = ((me_ref[1] - (n >> 1)) & (z.zz - 1)) * 2 + (n & 1)
        slot = slot_ref[pl.ds(held_at, 1), :]
        at = slot >> log2(z.piece)
        zz = (me_ref[1] - (at >> 1)) & (z.zz - 1)
        at = zz * 2 + ((at & 1) ^ me_ref[2])
        slot = at * z.piece + (slot & (z.piece - 1))
        return one_hot(iota((rows, rows), 0) == slot)

    def held_of(n):
        if packed:
            return y_refs[0][n]
        return jnp.concatenate(
            [
                y_refs[k * z.grp + s][rel, pl.ds(pl.multiple_of(n * z.pair, z.pair), z.pair), :]
                for k in range(z.zz)
                for rel in range(2)
                for s in range(z.grp)
            ],
            axis=0,
        )

    total[...] = jnp.zeros_like(total)
    panel[pl.ds(z.dom * rows, tile), :] = jnp.zeros((tile, half), BF16)

    @pl.loop(0, z.dom)
    def _(n):
        at = pl.multiple_of(n * rows, rows)
        panel[pl.ds(at, rows), :] = dot_rows(pick_of(n), held_of(n)).astype(BF16)

    for side, (vals, cot, hidden) in enumerate(
        ((vals_a, cot_a, hidden_a), (vals_b, cot_b, hidden_b))
    ):
        @pl.loop(0, z.tiles)
        def _(t):
            at = pl.multiple_of(t * tile, tile)
            starts = [
                pl.multiple_of(cols_ref[side * z.tiles + t, k] * tile, tile) for k in range(blocks)
            ]
            left = jnp.concatenate([vals[t, k] for k in range(blocks)], axis=1)
            right = jnp.concatenate([panel[pl.ds(s, tile), :] for s in starts], axis=0)
            agg = dot(left, right)
            sig = jax.nn.sigmoid(agg)
            hidden[pl.ds(at, tile), :] = (agg * sig).astype(BF16)
            slope = sig * (1.0 + agg * (1.0 - sig))
            grad = (cot[pl.ds(at, tile), :].astype(F32) * slope).astype(BF16)
            for k in range(blocks):
                total[pl.ds(starts[k], tile), :] += dot_rows(vals[t, k], grad)

    @pl.loop(0, z.dom)
    def _(n):
        at = pl.multiple_of(n * rows, rows)
        back = dot(pick_of(n), total[pl.ds(at, rows), :].astype(BF16)).astype(BF16)
        for p in range(z.dom):
            partial_refs[p][n] = back[p * z.piece:(p + 1) * z.piece, :]


def grad_kernel(z, me_ref, left_a, left_b, mine_a, mine_b, come_a, come_b, *refs):
    outs, whole = refs[:-1], refs[-1]
    grad_a = (mine_a[...].astype(F32) + come_a[...].astype(F32)).astype(BF16)
    grad_b = (mine_b[...].astype(F32) + come_b[...].astype(F32)).astype(BF16)
    grad_b = jnp.concatenate(
        [grad_b[(n ^ 1) * z.piece:((n ^ 1) + 1) * z.piece, :] for n in range(z.dom)], axis=0
    )
    whole[...] = (dot(left_a[...], grad_a) + dot(left_b[...], grad_b)).astype(BF16)
    share = whole.shape[0] // z.grp
    for s in range(z.grp):
        at = pl.multiple_of((me_ref[0] ^ s) * share, share)
        outs[s][...] = whole[pl.ds(at, share), :]


def sum_kernel(z, me_ref, *refs):
    terms, outs, whole = refs[:z.grp], refs[z.grp:-1], refs[-1]
    whole[...] = sum(term[...].astype(F32) for term in terms).astype(BF16)
    share = whole.shape[0] // z.zz
    for k in range(z.zz):
        at = pl.multiple_of(((me_ref[1] - k) & (z.zz - 1)) * share, share)
        outs[k][...] = whole[pl.ds(at, share), :]


def last_kernel(z, me_ref, *refs):
    pieces, out = refs[:-1], refs[-1]
    share, half = pieces[0].shape[1], pieces[0].shape[2]
    for rel in range(2):
        left = pl.multiple_of((me_ref[2] ^ rel) * half, half)
        for s in range(z.grp):
            for k in range(z.zz):
                at = (me_ref[0] ^ s) * z.zz + ((me_ref[1] - k) & (z.zz - 1))
                out[pl.ds(pl.multiple_of(at * share, share), share), pl.ds(left, half)] = (
                    pieces[rel * z.grp + s][k].astype(F32)
                )


def shards(features, node_order, block_cols, block_count, block_vals, weight, cotangent):
    rows, width_in = features.shape
    hidden_units = weight.shape[1]
    half = hidden_units // 2
    tiles, blocks, tile = block_vals.shape[0], block_vals.shape[1], block_vals.shape[-1]
    z = Sizes(rows, tiles)
    at_grp, at_zz, core = lax.axis_index("grp"), lax.axis_index("zz"), lax.axis_index("core")
    me = jnp.stack([at_grp, at_zz, core]).astype(I32)

    def to_core(x):
        return lax.ppermute(x, "core", [(0, 1), (1, 0)])

    def to_grp(x, s):
        return lax.ppermute(x, "grp", [(i, i ^ s) for i in range(z.grp)]) if s else x

    def to_zz(x, k):
        return lax.ppermute(x, "zz", [(i, (i + k) % z.zz) for i in range(z.zz)]) if k else x

    own, other = call(
        lambda *refs: product_kernel(z, *refs),
        [((rows, half), BF16)] * 2,
        [("s", me), ("v", features), ("v", weight)],
        "product", 24,
    )
    ring = [[own, to_core(other)]]
    for k in range(1, z.zz):
        ring.append([to_zz(part, 1) for part in ring[-1]])

    index = call(
        lambda *refs: index_kernel(z, *refs),
        [((z.dom, z.pair), I32)] * z.grp + [((1, rows), I32)],
        [("s", me), ("v", node_order.reshape(1, rows))],
        "index", 32,
    )
    table = jnp.concatenate([to_grp(index[s], s) for s in range(z.grp)], axis=0)
    table = jnp.concatenate([table, to_core(table)], axis=0)
    table = jnp.concatenate([to_zz(table, k) for k in range(z.zz)], axis=0)
    slots = jnp.concatenate([index[-1], to_core(index[-1])], axis=0)
    slots = jnp.concatenate([to_zz(slots, k) for k in range(z.zz)], axis=0)

    vals_b = to_core(block_vals)
    cot_a = lax.dynamic_slice_in_dim(cotangent, core * half, half, axis=1)
    cot_b = to_core(lax.dynamic_slice_in_dim(cotangent, (1 - core) * half, half, axis=1))
    cols_a = jnp.where(iota((tiles, blocks), 1) < block_count[:, None], block_cols, -1)
    cols = jnp.concatenate([cols_a, to_core(cols_a)], axis=0)
    dev = cols >> log2(tiles)
    cols = jnp.where(cols < 0, z.dom * tiles, (dev ^ core) * tiles + (cols & (tiles - 1)))

    y, picked = [], None
    for k in range(z.zz):
        outs = [((2, z.per_grp, half), BF16)] * z.grp
        ins = [("s", me), ("v", table), ("v", ring[k][0]), ("v", ring[k][1])]
        if k == 0:
            outs, ins = outs + [((z.per_grp, width_in), BF16)] * z.grp, ins + [("v", features)]
        got = call(
            lambda *refs, k=k: select_kernel(z, k, *refs), outs, ins, "select", 32
        )
        if k == 0:
            picked = got[z.grp:]
        y += [to_grp(got[s], s) for s in range(z.grp)]

    packed = z.pair % 16 != 0
    if packed:
        y = jnp.stack(y).reshape(z.zz, z.grp, 2, z.dom, z.pair, half)
        y = [y.transpose(3, 0, 2, 1, 4, 5).reshape(z.dom, rows, half)]
    layer = call(
        lambda *refs: layer_kernel(z, packed, *refs),
        [((rows, half), BF16)] * 2 + [((z.dom, z.piece, half), BF16)] * z.dom,
        [("s", me), ("s", cols), ("v", slots)]
        + [("v", part) for part in y]
        + [("v", block_vals), ("v", vals_b), ("v", cot_a), ("v", cot_b)],
        "layer", 52,
        (pltpu.VMEM((z.dom * rows + tile, half), BF16), pltpu.VMEM((z.dom * rows + tile, half), F32)),
    )
    hidden_a, hidden_b, partial = layer[0], layer[1], layer[2:]

    held = jnp.stack([to_grp(picked[s], s) for s in range(z.grp)])
    held = held.reshape(z.grp, z.dom, z.pair, width_in).transpose(3, 1, 0, 2).reshape(width_in, rows)
    held_b = to_core(held)

    came = [partial[2 * (z.zz - 1) + rel] for rel in range(2)]
    for k in range(z.zz - 2, -1, -1):
        came = [to_zz(part, -1) for part in came]
        if k:
            came = [
                (part.astype(F32) + partial[2 * k + rel].astype(F32)).astype(BF16)
                for rel, part in enumerate(came)
            ]

    come = to_core(hidden_b)
    first = core == 0
    hidden = jnp.concatenate(
        [jnp.where(first, hidden_a, come), jnp.where(first, come, hidden_a)], axis=1
    )

    share = width_in // z.grp
    terms = call(
        lambda *refs: grad_kernel(z, *refs),
        [((share, half), BF16)] * z.grp,
        [("s", me), ("v", held), ("v", held_b)]
        + [("v", part.reshape(rows, half)) for part in (partial[0], partial[1], came[0], came[1])],
        "grad", 32,
        (pltpu.VMEM((width_in, half), BF16),),
    )
    terms = [to_grp(terms[s], s) for s in range(z.grp)]
    parts = call(
        lambda *refs: sum_kernel(z, *refs),
        [((share // z.zz, half), BF16)] * z.zz,
        [("s", me)] + [("v", term) for term in terms],
        "sum", 16,
        (pltpu.VMEM((share, half), BF16),),
    )
    mine = sum(to_zz(parts[k], -k).astype(F32) for k in range(z.zz)).astype(BF16)
    mine = jnp.stack([to_zz(mine, k) for k in range(z.zz)])
    mine = [to_grp(mine, s) for s in range(z.grp)]
    pieces = mine + [to_core(part) for part in mine]
    (grad_weight,) = call(
        lambda *refs: last_kernel(z, *refs),
        [((width_in, hidden_units), F32)],
        [("s", me)] + [("v", part) for part in pieces],
        "last", 16,
    )
    return hidden, grad_weight


def solution(mesh):
    n_grp, n_dom = mesh.shape["grp"], mesh.shape["dom"]
    split = Mesh(mesh.devices.reshape(n_grp, n_dom // 2, 2), ("grp", "zz", "core"))
    by_rows = ("grp", "zz", "core")
    placed = (
        P(by_rows, None),
        P(by_rows),
        P(by_rows, None),
        P(by_rows),
        P(by_rows, None, None, None),
        P(),
        P(by_rows, None),
    )
    return jax.shard_map(
        shards,
        mesh=split,
        in_specs=placed,
        out_specs=(P(by_rows, None), P()),
        check_vma=False,
    )
```

time: 424 us -> 182 us (0.43)
  waiting for transfers between devices: 286 us -> 60.8 us
  starting transfers between devices: 3.08 us -> 79.7 us
  other arithmetic: 51.9 us -> 4.53 us
  Pallas kernels: 0 us -> 31.1 us
  matrix products: 26.5 us -> 0 us
  local copies, waits for them, and re-layouts: 27.2 us -> 4.52 us
  blocking collectives: 14.2 us -> 0 us
  between operations: 13.8 us -> 0.96 us
    psum x1 -> x0, waiting for transfers between devices: 135 us -> none  [shards(): grad_weight = lax.psum(local_grad, ('grp', 'dom'))]
    ppermute x0 -> x60, starting transfers between devices: none -> 79.7 us  [the longest x24 45.4 us: to_zz(): lax.ppermute(x, 'zz', [(i, (i + k) % z.zz) for i in range(z.zz)])]
    all_gather x1 -> x0, waiting for transfers between devices: 79.2 us -> none  [shards(): lax.all_gather(ordered, 'dom', axis=0, tiled=True)]
    ppermute x0 -> x60, waiting for transfers between devices: none -> 60.8 us  [the longest x24 36.1 us: to_zz(): lax.ppermute(x, 'zz', [(i, (i + k) % z.zz) for i in range(z.zz)])]
    reduce_scatter x1 -> x0, waiting for transfers between devices: 48.7 us -> none  [shards(): lax.psum_scatter(partial_value.astype(jnp.float32).astype(jnp.bfloat16),...]
    scatter-add x1 -> x0, other arithmetic: 36.8 us -> none  [shards(): partial_value.at[block_cols.reshape(-1)]]
    pallas_call x0 -> x10, Pallas kernels: none -> 31.1 us  [call(): pl.pallas_call(body, out_shape=tuple((jax.ShapeDtypeStruct(s, d) for s, d...]
    dot_general x4 -> x0, matrix products: 26.5 us -> none  [the longest x1 9.44 us: shards(): jnp.dot(lax.all_gather(ordered, 'dom', axis=0, tiled=True), weight, prefe...]
  transfers between devices with their start and end apart: 4 -> 60, of which waited for: 4 -> 29; matrix products, arithmetic and copies ran while one was open for 1% -> 3% of each run, Pallas kernels for 0% -> 14%
where the time goes in v1:
time: 182 us
  starting transfers between devices  79.7 us (44%)
  waiting for transfers between devices  60.8 us (33%)
  Pallas kernels  31.1 us (17%)
  other arithmetic  4.53 us (2%)
  local copies, waits for them, and re-layouts  4.52 us (2%)
    ppermute x24, starting transfers between devices, to_zz(): lax.ppermute(x, 'zz', [(i, (i + k) % z.zz) for i in range(z.zz)])  45.4 us
    ppermute x24, waiting for transfers between devices, to_zz(): lax.ppermute(x, 'zz', [(i, (i + k) % z.zz) for i in range(z.zz)])  36.1 us
    ppermute x24, starting transfers between devices, to_grp(): lax.ppermute(x, 'grp', [(i, i ^ s) for i in range(z.grp)])  33 us
    pallas_call x10, Pallas kernels, call(): pl.pallas_call(body, out_shape=tuple((jax.ShapeDtypeStruct(s, d) for s, d...  31.1 us
    ppermute x24, waiting for transfers between devices, to_grp(): lax.ppermute(x, 'grp', [(i, i ^ s) for i in range(z.grp)])  22.9 us
  transfers between devices with their start and end apart: 60, of which 29 were waited for; matrix products, arithmetic and copies ran while one was open for 3% of the time, Pallas kernels for 14%

profile of v1, /device:TPU:0, one launch (start us, length us, event | category | flops | bytes accessed | tf_op | source)
XLA Modules:
  0.0 181.5 jit_solution(13838550195057702256)
XLA Ops:
  2.5 3.0 %collective-permute-start.5 = (s32[8,16]{1,0:T(8,128)S(1)}, s32[8,16]{1,0:T(8,128)S(1)}, u32[]{:S(2)}, u32[]{:S(2)}) collective-permute-start(s32[8,16]{1,0:T(8,128)S(1)} %get-tuple-element.49), channel_id=1, source_target_pairs={{0,8},{8,0},{16,24},{24,16},{1,9},{9,1},{17,25},{25,17},{2,10},{10... | collective-permute-start | bytes 1544 | tf_op jit(solution)/shard_map/ppermute | solution.py:235
  5.5 1.5 collective-permute-start.6
  11.4 2.0 %collective-permute-start.16 = (bf16[512,256]{1,0:T(8,128)(2,1)S(1)}, bf16[512,256]{1,0:T(8,128)(2,1)S(1)}, u32[]{:S(2)}, u32[]{:S(2)}) collective-permute-start(bf16[512,256]{1,0:T(8,128)(2,1)S(1)} %get-tuple-element.52.refs_2_), channel_id=1, source_target_pairs={{0,2},{2,4},{4,6},{6,0},{1,3},{3,5},{5,7},{7,1},{8,10},{10,12},{12... | collective-permute-start | bytes 786440 | tf_op jit(solution)/shard_map/ppermute | solution.py:238
  14.0 1.4 collective-permute-done.1
  15.5 2.0 %collective-permute-start.17 = (bf16[512,256]{1,0:T(8,128)(2,1)S(1)}, bf16[512,256]{1,0:T(8,128)(2,1)S(1)}, u32[]{:S(2)}, u32[]{:S(2)}) collective-permute-start(bf16[512,256]{1,0:T(8,128)(2,1)S(1)} %collective-permute-done.12.refs_3_), channel_id=1, source_target_pairs={{0,2},{2,4},{4,6},{6,0},{1,3},{3,5},{5,7},{7,1},{8,10},{10,12},{12... | collective-permute-start | bytes 786440 | tf_op jit(solution)/shard_map/ppermute | solution.py:238
  17.6 1.6 collective-permute-start.2
  19.2 1.6 collective-permute-start.9
  21.5 6.6 %collective-permute-done.2 = s32[2,512]{1,0:T(2,128)S(1)} collective-permute-done((s32[2,512]{1,0:T(2,128)S(1)}, s32[2,512]{1,0:T(2,128)S(1)}, u32[]{:S(2)}, u32[]{:S(2)}) %collective-permute-start.2) | collective-permute-done | bytes 4128 | tf_op jit(solution)/shard_map/ppermute | solution.py:238
  28.8 2.2 %collective-permute-start.10 = (s32[64,16]{1,0:T(8,128)S(1)}, s32[64,16]{1,0:T(8,128)S(1)}, u32[]{:S(2)}, u32[]{:S(2)}) collective-permute-start(s32[64,16]{1,0:T(8,128)S(1)} %get-tuple-element.96), channel_id=1, source_target_pairs={{0,4},{2,6},{4,0},{6,2},{1,5},{3,7},{5,1},{7,3},{8,12},{10,14},{12... | collective-permute-start | bytes 12296 | tf_op jit(solution)/shard_map/ppermute | solution.py:238
  31.0 1.3 collective-permute-start.22
  33.6 1.8 %collective-permute-start.11 = (s32[64,16]{1,0:T(8,128)S(1)}, s32[64,16]{1,0:T(8,128)S(1)}, u32[]{:S(2)}, u32[]{:S(2)}) collective-permute-start(s32[64,16]{1,0:T(8,128)S(1)} %get-tuple-element.96), channel_id=1, source_target_pairs={{0,6},{2,0},{4,2},{6,4},{1,7},{3,1},{5,3},{7,5},{8,14},{10,8},{12,... | collective-permute-start | bytes 12296 | tf_op jit(solution)/shard_map/ppermute | solution.py:238
  35.5 10.9 %collective-permute-done.11 = s32[64,16]{1,0:T(8,128)S(1)} collective-permute-done((s32[64,16]{1,0:T(8,128)S(1)}, s32[64,16]{1,0:T(8,128)S(1)}, u32[]{:S(2)}, u32[]{:S(2)}) %collective-permute-start.11) | collective-permute-done | bytes 4128 | tf_op jit(solution)/shard_map/ppermute | solution.py:238
  47.1 2.3 %select.4 = (bf16[2,128,256]{2,1,0:T(8,128)(2,1)S(1)}, bf16[2,128,256]{2,1,0:T(8,128)(2,1)S(1)}, bf16[2,128,256]{2,1,0:T(8,128)(2,1)S(1)}, bf16[2,128,256]{2,1,0...) custom-call(s32[3]{0:T(128)S(1)} %pad_add_fusion.3.refs_0_, ...), custom_call_target="tpu_custom_call" | custom-call | tf_op jit(solution)/shard_map/select/pallas_call | solution.py:37
  52.5 1.5 collective-permute-start.14
  54.9 2.2 %collective-permute-start.15 = (bf16[2,128,256]{2,1,0:T(8,128)(2,1)S(1)}, bf16[2,128,256]{2,1,0:T(8,128)(2,1)S(1)}, u32[]{:S(2)}, u32[]{:S(2)}) collective-permute-start(bf16[2,128,256]{2,1,0:T(8,128)(2,1)S(1)} %get-tuple-element.57), channel_id=1, source_target_pairs={{0,24},{8,16},{16,8},{24,0},{1,25},{9,17},{17,9},{25,1},{2,26},{10... | collective-permute-start | bytes 393224 | tf_op jit(solution)/shard_map/ppermute | solution.py:235
  57.1 1.7 select.5
  59.7 2.1 %collective-permute-done.15.refs_6_ = bf16[2,128,256]{2,1,0:T(8,128)(2,1)S(1)} collective-permute-done((bf16[2,128,256]{2,1,0:T(8,128)(2,1)S(1)}, bf16[2,128,256]{2,1,0:T(8,128)(2,1)S(1)}, u32[]{:S(2)}, u32[]{:S(2)}) %collective-permute-start.15) | collective-permute-done | bytes 131104 | tf_op jit(solution)/shard_map/ppermute | solution.py:235
  61.8 1.6 collective-permute-start.19
  64.1 1.7 select.6
  67.1 1.7 select.7
  68.8 1.7 collective-permute-start.24
  72.4 1.6 collective-permute-start.29
  75.0 5.0 %collective-permute-start.36 = (bf16[128,1024]{1,0:T(8,128)(2,1)S(1)}, bf16[128,1024]{1,0:T(8,128)(2,1)}, u32[]{:S(2)}, u32[]{:S(2)}) collective-permute-start(bf16[128,1024]{1,0:T(8,128)(2,1)S(1)} %get-tuple-element.75), channel_id=1, source_target_pairs={{0,24},{8,16},{16,8},{24,0},{1,25},{9,17},{17,9},{25,1},{2,26},{10... | collective-permute-start | bytes 786440 | tf_op jit(solution)/shard_map/ppermute | solution.py:235
  80.7 1.7 collective-permute-done.29.refs_17_
  83.6 8.4 %collective-permute-done.30.refs_18_ = bf16[2,128,256]{2,1,0:T(8,128)(2,1)} collective-permute-done((bf16[2,128,256]{2,1,0:T(8,128)(2,1)S(1)}, bf16[2,128,256]{2,1,0:T(8,128)(2,1)}, u32[]{:S(2)}, u32[]{:S(2)}) %collective-permute-start.30) | collective-permute-done | bytes 131104 | tf_op jit(solution)/shard_map/ppermute | solution.py:235
  92.0 17.4 %layer.1 = (bf16[512,256]{1,0:T(8,128)(2,1)}, bf16[512,256]{1,0:T(8,128)(2,1)}, bf16[8,64,256]{2,1,0:T(8,128)(2,1)}, bf16[8,64,256]{2,1,0:T(8,128)(2,1)}, bf16[8...) custom-call(s32[3]{0:T(128)S(1)} %pad_add_fusion.3.refs_0_, ...), custom_call_target="tpu_custom_call" | custom-call | tf_op jit(solution)/shard_map/layer/pallas_call | solution.py:37
  109.4 2.3 %collective-permute-start.41 = (bf16[8,64,256]{2,1,0:T(8,128)(2,1)}, bf16[8,64,256]{2,1,0:T(8,128)(2,1)}, u32[]{:S(2)}, u32[]{:S(2)}) collective-permute-start(bf16[8,64,256]{2,1,0:T(8,128)(2,1)} %get-tuple-element.81), channel_id=1, source_target_pairs={{0,6},{2,0},{4,2},{6,4},{1,7},{3,1},{5,3},{7,5},{8,14},{10,8},{12,... | collective-permute-start | bytes 786440 | tf_op jit(solution)/shard_map/ppermute | solution.py:238
  114.9 2.9 %collective-permute-done.41 = bf16[8,64,256]{2,1,0:T(8,128)(2,1)} collective-permute-done((bf16[8,64,256]{2,1,0:T(8,128)(2,1)}, bf16[8,64,256]{2,1,0:T(8,128)(2,1)}, u32[]{:S(2)}, u32[]{:S(2)}) %collective-permute-start.41) | collective-permute-done | bytes 262176 | tf_op jit(solution)/shard_map/ppermute | solution.py:238
  118.8 4.3 %collective-permute-start.42 = (bf16[8,64,256]{2,1,0:T(8,128)(2,1)S(1)}, bf16[8,64,256]{2,1,0:T(8,128)(2,1)S(1)}, u32[]{:S(2)}, u32[]{:S(2)}) collective-permute-start(bf16[8,64,256]{2,1,0:T(8,128)(2,1)S(1)} %add_convert_fusion.1), channel_id=1, source_target_pairs={{0,6},{2,0},{4,2},{6,4},{1,7},{3,1},{5,3},{7,5},{8,14},{10,8},{12,... | collective-permute-start | bytes 786440 | tf_op jit(solution)/shard_map/ppermute | solution.py:238
  124.4 4.3 %collective-permute-start.39 = (bf16[8,64,256]{2,1,0:T(8,128)(2,1)S(1)}, bf16[8,64,256]{2,1,0:T(8,128)(2,1)S(1)}, u32[]{:S(2)}, u32[]{:S(2)}) collective-permute-start(bf16[8,64,256]{2,1,0:T(8,128)(2,1)S(1)} %add_convert_fusion.3), channel_id=1, source_target_pairs={{0,6},{2,0},{4,2},{6,4},{1,7},{3,1},{5,3},{7,5},{8,14},{10,8},{12,... | collective-permute-start | bytes 786440 | tf_op jit(solution)/shard_map/ppermute | solution.py:238
  129.8 4.3 %collective-permute-start.43 = (bf16[8,64,256]{2,1,0:T(8,128)(2,1)S(1)}, bf16[8,64,256]{2,1,0:T(8,128)(2,1)S(1)}, u32[]{:S(2)}, u32[]{:S(2)}) collective-permute-start(bf16[8,64,256]{2,1,0:T(8,128)(2,1)S(1)} %add_convert_fusion), channel_id=1, source_target_pairs={{0,6},{2,0},{4,2},{6,4},{1,7},{3,1},{5,3},{7,5},{8,14},{10,8},{12,... | collective-permute-start | bytes 786440 | tf_op jit(solution)/shard_map/ppermute | solution.py:238
  134.1 1.4 collective-permute-done.39
  135.6 4.3 %collective-permute-start.40 = (bf16[8,64,256]{2,1,0:T(8,128)(2,1)S(1)}, bf16[8,64,256]{2,1,0:T(8,128)(2,1)S(1)}, u32[]{:S(2)}, u32[]{:S(2)}) collective-permute-start(bf16[8,64,256]{2,1,0:T(8,128)(2,1)S(1)} %add_convert_fusion.2), channel_id=1, source_target_pairs={{0,6},{2,0},{4,2},{6,4},{1,7},{3,1},{5,3},{7,5},{8,14},{10,8},{12,... | collective-permute-start | bytes 786440 | tf_op jit(solution)/shard_map/ppermute | solution.py:238
  140.0 3.8 %collective-permute-done.40 = bf16[8,64,256]{2,1,0:T(8,128)(2,1)S(1)} collective-permute-done((bf16[8,64,256]{2,1,0:T(8,128)(2,1)S(1)}, bf16[8,64,256]{2,1,0:T(8,128)(2,1)S(1)}, u32[]{:S(2)}, u32[]{:S(2)}) %collective-permute-start.40) | collective-permute-done | bytes 262176 | tf_op jit(solution)/shard_map/ppermute | solution.py:238
  143.8 1.3 grad.1
  146.0 1.8 collective-permute-start.45
  148.7 1.5 collective-permute-done.44.refs_2_
  151.0 2.7 %collective-permute-done.46.refs_4_ = bf16[256,256]{1,0:T(8,128)(2,1)S(1)} collective-permute-done((bf16[256,256]{1,0:T(8,128)(2,1)S(1)}, bf16[256,256]{1,0:T(8,128)(2,1)S(1)}, u32[]{:S(2)}, u32[]{:S(2)}) %collective-permute-start.46) | collective-permute-done | bytes 131104 | tf_op jit(solution)/shard_map/ppermute | solution.py:235
  154.3 4.3 %collective-permute-start.47 = (bf16[64,256]{1,0:T(8,128)(2,1)S(1)}, bf16[64,256]{1,0:T(8,128)(2,1)S(1)}, u32[]{:S(2)}, u32[]{:S(2)}) collective-permute-start(bf16[64,256]{1,0:T(8,128)(2,1)S(1)} %get-tuple-element.89), channel_id=1, source_target_pairs={{0,6},{2,0},{4,2},{6,4},{1,7},{3,1},{5,3},{7,5},{8,14},{10,8},{12,... | collective-permute-start | bytes 98312 | tf_op jit(solution)/shard_map/ppermute | solution.py:238
  160.3 3.2 %collective-permute-done.48 = bf16[64,256]{1,0:T(8,128)(2,1)S(1)} collective-permute-done((bf16[64,256]{1,0:T(8,128)(2,1)S(1)}, bf16[64,256]{1,0:T(8,128)(2,1)S(1)}, u32[]{:S(2)}, u32[]{:S(2)}) %collective-permute-start.48) | collective-permute-done | bytes 32800 | tf_op jit(solution)/shard_map/ppermute | solution.py:238
  164.5 1.3 collective-permute-start.51
  165.8 2.7 %collective-permute-start.52 = (bf16[64,256]{1,0:T(8,128)(2,1)S(1)}, bf16[64,256]{1,0:T(8,128)(2,1)S(1)}, u32[]{:S(2)}, u32[]{:S(2)}) collective-permute-start(bf16[64,256]{1,0:T(8,128)(2,1)S(1)} %add_convert_fusion.4), channel_id=1, source_target_pairs={{0,6},{2,0},{4,2},{6,4},{1,7},{3,1},{5,3},{7,5},{8,14},{10,8},{12,... | collective-permute-start | bytes 98312 | tf_op jit(solution)/shard_map/ppermute | solution.py:238
  168.5 1.7 collective-permute-done.50
  170.9 1.4 collective-permute-start.54
  172.3 2.0 %collective-permute-start.55 = (bf16[4,64,256]{2,1,0:T(8,128)(2,1)S(1)}, bf16[4,64,256]{2,1,0:T(8,128)(2,1)S(1)}, u32[]{:S(2)}, u32[]{:S(2)}) collective-permute-start(bf16[4,64,256]{2,1,0:T(8,128)(2,1)S(1)} %pad_maximum_fusion.2.refs_1_), channel_id=1, source_target_pairs={{0,24},{8,16},{16,8},{24,0},{1,25},{9,17},{17,9},{25,1},{2,26},{10... | collective-permute-start | bytes 393224 | tf_op jit(solution)/shard_map/ppermute | solution.py:235
  174.3 1.6 collective-permute-done.53.refs_2_
  176.4 1.7 collective-permute-done.55.refs_4_
  179.5 2.0 %last.1 = f32[1024,512]{1,0:T(8,128)} custom-call(s32[3]{0:T(128)S(1)} %pad_add_fusion.3.refs_0_, bf16[4,64,256]{2,1,0:T(8,128)(2,1)S(1)} %pad_maximum_fusion.2.refs_1_, bf16[4,64,256]{2,1,0:T(8,128)(2,1)S(1)} %collective-permute-done.53.refs_2_, bf16[4,64,256]{2,1,0:T(8,128)(2,1)S(1)} %collective-permute-done.54.refs_3_, ...), custom_call_target="tpu_custom_call" | custom-call | tf_op jit(solution)/shard_map/last/pallas_call | solution.py:37
  (139 shorter events, 37.0 us)
Async XLA Ops:
  2.5 8.9 %collective-permute-start.5 = (s32[8,16]{1,0:T(8,128)S(1)}, s32[8,16]{1,0:T(8,128)S(1)}, u32[]{:S(2)}, u32[]{:S(2)}) collective-permute-start(s32[8,16]{1,0:T(8,128)S(1)} %get-tuple-element.49), channel_id=1, source_target_pairs={{0,8},{8,0},{16,24},{24,16},{1,9},{9,1},{17,25},{25,17},{2,10},{10... | collective-permute-start | bytes 1544 | tf_op jit(solution)/shard_map/ppermute | solution.py:235
  5.5 8.0 %collective-permute-start.6 = (s32[8,16]{1,0:T(8,128)S(1)}, s32[8,16]{1,0:T(8,128)S(1)}, u32[]{:S(2)}, u32[]{:S(2)}) collective-permute-start(s32[8,16]{1,0:T(8,128)S(1)} %get-tuple-element.50), channel_id=1, source_target_pairs={{0,16},{8,24},{16,0},{24,8},{1,17},{9,25},{17,1},{25,9},{2,18},{10... | collective-permute-start | bytes 1544 | tf_op jit(solution)/shard_map/ppermute | solution.py:235
  7.0 6.5 %collective-permute-start.7 = (s32[8,16]{1,0:T(8,128)S(1)}, s32[8,16]{1,0:T(8,128)S(1)}, u32[]{:S(2)}, u32[]{:S(2)}) collective-permute-start(s32[8,16]{1,0:T(8,128)S(1)} %get-tuple-element.51), channel_id=1, source_target_pairs={{0,24},{8,16},{16,8},{24,0},{1,25},{9,17},{17,9},{25,1},{2,26},{10... | collective-permute-start | bytes 1544 | tf_op jit(solution)/shard_map/ppermute | solution.py:235
  10.8 81.1 %collective-permute-start.31 = (bf16[4,16,128,128]{3,2,1,0:T(8,128)(2,1)}, bf16[4,16,128,128]{3,2,1,0:T(8,128)(2,1)}, u32[]{:S(2)}, u32[]{:S(2)}) collective-permute-start(bf16[4,16,128,128]{3,2,1,0:T(8,128)(2,1)} %refs_19_.1), channel_id=1, source_target_pairs={{0,1},{1,0},{2,3},{3,2},{4,5},{5,4},{6,7},{7,6},{8,9},{9,8},{10,11... | collective-permute-start | bytes 6291464 | tf_op jit(solution)/shard_map/ppermute | solution.py:232
  11.4 19.6 %collective-permute-start.16 = (bf16[512,256]{1,0:T(8,128)(2,1)S(1)}, bf16[512,256]{1,0:T(8,128)(2,1)S(1)}, u32[]{:S(2)}, u32[]{:S(2)}) collective-permute-start(bf16[512,256]{1,0:T(8,128)(2,1)S(1)} %get-tuple-element.52.refs_2_), channel_id=1, source_target_pairs={{0,2},{2,4},{4,6},{6,0},{1,3},{3,5},{5,7},{7,1},{8,10},{10,12},{12... | collective-permute-start | bytes 786440 | tf_op jit(solution)/shard_map/ppermute | solution.py:238
  13.5 5.7 %collective-permute-start = (s32[4,16]{1,0:T(4,128)S(1)}, s32[4,16]{1,0:T(4,128)S(1)}, u32[]{:S(2)}, u32[]{:S(2)}) collective-permute-start(s32[4,16]{1,0:T(4,128)S(1)} %fusion), channel_id=1, source_target_pairs={{0,1},{1,0},{2,3},{3,2},{4,5},{5,4},{6,7},{7,6},{8,9},{9,8},{10,11... | collective-permute-start | bytes 776 | tf_op jit(solution)/shard_map/ppermute | solution.py:232
  15.5 15.5 %collective-permute-start.17 = (bf16[512,256]{1,0:T(8,128)(2,1)S(1)}, bf16[512,256]{1,0:T(8,128)(2,1)S(1)}, u32[]{:S(2)}, u32[]{:S(2)}) collective-permute-start(bf16[512,256]{1,0:T(8,128)(2,1)S(1)} %collective-permute-done.12.refs_3_), channel_id=1, source_target_pairs={{0,2},{2,4},{4,6},{6,0},{1,3},{3,5},{5,7},{7,1},{8,10},{10,12},{12... | collective-permute-start | bytes 786440 | tf_op jit(solution)/shard_map/ppermute | solution.py:238
  17.6 10.5 %collective-permute-start.2 = (s32[2,512]{1,0:T(2,128)S(1)}, s32[2,512]{1,0:T(2,128)S(1)}, u32[]{:S(2)}, u32[]{:S(2)}) collective-permute-start(s32[2,512]{1,0:T(2,128)S(1)} %pad_add_fusion.2), channel_id=1, source_target_pairs={{0,2},{2,4},{4,6},{6,0},{1,3},{3,5},{5,7},{7,1},{8,10},{10,12},{12... | collective-permute-start | bytes 12296 | tf_op jit(solution)/shard_map/ppermute | solution.py:238
  19.2 9.6 %collective-permute-start.9 = (s32[64,16]{1,0:T(8,128)S(1)}, s32[64,16]{1,0:T(8,128)S(1)}, u32[]{:S(2)}, u32[]{:S(2)}) collective-permute-start(s32[64,16]{1,0:T(8,128)S(1)} %get-tuple-element.96), channel_id=1, source_target_pairs={{0,2},{2,4},{4,6},{6,0},{1,3},{3,5},{5,7},{7,1},{8,10},{10,12},{12... | collective-permute-start | bytes 12296 | tf_op jit(solution)/shard_map/ppermute | solution.py:238
  31.0 20.2 %collective-permute-start.21 = (bf16[512,256]{1,0:T(8,128)(2,1)S(1)}, bf16[512,256]{1,0:T(8,128)(2,1)S(1)}, u32[]{:S(2)}, u32[]{:S(2)}) collective-permute-start(bf16[512,256]{1,0:T(8,128)(2,1)S(1)} %collective-permute-done.16.refs_2_), channel_id=1, source_target_pairs={{0,2},{2,4},{4,6},{6,0},{1,3},{3,5},{5,7},{7,1},{8,10},{10,12},{12... | collective-permute-start | bytes 786440 | tf_op jit(solution)/shard_map/ppermute | solution.py:238
  31.0 21.0 %collective-permute-start.22 = (bf16[512,256]{1,0:T(8,128)(2,1)S(1)}, bf16[512,256]{1,0:T(8,128)(2,1)S(1)}, u32[]{:S(2)}, u32[]{:S(2)}) collective-permute-start(bf16[512,256]{1,0:T(8,128)(2,1)S(1)} %collective-permute-done.17.refs_3_), channel_id=1, source_target_pairs={{0,2},{2,4},{4,6},{6,0},{1,3},{3,5},{5,7},{7,1},{8,10},{10,12},{12... | collective-permute-start | bytes 786440 | tf_op jit(solution)/shard_map/ppermute | solution.py:238
  32.6 20.0 %collective-permute-start.32 = (bf16[512,256]{1,0:T(8,128)(2,1)S(1)}, bf16[512,256]{1,0:T(8,128)(2,1)S(1)}, u32[]{:S(2)}, u32[]{:S(2)}) collective-permute-start(bf16[512,256]{1,0:T(8,128)(2,1)S(1)} %get-tuple-element.94), channel_id=1, source_target_pairs={{0,1},{1,0},{2,3},{3,2},{4,5},{5,4},{6,7},{7,6},{8,9},{9,8},{10,11... | collective-permute-start | bytes 786440 | tf_op jit(solution)/shard_map/ppermute | solution.py:232
  33.6 12.7 %collective-permute-start.11 = (s32[64,16]{1,0:T(8,128)S(1)}, s32[64,16]{1,0:T(8,128)S(1)}, u32[]{:S(2)}, u32[]{:S(2)}) collective-permute-start(s32[64,16]{1,0:T(8,128)S(1)} %get-tuple-element.96), channel_id=1, source_target_pairs={{0,6},{2,0},{4,2},{6,4},{1,7},{3,1},{5,3},{7,5},{8,14},{10,8},{12,... | collective-permute-start | bytes 12296 | tf_op jit(solution)/shard_map/ppermute | solution.py:238
  49.9 5.0 %collective-permute-start.13 = (bf16[2,128,256]{2,1,0:T(8,128)(2,1)S(1)}, bf16[2,128,256]{2,1,0:T(8,128)(2,1)S(1)}, u32[]{:S(2)}, u32[]{:S(2)}) collective-permute-start(bf16[2,128,256]{2,1,0:T(8,128)(2,1)S(1)} %get-tuple-element.55), channel_id=1, source_target_pairs={{0,8},{8,0},{16,24},{24,16},{1,9},{9,1},{17,25},{25,17},{2,10},{10... | collective-permute-start | bytes 393224 | tf_op jit(solution)/shard_map/ppermute | solution.py:235
  51.2 12.2 %collective-permute-start.26 = (bf16[512,256]{1,0:T(8,128)(2,1)S(1)}, bf16[512,256]{1,0:T(8,128)(2,1)S(1)}, u32[]{:S(2)}, u32[]{:S(2)}) collective-permute-start(bf16[512,256]{1,0:T(8,128)(2,1)S(1)} %collective-permute-done.21.refs_2_), channel_id=1, source_target_pairs={{0,2},{2,4},{4,6},{6,0},{1,3},{3,5},{5,7},{7,1},{8,10},{10,12},{12... | collective-permute-start | bytes 786440 | tf_op jit(solution)/shard_map/ppermute | solution.py:238
  52.0 13.8 %collective-permute-start.27 = (bf16[512,256]{1,0:T(8,128)(2,1)S(1)}, bf16[512,256]{1,0:T(8,128)(2,1)S(1)}, u32[]{:S(2)}, u32[]{:S(2)}) collective-permute-start(bf16[512,256]{1,0:T(8,128)(2,1)S(1)} %collective-permute-done.22.refs_3_), channel_id=1, source_target_pairs={{0,2},{2,4},{4,6},{6,0},{1,3},{3,5},{5,7},{7,1},{8,10},{10,12},{12... | collective-permute-start | bytes 786440 | tf_op jit(solution)/shard_map/ppermute | solution.py:238
  52.5 6.4 %collective-permute-start.14 = (bf16[2,128,256]{2,1,0:T(8,128)(2,1)S(1)}, bf16[2,128,256]{2,1,0:T(8,128)(2,1)S(1)}, u32[]{:S(2)}, u32[]{:S(2)}) collective-permute-start(bf16[2,128,256]{2,1,0:T(8,128)(2,1)S(1)} %get-tuple-element.56), channel_id=1, source_target_pairs={{0,16},{8,24},{16,0},{24,8},{1,17},{9,25},{17,1},{25,9},{2,18},{10... | collective-permute-start | bytes 393224 | tf_op jit(solution)/shard_map/ppermute | solution.py:235
  54.9 6.9 %collective-permute-start.15 = (bf16[2,128,256]{2,1,0:T(8,128)(2,1)S(1)}, bf16[2,128,256]{2,1,0:T(8,128)(2,1)S(1)}, u32[]{:S(2)}, u32[]{:S(2)}) collective-permute-start(bf16[2,128,256]{2,1,0:T(8,128)(2,1)S(1)} %get-tuple-element.57), channel_id=1, source_target_pairs={{0,24},{8,16},{16,8},{24,0},{1,25},{9,17},{17,9},{25,1},{2,26},{10... | collective-permute-start | bytes 393224 | tf_op jit(solution)/shard_map/ppermute | solution.py:235
  58.9 9.9 %collective-permute-start.18 = (bf16[2,128,256]{2,1,0:T(8,128)(2,1)S(1)}, bf16[2,128,256]{2,1,0:T(8,128)(2,1)S(1)}, u32[]{:S(2)}, u32[]{:S(2)}) collective-permute-start(bf16[2,128,256]{2,1,0:T(8,128)(2,1)S(1)} %get-tuple-element.59), channel_id=1, source_target_pairs={{0,8},{8,0},{16,24},{24,16},{1,9},{9,1},{17,25},{25,17},{2,10},{10... | collective-permute-start | bytes 393224 | tf_op jit(solution)/shard_map/ppermute | solution.py:235
  61.8 8.7 %collective-permute-start.19 = (bf16[2,128,256]{2,1,0:T(8,128)(2,1)S(1)}, bf16[2,128,256]{2,1,0:T(8,128)(2,1)S(1)}, u32[]{:S(2)}, u32[]{:S(2)}) collective-permute-start(bf16[2,128,256]{2,1,0:T(8,128)(2,1)S(1)} %get-tuple-element.60), channel_id=1, source_target_pairs={{0,16},{8,24},{16,0},{24,8},{1,17},{9,25},{17,1},{25,9},{2,18},{10... | collective-permute-start | bytes 393224 | tf_op jit(solution)/shard_map/ppermute | solution.py:235
  63.4 7.7 %collective-permute-start.20 = (bf16[2,128,256]{2,1,0:T(8,128)(2,1)S(1)}, bf16[2,128,256]{2,1,0:T(8,128)(2,1)S(1)}, u32[]{:S(2)}, u32[]{:S(2)}) collective-permute-start(bf16[2,128,256]{2,1,0:T(8,128)(2,1)S(1)} %get-tuple-element.61), channel_id=1, source_target_pairs={{0,24},{8,16},{16,8},{24,0},{1,25},{9,17},{17,9},{25,1},{2,26},{10... | collective-permute-start | bytes 393224 | tf_op jit(solution)/shard_map/ppermute | solution.py:235
  65.8 6.5 %collective-permute-start.23 = (bf16[2,128,256]{2,1,0:T(8,128)(2,1)S(1)}, bf16[2,128,256]{2,1,0:T(8,128)(2,1)S(1)}, u32[]{:S(2)}, u32[]{:S(2)}) collective-permute-start(bf16[2,128,256]{2,1,0:T(8,128)(2,1)S(1)} %get-tuple-element.63), channel_id=1, source_target_pairs={{0,8},{8,0},{16,24},{24,16},{1,9},{9,1},{17,25},{25,17},{2,10},{10... | collective-permute-start | bytes 393224 | tf_op jit(solution)/shard_map/ppermute | solution.py:235
  68.8 6.2 %collective-permute-start.24 = (bf16[2,128,256]{2,1,0:T(8,128)(2,1)S(1)}, bf16[2,128,256]{2,1,0:T(8,128)(2,1)S(1)}, u32[]{:S(2)}, u32[]{:S(2)}) collective-permute-start(bf16[2,128,256]{2,1,0:T(8,128)(2,1)S(1)} %get-tuple-element.64), channel_id=1, source_target_pairs={{0,16},{8,24},{16,0},{24,8},{1,17},{9,25},{17,1},{25,9},{2,18},{10... | collective-permute-start | bytes 393224 | tf_op jit(solution)/shard_map/ppermute | solution.py:235
  70.5 9.5 %collective-permute-start.25 = (bf16[2,128,256]{2,1,0:T(8,128)(2,1)S(1)}, bf16[2,128,256]{2,1,0:T(8,128)(2,1)S(1)}, u32[]{:S(2)}, u32[]{:S(2)}) collective-permute-start(bf16[2,128,256]{2,1,0:T(8,128)(2,1)S(1)} %get-tuple-element.65), channel_id=1, source_target_pairs={{0,24},{8,16},{16,8},{24,0},{1,25},{9,17},{17,9},{25,1},{2,26},{10... | collective-permute-start | bytes 393224 | tf_op jit(solution)/shard_map/ppermute | solution.py:235
  71.2 8.8 %collective-permute-start.28 = (bf16[2,128,256]{2,1,0:T(8,128)(2,1)S(1)}, bf16[2,128,256]{2,1,0:T(8,128)(2,1)S(1)}, u32[]{:S(2)}, u32[]{:S(2)}) collective-permute-start(bf16[2,128,256]{2,1,0:T(8,128)(2,1)S(1)} %get-tuple-element.67), channel_id=1, source_target_pairs={{0,8},{8,0},{16,24},{24,16},{1,9},{9,1},{17,25},{25,17},{2,10},{10... | collective-permute-start | bytes 393224 | tf_op jit(solution)/shard_map/ppermute | solution.py:235
  72.4 10.0 %collective-permute-start.29 = (bf16[2,128,256]{2,1,0:T(8,128)(2,1)S(1)}, bf16[2,128,256]{2,1,0:T(8,128)(2,1)S(1)}, u32[]{:S(2)}, u32[]{:S(2)}) collective-permute-start(bf16[2,128,256]{2,1,0:T(8,128)(2,1)S(1)} %get-tuple-element.68), channel_id=1, source_target_pairs={{0,16},{8,24},{16,0},{24,8},{1,17},{9,25},{17,1},{25,9},{2,18},{10... | collective-permute-start | bytes 393224 | tf_op jit(solution)/shard_map/ppermute | solution.py:235
  75.0 37.9 %collective-permute-start.36 = (bf16[128,1024]{1,0:T(8,128)(2,1)S(1)}, bf16[128,1024]{1,0:T(8,128)(2,1)}, u32[]{:S(2)}, u32[]{:S(2)}) collective-permute-start(bf16[128,1024]{1,0:T(8,128)(2,1)S(1)} %get-tuple-element.75), channel_id=1, source_target_pairs={{0,24},{8,16},{16,8},{24,0},{1,25},{9,17},{17,9},{25,1},{2,26},{10... | collective-permute-start | bytes 786440 | tf_op jit(solution)/shard_map/ppermute | solution.py:235
  80.0 32.9 %collective-permute-start.34 = (bf16[128,1024]{1,0:T(8,128)(2,1)S(1)}, bf16[128,1024]{1,0:T(8,128)(2,1)}, u32[]{:S(2)}, u32[]{:S(2)}) collective-permute-start(bf16[128,1024]{1,0:T(8,128)(2,1)S(1)} %get-tuple-element.73), channel_id=1, source_target_pairs={{0,8},{8,0},{16,24},{24,16},{1,9},{9,1},{17,25},{25,17},{2,10},{10... | collective-permute-start | bytes 786440 | tf_op jit(solution)/shard_map/ppermute | solution.py:235
  80.0 32.9 %collective-permute-start.35 = (bf16[128,1024]{1,0:T(8,128)(2,1)S(1)}, bf16[128,1024]{1,0:T(8,128)(2,1)}, u32[]{:S(2)}, u32[]{:S(2)}) collective-permute-start(bf16[128,1024]{1,0:T(8,128)(2,1)S(1)} %get-tuple-element.74), channel_id=1, source_target_pairs={{0,16},{8,24},{16,0},{24,8},{1,17},{9,25},{17,1},{25,9},{2,18},{10... | collective-permute-start | bytes 786440 | tf_op jit(solution)/shard_map/ppermute | solution.py:235
  82.4 9.6 %collective-permute-start.30 = (bf16[2,128,256]{2,1,0:T(8,128)(2,1)S(1)}, bf16[2,128,256]{2,1,0:T(8,128)(2,1)}, u32[]{:S(2)}, u32[]{:S(2)}) collective-permute-start(bf16[2,128,256]{2,1,0:T(8,128)(2,1)S(1)} %get-tuple-element.69), channel_id=1, source_target_pairs={{0,24},{8,16},{16,8},{24,0},{1,25},{9,17},{17,9},{25,1},{2,26},{10... | collective-permute-start | bytes 393224 | tf_op jit(solution)/shard_map/ppermute | solution.py:235
  109.4 8.4 %collective-permute-start.41 = (bf16[8,64,256]{2,1,0:T(8,128)(2,1)}, bf16[8,64,256]{2,1,0:T(8,128)(2,1)}, u32[]{:S(2)}, u32[]{:S(2)}) collective-permute-start(bf16[8,64,256]{2,1,0:T(8,128)(2,1)} %get-tuple-element.81), channel_id=1, source_target_pairs={{0,6},{2,0},{4,2},{6,4},{1,7},{3,1},{5,3},{7,5},{8,14},{10,8},{12,... | collective-permute-start | bytes 786440 | tf_op jit(solution)/shard_map/ppermute | solution.py:238
  111.7 11.7 %collective-permute-start.38 = (bf16[8,64,256]{2,1,0:T(8,128)(2,1)}, bf16[8,64,256]{2,1,0:T(8,128)(2,1)}, u32[]{:S(2)}, u32[]{:S(2)}) collective-permute-start(bf16[8,64,256]{2,1,0:T(8,128)(2,1)} %get-tuple-element.78), channel_id=1, source_target_pairs={{0,6},{2,0},{4,2},{6,4},{1,7},{3,1},{5,3},{7,5},{8,14},{10,8},{12,... | collective-permute-start | bytes 786440 | tf_op jit(solution)/shard_map/ppermute | solution.py:238
  114.8 25.1 %collective-permute-start.37 = (bf16[1024,512]{1,0:T(8,128)(2,1)S(1)}, bf16[1024,512]{1,0:T(8,128)(2,1)S(1)}, u32[]{:S(2)}, u32[]{:S(2)}) collective-permute-start(bf16[1024,512]{1,0:T(8,128)(2,1)S(1)} %copy.58.refs_1_), channel_id=1, source_target_pairs={{0,1},{1,0},{2,3},{3,2},{4,5},{5,4},{6,7},{7,6},{8,9},{9,8},{10,11... | collective-permute-start | bytes 3145736 | tf_op jit(solution)/shard_map/ppermute | solution.py:232
  118.8 10.9 %collective-permute-start.42 = (bf16[8,64,256]{2,1,0:T(8,128)(2,1)S(1)}, bf16[8,64,256]{2,1,0:T(8,128)(2,1)S(1)}, u32[]{:S(2)}, u32[]{:S(2)}) collective-permute-start(bf16[8,64,256]{2,1,0:T(8,128)(2,1)S(1)} %add_convert_fusion.1), channel_id=1, source_target_pairs={{0,6},{2,0},{4,2},{6,4},{1,7},{3,1},{5,3},{7,5},{8,14},{10,8},{12,... | collective-permute-start | bytes 786440 | tf_op jit(solution)/shard_map/ppermute | solution.py:238
  124.4 11.1 %collective-permute-start.39 = (bf16[8,64,256]{2,1,0:T(8,128)(2,1)S(1)}, bf16[8,64,256]{2,1,0:T(8,128)(2,1)S(1)}, u32[]{:S(2)}, u32[]{:S(2)}) collective-permute-start(bf16[8,64,256]{2,1,0:T(8,128)(2,1)S(1)} %add_convert_fusion.3), channel_id=1, source_target_pairs={{0,6},{2,0},{4,2},{6,4},{1,7},{3,1},{5,3},{7,5},{8,14},{10,8},{12,... | collective-permute-start | bytes 786440 | tf_op jit(solution)/shard_map/ppermute | solution.py:238
  129.8 10.2 %collective-permute-start.43 = (bf16[8,64,256]{2,1,0:T(8,128)(2,1)S(1)}, bf16[8,64,256]{2,1,0:T(8,128)(2,1)S(1)}, u32[]{:S(2)}, u32[]{:S(2)}) collective-permute-start(bf16[8,64,256]{2,1,0:T(8,128)(2,1)S(1)} %add_convert_fusion), channel_id=1, source_target_pairs={{0,6},{2,0},{4,2},{6,4},{1,7},{3,1},{5,3},{7,5},{8,14},{10,8},{12,... | collective-permute-start | bytes 786440 | tf_op jit(solution)/shard_map/ppermute | solution.py:238
  135.6 8.2 %collective-permute-start.40 = (bf16[8,64,256]{2,1,0:T(8,128)(2,1)S(1)}, bf16[8,64,256]{2,1,0:T(8,128)(2,1)S(1)}, u32[]{:S(2)}, u32[]{:S(2)}) collective-permute-start(bf16[8,64,256]{2,1,0:T(8,128)(2,1)S(1)} %add_convert_fusion.2), channel_id=1, source_target_pairs={{0,6},{2,0},{4,2},{6,4},{1,7},{3,1},{5,3},{7,5},{8,14},{10,8},{12,... | collective-permute-start | bytes 786440 | tf_op jit(solution)/shard_map/ppermute | solution.py:238
  145.1 5.0 %collective-permute-start.44 = (bf16[256,256]{1,0:T(8,128)(2,1)S(1)}, bf16[256,256]{1,0:T(8,128)(2,1)S(1)}, u32[]{:S(2)}, u32[]{:S(2)}) collective-permute-start(bf16[256,256]{1,0:T(8,128)(2,1)S(1)} %get-tuple-element.85), channel_id=1, source_target_pairs={{0,8},{8,0},{16,24},{24,16},{1,9},{9,1},{17,25},{25,17},{2,10},{10... | collective-permute-start | bytes 393224 | tf_op jit(solution)/shard_map/ppermute | solution.py:235
  146.0 5.0 %collective-permute-start.45 = (bf16[256,256]{1,0:T(8,128)(2,1)S(1)}, bf16[256,256]{1,0:T(8,128)(2,1)S(1)}, u32[]{:S(2)}, u32[]{:S(2)}) collective-permute-start(bf16[256,256]{1,0:T(8,128)(2,1)S(1)} %get-tuple-element.86), channel_id=1, source_target_pairs={{0,16},{8,24},{16,0},{24,8},{1,17},{9,25},{17,1},{25,9},{2,18},{10... | collective-permute-start | bytes 393224 | tf_op jit(solution)/shard_map/ppermute | solution.py:235
  147.8 5.9 %collective-permute-start.46 = (bf16[256,256]{1,0:T(8,128)(2,1)S(1)}, bf16[256,256]{1,0:T(8,128)(2,1)S(1)}, u32[]{:S(2)}, u32[]{:S(2)}) collective-permute-start(bf16[256,256]{1,0:T(8,128)(2,1)S(1)} %get-tuple-element.87), channel_id=1, source_target_pairs={{0,24},{8,16},{16,8},{24,0},{1,25},{9,17},{17,9},{25,1},{2,26},{10... | collective-permute-start | bytes 393224 | tf_op jit(solution)/shard_map/ppermute | solution.py:235
  154.3 5.9 %collective-permute-start.47 = (bf16[64,256]{1,0:T(8,128)(2,1)S(1)}, bf16[64,256]{1,0:T(8,128)(2,1)S(1)}, u32[]{:S(2)}, u32[]{:S(2)}) collective-permute-start(bf16[64,256]{1,0:T(8,128)(2,1)S(1)} %get-tuple-element.89), channel_id=1, source_target_pairs={{0,6},{2,0},{4,2},{6,4},{1,7},{3,1},{5,3},{7,5},{8,14},{10,8},{12,... | collective-permute-start | bytes 98312 | tf_op jit(solution)/shard_map/ppermute | solution.py:238
  158.7 5.7 %collective-permute-start.49 = (bf16[64,256]{1,0:T(8,128)(2,1)S(1)}, bf16[64,256]{1,0:T(8,128)(2,1)S(1)}, u32[]{:S(2)}, u32[]{:S(2)}) collective-permute-start(bf16[64,256]{1,0:T(8,128)(2,1)S(1)} %get-tuple-element.91), channel_id=1, source_target_pairs={{0,2},{2,4},{4,6},{6,0},{1,3},{3,5},{5,7},{7,1},{8,10},{10,12},{12... | collective-permute-start | bytes 98312 | tf_op jit(solution)/shard_map/ppermute | solution.py:238
  164.4 5.8 %collective-permute-start.50 = (bf16[64,256]{1,0:T(8,128)(2,1)S(1)}, bf16[64,256]{1,0:T(8,128)(2,1)S(1)}, u32[]{:S(2)}, u32[]{:S(2)}) collective-permute-start(bf16[64,256]{1,0:T(8,128)(2,1)S(1)} %add_convert_fusion.4), channel_id=1, source_target_pairs={{0,2},{2,4},{4,6},{6,0},{1,3},{3,5},{5,7},{7,1},{8,10},{10,12},{12... | collective-permute-start | bytes 98312 | tf_op jit(solution)/shard_map/ppermute | solution.py:238
  164.5 5.7 %collective-permute-start.51 = (bf16[64,256]{1,0:T(8,128)(2,1)S(1)}, bf16[64,256]{1,0:T(8,128)(2,1)S(1)}, u32[]{:S(2)}, u32[]{:S(2)}) collective-permute-start(bf16[64,256]{1,0:T(8,128)(2,1)S(1)} %add_convert_fusion.4), channel_id=1, source_target_pairs={{0,4},{2,6},{4,0},{6,2},{1,5},{3,7},{5,1},{7,3},{8,12},{10,14},{12... | collective-permute-start | bytes 98312 | tf_op jit(solution)/shard_map/ppermute | solution.py:238
  168.5 9.6 %collective-permute-start.33 = (bf16[512,256]{1,0:T(8,128)(2,1)S(1)}, bf16[512,256]{1,0:T(8,128)(2,1)S(1)}, u32[]{:S(2)}, u32[]{:S(2)}) collective-permute-start(bf16[512,256]{1,0:T(8,128)(2,1)S(1)} %copy-done.15), channel_id=1, source_target_pairs={{0,1},{1,0},{2,3},{3,2},{4,5},{5,4},{6,7},{7,6},{8,9},{9,8},{10,11... | collective-permute-start | bytes 786440 | tf_op jit(solution)/shard_map/ppermute | solution.py:232
  170.8 5.2 %collective-permute-start.53 = (bf16[4,64,256]{2,1,0:T(8,128)(2,1)S(1)}, bf16[4,64,256]{2,1,0:T(8,128)(2,1)S(1)}, u32[]{:S(2)}, u32[]{:S(2)}) collective-permute-start(bf16[4,64,256]{2,1,0:T(8,128)(2,1)S(1)} %pad_maximum_fusion.2.refs_1_), channel_id=1, source_target_pairs={{0,8},{8,0},{16,24},{24,16},{1,9},{9,1},{17,25},{25,17},{2,10},{10... | collective-permute-start | bytes 393224 | tf_op jit(solution)/shard_map/ppermute | solution.py:235
  170.9 5.5 %collective-permute-start.54 = (bf16[4,64,256]{2,1,0:T(8,128)(2,1)S(1)}, bf16[4,64,256]{2,1,0:T(8,128)(2,1)S(1)}, u32[]{:S(2)}, u32[]{:S(2)}) collective-permute-start(bf16[4,64,256]{2,1,0:T(8,128)(2,1)S(1)} %pad_maximum_fusion.2.refs_1_), channel_id=1, source_target_pairs={{0,16},{8,24},{16,0},{24,8},{1,17},{9,25},{17,1},{25,9},{2,18},{10... | collective-permute-start | bytes 393224 | tf_op jit(solution)/shard_map/ppermute | solution.py:235
  172.3 5.9 %collective-permute-start.55 = (bf16[4,64,256]{2,1,0:T(8,128)(2,1)S(1)}, bf16[4,64,256]{2,1,0:T(8,128)(2,1)S(1)}, u32[]{:S(2)}, u32[]{:S(2)}) collective-permute-start(bf16[4,64,256]{2,1,0:T(8,128)(2,1)S(1)} %pad_maximum_fusion.2.refs_1_), channel_id=1, source_target_pairs={{0,24},{8,16},{16,8},{24,0},{1,25},{9,17},{17,9},{25,1},{2,26},{10... | collective-permute-start | bytes 393224 | tf_op jit(solution)/shard_map/ppermute | solution.py:235
  (28 other events, 340.6 us)

commit v2 on v1

v2 whole, which is shorter than its diff:
```python
import jax
import jax.numpy as jnp
from jax import lax
from jax.experimental import pallas as pl
from jax.experimental.pallas import tpu as pltpu
from jax.sharding import Mesh, PartitionSpec as P

BF16 = jnp.bfloat16
F32 = jnp.float32
I32 = jnp.int32


def log2(n):
    assert n & (n - 1) == 0
    return n.bit_length() - 1


def iota(shape, dim):
    return lax.broadcasted_iota(I32, shape, dim)


def one_hot(mask):
    return jnp.where(mask, 1.0, 0.0).astype(BF16)


def dot(a, b):
    return jnp.dot(a, b, preferred_element_type=F32)


def dot_rows(a, b):
    return lax.dot_general(a, b, (((0,), (0,)), ((), ())), preferred_element_type=F32)


def call(body, outs, ins, name, mib, us, scratch=()):
    smem = pl.BlockSpec(memory_space=pltpu.SMEM)
    vmem = pl.BlockSpec(memory_space=pltpu.VMEM)
    return pl.pallas_call(
        body,
        out_shape=tuple(jax.ShapeDtypeStruct(s, d) for s, d in outs),
        in_specs=[smem if where == "s" else vmem for where, _ in ins],
        out_specs=tuple(vmem for _ in outs),
        scratch_shapes=list(scratch),
        compiler_params=pltpu.CompilerParams(vmem_limit_bytes=mib << 20),
        cost_estimate=pl.CostEstimate(flops=int(us * 1e9), bytes_accessed=0, transcendentals=0),
        name=name,
    )(*(value for _, value in ins))


class Sizes:
    def __init__(self, rows, tiles):
        self.grp, self.zz = lax.axis_size("grp"), lax.axis_size("zz")
        self.dom = 2 * self.zz
        self.rows, self.tiles = rows, tiles
        self.pair = rows // (self.grp * self.dom)
        self.piece = self.grp * self.pair
        self.per_grp = self.dom * self.pair


def column(row):
    n = row.shape[1]
    on = iota((n, n), 0) == iota((n, n), 1)
    return jnp.sum(jnp.where(on, row.astype(F32), 0.0), axis=1, keepdims=True).astype(I32)


def index_kernel(z, me_ref, order_ref, out_ref):
    rows = z.rows
    shift = log2(rows)
    order_r = order_ref[...]
    order_c = column(order_r)
    down, across = iota((rows, rows), 0), iota((rows, rows), 1)
    source_r, source_c = order_r >> shift, order_c >> shift
    same = jnp.where(source_c == source_r, 1.0, 0.0)
    rank_c = jnp.sum(jnp.where(across < down, same, 0.0), axis=1, keepdims=True).astype(I32)
    rank_r = jnp.sum(jnp.where(down < across, same, 0.0), axis=0, keepdims=True).astype(I32)
    row_c = (order_c & (rows - 1)).astype(F32)
    asked = jnp.where(source_c * z.pair + rank_c == across, row_c, 0.0)
    out_ref[0:1, :] = jnp.sum(asked, axis=0, keepdims=True).astype(I32)
    across_grp = (source_r >> log2(z.dom)) ^ me_ref[0]
    inner = source_r & (z.dom - 1)
    out_ref[1:2, :] = (inner * z.grp + across_grp) * z.pair + rank_r


def product_kernel(z, me_ref, features_ref, weight_ref, own_ref, other_ref):
    half = own_ref.shape[1]
    for flip, out in ((0, own_ref), (1, other_ref)):
        at = pl.multiple_of((me_ref[2] ^ flip) * half, half)
        out[...] = dot(features_ref[...], weight_ref[:, pl.ds(at, half)]).astype(BF16)


def asked_rows(z, me_ref, table):
    shape = (z.rows, table.shape[0])
    row = iota(shape, 0)
    s, n = row >> log2(z.per_grp), (row >> log2(z.pair)) & (z.dom - 1)
    k = (me_ref[1] - (n >> 1)) & (z.zz - 1)
    spread = one_hot(iota(shape, 1) == ((s * 2 + (n & 1)) * z.zz + k) * 2)
    high = dot(spread, (table >> 4).astype(F32).astype(BF16))
    return high * 16.0 + dot(spread, (table & 15).astype(F32).astype(BF16))


def pick_of_source(z, me_ref, asked, k, rel):
    shape = (z.rows, z.rows)
    source = me_ref[0] * z.dom + ((me_ref[1] - k) & (z.zz - 1)) * 2 + (me_ref[2] ^ rel)
    mine = iota(shape, 1) == source * z.pair + (iota(shape, 0) & (z.pair - 1))
    wanted = jnp.sum(jnp.where(mine, asked, 0.0), axis=1, keepdims=True).astype(I32)
    return one_hot(iota(shape, 1) == wanted)


def select_own_kernel(z, me_ref, table_ref, own_ref, other_ref, features_ref, *outs):
    asked = asked_rows(z, me_ref, table_ref[...])
    for rel, part in enumerate((own_ref, other_ref)):
        pick = pick_of_source(z, me_ref, asked, 0, rel)
        got = dot(pick, part[...]).astype(BF16)
        for s in range(z.grp):
            outs[s][rel] = got[s * z.per_grp:(s + 1) * z.per_grp, :]
        if rel == 0:
            for s in range(z.grp):
                rows = pick[s * z.per_grp:(s + 1) * z.per_grp, :]
                outs[z.grp + s][...] = dot(rows, features_ref[...]).astype(BF16)


def picks_kernel(z, me_ref, table_ref, *outs):
    asked = asked_rows(z, me_ref, table_ref[...])
    for k in range(1, z.zz):
        for rel in range(2):
            outs[k - 1][rel] = pick_of_source(z, me_ref, asked, k, rel)


def select_kernel(z, pick_ref, own_ref, other_ref, *outs):
    for rel, part in enumerate((own_ref, other_ref)):
        got = dot(pick_ref[rel], part[...]).astype(BF16)
        for s in range(z.grp):
            outs[s][rel] = got[s * z.per_grp:(s + 1) * z.per_grp, :]


def place_kernel(z, me_ref, table_ref, pick_ref, back_ref):
    shape = (z.rows, z.rows)

    @pl.loop(0, z.dom)
    def _(n):
        k = (me_ref[1] - (n >> 1)) & (z.zz - 1)
        slot = table_ref[pl.ds(((n & 1) * z.zz + k) * 2 + 1, 1), :]
        at = slot >> log2(z.piece)
        zz = (me_ref[1] - (at >> 1)) & (z.zz - 1)
        at = zz * 2 + ((at & 1) ^ me_ref[2])
        slot = at * z.piece + (slot & (z.piece - 1))
        back_ref[n] = one_hot(iota(shape, 0) == slot)
        pick_ref[n] = one_hot(iota(shape, 1) == column(slot))


def turn_kernel(vals_ref, out_ref):
    tiles, blocks, tile, _ = vals_ref.shape

    @pl.loop(0, tiles)
    def _(t):
        for k in range(blocks):
            out_ref[t, k] = vals_ref[t, k].T


def layer_kernel(z, packed, cols_ref, pick_ref, back_ref, *refs):
    count = 1 if packed else z.zz * z.grp
    y_refs, refs = refs[:count], refs[count:]
    vals_a, vals_b, turned_a, turned_b, cot_a, cot_b, hidden_a, hidden_b = refs[:8]
    partial_refs, (panel, total) = refs[8:-2], refs[-2:]
    rows, blocks, tile = z.rows, vals_a.shape[1], vals_a.shape[2]
    half = cot_a.shape[1]

    def held_of(n):
        if packed:
            return y_refs[0][n]
        return jnp.concatenate(
            [
                y_refs[k * z.grp + s][rel, pl.ds(pl.multiple_of(n * z.pair, z.pair), z.pair), :]
                for k in range(z.zz)
                for rel in range(2)
                for s in range(z.grp)
            ],
            axis=0,
        )

    panel[pl.ds(z.dom * rows, tile), :] = jnp.zeros((tile, half), BF16)

    @pl.loop(0, z.dom)
    def _(n):
        at = pl.multiple_of(n * rows, rows)
        panel[pl.ds(at, rows), :] = dot(pick_ref[n], held_of(n)).astype(BF16)
        total[pl.ds(at, rows), :] = jnp.zeros((rows, half), F32)

    for side, (vals, turned, cot, hidden) in enumerate(
        ((vals_a, turned_a, cot_a, hidden_a), (vals_b, turned_b, cot_b, hidden_b))
    ):
        @pl.loop(0, z.tiles)
        def _(t):
            at = pl.multiple_of(t * tile, tile)
            starts = [
                pl.multiple_of(cols_ref[side * z.tiles + t, k] * tile, tile) for k in range(blocks)
            ]
            left = jnp.concatenate([vals[t, k] for k in range(blocks)], axis=1)
            right = jnp.concatenate([panel[pl.ds(s, tile), :] for s in starts], axis=0)
            agg = dot(left, right)
            sig = jax.nn.sigmoid(agg)
            hidden[pl.ds(at, tile), :] = (agg * sig).astype(BF16)
            slope = sig * (1.0 + agg * (1.0 - sig))
            grad = (cot[pl.ds(at, tile), :].astype(F32) * slope).astype(BF16)
            for k in range(blocks):
                total[pl.ds(starts[k], tile), :] += dot(turned[t, k], grad)

    @pl.loop(0, z.dom)
    def _(n):
        at = pl.multiple_of(n * rows, rows)
        back = dot(back_ref[n], total[pl.ds(at, rows), :].astype(BF16)).astype(BF16)
        for p in range(z.dom):
            partial_refs[p][n] = back[p * z.piece:(p + 1) * z.piece, :]


def grad_kernel(z, me_ref, left_a, left_b, mine_a, mine_b, come_a, come_b, *refs):
    outs, whole = refs[:-1], refs[-1]
    grad_a = (mine_a[...].astype(F32) + come_a[...].astype(F32)).astype(BF16)
    grad_b = (mine_b[...].astype(F32) + come_b[...].astype(F32)).astype(BF16)
    grad_b = jnp.concatenate(
        [grad_b[(n ^ 1) * z.piece:((n ^ 1) + 1) * z.piece, :] for n in range(z.dom)], axis=0
    )
    whole[...] = (dot(left_a[...], grad_a) + dot(left_b[...], grad_b)).astype(BF16)
    share = whole.shape[0] // z.grp
    for s in range(z.grp):
        at = pl.multiple_of((me_ref[0] ^ s) * share, share)
        outs[s][...] = whole[pl.ds(at, share), :]


def sum_kernel(*refs):
    refs[-1][...] = sum(term[...].astype(F32) for term in refs[:-1]).astype(BF16)


def last_kernel(z, me_ref, *refs):
    pieces, out = refs[:-1], refs[-1]
    share, half = pieces[0].shape
    for rel in range(2):
        left = pl.multiple_of((me_ref[2] ^ rel) * half, half)
        for s in range(z.grp):
            at = pl.multiple_of((me_ref[0] ^ s) * share, share)
            out[pl.ds(at, share), pl.ds(left, half)] = pieces[rel * z.grp + s][...].astype(F32)


def shards(features, node_order, block_cols, block_count, block_vals, weight, cotangent):
    rows, width_in = features.shape
    hidden_units = weight.shape[1]
    half = hidden_units // 2
    tiles, blocks, tile = block_vals.shape[0], block_vals.shape[1], block_vals.shape[-1]
    z = Sizes(rows, tiles)
    at_grp, at_zz, core = lax.axis_index("grp"), lax.axis_index("zz"), lax.axis_index("core")
    me = jnp.stack([at_grp, at_zz, core]).astype(I32)

    def to_core(x):
        return lax.ppermute(x, "core", [(0, 1), (1, 0)])

    def to_grp(x, s):
        return lax.ppermute(x, "grp", [(i, i ^ s) for i in range(z.grp)]) if s else x

    def to_zz(x, k):
        return lax.ppermute(x, "zz", [(i, (i + k) % z.zz) for i in range(z.zz)]) if k else x

    (index,) = call(
        lambda *refs: index_kernel(z, *refs),
        [((2, rows), I32)],
        [("s", me), ("v", node_order.reshape(1, rows))],
        "index", 24, 1,
    )
    domain = jnp.concatenate([to_zz(index, k) for k in range(z.zz)], axis=0)
    features, domain = lax.optimization_barrier((features, domain))
    domain = jnp.concatenate([domain, to_core(domain)], axis=0)
    table = jnp.concatenate([to_grp(domain, s) for s in range(z.grp)], axis=0)

    own, other = call(
        lambda *refs: product_kernel(z, *refs),
        [((rows, half), BF16)] * 2,
        [("s", me), ("v", features), ("v", weight)],
        "product", 16, 1.5,
    )
    ring = [[own, to_core(other)]]
    for k in range(1, z.zz):
        ring.append([to_zz(part, 1) for part in ring[-1]])

    vals_b = to_core(block_vals)
    cot_a = lax.dynamic_slice_in_dim(cotangent, core * half, half, axis=1)
    cot_b = to_core(lax.dynamic_slice_in_dim(cotangent, (1 - core) * half, half, axis=1))
    cols_a = jnp.where(iota((tiles, blocks), 1) < block_count[:, None], block_cols, -1)
    cols = jnp.concatenate([cols_a, to_core(cols_a)], axis=0)
    dev = cols >> log2(tiles)
    cols = jnp.where(cols < 0, z.dom * tiles, (dev ^ core) * tiles + (cols & (tiles - 1)))

    pieces = [((2, z.per_grp, half), BF16)] * z.grp
    got = call(
        lambda *refs: select_own_kernel(z, *refs),
        pieces + [((z.per_grp, width_in), BF16)] * z.grp,
        [("s", me), ("v", table), ("v", ring[0][0]), ("v", ring[0][1]), ("v", features)],
        "select_own", 24, 2.5,
    )
    y = [to_grp(got[s], s) for s in range(z.grp)]
    held = jnp.stack([to_grp(got[z.grp + s], s) for s in range(z.grp)])
    held = held.reshape(z.grp, z.dom, z.pair, width_in).transpose(3, 1, 0, 2).reshape(width_in, rows)
    held_b = to_core(held)
    picks = call(
        lambda *refs: picks_kernel(z, *refs),
        [((2, rows, rows), BF16)] * (z.zz - 1),
        [("s", me), ("v", table)],
        "picks", 24, 4,
    )
    for k in range(1, z.zz):
        got = call(
            lambda *refs: select_kernel(z, *refs), pieces,
            [("v", picks[k - 1]), ("v", ring[k][0]), ("v", ring[k][1])],
            "select", 16, 0.7,
        )
        y += [to_grp(got[s], s) for s in range(z.grp)]

    pick, back = call(
        lambda *refs: place_kernel(z, *refs),
        [((z.dom, rows, rows), BF16)] * 2,
        [("s", me), ("v", domain)],
        "place", 24, 6,
    )
    turned_a, turned_b = (
        call(turn_kernel, [(block_vals.shape, BF16)], [("v", vals)], "turn", 16, 3)[0]
        for vals in (block_vals, vals_b)
    )

    packed = z.pair % 16 != 0
    if packed:
        y = jnp.stack(y).reshape(z.zz, z.grp, 2, z.dom, z.pair, half)
        y = [y.transpose(3, 0, 2, 1, 4, 5).reshape(z.dom, rows, half)]
    layer = call(
        lambda *refs: layer_kernel(z, packed, *refs),
        [((rows, half), BF16)] * 2 + [((z.dom, z.piece, half), BF16)] * z.dom,
        [("s", cols), ("v", pick), ("v", back)]
        + [("v", part) for part in y]
        + [("v", block_vals), ("v", vals_b), ("v", turned_a), ("v", turned_b)]
        + [("v", cot_a), ("v", cot_b)],
        "layer", 36, 10,
        (pltpu.VMEM((z.dom * rows + tile, half), BF16), pltpu.VMEM((z.dom * rows + tile, half), F32)),
    )
    hidden_a, hidden_b, partial = layer[0], layer[1], layer[2:]

    come = to_core(hidden_b)
    came = [partial[2 * (z.zz - 1) + rel] for rel in range(2)]
    for k in range(z.zz - 2, -1, -1):
        came = [to_zz(part, -1) for part in came]
        if k:
            came = [
                (part.astype(F32) + partial[2 * k + rel].astype(F32)).astype(BF16)
                for rel, part in enumerate(came)
            ]
        if k == 1:
            came, come, held_b = lax.optimization_barrier((came, come, held_b))

    first = core == 0
    hidden = jnp.concatenate(
        [jnp.where(first, hidden_a, come), jnp.where(first, come, hidden_a)], axis=1
    )

    share = width_in // z.grp
    terms = call(
        lambda *refs: grad_kernel(z, *refs),
        [((share, half), BF16)] * z.grp,
        [("s", me), ("v", held), ("v", held_b)]
        + [("v", part.reshape(rows, half)) for part in (partial[0], partial[1], came[0], came[1])],
        "grad", 16, 1.5,
        (pltpu.VMEM((width_in, half), BF16),),
    )

    def total_of(parts):
        return call(
            sum_kernel, [((share, half), BF16)], [("v", part) for part in parts], "sum", 16, 0.5
        )[0]

    mine = total_of([to_grp(terms[s], s) for s in range(z.grp)])
    step = 1
    while step < z.zz:
        mine = total_of(
            [mine, lax.ppermute(mine, "zz", [(i, i ^ step) for i in range(z.zz)])]
        )
        step *= 2
    mine = [to_grp(mine, s) for s in range(z.grp)]
    (grad_weight,) = call(
        lambda *refs: last_kernel(z, *refs),
        [((width_in, hidden_units), F32)],
        [("s", me)] + [("v", part) for part in mine + [to_core(part) for part in mine]],
        "last", 16, 2,
    )
    return hidden, grad_weight


def solution(mesh):
    n_grp, n_dom = mesh.shape["grp"], mesh.shape["dom"]
    split = Mesh(mesh.devices.reshape(n_grp, n_dom // 2, 2), ("grp", "zz", "core"))
    by_rows = ("grp", "zz", "core")
    placed = (
        P(by_rows, None),
        P(by_rows),
        P(by_rows, None),
        P(by_rows),
        P(by_rows, None, None, None),
        P(),
        P(by_rows, None),
    )
    return jax.shard_map(
        shards,
        mesh=split,
        in_specs=placed,
        out_specs=(P(by_rows, None), P()),
        check_vma=False,
    )
```

time: 182 us -> 168 us (0.923)
  starting transfers between devices: 79.7 us -> 57.6 us
  waiting for transfers between devices: 60.8 us -> 70.2 us
    ppermute x24 -> x15, starting transfers between devices: 45.4 us -> 21.6 us  [to_zz(): lax.ppermute(x, 'zz', [(i, (i + k) % z.zz) for i in range(z.zz)])]
    ppermute x0 -> x2, waiting for transfers between devices: none -> 10.2 us  [shards(): lax.ppermute(mine, 'zz', [(i, i ^ step) for i in range(z.zz)])]
    ppermute x0 -> x2, starting transfers between devices: none -> 2.34 us  [shards(): lax.ppermute(mine, 'zz', [(i, i ^ step) for i in range(z.zz)])]
    ppermute x24 -> x15, waiting for transfers between devices: 36.1 us -> 35.6 us  [to_zz(): lax.ppermute(x, 'zz', [(i, (i + k) % z.zz) for i in range(z.zz)])]
    pallas_call x10 -> x16, Pallas kernels: 31.1 us -> 30.6 us  [call(): pl.pallas_call(body, out_shape=tuple((jax.ShapeDtypeStruct(s, d) for s, d...]
  transfers between devices with their start and end apart: 60 -> 52, of which waited for: 29 -> 25; matrix products, arithmetic and copies ran while one was open for 3% -> 4% of each run, Pallas kernels for 14% -> 16%
where the time goes in v2:
time: 168 us; the launch traced here: 167 us
  waiting for transfers between devices  70.2 us (42%)
  starting transfers between devices  57.6 us (34%)
  Pallas kernels  30.6 us (18%)
  local copies, waits for them, and re-layouts  4.52 us (3%)
  other arithmetic  3.37 us (2%)
    ppermute x15, waiting for transfers between devices, to_zz(): lax.ppermute(x, 'zz', [(i, (i + k) % z.zz) for i in range(z.zz)])  35.6 us
    ppermute x24, starting transfers between devices, to_grp(): lax.ppermute(x, 'grp', [(i, i ^ s) for i in range(z.grp)])  32.2 us
    pallas_call x16, Pallas kernels, call(): pl.pallas_call(body, out_shape=tuple((jax.ShapeDtypeStruct(s, d) for s, d...  30.6 us
    ppermute x24, waiting for transfers between devices, to_grp(): lax.ppermute(x, 'grp', [(i, i ^ s) for i in range(z.grp)])  23.1 us
    ppermute x15, starting transfers between devices, to_zz(): lax.ppermute(x, 'zz', [(i, (i + k) % z.zz) for i in range(z.zz)])  21.6 us
    ppermute x2, waiting for transfers between devices, shards(): lax.ppermute(mine, 'zz', [(i, i ^ step) for i in range(z.zz)])  10.2 us
  transfers between devices with their start and end apart: 52, of which 25 were waited for; matrix products, arithmetic and copies ran while one was open for 4% of the time, Pallas kernels for 16%

profile of v2, /device:TPU:0, one launch (start us, length us, event | category | flops | bytes accessed | tf_op | source)
XLA Modules:
  0.0 167.3 jit_solution(12119974779938290799)
XLA Ops:
  2.4 3.1 %collective-permute-start.1 = (s32[2,512]{1,0:T(2,128)S(1)}, s32[2,512]{1,0:T(2,128)S(1)}, u32[]{:S(2)}, u32[]{:S(2)}) collective-permute-start(s32[2,512]{1,0:T(2,128)S(1)} %index.1), channel_id=1, source_target_pairs={{0,2},{2,4},{4,6},{6,0},{1,3},{3,5},{5,7},{7,1},{8,10},{10,12},{12... | collective-permute-start | bytes 12296 | tf_op jit(solution)/shard_map/ppermute | solution.py:259
  5.5 2.6 %collective-permute-start.2 = (s32[2,512]{1,0:T(2,128)S(1)}, s32[2,512]{1,0:T(2,128)S(1)}, u32[]{:S(2)}, u32[]{:S(2)}) collective-permute-start(s32[2,512]{1,0:T(2,128)S(1)} %index.1), channel_id=1, source_target_pairs={{0,4},{2,6},{4,0},{6,2},{1,5},{3,7},{5,1},{7,3},{8,12},{10,14},{12... | collective-permute-start | bytes 12296 | tf_op jit(solution)/shard_map/ppermute | solution.py:259
  8.1 1.3 collective-permute-start.3
  17.0 1.5 collective-permute-start.5
  19.5 1.4 collective-permute-done.5
  20.9 1.5 collective-permute-start.6
  22.4 2.4 %collective-permute-done.6 = s32[16,512]{1,0:T(8,128)S(1)} collective-permute-done((s32[16,512]{1,0:T(8,128)S(1)}, s32[16,512]{1,0:T(8,128)S(1)}, u32[]{:S(2)}, u32[]{:S(2)}) %collective-permute-start.6) | collective-permute-done | bytes 32800 | tf_op jit(solution)/shard_map/ppermute | solution.py:256
  24.8 2.5 %collective-permute-start.7 = (s32[16,512]{1,0:T(8,128)S(1)}, s32[16,512]{1,0:T(8,128)S(1)}, u32[]{:S(2)}, u32[]{:S(2)}) collective-permute-start(s32[16,512]{1,0:T(8,128)S(1)} %get-tuple-element.101.refs_1_), channel_id=1, source_target_pairs={{0,24},{8,16},{16,8},{24,0},{1,25},{9,17},{17,9},{25,1},{2,26},{10... | collective-permute-start | bytes 98312 | tf_op jit(solution)/shard_map/ppermute | solution.py:256
  28.2 4.8 %collective-permute-done.13.refs_2_ = bf16[512,256]{1,0:T(8,128)(2,1)S(1)} collective-permute-done((bf16[512,256]{1,0:T(8,128)(2,1)S(1)}, bf16[512,256]{1,0:T(8,128)(2,1)S(1)}, u32[]{:S(2)}, u32[]{:S(2)}) %collective-permute-start.13) | collective-permute-done | bytes 262176 | tf_op jit(solution)/shard_map/ppermute | solution.py:259
  33.0 2.3 %select_own.1 = (bf16[2,128,256]{2,1,0:T(8,128)(2,1)S(1)}, bf16[2,128,256]{2,1,0:T(8,128)(2,1)S(1)}, bf16[2,128,256]{2,1,0:T(8,128)(2,1)S(1)}, bf16[2,128,256]{2...) custom-call(s32[3]{0:T(128)S(1)} %pad_add_fusion.2.refs_0_, ...), custom_call_target="tpu_custom_call" | custom-call | flops 2500000000 | tf_op jit(solution)/shard_map/select_own/pallas_call | solution.py:37
  35.3 1.6 collective-permute-start.10
  36.9 1.7 %collective-permute-done.17.refs_1_ = bf16[512,256]{1,0:T(8,128)(2,1)S(1)} collective-permute-done((bf16[512,256]{1,0:T(8,128)(2,1)S(1)}, bf16[512,256]{1,0:T(8,128)(2,1)S(1)}, u32[]{:S(2)}, u32[]{:S(2)}) %collective-permute-start.17) | collective-permute-done | bytes 262176 | tf_op jit(solution)/shard_map/ppermute | solution.py:259
  38.6 5.6 %collective-permute-done.18.refs_2_ = bf16[512,256]{1,0:T(8,128)(2,1)S(1)} collective-permute-done((bf16[512,256]{1,0:T(8,128)(2,1)S(1)}, bf16[512,256]{1,0:T(8,128)(2,1)S(1)}, u32[]{:S(2)}, u32[]{:S(2)}) %collective-permute-start.18) | collective-permute-done | bytes 262176 | tf_op jit(solution)/shard_map/ppermute | solution.py:259
  44.2 2.4 %picks.1 = (bf16[2,512,512]{2,1,0:T(8,128)(2,1)S(1)}, bf16[2,512,512]{2,1,0:T(8,128)(2,1)S(1)}, bf16[2,512,512]{2,1,0:T(8,128)(2,1)S(1)}) custom-call(s32[3]{0:T(128)S(1)} %pad_add_fusion.2.refs_0_, s32[64,512]{1,0:T(8,128)S(1)} %constant_dynamic-update-slice_fusion.2.refs_1_), custom_call_target="tpu_custom_call" | custom-call | flops 4000000000 | tf_op jit(solution)/shard_map/picks/pallas_call | solution.py:37
  46.7 2.5 %collective-permute-start.11 = (bf16[2,128,256]{2,1,0:T(8,128)(2,1)S(1)}, bf16[2,128,256]{2,1,0:T(8,128)(2,1)S(1)}, u32[]{:S(2)}, u32[]{:S(2)}) collective-permute-start(bf16[2,128,256]{2,1,0:T(8,128)(2,1)S(1)} %get-tuple-element.58), channel_id=1, source_target_pairs={{0,24},{8,16},{16,8},{24,0},{1,25},{9,17},{17,9},{25,1},{2,26},{10... | collective-permute-start | bytes 393224 | tf_op jit(solution)/shard_map/ppermute | solution.py:256
  50.6 2.8 %collective-permute-done.11.refs_6_ = bf16[2,128,256]{2,1,0:T(8,128)(2,1)S(1)} collective-permute-done((bf16[2,128,256]{2,1,0:T(8,128)(2,1)S(1)}, bf16[2,128,256]{2,1,0:T(8,128)(2,1)S(1)}, u32[]{:S(2)}, u32[]{:S(2)}) %collective-permute-start.11) | collective-permute-done | bytes 131104 | tf_op jit(solution)/shard_map/ppermute | solution.py:256
  53.4 1.5 collective-permute-start.14
  54.9 1.4 collective-permute-done.9.refs_4_
  56.6 2.7 %collective-permute-start.16 = (bf16[2,128,256]{2,1,0:T(8,128)(2,1)S(1)}, bf16[2,128,256]{2,1,0:T(8,128)(2,1)S(1)}, u32[]{:S(2)}, u32[]{:S(2)}) collective-permute-start(bf16[2,128,256]{2,1,0:T(8,128)(2,1)S(1)} %get-tuple-element.63), channel_id=1, source_target_pairs={{0,24},{8,16},{16,8},{24,0},{1,25},{9,17},{17,9},{25,1},{2,26},{10... | collective-permute-start | bytes 393224 | tf_op jit(solution)/shard_map/ppermute | solution.py:256
  59.8 2.4 %place.1 = (bf16[8,512,512]{2,1,0:T(8,128)(2,1)S(1)}, bf16[8,512,512]{2,1,0:T(8,128)(2,1)S(1)}) custom-call(s32[3]{0:T(128)S(1)} %pad_add_fusion.2.refs_0_, s32[16,512]{1,0:T(8,128)S(1)} %get-tuple-element.101.refs_1_), custom_call_target="tpu_custom_call" | custom-call | flops 6000000000 | tf_op jit(solution)/shard_map/place/pallas_call | solution.py:37
  63.0 2.7 %collective-permute-start.21 = (bf16[2,128,256]{2,1,0:T(8,128)(2,1)S(1)}, bf16[2,128,256]{2,1,0:T(8,128)(2,1)S(1)}, u32[]{:S(2)}, u32[]{:S(2)}) collective-permute-start(bf16[2,128,256]{2,1,0:T(8,128)(2,1)S(1)} %get-tuple-element.68), channel_id=1, source_target_pairs={{0,24},{8,16},{16,8},{24,0},{1,25},{9,17},{17,9},{25,1},{2,26},{10... | collective-permute-start | bytes 393224 | tf_op jit(solution)/shard_map/ppermute | solution.py:256
  66.5 2.7 %collective-permute-start.26 = (bf16[2,128,256]{2,1,0:T(8,128)(2,1)S(1)}, bf16[2,128,256]{2,1,0:T(8,128)(2,1)S(1)}, u32[]{:S(2)}, u32[]{:S(2)}) collective-permute-start(bf16[2,128,256]{2,1,0:T(8,128)(2,1)S(1)} %get-tuple-element.73), channel_id=1, source_target_pairs={{0,24},{8,16},{16,8},{24,0},{1,25},{9,17},{17,9},{25,1},{2,26},{10... | collective-permute-start | bytes 393224 | tf_op jit(solution)/shard_map/ppermute | solution.py:256
  69.9 6.2 %collective-permute-done.20.refs_13_ = bf16[2,128,256]{2,1,0:T(8,128)(2,1)S(1)} collective-permute-done((bf16[2,128,256]{2,1,0:T(8,128)(2,1)S(1)}, bf16[2,128,256]{2,1,0:T(8,128)(2,1)S(1)}, u32[]{:S(2)}, u32[]{:S(2)}) %collective-permute-start.20) | collective-permute-done | bytes 131104 | tf_op jit(solution)/shard_map/ppermute | solution.py:256
  77.7 2.0 %collective-permute-start.35 = (bf16[128,1024]{1,0:T(8,128)(2,1)S(1)}, bf16[128,1024]{1,0:T(8,128)(2,1)S(1)}, u32[]{:S(2)}, u32[]{:S(2)}) collective-permute-start(bf16[128,1024]{1,0:T(8,128)(2,1)S(1)} %get-tuple-element.84), channel_id=1, source_target_pairs={{0,16},{8,24},{16,0},{24,8},{1,17},{9,25},{17,1},{25,9},{2,18},{10... | collective-permute-start | bytes 786440 | tf_op jit(solution)/shard_map/ppermute | solution.py:256
  79.7 15.0 %layer.1 = (bf16[512,256]{1,0:T(8,128)(2,1)S(1)}, bf16[512,256]{1,0:T(8,128)(2,1)S(1)}, bf16[8,64,256]{2,1,0:T(8,128)(2,1)S(1)}, bf16[8,64,256]{2,1,0:T(8,128)(2...) custom-call(s32[8,16]{1,0:T(8,128)S(1)} %add_select_fusion.refs_0_, ...), custom_call_target="tpu_custom_call" | custom-call | flops 10000000000 | tf_op jit(solution)/shard_map/layer/pallas_call | solution.py:37
  94.7 2.8 %collective-permute-start.31 = (bf16[8,64,256]{2,1,0:T(8,128)(2,1)S(1)}, bf16[8,64,256]{2,1,0:T(8,128)(2,1)}, u32[]{:S(2)}, u32[]{:S(2)}) collective-permute-start(bf16[8,64,256]{2,1,0:T(8,128)(2,1)S(1)} %get-tuple-element.78), channel_id=1, source_target_pairs={{0,6},{2,0},{4,2},{6,4},{1,7},{3,1},{5,3},{7,5},{8,14},{10,8},{12,... | collective-permute-start | bytes 786440 | tf_op jit(solution)/shard_map/ppermute | solution.py:259
  98.7 1.5 copy.17.refs_1_
  102.7 4.6 %collective-permute-start.32 = (bf16[8,64,256]{2,1,0:T(8,128)(2,1)S(1)}, bf16[8,64,256]{2,1,0:T(8,128)(2,1)S(1)}, u32[]{:S(2)}, u32[]{:S(2)}) collective-permute-start(bf16[8,64,256]{2,1,0:T(8,128)(2,1)S(1)} %add_convert_fusion.1), channel_id=1, source_target_pairs={{0,6},{2,0},{4,2},{6,4},{1,7},{3,1},{5,3},{7,5},{8,14},{10,8},{12,... | collective-permute-start | bytes 786440 | tf_op jit(solution)/shard_map/ppermute | solution.py:259
  107.3 2.1 %collective-permute-done.29 = bf16[8,64,256]{2,1,0:T(8,128)(2,1)S(1)} collective-permute-done((bf16[8,64,256]{2,1,0:T(8,128)(2,1)S(1)}, bf16[8,64,256]{2,1,0:T(8,128)(2,1)S(1)}, u32[]{:S(2)}, u32[]{:S(2)}) %collective-permute-start.29) | collective-permute-done | bytes 262176 | tf_op jit(solution)/shard_map/ppermute | solution.py:259
  109.5 2.2 %collective-permute-start.30 = (bf16[8,64,256]{2,1,0:T(8,128)(2,1)S(1)}, bf16[8,64,256]{2,1,0:T(8,128)(2,1)S(1)}, u32[]{:S(2)}, u32[]{:S(2)}) collective-permute-start(bf16[8,64,256]{2,1,0:T(8,128)(2,1)S(1)} %add_convert_fusion.3), channel_id=1, source_target_pairs={{0,6},{2,0},{4,2},{6,4},{1,7},{3,1},{5,3},{7,5},{8,14},{10,8},{12,... | collective-permute-start | bytes 786440 | tf_op jit(solution)/shard_map/ppermute | solution.py:259
  111.7 3.4 %collective-permute-done.32 = bf16[8,64,256]{2,1,0:T(8,128)(2,1)S(1)} collective-permute-done((bf16[8,64,256]{2,1,0:T(8,128)(2,1)S(1)}, bf16[8,64,256]{2,1,0:T(8,128)(2,1)S(1)}, u32[]{:S(2)}, u32[]{:S(2)}) %collective-permute-start.32) | collective-permute-done | bytes 262176 | tf_op jit(solution)/shard_map/ppermute | solution.py:259
  115.1 5.1 %collective-permute-done.30 = bf16[8,64,256]{2,1,0:T(8,128)(2,1)S(1)} collective-permute-done((bf16[8,64,256]{2,1,0:T(8,128)(2,1)S(1)}, bf16[8,64,256]{2,1,0:T(8,128)(2,1)S(1)}, u32[]{:S(2)}, u32[]{:S(2)}) %collective-permute-start.30) | collective-permute-done | bytes 262176 | tf_op jit(solution)/shard_map/ppermute | solution.py:259
  120.3 2.4 %collective-permute-start.38 = (bf16[8,64,256]{2,1,0:T(8,128)(2,1)S(1)}, bf16[8,64,256]{2,1,0:T(8,128)(2,1)S(1)}, u32[]{:S(2)}, u32[]{:S(2)}) collective-permute-start(bf16[8,64,256]{2,1,0:T(8,128)(2,1)S(1)} %add_convert_fusion.2), channel_id=1, source_target_pairs={{0,6},{2,0},{4,2},{6,4},{1,7},{3,1},{5,3},{7,5},{8,14},{10,8},{12,... | collective-permute-start | bytes 786440 | tf_op jit(solution)/shard_map/ppermute | solution.py:259
  122.8 6.8 %collective-permute-done.38 = bf16[8,64,256]{2,1,0:T(8,128)(2,1)S(1)} collective-permute-done((bf16[8,64,256]{2,1,0:T(8,128)(2,1)S(1)}, bf16[8,64,256]{2,1,0:T(8,128)(2,1)S(1)}, u32[]{:S(2)}, u32[]{:S(2)}) %collective-permute-start.38) | collective-permute-done | bytes 262176 | tf_op jit(solution)/shard_map/ppermute | solution.py:259
  129.6 4.3 %collective-permute-done.39 = bf16[8,64,256]{2,1,0:T(8,128)(2,1)S(1)} collective-permute-done((bf16[8,64,256]{2,1,0:T(8,128)(2,1)S(1)}, bf16[8,64,256]{2,1,0:T(8,128)(2,1)S(1)}, u32[]{:S(2)}, u32[]{:S(2)}) %collective-permute-start.39) | collective-permute-done | bytes 262176 | tf_op jit(solution)/shard_map/ppermute | solution.py:259
  133.9 1.3 grad.1
  135.2 1.6 collective-permute-start.40
  136.7 2.0 %collective-permute-start.42 = (bf16[256,256]{1,0:T(8,128)(2,1)S(1)}, bf16[256,256]{1,0:T(8,128)(2,1)S(1)}, u32[]{:S(2)}, u32[]{:S(2)}) collective-permute-start(bf16[256,256]{1,0:T(8,128)(2,1)S(1)} %get-tuple-element.95), channel_id=1, source_target_pairs={{0,24},{8,16},{16,8},{24,0},{1,25},{9,17},{17,9},{25,1},{2,26},{10... | collective-permute-start | bytes 393224 | tf_op jit(solution)/shard_map/ppermute | solution.py:256
  138.7 2.7 %collective-permute-done.40.refs_1_ = bf16[256,256]{1,0:T(8,128)(2,1)S(1)} collective-permute-done((bf16[256,256]{1,0:T(8,128)(2,1)S(1)}, bf16[256,256]{1,0:T(8,128)(2,1)S(1)}, u32[]{:S(2)}, u32[]{:S(2)}) %collective-permute-start.40) | collective-permute-done | bytes 131104 | tf_op jit(solution)/shard_map/ppermute | solution.py:256
  141.4 2.3 %collective-permute-done.41.refs_2_ = bf16[256,256]{1,0:T(8,128)(2,1)S(1)} collective-permute-done((bf16[256,256]{1,0:T(8,128)(2,1)S(1)}, bf16[256,256]{1,0:T(8,128)(2,1)S(1)}, u32[]{:S(2)}, u32[]{:S(2)}) %collective-permute-start.41) | collective-permute-done | bytes 131104 | tf_op jit(solution)/shard_map/ppermute | solution.py:256
  143.8 5.5 %collective-permute-done.43.refs_1_ = bf16[256,256]{1,0:T(8,128)(2,1)S(1)} collective-permute-done((bf16[256,256]{1,0:T(8,128)(2,1)S(1)}, bf16[256,256]{1,0:T(8,128)(2,1)S(1)}, u32[]{:S(2)}, u32[]{:S(2)}) %collective-permute-start.43) | collective-permute-done | bytes 131104 | tf_op jit(solution)/shard_map/ppermute | solution.py:378
  149.3 2.3 %collective-permute-start.44 = (bf16[256,256]{1,0:T(8,128)(2,1)S(1)}, bf16[256,256]{1,0:T(8,128)(2,1)S(1)}, u32[]{:S(2)}, u32[]{:S(2)}) collective-permute-start(bf16[256,256]{1,0:T(8,128)(2,1)S(1)} %sum.4.refs_0_), channel_id=1, source_target_pairs={{0,4},{2,6},{4,0},{6,2},{1,5},{3,7},{5,1},{7,3},{8,12},{10,14},{12... | collective-permute-start | bytes 393224 | tf_op jit(solution)/shard_map/ppermute | solution.py:378
  151.6 4.7 %collective-permute-done.44.refs_1_ = bf16[256,256]{1,0:T(8,128)(2,1)S(1)} collective-permute-done((bf16[256,256]{1,0:T(8,128)(2,1)S(1)}, bf16[256,256]{1,0:T(8,128)(2,1)S(1)}, u32[]{:S(2)}, u32[]{:S(2)}) %collective-permute-start.44) | collective-permute-done | bytes 131104 | tf_op jit(solution)/shard_map/ppermute | solution.py:378
  156.8 1.3 collective-permute-start.46
  158.1 1.8 %collective-permute-start.47 = (bf16[256,256]{1,0:T(8,128)(2,1)S(1)}, bf16[256,256]{1,0:T(8,128)(2,1)S(1)}, u32[]{:S(2)}, u32[]{:S(2)}) collective-permute-start(bf16[256,256]{1,0:T(8,128)(2,1)S(1)} %sum.5.refs_1_), channel_id=1, source_target_pairs={{0,24},{8,16},{16,8},{24,0},{1,25},{9,17},{17,9},{25,1},{2,26},{10... | collective-permute-start | bytes 393224 | tf_op jit(solution)/shard_map/ppermute | solution.py:256
  159.9 1.5 collective-permute-done.45.refs_2_
  161.9 2.1 %collective-permute-done.47.refs_4_ = bf16[256,256]{1,0:T(8,128)(2,1)S(1)} collective-permute-done((bf16[256,256]{1,0:T(8,128)(2,1)S(1)}, bf16[256,256]{1,0:T(8,128)(2,1)S(1)}, u32[]{:S(2)}, u32[]{:S(2)}) %collective-permute-start.47) | collective-permute-done | bytes 131104 | tf_op jit(solution)/shard_map/ppermute | solution.py:256
  165.3 2.0 %last.1 = f32[1024,512]{1,0:T(8,128)} custom-call(s32[3]{0:T(128)S(1)} %pad_add_fusion.2.refs_0_, bf16[256,256]{1,0:T(8,128)(2,1)S(1)} %sum.5.refs_1_, bf16[256,256]{1,0:T(8,128)(2,1)S(1)} %collective-permute-done.45.refs_2_, bf16[256,256]{1,0:T(8,128)(2,1)S(1)} %collective-permute-done.46.refs_3_, bf16[256,256]{1,0:T(8,128)(2,1)S(1)} %collective-permute-done.47.refs_4_, ...), custom_call_target="tpu_custom_call" | custom-call | flops 2000000000 | tf_op jit(solution)/shard_map/last/pallas_call | solution.py:37
  (112 shorter events, 23.6 us)
Async XLA Ops:
  2.4 8.7 %collective-permute-start.1 = (s32[2,512]{1,0:T(2,128)S(1)}, s32[2,512]{1,0:T(2,128)S(1)}, u32[]{:S(2)}, u32[]{:S(2)}) collective-permute-start(s32[2,512]{1,0:T(2,128)S(1)} %index.1), channel_id=1, source_target_pairs={{0,2},{2,4},{4,6},{6,0},{1,3},{3,5},{5,7},{7,1},{8,10},{10,12},{12... | collective-permute-start | bytes 12296 | tf_op jit(solution)/shard_map/ppermute | solution.py:259
  5.5 5.8 %collective-permute-start.2 = (s32[2,512]{1,0:T(2,128)S(1)}, s32[2,512]{1,0:T(2,128)S(1)}, u32[]{:S(2)}, u32[]{:S(2)}) collective-permute-start(s32[2,512]{1,0:T(2,128)S(1)} %index.1), channel_id=1, source_target_pairs={{0,4},{2,6},{4,0},{6,2},{1,5},{3,7},{5,1},{7,3},{8,12},{10,14},{12... | collective-permute-start | bytes 12296 | tf_op jit(solution)/shard_map/ppermute | solution.py:259
  8.1 3.6 %collective-permute-start.3 = (s32[2,512]{1,0:T(2,128)S(1)}, s32[2,512]{1,0:T(2,128)S(1)}, u32[]{:S(2)}, u32[]{:S(2)}) collective-permute-start(s32[2,512]{1,0:T(2,128)S(1)} %index.1), channel_id=1, source_target_pairs={{0,6},{2,0},{4,2},{6,4},{1,7},{3,1},{5,3},{7,5},{8,14},{10,8},{12,... | collective-permute-start | bytes 12296 | tf_op jit(solution)/shard_map/ppermute | solution.py:259
  10.5 36.2 %collective-permute-start.28 = (bf16[512,256]{1,0:T(8,128)(2,1)S(1)}, bf16[512,256]{1,0:T(8,128)(2,1)S(1)}, u32[]{:S(2)}, u32[]{:S(2)}) collective-permute-start(bf16[512,256]{1,0:T(8,128)(2,1)S(1)} %get-tuple-element.98), channel_id=1, source_target_pairs={{0,1},{1,0},{2,3},{3,2},{4,5},{5,4},{6,7},{7,6},{8,9},{9,8},{10,11... | collective-permute-start | bytes 786440 | tf_op jit(solution)/shard_map/ppermute | solution.py:253
  10.7 6.3 %collective-permute-start = (s32[4,16]{1,0:T(4,128)S(1)}, s32[4,16]{1,0:T(4,128)S(1)}, u32[]{:S(2)}, u32[]{:S(2)}) collective-permute-start(s32[4,16]{1,0:T(4,128)S(1)} %fusion), channel_id=1, source_target_pairs={{0,1},{1,0},{2,3},{3,2},{4,5},{5,4},{6,7},{7,6},{8,9},{9,8},{10,11... | collective-permute-start | bytes 776 | tf_op jit(solution)/shard_map/ppermute | solution.py:253
  11.2 55.3 %collective-permute-start.27 = (bf16[4,16,128,128]{3,2,1,0:T(8,128)(2,1)S(1)}, bf16[4,16,128,128]{3,2,1,0:T(8,128)(2,1)S(1)}, u32[]{:S(2)}, u32[]{:S(2)}) collective-permute-start(bf16[4,16,128,128]{3,2,1,0:T(8,128)(2,1)S(1)} %copy-done), channel_id=1, source_target_pairs={{0,1},{1,0},{2,3},{3,2},{4,5},{5,4},{6,7},{7,6},{8,9},{9,8},{10,11... | collective-permute-start | bytes 6291464 | tf_op jit(solution)/shard_map/ppermute | solution.py:253
  14.2 4.3 %collective-permute-start.8 = (bf16[512,256]{1,0:T(8,128)(2,1)S(1)}, bf16[512,256]{1,0:T(8,128)(2,1)S(1)}, u32[]{:S(2)}, u32[]{:S(2)}) collective-permute-start(bf16[512,256]{1,0:T(8,128)(2,1)S(1)} %get-tuple-element.54), channel_id=1, source_target_pairs={{0,1},{1,0},{2,3},{3,2},{4,5},{5,4},{6,7},{7,6},{8,9},{9,8},{10,11... | collective-permute-start | bytes 786440 | tf_op jit(solution)/shard_map/ppermute | solution.py:253
  16.5 10.9 %collective-permute-start.12 = (bf16[512,256]{1,0:T(8,128)(2,1)S(1)}, bf16[512,256]{1,0:T(8,128)(2,1)S(1)}, u32[]{:S(2)}, u32[]{:S(2)}) collective-permute-start(bf16[512,256]{1,0:T(8,128)(2,1)S(1)} %get-tuple-element.53.refs_2_), channel_id=1, source_target_pairs={{0,2},{2,4},{4,6},{6,0},{1,3},{3,5},{5,7},{7,1},{8,10},{10,12},{12... | collective-permute-start | bytes 786440 | tf_op jit(solution)/shard_map/ppermute | solution.py:259
  17.0 3.9 %collective-permute-start.5 = (s32[16,512]{1,0:T(8,128)S(1)}, s32[16,512]{1,0:T(8,128)S(1)}, u32[]{:S(2)}, u32[]{:S(2)}) collective-permute-start(s32[16,512]{1,0:T(8,128)S(1)} %get-tuple-element.101.refs_1_), channel_id=1, source_target_pairs={{0,8},{8,0},{16,24},{24,16},{1,9},{9,1},{17,25},{25,17},{2,10},{10... | collective-permute-start | bytes 98312 | tf_op jit(solution)/shard_map/ppermute | solution.py:256
  18.5 14.5 %collective-permute-start.13 = (bf16[512,256]{1,0:T(8,128)(2,1)S(1)}, bf16[512,256]{1,0:T(8,128)(2,1)S(1)}, u32[]{:S(2)}, u32[]{:S(2)}) collective-permute-start(bf16[512,256]{1,0:T(8,128)(2,1)S(1)} %collective-permute-done.8.refs_3_), channel_id=1, source_target_pairs={{0,2},{2,4},{4,6},{6,0},{1,3},{3,5},{5,7},{7,1},{8,10},{10,12},{12... | collective-permute-start | bytes 786440 | tf_op jit(solution)/shard_map/ppermute | solution.py:259
  20.9 3.9 %collective-permute-start.6 = (s32[16,512]{1,0:T(8,128)S(1)}, s32[16,512]{1,0:T(8,128)S(1)}, u32[]{:S(2)}, u32[]{:S(2)}) collective-permute-start(s32[16,512]{1,0:T(8,128)S(1)} %get-tuple-element.101.refs_1_), channel_id=1, source_target_pairs={{0,16},{8,24},{16,0},{24,8},{1,17},{9,25},{17,1},{25,9},{2,18},{10... | collective-permute-start | bytes 98312 | tf_op jit(solution)/shard_map/ppermute | solution.py:256
  24.8 8.2 %collective-permute-start.7 = (s32[16,512]{1,0:T(8,128)S(1)}, s32[16,512]{1,0:T(8,128)S(1)}, u32[]{:S(2)}, u32[]{:S(2)}) collective-permute-start(s32[16,512]{1,0:T(8,128)S(1)} %get-tuple-element.101.refs_1_), channel_id=1, source_target_pairs={{0,24},{8,16},{16,8},{24,0},{1,25},{9,17},{17,9},{25,1},{2,26},{10... | collective-permute-start | bytes 98312 | tf_op jit(solution)/shard_map/ppermute | solution.py:256
  27.4 11.2 %collective-permute-start.17 = (bf16[512,256]{1,0:T(8,128)(2,1)S(1)}, bf16[512,256]{1,0:T(8,128)(2,1)S(1)}, u32[]{:S(2)}, u32[]{:S(2)}) collective-permute-start(bf16[512,256]{1,0:T(8,128)(2,1)S(1)} %collective-permute-done.12.refs_1_), channel_id=1, source_target_pairs={{0,2},{2,4},{4,6},{6,0},{1,3},{3,5},{5,7},{7,1},{8,10},{10,12},{12... | collective-permute-start | bytes 786440 | tf_op jit(solution)/shard_map/ppermute | solution.py:259
  33.0 11.2 %collective-permute-start.18 = (bf16[512,256]{1,0:T(8,128)(2,1)S(1)}, bf16[512,256]{1,0:T(8,128)(2,1)S(1)}, u32[]{:S(2)}, u32[]{:S(2)}) collective-permute-start(bf16[512,256]{1,0:T(8,128)(2,1)S(1)} %collective-permute-done.13.refs_2_), channel_id=1, source_target_pairs={{0,2},{2,4},{4,6},{6,0},{1,3},{3,5},{5,7},{7,1},{8,10},{10,12},{12... | collective-permute-start | bytes 786440 | tf_op jit(solution)/shard_map/ppermute | solution.py:259
  35.3 13.9 %collective-permute-start.10 = (bf16[2,128,256]{2,1,0:T(8,128)(2,1)S(1)}, bf16[2,128,256]{2,1,0:T(8,128)(2,1)S(1)}, u32[]{:S(2)}, u32[]{:S(2)}) collective-permute-start(bf16[2,128,256]{2,1,0:T(8,128)(2,1)S(1)} %get-tuple-element.57), channel_id=1, source_target_pairs={{0,16},{8,24},{16,0},{24,8},{1,17},{9,25},{17,1},{25,9},{2,18},{10... | collective-permute-start | bytes 393224 | tf_op jit(solution)/shard_map/ppermute | solution.py:256
  38.6 17.9 %collective-permute-start.22 = (bf16[512,256]{1,0:T(8,128)(2,1)S(1)}, bf16[512,256]{1,0:T(8,128)(2,1)S(1)}, u32[]{:S(2)}, u32[]{:S(2)}) collective-permute-start(bf16[512,256]{1,0:T(8,128)(2,1)S(1)} %collective-permute-done.17.refs_1_), channel_id=1, source_target_pairs={{0,2},{2,4},{4,6},{6,0},{1,3},{3,5},{5,7},{7,1},{8,10},{10,12},{12... | collective-permute-start | bytes 786440 | tf_op jit(solution)/shard_map/ppermute | solution.py:259
  44.2 15.0 %collective-permute-start.23 = (bf16[512,256]{1,0:T(8,128)(2,1)S(1)}, bf16[512,256]{1,0:T(8,128)(2,1)S(1)}, u32[]{:S(2)}, u32[]{:S(2)}) collective-permute-start(bf16[512,256]{1,0:T(8,128)(2,1)S(1)} %collective-permute-done.18.refs_2_), channel_id=1, source_target_pairs={{0,2},{2,4},{4,6},{6,0},{1,3},{3,5},{5,7},{7,1},{8,10},{10,12},{12... | collective-permute-start | bytes 786440 | tf_op jit(solution)/shard_map/ppermute | solution.py:259
  46.7 6.7 %collective-permute-start.11 = (bf16[2,128,256]{2,1,0:T(8,128)(2,1)S(1)}, bf16[2,128,256]{2,1,0:T(8,128)(2,1)S(1)}, u32[]{:S(2)}, u32[]{:S(2)}) collective-permute-start(bf16[2,128,256]{2,1,0:T(8,128)(2,1)S(1)} %get-tuple-element.58), channel_id=1, source_target_pairs={{0,24},{8,16},{16,8},{24,0},{1,25},{9,17},{17,9},{25,1},{2,26},{10... | collective-permute-start | bytes 393224 | tf_op jit(solution)/shard_map/ppermute | solution.py:256
  49.2 7.1 %collective-permute-start.9 = (bf16[2,128,256]{2,1,0:T(8,128)(2,1)S(1)}, bf16[2,128,256]{2,1,0:T(8,128)(2,1)S(1)}, u32[]{:S(2)}, u32[]{:S(2)}) collective-permute-start(bf16[2,128,256]{2,1,0:T(8,128)(2,1)S(1)} %get-tuple-element.56), channel_id=1, source_target_pairs={{0,8},{8,0},{16,24},{24,16},{1,9},{9,1},{17,25},{25,17},{2,10},{10... | collective-permute-start | bytes 393224 | tf_op jit(solution)/shard_map/ppermute | solution.py:256
  53.4 9.2 %collective-permute-start.14 = (bf16[2,128,256]{2,1,0:T(8,128)(2,1)S(1)}, bf16[2,128,256]{2,1,0:T(8,128)(2,1)S(1)}, u32[]{:S(2)}, u32[]{:S(2)}) collective-permute-start(bf16[2,128,256]{2,1,0:T(8,128)(2,1)S(1)} %get-tuple-element.61), channel_id=1, source_target_pairs={{0,8},{8,0},{16,24},{24,16},{1,9},{9,1},{17,25},{25,17},{2,10},{10... | collective-permute-start | bytes 393224 | tf_op jit(solution)/shard_map/ppermute | solution.py:256
  56.3 6.6 %collective-permute-start.15 = (bf16[2,128,256]{2,1,0:T(8,128)(2,1)S(1)}, bf16[2,128,256]{2,1,0:T(8,128)(2,1)S(1)}, u32[]{:S(2)}, u32[]{:S(2)}) collective-permute-start(bf16[2,128,256]{2,1,0:T(8,128)(2,1)S(1)} %get-tuple-element.62), channel_id=1, source_target_pairs={{0,16},{8,24},{16,0},{24,8},{1,17},{9,25},{17,1},{25,9},{2,18},{10... | collective-permute-start | bytes 393224 | tf_op jit(solution)/shard_map/ppermute | solution.py:256
  56.6 9.1 %collective-permute-start.16 = (bf16[2,128,256]{2,1,0:T(8,128)(2,1)S(1)}, bf16[2,128,256]{2,1,0:T(8,128)(2,1)S(1)}, u32[]{:S(2)}, u32[]{:S(2)}) collective-permute-start(bf16[2,128,256]{2,1,0:T(8,128)(2,1)S(1)} %get-tuple-element.63), channel_id=1, source_target_pairs={{0,24},{8,16},{16,8},{24,0},{1,25},{9,17},{17,9},{25,1},{2,26},{10... | collective-permute-start | bytes 393224 | tf_op jit(solution)/shard_map/ppermute | solution.py:256
  59.3 6.9 %collective-permute-start.19 = (bf16[2,128,256]{2,1,0:T(8,128)(2,1)S(1)}, bf16[2,128,256]{2,1,0:T(8,128)(2,1)S(1)}, u32[]{:S(2)}, u32[]{:S(2)}) collective-permute-start(bf16[2,128,256]{2,1,0:T(8,128)(2,1)S(1)} %get-tuple-element.66), channel_id=1, source_target_pairs={{0,8},{8,0},{16,24},{24,16},{1,9},{9,1},{17,25},{25,17},{2,10},{10... | collective-permute-start | bytes 393224 | tf_op jit(solution)/shard_map/ppermute | solution.py:256
  62.6 13.5 %collective-permute-start.20 = (bf16[2,128,256]{2,1,0:T(8,128)(2,1)S(1)}, bf16[2,128,256]{2,1,0:T(8,128)(2,1)S(1)}, u32[]{:S(2)}, u32[]{:S(2)}) collective-permute-start(bf16[2,128,256]{2,1,0:T(8,128)(2,1)S(1)} %get-tuple-element.67), channel_id=1, source_target_pairs={{0,16},{8,24},{16,0},{24,8},{1,17},{9,25},{17,1},{25,9},{2,18},{10... | collective-permute-start | bytes 393224 | tf_op jit(solution)/shard_map/ppermute | solution.py:256
  63.0 13.6 %collective-permute-start.21 = (bf16[2,128,256]{2,1,0:T(8,128)(2,1)S(1)}, bf16[2,128,256]{2,1,0:T(8,128)(2,1)S(1)}, u32[]{:S(2)}, u32[]{:S(2)}) collective-permute-start(bf16[2,128,256]{2,1,0:T(8,128)(2,1)S(1)} %get-tuple-element.68), channel_id=1, source_target_pairs={{0,24},{8,16},{16,8},{24,0},{1,25},{9,17},{17,9},{25,1},{2,26},{10... | collective-permute-start | bytes 393224 | tf_op jit(solution)/shard_map/ppermute | solution.py:256
  65.7 12.0 %collective-permute-start.24 = (bf16[2,128,256]{2,1,0:T(8,128)(2,1)S(1)}, bf16[2,128,256]{2,1,0:T(8,128)(2,1)S(1)}, u32[]{:S(2)}, u32[]{:S(2)}) collective-permute-start(bf16[2,128,256]{2,1,0:T(8,128)(2,1)S(1)} %get-tuple-element.71), channel_id=1, source_target_pairs={{0,8},{8,0},{16,24},{24,16},{1,9},{9,1},{17,25},{25,17},{2,10},{10... | collective-permute-start | bytes 393224 | tf_op jit(solution)/shard_map/ppermute | solution.py:256
  66.2 13.5 %collective-permute-start.25 = (bf16[2,128,256]{2,1,0:T(8,128)(2,1)S(1)}, bf16[2,128,256]{2,1,0:T(8,128)(2,1)S(1)}, u32[]{:S(2)}, u32[]{:S(2)}) collective-permute-start(bf16[2,128,256]{2,1,0:T(8,128)(2,1)S(1)} %get-tuple-element.72), channel_id=1, source_target_pairs={{0,16},{8,24},{16,0},{24,8},{1,17},{9,25},{17,1},{25,9},{2,18},{10... | collective-permute-start | bytes 393224 | tf_op jit(solution)/shard_map/ppermute | solution.py:256
  66.5 13.2 %collective-permute-start.26 = (bf16[2,128,256]{2,1,0:T(8,128)(2,1)S(1)}, bf16[2,128,256]{2,1,0:T(8,128)(2,1)S(1)}, u32[]{:S(2)}, u32[]{:S(2)}) collective-permute-start(bf16[2,128,256]{2,1,0:T(8,128)(2,1)S(1)} %get-tuple-element.73), channel_id=1, source_target_pairs={{0,24},{8,16},{16,8},{24,0},{1,25},{9,17},{17,9},{25,1},{2,26},{10... | collective-permute-start | bytes 393224 | tf_op jit(solution)/shard_map/ppermute | solution.py:256
  76.2 21.4 %collective-permute-start.36 = (bf16[128,1024]{1,0:T(8,128)(2,1)S(1)}, bf16[128,1024]{1,0:T(8,128)(2,1)S(1)}, u32[]{:S(2)}, u32[]{:S(2)}) collective-permute-start(bf16[128,1024]{1,0:T(8,128)(2,1)S(1)} %get-tuple-element.85), channel_id=1, source_target_pairs={{0,24},{8,16},{16,8},{24,0},{1,25},{9,17},{17,9},{25,1},{2,26},{10... | collective-permute-start | bytes 786440 | tf_op jit(solution)/shard_map/ppermute | solution.py:256
  76.5 21.1 %collective-permute-start.34 = (bf16[128,1024]{1,0:T(8,128)(2,1)S(1)}, bf16[128,1024]{1,0:T(8,128)(2,1)S(1)}, u32[]{:S(2)}, u32[]{:S(2)}) collective-permute-start(bf16[128,1024]{1,0:T(8,128)(2,1)S(1)} %get-tuple-element.83), channel_id=1, source_target_pairs={{0,8},{8,0},{16,24},{24,16},{1,9},{9,1},{17,25},{25,17},{2,10},{10... | collective-permute-start | bytes 786440 | tf_op jit(solution)/shard_map/ppermute | solution.py:256
  77.7 19.9 %collective-permute-start.35 = (bf16[128,1024]{1,0:T(8,128)(2,1)S(1)}, bf16[128,1024]{1,0:T(8,128)(2,1)S(1)}, u32[]{:S(2)}, u32[]{:S(2)}) collective-permute-start(bf16[128,1024]{1,0:T(8,128)(2,1)S(1)} %get-tuple-element.84), channel_id=1, source_target_pairs={{0,16},{8,24},{16,0},{24,8},{1,17},{9,25},{17,1},{25,9},{2,18},{10... | collective-permute-start | bytes 786440 | tf_op jit(solution)/shard_map/ppermute | solution.py:256
  94.7 7.0 %collective-permute-start.31 = (bf16[8,64,256]{2,1,0:T(8,128)(2,1)S(1)}, bf16[8,64,256]{2,1,0:T(8,128)(2,1)}, u32[]{:S(2)}, u32[]{:S(2)}) collective-permute-start(bf16[8,64,256]{2,1,0:T(8,128)(2,1)S(1)} %get-tuple-element.78), channel_id=1, source_target_pairs={{0,6},{2,0},{4,2},{6,4},{1,7},{3,1},{5,3},{7,5},{8,14},{10,8},{12,... | collective-permute-start | bytes 786440 | tf_op jit(solution)/shard_map/ppermute | solution.py:259
  100.2 20.1 %collective-permute-start.37 = (bf16[1024,512]{1,0:T(8,128)(2,1)S(1)}, bf16[1024,512]{1,0:T(8,128)(2,1)S(1)}, u32[]{:S(2)}, u32[]{:S(2)}) collective-permute-start(bf16[1024,512]{1,0:T(8,128)(2,1)S(1)} %copy.17.refs_1_), channel_id=1, source_target_pairs={{0,1},{1,0},{2,3},{3,2},{4,5},{5,4},{6,7},{7,6},{8,9},{9,8},{10,11... | collective-permute-start | bytes 3145736 | tf_op jit(solution)/shard_map/ppermute | solution.py:253
  100.3 9.2 %collective-permute-start.29 = (bf16[8,64,256]{2,1,0:T(8,128)(2,1)S(1)}, bf16[8,64,256]{2,1,0:T(8,128)(2,1)S(1)}, u32[]{:S(2)}, u32[]{:S(2)}) collective-permute-start(bf16[8,64,256]{2,1,0:T(8,128)(2,1)S(1)} %get-tuple-element.75), channel_id=1, source_target_pairs={{0,6},{2,0},{4,2},{6,4},{1,7},{3,1},{5,3},{7,5},{8,14},{10,8},{12,... | collective-permute-start | bytes 786440 | tf_op jit(solution)/shard_map/ppermute | solution.py:259
  102.7 12.4 %collective-permute-start.32 = (bf16[8,64,256]{2,1,0:T(8,128)(2,1)S(1)}, bf16[8,64,256]{2,1,0:T(8,128)(2,1)S(1)}, u32[]{:S(2)}, u32[]{:S(2)}) collective-permute-start(bf16[8,64,256]{2,1,0:T(8,128)(2,1)S(1)} %add_convert_fusion.1), channel_id=1, source_target_pairs={{0,6},{2,0},{4,2},{6,4},{1,7},{3,1},{5,3},{7,5},{8,14},{10,8},{12,... | collective-permute-start | bytes 786440 | tf_op jit(solution)/shard_map/ppermute | solution.py:259
  109.5 10.7 %collective-permute-start.30 = (bf16[8,64,256]{2,1,0:T(8,128)(2,1)S(1)}, bf16[8,64,256]{2,1,0:T(8,128)(2,1)S(1)}, u32[]{:S(2)}, u32[]{:S(2)}) collective-permute-start(bf16[8,64,256]{2,1,0:T(8,128)(2,1)S(1)} %add_convert_fusion.3), channel_id=1, source_target_pairs={{0,6},{2,0},{4,2},{6,4},{1,7},{3,1},{5,3},{7,5},{8,14},{10,8},{12,... | collective-permute-start | bytes 786440 | tf_op jit(solution)/shard_map/ppermute | solution.py:259
  111.7 8.6 %collective-permute-start.33 = (bf16[512,256]{1,0:T(8,128)(2,1)S(1)}, bf16[512,256]{1,0:T(8,128)(2,1)S(1)}, u32[]{:S(2)}, u32[]{:S(2)}) collective-permute-start(bf16[512,256]{1,0:T(8,128)(2,1)S(1)} %get-tuple-element.81), channel_id=1, source_target_pairs={{0,1},{1,0},{2,3},{3,2},{4,5},{5,4},{6,7},{7,6},{8,9},{9,8},{10,11... | collective-permute-start | bytes 786440 | tf_op jit(solution)/shard_map/ppermute | solution.py:253
  120.3 9.3 %collective-permute-start.38 = (bf16[8,64,256]{2,1,0:T(8,128)(2,1)S(1)}, bf16[8,64,256]{2,1,0:T(8,128)(2,1)S(1)}, u32[]{:S(2)}, u32[]{:S(2)}) collective-permute-start(bf16[8,64,256]{2,1,0:T(8,128)(2,1)S(1)} %add_convert_fusion.2), channel_id=1, source_target_pairs={{0,6},{2,0},{4,2},{6,4},{1,7},{3,1},{5,3},{7,5},{8,14},{10,8},{12,... | collective-permute-start | bytes 786440 | tf_op jit(solution)/shard_map/ppermute | solution.py:259
  122.7 11.1 %collective-permute-start.39 = (bf16[8,64,256]{2,1,0:T(8,128)(2,1)S(1)}, bf16[8,64,256]{2,1,0:T(8,128)(2,1)S(1)}, u32[]{:S(2)}, u32[]{:S(2)}) collective-permute-start(bf16[8,64,256]{2,1,0:T(8,128)(2,1)S(1)} %add_convert_fusion), channel_id=1, source_target_pairs={{0,6},{2,0},{4,2},{6,4},{1,7},{3,1},{5,3},{7,5},{8,14},{10,8},{12,... | collective-permute-start | bytes 786440 | tf_op jit(solution)/shard_map/ppermute | solution.py:259
  135.2 6.2 %collective-permute-start.40 = (bf16[256,256]{1,0:T(8,128)(2,1)S(1)}, bf16[256,256]{1,0:T(8,128)(2,1)S(1)}, u32[]{:S(2)}, u32[]{:S(2)}) collective-permute-start(bf16[256,256]{1,0:T(8,128)(2,1)S(1)} %get-tuple-element.93), channel_id=1, source_target_pairs={{0,8},{8,0},{16,24},{24,16},{1,9},{9,1},{17,25},{25,17},{2,10},{10... | collective-permute-start | bytes 393224 | tf_op jit(solution)/shard_map/ppermute | solution.py:256
  136.7 6.9 %collective-permute-start.41 = (bf16[256,256]{1,0:T(8,128)(2,1)S(1)}, bf16[256,256]{1,0:T(8,128)(2,1)S(1)}, u32[]{:S(2)}, u32[]{:S(2)}) collective-permute-start(bf16[256,256]{1,0:T(8,128)(2,1)S(1)} %get-tuple-element.94), channel_id=1, source_target_pairs={{0,16},{8,24},{16,0},{24,8},{1,17},{9,25},{17,1},{25,9},{2,18},{10... | collective-permute-start | bytes 393224 | tf_op jit(solution)/shard_map/ppermute | solution.py:256
  136.7 6.9 %collective-permute-start.42 = (bf16[256,256]{1,0:T(8,128)(2,1)S(1)}, bf16[256,256]{1,0:T(8,128)(2,1)S(1)}, u32[]{:S(2)}, u32[]{:S(2)}) collective-permute-start(bf16[256,256]{1,0:T(8,128)(2,1)S(1)} %get-tuple-element.95), channel_id=1, source_target_pairs={{0,24},{8,16},{16,8},{24,0},{1,25},{9,17},{17,9},{25,1},{2,26},{10... | collective-permute-start | bytes 393224 | tf_op jit(solution)/shard_map/ppermute | solution.py:256
  143.8 5.5 %collective-permute-start.43 = (bf16[256,256]{1,0:T(8,128)(2,1)S(1)}, bf16[256,256]{1,0:T(8,128)(2,1)S(1)}, u32[]{:S(2)}, u32[]{:S(2)}) collective-permute-start(bf16[256,256]{1,0:T(8,128)(2,1)S(1)} %sum.3.refs_0_), channel_id=1, source_target_pairs={{0,2},{2,0},{4,6},{6,4},{1,3},{3,1},{5,7},{7,5},{8,10},{10,8},{12,... | collective-permute-start | bytes 393224 | tf_op jit(solution)/shard_map/ppermute | solution.py:378
  149.3 7.0 %collective-permute-start.44 = (bf16[256,256]{1,0:T(8,128)(2,1)S(1)}, bf16[256,256]{1,0:T(8,128)(2,1)S(1)}, u32[]{:S(2)}, u32[]{:S(2)}) collective-permute-start(bf16[256,256]{1,0:T(8,128)(2,1)S(1)} %sum.4.refs_0_), channel_id=1, source_target_pairs={{0,4},{2,6},{4,0},{6,2},{1,5},{3,7},{5,1},{7,3},{8,12},{10,14},{12... | collective-permute-start | bytes 393224 | tf_op jit(solution)/shard_map/ppermute | solution.py:378
  156.4 5.0 %collective-permute-start.45 = (bf16[256,256]{1,0:T(8,128)(2,1)S(1)}, bf16[256,256]{1,0:T(8,128)(2,1)S(1)}, u32[]{:S(2)}, u32[]{:S(2)}) collective-permute-start(bf16[256,256]{1,0:T(8,128)(2,1)S(1)} %sum.5.refs_1_), channel_id=1, source_target_pairs={{0,8},{8,0},{16,24},{24,16},{1,9},{9,1},{17,25},{25,17},{2,10},{10... | collective-permute-start | bytes 393224 | tf_op jit(solution)/shard_map/ppermute | solution.py:256
  156.8 5.0 %collective-permute-start.46 = (bf16[256,256]{1,0:T(8,128)(2,1)S(1)}, bf16[256,256]{1,0:T(8,128)(2,1)S(1)}, u32[]{:S(2)}, u32[]{:S(2)}) collective-permute-start(bf16[256,256]{1,0:T(8,128)(2,1)S(1)} %sum.5.refs_1_), channel_id=1, source_target_pairs={{0,16},{8,24},{16,0},{24,8},{1,17},{9,25},{17,1},{25,9},{2,18},{10... | collective-permute-start | bytes 393224 | tf_op jit(solution)/shard_map/ppermute | solution.py:256
  158.1 5.9 %collective-permute-start.47 = (bf16[256,256]{1,0:T(8,128)(2,1)S(1)}, bf16[256,256]{1,0:T(8,128)(2,1)S(1)}, u32[]{:S(2)}, u32[]{:S(2)}) collective-permute-start(bf16[256,256]{1,0:T(8,128)(2,1)S(1)} %sum.5.refs_1_), channel_id=1, source_target_pairs={{0,24},{8,16},{16,8},{24,0},{1,25},{9,17},{17,9},{25,1},{2,26},{10... | collective-permute-start | bytes 393224 | tf_op jit(solution)/shard_map/ppermute | solution.py:256
  159.9 4.9 %collective-permute-start.48 = (bf16[256,256]{1,0:T(8,128)(2,1)S(1)}, bf16[256,256]{1,0:T(8,128)(2,1)S(1)}, u32[]{:S(2)}, u32[]{:S(2)}) collective-permute-start(bf16[256,256]{1,0:T(8,128)(2,1)S(1)} %sum.5.refs_1_), channel_id=1, source_target_pairs={{0,1},{1,0},{2,3},{3,2},{4,5},{5,4},{6,7},{7,6},{8,9},{9,8},{10,11... | collective-permute-start | bytes 393224 | tf_op jit(solution)/shard_map/ppermute | solution.py:253
  (15 other events, 127.1 us)

commit v3 on v2

--- a/solution.py
+++ b/solution.py
@@ -91,8 +91,8 @@
     shape = (z.rows, table.shape[0])
     row = iota(shape, 0)
     s, n = row >> log2(z.per_grp), (row >> log2(z.pair)) & (z.dom - 1)
-    k = (me_ref[1] - (n >> 1)) & (z.zz - 1)
-    spread = one_hot(iota(shape, 1) == ((s * 2 + (n & 1)) * z.zz + k) * 2)
+    k, rel = (me_ref[1] - (n >> 1)) & (z.zz - 1), (n & 1) ^ me_ref[2]
+    spread = one_hot(iota(shape, 1) == ((s * 2 + rel) * z.zz + k) * 2)
     high = dot(spread, (table >> 4).astype(F32).astype(BF16))
     return high * 16.0 + dot(spread, (table & 15).astype(F32).astype(BF16))
 
@@ -132,94 +132,112 @@
             outs[s][rel] = got[s * z.per_grp:(s + 1) * z.per_grp, :]
 
 
-def place_kernel(z, me_ref, table_ref, pick_ref, back_ref):
-    shape = (z.rows, z.rows)
-
+def place_kernel(z, me_ref, domain_ref, out_ref):
     @pl.loop(0, z.dom)
     def _(n):
-        k = (me_ref[1] - (n >> 1)) & (z.zz - 1)
-        slot = table_ref[pl.ds(((n & 1) * z.zz + k) * 2 + 1, 1), :]
-        at = slot >> log2(z.piece)
-        zz = (me_ref[1] - (at >> 1)) & (z.zz - 1)
-        at = zz * 2 + ((at & 1) ^ me_ref[2])
-        slot = at * z.piece + (slot & (z.piece - 1))
-        back_ref[n] = one_hot(iota(shape, 0) == slot)
-        pick_ref[n] = one_hot(iota(shape, 1) == column(slot))
-
-
-def turn_kernel(vals_ref, out_ref):
+        k, rel = (me_ref[1] - (n >> 1)) & (z.zz - 1), (n & 1) ^ me_ref[2]
+        slot = domain_ref[pl.ds((rel * z.zz + k) * 2 + 1, 1), :]
+        rank, at = slot & (z.pair - 1), slot >> log2(z.pair)
+        s, at = at & (z.grp - 1), at >> log2(z.grp)
+        k, rel = (me_ref[1] - (at >> 1)) & (z.zz - 1), (at & 1) ^ me_ref[2]
+        slot = ((k * z.grp + s) * 2 + rel) * z.pair + rank
+        out_ref[n] = one_hot(iota((z.rows, z.rows), 0) == slot)
+
+
+def dense_kernel(cols_ref, vals_ref, out_ref, total):
     tiles, blocks, tile, _ = vals_ref.shape
+    count = out_ref.shape[0]
 
     @pl.loop(0, tiles)
     def _(t):
+        total[...] = jnp.zeros_like(total)
         for k in range(blocks):
-            out_ref[t, k] = vals_ref[t, k].T
-
-
-def layer_kernel(z, packed, cols_ref, pick_ref, back_ref, *refs):
-    count = 1 if packed else z.zz * z.grp
-    y_refs, refs = refs[:count], refs[count:]
-    vals_a, vals_b, turned_a, turned_b, cot_a, cot_b, hidden_a, hidden_b = refs[:8]
-    partial_refs, (panel, total) = refs[8:-2], refs[-2:]
-    rows, blocks, tile = z.rows, vals_a.shape[1], vals_a.shape[2]
-    half = cot_a.shape[1]
-
-    def held_of(n):
-        if packed:
-            return y_refs[0][n]
-        return jnp.concatenate(
-            [
-                y_refs[k * z.grp + s][rel, pl.ds(pl.multiple_of(n * z.pair, z.pair), z.pair), :]
-                for k in range(z.zz)
-                for rel in range(2)
-                for s in range(z.grp)
-            ],
-            axis=0,
-        )
-
-    panel[pl.ds(z.dom * rows, tile), :] = jnp.zeros((tile, half), BF16)
+            at = pl.multiple_of(cols_ref[t, k] * tile, tile)
+            total[pl.ds(at, tile), :] += vals_ref[t, k].T.astype(F32)
+        left = pl.multiple_of(t * tile, tile)
+        out_ref[:, pl.ds(left, tile)] = total[pl.ds(0, count), :].astype(BF16)
+
+
+def arrange_kernel(z, place_ref, dense_ref, *outs):
+    turned, plain = outs[:z.zz], outs[z.zz:]
 
     @pl.loop(0, z.dom)
     def _(n):
-        at = pl.multiple_of(n * rows, rows)
-        panel[pl.ds(at, rows), :] = dot(pick_ref[n], held_of(n)).astype(BF16)
-        total[pl.ds(at, rows), :] = jnp.zeros((rows, half), F32)
-
-    for side, (vals, turned, cot, hidden) in enumerate(
-        ((vals_a, turned_a, cot_a, hidden_a), (vals_b, turned_b, cot_b, hidden_b))
-    ):
-        @pl.loop(0, z.tiles)
-        def _(t):
-            at = pl.multiple_of(t * tile, tile)
-            starts = [
-                pl.multiple_of(cols_ref[side * z.tiles + t, k] * tile, tile) for k in range(blocks)
-            ]
-            left = jnp.concatenate([vals[t, k] for k in range(blocks)], axis=1)
-            right = jnp.concatenate([panel[pl.ds(s, tile), :] for s in starts], axis=0)
-            agg = dot(left, right)
-            sig = jax.nn.sigmoid(agg)
-            hidden[pl.ds(at, tile), :] = (agg * sig).astype(BF16)
-            slope = sig * (1.0 + agg * (1.0 - sig))
-            grad = (cot[pl.ds(at, tile), :].astype(F32) * slope).astype(BF16)
-            for k in range(blocks):
-                total[pl.ds(starts[k], tile), :] += dot(turned[t, k], grad)
-
-    @pl.loop(0, z.dom)
-    def _(n):
-        at = pl.multiple_of(n * rows, rows)
-        back = dot(back_ref[n], total[pl.ds(at, rows), :].astype(BF16)).astype(BF16)
-        for p in range(z.dom):
-            partial_refs[p][n] = back[p * z.piece:(p + 1) * z.piece, :]
+        at = pl.multiple_of(n * z.rows, z.rows)
+        part = dot(place_ref[n], dense_ref[pl.ds(at, z.rows), :]).astype(BF16)
+        for k in range(z.zz):
+            for p in range(2 * z.grp):
+                first = (k * 2 * z.grp + p) * z.pair
+                to = p * z.per_grp + n * z.pair
+                if z.pair % 16 == 0:
+                    to = pl.multiple_of(to, z.pair)
+                    turned[k][pl.ds(to, z.pair), :] = part[first:first + z.pair, :]
+                else:
+                    turned[k][p, n] = part[first:first + z.pair, :]
+
+    for out, source in zip(plain, turned):
+        out[...] = source[...].reshape(out.shape[::-1]).T
+
+
+def turn_kernel(*refs):
+    out, height = refs[-1], refs[0].shape[0]
+    for i, ref in enumerate(refs[:-1]):
+        out[:, i * height:(i + 1) * height] = ref[...].T
+
+
+def forward_kernel(z, first, last, *refs):
+    plain, refs = refs[:2], refs[2:]
+    pieces, refs = refs[:z.grp], refs[z.grp:]
+    half = pieces[0].shape[2]
+    rows = jnp.concatenate([ref[...].reshape(2 * z.per_grp, half) for ref in pieces], axis=0)
+    agg = [dot(ref[...], rows) for ref in plain]
+    if not first:
+        agg = [part + ref[...] for part, ref in zip(agg, refs)]
+        refs = refs[2:]
+    if not last:
+        for ref, part in zip(refs, agg):
+            ref[...] = part
+        return
+    cots, turned, hiddens, grads, parts = (refs[2 * i:2 * i + 2] for i in range(5))
+    for part, cot, hidden, grad in zip(agg, cots, hiddens, grads):
+        sig = jax.nn.sigmoid(part)
+        hidden[...] = (part * sig).astype(BF16)
+        grad[...] = (cot[...].astype(F32) * (sig * (1.0 + part * (1.0 - sig)))).astype(BF16)
+    back_into(parts, turned, grads)
+
+
+def back_into(outs, turned, grads):
+    size = outs[0].shape[0]
+    for i, out in enumerate(outs):
+        rows = pl.ds(i * size, size)
+        value = dot(turned[0][rows, :], grads[0][...]) + dot(turned[1][rows, :], grads[1][...])
+        out[...] = value.astype(out.dtype)
+
+
+def back_kernel(turned_a, turned_b, grad_a, grad_b, *outs):
+    back_into(outs, (turned_a, turned_b), (grad_a, grad_b))
+
+
+def pass_kernel(mine_ref, come_ref, out_ref):
+    out_ref[...] = (mine_ref[...] + come_ref[...].astype(F32)).astype(BF16)
 
 
 def grad_kernel(z, me_ref, left_a, left_b, mine_a, mine_b, come_a, come_b, *refs):
     outs, whole = refs[:-1], refs[-1]
-    grad_a = (mine_a[...].astype(F32) + come_a[...].astype(F32)).astype(BF16)
-    grad_b = (mine_b[...].astype(F32) + come_b[...].astype(F32)).astype(BF16)
-    grad_b = jnp.concatenate(
-        [grad_b[(n ^ 1) * z.piece:((n ^ 1) + 1) * z.piece, :] for n in range(z.dom)], axis=0
-    )
-    whole[...] = (dot(left_a[...], grad_a) + dot(left_b[...], grad_b)).astype(BF16)
+    grads = jnp.concatenate(
+        [
+            (mine[...] + come[...].astype(F32)).astype(BF16)
+            for mine, come in ((mine_a, come_a), (mine_b, come_b))
+        ],
+        axis=0,
+    )
+    total = 0.0
+    for rel, left in enumerate((left_a, left_b)):
+        of_rel = [
+            grads[(2 * s + rel) * z.per_grp:(2 * s + rel + 1) * z.per_grp] for s in range(z.grp)
+        ]
+        total = total + dot(left[...], jnp.concatenate(of_rel, axis=0))
+    whole[...] = total.astype(BF16)
     share = whole.shape[0] // z.grp
     for s in range(z.grp):
         at = pl.multiple_of((me_ref[0] ^ s) * share, share)
@@ -240,6 +258,17 @@
             out[pl.ds(at, share), pl.ds(left, half)] = pieces[rel * z.grp + s][...].astype(F32)
 
 
+def arrange(z, place, dense, wide):
+    inner = (wide, z.rows) if z.pair % 16 == 0 else (2 * z.grp, z.dom, z.pair, z.rows)
+    got = call(
+        lambda *refs: arrange_kernel(z, *refs),
+        [(inner, BF16)] * z.zz + [((z.rows, wide), BF16)] * z.zz,
+        [("v", place), ("v", dense)],
+        "arrange", 32, 4,
+    )
+    return [part.reshape(wide, z.rows) for part in got[:z.zz]] + list(got[z.zz:])
+
+
 def shards(features, node_order, block_cols, block_count, block_vals, weight, cotangent):
     rows, width_in = features.shape
     hidden_units = weight.shape[1]
@@ -265,7 +294,6 @@
         "index", 24, 1,
     )
     domain = jnp.concatenate([to_zz(index, k) for k in range(z.zz)], axis=0)
-    features, domain = lax.optimization_barrier((features, domain))
     domain = jnp.concatenate([domain, to_core(domain)], axis=0)
     table = jnp.concatenate([to_grp(domain, s) for s in range(z.grp)], axis=0)
 
@@ -282,10 +310,9 @@
     vals_b = to_core(block_vals)
     cot_a = lax.dynamic_slice_in_dim(cotangent, core * half, half, axis=1)
     cot_b = to_core(lax.dynamic_slice_in_dim(cotangent, (1 - core) * half, half, axis=1))
-    cols_a = jnp.where(iota((tiles, blocks), 1) < block_count[:, None], block_cols, -1)
-    cols = jnp.concatenate([cols_a, to_core(cols_a)], axis=0)
-    dev = cols >> log2(tiles)
-    cols = jnp.where(cols < 0, z.dom * tiles, (dev ^ core) * tiles + (cols & (tiles - 1)))
+    live = iota((tiles, blocks), 1) < block_count[:, None]
+    cols_a = jnp.where(live, block_cols, z.dom * tiles)
+    cols_b = to_core(cols_a)
 
     pieces = [((2, z.per_grp, half), BF16)] * z.grp
     got = call(
@@ -294,63 +321,81 @@
         [("s", me), ("v", table), ("v", ring[0][0]), ("v", ring[0][1]), ("v", features)],
         "select_own", 24, 2.5,
     )
-    y = [to_grp(got[s], s) for s in range(z.grp)]
-    held = jnp.stack([to_grp(got[z.grp + s], s) for s in range(z.grp)])
-    held = held.reshape(z.grp, z.dom, z.pair, width_in).transpose(3, 1, 0, 2).reshape(width_in, rows)
-    held_b = to_core(held)
+    picked = got[z.grp:]
+    y = [[to_grp(got[s], s) for s in range(z.grp)]]
     picks = call(
         lambda *refs: picks_kernel(z, *refs),
         [((2, rows, rows), BF16)] * (z.zz - 1),
         [("s", me), ("v", table)],
-        "picks", 24, 4,
+        "picks", 24, 2.5,
     )
     for k in range(1, z.zz):
         got = call(
             lambda *refs: select_kernel(z, *refs), pieces,
             [("v", picks[k - 1]), ("v", ring[k][0]), ("v", ring[k][1])],
-            "select", 16, 0.7,
+            "select", 16, 0.5,
         )
-        y += [to_grp(got[s], s) for s in range(z.grp)]
-
-    pick, back = call(
+        y.append([to_grp(got[s], s) for s in range(z.grp)])
+
+    (place,) = call(
         lambda *refs: place_kernel(z, *refs),
-        [((z.dom, rows, rows), BF16)] * 2,
+        [((z.dom, rows, rows), BF16)],
         [("s", me), ("v", domain)],
-        "place", 24, 6,
-    )
-    turned_a, turned_b = (
-        call(turn_kernel, [(block_vals.shape, BF16)], [("v", vals)], "turn", 16, 3)[0]
-        for vals in (block_vals, vals_b)
-    )
-
-    packed = z.pair % 16 != 0
-    if packed:
-        y = jnp.stack(y).reshape(z.zz, z.grp, 2, z.dom, z.pair, half)
-        y = [y.transpose(3, 0, 2, 1, 4, 5).reshape(z.dom, rows, half)]
-    layer = call(
-        lambda *refs: layer_kernel(z, packed, *refs),
-        [((rows, half), BF16)] * 2 + [((z.dom, z.piece, half), BF16)] * z.dom,
-        [("s", cols), ("v", pick), ("v", back)]
-        + [("v", part) for part in y]
-        + [("v", block_vals), ("v", vals_b), ("v", turned_a), ("v", turned_b)]
-        + [("v", cot_a), ("v", cot_b)],
-        "layer", 36, 10,
-        (pltpu.VMEM((z.dom * rows + tile, half), BF16), pltpu.VMEM((z.dom * rows + tile, half), F32)),
-    )
-    hidden_a, hidden_b, partial = layer[0], layer[1], layer[2:]
-
+        "place", 16, 1.5,
+    )
+    wide = 2 * z.grp * z.per_grp
+    turned, plain = [], []
+    for cols, vals in ((cols_a, block_vals), (cols_b, vals_b)):
+        (dense,) = call(
+            dense_kernel,
+            [((z.dom * rows, rows), BF16)],
+            [("s", cols), ("v", vals)],
+            "dense", 24, 2.5,
+            (pltpu.VMEM((z.dom * rows + tile, tile), F32),),
+        )
+        got = arrange(z, place, dense, wide)
+        turned.append(got[:z.zz])
+        plain.append(got[z.zz:])
+
+    agg = []
+    for k in range(z.zz):
+        ins = [("v", plain[0][k]), ("v", plain[1][k])] + [("v", part) for part in y[k]]
+        ins += [("v", part) for part in agg]
+        outs = [((rows, half), F32)] * 2
+        last = k == z.zz - 1
+        if last:
+            ins += [("v", part) for part in (cot_a, cot_b, turned[0][k], turned[1][k])]
+            outs = [((rows, half), BF16)] * 4 + [((wide // 2, half), BF16)] * 2
+        agg = call(
+            lambda *refs, k=k, last=last: forward_kernel(z, k == 0, last, *refs),
+            outs, ins, "forward", 24, 3 if last else 1,
+        )
+    hidden_a, hidden_b, grad_a, grad_b = agg[:4]
+    came = agg[4:]
+
+    came, picked, hidden_b = lax.optimization_barrier((came, picked, hidden_b))
     come = to_core(hidden_b)
-    came = [partial[2 * (z.zz - 1) + rel] for rel in range(2)]
     for k in range(z.zz - 2, -1, -1):
         came = [to_zz(part, -1) for part in came]
+        mine = call(
+            back_kernel,
+            [((wide // 2, half), F32)] * 2,
+            [("v", part) for part in (turned[0][k], turned[1][k], grad_a, grad_b)],
+            "back", 16, 1,
+        )
         if k:
             came = [
-                (part.astype(F32) + partial[2 * k + rel].astype(F32)).astype(BF16)
-                for rel, part in enumerate(came)
+                call(
+                    pass_kernel, [((wide // 2, half), BF16)], [("v", part), ("v", moved)],
+                    "pass", 16, 0.5,
+                )[0]
+                for part, moved in zip(mine, came)
             ]
-        if k == 1:
-            came, come, held_b = lax.optimization_barrier((came, come, held_b))
-
+    held = [to_grp(picked[s], s) for s in range(z.grp)]
+    (held,) = call(
+        turn_kernel, [((width_in, rows), BF16)], [("v", part) for part in held], "turn", 16, 1
+    )
+    held_b = to_core(held)
     first = core == 0
     hidden = jnp.concatenate(
         [jnp.where(first, hidden_a, come), jnp.where(first, come, hidden_a)], axis=1
@@ -360,8 +405,7 @@
     terms = call(
         lambda *refs: grad_kernel(z, *refs),
         [((share, half), BF16)] * z.grp,
-        [("s", me), ("v", held), ("v", held_b)]
-        + [("v", part.reshape(rows, half)) for part in (partial[0], partial[1], came[0], came[1])],
+        [("s", me), ("v", held), ("v", held_b)] + [("v", part) for part in (*mine, *came)],
         "grad", 16, 1.5,
         (pltpu.VMEM((width_in, half), BF16),),
     )

time: 168 us -> 183 us (1.089)
  local copies, waits for them, and re-layouts: 4.52 us -> 13.3 us
  Pallas kernels: 30.6 us -> 35 us
  other arithmetic: 3.37 us -> 1.03 us
  waiting for transfers between devices: 70.2 us -> 72.4 us
  starting transfers between devices: 57.6 us -> 59.5 us
    unnamed x26 -> x56, local copies, waits for them, and re-layouts: 1.96 us -> 13.2 us
    pallas_call x16 -> x29, Pallas kernels: 30.6 us -> 35 us  [call(): pl.pallas_call(body, out_shape=tuple((jax.ShapeDtypeStruct(s, d) for s, d...]
    ppermute x15, starting transfers between devices: 21.6 us -> 24.7 us  [to_zz(): lax.ppermute(x, 'zz', [(i, (i + k) % z.zz) for i in range(z.zz)])]
    ppermute x24, waiting for transfers between devices: 23.1 us -> 25.4 us  [to_grp(): lax.ppermute(x, 'grp', [(i, i ^ s) for i in range(z.grp)])]
  transfers between devices with their start and end apart: 52 -> 52, of which waited for: 25 -> 24; matrix products, arithmetic and copies ran while one was open for 4% -> 1% of each run, Pallas kernels for 16% -> 16%
where the time goes in v3:
time: 183 us; the launch traced here: 182 us
  waiting for transfers between devices  72.4 us (40%)
  starting transfers between devices  59.5 us (33%)
  Pallas kernels  35 us (19%)
  local copies, waits for them, and re-layouts  13.3 us (7%)
    ppermute x15, waiting for transfers between devices, to_zz(): lax.ppermute(x, 'zz', [(i, (i + k) % z.zz) for i in range(z.zz)])  35.6 us
    pallas_call x29, Pallas kernels, call(): pl.pallas_call(body, out_shape=tuple((jax.ShapeDtypeStruct(s, d) for s, d...  35 us
    ppermute x24, starting transfers between devices, to_grp(): lax.ppermute(x, 'grp', [(i, i ^ s) for i in range(z.grp)])  31.6 us
    ppermute x24, waiting for transfers between devices, to_grp(): lax.ppermute(x, 'grp', [(i, i ^ s) for i in range(z.grp)])  25.4 us
    ppermute x15, starting transfers between devices, to_zz(): lax.ppermute(x, 'zz', [(i, (i + k) % z.zz) for i in range(z.zz)])  24.7 us
    unnamed x56, local copies, waits for them, and re-layouts  13.2 us
    ppermute x2, waiting for transfers between devices, shards(): lax.ppermute(mine, 'zz', [(i, i ^ step) for i in range(z.zz)])  10.2 us
  transfers between devices with their start and end apart: 52, of which 24 were waited for; matrix products, arithmetic and copies ran while one was open for 1% of the time, Pallas kernels for 16%

profile of v3, /device:TPU:0, one launch (start us, length us, event | category | flops | bytes accessed | tf_op | source)
XLA Modules:
  0.0 182.4 jit_solution(3257491201037837604)
XLA Ops:
  2.9 2.6 %collective-permute-start = (s32[2,512]{1,0:T(2,128)S(1)}, s32[2,512]{1,0:T(2,128)S(1)}, u32[]{:S(2)}, u32[]{:S(2)}) collective-permute-start(s32[2,512]{1,0:T(2,128)S(1)} %index.1), channel_id=1, source_target_pairs={{0,2},{2,4},{4,6},{6,0},{1,3},{3,5},{5,7},{7,1},{8,10},{10,12},{12... | collective-permute-start | bytes 12296 | tf_op jit(solution)/shard_map/ppermute | solution.py:288
  5.6 2.6 %collective-permute-start.1 = (s32[2,512]{1,0:T(2,128)S(1)}, s32[2,512]{1,0:T(2,128)S(1)}, u32[]{:S(2)}, u32[]{:S(2)}) collective-permute-start(s32[2,512]{1,0:T(2,128)S(1)} %index.1), channel_id=1, source_target_pairs={{0,4},{2,6},{4,0},{6,2},{1,5},{3,7},{5,1},{7,3},{8,12},{10,14},{12... | collective-permute-start | bytes 12296 | tf_op jit(solution)/shard_map/ppermute | solution.py:288
  8.2 1.3 collective-permute-start.2
  13.4 2.4 %dense.2.refs_1_ = bf16[4096,512]{1,0:T(8,128)(2,1)S(1)} custom-call(s32[4,16]{1,0:T(4,128)S(1)} %fusion.cols_ref, bf16[4,16,128,128]{3,2,1,0:T(8,128)(2,1)S(1)} %copy-done), custom_call_target="tpu_custom_call" | custom-call | flops 2500000000 | tf_op jit(solution)/shard_map/dense/pallas_call | solution.py:37
  15.8 2.0 %copy-done.19 = bf16[4096,512]{1,0:T(8,128)(2,1)} copy-done((bf16[4096,512]{1,0:T(8,128)(2,1)}, bf16[4096,512]{1,0:T(8,128)(2,1)S(1)}, u32[]{:S(2)}) %copy-start.19) | copy-done | bytes 4194328
  19.8 1.5 collective-permute-start.6
  21.4 1.4 place.1.refs_0_
  22.8 1.6 collective-permute-start.7
  24.4 1.8 %collective-permute-start.8 = (s32[16,512]{1,0:T(8,128)S(1)}, s32[16,512]{1,0:T(8,128)S(1)}, u32[]{:S(2)}, u32[]{:S(2)}) collective-permute-start(s32[16,512]{1,0:T(8,128)S(1)} %concatenate.15.refs_1_), channel_id=1, source_target_pairs={{0,24},{8,16},{16,8},{24,0},{1,25},{9,17},{17,9},{25,1},{2,26},{10... | collective-permute-start | bytes 98312 | tf_op jit(solution)/shard_map/ppermute | solution.py:285
  26.3 2.5 %collective-permute-done.9.refs_1_ = bf16[512,256]{1,0:T(8,128)(2,1)S(1)} collective-permute-done((bf16[512,256]{1,0:T(8,128)(2,1)S(1)}, bf16[512,256]{1,0:T(8,128)(2,1)S(1)}, u32[]{:S(2)}, u32[]{:S(2)}) %collective-permute-start.9) | collective-permute-done | bytes 262176 | tf_op jit(solution)/shard_map/ppermute | solution.py:288
  28.8 5.6 %collective-permute-done.13.refs_2_ = bf16[512,256]{1,0:T(8,128)(2,1)S(1)} collective-permute-done((bf16[512,256]{1,0:T(8,128)(2,1)S(1)}, bf16[512,256]{1,0:T(8,128)(2,1)S(1)}, u32[]{:S(2)}, u32[]{:S(2)}) %collective-permute-start.13) | collective-permute-done | bytes 262176 | tf_op jit(solution)/shard_map/ppermute | solution.py:288
  34.4 4.7 %arrange.2 = (bf16[1024,512]{1,0:T(8,128)(2,1)S(1)}, bf16[1024,512]{1,0:T(8,128)(2,1)S(1)}, bf16[1024,512]{1,0:T(8,128)(2,1)S(1)}, bf16[1024,512]{1,0:T(8,128)(2...) custom-call(bf16[8,512,512]{2,1,0:T(8,128)(2,1)S(1)} %place.1.refs_0, ...), custom_call_target="tpu_custom_call" | custom-call | flops 4000000000 | tf_op jit(solution)/shard_map/arrange/pallas_call | solution.py:37
  47.2 2.5 %picks.1 = (bf16[2,512,512]{2,1,0:T(8,128)(2,1)S(1)}, bf16[2,512,512]{2,1,0:T(8,128)(2,1)S(1)}, bf16[2,512,512]{2,1,0:T(8,128)(2,1)S(1)}) custom-call(s32[3]{0:T(128)S(1)} %pad_add_fusion.1.refs_0_, s32[64,512]{1,0:T(8,128)S(1)} %concatenate.16.refs_1_), custom_call_target="tpu_custom_call" | custom-call | flops 2500000000 | tf_op jit(solution)/shard_map/picks/pallas_call | solution.py:37
  50.4 2.3 %select_own.1 = (bf16[2,128,256]{2,1,0:T(8,128)(2,1)S(1)}, bf16[2,128,256]{2,1,0:T(8,128)(2,1)S(1)}, bf16[2,128,256]{2,1,0:T(8,128)(2,1)S(1)}, bf16[2,128,256]{2...) custom-call(s32[3]{0:T(128)S(1)} %pad_add_fusion.1.refs_0_, ...), custom_call_target="tpu_custom_call" | custom-call | flops 2500000000 | tf_op jit(solution)/shard_map/select_own/pallas_call | solution.py:37
  52.7 1.6 collective-permute-start.25
  55.1 5.6 %collective-permute-done.11.refs_1_ = bf16[512,256]{1,0:T(8,128)(2,1)S(1)} collective-permute-done((bf16[512,256]{1,0:T(8,128)(2,1)S(1)}, bf16[512,256]{1,0:T(8,128)(2,1)S(1)}, u32[]{:S(2)}, u32[]{:S(2)}) %collective-permute-start.11) | collective-permute-done | bytes 262176 | tf_op jit(solution)/shard_map/ppermute | solution.py:288
  60.7 1.5 collective-permute-start.26
  62.2 3.9 %collective-permute-done.15.refs_2_ = bf16[512,256]{1,0:T(8,128)(2,1)S(1)} collective-permute-done((bf16[512,256]{1,0:T(8,128)(2,1)S(1)}, bf16[512,256]{1,0:T(8,128)(2,1)S(1)}, u32[]{:S(2)}, u32[]{:S(2)}) %collective-permute-start.15) | collective-permute-done | bytes 262176 | tf_op jit(solution)/shard_map/ppermute | solution.py:288
  66.1 2.4 %collective-permute-start.27 = (bf16[2,128,256]{2,1,0:T(8,128)(2,1)S(1)}, bf16[2,128,256]{2,1,0:T(8,128)(2,1)S(1)}, u32[]{:S(2)}, u32[]{:S(2)}) collective-permute-start(bf16[2,128,256]{2,1,0:T(8,128)(2,1)S(1)} %get-tuple-element.100), channel_id=1, source_target_pairs={{0,24},{8,16},{16,8},{24,0},{1,25},{9,17},{17,9},{25,1},{2,26},{10... | collective-permute-start | bytes 393224 | tf_op jit(solution)/shard_map/ppermute | solution.py:285
  70.2 3.7 %dense.3.refs_1_ = bf16[4096,512]{1,0:T(8,128)(2,1)S(1)} custom-call(s32[4,16]{1,0:T(4,128)S(1)} %collective-permute-done.4.cols_ref, bf16[4,16,128,128]{3,2,1,0:T(8,128)(2,1)} %collective-permute-done.5.vals_ref), custom_call_target="tpu_custom_call" | custom-call | flops 2500000000 | tf_op jit(solution)/shard_map/dense/pallas_call | solution.py:37
  73.8 2.3 %collective-permute-start.24 = (bf16[2,128,256]{2,1,0:T(8,128)(2,1)S(1)}, bf16[2,128,256]{2,1,0:T(8,128)(2,1)S(1)}, u32[]{:S(2)}, u32[]{:S(2)}) collective-permute-start(bf16[2,128,256]{2,1,0:T(8,128)(2,1)S(1)} %get-tuple-element.94), channel_id=1, source_target_pairs={{0,24},{8,16},{16,8},{24,0},{1,25},{9,17},{17,9},{25,1},{2,26},{10... | collective-permute-start | bytes 393224 | tf_op jit(solution)/shard_map/ppermute | solution.py:285
  77.4 4.7 %arrange.3 = (bf16[1024,512]{1,0:T(8,128)(2,1)S(1)}, bf16[1024,512]{1,0:T(8,128)(2,1)S(1)}, bf16[1024,512]{1,0:T(8,128)(2,1)S(1)}, bf16[1024,512]{1,0:T(8,128)(2...) custom-call(bf16[8,512,512]{2,1,0:T(8,128)(2,1)S(1)} %copy-done.10, ...), custom_call_target="tpu_custom_call" | custom-call | flops 4000000000 | tf_op jit(solution)/shard_map/arrange/pallas_call | solution.py:37
  82.3 2.3 %collective-permute-start.21 = (bf16[2,128,256]{2,1,0:T(8,128)(2,1)S(1)}, bf16[2,128,256]{2,1,0:T(8,128)(2,1)S(1)}, u32[]{:S(2)}, u32[]{:S(2)}) collective-permute-start(bf16[2,128,256]{2,1,0:T(8,128)(2,1)S(1)} %get-tuple-element.87), channel_id=1, source_target_pairs={{0,24},{8,16},{16,8},{24,0},{1,25},{9,17},{17,9},{25,1},{2,26},{10... | collective-permute-start | bytes 393224 | tf_op jit(solution)/shard_map/ppermute | solution.py:285
  86.6 2.2 %collective-permute-start.18 = (bf16[2,128,256]{2,1,0:T(8,128)(2,1)S(1)}, bf16[2,128,256]{2,1,0:T(8,128)(2,1)S(1)}, u32[]{:S(2)}, u32[]{:S(2)}) collective-permute-start(bf16[2,128,256]{2,1,0:T(8,128)(2,1)S(1)} %get-tuple-element.80), channel_id=1, source_target_pairs={{0,24},{8,16},{16,8},{24,0},{1,25},{9,17},{17,9},{25,1},{2,26},{10... | collective-permute-start | bytes 393224 | tf_op jit(solution)/shard_map/ppermute | solution.py:285
  90.3 1.9 %collective-permute-done.16.refs_3_ = bf16[2,128,256]{2,1,0:T(8,128)(2,1)S(1)} collective-permute-done((bf16[2,128,256]{2,1,0:T(8,128)(2,1)S(1)}, bf16[2,128,256]{2,1,0:T(8,128)(2,1)S(1)}, u32[]{:S(2)}, u32[]{:S(2)}) %collective-permute-start.16) | collective-permute-done | bytes 131104 | tf_op jit(solution)/shard_map/ppermute | solution.py:285
  92.3 2.3 %collective-permute-done.18.refs_5_ = bf16[2,128,256]{2,1,0:T(8,128)(2,1)S(1)} collective-permute-done((bf16[2,128,256]{2,1,0:T(8,128)(2,1)S(1)}, bf16[2,128,256]{2,1,0:T(8,128)(2,1)S(1)}, u32[]{:S(2)}, u32[]{:S(2)}) %collective-permute-start.18) | collective-permute-done | bytes 131104 | tf_op jit(solution)/shard_map/ppermute | solution.py:285
  94.7 1.6 forward.7
  96.3 1.6 collective-permute-start.30
  99.8 5.7 %collective-permute-done.30.refs_1_ = bf16[128,1024]{1,0:T(8,128)(2,1)S(1)} collective-permute-done((bf16[128,1024]{1,0:T(8,128)(2,1)S(1)}, bf16[128,1024]{1,0:T(8,128)(2,1)S(1)}, u32[]{:S(2)}, u32[]{:S(2)}) %collective-permute-start.30) | collective-permute-done | bytes 262176 | tf_op jit(solution)/shard_map/ppermute | solution.py:285
  105.6 5.5 %collective-permute-done.31.refs_2_ = bf16[128,1024]{1,0:T(8,128)(2,1)S(1)} collective-permute-done((bf16[128,1024]{1,0:T(8,128)(2,1)S(1)}, bf16[128,1024]{1,0:T(8,128)(2,1)S(1)}, u32[]{:S(2)}, u32[]{:S(2)}) %collective-permute-start.31) | collective-permute-done | bytes 262176 | tf_op jit(solution)/shard_map/ppermute | solution.py:285
  111.4 1.8 collective-permute-start.34
  114.0 6.6 %collective-permute-done.34.come_ref = bf16[512,256]{1,0:T(8,128)(2,1)S(1)} collective-permute-done((bf16[512,256]{1,0:T(8,128)(2,1)S(1)}, bf16[512,256]{1,0:T(8,128)(2,1)S(1)}, u32[]{:S(2)}, u32[]{:S(2)}) %collective-permute-start.34) | collective-permute-done | bytes 262176 | tf_op jit(solution)/shard_map/ppermute | solution.py:288
  120.7 3.6 %collective-permute-start.35 = (bf16[512,256]{1,0:T(8,128)(2,1)S(1)}, bf16[512,256]{1,0:T(8,128)(2,1)S(1)}, u32[]{:S(2)}, u32[]{:S(2)}) collective-permute-start(bf16[512,256]{1,0:T(8,128)(2,1)S(1)} %pass.4), channel_id=1, source_target_pairs={{0,6},{2,0},{4,2},{6,4},{1,7},{3,1},{5,3},{7,5},{8,14},{10,8},{12,... | collective-permute-start | bytes 786440 | tf_op jit(solution)/shard_map/ppermute | solution.py:288
  124.2 2.0 %collective-permute-done.37.come_ref = bf16[512,256]{1,0:T(8,128)(2,1)S(1)} collective-permute-done((bf16[512,256]{1,0:T(8,128)(2,1)S(1)}, bf16[512,256]{1,0:T(8,128)(2,1)S(1)}, u32[]{:S(2)}, u32[]{:S(2)}) %collective-permute-start.37) | collective-permute-done | bytes 262176 | tf_op jit(solution)/shard_map/ppermute | solution.py:288
  126.3 3.6 %collective-permute-start.38 = (bf16[512,256]{1,0:T(8,128)(2,1)S(1)}, bf16[512,256]{1,0:T(8,128)(2,1)S(1)}, u32[]{:S(2)}, u32[]{:S(2)}) collective-permute-start(bf16[512,256]{1,0:T(8,128)(2,1)S(1)} %pass.6), channel_id=1, source_target_pairs={{0,6},{2,0},{4,2},{6,4},{1,7},{3,1},{5,3},{7,5},{8,14},{10,8},{12,... | collective-permute-start | bytes 786440 | tf_op jit(solution)/shard_map/ppermute | solution.py:288
  131.9 3.6 %collective-permute-start.36 = (bf16[512,256]{1,0:T(8,128)(2,1)S(1)}, bf16[512,256]{1,0:T(8,128)(2,1)S(1)}, u32[]{:S(2)}, u32[]{:S(2)}) collective-permute-start(bf16[512,256]{1,0:T(8,128)(2,1)S(1)} %pass.5), channel_id=1, source_target_pairs={{0,6},{2,0},{4,2},{6,4},{1,7},{3,1},{5,3},{7,5},{8,14},{10,8},{12,... | collective-permute-start | bytes 786440 | tf_op jit(solution)/shard_map/ppermute | solution.py:288
  135.5 2.0 %collective-permute-done.38.come_ref = bf16[512,256]{1,0:T(8,128)(2,1)S(1)} collective-permute-done((bf16[512,256]{1,0:T(8,128)(2,1)S(1)}, bf16[512,256]{1,0:T(8,128)(2,1)S(1)}, u32[]{:S(2)}, u32[]{:S(2)}) %collective-permute-start.38) | collective-permute-done | bytes 262176 | tf_op jit(solution)/shard_map/ppermute | solution.py:288
  137.5 3.8 %collective-permute-start.39 = (bf16[512,256]{1,0:T(8,128)(2,1)S(1)}, bf16[512,256]{1,0:T(8,128)(2,1)S(1)}, u32[]{:S(2)}, u32[]{:S(2)}) collective-permute-start(bf16[512,256]{1,0:T(8,128)(2,1)S(1)} %pass.7), channel_id=1, source_target_pairs={{0,6},{2,0},{4,2},{6,4},{1,7},{3,1},{5,3},{7,5},{8,14},{10,8},{12,... | collective-permute-start | bytes 786440 | tf_op jit(solution)/shard_map/ppermute | solution.py:288
  143.1 5.2 %collective-permute-done.39.refs_6_ = bf16[512,256]{1,0:T(8,128)(2,1)S(1)} collective-permute-done((bf16[512,256]{1,0:T(8,128)(2,1)S(1)}, bf16[512,256]{1,0:T(8,128)(2,1)S(1)}, u32[]{:S(2)}, u32[]{:S(2)}) %collective-permute-start.39) | collective-permute-done | bytes 262176 | tf_op jit(solution)/shard_map/ppermute | solution.py:288
  151.4 1.7 collective-permute-start.42
  153.1 2.6 %collective-permute-done.40.refs_1_ = bf16[256,256]{1,0:T(8,128)(2,1)S(1)} collective-permute-done((bf16[256,256]{1,0:T(8,128)(2,1)S(1)}, bf16[256,256]{1,0:T(8,128)(2,1)S(1)}, u32[]{:S(2)}, u32[]{:S(2)}) %collective-permute-start.40) | collective-permute-done | bytes 131104 | tf_op jit(solution)/shard_map/ppermute | solution.py:285
  155.7 2.6 %collective-permute-done.41.refs_2_ = bf16[256,256]{1,0:T(8,128)(2,1)S(1)} collective-permute-done((bf16[256,256]{1,0:T(8,128)(2,1)S(1)}, bf16[256,256]{1,0:T(8,128)(2,1)S(1)}, u32[]{:S(2)}, u32[]{:S(2)}) %collective-permute-start.41) | collective-permute-done | bytes 131104 | tf_op jit(solution)/shard_map/ppermute | solution.py:285
  158.5 5.0 %collective-permute-done.43.refs_1_ = bf16[256,256]{1,0:T(8,128)(2,1)S(1)} collective-permute-done((bf16[256,256]{1,0:T(8,128)(2,1)S(1)}, bf16[256,256]{1,0:T(8,128)(2,1)S(1)}, u32[]{:S(2)}, u32[]{:S(2)}) %collective-permute-start.43) | collective-permute-done | bytes 131104 | tf_op jit(solution)/shard_map/ppermute | solution.py:422
  163.5 2.1 %collective-permute-start.44 = (bf16[256,256]{1,0:T(8,128)(2,1)S(1)}, bf16[256,256]{1,0:T(8,128)(2,1)S(1)}, u32[]{:S(2)}, u32[]{:S(2)}) collective-permute-start(bf16[256,256]{1,0:T(8,128)(2,1)S(1)} %sum.4.refs_0_), channel_id=1, source_target_pairs={{0,4},{2,6},{4,0},{6,2},{1,5},{3,7},{5,1},{7,3},{8,12},{10,14},{12... | collective-permute-start | bytes 393224 | tf_op jit(solution)/shard_map/ppermute | solution.py:422
  165.5 5.3 %collective-permute-done.44.refs_1_ = bf16[256,256]{1,0:T(8,128)(2,1)S(1)} collective-permute-done((bf16[256,256]{1,0:T(8,128)(2,1)S(1)}, bf16[256,256]{1,0:T(8,128)(2,1)S(1)}, u32[]{:S(2)}, u32[]{:S(2)}) %collective-permute-start.44) | collective-permute-done | bytes 131104 | tf_op jit(solution)/shard_map/ppermute | solution.py:422
  174.4 1.5 collective-permute-done.45.refs_2_
  177.0 2.0 %collective-permute-done.47.refs_4_ = bf16[256,256]{1,0:T(8,128)(2,1)S(1)} collective-permute-done((bf16[256,256]{1,0:T(8,128)(2,1)S(1)}, bf16[256,256]{1,0:T(8,128)(2,1)S(1)}, u32[]{:S(2)}, u32[]{:S(2)}) %collective-permute-start.47) | collective-permute-done | bytes 131104 | tf_op jit(solution)/shard_map/ppermute | solution.py:285
  180.4 2.0 %last.1 = f32[1024,512]{1,0:T(8,128)} custom-call(s32[3]{0:T(128)S(1)} %pad_add_fusion.1.refs_0_, bf16[256,256]{1,0:T(8,128)(2,1)S(1)} %sum.5.refs_1_, bf16[256,256]{1,0:T(8,128)(2,1)S(1)} %collective-permute-done.45.refs_2_, bf16[256,256]{1,0:T(8,128)(2,1)S(1)} %collective-permute-done.46.refs_3_, bf16[256,256]{1,0:T(8,128)(2,1)S(1)} %collective-permute-done.47.refs_4_, ...), custom_call_target="tpu_custom_call" | custom-call | flops 2000000000 | tf_op jit(solution)/shard_map/last/pallas_call | solution.py:37
  (149 shorter events, 41.0 us)
Async XLA Ops:
  0.6 69.0 %collective-permute-start.5 = (bf16[4,16,128,128]{3,2,1,0:T(8,128)(2,1)}, bf16[4,16,128,128]{3,2,1,0:T(8,128)(2,1)}, u32[]{:S(2)}, u32[]{:S(2)}) collective-permute-start(bf16[4,16,128,128]{3,2,1,0:T(8,128)(2,1)} %vals_ref.1), channel_id=1, source_target_pairs={{0,1},{1,0},{2,3},{3,2},{4,5},{5,4},{6,7},{7,6},{8,9},{9,8},{10,11... | collective-permute-start | bytes 6291464 | tf_op jit(solution)/shard_map/ppermute | solution.py:282
  2.9 14.9 %collective-permute-start = (s32[2,512]{1,0:T(2,128)S(1)}, s32[2,512]{1,0:T(2,128)S(1)}, u32[]{:S(2)}, u32[]{:S(2)}) collective-permute-start(s32[2,512]{1,0:T(2,128)S(1)} %index.1), channel_id=1, source_target_pairs={{0,2},{2,4},{4,6},{6,0},{1,3},{3,5},{5,7},{7,1},{8,10},{10,12},{12... | collective-permute-start | bytes 12296 | tf_op jit(solution)/shard_map/ppermute | solution.py:288
  5.6 12.9 %collective-permute-start.1 = (s32[2,512]{1,0:T(2,128)S(1)}, s32[2,512]{1,0:T(2,128)S(1)}, u32[]{:S(2)}, u32[]{:S(2)}) collective-permute-start(s32[2,512]{1,0:T(2,128)S(1)} %index.1), channel_id=1, source_target_pairs={{0,4},{2,6},{4,0},{6,2},{1,5},{3,7},{5,1},{7,3},{8,12},{10,14},{12... | collective-permute-start | bytes 12296 | tf_op jit(solution)/shard_map/ppermute | solution.py:288
  8.2 10.4 %collective-permute-start.2 = (s32[2,512]{1,0:T(2,128)S(1)}, s32[2,512]{1,0:T(2,128)S(1)}, u32[]{:S(2)}, u32[]{:S(2)}) collective-permute-start(s32[2,512]{1,0:T(2,128)S(1)} %index.1), channel_id=1, source_target_pairs={{0,6},{2,0},{4,2},{6,4},{1,7},{3,1},{5,3},{7,5},{8,14},{10,8},{12,... | collective-permute-start | bytes 12296 | tf_op jit(solution)/shard_map/ppermute | solution.py:288
  13.2 5.6 %collective-permute-start.12 = (bf16[512,256]{1,0:T(8,128)(2,1)S(1)}, bf16[512,256]{1,0:T(8,128)(2,1)S(1)}, u32[]{:S(2)}, u32[]{:S(2)}) collective-permute-start(bf16[512,256]{1,0:T(8,128)(2,1)S(1)} %get-tuple-element.76), channel_id=1, source_target_pairs={{0,1},{1,0},{2,3},{3,2},{4,5},{5,4},{6,7},{7,6},{8,9},{9,8},{10,11... | collective-permute-start | bytes 786440 | tf_op jit(solution)/shard_map/ppermute | solution.py:282
  17.8 10.9 %collective-permute-start.9 = (bf16[512,256]{1,0:T(8,128)(2,1)S(1)}, bf16[512,256]{1,0:T(8,128)(2,1)S(1)}, u32[]{:S(2)}, u32[]{:S(2)}) collective-permute-start(bf16[512,256]{1,0:T(8,128)(2,1)S(1)} %get-tuple-element.75.refs_2_), channel_id=1, source_target_pairs={{0,2},{2,4},{4,6},{6,0},{1,3},{3,5},{5,7},{7,1},{8,10},{10,12},{12... | collective-permute-start | bytes 786440 | tf_op jit(solution)/shard_map/ppermute | solution.py:288
  18.8 15.6 %collective-permute-start.13 = (bf16[512,256]{1,0:T(8,128)(2,1)S(1)}, bf16[512,256]{1,0:T(8,128)(2,1)S(1)}, u32[]{:S(2)}, u32[]{:S(2)}) collective-permute-start(bf16[512,256]{1,0:T(8,128)(2,1)S(1)} %collective-permute-done.12.refs_3_), channel_id=1, source_target_pairs={{0,2},{2,4},{4,6},{6,0},{1,3},{3,5},{5,7},{7,1},{8,10},{10,12},{12... | collective-permute-start | bytes 786440 | tf_op jit(solution)/shard_map/ppermute | solution.py:288
  19.8 4.6 %collective-permute-start.6 = (s32[16,512]{1,0:T(8,128)S(1)}, s32[16,512]{1,0:T(8,128)S(1)}, u32[]{:S(2)}, u32[]{:S(2)}) collective-permute-start(s32[16,512]{1,0:T(8,128)S(1)} %concatenate.15.refs_1_), channel_id=1, source_target_pairs={{0,8},{8,0},{16,24},{24,16},{1,9},{9,1},{17,25},{25,17},{2,10},{10... | collective-permute-start | bytes 98312 | tf_op jit(solution)/shard_map/ppermute | solution.py:285
  22.8 24.3 %collective-permute-start.7 = (s32[16,512]{1,0:T(8,128)S(1)}, s32[16,512]{1,0:T(8,128)S(1)}, u32[]{:S(2)}, u32[]{:S(2)}) collective-permute-start(s32[16,512]{1,0:T(8,128)S(1)} %concatenate.15.refs_1_), channel_id=1, source_target_pairs={{0,16},{8,24},{16,0},{24,8},{1,17},{9,25},{17,1},{25,9},{2,18},{10... | collective-permute-start | bytes 98312 | tf_op jit(solution)/shard_map/ppermute | solution.py:285
  24.4 22.7 %collective-permute-start.8 = (s32[16,512]{1,0:T(8,128)S(1)}, s32[16,512]{1,0:T(8,128)S(1)}, u32[]{:S(2)}, u32[]{:S(2)}) collective-permute-start(s32[16,512]{1,0:T(8,128)S(1)} %concatenate.15.refs_1_), channel_id=1, source_target_pairs={{0,24},{8,16},{16,8},{24,0},{1,25},{9,17},{17,9},{25,1},{2,26},{10... | collective-permute-start | bytes 98312 | tf_op jit(solution)/shard_map/ppermute | solution.py:285
  28.7 20.9 %collective-permute-start.10 = (bf16[512,256]{1,0:T(8,128)(2,1)S(1)}, bf16[512,256]{1,0:T(8,128)(2,1)S(1)}, u32[]{:S(2)}, u32[]{:S(2)}) collective-permute-start(bf16[512,256]{1,0:T(8,128)(2,1)S(1)} %collective-permute-done.9.refs_1_), channel_id=1, source_target_pairs={{0,2},{2,4},{4,6},{6,0},{1,3},{3,5},{5,7},{7,1},{8,10},{10,12},{12... | collective-permute-start | bytes 786440 | tf_op jit(solution)/shard_map/ppermute | solution.py:288
  34.4 15.4 %collective-permute-start.14 = (bf16[512,256]{1,0:T(8,128)(2,1)S(1)}, bf16[512,256]{1,0:T(8,128)(2,1)S(1)}, u32[]{:S(2)}, u32[]{:S(2)}) collective-permute-start(bf16[512,256]{1,0:T(8,128)(2,1)S(1)} %collective-permute-done.13.refs_2_), channel_id=1, source_target_pairs={{0,2},{2,4},{4,6},{6,0},{1,3},{3,5},{5,7},{7,1},{8,10},{10,12},{12... | collective-permute-start | bytes 786440 | tf_op jit(solution)/shard_map/ppermute | solution.py:288
  47.1 21.9 %collective-permute-start.4 = (s32[4,16]{1,0:T(4,128)S(1)}, s32[4,16]{1,0:T(4,128)S(1)}, u32[]{:S(2)}, u32[]{:S(2)}) collective-permute-start(s32[4,16]{1,0:T(4,128)S(1)} %fusion.cols_ref), channel_id=1, source_target_pairs={{0,1},{1,0},{2,3},{3,2},{4,5},{5,4},{6,7},{7,6},{8,9},{9,8},{10,11... | collective-permute-start | bytes 776 | tf_op jit(solution)/shard_map/ppermute | solution.py:282
  49.7 11.0 %collective-permute-start.11 = (bf16[512,256]{1,0:T(8,128)(2,1)S(1)}, bf16[512,256]{1,0:T(8,128)(2,1)S(1)}, u32[]{:S(2)}, u32[]{:S(2)}) collective-permute-start(bf16[512,256]{1,0:T(8,128)(2,1)S(1)} %collective-permute-done.10.refs_1_), channel_id=1, source_target_pairs={{0,2},{2,4},{4,6},{6,0},{1,3},{3,5},{5,7},{7,1},{8,10},{10,12},{12... | collective-permute-start | bytes 786440 | tf_op jit(solution)/shard_map/ppermute | solution.py:288
  49.7 16.4 %collective-permute-start.15 = (bf16[512,256]{1,0:T(8,128)(2,1)S(1)}, bf16[512,256]{1,0:T(8,128)(2,1)S(1)}, u32[]{:S(2)}, u32[]{:S(2)}) collective-permute-start(bf16[512,256]{1,0:T(8,128)(2,1)S(1)} %collective-permute-done.14.refs_2_), channel_id=1, source_target_pairs={{0,2},{2,4},{4,6},{6,0},{1,3},{3,5},{5,7},{7,1},{8,10},{10,12},{12... | collective-permute-start | bytes 786440 | tf_op jit(solution)/shard_map/ppermute | solution.py:288
  52.7 21.2 %collective-permute-start.25 = (bf16[2,128,256]{2,1,0:T(8,128)(2,1)S(1)}, bf16[2,128,256]{2,1,0:T(8,128)(2,1)S(1)}, u32[]{:S(2)}, u32[]{:S(2)}) collective-permute-start(bf16[2,128,256]{2,1,0:T(8,128)(2,1)S(1)} %get-tuple-element.98), channel_id=1, source_target_pairs={{0,8},{8,0},{16,24},{24,16},{1,9},{9,1},{17,25},{25,17},{2,10},{10... | collective-permute-start | bytes 393224 | tf_op jit(solution)/shard_map/ppermute | solution.py:285
  60.7 15.4 %collective-permute-start.26 = (bf16[2,128,256]{2,1,0:T(8,128)(2,1)S(1)}, bf16[2,128,256]{2,1,0:T(8,128)(2,1)S(1)}, u32[]{:S(2)}, u32[]{:S(2)}) collective-permute-start(bf16[2,128,256]{2,1,0:T(8,128)(2,1)S(1)} %get-tuple-element.99), channel_id=1, source_target_pairs={{0,16},{8,24},{16,0},{24,8},{1,17},{9,25},{17,1},{25,9},{2,18},{10... | collective-permute-start | bytes 393224 | tf_op jit(solution)/shard_map/ppermute | solution.py:285
  66.1 10.5 %collective-permute-start.27 = (bf16[2,128,256]{2,1,0:T(8,128)(2,1)S(1)}, bf16[2,128,256]{2,1,0:T(8,128)(2,1)S(1)}, u32[]{:S(2)}, u32[]{:S(2)}) collective-permute-start(bf16[2,128,256]{2,1,0:T(8,128)(2,1)S(1)} %get-tuple-element.100), channel_id=1, source_target_pairs={{0,24},{8,16},{16,8},{24,0},{1,25},{9,17},{17,9},{25,1},{2,26},{10... | collective-permute-start | bytes 393224 | tf_op jit(solution)/shard_map/ppermute | solution.py:285
  69.0 13.1 %collective-permute-start.22 = (bf16[2,128,256]{2,1,0:T(8,128)(2,1)S(1)}, bf16[2,128,256]{2,1,0:T(8,128)(2,1)S(1)}, u32[]{:S(2)}, u32[]{:S(2)}) collective-permute-start(bf16[2,128,256]{2,1,0:T(8,128)(2,1)S(1)} %get-tuple-element.92), channel_id=1, source_target_pairs={{0,8},{8,0},{16,24},{24,16},{1,9},{9,1},{17,25},{25,17},{2,10},{10... | collective-permute-start | bytes 393224 | tf_op jit(solution)/shard_map/ppermute | solution.py:285
  69.6 12.6 %collective-permute-start.23 = (bf16[2,128,256]{2,1,0:T(8,128)(2,1)S(1)}, bf16[2,128,256]{2,1,0:T(8,128)(2,1)S(1)}, u32[]{:S(2)}, u32[]{:S(2)}) collective-permute-start(bf16[2,128,256]{2,1,0:T(8,128)(2,1)S(1)} %get-tuple-element.93), channel_id=1, source_target_pairs={{0,16},{8,24},{16,0},{24,8},{1,17},{9,25},{17,1},{25,9},{2,18},{10... | collective-permute-start | bytes 393224 | tf_op jit(solution)/shard_map/ppermute | solution.py:285
  73.8 11.4 %collective-permute-start.24 = (bf16[2,128,256]{2,1,0:T(8,128)(2,1)S(1)}, bf16[2,128,256]{2,1,0:T(8,128)(2,1)S(1)}, u32[]{:S(2)}, u32[]{:S(2)}) collective-permute-start(bf16[2,128,256]{2,1,0:T(8,128)(2,1)S(1)} %get-tuple-element.94), channel_id=1, source_target_pairs={{0,24},{8,16},{16,8},{24,0},{1,25},{9,17},{17,9},{25,1},{2,26},{10... | collective-permute-start | bytes 393224 | tf_op jit(solution)/shard_map/ppermute | solution.py:285
  76.1 9.8 %collective-permute-start.19 = (bf16[2,128,256]{2,1,0:T(8,128)(2,1)S(1)}, bf16[2,128,256]{2,1,0:T(8,128)(2,1)S(1)}, u32[]{:S(2)}, u32[]{:S(2)}) collective-permute-start(bf16[2,128,256]{2,1,0:T(8,128)(2,1)S(1)} %get-tuple-element.85), channel_id=1, source_target_pairs={{0,8},{8,0},{16,24},{24,16},{1,9},{9,1},{17,25},{25,17},{2,10},{10... | collective-permute-start | bytes 393224 | tf_op jit(solution)/shard_map/ppermute | solution.py:285
  76.7 10.0 %collective-permute-start.20 = (bf16[2,128,256]{2,1,0:T(8,128)(2,1)S(1)}, bf16[2,128,256]{2,1,0:T(8,128)(2,1)S(1)}, u32[]{:S(2)}, u32[]{:S(2)}) collective-permute-start(bf16[2,128,256]{2,1,0:T(8,128)(2,1)S(1)} %get-tuple-element.86), channel_id=1, source_target_pairs={{0,16},{8,24},{16,0},{24,8},{1,17},{9,25},{17,1},{25,9},{2,18},{10... | collective-permute-start | bytes 393224 | tf_op jit(solution)/shard_map/ppermute | solution.py:285
  82.2 8.1 %collective-permute-start.28 = (bf16[512,256]{1,0:T(8,128)(2,1)S(1)}, bf16[512,256]{1,0:T(8,128)(2,1)S(1)}, u32[]{:S(2)}, u32[]{:S(2)}) collective-permute-start(bf16[512,256]{1,0:T(8,128)(2,1)S(1)} %get-tuple-element.144), channel_id=1, source_target_pairs={{0,1},{1,0},{2,3},{3,2},{4,5},{5,4},{6,7},{7,6},{8,9},{9,8},{10,11... | collective-permute-start | bytes 786440 | tf_op jit(solution)/shard_map/ppermute | solution.py:282
  82.3 7.3 %collective-permute-start.21 = (bf16[2,128,256]{2,1,0:T(8,128)(2,1)S(1)}, bf16[2,128,256]{2,1,0:T(8,128)(2,1)S(1)}, u32[]{:S(2)}, u32[]{:S(2)}) collective-permute-start(bf16[2,128,256]{2,1,0:T(8,128)(2,1)S(1)} %get-tuple-element.87), channel_id=1, source_target_pairs={{0,24},{8,16},{16,8},{24,0},{1,25},{9,17},{17,9},{25,1},{2,26},{10... | collective-permute-start | bytes 393224 | tf_op jit(solution)/shard_map/ppermute | solution.py:285
  85.3 6.9 %collective-permute-start.16 = (bf16[2,128,256]{2,1,0:T(8,128)(2,1)S(1)}, bf16[2,128,256]{2,1,0:T(8,128)(2,1)S(1)}, u32[]{:S(2)}, u32[]{:S(2)}) collective-permute-start(bf16[2,128,256]{2,1,0:T(8,128)(2,1)S(1)} %get-tuple-element.78), channel_id=1, source_target_pairs={{0,8},{8,0},{16,24},{24,16},{1,9},{9,1},{17,25},{25,17},{2,10},{10... | collective-permute-start | bytes 393224 | tf_op jit(solution)/shard_map/ppermute | solution.py:285
  85.9 6.5 %collective-permute-start.17 = (bf16[2,128,256]{2,1,0:T(8,128)(2,1)S(1)}, bf16[2,128,256]{2,1,0:T(8,128)(2,1)S(1)}, u32[]{:S(2)}, u32[]{:S(2)}) collective-permute-start(bf16[2,128,256]{2,1,0:T(8,128)(2,1)S(1)} %get-tuple-element.79), channel_id=1, source_target_pairs={{0,16},{8,24},{16,0},{24,8},{1,17},{9,25},{17,1},{25,9},{2,18},{10... | collective-permute-start | bytes 393224 | tf_op jit(solution)/shard_map/ppermute | solution.py:285
  86.6 8.0 %collective-permute-start.18 = (bf16[2,128,256]{2,1,0:T(8,128)(2,1)S(1)}, bf16[2,128,256]{2,1,0:T(8,128)(2,1)S(1)}, u32[]{:S(2)}, u32[]{:S(2)}) collective-permute-start(bf16[2,128,256]{2,1,0:T(8,128)(2,1)S(1)} %get-tuple-element.80), channel_id=1, source_target_pairs={{0,24},{8,16},{16,8},{24,0},{1,25},{9,17},{17,9},{25,1},{2,26},{10... | collective-permute-start | bytes 393224 | tf_op jit(solution)/shard_map/ppermute | solution.py:285
  96.3 9.3 %collective-permute-start.30 = (bf16[128,1024]{1,0:T(8,128)(2,1)S(1)}, bf16[128,1024]{1,0:T(8,128)(2,1)S(1)}, u32[]{:S(2)}, u32[]{:S(2)}) collective-permute-start(bf16[128,1024]{1,0:T(8,128)(2,1)S(1)} %get-tuple-element.119), channel_id=1, source_target_pairs={{0,8},{8,0},{16,24},{24,16},{1,9},{9,1},{17,25},{25,17},{2,10},{10... | collective-permute-start | bytes 786440 | tf_op jit(solution)/shard_map/ppermute | solution.py:285
  97.8 13.2 %collective-permute-start.31 = (bf16[128,1024]{1,0:T(8,128)(2,1)S(1)}, bf16[128,1024]{1,0:T(8,128)(2,1)S(1)}, u32[]{:S(2)}, u32[]{:S(2)}) collective-permute-start(bf16[128,1024]{1,0:T(8,128)(2,1)S(1)} %get-tuple-element.120), channel_id=1, source_target_pairs={{0,16},{8,24},{16,0},{24,8},{1,17},{9,25},{17,1},{25,9},{2,18},{10... | collective-permute-start | bytes 786440 | tf_op jit(solution)/shard_map/ppermute | solution.py:285
  99.1 11.9 %collective-permute-start.32 = (bf16[128,1024]{1,0:T(8,128)(2,1)S(1)}, bf16[128,1024]{1,0:T(8,128)(2,1)S(1)}, u32[]{:S(2)}, u32[]{:S(2)}) collective-permute-start(bf16[128,1024]{1,0:T(8,128)(2,1)S(1)} %get-tuple-element.121), channel_id=1, source_target_pairs={{0,24},{8,16},{16,8},{24,0},{1,25},{9,17},{17,9},{25,1},{2,26},{10... | collective-permute-start | bytes 786440 | tf_op jit(solution)/shard_map/ppermute | solution.py:285
  111.4 36.9 %collective-permute-start.33 = (bf16[1024,512]{1,0:T(8,128)(2,1)S(1)}, bf16[1024,512]{1,0:T(8,128)(2,1)S(1)}, u32[]{:S(2)}, u32[]{:S(2)}) collective-permute-start(bf16[1024,512]{1,0:T(8,128)(2,1)S(1)} %turn.1.refs_1_), channel_id=1, source_target_pairs={{0,1},{1,0},{2,3},{3,2},{4,5},{5,4},{6,7},{7,6},{8,9},{9,8},{10,11... | collective-permute-start | bytes 3145736 | tf_op jit(solution)/shard_map/ppermute | solution.py:282
  111.4 9.2 %collective-permute-start.34 = (bf16[512,256]{1,0:T(8,128)(2,1)S(1)}, bf16[512,256]{1,0:T(8,128)(2,1)S(1)}, u32[]{:S(2)}, u32[]{:S(2)}) collective-permute-start(bf16[512,256]{1,0:T(8,128)(2,1)S(1)} %get-tuple-element.134), channel_id=1, source_target_pairs={{0,6},{2,0},{4,2},{6,4},{1,7},{3,1},{5,3},{7,5},{8,14},{10,8},{12,... | collective-permute-start | bytes 786440 | tf_op jit(solution)/shard_map/ppermute | solution.py:288
  113.2 13.0 %collective-permute-start.37 = (bf16[512,256]{1,0:T(8,128)(2,1)S(1)}, bf16[512,256]{1,0:T(8,128)(2,1)S(1)}, u32[]{:S(2)}, u32[]{:S(2)}) collective-permute-start(bf16[512,256]{1,0:T(8,128)(2,1)S(1)} %get-tuple-element.137), channel_id=1, source_target_pairs={{0,6},{2,0},{4,2},{6,4},{1,7},{3,1},{5,3},{7,5},{8,14},{10,8},{12,... | collective-permute-start | bytes 786440 | tf_op jit(solution)/shard_map/ppermute | solution.py:288
  120.7 11.2 %collective-permute-start.35 = (bf16[512,256]{1,0:T(8,128)(2,1)S(1)}, bf16[512,256]{1,0:T(8,128)(2,1)S(1)}, u32[]{:S(2)}, u32[]{:S(2)}) collective-permute-start(bf16[512,256]{1,0:T(8,128)(2,1)S(1)} %pass.4), channel_id=1, source_target_pairs={{0,6},{2,0},{4,2},{6,4},{1,7},{3,1},{5,3},{7,5},{8,14},{10,8},{12,... | collective-permute-start | bytes 786440 | tf_op jit(solution)/shard_map/ppermute | solution.py:288
  126.3 11.2 %collective-permute-start.38 = (bf16[512,256]{1,0:T(8,128)(2,1)S(1)}, bf16[512,256]{1,0:T(8,128)(2,1)S(1)}, u32[]{:S(2)}, u32[]{:S(2)}) collective-permute-start(bf16[512,256]{1,0:T(8,128)(2,1)S(1)} %pass.6), channel_id=1, source_target_pairs={{0,6},{2,0},{4,2},{6,4},{1,7},{3,1},{5,3},{7,5},{8,14},{10,8},{12,... | collective-permute-start | bytes 786440 | tf_op jit(solution)/shard_map/ppermute | solution.py:288
  131.9 11.2 %collective-permute-start.36 = (bf16[512,256]{1,0:T(8,128)(2,1)S(1)}, bf16[512,256]{1,0:T(8,128)(2,1)S(1)}, u32[]{:S(2)}, u32[]{:S(2)}) collective-permute-start(bf16[512,256]{1,0:T(8,128)(2,1)S(1)} %pass.5), channel_id=1, source_target_pairs={{0,6},{2,0},{4,2},{6,4},{1,7},{3,1},{5,3},{7,5},{8,14},{10,8},{12,... | collective-permute-start | bytes 786440 | tf_op jit(solution)/shard_map/ppermute | solution.py:288
  137.5 10.7 %collective-permute-start.39 = (bf16[512,256]{1,0:T(8,128)(2,1)S(1)}, bf16[512,256]{1,0:T(8,128)(2,1)S(1)}, u32[]{:S(2)}, u32[]{:S(2)}) collective-permute-start(bf16[512,256]{1,0:T(8,128)(2,1)S(1)} %pass.7), channel_id=1, source_target_pairs={{0,6},{2,0},{4,2},{6,4},{1,7},{3,1},{5,3},{7,5},{8,14},{10,8},{12,... | collective-permute-start | bytes 786440 | tf_op jit(solution)/shard_map/ppermute | solution.py:288
  149.6 6.1 %collective-permute-start.40 = (bf16[256,256]{1,0:T(8,128)(2,1)S(1)}, bf16[256,256]{1,0:T(8,128)(2,1)S(1)}, u32[]{:S(2)}, u32[]{:S(2)}) collective-permute-start(bf16[256,256]{1,0:T(8,128)(2,1)S(1)} %get-tuple-element.139), channel_id=1, source_target_pairs={{0,8},{8,0},{16,24},{24,16},{1,9},{9,1},{17,25},{25,17},{2,10},{10... | collective-permute-start | bytes 393224 | tf_op jit(solution)/shard_map/ppermute | solution.py:285
  150.6 7.7 %collective-permute-start.41 = (bf16[256,256]{1,0:T(8,128)(2,1)S(1)}, bf16[256,256]{1,0:T(8,128)(2,1)S(1)}, u32[]{:S(2)}, u32[]{:S(2)}) collective-permute-start(bf16[256,256]{1,0:T(8,128)(2,1)S(1)} %get-tuple-element.140), channel_id=1, source_target_pairs={{0,16},{8,24},{16,0},{24,8},{1,17},{9,25},{17,1},{25,9},{2,18},{10... | collective-permute-start | bytes 393224 | tf_op jit(solution)/shard_map/ppermute | solution.py:285
  151.4 6.9 %collective-permute-start.42 = (bf16[256,256]{1,0:T(8,128)(2,1)S(1)}, bf16[256,256]{1,0:T(8,128)(2,1)S(1)}, u32[]{:S(2)}, u32[]{:S(2)}) collective-permute-start(bf16[256,256]{1,0:T(8,128)(2,1)S(1)} %get-tuple-element.141), channel_id=1, source_target_pairs={{0,24},{8,16},{16,8},{24,0},{1,25},{9,17},{17,9},{25,1},{2,26},{10... | collective-permute-start | bytes 393224 | tf_op jit(solution)/shard_map/ppermute | solution.py:285
  158.4 5.0 %collective-permute-start.43 = (bf16[256,256]{1,0:T(8,128)(2,1)S(1)}, bf16[256,256]{1,0:T(8,128)(2,1)S(1)}, u32[]{:S(2)}, u32[]{:S(2)}) collective-permute-start(bf16[256,256]{1,0:T(8,128)(2,1)S(1)} %sum.3.refs_0_), channel_id=1, source_target_pairs={{0,2},{2,0},{4,6},{6,4},{1,3},{3,1},{5,7},{7,5},{8,10},{10,8},{12,... | collective-permute-start | bytes 393224 | tf_op jit(solution)/shard_map/ppermute | solution.py:422
  163.5 7.3 %collective-permute-start.44 = (bf16[256,256]{1,0:T(8,128)(2,1)S(1)}, bf16[256,256]{1,0:T(8,128)(2,1)S(1)}, u32[]{:S(2)}, u32[]{:S(2)}) collective-permute-start(bf16[256,256]{1,0:T(8,128)(2,1)S(1)} %sum.4.refs_0_), channel_id=1, source_target_pairs={{0,4},{2,6},{4,0},{6,2},{1,5},{3,7},{5,1},{7,3},{8,12},{10,14},{12... | collective-permute-start | bytes 393224 | tf_op jit(solution)/shard_map/ppermute | solution.py:422
  165.5 13.5 %collective-permute-start.29 = (bf16[512,256]{1,0:T(8,128)(2,1)S(1)}, bf16[512,256]{1,0:T(8,128)(2,1)S(1)}, u32[]{:S(2)}, u32[]{:S(2)}) collective-permute-start(bf16[512,256]{1,0:T(8,128)(2,1)S(1)} %get-tuple-element.117), channel_id=1, source_target_pairs={{0,1},{1,0},{2,3},{3,2},{4,5},{5,4},{6,7},{7,6},{8,9},{9,8},{10,11... | collective-permute-start | bytes 786440 | tf_op jit(solution)/shard_map/ppermute | solution.py:282
  170.8 5.0 %collective-permute-start.45 = (bf16[256,256]{1,0:T(8,128)(2,1)S(1)}, bf16[256,256]{1,0:T(8,128)(2,1)S(1)}, u32[]{:S(2)}, u32[]{:S(2)}) collective-permute-start(bf16[256,256]{1,0:T(8,128)(2,1)S(1)} %sum.5.refs_1_), channel_id=1, source_target_pairs={{0,8},{8,0},{16,24},{24,16},{1,9},{9,1},{17,25},{25,17},{2,10},{10... | collective-permute-start | bytes 393224 | tf_op jit(solution)/shard_map/ppermute | solution.py:285
  172.0 5.0 %collective-permute-start.46 = (bf16[256,256]{1,0:T(8,128)(2,1)S(1)}, bf16[256,256]{1,0:T(8,128)(2,1)S(1)}, u32[]{:S(2)}, u32[]{:S(2)}) collective-permute-start(bf16[256,256]{1,0:T(8,128)(2,1)S(1)} %sum.5.refs_1_), channel_id=1, source_target_pairs={{0,16},{8,24},{16,0},{24,8},{1,17},{9,25},{17,1},{25,9},{2,18},{10... | collective-permute-start | bytes 393224 | tf_op jit(solution)/shard_map/ppermute | solution.py:285
  173.1 5.9 %collective-permute-start.47 = (bf16[256,256]{1,0:T(8,128)(2,1)S(1)}, bf16[256,256]{1,0:T(8,128)(2,1)S(1)}, u32[]{:S(2)}, u32[]{:S(2)}) collective-permute-start(bf16[256,256]{1,0:T(8,128)(2,1)S(1)} %sum.5.refs_1_), channel_id=1, source_target_pairs={{0,24},{8,16},{16,8},{24,0},{1,25},{9,17},{17,9},{25,1},{2,26},{10... | collective-permute-start | bytes 393224 | tf_op jit(solution)/shard_map/ppermute | solution.py:285
  174.4 5.5 %collective-permute-start.48 = (bf16[256,256]{1,0:T(8,128)(2,1)S(1)}, bf16[256,256]{1,0:T(8,128)(2,1)S(1)}, u32[]{:S(2)}, u32[]{:S(2)}) collective-permute-start(bf16[256,256]{1,0:T(8,128)(2,1)S(1)} %sum.5.refs_1_), channel_id=1, source_target_pairs={{0,1},{1,0},{2,3},{3,2},{4,5},{5,4},{6,7},{7,6},{8,9},{9,8},{10,11... | collective-permute-start | bytes 393224 | tf_op jit(solution)/shard_map/ppermute | solution.py:282
  (32 other events, 203.2 us)

commit v4 on v3

v4 whole, which is shorter than its diff:
```python
import jax
import jax.numpy as jnp
from jax import lax
from jax.experimental import pallas as pl
from jax.experimental.pallas import tpu as pltpu
from jax.sharding import Mesh, PartitionSpec as P

BF16 = jnp.bfloat16
F32 = jnp.float32
I32 = jnp.int32


def log2(n):
    assert n & (n - 1) == 0
    return n.bit_length() - 1


def iota(shape, dim):
    return lax.broadcasted_iota(I32, shape, dim)


def one_hot(mask):
    return jnp.where(mask, 1.0, 0.0).astype(BF16)


def dot(a, b):
    return jnp.dot(a, b, preferred_element_type=F32)


def dot_rows(a, b):
    return lax.dot_general(a, b, (((0,), (0,)), ((), ())), preferred_element_type=F32)


def call(body, outs, ins, name, us, scratch=()):
    smem = pl.BlockSpec(memory_space=pltpu.SMEM)
    vmem = pl.BlockSpec(memory_space=pltpu.VMEM)
    arrays = [jax.ShapeDtypeStruct(s, d) for s, d in outs] + [value for _, value in ins]
    size = sum(a.size * a.dtype.itemsize for a in arrays + [m.get_array_aval() for m in scratch])
    return pl.pallas_call(
        body,
        out_shape=tuple(jax.ShapeDtypeStruct(s, d) for s, d in outs),
        in_specs=[smem if where == "s" else vmem for where, _ in ins],
        out_specs=tuple(vmem for _ in outs),
        scratch_shapes=list(scratch),
        compiler_params=pltpu.CompilerParams(vmem_limit_bytes=size + (6 << 20)),
        cost_estimate=pl.CostEstimate(flops=int(us * 1e9), bytes_accessed=0, transcendentals=0),
        name=name,
    )(*(value for _, value in ins))


class Sizes:
    def __init__(self, rows, tiles):
        self.grp, self.zz = lax.axis_size("grp"), lax.axis_size("zz")
        self.dom = 2 * self.zz
        self.rows, self.tiles = rows, tiles
        self.pair = rows // (self.grp * self.dom)
        self.piece = self.grp * self.pair
        self.per_grp = self.dom * self.pair


def column(row):
    n = row.shape[1]
    on = iota((n, n), 0) == iota((n, n), 1)
    return jnp.sum(jnp.where(on, row.astype(F32), 0.0), axis=1, keepdims=True).astype(I32)


def index_kernel(z, me_ref, order_ref, want_ref, slot_ref):
    rows = z.rows
    shift = log2(rows)
    order_r = order_ref[...]
    order_c = column(order_r)
    down, across = iota((rows, rows), 0), iota((rows, rows), 1)
    source_r, source_c = order_r >> shift, order_c >> shift
    row_c = order_c & (rows - 1)
    same = jnp.where(source_c == source_r, 1.0, 0.0)
    rank_c = jnp.sum(jnp.where(across < down, same, 0.0), axis=1, keepdims=True).astype(I32)
    rank_r = jnp.sum(jnp.where(down < across, same, 0.0), axis=0, keepdims=True).astype(I32)
    owner = one_hot(iota((z.grp * z.dom, rows), 0) == source_r)
    at_rank = iota((rows, z.pair), 1) == rank_c
    high = jnp.where(at_rank, (row_c >> 4).astype(F32), 0.0).astype(BF16)
    low = jnp.where(at_rank, (row_c & 15).astype(F32), 0.0).astype(BF16)
    want_ref[...] = (dot(owner, high) * 16.0 + dot(owner, low)).astype(I32)
    across_grp = (source_r >> log2(z.dom)) ^ me_ref[0]
    inner = source_r & (z.dom - 1)
    slot_ref[...] = (inner * z.grp + across_grp) * z.pair + rank_r


def send_kernel(z, me_ref, asked_ref, features_ref, weight_ref, *refs):
    picked_refs, out_refs, rows_ref = refs[:z.grp], refs[z.grp:-1], refs[-1]
    asked = asked_ref[...]
    devices, half = asked.shape[0], out_refs[0].shape[2]
    row, device = iota((z.rows, devices), 0), iota((z.rows, devices), 1)
    asker = (row >> log2(z.pair)) ^ (me_ref[0] * z.dom)
    spread = one_hot(device == asker)
    high = dot(spread, (asked >> 4).astype(F32).astype(BF16))
    low = dot(spread, (asked & 15).astype(F32).astype(BF16))
    mine = iota((z.rows, z.pair), 1) == (iota((z.rows, z.pair), 0) & (z.pair - 1))
    wanted = jnp.sum(jnp.where(mine, high * 16.0 + low, 0.0), axis=1, keepdims=True).astype(I32)
    pick = one_hot(iota((z.rows, z.rows), 1) == wanted)
    rows_ref[...] = dot(pick, features_ref[...]).astype(BF16)
    for flip in range(2):
        at = pl.multiple_of((me_ref[2] ^ flip) * half, half)
        product = dot(rows_ref[...], weight_ref[:, pl.ds(at, half)]).astype(BF16)
        for s in range(z.grp):
            out_refs[s][flip] = product[s * z.per_grp:(s + 1) * z.per_grp, :]
    for s in range(z.grp):
        picked_refs[s][...] = rows_ref[s * z.per_grp:(s + 1) * z.per_grp, :]


def pack_kernel(z, *refs):
    ins, outs = refs[:z.grp], refs[z.grp:]
    for flip in range(2):
        for s in range(z.grp):
            outs[flip][s * z.per_grp:(s + 1) * z.per_grp, :] = ins[s][flip]


def place_kernel(z, me_ref, domain_ref, out_ref):
    @pl.loop(0, z.dom)
    def _(n):
        k, rel = (me_ref[1] - (n >> 1)) & (z.zz - 1), (n & 1) ^ me_ref[2]
        slot = domain_ref[pl.ds(rel * z.zz + k, 1), :]
        rank, at = slot & (z.pair - 1), slot >> log2(z.pair)
        s, at = at & (z.grp - 1), at >> log2(z.grp)
        k, rel = (me_ref[1] - (at >> 1)) & (z.zz - 1), (at & 1) ^ me_ref[2]
        slot = ((k * 2 + rel) * z.grp + s) * z.pair + rank
        out_ref[n] = one_hot(iota((z.rows, z.rows), 0) == slot)


def dense_kernel(cols_ref, vals_ref, out_ref, total):
    tiles, blocks, tile, _ = vals_ref.shape
    count = out_ref.shape[0]

    @pl.loop(0, tiles)
    def _(t):
        total[...] = jnp.zeros_like(total)
        for k in range(blocks):
            at = pl.multiple_of(cols_ref[t, k] * tile, tile)
            total[pl.ds(at, tile), :] += vals_ref[t, k].T.astype(F32)
        left = pl.multiple_of(t * tile, tile)
        out_ref[:, pl.ds(left, tile)] = total[pl.ds(0, count), :].astype(BF16)


def arrange_kernel(z, place_ref, dense_ref, *outs):
    turned, plain = outs[:z.zz], outs[z.zz:]

    @pl.loop(0, z.dom)
    def _(n):
        at = pl.multiple_of(n * z.rows, z.rows)
        part = dot(place_ref[n], dense_ref[pl.ds(at, z.rows), :]).astype(BF16)
        for k in range(z.zz):
            for p in range(2 * z.grp):
                first = (k * 2 * z.grp + p) * z.pair
                to = p * z.per_grp + n * z.pair
                if z.pair % 16 == 0:
                    to = pl.multiple_of(to, z.pair)
                    turned[k][pl.ds(to, z.pair), :] = part[first:first + z.pair, :]
                else:
                    turned[k][p, n] = part[first:first + z.pair, :]

    for out, source in zip(plain, turned):
        out[...] = source[...].reshape(out.shape[::-1]).T


def turn_kernel(*refs):
    out, height = refs[-1], refs[0].shape[0]
    for i, ref in enumerate(refs[:-1]):
        out[:, i * height:(i + 1) * height] = ref[...].T


def forward_kernel(z, first, last, *refs):
    plain, refs = refs[:2], refs[2:]
    pieces, refs = refs[:2], refs[2:]
    rows = jnp.concatenate([ref[...] for ref in pieces], axis=0)
    agg = [dot(ref[...], rows) for ref in plain]
    if not first:
        agg = [part + ref[...] for part, ref in zip(agg, refs)]
        refs = refs[2:]
    if not last:
        for ref, part in zip(refs, agg):
            ref[...] = part
        return
    cots, turned, hiddens, grads, parts = (refs[2 * i:2 * i + 2] for i in range(5))
    for part, cot, hidden, grad in zip(agg, cots, hiddens, grads):
        sig = jax.nn.sigmoid(part)
        hidden[...] = (part * sig).astype(BF16)
        grad[...] = (cot[...].astype(F32) * (sig * (1.0 + part * (1.0 - sig)))).astype(BF16)
    back_into(parts, turned, grads)


def back_into(outs, turned, grads):
    size = outs[0].shape[0]
    for i, out in enumerate(outs):
        rows = pl.ds(i * size, size)
        value = dot(turned[0][rows, :], grads[0][...]) + dot(turned[1][rows, :], grads[1][...])
        out[...] = value.astype(out.dtype)


def back_kernel(turned_a, turned_b, grad_a, grad_b, *outs):
    back_into(outs, (turned_a, turned_b), (grad_a, grad_b))


def pass_kernel(mine_ref, come_ref, out_ref):
    out_ref[...] = (mine_ref[...] + come_ref[...].astype(F32)).astype(BF16)


def grad_kernel(z, me_ref, left_a, left_b, mine_a, mine_b, come_a, come_b, *refs):
    outs, whole = refs[:-1], refs[-1]
    grads = [
        (mine[...] + come[...].astype(F32)).astype(BF16)
        for mine, come in ((mine_a, come_a), (mine_b, come_b))
    ]
    whole[...] = (dot(left_a[...], grads[0]) + dot(left_b[...], grads[1])).astype(BF16)
    share = whole.shape[0] // z.grp
    for s in range(z.grp):
        at = pl.multiple_of((me_ref[0] ^ s) * share, share)
        outs[s][...] = whole[pl.ds(at, share), :]


def sum_kernel(*refs):
    refs[-1][...] = sum(term[...].astype(F32) for term in refs[:-1]).astype(BF16)


def last_kernel(z, me_ref, *refs):
    pieces, out = refs[:-1], refs[-1]
    share, half = pieces[0].shape
    for rel in range(2):
        left = pl.multiple_of((me_ref[2] ^ rel) * half, half)
        for s in range(z.grp):
            at = pl.multiple_of((me_ref[0] ^ s) * share, share)
            out[pl.ds(at, share), pl.ds(left, half)] = pieces[rel * z.grp + s][...].astype(F32)


def arrange(z, place, dense, wide):
    inner = (wide, z.rows) if z.pair % 16 == 0 else (2 * z.grp, z.dom, z.pair, z.rows)
    got = call(
        lambda *refs: arrange_kernel(z, *refs),
        [(inner, BF16)] * z.zz + [((z.rows, wide), BF16)] * z.zz,
        [("v", place), ("v", dense)],
        "arrange", 4,
    )
    return [part.reshape(wide, z.rows) for part in got[:z.zz]] + list(got[z.zz:])


def shards(features, node_order, block_cols, block_count, block_vals, weight, cotangent):
    rows, width_in = features.shape
    hidden_units = weight.shape[1]
    half = hidden_units // 2
    tiles, blocks, tile = block_vals.shape[0], block_vals.shape[1], block_vals.shape[-1]
    z = Sizes(rows, tiles)
    at_grp, at_zz, core = lax.axis_index("grp"), lax.axis_index("zz"), lax.axis_index("core")
    me = jnp.stack([at_grp, at_zz, core]).astype(I32)

    def to_core(x):
        return lax.ppermute(x, "core", [(0, 1), (1, 0)])

    def to_grp(x, s):
        return lax.ppermute(x, "grp", [(i, i ^ s) for i in range(z.grp)]) if s else x

    def to_zz(x, k):
        return lax.ppermute(x, "zz", [(i, (i + k) % z.zz) for i in range(z.zz)]) if k else x

    want, slot = call(
        lambda *refs: index_kernel(z, *refs),
        [((z.grp * z.dom, z.pair), I32), ((1, rows), I32)],
        [("s", me), ("v", node_order.reshape(1, rows))],
        "index", 1,
    )
    asked = lax.all_to_all(want, ("grp", "zz", "core"), split_axis=0, concat_axis=0, tiled=True)
    domain = jnp.concatenate([to_zz(slot, k) for k in range(z.zz)], axis=0)
    domain = jnp.concatenate([domain, to_core(domain)], axis=0)

    vals_b = to_core(block_vals)
    cot_a = lax.dynamic_slice_in_dim(cotangent, core * half, half, axis=1)
    cot_b = to_core(lax.dynamic_slice_in_dim(cotangent, (1 - core) * half, half, axis=1))
    live = iota((tiles, blocks), 1) < block_count[:, None]
    cols_a = jnp.where(live, block_cols, z.dom * tiles)
    cols_b = to_core(cols_a)

    got = call(
        lambda *refs: send_kernel(z, *refs),
        [((z.per_grp, width_in), BF16)] * z.grp + [((2, z.per_grp, half), BF16)] * z.grp,
        [("s", me), ("v", asked), ("v", features), ("v", weight)],
        "send", 2,
        (pltpu.VMEM((rows, width_in), BF16),),
    )
    picked = got[:z.grp]
    came = [to_grp(got[z.grp + s], s) for s in range(z.grp)]

    dense = [
        call(
            dense_kernel,
            [((z.dom * rows, rows), BF16)],
            [("s", cols), ("v", vals)],
            "dense", 2.5,
            (pltpu.VMEM((z.dom * rows + tile, tile), F32),),
        )[0]
        for cols, vals in ((cols_a, block_vals), (cols_b, vals_b))
    ]
    came, dense, domain, cot_b = lax.optimization_barrier((came, dense, domain, cot_b))

    own, other = call(
        lambda *refs: pack_kernel(z, *refs),
        [((rows, half), BF16)] * 2,
        [("v", part) for part in came],
        "pack", 0.5,
    )
    ring = [[own, to_core(other)]]
    for k in range(1, z.zz):
        ring.append([to_zz(part, 1) for part in ring[-1]])
        if k == 1:
            ring[1], picked = lax.optimization_barrier((ring[1], picked))

    held = [to_grp(picked[s], s) for s in range(z.grp)]
    (held,) = call(
        turn_kernel, [((width_in, rows), BF16)], [("v", part) for part in held], "turn", 0.5
    )
    held_b = to_core(held)

    (place,) = call(
        lambda *refs: place_kernel(z, *refs),
        [((z.dom, rows, rows), BF16)],
        [("s", me), ("v", domain)],
        "place", 1.5,
    )
    wide = 2 * z.grp * z.per_grp
    turned, plain = [], []
    for matrix in dense:
        got = arrange(z, place, matrix, wide)
        turned.append(got[:z.zz])
        plain.append(got[z.zz:])

    agg = []
    for k in range(z.zz):
        ins = [("v", plain[0][k]), ("v", plain[1][k])] + [("v", part) for part in ring[k]]
        ins += [("v", part) for part in agg]
        outs = [((rows, half), F32)] * 2
        last = k == z.zz - 1
        if last:
            ins += [("v", part) for part in (cot_a, cot_b, turned[0][k], turned[1][k])]
            outs = [((rows, half), BF16)] * 4 + [((wide // 2, half), BF16)] * 2
        agg = call(
            lambda *refs, k=k, last=last: forward_kernel(z, k == 0, last, *refs),
            outs, ins, "forward", 3 if last else 1,
        )
    hidden_a, hidden_b, grad_a, grad_b = agg[:4]
    came = agg[4:]

    for k in range(z.zz - 2, -1, -1):
        came = [to_zz(part, -1) for part in came]
        if k == z.zz - 2:
            came, hidden_b = lax.optimization_barrier((came, hidden_b))
            come = to_core(hidden_b)
        mine = call(
            back_kernel,
            [((wide // 2, half), F32)] * 2,
            [("v", part) for part in (turned[0][k], turned[1][k], grad_a, grad_b)],
            "back", 1,
        )
        if k:
            came = [
                call(
                    pass_kernel, [((wide // 2, half), BF16)], [("v", part), ("v", moved)],
                    "pass", 0.5,
                )[0]
                for part, moved in zip(mine, came)
            ]
    first = core == 0
    hidden = jnp.concatenate(
        [jnp.where(first, hidden_a, come), jnp.where(first, come, hidden_a)], axis=1
    )

    share = width_in // z.grp
    terms = call(
        lambda *refs: grad_kernel(z, *refs),
        [((share, half), BF16)] * z.grp,
        [("s", me), ("v", held), ("v", held_b)] + [("v", part) for part in (*mine, *came)],
        "grad", 1.5,
        (pltpu.VMEM((width_in, half), BF16),),
    )

    def total_of(parts):
        return call(
            sum_kernel, [((share, half), BF16)], [("v", part) for part in parts], "sum", 0.5
        )[0]

    mine = total_of([to_grp(terms[s], s) for s in range(z.grp)])
    step = 1
    while step < z.zz:
        mine = total_of(
            [mine, lax.ppermute(mine, "zz", [(i, i ^ step) for i in range(z.zz)])]
        )
        step *= 2
    mine = [to_grp(mine, s) for s in range(z.grp)]
    (grad_weight,) = call(
        lambda *refs: last_kernel(z, *refs),
        [((width_in, hidden_units), F32)],
        [("s", me)] + [("v", part) for part in mine + [to_core(part) for part in mine]],
        "last", 2,
    )
    return hidden, grad_weight


def solution(mesh):
    n_grp, n_dom = mesh.shape["grp"], mesh.shape["dom"]
    split = Mesh(mesh.devices.reshape(n_grp, n_dom // 2, 2), ("grp", "zz", "core"))
    by_rows = ("grp", "zz", "core")
    placed = (
        P(by_rows, None),
        P(by_rows),
        P(by_rows, None),
        P(by_rows),
        P(by_rows, None, None, None),
        P(),
        P(by_rows, None),
    )
    return jax.shard_map(
        shards,
        mesh=split,
        in_specs=placed,
        out_specs=(P(by_rows, None), P()),
        check_vma=False,
    )
```

time: 183 us -> 153 us (0.84)
  starting transfers between devices: 59.5 us -> 42.6 us
  waiting for transfers between devices: 72.4 us -> 67.4 us
  Pallas kernels: 35 us -> 30.8 us
  local copies, waits for them, and re-layouts: 13.3 us -> 9.49 us
    ppermute x24 -> x12, starting transfers between devices: 31.6 us -> 14.1 us  [to_grp(): lax.ppermute(x, 'grp', [(i, i ^ s) for i in range(z.grp)])]
    ppermute x24 -> x12, waiting for transfers between devices: 25.4 us -> 13.4 us  [to_grp(): lax.ppermute(x, 'grp', [(i, i ^ s) for i in range(z.grp)])]
    ppermute x15, waiting for transfers between devices: 35.6 us -> 44.3 us  [to_zz(): lax.ppermute(x, 'zz', [(i, (i + k) % z.zz) for i in range(z.zz)])]
    unnamed x56 -> x24, local copies, waits for them, and re-layouts: 13.2 us -> 8.72 us
    pallas_call x29 -> x25, Pallas kernels: 35 us -> 30.8 us  [call(): pl.pallas_call(body, out_shape=tuple((jax.ShapeDtypeStruct(s, d) for s, d...]
    ppermute x15, starting transfers between devices: 24.7 us -> 21.3 us  [to_zz(): lax.ppermute(x, 'zz', [(i, (i + k) % z.zz) for i in range(z.zz)])]
    all_to_all x0 -> x1, starting transfers between devices: none -> 2.92 us  [shards(): lax.all_to_all(want, ('grp', 'zz', 'core'), split_axis=0, concat_axis=0,...]
  transfers between devices with their start and end apart: 52 -> 41, of which waited for: 24 -> 22; matrix products, arithmetic and copies ran while one was open for 1% -> 2% of each run, Pallas kernels for 16% -> 16%
where the time goes in v4:
time: 153 us
  waiting for transfers between devices  67.4 us (44%)
  starting transfers between devices  42.6 us (28%)
  Pallas kernels  30.8 us (20%)
  local copies, waits for them, and re-layouts  9.49 us (6%)
  other arithmetic  1.72 us (1%)
    ppermute x15, waiting for transfers between devices, to_zz(): lax.ppermute(x, 'zz', [(i, (i + k) % z.zz) for i in range(z.zz)])  44.3 us
    pallas_call x25, Pallas kernels, call(): pl.pallas_call(body, out_shape=tuple((jax.ShapeDtypeStruct(s, d) for s, d...  30.8 us
    ppermute x15, starting transfers between devices, to_zz(): lax.ppermute(x, 'zz', [(i, (i + k) % z.zz) for i in range(z.zz)])  21.3 us
    ppermute x12, starting transfers between devices, to_grp(): lax.ppermute(x, 'grp', [(i, i ^ s) for i in range(z.grp)])  14.1 us
    ppermute x12, waiting for transfers between devices, to_grp(): lax.ppermute(x, 'grp', [(i, i ^ s) for i in range(z.grp)])  13.4 us
    ppermute x2, waiting for transfers between devices, shards(): lax.ppermute(mine, 'zz', [(i, i ^ step) for i in range(z.zz)])  9.3 us
    unnamed x24, local copies, waits for them, and re-layouts  8.72 us
  transfers between devices with their start and end apart: 41, of which 22 were waited for; matrix products, arithmetic and copies ran while one was open for 2% of the time, Pallas kernels for 16%

profile of v4, /device:TPU:0, one launch (start us, length us, event | category | flops | bytes accessed | tf_op | source)
XLA Modules:
  0.0 152.9 jit_solution(5373347619835707780)
XLA Ops:
  1.9 1.7 %index.1 = (s32[32,16]{1,0:T(8,128)}, s32[1,512]{1,0:T(1,128)S(1)}) custom-call(s32[3]{0:T(128)S(1)} %pad_add_fusion.1.refs_0_, s32[1,512]{1,0:T(1,128)S(1)} %bitcast.9), custom_call_target="tpu_custom_call" | custom-call | flops 1000000000 | tf_op jit(solution)/shard_map/index/pallas_call | solution.py:39
  3.6 2.6 %collective-permute-start.5 = (s32[1,512]{1,0:T(1,128)S(1)}, s32[1,512]{1,0:T(1,128)S(1)}, u32[]{:S(2)}, u32[]{:S(2)}) collective-permute-start(s32[1,512]{1,0:T(1,128)S(1)} %get-tuple-element.74), channel_id=1, source_target_pairs={{0,2},{2,4},{4,6},{6,0},{1,3},{3,5},{5,7},{7,1},{8,10},{10,12},{12... | collective-permute-start | bytes 6152 | tf_op jit(solution)/shard_map/ppermute | solution.py:260
  6.2 2.6 %collective-permute-start.6 = (s32[1,512]{1,0:T(1,128)S(1)}, s32[1,512]{1,0:T(1,128)S(1)}, u32[]{:S(2)}, u32[]{:S(2)}) collective-permute-start(s32[1,512]{1,0:T(1,128)S(1)} %get-tuple-element.74), channel_id=1, source_target_pairs={{0,4},{2,6},{4,0},{6,2},{1,5},{3,7},{5,1},{7,3},{8,12},{10,14},{12... | collective-permute-start | bytes 6152 | tf_op jit(solution)/shard_map/ppermute | solution.py:260
  8.8 1.3 collective-permute-start.7
  10.1 2.9 %all-to-all-start = ((s32[32,1,16]{2,1,0:T(1,128)}), s32[32,1,16]{2,1,0:T(1,128)S(1)}, u32[]{:S(2)}, u32[]{:S(2)}) async-start(s32[32,1,16]{2,1,0:T(1,128)} %bitcast.5), calls=%async_computation | async-start | bytes 32768 | tf_op jit(solution)/shard_map/all_to_all | solution.py:268
  14.1 1.6 %copy-done = bf16[4,16,128,128]{3,2,1,0:T(8,128)(2,1)S(1)} copy-done((bf16[4,16,128,128]{3,2,1,0:T(8,128)(2,1)S(1)}, bf16[4,16,128,128]{3,2,1,0:T(8,128)(2,1)}, u32[]{:S(2)}) %copy-start) | copy-done | bytes 2097176
  15.7 2.4 %dense.2.refs_1_ = bf16[4096,512]{1,0:T(8,128)(2,1)S(1)} custom-call(s32[4,16]{1,0:T(4,128)S(1)} %fusion.cols_ref, bf16[4,16,128,128]{3,2,1,0:T(8,128)(2,1)S(1)} %copy-done), custom_call_target="tpu_custom_call" | custom-call | flops 2500000000 | tf_op jit(solution)/shard_map/dense/pallas_call | solution.py:39
  18.1 2.0 %copy-done.7 = bf16[4096,512]{1,0:T(8,128)(2,1)} copy-done((bf16[4096,512]{1,0:T(8,128)(2,1)}, bf16[4096,512]{1,0:T(8,128)(2,1)S(1)}, u32[]{:S(2)}) %copy-start.7) | copy-done | bytes 4194328
  21.4 1.2 copy-done.1
  22.6 1.2 copy-done.2
  23.9 2.6 %send.1 = (bf16[128,1024]{1,0:T(8,128)(2,1)S(1)}, bf16[128,1024]{1,0:T(8,128)(2,1)S(1)}, bf16[128,1024]{1,0:T(8,128)(2,1)S(1)}, bf16[128,1024]{1,0:T(8,128)(2,1)...) custom-call(s32[3]{0:T(128)S(1)} %pad_add_fusion.1.refs_0_, ...), custom_call_target="tpu_custom_call" | custom-call | flops 2000000000 | tf_op jit(solution)/shard_map/send/pallas_call | solution.py:39
  28.5 1.7 %collective-permute-start = (bf16[2,128,256]{2,1,0:T(8,128)(2,1)}, bf16[2,128,256]{2,1,0:T(8,128)(2,1)}, u32[]{:S(2)}, u32[]{:S(2)}) collective-permute-start(bf16[2,128,256]{2,1,0:T(8,128)(2,1)} %get-tuple-element.71), channel_id=1, source_target_pairs={{0,8},{8,0},{16,24},{24,16},{1,9},{9,1},{17,25},{25,17},{2,10},{10... | collective-permute-start | bytes 393224 | tf_op jit(solution)/shard_map/ppermute | solution.py:257
  30.2 1.5 collective-permute-start.1
  32.1 2.4 %dense.3.refs_1_ = bf16[4096,512]{1,0:T(8,128)(2,1)S(1)} custom-call(s32[4,16]{1,0:T(4,128)S(1)} %collective-permute-done.3.cols_ref, bf16[4,16,128,128]{3,2,1,0:T(8,128)(2,1)S(1)} %collective-permute-done.4.vals_ref), custom_call_target="tpu_custom_call" | custom-call | flops 2500000000 | tf_op jit(solution)/shard_map/dense/pallas_call | solution.py:39
  34.5 4.2 %collective-permute-done.1.refs_2_ = bf16[2,128,256]{2,1,0:T(8,128)(2,1)} collective-permute-done((bf16[2,128,256]{2,1,0:T(8,128)(2,1)}, bf16[2,128,256]{2,1,0:T(8,128)(2,1)}, u32[]{:S(2)}, u32[]{:S(2)}) %collective-permute-start.1) | collective-permute-done | bytes 131104 | tf_op jit(solution)/shard_map/ppermute | solution.py:257
  39.9 1.5 collective-permute-start.10
  41.4 1.4 place.1.refs_0_
  42.8 1.5 collective-permute-start.12
  44.4 4.7 %arrange.3 = (bf16[1024,512]{1,0:T(8,128)(2,1)S(1)}, bf16[1024,512]{1,0:T(8,128)(2,1)S(1)}, bf16[1024,512]{1,0:T(8,128)(2,1)S(1)}, bf16[1024,512]{1,0:T(8,128)(2...) custom-call(bf16[8,512,512]{2,1,0:T(8,128)(2,1)S(1)} %place.1.refs_0, ...), custom_call_target="tpu_custom_call" | custom-call | flops 4000000000 | tf_op jit(solution)/shard_map/arrange/pallas_call | solution.py:39
  49.1 1.7 %collective-permute-done.10.refs_2_ = bf16[512,256]{1,0:T(8,128)(2,1)S(1)} collective-permute-done((bf16[512,256]{1,0:T(8,128)(2,1)S(1)}, bf16[512,256]{1,0:T(8,128)(2,1)S(1)}, u32[]{:S(2)}, u32[]{:S(2)}) %collective-permute-start.10) | collective-permute-done | bytes 262176 | tf_op jit(solution)/shard_map/ppermute | solution.py:260
  50.8 5.2 %collective-permute-done.12.refs_3_ = bf16[512,256]{1,0:T(8,128)(2,1)S(1)} collective-permute-done((bf16[512,256]{1,0:T(8,128)(2,1)S(1)}, bf16[512,256]{1,0:T(8,128)(2,1)S(1)}, u32[]{:S(2)}, u32[]{:S(2)}) %collective-permute-start.12) | collective-permute-done | bytes 262176 | tf_op jit(solution)/shard_map/ppermute | solution.py:260
  59.2 1.4 collective-permute-start.22
  60.6 4.7 %arrange.2 = (bf16[1024,512]{1,0:T(8,128)(2,1)S(1)}, bf16[1024,512]{1,0:T(8,128)(2,1)S(1)}, bf16[1024,512]{1,0:T(8,128)(2,1)S(1)}, bf16[1024,512]{1,0:T(8,128)(2...) custom-call(bf16[8,512,512]{2,1,0:T(8,128)(2,1)S(1)} %place.1.refs_0, ...), custom_call_target="tpu_custom_call" | custom-call | flops 4000000000 | tf_op jit(solution)/shard_map/arrange/pallas_call | solution.py:39
  65.4 1.6 %collective-permute-done.13.refs_2_ = bf16[512,256]{1,0:T(8,128)(2,1)S(1)} collective-permute-done((bf16[512,256]{1,0:T(8,128)(2,1)S(1)}, bf16[512,256]{1,0:T(8,128)(2,1)S(1)}, u32[]{:S(2)}, u32[]{:S(2)}) %collective-permute-start.13) | collective-permute-done | bytes 262176 | tf_op jit(solution)/shard_map/ppermute | solution.py:260
  67.0 5.6 %collective-permute-done.15.refs_3_ = bf16[512,256]{1,0:T(8,128)(2,1)S(1)} collective-permute-done((bf16[512,256]{1,0:T(8,128)(2,1)S(1)}, bf16[512,256]{1,0:T(8,128)(2,1)S(1)}, u32[]{:S(2)}, u32[]{:S(2)}) %collective-permute-start.15) | collective-permute-done | bytes 262176 | tf_op jit(solution)/shard_map/ppermute | solution.py:260
  75.2 3.0 %collective-permute-done.14.refs_2_ = bf16[512,256]{1,0:T(8,128)(2,1)S(1)} collective-permute-done((bf16[512,256]{1,0:T(8,128)(2,1)S(1)}, bf16[512,256]{1,0:T(8,128)(2,1)S(1)}, u32[]{:S(2)}, u32[]{:S(2)}) %collective-permute-start.14) | collective-permute-done | bytes 262176 | tf_op jit(solution)/shard_map/ppermute | solution.py:260
  78.2 4.3 %collective-permute-done.16.refs_3_ = bf16[512,256]{1,0:T(8,128)(2,1)S(1)} collective-permute-done((bf16[512,256]{1,0:T(8,128)(2,1)S(1)}, bf16[512,256]{1,0:T(8,128)(2,1)S(1)}, u32[]{:S(2)}, u32[]{:S(2)}) %collective-permute-start.16) | collective-permute-done | bytes 262176 | tf_op jit(solution)/shard_map/ppermute | solution.py:260
  82.5 1.6 %forward.7 = (bf16[512,256]{1,0:T(8,128)(2,1)S(1)}, bf16[512,256]{1,0:T(8,128)(2,1)S(1)}, bf16[512,256]{1,0:T(8,128)(2,1)S(1)}, bf16[512,256]{1,0:T(8,128)(2,1)S...) custom-call(bf16[512,1024]{1,0:T(8,128)(2,1)S(1)} %get-tuple-element.77.refs_0_, ...), custom_call_target="tpu_custom_call" | custom-call | flops 3000000000 | tf_op jit(solution)/shard_map/forward/pallas_call | solution.py:39
  85.1 8.3 %collective-permute-done.17.come_ref = bf16[512,256]{1,0:T(8,128)(2,1)S(1)} collective-permute-done((bf16[512,256]{1,0:T(8,128)(2,1)S(1)}, bf16[512,256]{1,0:T(8,128)(2,1)S(1)}, u32[]{:S(2)}, u32[]{:S(2)}) %collective-permute-start.17) | collective-permute-done | bytes 262176 | tf_op jit(solution)/shard_map/ppermute | solution.py:260
  93.4 3.4 %collective-permute-done.18.come_ref = bf16[512,256]{1,0:T(8,128)(2,1)S(1)} collective-permute-done((bf16[512,256]{1,0:T(8,128)(2,1)S(1)}, bf16[512,256]{1,0:T(8,128)(2,1)S(1)}, u32[]{:S(2)}, u32[]{:S(2)}) %collective-permute-start.18) | collective-permute-done | bytes 262176 | tf_op jit(solution)/shard_map/ppermute | solution.py:260
  96.8 2.1 %collective-permute-start.26 = (bf16[512,256]{1,0:T(8,128)(2,1)S(1)}, bf16[512,256]{1,0:T(8,128)(2,1)S(1)}, u32[]{:S(2)}, u32[]{:S(2)}) collective-permute-start(bf16[512,256]{1,0:T(8,128)(2,1)S(1)} %pass.6), channel_id=1, source_target_pairs={{0,6},{2,0},{4,2},{6,4},{1,7},{3,1},{5,3},{7,5},{8,14},{10,8},{12,... | collective-permute-start | bytes 786440 | tf_op jit(solution)/shard_map/ppermute | solution.py:260
  99.8 6.3 %collective-permute-done.26.come_ref = bf16[512,256]{1,0:T(8,128)(2,1)S(1)} collective-permute-done((bf16[512,256]{1,0:T(8,128)(2,1)S(1)}, bf16[512,256]{1,0:T(8,128)(2,1)S(1)}, u32[]{:S(2)}, u32[]{:S(2)}) %collective-permute-start.26) | collective-permute-done | bytes 262176 | tf_op jit(solution)/shard_map/ppermute | solution.py:260
  106.1 3.9 %collective-permute-start.27 = (bf16[512,256]{1,0:T(8,128)(2,1)S(1)}, bf16[512,256]{1,0:T(8,128)(2,1)S(1)}, u32[]{:S(2)}, u32[]{:S(2)}) collective-permute-start(bf16[512,256]{1,0:T(8,128)(2,1)S(1)} %pass.7), channel_id=1, source_target_pairs={{0,6},{2,0},{4,2},{6,4},{1,7},{3,1},{5,3},{7,5},{8,14},{10,8},{12,... | collective-permute-start | bytes 786440 | tf_op jit(solution)/shard_map/ppermute | solution.py:260
  110.1 1.6 %collective-permute-done.24.come_ref = bf16[512,256]{1,0:T(8,128)(2,1)S(1)} collective-permute-done((bf16[512,256]{1,0:T(8,128)(2,1)S(1)}, bf16[512,256]{1,0:T(8,128)(2,1)S(1)}, u32[]{:S(2)}, u32[]{:S(2)}) %collective-permute-start.24) | collective-permute-done | bytes 262176 | tf_op jit(solution)/shard_map/ppermute | solution.py:260
  111.8 4.1 %collective-permute-start.25 = (bf16[512,256]{1,0:T(8,128)(2,1)S(1)}, bf16[512,256]{1,0:T(8,128)(2,1)S(1)}, u32[]{:S(2)}, u32[]{:S(2)}) collective-permute-start(bf16[512,256]{1,0:T(8,128)(2,1)S(1)} %pass.5), channel_id=1, source_target_pairs={{0,6},{2,0},{4,2},{6,4},{1,7},{3,1},{5,3},{7,5},{8,14},{10,8},{12,... | collective-permute-start | bytes 786440 | tf_op jit(solution)/shard_map/ppermute | solution.py:260
  117.0 2.8 %collective-permute-done.25.refs_5_ = bf16[512,256]{1,0:T(8,128)(2,1)S(1)} collective-permute-done((bf16[512,256]{1,0:T(8,128)(2,1)S(1)}, bf16[512,256]{1,0:T(8,128)(2,1)S(1)}, u32[]{:S(2)}, u32[]{:S(2)}) %collective-permute-start.25) | collective-permute-done | bytes 262176 | tf_op jit(solution)/shard_map/ppermute | solution.py:260
  119.8 1.3 grad.1
  123.2 1.5 collective-permute-start.30
  124.6 1.5 collective-permute-done.28.refs_1_
  127.2 1.9 %collective-permute-done.30.refs_3_ = bf16[256,256]{1,0:T(8,128)(2,1)S(1)} collective-permute-done((bf16[256,256]{1,0:T(8,128)(2,1)S(1)}, bf16[256,256]{1,0:T(8,128)(2,1)S(1)}, u32[]{:S(2)}, u32[]{:S(2)}) %collective-permute-start.30) | collective-permute-done | bytes 131104 | tf_op jit(solution)/shard_map/ppermute | solution.py:257
  129.2 6.1 %collective-permute-done.31.refs_1_ = bf16[256,256]{1,0:T(8,128)(2,1)S(1)} collective-permute-done((bf16[256,256]{1,0:T(8,128)(2,1)S(1)}, bf16[256,256]{1,0:T(8,128)(2,1)S(1)}, u32[]{:S(2)}, u32[]{:S(2)}) %collective-permute-start.31) | collective-permute-done | bytes 131104 | tf_op jit(solution)/shard_map/ppermute | solution.py:390
  135.3 2.7 %collective-permute-start.32 = (bf16[256,256]{1,0:T(8,128)(2,1)S(1)}, bf16[256,256]{1,0:T(8,128)(2,1)S(1)}, u32[]{:S(2)}, u32[]{:S(2)}) collective-permute-start(bf16[256,256]{1,0:T(8,128)(2,1)S(1)} %sum.4.refs_0_), channel_id=1, source_target_pairs={{0,4},{2,6},{4,0},{6,2},{1,5},{3,7},{5,1},{7,3},{8,12},{10,14},{12... | collective-permute-start | bytes 393224 | tf_op jit(solution)/shard_map/ppermute | solution.py:390
  138.0 3.2 %collective-permute-done.32.refs_1_ = bf16[256,256]{1,0:T(8,128)(2,1)S(1)} collective-permute-done((bf16[256,256]{1,0:T(8,128)(2,1)S(1)}, bf16[256,256]{1,0:T(8,128)(2,1)S(1)}, u32[]{:S(2)}, u32[]{:S(2)}) %collective-permute-start.32) | collective-permute-done | bytes 131104 | tf_op jit(solution)/shard_map/ppermute | solution.py:390
  141.3 1.5 collective-permute-start.33
  144.8 1.5 %collective-permute-done.33.refs_2_ = bf16[256,256]{1,0:T(8,128)(2,1)S(1)} collective-permute-done((bf16[256,256]{1,0:T(8,128)(2,1)S(1)}, bf16[256,256]{1,0:T(8,128)(2,1)S(1)}, u32[]{:S(2)}, u32[]{:S(2)}) %collective-permute-start.33) | collective-permute-done | bytes 131104 | tf_op jit(solution)/shard_map/ppermute | solution.py:257
  146.4 1.4 collective-permute-done.34.refs_3_
  147.7 1.8 %collective-permute-done.35.refs_4_ = bf16[256,256]{1,0:T(8,128)(2,1)S(1)} collective-permute-done((bf16[256,256]{1,0:T(8,128)(2,1)S(1)}, bf16[256,256]{1,0:T(8,128)(2,1)S(1)}, u32[]{:S(2)}, u32[]{:S(2)}) %collective-permute-start.35) | collective-permute-done | bytes 131104 | tf_op jit(solution)/shard_map/ppermute | solution.py:257
  150.9 2.0 %last.1 = f32[1024,512]{1,0:T(8,128)} custom-call(s32[3]{0:T(128)S(1)} %pad_add_fusion.1.refs_0_, bf16[256,256]{1,0:T(8,128)(2,1)S(1)} %sum.5.refs_1_, bf16[256,256]{1,0:T(8,128)(2,1)S(1)} %collective-permute-done.33.refs_2_, bf16[256,256]{1,0:T(8,128)(2,1)S(1)} %collective-permute-done.34.refs_3_, bf16[256,256]{1,0:T(8,128)(2,1)S(1)} %collective-permute-done.35.refs_4_, ...), custom_call_target="tpu_custom_call" | custom-call | flops 2000000000 | tf_op jit(solution)/shard_map/last/pallas_call | solution.py:39
  (90 shorter events, 22.7 us)
Async XLA Ops:
  0.6 31.5 %collective-permute-start.4 = (bf16[4,16,128,128]{3,2,1,0:T(8,128)(2,1)}, bf16[4,16,128,128]{3,2,1,0:T(8,128)(2,1)S(1)}, u32[]{:S(2)}, u32[]{:S(2)}) collective-permute-start(bf16[4,16,128,128]{3,2,1,0:T(8,128)(2,1)} %vals_ref.1), channel_id=1, source_target_pairs={{0,1},{1,0},{2,3},{3,2},{4,5},{5,4},{6,7},{7,6},{8,9},{9,8},{10,11... | collective-permute-start | bytes 6291464 | tf_op jit(solution)/shard_map/ppermute | solution.py:254
  3.6 17.2 %collective-permute-start.5 = (s32[1,512]{1,0:T(1,128)S(1)}, s32[1,512]{1,0:T(1,128)S(1)}, u32[]{:S(2)}, u32[]{:S(2)}) collective-permute-start(s32[1,512]{1,0:T(1,128)S(1)} %get-tuple-element.74), channel_id=1, source_target_pairs={{0,2},{2,4},{4,6},{6,0},{1,3},{3,5},{5,7},{7,1},{8,10},{10,12},{12... | collective-permute-start | bytes 6152 | tf_op jit(solution)/shard_map/ppermute | solution.py:260
  6.2 14.9 %collective-permute-start.6 = (s32[1,512]{1,0:T(1,128)S(1)}, s32[1,512]{1,0:T(1,128)S(1)}, u32[]{:S(2)}, u32[]{:S(2)}) collective-permute-start(s32[1,512]{1,0:T(1,128)S(1)} %get-tuple-element.74), channel_id=1, source_target_pairs={{0,4},{2,6},{4,0},{6,2},{1,5},{3,7},{5,1},{7,3},{8,12},{10,14},{12... | collective-permute-start | bytes 6152 | tf_op jit(solution)/shard_map/ppermute | solution.py:260
  8.8 12.3 %collective-permute-start.7 = (s32[1,512]{1,0:T(1,128)S(1)}, s32[1,512]{1,0:T(1,128)S(1)}, u32[]{:S(2)}, u32[]{:S(2)}) collective-permute-start(s32[1,512]{1,0:T(1,128)S(1)} %get-tuple-element.74), channel_id=1, source_target_pairs={{0,6},{2,0},{4,2},{6,4},{1,7},{3,1},{5,3},{7,5},{8,14},{10,8},{12,... | collective-permute-start | bytes 6152 | tf_op jit(solution)/shard_map/ppermute | solution.py:260
  10.1 11.3 %all-to-all-start = ((s32[32,1,16]{2,1,0:T(1,128)}), s32[32,1,16]{2,1,0:T(1,128)S(1)}, u32[]{:S(2)}, u32[]{:S(2)}) async-start(s32[32,1,16]{2,1,0:T(1,128)} %bitcast.5), calls=%async_computation | async-start | bytes 32768 | tf_op jit(solution)/shard_map/all_to_all | solution.py:268
  13.8 17.9 %collective-permute-start.3 = (s32[4,16]{1,0:T(4,128)S(1)}, s32[4,16]{1,0:T(4,128)S(1)}, u32[]{:S(2)}, u32[]{:S(2)}) collective-permute-start(s32[4,16]{1,0:T(4,128)S(1)} %fusion.cols_ref), channel_id=1, source_target_pairs={{0,1},{1,0},{2,3},{3,2},{4,5},{5,4},{6,7},{7,6},{8,9},{9,8},{10,11... | collective-permute-start | bytes 776 | tf_op jit(solution)/shard_map/ppermute | solution.py:254
  14.1 1.6 %copy-start = (bf16[4,16,128,128]{3,2,1,0:T(8,128)(2,1)S(1)}, bf16[4,16,128,128]{3,2,1,0:T(8,128)(2,1)}, u32[]{:S(2)}) copy-start(bf16[4,16,128,128]{3,2,1,0:T(8,128)(2,1)} %vals_ref.1) | copy-start | bytes 6291460
  15.7 4.4 %copy-start.11 = (bf16[512,512]{1,0:T(8,128)(2,1)S(1)}, bf16[512,512]{1,0:T(8,128)(2,1)}, u32[]{:S(2)}) copy-start(bf16[512,512]{1,0:T(8,128)(2,1)} %param.13) | copy-start | bytes 1572868
  18.1 2.0 %copy-start.7 = (bf16[4096,512]{1,0:T(8,128)(2,1)}, bf16[4096,512]{1,0:T(8,128)(2,1)S(1)}, u32[]{:S(2)}) copy-start(bf16[4096,512]{1,0:T(8,128)(2,1)S(1)} %dense.2.refs_1_) | copy-start | bytes 12582916
  20.8 18.0 %collective-permute-start.9 = (bf16[512,256]{1,0:T(8,128)(2,1)}, bf16[512,256]{1,0:T(8,128)(2,1)S(1)}, u32[]{:S(2)}, u32[]{:S(2)}) collective-permute-start(bf16[512,256]{1,0:T(8,128)(2,1)} %get-tuple-element.139), channel_id=1, source_target_pairs={{0,1},{1,0},{2,3},{3,2},{4,5},{5,4},{6,7},{7,6},{8,9},{9,8},{10,11... | collective-permute-start | bytes 786440 | tf_op jit(solution)/shard_map/ppermute | solution.py:254
  21.1 9.1 %collective-permute-start.8 = (s32[4,512]{1,0:T(4,128)S(1)}, s32[4,512]{1,0:T(4,128)S(1)}, u32[]{:S(2)}, u32[]{:S(2)}) collective-permute-start(s32[4,512]{1,0:T(4,128)S(1)} %pad_add_fusion), channel_id=1, source_target_pairs={{0,1},{1,0},{2,3},{3,2},{4,5},{5,4},{6,7},{7,6},{8,9},{9,8},{10,11... | collective-permute-start | bytes 24584 | tf_op jit(solution)/shard_map/ppermute | solution.py:254
  21.4 1.2 copy-start.1
  28.5 6.0 %collective-permute-start = (bf16[2,128,256]{2,1,0:T(8,128)(2,1)}, bf16[2,128,256]{2,1,0:T(8,128)(2,1)}, u32[]{:S(2)}, u32[]{:S(2)}) collective-permute-start(bf16[2,128,256]{2,1,0:T(8,128)(2,1)} %get-tuple-element.71), channel_id=1, source_target_pairs={{0,8},{8,0},{16,24},{24,16},{1,9},{9,1},{17,25},{25,17},{2,10},{10... | collective-permute-start | bytes 393224 | tf_op jit(solution)/shard_map/ppermute | solution.py:257
  30.2 8.6 %collective-permute-start.1 = (bf16[2,128,256]{2,1,0:T(8,128)(2,1)}, bf16[2,128,256]{2,1,0:T(8,128)(2,1)}, u32[]{:S(2)}, u32[]{:S(2)}) collective-permute-start(bf16[2,128,256]{2,1,0:T(8,128)(2,1)} %get-tuple-element.72), channel_id=1, source_target_pairs={{0,16},{8,24},{16,0},{24,8},{1,17},{9,25},{17,1},{25,9},{2,18},{10... | collective-permute-start | bytes 393224 | tf_op jit(solution)/shard_map/ppermute | solution.py:257
  31.7 7.1 %copy-start.10 = (bf16[2,128,256]{2,1,0:T(8,128)(2,1)S(1)}, bf16[2,128,256]{2,1,0:T(8,128)(2,1)}, u32[]{:S(2)}) copy-start(bf16[2,128,256]{2,1,0:T(8,128)(2,1)} %copy-done.9) | copy-start | bytes 393220
  31.7 7.1 %collective-permute-start.2 = (bf16[2,128,256]{2,1,0:T(8,128)(2,1)}, bf16[2,128,256]{2,1,0:T(8,128)(2,1)S(1)}, u32[]{:S(2)}, u32[]{:S(2)}) collective-permute-start(bf16[2,128,256]{2,1,0:T(8,128)(2,1)} %copy-done.5), channel_id=1, source_target_pairs={{0,24},{8,16},{16,8},{24,0},{1,25},{9,17},{17,9},{25,1},{2,26},{10... | collective-permute-start | bytes 393224 | tf_op jit(solution)/shard_map/ppermute | solution.py:257
  39.8 3.0 %collective-permute-start.11 = (bf16[512,256]{1,0:T(8,128)(2,1)S(1)}, bf16[512,256]{1,0:T(8,128)(2,1)S(1)}, u32[]{:S(2)}, u32[]{:S(2)}) collective-permute-start(bf16[512,256]{1,0:T(8,128)(2,1)S(1)} %get-tuple-element.85), channel_id=1, source_target_pairs={{0,1},{1,0},{2,3},{3,2},{4,5},{5,4},{6,7},{7,6},{8,9},{9,8},{10,11... | collective-permute-start | bytes 786440 | tf_op jit(solution)/shard_map/ppermute | solution.py:254
  39.9 11.0 %collective-permute-start.10 = (bf16[512,256]{1,0:T(8,128)(2,1)S(1)}, bf16[512,256]{1,0:T(8,128)(2,1)S(1)}, u32[]{:S(2)}, u32[]{:S(2)}) collective-permute-start(bf16[512,256]{1,0:T(8,128)(2,1)S(1)} %get-tuple-element.84.refs_2_), channel_id=1, source_target_pairs={{0,2},{2,4},{4,6},{6,0},{1,3},{3,5},{5,7},{7,1},{8,10},{10,12},{12... | collective-permute-start | bytes 786440 | tf_op jit(solution)/shard_map/ppermute | solution.py:260
  42.8 14.3 %copy-start.4 = (bf16[128,1024]{1,0:T(8,128)(2,1)S(1)}, bf16[128,1024]{1,0:T(8,128)(2,1)}, u32[]{:S(2)}) copy-start(bf16[128,1024]{1,0:T(8,128)(2,1)} %copy-done.3) | copy-start | bytes 786436
  42.8 17.8 %copy-start.8 = (bf16[4096,512]{1,0:T(8,128)(2,1)S(1)}, bf16[4096,512]{1,0:T(8,128)(2,1)}, u32[]{:S(2)}) copy-start(bf16[4096,512]{1,0:T(8,128)(2,1)} %copy-done.7) | copy-start | bytes 12582916
  42.8 13.2 %collective-permute-start.12 = (bf16[512,256]{1,0:T(8,128)(2,1)S(1)}, bf16[512,256]{1,0:T(8,128)(2,1)S(1)}, u32[]{:S(2)}, u32[]{:S(2)}) collective-permute-start(bf16[512,256]{1,0:T(8,128)(2,1)S(1)} %collective-permute-done.11.refs_3_), channel_id=1, source_target_pairs={{0,2},{2,4},{4,6},{6,0},{1,3},{3,5},{5,7},{7,1},{8,10},{10,12},{12... | collective-permute-start | bytes 786440 | tf_op jit(solution)/shard_map/ppermute | solution.py:260
  56.0 11.0 %collective-permute-start.13 = (bf16[512,256]{1,0:T(8,128)(2,1)S(1)}, bf16[512,256]{1,0:T(8,128)(2,1)S(1)}, u32[]{:S(2)}, u32[]{:S(2)}) collective-permute-start(bf16[512,256]{1,0:T(8,128)(2,1)S(1)} %collective-permute-done.10.refs_2_), channel_id=1, source_target_pairs={{0,2},{2,4},{4,6},{6,0},{1,3},{3,5},{5,7},{7,1},{8,10},{10,12},{12... | collective-permute-start | bytes 786440 | tf_op jit(solution)/shard_map/ppermute | solution.py:260
  56.0 16.6 %collective-permute-start.15 = (bf16[512,256]{1,0:T(8,128)(2,1)S(1)}, bf16[512,256]{1,0:T(8,128)(2,1)S(1)}, u32[]{:S(2)}, u32[]{:S(2)}) collective-permute-start(bf16[512,256]{1,0:T(8,128)(2,1)S(1)} %collective-permute-done.12.refs_3_), channel_id=1, source_target_pairs={{0,2},{2,4},{4,6},{6,0},{1,3},{3,5},{5,7},{7,1},{8,10},{10,12},{12... | collective-permute-start | bytes 786440 | tf_op jit(solution)/shard_map/ppermute | solution.py:260
  57.1 16.9 %collective-permute-start.20 = (bf16[128,1024]{1,0:T(8,128)(2,1)S(1)}, bf16[128,1024]{1,0:T(8,128)(2,1)S(1)}, u32[]{:S(2)}, u32[]{:S(2)}) collective-permute-start(bf16[128,1024]{1,0:T(8,128)(2,1)S(1)} %copy-done.4), channel_id=1, source_target_pairs={{0,8},{8,0},{16,24},{24,16},{1,9},{9,1},{17,25},{25,17},{2,10},{10... | collective-permute-start | bytes 786440 | tf_op jit(solution)/shard_map/ppermute | solution.py:257
  58.2 15.8 %collective-permute-start.21 = (bf16[128,1024]{1,0:T(8,128)(2,1)S(1)}, bf16[128,1024]{1,0:T(8,128)(2,1)S(1)}, u32[]{:S(2)}, u32[]{:S(2)}) collective-permute-start(bf16[128,1024]{1,0:T(8,128)(2,1)S(1)} %get-tuple-element.114), channel_id=1, source_target_pairs={{0,16},{8,24},{16,0},{24,8},{1,17},{9,25},{17,1},{25,9},{2,18},{10... | collective-permute-start | bytes 786440 | tf_op jit(solution)/shard_map/ppermute | solution.py:257
  59.2 14.9 %collective-permute-start.22 = (bf16[128,1024]{1,0:T(8,128)(2,1)S(1)}, bf16[128,1024]{1,0:T(8,128)(2,1)S(1)}, u32[]{:S(2)}, u32[]{:S(2)}) collective-permute-start(bf16[128,1024]{1,0:T(8,128)(2,1)S(1)} %get-tuple-element.115), channel_id=1, source_target_pairs={{0,24},{8,16},{16,8},{24,0},{1,25},{9,17},{17,9},{25,1},{2,26},{10... | collective-permute-start | bytes 786440 | tf_op jit(solution)/shard_map/ppermute | solution.py:257
  67.0 11.2 %collective-permute-start.14 = (bf16[512,256]{1,0:T(8,128)(2,1)S(1)}, bf16[512,256]{1,0:T(8,128)(2,1)S(1)}, u32[]{:S(2)}, u32[]{:S(2)}) collective-permute-start(bf16[512,256]{1,0:T(8,128)(2,1)S(1)} %collective-permute-done.13.refs_2_), channel_id=1, source_target_pairs={{0,2},{2,4},{4,6},{6,0},{1,3},{3,5},{5,7},{7,1},{8,10},{10,12},{12... | collective-permute-start | bytes 786440 | tf_op jit(solution)/shard_map/ppermute | solution.py:260
  72.6 9.9 %collective-permute-start.16 = (bf16[512,256]{1,0:T(8,128)(2,1)S(1)}, bf16[512,256]{1,0:T(8,128)(2,1)S(1)}, u32[]{:S(2)}, u32[]{:S(2)}) collective-permute-start(bf16[512,256]{1,0:T(8,128)(2,1)S(1)} %collective-permute-done.15.refs_3_), channel_id=1, source_target_pairs={{0,2},{2,4},{4,6},{6,0},{1,3},{3,5},{5,7},{7,1},{8,10},{10,12},{12... | collective-permute-start | bytes 786440 | tf_op jit(solution)/shard_map/ppermute | solution.py:260
  74.4 45.4 %collective-permute-start.23 = (bf16[1024,512]{1,0:T(8,128)(2,1)S(1)}, bf16[1024,512]{1,0:T(8,128)(2,1)S(1)}, u32[]{:S(2)}, u32[]{:S(2)}) collective-permute-start(bf16[1024,512]{1,0:T(8,128)(2,1)S(1)} %turn.1.refs_1_), channel_id=1, source_target_pairs={{0,1},{1,0},{2,3},{3,2},{4,5},{5,4},{6,7},{7,6},{8,9},{9,8},{10,11... | collective-permute-start | bytes 3145736 | tf_op jit(solution)/shard_map/ppermute | solution.py:254
  84.1 9.3 %collective-permute-start.17 = (bf16[512,256]{1,0:T(8,128)(2,1)S(1)}, bf16[512,256]{1,0:T(8,128)(2,1)S(1)}, u32[]{:S(2)}, u32[]{:S(2)}) collective-permute-start(bf16[512,256]{1,0:T(8,128)(2,1)S(1)} %get-tuple-element.108), channel_id=1, source_target_pairs={{0,6},{2,0},{4,2},{6,4},{1,7},{3,1},{5,3},{7,5},{8,14},{10,8},{12,... | collective-permute-start | bytes 786440 | tf_op jit(solution)/shard_map/ppermute | solution.py:260
  84.2 12.6 %collective-permute-start.18 = (bf16[512,256]{1,0:T(8,128)(2,1)S(1)}, bf16[512,256]{1,0:T(8,128)(2,1)S(1)}, u32[]{:S(2)}, u32[]{:S(2)}) collective-permute-start(bf16[512,256]{1,0:T(8,128)(2,1)S(1)} %get-tuple-element.109), channel_id=1, source_target_pairs={{0,6},{2,0},{4,2},{6,4},{1,7},{3,1},{5,3},{7,5},{8,14},{10,8},{12,... | collective-permute-start | bytes 786440 | tf_op jit(solution)/shard_map/ppermute | solution.py:260
  96.8 9.3 %collective-permute-start.26 = (bf16[512,256]{1,0:T(8,128)(2,1)S(1)}, bf16[512,256]{1,0:T(8,128)(2,1)S(1)}, u32[]{:S(2)}, u32[]{:S(2)}) collective-permute-start(bf16[512,256]{1,0:T(8,128)(2,1)S(1)} %pass.6), channel_id=1, source_target_pairs={{0,6},{2,0},{4,2},{6,4},{1,7},{3,1},{5,3},{7,5},{8,14},{10,8},{12,... | collective-permute-start | bytes 786440 | tf_op jit(solution)/shard_map/ppermute | solution.py:260
  99.0 12.7 %collective-permute-start.24 = (bf16[512,256]{1,0:T(8,128)(2,1)S(1)}, bf16[512,256]{1,0:T(8,128)(2,1)S(1)}, u32[]{:S(2)}, u32[]{:S(2)}) collective-permute-start(bf16[512,256]{1,0:T(8,128)(2,1)S(1)} %pass.4), channel_id=1, source_target_pairs={{0,6},{2,0},{4,2},{6,4},{1,7},{3,1},{5,3},{7,5},{8,14},{10,8},{12,... | collective-permute-start | bytes 786440 | tf_op jit(solution)/shard_map/ppermute | solution.py:260
  106.1 10.8 %collective-permute-start.27 = (bf16[512,256]{1,0:T(8,128)(2,1)S(1)}, bf16[512,256]{1,0:T(8,128)(2,1)S(1)}, u32[]{:S(2)}, u32[]{:S(2)}) collective-permute-start(bf16[512,256]{1,0:T(8,128)(2,1)S(1)} %pass.7), channel_id=1, source_target_pairs={{0,6},{2,0},{4,2},{6,4},{1,7},{3,1},{5,3},{7,5},{8,14},{10,8},{12,... | collective-permute-start | bytes 786440 | tf_op jit(solution)/shard_map/ppermute | solution.py:260
  111.8 8.0 %collective-permute-start.25 = (bf16[512,256]{1,0:T(8,128)(2,1)S(1)}, bf16[512,256]{1,0:T(8,128)(2,1)S(1)}, u32[]{:S(2)}, u32[]{:S(2)}) collective-permute-start(bf16[512,256]{1,0:T(8,128)(2,1)S(1)} %pass.5), channel_id=1, source_target_pairs={{0,6},{2,0},{4,2},{6,4},{1,7},{3,1},{5,3},{7,5},{8,14},{10,8},{12,... | collective-permute-start | bytes 786440 | tf_op jit(solution)/shard_map/ppermute | solution.py:260
  121.1 5.0 %collective-permute-start.28 = (bf16[256,256]{1,0:T(8,128)(2,1)S(1)}, bf16[256,256]{1,0:T(8,128)(2,1)S(1)}, u32[]{:S(2)}, u32[]{:S(2)}) collective-permute-start(bf16[256,256]{1,0:T(8,128)(2,1)S(1)} %get-tuple-element.133), channel_id=1, source_target_pairs={{0,8},{8,0},{16,24},{24,16},{1,9},{9,1},{17,25},{25,17},{2,10},{10... | collective-permute-start | bytes 393224 | tf_op jit(solution)/shard_map/ppermute | solution.py:257
  122.2 5.0 %collective-permute-start.29 = (bf16[256,256]{1,0:T(8,128)(2,1)S(1)}, bf16[256,256]{1,0:T(8,128)(2,1)S(1)}, u32[]{:S(2)}, u32[]{:S(2)}) collective-permute-start(bf16[256,256]{1,0:T(8,128)(2,1)S(1)} %get-tuple-element.134), channel_id=1, source_target_pairs={{0,16},{8,24},{16,0},{24,8},{1,17},{9,25},{17,1},{25,9},{2,18},{10... | collective-permute-start | bytes 393224 | tf_op jit(solution)/shard_map/ppermute | solution.py:257
  123.2 5.9 %collective-permute-start.30 = (bf16[256,256]{1,0:T(8,128)(2,1)S(1)}, bf16[256,256]{1,0:T(8,128)(2,1)S(1)}, u32[]{:S(2)}, u32[]{:S(2)}) collective-permute-start(bf16[256,256]{1,0:T(8,128)(2,1)S(1)} %get-tuple-element.135), channel_id=1, source_target_pairs={{0,24},{8,16},{16,8},{24,0},{1,25},{9,17},{17,9},{25,1},{2,26},{10... | collective-permute-start | bytes 393224 | tf_op jit(solution)/shard_map/ppermute | solution.py:257
  129.1 6.1 %collective-permute-start.31 = (bf16[256,256]{1,0:T(8,128)(2,1)S(1)}, bf16[256,256]{1,0:T(8,128)(2,1)S(1)}, u32[]{:S(2)}, u32[]{:S(2)}) collective-permute-start(bf16[256,256]{1,0:T(8,128)(2,1)S(1)} %sum.3.refs_0_), channel_id=1, source_target_pairs={{0,2},{2,0},{4,6},{6,4},{1,3},{3,1},{5,7},{7,5},{8,10},{10,8},{12,... | collective-permute-start | bytes 393224 | tf_op jit(solution)/shard_map/ppermute | solution.py:390
  135.3 5.9 %collective-permute-start.32 = (bf16[256,256]{1,0:T(8,128)(2,1)S(1)}, bf16[256,256]{1,0:T(8,128)(2,1)S(1)}, u32[]{:S(2)}, u32[]{:S(2)}) collective-permute-start(bf16[256,256]{1,0:T(8,128)(2,1)S(1)} %sum.4.refs_0_), channel_id=1, source_target_pairs={{0,4},{2,6},{4,0},{6,2},{1,5},{3,7},{5,1},{7,3},{8,12},{10,14},{12... | collective-permute-start | bytes 393224 | tf_op jit(solution)/shard_map/ppermute | solution.py:390
  138.0 11.6 %collective-permute-start.19 = (bf16[512,256]{1,0:T(8,128)(2,1)S(1)}, bf16[512,256]{1,0:T(8,128)(2,1)S(1)}, u32[]{:S(2)}, u32[]{:S(2)}) collective-permute-start(bf16[512,256]{1,0:T(8,128)(2,1)S(1)} %get-tuple-element.111), channel_id=1, source_target_pairs={{0,1},{1,0},{2,3},{3,2},{4,5},{5,4},{6,7},{7,6},{8,9},{9,8},{10,11... | collective-permute-start | bytes 786440 | tf_op jit(solution)/shard_map/ppermute | solution.py:254
  141.3 5.1 %collective-permute-start.33 = (bf16[256,256]{1,0:T(8,128)(2,1)S(1)}, bf16[256,256]{1,0:T(8,128)(2,1)S(1)}, u32[]{:S(2)}, u32[]{:S(2)}) collective-permute-start(bf16[256,256]{1,0:T(8,128)(2,1)S(1)} %sum.5.refs_1_), channel_id=1, source_target_pairs={{0,8},{8,0},{16,24},{24,16},{1,9},{9,1},{17,25},{25,17},{2,10},{10... | collective-permute-start | bytes 393224 | tf_op jit(solution)/shard_map/ppermute | solution.py:257
  142.8 5.0 %collective-permute-start.34 = (bf16[256,256]{1,0:T(8,128)(2,1)S(1)}, bf16[256,256]{1,0:T(8,128)(2,1)S(1)}, u32[]{:S(2)}, u32[]{:S(2)}) collective-permute-start(bf16[256,256]{1,0:T(8,128)(2,1)S(1)} %sum.5.refs_1_), channel_id=1, source_target_pairs={{0,16},{8,24},{16,0},{24,8},{1,17},{9,25},{17,1},{25,9},{2,18},{10... | collective-permute-start | bytes 393224 | tf_op jit(solution)/shard_map/ppermute | solution.py:257
  143.7 5.9 %collective-permute-start.35 = (bf16[256,256]{1,0:T(8,128)(2,1)S(1)}, bf16[256,256]{1,0:T(8,128)(2,1)S(1)}, u32[]{:S(2)}, u32[]{:S(2)}) collective-permute-start(bf16[256,256]{1,0:T(8,128)(2,1)S(1)} %sum.5.refs_1_), channel_id=1, source_target_pairs={{0,24},{8,16},{16,8},{24,0},{1,25},{9,17},{17,9},{25,1},{2,26},{10... | collective-permute-start | bytes 393224 | tf_op jit(solution)/shard_map/ppermute | solution.py:257
  144.8 5.6 %collective-permute-start.36 = (bf16[256,256]{1,0:T(8,128)(2,1)S(1)}, bf16[256,256]{1,0:T(8,128)(2,1)S(1)}, u32[]{:S(2)}, u32[]{:S(2)}) collective-permute-start(bf16[256,256]{1,0:T(8,128)(2,1)S(1)} %sum.5.refs_1_), channel_id=1, source_target_pairs={{0,1},{1,0},{2,3},{3,2},{4,5},{5,4},{6,7},{7,6},{8,9},{9,8},{10,11... | collective-permute-start | bytes 393224 | tf_op jit(solution)/shard_map/ppermute | solution.py:254
  146.4 4.1 %collective-permute-start.37 = (bf16[256,256]{1,0:T(8,128)(2,1)S(1)}, bf16[256,256]{1,0:T(8,128)(2,1)S(1)}, u32[]{:S(2)}, u32[]{:S(2)}) collective-permute-start(bf16[256,256]{1,0:T(8,128)(2,1)S(1)} %collective-permute-done.33.refs_2_), channel_id=1, source_target_pairs={{0,1},{1,0},{2,3},{3,2},{4,5},{5,4},{6,7},{7,6},{8,9},{9,8},{10,11... | collective-permute-start | bytes 393224 | tf_op jit(solution)/shard_map/ppermute | solution.py:254
  147.7 2.7 %collective-permute-start.38 = (bf16[256,256]{1,0:T(8,128)(2,1)S(1)}, bf16[256,256]{1,0:T(8,128)(2,1)S(1)}, u32[]{:S(2)}, u32[]{:S(2)}) collective-permute-start(bf16[256,256]{1,0:T(8,128)(2,1)S(1)} %collective-permute-done.34.refs_3_), channel_id=1, source_target_pairs={{0,1},{1,0},{2,3},{3,2},{4,5},{5,4},{6,7},{7,6},{8,9},{9,8},{10,11... | collective-permute-start | bytes 393224 | tf_op jit(solution)/shard_map/ppermute | solution.py:254
  149.5 1.3 collective-permute-start.39
  (5 other events, 3.9 us)

commit v5 on v4

--- a/solution.py
+++ b/solution.py
@@ -56,6 +56,7 @@
         self.pair = rows // (self.grp * self.dom)
         self.piece = self.grp * self.pair
         self.per_grp = self.dom * self.pair
+        assert rows // 128 < 8 and self.pair <= 128
 
 
 def column(row):
@@ -64,7 +65,7 @@
     return jnp.sum(jnp.where(on, row.astype(F32), 0.0), axis=1, keepdims=True).astype(I32)
 
 
-def index_kernel(z, me_ref, order_ref, want_ref, slot_ref):
+def index_kernel(z, me_ref, order_ref, out_ref):
     rows = z.rows
     shift = log2(rows)
     order_r = order_ref[...]
@@ -79,32 +80,46 @@
     at_rank = iota((rows, z.pair), 1) == rank_c
     high = jnp.where(at_rank, (row_c >> 4).astype(F32), 0.0).astype(BF16)
     low = jnp.where(at_rank, (row_c & 15).astype(F32), 0.0).astype(BF16)
-    want_ref[...] = (dot(owner, high) * 16.0 + dot(owner, low)).astype(I32)
+    want = (dot(owner, high) * 16.0 + dot(owner, low)).astype(I32)
+    out_ref[...] = jnp.zeros_like(out_ref)
+    for d in range(z.grp * z.dom):
+        out_ref[d, 0:1, 0:z.pair] = want[d:d + 1, :]
     across_grp = (source_r >> log2(z.dom)) ^ me_ref[0]
     inner = source_r & (z.dom - 1)
-    slot_ref[...] = (inner * z.grp + across_grp) * z.pair + rank_r
-
-
-def send_kernel(z, me_ref, asked_ref, features_ref, weight_ref, *refs):
-    picked_refs, out_refs, rows_ref = refs[:z.grp], refs[z.grp:-1], refs[-1]
-    asked = asked_ref[...]
-    devices, half = asked.shape[0], out_refs[0].shape[2]
-    row, device = iota((z.rows, devices), 0), iota((z.rows, devices), 1)
-    asker = (row >> log2(z.pair)) ^ (me_ref[0] * z.dom)
-    spread = one_hot(device == asker)
-    high = dot(spread, (asked >> 4).astype(F32).astype(BF16))
-    low = dot(spread, (asked & 15).astype(F32).astype(BF16))
-    mine = iota((z.rows, z.pair), 1) == (iota((z.rows, z.pair), 0) & (z.pair - 1))
+    slot = (inner * z.grp + across_grp) * z.pair + rank_r
+    for i in range(rows // 128):
+        lanes = slot[:, i * 128:(i + 1) * 128]
+        out_ref[:, 1 + i:2 + i, :] = jnp.broadcast_to(lanes[None], (z.grp * z.dom, 1, 128))
+
+
+def product_kernel(z, me_ref, features_ref, weight_ref, *outs):
+    half = outs[0].shape[1]
+    for flip, out in enumerate(outs):
+        at = pl.multiple_of((me_ref[2] ^ flip) * half, half)
+        out[...] = dot(features_ref[...], weight_ref[:, pl.ds(at, half)]).astype(BF16)
+
+
+def send_kernel(z, me_ref, message_ref, own_ref, other_ref, pick_ref, *outs):
+    devices, height, width = message_ref.shape
+    message = message_ref[...].reshape(devices * height, width)
+    shape = (z.rows, devices * height)
+    asker = (iota(shape, 0) >> log2(z.pair)) ^ (me_ref[0] * z.dom)
+    spread = one_hot(iota(shape, 1) == asker * height)
+    high = dot(spread, (message >> 4).astype(F32).astype(BF16))
+    low = dot(spread, (message & 15).astype(F32).astype(BF16))
+    mine = iota((z.rows, width), 1) == (iota((z.rows, width), 0) & (z.pair - 1))
     wanted = jnp.sum(jnp.where(mine, high * 16.0 + low, 0.0), axis=1, keepdims=True).astype(I32)
-    pick = one_hot(iota((z.rows, z.rows), 1) == wanted)
-    rows_ref[...] = dot(pick, features_ref[...]).astype(BF16)
-    for flip in range(2):
-        at = pl.multiple_of((me_ref[2] ^ flip) * half, half)
-        product = dot(rows_ref[...], weight_ref[:, pl.ds(at, half)]).astype(BF16)
+    pick_ref[...] = one_hot(iota((z.rows, z.rows), 1) == wanted)
+    for flip, product in enumerate((own_ref, other_ref)):
+        got = dot(pick_ref[...], product[...]).astype(BF16)
         for s in range(z.grp):
-            out_refs[s][flip] = product[s * z.per_grp:(s + 1) * z.per_grp, :]
-    for s in range(z.grp):
-        picked_refs[s][...] = rows_ref[s * z.per_grp:(s + 1) * z.per_grp, :]
+            outs[s][flip] = got[s * z.per_grp:(s + 1) * z.per_grp, :]
+
+
+def rows_kernel(z, pick_ref, features_ref, *outs):
+    for s, out in enumerate(outs):
+        pick = pick_ref[s * z.per_grp:(s + 1) * z.per_grp, :]
+        out[...] = dot(pick, features_ref[...]).astype(BF16)
 
 
 def pack_kernel(z, *refs):
@@ -114,11 +129,11 @@
             outs[flip][s * z.per_grp:(s + 1) * z.per_grp, :] = ins[s][flip]
 
 
-def place_kernel(z, me_ref, domain_ref, out_ref):
+def place_kernel(z, me_ref, message_ref, out_ref):
     @pl.loop(0, z.dom)
     def _(n):
-        k, rel = (me_ref[1] - (n >> 1)) & (z.zz - 1), (n & 1) ^ me_ref[2]
-        slot = domain_ref[pl.ds(rel * z.zz + k, 1), :]
+        message = message_ref[me_ref[0] * z.dom + n]
+        slot = jnp.concatenate([message[1 + i:2 + i, :] for i in range(z.rows // 128)], axis=1)
         rank, at = slot & (z.pair - 1), slot >> log2(z.pair)
         s, at = at & (z.grp - 1), at >> log2(z.grp)
         k, rel = (me_ref[1] - (at >> 1)) & (z.zz - 1), (at & 1) ^ me_ref[2]
@@ -259,44 +274,61 @@
     def to_zz(x, k):
         return lax.ppermute(x, "zz", [(i, (i + k) % z.zz) for i in range(z.zz)]) if k else x
 
-    want, slot = call(
+    (message,) = call(
         lambda *refs: index_kernel(z, *refs),
-        [((z.grp * z.dom, z.pair), I32), ((1, rows), I32)],
+        [((z.grp * z.dom, 8, 128), I32)],
         [("s", me), ("v", node_order.reshape(1, rows))],
         "index", 1,
     )
-    asked = lax.all_to_all(want, ("grp", "zz", "core"), split_axis=0, concat_axis=0, tiled=True)
-    domain = jnp.concatenate([to_zz(slot, k) for k in range(z.zz)], axis=0)
-    domain = jnp.concatenate([domain, to_core(domain)], axis=0)
-
+    message = lax.all_to_all(
+        message, ("grp", "zz", "core"), split_axis=0, concat_axis=0, tiled=True
+    )
     vals_b = to_core(block_vals)
-    cot_a = lax.dynamic_slice_in_dim(cotangent, core * half, half, axis=1)
-    cot_b = to_core(lax.dynamic_slice_in_dim(cotangent, (1 - core) * half, half, axis=1))
+
+    products = call(
+        lambda *refs: product_kernel(z, *refs),
+        [((rows, half), BF16)] * 2,
+        [("s", me), ("v", features), ("v", weight)],
+        "product", 1.5,
+    )
+    pick, *got = call(
+        lambda *refs: send_kernel(z, *refs),
+        [((rows, rows), BF16)] + [((2, z.per_grp, half), BF16)] * z.grp,
+        [("s", me), ("v", message)] + [("v", part) for part in products],
+        "send", 1.5,
+    )
+    got, message, cotangent, block_cols = lax.optimization_barrier(
+        (got, message, cotangent, block_cols)
+    )
+    came = [to_grp(got[s], s) for s in range(z.grp)]
+
     live = iota((tiles, blocks), 1) < block_count[:, None]
     cols_a = jnp.where(live, block_cols, z.dom * tiles)
     cols_b = to_core(cols_a)
-
-    got = call(
-        lambda *refs: send_kernel(z, *refs),
-        [((z.per_grp, width_in), BF16)] * z.grp + [((2, z.per_grp, half), BF16)] * z.grp,
-        [("s", me), ("v", asked), ("v", features), ("v", weight)],
-        "send", 2,
-        (pltpu.VMEM((rows, width_in), BF16),),
-    )
-    picked = got[:z.grp]
-    came = [to_grp(got[z.grp + s], s) for s in range(z.grp)]
-
-    dense = [
-        call(
+    cot_a = lax.dynamic_slice_in_dim(cotangent, core * half, half, axis=1)
+    cot_b = to_core(lax.dynamic_slice_in_dim(cotangent, (1 - core) * half, half, axis=1))
+
+    (place,) = call(
+        lambda *refs: place_kernel(z, *refs),
+        [((z.dom, rows, rows), BF16)],
+        [("s", me), ("v", message)],
+        "place", 1.5,
+    )
+    wide = 2 * z.grp * z.per_grp
+
+    def arranged(cols, vals):
+        (dense,) = call(
             dense_kernel,
             [((z.dom * rows, rows), BF16)],
             [("s", cols), ("v", vals)],
             "dense", 2.5,
             (pltpu.VMEM((z.dom * rows + tile, tile), F32),),
-        )[0]
-        for cols, vals in ((cols_a, block_vals), (cols_b, vals_b))
-    ]
-    came, dense, domain, cot_b = lax.optimization_barrier((came, dense, domain, cot_b))
+        )
+        got = arrange(z, place, dense, wide)
+        return got[:z.zz], got[z.zz:]
+
+    turned_a, plain_a = arranged(cols_a, block_vals)
+    came, plain_a = lax.optimization_barrier((came, plain_a))
 
     own, other = call(
         lambda *refs: pack_kernel(z, *refs),
@@ -305,29 +337,27 @@
         "pack", 0.5,
     )
     ring = [[own, to_core(other)]]
+    turned_b, plain_b = arranged(cols_b, vals_b)
+    turned, plain = (turned_a, turned_b), (plain_a, plain_b)
     for k in range(1, z.zz):
         ring.append([to_zz(part, 1) for part in ring[-1]])
         if k == 1:
-            ring[1], picked = lax.optimization_barrier((ring[1], picked))
-
+            ring[1][0], plain_b = lax.optimization_barrier((ring[1][0], plain_b))
+            plain = (plain_a, plain_b)
+        if k == 2:
+            ring[2][0], pick = lax.optimization_barrier((ring[2][0], pick))
+
+    picked = call(
+        lambda *refs: rows_kernel(z, *refs),
+        [((z.per_grp, width_in), BF16)] * z.grp,
+        [("v", pick), ("v", features)],
+        "rows", 1,
+    )
     held = [to_grp(picked[s], s) for s in range(z.grp)]
     (held,) = call(
         turn_kernel, [((width_in, rows), BF16)], [("v", part) for part in held], "turn", 0.5
     )
     held_b = to_core(held)
-
-    (place,) = call(
-        lambda *refs: place_kernel(z, *refs),
-        [((z.dom, rows, rows), BF16)],
-        [("s", me), ("v", domain)],
-        "place", 1.5,
-    )
-    wide = 2 * z.grp * z.per_grp
-    turned, plain = [], []
-    for matrix in dense:
-        got = arrange(z, place, matrix, wide)
-        turned.append(got[:z.zz])
-        plain.append(got[z.zz:])
 
     agg = []
     for k in range(z.zz):
@@ -342,14 +372,15 @@
             lambda *refs, k=k, last=last: forward_kernel(z, k == 0, last, *refs),
             outs, ins, "forward", 3 if last else 1,
         )
-    hidden_a, hidden_b, grad_a, grad_b = agg[:4]
-    came = agg[4:]
+    hidden_a, hidden_b, grad_a, grad_b, *came = agg
 
     for k in range(z.zz - 2, -1, -1):
         came = [to_zz(part, -1) for part in came]
-        if k == z.zz - 2:
-            came, hidden_b = lax.optimization_barrier((came, hidden_b))
+        if k == 1:
+            came[0], hidden_b = lax.optimization_barrier((came[0], hidden_b))
             come = to_core(hidden_b)
+        if k == 0:
+            came[1], come = lax.optimization_barrier((came[1], come))
         mine = call(
             back_kernel,
             [((wide // 2, half), F32)] * 2,

time: 153 us -> 160 us (1.046)
  local copies, waits for them, and re-layouts: 9.49 us -> 17.6 us
  waiting for transfers between devices: 67.4 us -> 62.4 us
  starting transfers between devices: 42.6 us -> 46 us
    unnamed x24 -> x80, local copies, waits for them, and re-layouts: 8.72 us -> 17.5 us
    ppermute x15 -> x12, waiting for transfers between devices: 44.3 us -> 35.5 us  [to_zz(): lax.ppermute(x, 'zz', [(i, (i + k) % z.zz) for i in range(z.zz)])]
    all_to_all x1, waiting for transfers between devices: 0.01 us -> 4.45 us  [shards(): lax.all_to_all(message, ('grp', 'zz', 'core'), split_axis=0, concat_axis=...]
    all_to_all x1, starting transfers between devices: 2.92 us -> 6.96 us  [shards(): lax.all_to_all(message, ('grp', 'zz', 'core'), split_axis=0, concat_axis=...]
    pallas_call x25 -> x27, Pallas kernels: 30.8 us -> 31.6 us  [call(): pl.pallas_call(body, out_shape=tuple((jax.ShapeDtypeStruct(s, d) for s, d...]
    ppermute x15 -> x12, starting transfers between devices: 21.3 us -> 20.7 us  [to_zz(): lax.ppermute(x, 'zz', [(i, (i + k) % z.zz) for i in range(z.zz)])]
  transfers between devices with their start and end apart: 41 -> 37, of which waited for: 22 -> 21; matrix products, arithmetic and copies ran while one was open for 2% -> 1% of each run, Pallas kernels for 16% -> 17%
where the time goes in v5:
time: 160 us
  waiting for transfers between devices  62.4 us (39%)
  starting transfers between devices  46 us (29%)
  Pallas kernels  31.6 us (20%)
  local copies, waits for them, and re-layouts  17.6 us (11%)
    ppermute x12, waiting for transfers between devices, to_zz(): lax.ppermute(x, 'zz', [(i, (i + k) % z.zz) for i in range(z.zz)])  35.5 us
    pallas_call x27, Pallas kernels, call(): pl.pallas_call(body, out_shape=tuple((jax.ShapeDtypeStruct(s, d) for s, d...  31.6 us
    ppermute x12, starting transfers between devices, to_zz(): lax.ppermute(x, 'zz', [(i, (i + k) % z.zz) for i in range(z.zz)])  20.7 us
    unnamed x80, local copies, waits for them, and re-layouts  17.5 us
    ppermute x12, starting transfers between devices, to_grp(): lax.ppermute(x, 'grp', [(i, i ^ s) for i in range(z.grp)])  12.8 us
    ppermute x12, waiting for transfers between devices, to_grp(): lax.ppermute(x, 'grp', [(i, i ^ s) for i in range(z.grp)])  12.8 us
    ppermute x2, waiting for transfers between devices, shards(): lax.ppermute(mine, 'zz', [(i, i ^ step) for i in range(z.zz)])  9.13 us
    all_to_all x1, starting transfers between devices, shards(): lax.all_to_all(message, ('grp', 'zz', 'core'), split_axis=0, concat_axis=...  6.96 us
  transfers between devices with their start and end apart: 37, of which 21 were waited for; matrix products, arithmetic and copies ran while one was open for 1% of the time, Pallas kernels for 17%

profile of v5, /device:TPU:0, one launch (start us, length us, event | category | flops | bytes accessed | tf_op | source)
XLA Modules:
  0.0 159.7 jit_solution(5287537584078844450)
XLA Ops:
  1.9 1.8 %index.1 = s32[32,8,128]{2,1,0:T(8,128)} custom-call(s32[3]{0:T(128)S(1)} %pad_add_fusion.refs_0_, s32[1,512]{1,0:T(1,128)S(1)} %bitcast.4), custom_call_target="tpu_custom_call" | custom-call | flops 1000000000 | tf_op jit(solution)/shard_map/index/pallas_call | solution.py:39
  3.7 7.0 %all-to-all-start = ((s32[32,8,128]{2,1,0:T(8,128)}), s32[32,8,128]{2,1,0:T(8,128)S(1)}, u32[]{:S(2)}, u32[]{:S(2)}) async-start(s32[32,8,128]{2,1,0:T(8,128)} %index.1), calls=%async_computation | async-start | bytes 262144 | tf_op jit(solution)/shard_map/all_to_all | solution.py:283
  10.6 1.2 copy-done.1
  11.9 1.2 copy-done.2
  13.1 1.3 product.1
  14.4 4.5 %all-to-all-done.refs_1_ = s32[32,8,128]{2,1,0:T(8,128)S(1)} async-done(((s32[32,8,128]{2,1,0:T(8,128)}), s32[32,8,128]{2,1,0:T(8,128)S(1)}, u32[]{:S(2)}, u32[]{:S(2)}) %all-to-all-start) | async-done | bytes 131104 | tf_op jit(solution)/shard_map/all_to_all | solution.py:283
  18.8 1.2 send.1
  21.6 2.0 %collective-permute-start.2 = (bf16[2,128,256]{2,1,0:T(8,128)(2,1)S(1)}, bf16[2,128,256]{2,1,0:T(8,128)(2,1)S(1)}, u32[]{:S(2)}, u32[]{:S(2)}) collective-permute-start(bf16[2,128,256]{2,1,0:T(8,128)(2,1)S(1)} %get-tuple-element.88), channel_id=1, source_target_pairs={{0,24},{8,16},{16,8},{24,0},{1,25},{9,17},{17,9},{25,1},{2,26},{10... | collective-permute-start | bytes 393224 | tf_op jit(solution)/shard_map/ppermute | solution.py:272
  23.6 1.4 place.1.refs_0_
  25.1 2.4 %dense.2.refs_1_ = bf16[4096,512]{1,0:T(8,128)(2,1)S(1)} custom-call(s32[4,16]{1,0:T(4,128)S(1)} %fusion.cols_ref, bf16[4,16,128,128]{3,2,1,0:T(8,128)(2,1)S(1)} %copy-done), custom_call_target="tpu_custom_call" | custom-call | flops 2500000000 | tf_op jit(solution)/shard_map/dense/pallas_call | solution.py:39
  27.5 4.7 %arrange.2 = (bf16[1024,512]{1,0:T(8,128)(2,1)S(1)}, bf16[1024,512]{1,0:T(8,128)(2,1)S(1)}, bf16[1024,512]{1,0:T(8,128)(2,1)S(1)}, bf16[1024,512]{1,0:T(8,128)(2...) custom-call(bf16[8,512,512]{2,1,0:T(8,128)(2,1)S(1)} %place.1.refs_0, ...), custom_call_target="tpu_custom_call" | custom-call | flops 4000000000 | tf_op jit(solution)/shard_map/arrange/pallas_call | solution.py:39
  36.1 1.0 copy-done.25
  41.3 2.4 %dense.3.refs_1_ = bf16[4096,512]{1,0:T(8,128)(2,1)S(1)} custom-call(s32[4,16]{1,0:T(4,128)S(1)} %collective-permute-done.4.cols_ref, bf16[4,16,128,128]{3,2,1,0:T(8,128)(2,1)S(1)} %collective-permute-done.5.vals_ref), custom_call_target="tpu_custom_call" | custom-call | flops 2500000000 | tf_op jit(solution)/shard_map/dense/pallas_call | solution.py:39
  43.8 4.7 %arrange.3 = (bf16[1024,512]{1,0:T(8,128)(2,1)S(1)}, bf16[1024,512]{1,0:T(8,128)(2,1)S(1)}, bf16[1024,512]{1,0:T(8,128)(2,1)S(1)}, bf16[1024,512]{1,0:T(8,128)(2...) custom-call(bf16[8,512,512]{2,1,0:T(8,128)(2,1)S(1)} %place.1.refs_0, ...), custom_call_target="tpu_custom_call" | custom-call | flops 4000000000 | tf_op jit(solution)/shard_map/arrange/pallas_call | solution.py:39
  49.5 1.1 copy-done.23
  54.0 1.5 collective-permute-done.9.refs_3_
  55.5 1.5 collective-permute-start.10
  57.0 7.6 %collective-permute-done.6.refs_2_ = bf16[512,256]{1,0:T(8,128)(2,1)S(1)} collective-permute-done((bf16[512,256]{1,0:T(8,128)(2,1)S(1)}, bf16[512,256]{1,0:T(8,128)(2,1)S(1)}, u32[]{:S(2)}, u32[]{:S(2)}) %collective-permute-start.6) | collective-permute-done | bytes 262176 | tf_op jit(solution)/shard_map/ppermute | solution.py:275
  66.1 3.1 %collective-permute-done.10.refs_3_ = bf16[512,256]{1,0:T(8,128)(2,1)S(1)} collective-permute-done((bf16[512,256]{1,0:T(8,128)(2,1)}, bf16[512,256]{1,0:T(8,128)(2,1)S(1)}, u32[]{:S(2)}, u32[]{:S(2)}) %collective-permute-start.10) | collective-permute-done | bytes 262176 | tf_op jit(solution)/shard_map/ppermute | solution.py:275
  69.1 1.2 collective-permute-start.7
  72.7 1.2 copy-done.26
  73.9 1.2 copy-done.28
  75.9 1.8 %forward.5 = (f32[512,256]{1,0:T(8,128)S(1)}, f32[512,256]{1,0:T(8,128)S(1)}) custom-call(bf16[512,1024]{1,0:T(8,128)(2,1)S(1)} %copy-done.8, bf16[512,1024]{1,0:T(8,128)(2,1)S(1)} %copy-done.12, bf16[512,256]{1,0:T(8,128)(2,1)S(1)} %collective-permute-done.3.refs_2_, bf16[512,256]{1,0:T(8,128)(2,1)} %collective-permute-done.9.refs_3_, ...), custom_call_target="tpu_custom_call" | custom-call | flops 1000000000 | tf_op jit(solution)/shard_map/forward/pallas_call | solution.py:39
  78.4 3.8 %collective-permute-done.20.refs_2_ = bf16[128,1024]{1,0:T(8,128)(2,1)S(1)} collective-permute-done((bf16[128,1024]{1,0:T(8,128)(2,1)S(1)}, bf16[128,1024]{1,0:T(8,128)(2,1)S(1)}, u32[]{:S(2)}, u32[]{:S(2)}) %collective-permute-start.20) | collective-permute-done | bytes 262176 | tf_op jit(solution)/shard_map/ppermute | solution.py:272
  82.6 1.1 collective-permute-done.7.refs_2_
  83.8 1.6 forward.7
  85.4 2.3 %collective-permute-start.16 = (bf16[512,256]{1,0:T(8,128)(2,1)S(1)}, bf16[512,256]{1,0:T(8,128)(2,1)S(1)}, u32[]{:S(2)}, u32[]{:S(2)}) collective-permute-start(bf16[512,256]{1,0:T(8,128)(2,1)S(1)} %get-tuple-element.136), channel_id=1, source_target_pairs={{0,6},{2,0},{4,2},{6,4},{1,7},{3,1},{5,3},{7,5},{8,14},{10,8},{12,... | collective-permute-start | bytes 786440 | tf_op jit(solution)/shard_map/ppermute | solution.py:275
  87.7 1.7 %collective-permute-start.13 = (bf16[512,256]{1,0:T(8,128)(2,1)S(1)}, bf16[512,256]{1,0:T(8,128)(2,1)S(1)}, u32[]{:S(2)}, u32[]{:S(2)}) collective-permute-start(bf16[512,256]{1,0:T(8,128)(2,1)S(1)} %get-tuple-element.134), channel_id=1, source_target_pairs={{0,6},{2,0},{4,2},{6,4},{1,7},{3,1},{5,3},{7,5},{8,14},{10,8},{12,... | collective-permute-start | bytes 786440 | tf_op jit(solution)/shard_map/ppermute | solution.py:275
  90.1 4.6 %collective-permute-done.16.come_ref = bf16[512,256]{1,0:T(8,128)(2,1)S(1)} collective-permute-done((bf16[512,256]{1,0:T(8,128)(2,1)S(1)}, bf16[512,256]{1,0:T(8,128)(2,1)S(1)}, u32[]{:S(2)}, u32[]{:S(2)}) %collective-permute-start.16) | collective-permute-done | bytes 262176 | tf_op jit(solution)/shard_map/ppermute | solution.py:275
  94.8 3.9 %collective-permute-start.17 = (bf16[512,256]{1,0:T(8,128)(2,1)S(1)}, bf16[512,256]{1,0:T(8,128)(2,1)S(1)}, u32[]{:S(2)}, u32[]{:S(2)}) collective-permute-start(bf16[512,256]{1,0:T(8,128)(2,1)S(1)} %pass.6), channel_id=1, source_target_pairs={{0,6},{2,0},{4,2},{6,4},{1,7},{3,1},{5,3},{7,5},{8,14},{10,8},{12,... | collective-permute-start | bytes 786440 | tf_op jit(solution)/shard_map/ppermute | solution.py:275
  98.7 1.6 %collective-permute-done.13.come_ref = bf16[512,256]{1,0:T(8,128)(2,1)S(1)} collective-permute-done((bf16[512,256]{1,0:T(8,128)(2,1)S(1)}, bf16[512,256]{1,0:T(8,128)(2,1)S(1)}, u32[]{:S(2)}, u32[]{:S(2)}) %collective-permute-start.13) | collective-permute-done | bytes 262176 | tf_op jit(solution)/shard_map/ppermute | solution.py:275
  100.4 3.9 %collective-permute-start.14 = (bf16[512,256]{1,0:T(8,128)(2,1)S(1)}, bf16[512,256]{1,0:T(8,128)(2,1)S(1)}, u32[]{:S(2)}, u32[]{:S(2)}) collective-permute-start(bf16[512,256]{1,0:T(8,128)(2,1)S(1)} %pass.4), channel_id=1, source_target_pairs={{0,6},{2,0},{4,2},{6,4},{1,7},{3,1},{5,3},{7,5},{8,14},{10,8},{12,... | collective-permute-start | bytes 786440 | tf_op jit(solution)/shard_map/ppermute | solution.py:275
  105.9 4.8 %collective-permute-done.14.come_ref = bf16[512,256]{1,0:T(8,128)(2,1)S(1)} collective-permute-done((bf16[512,256]{1,0:T(8,128)(2,1)S(1)}, bf16[512,256]{1,0:T(8,128)(2,1)S(1)}, u32[]{:S(2)}, u32[]{:S(2)}) %collective-permute-start.14) | collective-permute-done | bytes 262176 | tf_op jit(solution)/shard_map/ppermute | solution.py:275
  110.8 4.5 %collective-permute-start.15 = (bf16[512,256]{1,0:T(8,128)(2,1)S(1)}, bf16[512,256]{1,0:T(8,128)(2,1)S(1)}, u32[]{:S(2)}, u32[]{:S(2)}) collective-permute-start(bf16[512,256]{1,0:T(8,128)(2,1)S(1)} %pass.5), channel_id=1, source_target_pairs={{0,6},{2,0},{4,2},{6,4},{1,7},{3,1},{5,3},{7,5},{8,14},{10,8},{12,... | collective-permute-start | bytes 786440 | tf_op jit(solution)/shard_map/ppermute | solution.py:275
  116.2 5.9 %collective-permute-done.15.refs_6_ = bf16[512,256]{1,0:T(8,128)(2,1)S(1)} collective-permute-done((bf16[512,256]{1,0:T(8,128)(2,1)S(1)}, bf16[512,256]{1,0:T(8,128)(2,1)S(1)}, u32[]{:S(2)}, u32[]{:S(2)}) %collective-permute-start.15) | collective-permute-done | bytes 262176 | tf_op jit(solution)/shard_map/ppermute | solution.py:275
  122.1 4.3 %collective-permute-done.23.refs_5_ = bf16[512,256]{1,0:T(8,128)(2,1)S(1)} collective-permute-done((bf16[512,256]{1,0:T(8,128)(2,1)S(1)}, bf16[512,256]{1,0:T(8,128)(2,1)S(1)}, u32[]{:S(2)}, u32[]{:S(2)}) %collective-permute-start.23) | collective-permute-done | bytes 262176 | tf_op jit(solution)/shard_map/ppermute | solution.py:275
  126.4 1.3 grad.1
  129.0 2.2 %collective-permute-start.26 = (bf16[256,256]{1,0:T(8,128)(2,1)S(1)}, bf16[256,256]{1,0:T(8,128)(2,1)S(1)}, u32[]{:S(2)}, u32[]{:S(2)}) collective-permute-start(bf16[256,256]{1,0:T(8,128)(2,1)S(1)} %get-tuple-element.155), channel_id=1, source_target_pairs={{0,24},{8,16},{16,8},{24,0},{1,25},{9,17},{17,9},{25,1},{2,26},{10... | collective-permute-start | bytes 393224 | tf_op jit(solution)/shard_map/ppermute | solution.py:272
  131.2 2.3 %collective-permute-done.24.refs_1_ = bf16[256,256]{1,0:T(8,128)(2,1)S(1)} collective-permute-done((bf16[256,256]{1,0:T(8,128)(2,1)S(1)}, bf16[256,256]{1,0:T(8,128)(2,1)S(1)}, u32[]{:S(2)}, u32[]{:S(2)}) %collective-permute-start.24) | collective-permute-done | bytes 131104 | tf_op jit(solution)/shard_map/ppermute | solution.py:272
  133.5 1.8 %collective-permute-done.25.refs_2_ = bf16[256,256]{1,0:T(8,128)(2,1)S(1)} collective-permute-done((bf16[256,256]{1,0:T(8,128)(2,1)S(1)}, bf16[256,256]{1,0:T(8,128)(2,1)S(1)}, u32[]{:S(2)}, u32[]{:S(2)}) %collective-permute-start.25) | collective-permute-done | bytes 131104 | tf_op jit(solution)/shard_map/ppermute | solution.py:272
  135.7 4.8 %collective-permute-done.27.refs_1_ = bf16[256,256]{1,0:T(8,128)(2,1)S(1)} collective-permute-done((bf16[256,256]{1,0:T(8,128)(2,1)S(1)}, bf16[256,256]{1,0:T(8,128)(2,1)S(1)}, u32[]{:S(2)}, u32[]{:S(2)}) %collective-permute-start.27) | collective-permute-done | bytes 131104 | tf_op jit(solution)/shard_map/ppermute | solution.py:421
  140.5 3.5 %collective-permute-start.28 = (bf16[256,256]{1,0:T(8,128)(2,1)S(1)}, bf16[256,256]{1,0:T(8,128)(2,1)S(1)}, u32[]{:S(2)}, u32[]{:S(2)}) collective-permute-start(bf16[256,256]{1,0:T(8,128)(2,1)S(1)} %sum.4.refs_0_), channel_id=1, source_target_pairs={{0,4},{2,6},{4,0},{6,2},{1,5},{3,7},{5,1},{7,3},{8,12},{10,14},{12... | collective-permute-start | bytes 393224 | tf_op jit(solution)/shard_map/ppermute | solution.py:421
  144.0 4.4 %collective-permute-done.28.refs_1_ = bf16[256,256]{1,0:T(8,128)(2,1)S(1)} collective-permute-done((bf16[256,256]{1,0:T(8,128)(2,1)S(1)}, bf16[256,256]{1,0:T(8,128)(2,1)S(1)}, u32[]{:S(2)}, u32[]{:S(2)}) %collective-permute-start.28) | collective-permute-done | bytes 131104 | tf_op jit(solution)/shard_map/ppermute | solution.py:421
  148.4 1.4 collective-permute-start.29
  149.8 2.2 %collective-permute-start.31 = (bf16[256,256]{1,0:T(8,128)(2,1)S(1)}, bf16[256,256]{1,0:T(8,128)(2,1)S(1)}, u32[]{:S(2)}, u32[]{:S(2)}) collective-permute-start(bf16[256,256]{1,0:T(8,128)(2,1)S(1)} %sum.5.refs_1_), channel_id=1, source_target_pairs={{0,24},{8,16},{16,8},{24,0},{1,25},{9,17},{17,9},{25,1},{2,26},{10... | collective-permute-start | bytes 393224 | tf_op jit(solution)/shard_map/ppermute | solution.py:272
  152.0 1.5 collective-permute-done.29.refs_2_
  153.4 2.7 %collective-permute-done.30.refs_3_ = bf16[256,256]{1,0:T(8,128)(2,1)S(1)} collective-permute-done((bf16[256,256]{1,0:T(8,128)(2,1)S(1)}, bf16[256,256]{1,0:T(8,128)(2,1)S(1)}, u32[]{:S(2)}, u32[]{:S(2)}) %collective-permute-start.30) | collective-permute-done | bytes 131104 | tf_op jit(solution)/shard_map/ppermute | solution.py:272
  157.7 2.0 %last.1 = f32[1024,512]{1,0:T(8,128)} custom-call(s32[3]{0:T(128)S(1)} %pad_add_fusion.refs_0_, bf16[256,256]{1,0:T(8,128)(2,1)S(1)} %sum.5.refs_1_, bf16[256,256]{1,0:T(8,128)(2,1)S(1)} %collective-permute-done.29.refs_2_, bf16[256,256]{1,0:T(8,128)(2,1)S(1)} %collective-permute-done.30.refs_3_, bf16[256,256]{1,0:T(8,128)(2,1)S(1)} %collective-permute-done.31.refs_4_, ...), custom_call_target="tpu_custom_call" | custom-call | flops 2000000000 | tf_op jit(solution)/shard_map/last/pallas_call | solution.py:39
  (138 shorter events, 27.5 us)
Async XLA Ops:
  0.6 40.7 %collective-permute-start.5 = (bf16[4,16,128,128]{3,2,1,0:T(8,128)(2,1)}, bf16[4,16,128,128]{3,2,1,0:T(8,128)(2,1)S(1)}, u32[]{:S(2)}, u32[]{:S(2)}) collective-permute-start(bf16[4,16,128,128]{3,2,1,0:T(8,128)(2,1)} %vals_ref.1), channel_id=1, source_target_pairs={{0,1},{1,0},{2,3},{3,2},{4,5},{5,4},{6,7},{7,6},{8,9},{9,8},{10,11... | collective-permute-start | bytes 6291464 | tf_op jit(solution)/shard_map/ppermute | solution.py:269
  3.7 15.1 %all-to-all-start = ((s32[32,8,128]{2,1,0:T(8,128)}), s32[32,8,128]{2,1,0:T(8,128)S(1)}, u32[]{:S(2)}, u32[]{:S(2)}) async-start(s32[32,8,128]{2,1,0:T(8,128)} %index.1), calls=%async_computation | async-start | bytes 262144 | tf_op jit(solution)/shard_map/all_to_all | solution.py:283
  20.0 19.1 %collective-permute-start = (bf16[2,128,256]{2,1,0:T(8,128)(2,1)S(1)}, bf16[2,128,256]{2,1,0:T(8,128)(2,1)S(1)}, u32[]{:S(2)}, u32[]{:S(2)}) collective-permute-start(bf16[2,128,256]{2,1,0:T(8,128)(2,1)S(1)} %get-tuple-element.86), channel_id=1, source_target_pairs={{0,8},{8,0},{16,24},{24,16},{1,9},{9,1},{17,25},{25,17},{2,10},{10... | collective-permute-start | bytes 393224 | tf_op jit(solution)/shard_map/ppermute | solution.py:272
  20.9 18.1 %collective-permute-start.1 = (bf16[2,128,256]{2,1,0:T(8,128)(2,1)S(1)}, bf16[2,128,256]{2,1,0:T(8,128)(2,1)S(1)}, u32[]{:S(2)}, u32[]{:S(2)}) collective-permute-start(bf16[2,128,256]{2,1,0:T(8,128)(2,1)S(1)} %get-tuple-element.87), channel_id=1, source_target_pairs={{0,16},{8,24},{16,0},{24,8},{1,17},{9,25},{17,1},{25,9},{2,18},{10... | collective-permute-start | bytes 393224 | tf_op jit(solution)/shard_map/ppermute | solution.py:272
  21.6 17.5 %collective-permute-start.2 = (bf16[2,128,256]{2,1,0:T(8,128)(2,1)S(1)}, bf16[2,128,256]{2,1,0:T(8,128)(2,1)S(1)}, u32[]{:S(2)}, u32[]{:S(2)}) collective-permute-start(bf16[2,128,256]{2,1,0:T(8,128)(2,1)S(1)} %get-tuple-element.88), channel_id=1, source_target_pairs={{0,24},{8,16},{16,8},{24,0},{1,25},{9,17},{17,9},{25,1},{2,26},{10... | collective-permute-start | bytes 393224 | tf_op jit(solution)/shard_map/ppermute | solution.py:272
  39.1 1.6 %collective-permute-start.8 = (bf16[512,256]{1,0:T(8,128)(2,1)S(1)}, bf16[512,256]{1,0:T(8,128)(2,1)S(1)}, u32[]{:S(2)}, u32[]{:S(2)}) collective-permute-start(bf16[512,256]{1,0:T(8,128)(2,1)S(1)} %get-tuple-element.109), channel_id=1, source_target_pairs={{0,1},{1,0},{2,3},{3,2},{4,5},{5,4},{6,7},{7,6},{8,9},{9,8},{10,11... | collective-permute-start | bytes 786440 | tf_op jit(solution)/shard_map/ppermute | solution.py:269
  39.2 2.1 %collective-permute-start.4 = (s32[4,16]{1,0:T(4,128)S(1)}, s32[4,16]{1,0:T(4,128)S(1)}, u32[]{:S(2)}, u32[]{:S(2)}) collective-permute-start(s32[4,16]{1,0:T(4,128)S(1)} %fusion.cols_ref), channel_id=1, source_target_pairs={{0,1},{1,0},{2,3},{3,2},{4,5},{5,4},{6,7},{7,6},{8,9},{9,8},{10,11... | collective-permute-start | bytes 776 | tf_op jit(solution)/shard_map/ppermute | solution.py:269
  39.7 13.9 %collective-permute-start.3 = (bf16[512,256]{1,0:T(8,128)(2,1)S(1)}, bf16[512,256]{1,0:T(8,128)(2,1)S(1)}, u32[]{:S(2)}, u32[]{:S(2)}) collective-permute-start(bf16[512,256]{1,0:T(8,128)(2,1)S(1)} %get-tuple-element.100.refs_2_), channel_id=1, source_target_pairs={{0,2},{2,4},{4,6},{6,0},{1,3},{3,5},{5,7},{7,1},{8,10},{10,12},{12... | collective-permute-start | bytes 786440 | tf_op jit(solution)/shard_map/ppermute | solution.py:275
  40.7 14.8 %collective-permute-start.9 = (bf16[512,256]{1,0:T(8,128)(2,1)S(1)}, bf16[512,256]{1,0:T(8,128)(2,1)}, u32[]{:S(2)}, u32[]{:S(2)}) collective-permute-start(bf16[512,256]{1,0:T(8,128)(2,1)S(1)} %collective-permute-done.8.refs_3_), channel_id=1, source_target_pairs={{0,2},{2,4},{4,6},{6,0},{1,3},{3,5},{5,7},{7,1},{8,10},{10,12},{12... | collective-permute-start | bytes 786440 | tf_op jit(solution)/shard_map/ppermute | solution.py:275
  43.8 20.9 %copy-start.3 = (bf16[512,1024]{1,0:T(8,128)(2,1)S(1)}, bf16[512,1024]{1,0:T(8,128)(2,1)}, u32[]{:S(2)}) copy-start(bf16[512,1024]{1,0:T(8,128)(2,1)} %refs_1_.3) | copy-start | bytes 3145732
  43.8 22.1 %copy-start.37 = (bf16[512,512]{1,0:T(8,128)(2,1)S(1)}, bf16[512,512]{1,0:T(8,128)(2,1)}, u32[]{:S(2)}) copy-start(bf16[512,512]{1,0:T(8,128)(2,1)} %param.13) | copy-start | bytes 1572868
  53.6 11.8 %copy-start.9 = (bf16[512,1024]{1,0:T(8,128)(2,1)}, bf16[512,1024]{1,0:T(8,128)(2,1)S(1)}, u32[]{:S(2)}) copy-start(bf16[512,1024]{1,0:T(8,128)(2,1)S(1)} %get-tuple-element.111.refs_1_) | copy-start | bytes 3145732
  53.6 11.8 %copy-start.11 = (bf16[512,1024]{1,0:T(8,128)(2,1)}, bf16[512,1024]{1,0:T(8,128)(2,1)S(1)}, u32[]{:S(2)}) copy-start(bf16[512,1024]{1,0:T(8,128)(2,1)S(1)} %get-tuple-element.113.refs_1_) | copy-start | bytes 3145732
  53.6 11.8 %copy-start.19 = (bf16[1024,512]{1,0:T(8,128)(2,1)}, bf16[1024,512]{1,0:T(8,128)(2,1)S(1)}, u32[]{:S(2)}) copy-start(bf16[1024,512]{1,0:T(8,128)(2,1)S(1)} %get-tuple-element.146.turned_b) | copy-start | bytes 3145732
  53.6 11.0 %collective-permute-start.6 = (bf16[512,256]{1,0:T(8,128)(2,1)S(1)}, bf16[512,256]{1,0:T(8,128)(2,1)S(1)}, u32[]{:S(2)}, u32[]{:S(2)}) collective-permute-start(bf16[512,256]{1,0:T(8,128)(2,1)S(1)} %collective-permute-done.3.refs_2_), channel_id=1, source_target_pairs={{0,2},{2,4},{4,6},{6,0},{1,3},{3,5},{5,7},{7,1},{8,10},{10,12},{12... | collective-permute-start | bytes 786440 | tf_op jit(solution)/shard_map/ppermute | solution.py:275
  55.5 13.6 %collective-permute-start.10 = (bf16[512,256]{1,0:T(8,128)(2,1)}, bf16[512,256]{1,0:T(8,128)(2,1)S(1)}, u32[]{:S(2)}, u32[]{:S(2)}) collective-permute-start(bf16[512,256]{1,0:T(8,128)(2,1)} %collective-permute-done.9.refs_3_), channel_id=1, source_target_pairs={{0,2},{2,4},{4,6},{6,0},{1,3},{3,5},{5,7},{7,1},{8,10},{10,12},{12... | collective-permute-start | bytes 786440 | tf_op jit(solution)/shard_map/ppermute | solution.py:275
  65.4 6.4 %collective-permute-start.19 = (bf16[128,1024]{1,0:T(8,128)(2,1)S(1)}, bf16[128,1024]{1,0:T(8,128)(2,1)S(1)}, u32[]{:S(2)}, u32[]{:S(2)}) collective-permute-start(bf16[128,1024]{1,0:T(8,128)(2,1)S(1)} %get-tuple-element.142), channel_id=1, source_target_pairs={{0,8},{8,0},{16,24},{24,16},{1,9},{9,1},{17,25},{25,17},{2,10},{10... | collective-permute-start | bytes 786440 | tf_op jit(solution)/shard_map/ppermute | solution.py:272
  65.9 11.8 %copy-start.6 = (bf16[512,1024]{1,0:T(8,128)(2,1)S(1)}, bf16[512,1024]{1,0:T(8,128)(2,1)}, u32[]{:S(2)}) copy-start(bf16[512,1024]{1,0:T(8,128)(2,1)} %copy-done.5) | copy-start | bytes 3145732
  65.9 11.8 %copy-start.10 = (bf16[512,1024]{1,0:T(8,128)(2,1)S(1)}, bf16[512,1024]{1,0:T(8,128)(2,1)}, u32[]{:S(2)}) copy-start(bf16[512,1024]{1,0:T(8,128)(2,1)} %copy-done.9) | copy-start | bytes 3145732
  66.0 16.7 %collective-permute-start.12 = (bf16[512,256]{1,0:T(8,128)(2,1)S(1)}, bf16[512,256]{1,0:T(8,128)(2,1)S(1)}, u32[]{:S(2)}, u32[]{:S(2)}) collective-permute-start(bf16[512,256]{1,0:T(8,128)(2,1)S(1)} %get-tuple-element.158), channel_id=1, source_target_pairs={{0,1},{1,0},{2,3},{3,2},{4,5},{5,4},{6,7},{7,6},{8,9},{9,8},{10,11... | collective-permute-start | bytes 786440 | tf_op jit(solution)/shard_map/ppermute | solution.py:269
  69.1 13.5 %collective-permute-start.11 = (bf16[512,256]{1,0:T(8,128)(2,1)S(1)}, bf16[512,256]{1,0:T(8,128)(2,1)S(1)}, u32[]{:S(2)}, u32[]{:S(2)}) collective-permute-start(bf16[512,256]{1,0:T(8,128)(2,1)S(1)} %collective-permute-done.10.refs_3_), channel_id=1, source_target_pairs={{0,2},{2,4},{4,6},{6,0},{1,3},{3,5},{5,7},{7,1},{8,10},{10,12},{12... | collective-permute-start | bytes 786440 | tf_op jit(solution)/shard_map/ppermute | solution.py:275
  69.1 14.6 %collective-permute-start.7 = (bf16[512,256]{1,0:T(8,128)(2,1)S(1)}, bf16[512,256]{1,0:T(8,128)(2,1)S(1)}, u32[]{:S(2)}, u32[]{:S(2)}) collective-permute-start(bf16[512,256]{1,0:T(8,128)(2,1)S(1)} %collective-permute-done.6.refs_2_), channel_id=1, source_target_pairs={{0,2},{2,4},{4,6},{6,0},{1,3},{3,5},{5,7},{7,1},{8,10},{10,12},{12... | collective-permute-start | bytes 786440 | tf_op jit(solution)/shard_map/ppermute | solution.py:275
  70.3 11.9 %collective-permute-start.20 = (bf16[128,1024]{1,0:T(8,128)(2,1)S(1)}, bf16[128,1024]{1,0:T(8,128)(2,1)S(1)}, u32[]{:S(2)}, u32[]{:S(2)}) collective-permute-start(bf16[128,1024]{1,0:T(8,128)(2,1)S(1)} %get-tuple-element.143), channel_id=1, source_target_pairs={{0,16},{8,24},{16,0},{24,8},{1,17},{9,25},{17,1},{25,9},{2,18},{10... | collective-permute-start | bytes 786440 | tf_op jit(solution)/shard_map/ppermute | solution.py:272
  71.9 10.4 %collective-permute-start.21 = (bf16[128,1024]{1,0:T(8,128)(2,1)S(1)}, bf16[128,1024]{1,0:T(8,128)(2,1)S(1)}, u32[]{:S(2)}, u32[]{:S(2)}) collective-permute-start(bf16[128,1024]{1,0:T(8,128)(2,1)S(1)} %get-tuple-element.144), channel_id=1, source_target_pairs={{0,24},{8,16},{16,8},{24,0},{1,25},{9,17},{17,9},{25,1},{2,26},{10... | collective-permute-start | bytes 786440 | tf_op jit(solution)/shard_map/ppermute | solution.py:272
  82.5 43.8 %collective-permute-start.22 = (bf16[1024,512]{1,0:T(8,128)(2,1)S(1)}, bf16[1024,512]{1,0:T(8,128)(2,1)S(1)}, u32[]{:S(2)}, u32[]{:S(2)}) collective-permute-start(bf16[1024,512]{1,0:T(8,128)(2,1)S(1)} %turn.1.refs_1_), channel_id=1, source_target_pairs={{0,1},{1,0},{2,3},{3,2},{4,5},{5,4},{6,7},{7,6},{8,9},{9,8},{10,11... | collective-permute-start | bytes 3145736 | tf_op jit(solution)/shard_map/ppermute | solution.py:269
  85.4 18.9 %copy-start.16 = (bf16[1024,512]{1,0:T(8,128)(2,1)S(1)}, bf16[1024,512]{1,0:T(8,128)(2,1)}, u32[]{:S(2)}) copy-start(bf16[1024,512]{1,0:T(8,128)(2,1)} %copy-done.15) | copy-start | bytes 3145732
  85.4 18.9 %copy-start.22 = (bf16[1024,512]{1,0:T(8,128)(2,1)S(1)}, bf16[1024,512]{1,0:T(8,128)(2,1)}, u32[]{:S(2)}) copy-start(bf16[1024,512]{1,0:T(8,128)(2,1)} %copy-done.21) | copy-start | bytes 3145732
  85.4 9.3 %collective-permute-start.16 = (bf16[512,256]{1,0:T(8,128)(2,1)S(1)}, bf16[512,256]{1,0:T(8,128)(2,1)S(1)}, u32[]{:S(2)}, u32[]{:S(2)}) collective-permute-start(bf16[512,256]{1,0:T(8,128)(2,1)S(1)} %get-tuple-element.136), channel_id=1, source_target_pairs={{0,6},{2,0},{4,2},{6,4},{1,7},{3,1},{5,3},{7,5},{8,14},{10,8},{12,... | collective-permute-start | bytes 786440 | tf_op jit(solution)/shard_map/ppermute | solution.py:275
  87.7 12.6 %collective-permute-start.13 = (bf16[512,256]{1,0:T(8,128)(2,1)S(1)}, bf16[512,256]{1,0:T(8,128)(2,1)S(1)}, u32[]{:S(2)}, u32[]{:S(2)}) collective-permute-start(bf16[512,256]{1,0:T(8,128)(2,1)S(1)} %get-tuple-element.134), channel_id=1, source_target_pairs={{0,6},{2,0},{4,2},{6,4},{1,7},{3,1},{5,3},{7,5},{8,14},{10,8},{12,... | collective-permute-start | bytes 786440 | tf_op jit(solution)/shard_map/ppermute | solution.py:275
  94.8 11.2 %collective-permute-start.17 = (bf16[512,256]{1,0:T(8,128)(2,1)S(1)}, bf16[512,256]{1,0:T(8,128)(2,1)S(1)}, u32[]{:S(2)}, u32[]{:S(2)}) collective-permute-start(bf16[512,256]{1,0:T(8,128)(2,1)S(1)} %pass.6), channel_id=1, source_target_pairs={{0,6},{2,0},{4,2},{6,4},{1,7},{3,1},{5,3},{7,5},{8,14},{10,8},{12,... | collective-permute-start | bytes 786440 | tf_op jit(solution)/shard_map/ppermute | solution.py:275
  100.3 15.1 %copy-start.14 = (bf16[1024,512]{1,0:T(8,128)(2,1)S(1)}, bf16[1024,512]{1,0:T(8,128)(2,1)}, u32[]{:S(2)}) copy-start(bf16[1024,512]{1,0:T(8,128)(2,1)} %copy-done.13) | copy-start | bytes 3145732
  100.3 15.1 %copy-start.20 = (bf16[1024,512]{1,0:T(8,128)(2,1)S(1)}, bf16[1024,512]{1,0:T(8,128)(2,1)}, u32[]{:S(2)}) copy-start(bf16[1024,512]{1,0:T(8,128)(2,1)} %copy-done.19) | copy-start | bytes 3145732
  100.4 10.4 %collective-permute-start.14 = (bf16[512,256]{1,0:T(8,128)(2,1)S(1)}, bf16[512,256]{1,0:T(8,128)(2,1)S(1)}, u32[]{:S(2)}, u32[]{:S(2)}) collective-permute-start(bf16[512,256]{1,0:T(8,128)(2,1)S(1)} %pass.4), channel_id=1, source_target_pairs={{0,6},{2,0},{4,2},{6,4},{1,7},{3,1},{5,3},{7,5},{8,14},{10,8},{12,... | collective-permute-start | bytes 786440 | tf_op jit(solution)/shard_map/ppermute | solution.py:275
  105.9 10.2 %collective-permute-start.18 = (bf16[512,256]{1,0:T(8,128)(2,1)S(1)}, bf16[512,256]{1,0:T(8,128)(2,1)S(1)}, u32[]{:S(2)}, u32[]{:S(2)}) collective-permute-start(bf16[512,256]{1,0:T(8,128)(2,1)S(1)} %get-tuple-element.138), channel_id=1, source_target_pairs={{0,1},{1,0},{2,3},{3,2},{4,5},{5,4},{6,7},{7,6},{8,9},{9,8},{10,11... | collective-permute-start | bytes 786440 | tf_op jit(solution)/shard_map/ppermute | solution.py:269
  110.8 11.2 %collective-permute-start.15 = (bf16[512,256]{1,0:T(8,128)(2,1)S(1)}, bf16[512,256]{1,0:T(8,128)(2,1)S(1)}, u32[]{:S(2)}, u32[]{:S(2)}) collective-permute-start(bf16[512,256]{1,0:T(8,128)(2,1)S(1)} %pass.5), channel_id=1, source_target_pairs={{0,6},{2,0},{4,2},{6,4},{1,7},{3,1},{5,3},{7,5},{8,14},{10,8},{12,... | collective-permute-start | bytes 786440 | tf_op jit(solution)/shard_map/ppermute | solution.py:275
  115.4 11.0 %collective-permute-start.23 = (bf16[512,256]{1,0:T(8,128)(2,1)S(1)}, bf16[512,256]{1,0:T(8,128)(2,1)S(1)}, u32[]{:S(2)}, u32[]{:S(2)}) collective-permute-start(bf16[512,256]{1,0:T(8,128)(2,1)S(1)} %pass.7), channel_id=1, source_target_pairs={{0,6},{2,0},{4,2},{6,4},{1,7},{3,1},{5,3},{7,5},{8,14},{10,8},{12,... | collective-permute-start | bytes 786440 | tf_op jit(solution)/shard_map/ppermute | solution.py:275
  127.7 5.8 %collective-permute-start.24 = (bf16[256,256]{1,0:T(8,128)(2,1)S(1)}, bf16[256,256]{1,0:T(8,128)(2,1)S(1)}, u32[]{:S(2)}, u32[]{:S(2)}) collective-permute-start(bf16[256,256]{1,0:T(8,128)(2,1)S(1)} %get-tuple-element.153), channel_id=1, source_target_pairs={{0,8},{8,0},{16,24},{24,16},{1,9},{9,1},{17,25},{25,17},{2,10},{10... | collective-permute-start | bytes 393224 | tf_op jit(solution)/shard_map/ppermute | solution.py:272
  128.4 6.9 %collective-permute-start.25 = (bf16[256,256]{1,0:T(8,128)(2,1)S(1)}, bf16[256,256]{1,0:T(8,128)(2,1)S(1)}, u32[]{:S(2)}, u32[]{:S(2)}) collective-permute-start(bf16[256,256]{1,0:T(8,128)(2,1)S(1)} %get-tuple-element.154), channel_id=1, source_target_pairs={{0,16},{8,24},{16,0},{24,8},{1,17},{9,25},{17,1},{25,9},{2,18},{10... | collective-permute-start | bytes 393224 | tf_op jit(solution)/shard_map/ppermute | solution.py:272
  129.0 6.3 %collective-permute-start.26 = (bf16[256,256]{1,0:T(8,128)(2,1)S(1)}, bf16[256,256]{1,0:T(8,128)(2,1)S(1)}, u32[]{:S(2)}, u32[]{:S(2)}) collective-permute-start(bf16[256,256]{1,0:T(8,128)(2,1)S(1)} %get-tuple-element.155), channel_id=1, source_target_pairs={{0,24},{8,16},{16,8},{24,0},{1,25},{9,17},{17,9},{25,1},{2,26},{10... | collective-permute-start | bytes 393224 | tf_op jit(solution)/shard_map/ppermute | solution.py:272
  135.4 5.0 %collective-permute-start.27 = (bf16[256,256]{1,0:T(8,128)(2,1)S(1)}, bf16[256,256]{1,0:T(8,128)(2,1)S(1)}, u32[]{:S(2)}, u32[]{:S(2)}) collective-permute-start(bf16[256,256]{1,0:T(8,128)(2,1)S(1)} %sum.3.refs_0_), channel_id=1, source_target_pairs={{0,2},{2,0},{4,6},{6,4},{1,3},{3,1},{5,7},{7,5},{8,10},{10,8},{12,... | collective-permute-start | bytes 393224 | tf_op jit(solution)/shard_map/ppermute | solution.py:421
  140.5 7.9 %collective-permute-start.28 = (bf16[256,256]{1,0:T(8,128)(2,1)S(1)}, bf16[256,256]{1,0:T(8,128)(2,1)S(1)}, u32[]{:S(2)}, u32[]{:S(2)}) collective-permute-start(bf16[256,256]{1,0:T(8,128)(2,1)S(1)} %sum.4.refs_0_), channel_id=1, source_target_pairs={{0,4},{2,6},{4,0},{6,2},{1,5},{3,7},{5,1},{7,3},{8,12},{10,14},{12... | collective-permute-start | bytes 393224 | tf_op jit(solution)/shard_map/ppermute | solution.py:421
  148.4 5.0 %collective-permute-start.29 = (bf16[256,256]{1,0:T(8,128)(2,1)S(1)}, bf16[256,256]{1,0:T(8,128)(2,1)S(1)}, u32[]{:S(2)}, u32[]{:S(2)}) collective-permute-start(bf16[256,256]{1,0:T(8,128)(2,1)S(1)} %sum.5.refs_1_), channel_id=1, source_target_pairs={{0,8},{8,0},{16,24},{24,16},{1,9},{9,1},{17,25},{25,17},{2,10},{10... | collective-permute-start | bytes 393224 | tf_op jit(solution)/shard_map/ppermute | solution.py:272
  149.8 6.4 %collective-permute-start.30 = (bf16[256,256]{1,0:T(8,128)(2,1)S(1)}, bf16[256,256]{1,0:T(8,128)(2,1)S(1)}, u32[]{:S(2)}, u32[]{:S(2)}) collective-permute-start(bf16[256,256]{1,0:T(8,128)(2,1)S(1)} %sum.5.refs_1_), channel_id=1, source_target_pairs={{0,16},{8,24},{16,0},{24,8},{1,17},{9,25},{17,1},{25,9},{2,18},{10... | collective-permute-start | bytes 393224 | tf_op jit(solution)/shard_map/ppermute | solution.py:272
  149.8 6.4 %collective-permute-start.31 = (bf16[256,256]{1,0:T(8,128)(2,1)S(1)}, bf16[256,256]{1,0:T(8,128)(2,1)S(1)}, u32[]{:S(2)}, u32[]{:S(2)}) collective-permute-start(bf16[256,256]{1,0:T(8,128)(2,1)S(1)} %sum.5.refs_1_), channel_id=1, source_target_pairs={{0,24},{8,16},{16,8},{24,0},{1,25},{9,17},{17,9},{25,1},{2,26},{10... | collective-permute-start | bytes 393224 | tf_op jit(solution)/shard_map/ppermute | solution.py:272
  152.0 5.6 %collective-permute-start.32 = (bf16[256,256]{1,0:T(8,128)(2,1)S(1)}, bf16[256,256]{1,0:T(8,128)(2,1)S(1)}, u32[]{:S(2)}, u32[]{:S(2)}) collective-permute-start(bf16[256,256]{1,0:T(8,128)(2,1)S(1)} %sum.5.refs_1_), channel_id=1, source_target_pairs={{0,1},{1,0},{2,3},{3,2},{4,5},{5,4},{6,7},{7,6},{8,9},{9,8},{10,11... | collective-permute-start | bytes 393224 | tf_op jit(solution)/shard_map/ppermute | solution.py:269
  153.4 4.1 %collective-permute-start.33 = (bf16[256,256]{1,0:T(8,128)(2,1)S(1)}, bf16[256,256]{1,0:T(8,128)(2,1)S(1)}, u32[]{:S(2)}, u32[]{:S(2)}) collective-permute-start(bf16[256,256]{1,0:T(8,128)(2,1)S(1)} %collective-permute-done.29.refs_2_), channel_id=1, source_target_pairs={{0,1},{1,0},{2,3},{3,2},{4,5},{5,4},{6,7},{7,6},{8,9},{9,8},{10,11... | collective-permute-start | bytes 393224 | tf_op jit(solution)/shard_map/ppermute | solution.py:269
  156.1 1.4 collective-permute-start.34
  156.1 1.5 collective-permute-start.35
  (29 other events, 101.2 us)

commit v6 on v5

--- a/solution.py
+++ b/solution.py
@@ -43,7 +43,7 @@
         out_specs=tuple(vmem for _ in outs),
         scratch_shapes=list(scratch),
         compiler_params=pltpu.CompilerParams(vmem_limit_bytes=size + (6 << 20)),
-        cost_estimate=pl.CostEstimate(flops=int(us * 1e9), bytes_accessed=0, transcendentals=0),
+        cost_estimate=pl.CostEstimate(flops=int(us * 2.5e8), bytes_accessed=0, transcendentals=0),
         name=name,
     )(*(value for _, value in ins))
 
@@ -56,7 +56,11 @@
         self.pair = rows // (self.grp * self.dom)
         self.piece = self.grp * self.pair
         self.per_grp = self.dom * self.pair
-        assert rows // 128 < 8 and self.pair <= 128
+        assert rows // 128 < 7 and self.pair <= 128
+
+    def before(self, d):
+        inner = d % self.dom
+        return d - inner + (inner - 2) % self.dom
 
 
 def column(row):
@@ -84,6 +88,8 @@
     out_ref[...] = jnp.zeros_like(out_ref)
     for d in range(z.grp * z.dom):
         out_ref[d, 0:1, 0:z.pair] = want[d:d + 1, :]
+        near = z.before(d)
+        out_ref[d, 7:8, 0:z.pair] = want[near:near + 1, :]
     across_grp = (source_r >> log2(z.dom)) ^ me_ref[0]
     inner = source_r & (z.dom - 1)
     slot = (inner * z.grp + across_grp) * z.pair + rank_r
@@ -92,19 +98,22 @@
         out_ref[:, 1 + i:2 + i, :] = jnp.broadcast_to(lanes[None], (z.grp * z.dom, 1, 128))
 
 
-def product_kernel(z, me_ref, features_ref, weight_ref, *outs):
-    half = outs[0].shape[1]
+def product_kernel(z, me_ref, weight_ref, *refs):
+    parts, outs = refs[:-2], refs[-2:]
+    half, size = outs[0].shape[1], parts[0].shape[0]
     for flip, out in enumerate(outs):
         at = pl.multiple_of((me_ref[2] ^ flip) * half, half)
-        out[...] = dot(features_ref[...], weight_ref[:, pl.ds(at, half)]).astype(BF16)
-
-
-def send_kernel(z, me_ref, message_ref, own_ref, other_ref, pick_ref, *outs):
+        for i, part in enumerate(parts):
+            product = dot(part[...], weight_ref[:, pl.ds(at, half)])
+            out[i * size:(i + 1) * size, :] = product.astype(BF16)
+
+
+def send_kernel(z, line, me_ref, message_ref, own_ref, other_ref, pick_ref, *outs):
     devices, height, width = message_ref.shape
     message = message_ref[...].reshape(devices * height, width)
     shape = (z.rows, devices * height)
     asker = (iota(shape, 0) >> log2(z.pair)) ^ (me_ref[0] * z.dom)
-    spread = one_hot(iota(shape, 1) == asker * height)
+    spread = one_hot(iota(shape, 1) == asker * height + line)
     high = dot(spread, (message >> 4).astype(F32).astype(BF16))
     low = dot(spread, (message & 15).astype(F32).astype(BF16))
     mine = iota((z.rows, width), 1) == (iota((z.rows, width), 0) & (z.pair - 1))
@@ -116,10 +125,15 @@
             outs[s][flip] = got[s * z.per_grp:(s + 1) * z.per_grp, :]
 
 
-def rows_kernel(z, pick_ref, features_ref, *outs):
+def rows_kernel(z, pick_ref, *refs):
+    parts, outs = refs[:-z.grp], refs[-z.grp:]
+    size = parts[0].shape[0]
     for s, out in enumerate(outs):
-        pick = pick_ref[s * z.per_grp:(s + 1) * z.per_grp, :]
-        out[...] = dot(pick, features_ref[...]).astype(BF16)
+        at = pl.ds(s * z.per_grp, z.per_grp)
+        rows = sum(
+            dot(pick_ref[at, i * size:(i + 1) * size], part[...]) for i, part in enumerate(parts)
+        )
+        out[...] = rows.astype(BF16)
 
 
 def pack_kernel(z, *refs):
@@ -156,8 +170,6 @@
 
 
 def arrange_kernel(z, place_ref, dense_ref, *outs):
-    turned, plain = outs[:z.zz], outs[z.zz:]
-
     @pl.loop(0, z.dom)
     def _(n):
         at = pl.multiple_of(n * z.rows, z.rows)
@@ -165,28 +177,25 @@
         for k in range(z.zz):
             for p in range(2 * z.grp):
                 first = (k * 2 * z.grp + p) * z.pair
-                to = p * z.per_grp + n * z.pair
+                rows = part[first:first + z.pair, :]
                 if z.pair % 16 == 0:
-                    to = pl.multiple_of(to, z.pair)
-                    turned[k][pl.ds(to, z.pair), :] = part[first:first + z.pair, :]
+                    to = pl.multiple_of(p * z.per_grp + n * z.pair, z.pair)
+                    outs[k][pl.ds(to, z.pair), :] = rows
                 else:
-                    turned[k][p, n] = part[first:first + z.pair, :]
-
-    for out, source in zip(plain, turned):
-        out[...] = source[...].reshape(out.shape[::-1]).T
+                    outs[k][p, n] = rows
 
 
 def turn_kernel(*refs):
     out, height = refs[-1], refs[0].shape[0]
-    for i, ref in enumerate(refs[:-1]):
-        out[:, i * height:(i + 1) * height] = ref[...].T
+    for s, part in enumerate(refs[:-1]):
+        out[:, s * height:(s + 1) * height] = part[...].T
 
 
 def forward_kernel(z, first, last, *refs):
-    plain, refs = refs[:2], refs[2:]
+    turned, refs = refs[:2], refs[2:]
     pieces, refs = refs[:2], refs[2:]
     rows = jnp.concatenate([ref[...] for ref in pieces], axis=0)
-    agg = [dot(ref[...], rows) for ref in plain]
+    agg = [dot_rows(ref[...], rows) for ref in turned]
     if not first:
         agg = [part + ref[...] for part, ref in zip(agg, refs)]
         refs = refs[2:]
@@ -194,12 +203,12 @@
         for ref, part in zip(refs, agg):
             ref[...] = part
         return
-    cots, turned, hiddens, grads, parts = (refs[2 * i:2 * i + 2] for i in range(5))
+    cots, ahead, hiddens, grads, parts = (refs[2 * i:2 * i + 2] for i in range(5))
     for part, cot, hidden, grad in zip(agg, cots, hiddens, grads):
         sig = jax.nn.sigmoid(part)
         hidden[...] = (part * sig).astype(BF16)
         grad[...] = (cot[...].astype(F32) * (sig * (1.0 + part * (1.0 - sig)))).astype(BF16)
-    back_into(parts, turned, grads)
+    back_into(parts, ahead, grads)
 
 
 def back_into(outs, turned, grads):
@@ -218,13 +227,15 @@
     out_ref[...] = (mine_ref[...] + come_ref[...].astype(F32)).astype(BF16)
 
 
-def grad_kernel(z, me_ref, left_a, left_b, mine_a, mine_b, come_a, come_b, *refs):
-    outs, whole = refs[:-1], refs[-1]
-    grads = [
-        (mine[...] + come[...].astype(F32)).astype(BF16)
-        for mine, come in ((mine_a, come_a), (mine_b, come_b))
-    ]
-    whole[...] = (dot(left_a[...], grads[0]) + dot(left_b[...], grads[1])).astype(BF16)
+def grad_kernel(z, me_ref, *refs):
+    own_left, near_left = refs[0:2], refs[2:4]
+    own, mine, come, outs, whole = refs[4:6], refs[6:8], refs[8:10], refs[10:-1], refs[-1]
+    total = 0.0
+    for left, part in zip(own_left, own):
+        total = total + dot(left[...], part[...].astype(BF16))
+    for left, part, moved in zip(near_left, mine, come):
+        total = total + dot(left[...], (part[...] + moved[...].astype(F32)).astype(BF16))
+    whole[...] = total.astype(BF16)
     share = whole.shape[0] // z.grp
     for s in range(z.grp):
         at = pl.multiple_of((me_ref[0] ^ s) * share, share)
@@ -249,11 +260,11 @@
     inner = (wide, z.rows) if z.pair % 16 == 0 else (2 * z.grp, z.dom, z.pair, z.rows)
     got = call(
         lambda *refs: arrange_kernel(z, *refs),
-        [(inner, BF16)] * z.zz + [((z.rows, wide), BF16)] * z.zz,
+        [(inner, BF16)] * z.zz,
         [("v", place), ("v", dense)],
         "arrange", 4,
     )
-    return [part.reshape(wide, z.rows) for part in got[:z.zz]] + list(got[z.zz:])
+    return [part.reshape(wide, z.rows) for part in got]
 
 
 def shards(features, node_order, block_cols, block_count, block_vals, weight, cotangent):
@@ -274,29 +285,50 @@
     def to_zz(x, k):
         return lax.ppermute(x, "zz", [(i, (i + k) % z.zz) for i in range(z.zz)]) if k else x
 
+    first_half = features[:rows // 2]
     (message,) = call(
         lambda *refs: index_kernel(z, *refs),
         [((z.grp * z.dom, 8, 128), I32)],
         [("s", me), ("v", node_order.reshape(1, rows))],
         "index", 1,
     )
+    message, features = lax.optimization_barrier((message, features))
     message = lax.all_to_all(
         message, ("grp", "zz", "core"), split_axis=0, concat_axis=0, tiled=True
     )
     vals_b = to_core(block_vals)
 
-    products = call(
-        lambda *refs: product_kernel(z, *refs),
-        [((rows, half), BF16)] * 2,
-        [("s", me), ("v", features), ("v", weight)],
-        "product", 1.5,
-    )
-    pick, *got = call(
-        lambda *refs: send_kernel(z, *refs),
-        [((rows, rows), BF16)] + [((2, z.per_grp, half), BF16)] * z.grp,
-        [("s", me), ("v", message)] + [("v", part) for part in products],
-        "send", 1.5,
-    )
+    def products_of(parts):
+        return call(
+            lambda *refs: product_kernel(z, *refs),
+            [((rows, half), BF16)] * 2,
+            [("s", me), ("v", weight)] + [("v", part) for part in parts],
+            "product", 1.5,
+        )
+
+    def send_of(line, products):
+        return call(
+            lambda *refs: send_kernel(z, line, *refs),
+            [((rows, rows), BF16)] + [((2, z.per_grp, half), BF16)] * z.grp,
+            [("s", me), ("v", message)] + [("v", part) for part in products],
+            "send", 1.5,
+        )
+
+    def pack(parts):
+        own, other = call(
+            lambda *refs: pack_kernel(z, *refs),
+            [((rows, half), BF16)] * 2,
+            [("v", part) for part in parts],
+            "pack", 0.5,
+        )
+        return [own, to_core(other)]
+
+    near = [to_zz(first_half, 1)]
+    products = products_of([features])
+    products, later = lax.optimization_barrier((products, features[rows // 2:]))
+    near.append(to_zz(later, 1))
+    message, vals_b, near[0] = lax.optimization_barrier((message, vals_b, near[0]))
+    pick, *got = send_of(0, products)
     got, message, cotangent, block_cols = lax.optimization_barrier(
         (got, message, cotangent, block_cols)
     )
@@ -308,12 +340,6 @@
     cot_a = lax.dynamic_slice_in_dim(cotangent, core * half, half, axis=1)
     cot_b = to_core(lax.dynamic_slice_in_dim(cotangent, (1 - core) * half, half, axis=1))
 
-    (place,) = call(
-        lambda *refs: place_kernel(z, *refs),
-        [((z.dom, rows, rows), BF16)],
-        [("s", me), ("v", message)],
-        "place", 1.5,
-    )
     wide = 2 * z.grp * z.per_grp
 
     def arranged(cols, vals):
@@ -324,49 +350,56 @@
             "dense", 2.5,
             (pltpu.VMEM((z.dom * rows + tile, tile), F32),),
         )
-        got = arrange(z, place, dense, wide)
-        return got[:z.zz], got[z.zz:]
-
-    turned_a, plain_a = arranged(cols_a, block_vals)
-    came, plain_a = lax.optimization_barrier((came, plain_a))
-
-    own, other = call(
-        lambda *refs: pack_kernel(z, *refs),
-        [((rows, half), BF16)] * 2,
-        [("v", part) for part in came],
-        "pack", 0.5,
-    )
-    ring = [[own, to_core(other)]]
-    turned_b, plain_b = arranged(cols_b, vals_b)
-    turned, plain = (turned_a, turned_b), (plain_a, plain_b)
-    for k in range(1, z.zz):
-        ring.append([to_zz(part, 1) for part in ring[-1]])
-        if k == 1:
-            ring[1][0], plain_b = lax.optimization_barrier((ring[1][0], plain_b))
-            plain = (plain_a, plain_b)
-        if k == 2:
-            ring[2][0], pick = lax.optimization_barrier((ring[2][0], pick))
-
-    picked = call(
-        lambda *refs: rows_kernel(z, *refs),
-        [((z.per_grp, width_in), BF16)] * z.grp,
-        [("v", pick), ("v", features)],
-        "rows", 1,
-    )
-    held = [to_grp(picked[s], s) for s in range(z.grp)]
-    (held,) = call(
-        turn_kernel, [((width_in, rows), BF16)], [("v", part) for part in held], "turn", 0.5
-    )
-    held_b = to_core(held)
+        return arrange(z, place, dense, wide)
+
+    pick_near, *got = send_of(7, products_of(near))
+    came, got = lax.optimization_barrier((came, got))
+
+    def lefts_of(pick, parts):
+        picked = call(
+            lambda *refs: rows_kernel(z, *refs),
+            [((z.per_grp, width_in), BF16)] * z.grp,
+            [("v", pick)] + [("v", part) for part in parts],
+            "rows", 1,
+        )
+        return [to_grp(picked[s], s) for s in range(z.grp)]
+
+    def turned_of(parts):
+        (left,) = call(
+            turn_kernel, [((width_in, rows), BF16)], [("v", part) for part in parts], "turn", 0.5
+        )
+        return [left, to_core(left)]
+
+    ring = {0: pack(came)}
+    came = [to_grp(got[s], s) for s in range(z.grp)]
+    ring[0][1], pick, message = lax.optimization_barrier((ring[0][1], pick, message))
+    (place,) = call(
+        lambda *refs: place_kernel(z, *refs),
+        [((z.dom, rows, rows), BF16)],
+        [("s", me), ("v", message)],
+        "place", 1.5,
+    )
+    turned = [arranged(cols_a, block_vals)]
+    order = list(range(z.zz - 1, 1, -1))
+    for k in order:
+        ring[k] = [to_zz(part, -1) for part in ring[(k + 1) % z.zz]]
+        if k == order[0]:
+            ring[k][0], vals_b = lax.optimization_barrier((ring[k][0], vals_b))
+            turned.append(arranged(cols_b, vals_b))
+    came, left = lax.optimization_barrier((came, lefts_of(pick, [features])))
+    ring[1] = pack(came)
+    lefts = turned_of(left)
 
     agg = []
-    for k in range(z.zz):
-        ins = [("v", plain[0][k]), ("v", plain[1][k])] + [("v", part) for part in ring[k]]
+    order = [0, 1] + order
+    for k in order:
+        ins = [("v", turned[0][k]), ("v", turned[1][k])] + [("v", part) for part in ring[k]]
         ins += [("v", part) for part in agg]
         outs = [((rows, half), F32)] * 2
-        last = k == z.zz - 1
+        last = k == order[-1]
         if last:
-            ins += [("v", part) for part in (cot_a, cot_b, turned[0][k], turned[1][k])]
+            ahead = (turned[0][z.zz - 1], turned[1][z.zz - 1])
+            ins += [("v", part) for part in (cot_a, cot_b, *ahead)]
             outs = [((rows, half), BF16)] * 4 + [((wide // 2, half), BF16)] * 2
         agg = call(
             lambda *refs, k=k, last=last: forward_kernel(z, k == 0, last, *refs),
@@ -374,27 +407,33 @@
         )
     hidden_a, hidden_b, grad_a, grad_b, *came = agg
 
-    for k in range(z.zz - 2, -1, -1):
-        came = [to_zz(part, -1) for part in came]
-        if k == 1:
-            came[0], hidden_b = lax.optimization_barrier((came[0], hidden_b))
-            come = to_core(hidden_b)
-        if k == 0:
-            came[1], come = lax.optimization_barrier((came[1], come))
-        mine = call(
+    def back(k):
+        return call(
             back_kernel,
             [((wide // 2, half), F32)] * 2,
             [("v", part) for part in (turned[0][k], turned[1][k], grad_a, grad_b)],
             "back", 1,
         )
-        if k:
-            came = [
-                call(
-                    pass_kernel, [((wide // 2, half), BF16)], [("v", part), ("v", moved)],
-                    "pass", 0.5,
-                )[0]
-                for part, moved in zip(mine, came)
-            ]
+
+    for k in range(z.zz - 2, 0, -1):
+        came = [to_zz(part, -1) for part in came]
+        if k == z.zz - 2:
+            came[0], pick_near = lax.optimization_barrier((came[0], pick_near))
+            lefts += turned_of(lefts_of(pick_near, near))
+        mine = back(k)
+        if k == 1:
+            came[1], come = lax.optimization_barrier((came[1], come))
+            break
+        came = [
+            call(
+                pass_kernel, [((wide // 2, half), BF16)], [("v", part), ("v", moved)],
+                "pass", 0.5,
+            )[0]
+            for part, moved in zip(mine, came)
+        ]
+        if k == z.zz - 2:
+            came[1], hidden_b = lax.optimization_barrier((came[1], hidden_b))
+            come = to_core(hidden_b)
     first = core == 0
     hidden = jnp.concatenate(
         [jnp.where(first, hidden_a, come), jnp.where(first, come, hidden_a)], axis=1
@@ -404,7 +443,7 @@
     terms = call(
         lambda *refs: grad_kernel(z, *refs),
         [((share, half), BF16)] * z.grp,
-        [("s", me), ("v", held), ("v", held_b)] + [("v", part) for part in (*mine, *came)],
+        [("s", me)] + [("v", part) for part in (*lefts, *back(0), *mine, *came)],
         "grad", 1.5,
         (pltpu.VMEM((width_in, half), BF16),),
     )

time: 160 us -> 174 us (1.087)
  blocking collectives: 0 us -> 22.2 us
  local copies, waits for them, and re-layouts: 17.6 us -> 10.3 us
  Pallas kernels: 31.6 us -> 35.8 us
  waiting for transfers between devices: 62.4 us -> 59.2 us
  starting transfers between devices: 46 us -> 43.6 us
    all_to_all x0 -> x1, blocking collectives: none -> 22.2 us  [shards(): lax.all_to_all(message, ('grp', 'zz', 'core'), split_axis=0, concat_axis=...]
    ppermute x12 -> x18, waiting for transfers between devices: 12.8 us -> 26.8 us  [to_grp(): lax.ppermute(x, 'grp', [(i, i ^ s) for i in range(z.grp)])]
    ppermute x12 -> x10, waiting for transfers between devices: 35.5 us -> 22.6 us  [to_zz(): lax.ppermute(x, 'zz', [(i, (i + k) % z.zz) for i in range(z.zz)])]
    unnamed x80 -> x28, local copies, waits for them, and re-layouts: 17.5 us -> 7.23 us
    ppermute x12 -> x18, starting transfers between devices: 12.8 us -> 21.1 us  [to_grp(): lax.ppermute(x, 'grp', [(i, i ^ s) for i in range(z.grp)])]
    all_to_all x1 -> x0, starting transfers between devices: 6.96 us -> none  [shards(): lax.all_to_all(message, ('grp', 'zz', 'core'), split_axis=0, concat_axis=...]
    all_to_all x1 -> x0, waiting for transfers between devices: 4.45 us -> none  [shards(): lax.all_to_all(message, ('grp', 'zz', 'core'), split_axis=0, concat_axis=...]
    pallas_call x27 -> x30, Pallas kernels: 31.6 us -> 35.8 us  [call(): pl.pallas_call(body, out_shape=tuple((jax.ShapeDtypeStruct(s, d) for s, d...]
  transfers between devices with their start and end apart: 37 -> 42, of which waited for: 21 -> 17; matrix products, arithmetic and copies ran while one was open for 1% -> 2% of each run, Pallas kernels for 17% -> 15%
where the time goes in v6:
time: 174 us; the launch traced here: 173 us
  waiting for transfers between devices  59.2 us (34%)
  starting transfers between devices  43.6 us (25%)
  Pallas kernels  35.8 us (21%)
  blocking collectives  22.2 us (13%)
  local copies, waits for them, and re-layouts  10.3 us (6%)
    pallas_call x30, Pallas kernels, call(): pl.pallas_call(body, out_shape=tuple((jax.ShapeDtypeStruct(s, d) for s, d...  35.8 us
    ppermute x18, waiting for transfers between devices, to_grp(): lax.ppermute(x, 'grp', [(i, i ^ s) for i in range(z.grp)])  26.8 us
    ppermute x10, waiting for transfers between devices, to_zz(): lax.ppermute(x, 'zz', [(i, (i + k) % z.zz) for i in range(z.zz)])  22.6 us
    all_to_all x1, blocking collectives, shards(): lax.all_to_all(message, ('grp', 'zz', 'core'), split_axis=0, concat_axis=...  22.2 us
    ppermute x18, starting transfers between devices, to_grp(): lax.ppermute(x, 'grp', [(i, i ^ s) for i in range(z.grp)])  21.1 us
    ppermute x10, starting transfers between devices, to_zz(): lax.ppermute(x, 'zz', [(i, (i + k) % z.zz) for i in range(z.zz)])  17.9 us
    ppermute x2, waiting for transfers between devices, shards(): lax.ppermute(mine, 'zz', [(i, i ^ step) for i in range(z.zz)])  9.31 us
    unnamed x28, local copies, waits for them, and re-layouts  7.23 us
  transfers between devices with their start and end apart: 42, of which 17 were waited for; matrix products, arithmetic and copies ran while one was open for 2% of the time, Pallas kernels for 15%

profile of v6, /device:TPU:0, one launch (start us, length us, event | category | flops | bytes accessed | tf_op | source)
XLA Modules:
  0.0 173.2 jit_solution(7937652457886445952)
XLA Ops:
  1.2 1.9 %slice.6 = bf16[256,1024]{1,0:T(8,128)(2,1)} slice(bf16[512,1024]{1,0:T(8,128)(2,1)} %refs_1_.4), slice={[0:256], [0:1024]} | slice | bytes 1048576 | tf_op jit(solution)/shard_map/slice | solution.py:288
  3.0 2.7 %collective-permute-start.1 = (bf16[256,1024]{1,0:T(8,128)(2,1)}, bf16[256,1024]{1,0:T(8,128)(2,1)S(1)}, u32[]{:S(2)}, u32[]{:S(2)}) collective-permute-start(bf16[256,1024]{1,0:T(8,128)(2,1)} %slice.6), channel_id=1, source_target_pairs={{0,2},{2,4},{4,6},{6,0},{1,3},{3,5},{5,7},{7,1},{8,10},{10,12},{12... | collective-permute-start | bytes 1572872 | tf_op jit(solution)/shard_map/ppermute | solution.py:286
  8.8 1.2 copy-done
  10.0 1.2 copy-done.2
  11.2 1.3 product.2
  12.5 1.6 collective-permute-start.5
  14.1 22.2 %all_to_all.5.refs_1_ = s32[32,8,128]{2,1,0:T(8,128)S(1)} all-to-all(s32[32,8,128]{2,1,0:T(8,128)S(1)} %index.1), channel_id=1, replica_groups=mesh['grp'=4,'zz'=4,'core'=2] {'grp','zz','core'}, dimensions={0} | all-to-all | bytes 262144 | tf_op jit(solution)/shard_map/all_to_all | solution.py:296
  36.3 1.2 send.2
  39.4 2.4 %collective-permute-start.4 = (bf16[2,128,256]{2,1,0:T(8,128)(2,1)S(1)}, bf16[2,128,256]{2,1,0:T(8,128)(2,1)S(1)}, u32[]{:S(2)}, u32[]{:S(2)}) collective-permute-start(bf16[2,128,256]{2,1,0:T(8,128)(2,1)S(1)} %get-tuple-element.114), channel_id=1, source_target_pairs={{0,24},{8,16},{16,8},{24,0},{1,25},{9,17},{17,9},{25,1},{2,26},{10... | collective-permute-start | bytes 393224 | tf_op jit(solution)/shard_map/ppermute | solution.py:283
  41.8 1.3 product.3
  43.1 1.9 %send.3 = (bf16[512,512]{1,0:T(8,128)(2,1)S(1)}, bf16[2,128,256]{2,1,0:T(8,128)(2,1)S(1)}, bf16[2,128,256]{2,1,0:T(8,128)(2,1)}, bf16[2,128,256]{2,1,0:T(8,128)(2,1)}, bf16[2,128,256]{2,1,0:T(8,128)(2,1)S(1)}) custom-call(s32[3]{0:T(128)S(1)} %pad_add_fusion.refs_0_, s32[32,8,128]{2,1,0:T(8,128)S(1)} %all_to_all.5.refs_1_, ...), custom_call_target="tpu_custom_call" | custom-call | flops 375000000 | tf_op jit(solution)/shard_map/send/pallas_call | solution.py:39
  47.4 1.4 collective-permute-start.12
  49.7 1.3 collective-permute-start.8
  52.7 1.3 collective-permute-start.15
  55.0 1.3 collective-permute-start.17
  58.1 1.2 collective-permute-start.14
  59.3 1.6 copy-done.4
  60.9 2.4 %dense.2.refs_1_ = bf16[4096,512]{1,0:T(8,128)(2,1)S(1)} custom-call(s32[4,16]{1,0:T(4,128)S(1)} %fusion.cols_ref, bf16[4,16,128,128]{3,2,1,0:T(8,128)(2,1)S(1)} %copy-done.4), custom_call_target="tpu_custom_call" | custom-call | flops 625000000 | tf_op jit(solution)/shard_map/dense/pallas_call | solution.py:39
  63.4 6.7 %collective-permute-done.14.refs_3_ = bf16[2,128,256]{2,1,0:T(8,128)(2,1)S(1)} collective-permute-done((bf16[2,128,256]{2,1,0:T(8,128)(2,1)}, bf16[2,128,256]{2,1,0:T(8,128)(2,1)S(1)}, u32[]{:S(2)}, u32[]{:S(2)}) %collective-permute-start.14) | collective-permute-done | bytes 131104 | tf_op jit(solution)/shard_map/ppermute | solution.py:283
  72.0 3.4 %dense.3.refs_1_ = bf16[4096,512]{1,0:T(8,128)(2,1)S(1)} custom-call(s32[4,16]{1,0:T(4,128)S(1)} %collective-permute-done.7.cols_ref, bf16[4,16,128,128]{3,2,1,0:T(8,128)(2,1)} %collective-permute-done.vals_ref), custom_call_target="tpu_custom_call" | custom-call | flops 625000000 | tf_op jit(solution)/shard_map/dense/pallas_call | solution.py:39
  75.5 1.4 collective-permute-start.11
  76.9 1.4 place.1.refs_0_
  78.3 3.5 %arrange.3 = (bf16[1024,512]{1,0:T(8,128)(2,1)S(1)}, bf16[1024,512]{1,0:T(8,128)(2,1)S(1)}, bf16[1024,512]{1,0:T(8,128)(2,1)S(1)}, bf16[1024,512]{1,0:T(8,128)(2,1)S(1)}) custom-call(bf16[8,512,512]{2,1,0:T(8,128)(2,1)S(1)} %place.1.refs_0_, bf16[4096,512]{1,0:T(8,128)(2,1)S(1)} %dense.3.refs_1_), custom_call_target="tpu_custom_call" | custom-call | flops 1000000000 | tf_op jit(solution)/shard_map/arrange/pallas_call | solution.py:39
  81.8 3.5 %arrange.2 = (bf16[1024,512]{1,0:T(8,128)(2,1)S(1)}, bf16[1024,512]{1,0:T(8,128)(2,1)S(1)}, bf16[1024,512]{1,0:T(8,128)(2,1)S(1)}, bf16[1024,512]{1,0:T(8,128)(2,1)S(1)}) custom-call(bf16[8,512,512]{2,1,0:T(8,128)(2,1)S(1)} %place.1.refs_0_, bf16[4096,512]{1,0:T(8,128)(2,1)S(1)} %dense.2.refs_1_), custom_call_target="tpu_custom_call" | custom-call | flops 1000000000 | tf_op jit(solution)/shard_map/arrange/pallas_call | solution.py:39
  85.3 1.8 %forward.4 = (f32[512,256]{1,0:T(8,128)S(1)}, f32[512,256]{1,0:T(8,128)S(1)}) custom-call(bf16[1024,512]{1,0:T(8,128)(2,1)S(1)} %get-tuple-element.158.refs_0_.turned_a, bf16[1024,512]{1,0:T(8,128)(2,1)S(1)} %get-tuple-element.159.refs_1_.turned_b, bf16[512,256]{1,0:T(8,128)(2,1)} %get-tuple-element.133.refs_2_, bf16[512,256]{1,0:T(8,128)(2,1)} %collective-permute-done.6.refs_3_), custom_call_target="tpu_custom_call" | custom-call | flops 250000000 | tf_op jit(solution)/shard_map/forward/pallas_call | solution.py:39
  88.7 1.6 forward.7
  90.3 2.0 %collective-permute-start.24 = (bf16[512,256]{1,0:T(8,128)(2,1)S(1)}, bf16[512,256]{1,0:T(8,128)(2,1)S(1)}, u32[]{:S(2)}, u32[]{:S(2)}) collective-permute-start(bf16[512,256]{1,0:T(8,128)(2,1)S(1)} %get-tuple-element.180), channel_id=1, source_target_pairs={{0,6},{2,0},{4,2},{6,4},{1,7},{3,1},{5,3},{7,5},{8,14},{10,8},{12,... | collective-permute-start | bytes 786440 | tf_op jit(solution)/shard_map/ppermute | solution.py:286
  92.2 6.7 %collective-permute-done.24.come_ref = bf16[512,256]{1,0:T(8,128)(2,1)S(1)} collective-permute-done((bf16[512,256]{1,0:T(8,128)(2,1)S(1)}, bf16[512,256]{1,0:T(8,128)(2,1)S(1)}, u32[]{:S(2)}, u32[]{:S(2)}) %collective-permute-start.24) | collective-permute-done | bytes 262176 | tf_op jit(solution)/shard_map/ppermute | solution.py:286
  101.5 1.7 collective-permute-start.27
  103.6 5.4 %collective-permute-done.25.refs_1_ = bf16[128,1024]{1,0:T(8,128)(2,1)S(1)} collective-permute-done((bf16[128,1024]{1,0:T(8,128)(2,1)S(1)}, bf16[128,1024]{1,0:T(8,128)(2,1)S(1)}, u32[]{:S(2)}, u32[]{:S(2)}) %collective-permute-start.25) | collective-permute-done | bytes 262176 | tf_op jit(solution)/shard_map/ppermute | solution.py:283
  108.9 4.5 %collective-permute-done.26.refs_2_ = bf16[128,1024]{1,0:T(8,128)(2,1)S(1)} collective-permute-done((bf16[128,1024]{1,0:T(8,128)(2,1)S(1)}, bf16[128,1024]{1,0:T(8,128)(2,1)S(1)}, u32[]{:S(2)}, u32[]{:S(2)}) %collective-permute-start.26) | collective-permute-done | bytes 262176 | tf_op jit(solution)/shard_map/ppermute | solution.py:283
  113.9 3.5 %collective-permute-start.20 = (bf16[512,256]{1,0:T(8,128)(2,1)S(1)}, bf16[512,256]{1,0:T(8,128)(2,1)S(1)}, u32[]{:S(2)}, u32[]{:S(2)}) collective-permute-start(bf16[512,256]{1,0:T(8,128)(2,1)S(1)} %get-tuple-element.171), channel_id=1, source_target_pairs={{0,6},{2,0},{4,2},{6,4},{1,7},{3,1},{5,3},{7,5},{8,14},{10,8},{12,... | collective-permute-start | bytes 786440 | tf_op jit(solution)/shard_map/ppermute | solution.py:286
  118.0 5.5 %collective-permute-done.20.come_ref = bf16[512,256]{1,0:T(8,128)(2,1)S(1)} collective-permute-done((bf16[512,256]{1,0:T(8,128)(2,1)S(1)}, bf16[512,256]{1,0:T(8,128)(2,1)S(1)}, u32[]{:S(2)}, u32[]{:S(2)}) %collective-permute-start.20) | collective-permute-done | bytes 262176 | tf_op jit(solution)/shard_map/ppermute | solution.py:286
  123.5 4.3 %collective-permute-start.21 = (bf16[512,256]{1,0:T(8,128)(2,1)S(1)}, bf16[512,256]{1,0:T(8,128)(2,1)S(1)}, u32[]{:S(2)}, u32[]{:S(2)}) collective-permute-start(bf16[512,256]{1,0:T(8,128)(2,1)S(1)} %pass.2), channel_id=1, source_target_pairs={{0,6},{2,0},{4,2},{6,4},{1,7},{3,1},{5,3},{7,5},{8,14},{10,8},{12,... | collective-permute-start | bytes 786440 | tf_op jit(solution)/shard_map/ppermute | solution.py:286
  129.5 5.1 %collective-permute-done.21.refs_10_ = bf16[512,256]{1,0:T(8,128)(2,1)S(1)} collective-permute-done((bf16[512,256]{1,0:T(8,128)(2,1)S(1)}, bf16[512,256]{1,0:T(8,128)(2,1)S(1)}, u32[]{:S(2)}, u32[]{:S(2)}) %collective-permute-start.21) | collective-permute-done | bytes 262176 | tf_op jit(solution)/shard_map/ppermute | solution.py:286
  134.6 4.3 %collective-permute-done.29.refs_9_ = bf16[512,256]{1,0:T(8,128)(2,1)S(1)} collective-permute-done((bf16[512,256]{1,0:T(8,128)(2,1)S(1)}, bf16[512,256]{1,0:T(8,128)(2,1)S(1)}, u32[]{:S(2)}, u32[]{:S(2)}) %collective-permute-start.29) | collective-permute-done | bytes 262176 | tf_op jit(solution)/shard_map/ppermute | solution.py:286
  138.9 1.8 %grad.1 = (bf16[256,256]{1,0:T(8,128)(2,1)S(1)}, bf16[256,256]{1,0:T(8,128)(2,1)S(1)}, bf16[256,256]{1,0:T(8,128)(2,1)S(1)}, bf16[256,256]{1,0:T(8,128)(2,1)S(1)}) custom-call(s32[3]{0:T(128)S(1)} %pad_add_fusion.refs_0_, bf16[1024,512]{1,0:T(8,128)(2,1)S(1)} %turn.2.refs_1_, bf16[1024,512]{1,0:T(8,128)(2,1)S(1)} %collective-permute-done.23.refs_2_, ...), custom_call_target="tpu_custom_call" | custom-call | flops 375000000 | tf_op jit(solution)/shard_map/grad/pallas_call | solution.py:39
  140.7 1.4 collective-permute-start.30
  143.0 1.3 collective-permute-start.32
  144.3 2.8 %collective-permute-done.30.refs_1_ = bf16[256,256]{1,0:T(8,128)(2,1)S(1)} collective-permute-done((bf16[256,256]{1,0:T(8,128)(2,1)S(1)}, bf16[256,256]{1,0:T(8,128)(2,1)S(1)}, u32[]{:S(2)}, u32[]{:S(2)}) %collective-permute-start.30) | collective-permute-done | bytes 131104 | tf_op jit(solution)/shard_map/ppermute | solution.py:283
  147.1 2.2 %collective-permute-done.31.refs_2_ = bf16[256,256]{1,0:T(8,128)(2,1)S(1)} collective-permute-done((bf16[256,256]{1,0:T(8,128)(2,1)S(1)}, bf16[256,256]{1,0:T(8,128)(2,1)S(1)}, u32[]{:S(2)}, u32[]{:S(2)}) %collective-permute-start.31) | collective-permute-done | bytes 131104 | tf_op jit(solution)/shard_map/ppermute | solution.py:283
  149.5 5.0 %collective-permute-done.33.refs_1_ = bf16[256,256]{1,0:T(8,128)(2,1)S(1)} collective-permute-done((bf16[256,256]{1,0:T(8,128)(2,1)S(1)}, bf16[256,256]{1,0:T(8,128)(2,1)S(1)}, u32[]{:S(2)}, u32[]{:S(2)}) %collective-permute-start.33) | collective-permute-done | bytes 131104 | tf_op jit(solution)/shard_map/ppermute | solution.py:460
  154.5 3.2 %collective-permute-start.34 = (bf16[256,256]{1,0:T(8,128)(2,1)S(1)}, bf16[256,256]{1,0:T(8,128)(2,1)S(1)}, u32[]{:S(2)}, u32[]{:S(2)}) collective-permute-start(bf16[256,256]{1,0:T(8,128)(2,1)S(1)} %sum.4.refs_0_), channel_id=1, source_target_pairs={{0,4},{2,6},{4,0},{6,2},{1,5},{3,7},{5,1},{7,3},{8,12},{10,14},{12... | collective-permute-start | bytes 393224 | tf_op jit(solution)/shard_map/ppermute | solution.py:460
  157.7 4.4 %collective-permute-done.34.refs_1_ = bf16[256,256]{1,0:T(8,128)(2,1)S(1)} collective-permute-done((bf16[256,256]{1,0:T(8,128)(2,1)S(1)}, bf16[256,256]{1,0:T(8,128)(2,1)S(1)}, u32[]{:S(2)}, u32[]{:S(2)}) %collective-permute-start.34) | collective-permute-done | bytes 131104 | tf_op jit(solution)/shard_map/ppermute | solution.py:460
  164.0 1.7 collective-permute-start.37
  165.6 1.5 collective-permute-done.35.refs_2_
  167.8 2.0 %collective-permute-done.37.refs_4_ = bf16[256,256]{1,0:T(8,128)(2,1)S(1)} collective-permute-done((bf16[256,256]{1,0:T(8,128)(2,1)S(1)}, bf16[256,256]{1,0:T(8,128)(2,1)S(1)}, u32[]{:S(2)}, u32[]{:S(2)}) %collective-permute-start.37) | collective-permute-done | bytes 131104 | tf_op jit(solution)/shard_map/ppermute | solution.py:283
  171.2 2.0 %last.1 = f32[1024,512]{1,0:T(8,128)} custom-call(s32[3]{0:T(128)S(1)} %pad_add_fusion.refs_0_, bf16[256,256]{1,0:T(8,128)(2,1)S(1)} %sum.5.refs_1_, bf16[256,256]{1,0:T(8,128)(2,1)S(1)} %collective-permute-done.35.refs_2_, bf16[256,256]{1,0:T(8,128)(2,1)S(1)} %collective-permute-done.36.refs_3_, bf16[256,256]{1,0:T(8,128)(2,1)S(1)} %collective-permute-done.37.refs_4_, ...), custom_call_target="tpu_custom_call" | custom-call | flops 500000000 | tf_op jit(solution)/shard_map/last/pallas_call | solution.py:39
  (102 shorter events, 27.5 us)
Async XLA Ops:
  0.6 41.2 %copy-start.3 = (bf16[1024,512]{1,0:T(8,128)(2,1)S(1)}, bf16[1024,512]{1,0:T(8,128)(2,1)}, u32[]{:S(2)}) copy-start(bf16[1024,512]{1,0:T(8,128)(2,1)} %refs_1_.3) | copy-start | bytes 3145732
  0.6 35.7 %collective-permute-start = (bf16[4,16,128,128]{3,2,1,0:T(8,128)(2,1)}, bf16[4,16,128,128]{3,2,1,0:T(8,128)(2,1)}, u32[]{:S(2)}, u32[]{:S(2)}) collective-permute-start(bf16[4,16,128,128]{3,2,1,0:T(8,128)(2,1)} %vals_ref.1), channel_id=1, source_target_pairs={{0,1},{1,0},{2,3},{3,2},{4,5},{5,4},{6,7},{7,6},{8,9},{9,8},{10,11... | collective-permute-start | bytes 6291464 | tf_op jit(solution)/shard_map/ppermute | solution.py:280
  3.0 33.3 %collective-permute-start.1 = (bf16[256,1024]{1,0:T(8,128)(2,1)}, bf16[256,1024]{1,0:T(8,128)(2,1)S(1)}, u32[]{:S(2)}, u32[]{:S(2)}) collective-permute-start(bf16[256,1024]{1,0:T(8,128)(2,1)} %slice.6), channel_id=1, source_target_pairs={{0,2},{2,4},{4,6},{6,0},{1,3},{3,5},{5,7},{7,1},{8,10},{10,12},{12... | collective-permute-start | bytes 1572872 | tf_op jit(solution)/shard_map/ppermute | solution.py:286
  7.6 43.4 %copy-start.1 = (bf16[512,1024]{1,0:T(8,128)(2,1)S(1)}, bf16[512,1024]{1,0:T(8,128)(2,1)}, u32[]{:S(2)}) copy-start(bf16[512,1024]{1,0:T(8,128)(2,1)} %refs_1_.4) | copy-start | bytes 3145732
  11.2 45.8 %copy-start.12 = (s32[4,16]{1,0:T(4,128)S(1)}, s32[4,16]{1,0:T(4,128)}, u32[]{:S(2)}) copy-start(s32[4,16]{1,0:T(4,128)} %param.9) | copy-start | bytes 772
  11.2 45.8 %copy-start.13 = (s32[4]{0:T(128)S(1)}, s32[4]{0:T(128)}, u32[]{:S(2)}) copy-start(s32[4]{0:T(128)} %param.10) | copy-start | bytes 52
  12.5 29.4 %collective-permute-start.5 = (bf16[256,1024]{1,0:T(8,128)(2,1)S(1)}, bf16[256,1024]{1,0:T(8,128)(2,1)S(1)}, u32[]{:S(2)}, u32[]{:S(2)}) collective-permute-start(bf16[256,1024]{1,0:T(8,128)(2,1)S(1)} %slice.7), channel_id=1, source_target_pairs={{0,2},{2,4},{4,6},{6,0},{1,3},{3,5},{5,7},{7,1},{8,10},{10,12},{12... | collective-permute-start | bytes 1572872 | tf_op jit(solution)/shard_map/ppermute | solution.py:286
  38.3 7.3 %collective-permute-start.2 = (bf16[2,128,256]{2,1,0:T(8,128)(2,1)S(1)}, bf16[2,128,256]{2,1,0:T(8,128)(2,1)S(1)}, u32[]{:S(2)}, u32[]{:S(2)}) collective-permute-start(bf16[2,128,256]{2,1,0:T(8,128)(2,1)S(1)} %get-tuple-element.112), channel_id=1, source_target_pairs={{0,8},{8,0},{16,24},{24,16},{1,9},{9,1},{17,25},{25,17},{2,10},{10... | collective-permute-start | bytes 393224 | tf_op jit(solution)/shard_map/ppermute | solution.py:283
  38.3 7.3 %collective-permute-start.3 = (bf16[2,128,256]{2,1,0:T(8,128)(2,1)S(1)}, bf16[2,128,256]{2,1,0:T(8,128)(2,1)S(1)}, u32[]{:S(2)}, u32[]{:S(2)}) collective-permute-start(bf16[2,128,256]{2,1,0:T(8,128)(2,1)S(1)} %get-tuple-element.113), channel_id=1, source_target_pairs={{0,16},{8,24},{16,0},{24,8},{1,17},{9,25},{17,1},{25,9},{2,18},{10... | collective-permute-start | bytes 393224 | tf_op jit(solution)/shard_map/ppermute | solution.py:283
  39.4 7.3 %collective-permute-start.4 = (bf16[2,128,256]{2,1,0:T(8,128)(2,1)S(1)}, bf16[2,128,256]{2,1,0:T(8,128)(2,1)S(1)}, u32[]{:S(2)}, u32[]{:S(2)}) collective-permute-start(bf16[2,128,256]{2,1,0:T(8,128)(2,1)S(1)} %get-tuple-element.114), channel_id=1, source_target_pairs={{0,24},{8,16},{16,8},{24,0},{1,25},{9,17},{17,9},{25,1},{2,26},{10... | collective-permute-start | bytes 393224 | tf_op jit(solution)/shard_map/ppermute | solution.py:283
  47.4 3.5 %collective-permute-start.6 = (bf16[512,256]{1,0:T(8,128)(2,1)S(1)}, bf16[512,256]{1,0:T(8,128)(2,1)}, u32[]{:S(2)}, u32[]{:S(2)}) collective-permute-start(bf16[512,256]{1,0:T(8,128)(2,1)S(1)} %get-tuple-element.128), channel_id=1, source_target_pairs={{0,1},{1,0},{2,3},{3,2},{4,5},{5,4},{6,7},{7,6},{8,9},{9,8},{10,11... | collective-permute-start | bytes 786440 | tf_op jit(solution)/shard_map/ppermute | solution.py:280
  47.4 7.5 %collective-permute-start.12 = (bf16[2,128,256]{2,1,0:T(8,128)(2,1)}, bf16[2,128,256]{2,1,0:T(8,128)(2,1)}, u32[]{:S(2)}, u32[]{:S(2)}) collective-permute-start(bf16[2,128,256]{2,1,0:T(8,128)(2,1)} %get-tuple-element.144), channel_id=1, source_target_pairs={{0,8},{8,0},{16,24},{24,16},{1,9},{9,1},{17,25},{25,17},{2,10},{10... | collective-permute-start | bytes 393224 | tf_op jit(solution)/shard_map/ppermute | solution.py:283
  48.9 7.4 %collective-permute-start.13 = (bf16[2,128,256]{2,1,0:T(8,128)(2,1)}, bf16[2,128,256]{2,1,0:T(8,128)(2,1)}, u32[]{:S(2)}, u32[]{:S(2)}) collective-permute-start(bf16[2,128,256]{2,1,0:T(8,128)(2,1)} %get-tuple-element.145), channel_id=1, source_target_pairs={{0,16},{8,24},{16,0},{24,8},{1,17},{9,25},{17,1},{25,9},{2,18},{10... | collective-permute-start | bytes 393224 | tf_op jit(solution)/shard_map/ppermute | solution.py:283
  49.7 8.4 %collective-permute-start.8 = (bf16[512,256]{1,0:T(8,128)(2,1)}, bf16[512,256]{1,0:T(8,128)(2,1)S(1)}, u32[]{:S(2)}, u32[]{:S(2)}) collective-permute-start(bf16[512,256]{1,0:T(8,128)(2,1)} %get-tuple-element.133.refs_2_), channel_id=1, source_target_pairs={{0,6},{2,0},{4,2},{6,4},{1,7},{3,1},{5,3},{7,5},{8,14},{10,8},{12,... | collective-permute-start | bytes 786440 | tf_op jit(solution)/shard_map/ppermute | solution.py:286
  52.0 11.3 %copy-start.11 = (bf16[512,512]{1,0:T(8,128)(2,1)S(1)}, bf16[512,512]{1,0:T(8,128)(2,1)}, u32[]{:S(2)}) copy-start(bf16[512,512]{1,0:T(8,128)(2,1)} %param.13) | copy-start | bytes 1572868
  52.0 18.9 %copy-start.8 = (bf16[2,128,256]{2,1,0:T(8,128)(2,1)S(1)}, bf16[2,128,256]{2,1,0:T(8,128)(2,1)}, u32[]{:S(2)}) copy-start(bf16[2,128,256]{2,1,0:T(8,128)(2,1)} %copy-done.7) | copy-start | bytes 393220
  52.7 17.3 %collective-permute-start.15 = (bf16[128,1024]{1,0:T(8,128)(2,1)S(1)}, bf16[128,1024]{1,0:T(8,128)(2,1)S(1)}, u32[]{:S(2)}, u32[]{:S(2)}) collective-permute-start(bf16[128,1024]{1,0:T(8,128)(2,1)S(1)} %get-tuple-element.149), channel_id=1, source_target_pairs={{0,8},{8,0},{16,24},{24,16},{1,9},{9,1},{17,25},{25,17},{2,10},{10... | collective-permute-start | bytes 786440 | tf_op jit(solution)/shard_map/ppermute | solution.py:283
  54.0 16.5 %collective-permute-start.16 = (bf16[128,1024]{1,0:T(8,128)(2,1)S(1)}, bf16[128,1024]{1,0:T(8,128)(2,1)S(1)}, u32[]{:S(2)}, u32[]{:S(2)}) collective-permute-start(bf16[128,1024]{1,0:T(8,128)(2,1)S(1)} %get-tuple-element.150), channel_id=1, source_target_pairs={{0,16},{8,24},{16,0},{24,8},{1,17},{9,25},{17,1},{25,9},{2,18},{10... | collective-permute-start | bytes 786440 | tf_op jit(solution)/shard_map/ppermute | solution.py:283
  55.0 16.0 %collective-permute-start.17 = (bf16[128,1024]{1,0:T(8,128)(2,1)S(1)}, bf16[128,1024]{1,0:T(8,128)(2,1)S(1)}, u32[]{:S(2)}, u32[]{:S(2)}) collective-permute-start(bf16[128,1024]{1,0:T(8,128)(2,1)S(1)} %get-tuple-element.151), channel_id=1, source_target_pairs={{0,24},{8,16},{16,8},{24,0},{1,25},{9,17},{17,9},{25,1},{2,26},{10... | collective-permute-start | bytes 786440 | tf_op jit(solution)/shard_map/ppermute | solution.py:283
  56.3 19.2 %collective-permute-start.10 = (bf16[512,256]{1,0:T(8,128)(2,1)}, bf16[512,256]{1,0:T(8,128)(2,1)S(1)}, u32[]{:S(2)}, u32[]{:S(2)}) collective-permute-start(bf16[512,256]{1,0:T(8,128)(2,1)} %collective-permute-done.6.refs_3_), channel_id=1, source_target_pairs={{0,6},{2,0},{4,2},{6,4},{1,7},{3,1},{5,3},{7,5},{8,14},{10,8},{12,... | collective-permute-start | bytes 786440 | tf_op jit(solution)/shard_map/ppermute | solution.py:286
  58.1 11.9 %collective-permute-start.14 = (bf16[2,128,256]{2,1,0:T(8,128)(2,1)}, bf16[2,128,256]{2,1,0:T(8,128)(2,1)S(1)}, u32[]{:S(2)}, u32[]{:S(2)}) collective-permute-start(bf16[2,128,256]{2,1,0:T(8,128)(2,1)} %copy-done.9), channel_id=1, source_target_pairs={{0,24},{8,16},{16,8},{24,0},{1,25},{9,17},{17,9},{25,1},{2,26},{10... | collective-permute-start | bytes 393224 | tf_op jit(solution)/shard_map/ppermute | solution.py:283
  70.0 2.0 %collective-permute-start.7 = (s32[4,16]{1,0:T(4,128)S(1)}, s32[4,16]{1,0:T(4,128)S(1)}, u32[]{:S(2)}, u32[]{:S(2)}) collective-permute-start(s32[4,16]{1,0:T(4,128)S(1)} %fusion.cols_ref), channel_id=1, source_target_pairs={{0,1},{1,0},{2,3},{3,2},{4,5},{5,4},{6,7},{7,6},{8,9},{9,8},{10,11... | collective-permute-start | bytes 776 | tf_op jit(solution)/shard_map/ppermute | solution.py:280
  70.0 18.6 %collective-permute-start.19 = (bf16[512,256]{1,0:T(8,128)(2,1)S(1)}, bf16[512,256]{1,0:T(8,128)(2,1)S(1)}, u32[]{:S(2)}, u32[]{:S(2)}) collective-permute-start(bf16[512,256]{1,0:T(8,128)(2,1)S(1)} %get-tuple-element.200), channel_id=1, source_target_pairs={{0,1},{1,0},{2,3},{3,2},{4,5},{5,4},{6,7},{7,6},{8,9},{9,8},{10,11... | collective-permute-start | bytes 786440 | tf_op jit(solution)/shard_map/ppermute | solution.py:280
  70.5 18.1 %collective-permute-start.9 = (bf16[512,256]{1,0:T(8,128)(2,1)S(1)}, bf16[512,256]{1,0:T(8,128)(2,1)S(1)}, u32[]{:S(2)}, u32[]{:S(2)}) collective-permute-start(bf16[512,256]{1,0:T(8,128)(2,1)S(1)} %collective-permute-done.8.refs_2_), channel_id=1, source_target_pairs={{0,6},{2,0},{4,2},{6,4},{1,7},{3,1},{5,3},{7,5},{8,14},{10,8},{12,... | collective-permute-start | bytes 786440 | tf_op jit(solution)/shard_map/ppermute | solution.py:286
  71.9 15.2 %collective-permute-start.18 = (bf16[512,256]{1,0:T(8,128)(2,1)S(1)}, bf16[512,256]{1,0:T(8,128)(2,1)S(1)}, u32[]{:S(2)}, u32[]{:S(2)}) collective-permute-start(bf16[512,256]{1,0:T(8,128)(2,1)S(1)} %get-tuple-element.157), channel_id=1, source_target_pairs={{0,1},{1,0},{2,3},{3,2},{4,5},{5,4},{6,7},{7,6},{8,9},{9,8},{10,11... | collective-permute-start | bytes 786440 | tf_op jit(solution)/shard_map/ppermute | solution.py:280
  75.5 13.2 %collective-permute-start.11 = (bf16[512,256]{1,0:T(8,128)(2,1)S(1)}, bf16[512,256]{1,0:T(8,128)(2,1)S(1)}, u32[]{:S(2)}, u32[]{:S(2)}) collective-permute-start(bf16[512,256]{1,0:T(8,128)(2,1)S(1)} %collective-permute-done.10.refs_3_), channel_id=1, source_target_pairs={{0,6},{2,0},{4,2},{6,4},{1,7},{3,1},{5,3},{7,5},{8,14},{10,8},{12,... | collective-permute-start | bytes 786440 | tf_op jit(solution)/shard_map/ppermute | solution.py:286
  90.3 8.7 %collective-permute-start.24 = (bf16[512,256]{1,0:T(8,128)(2,1)S(1)}, bf16[512,256]{1,0:T(8,128)(2,1)S(1)}, u32[]{:S(2)}, u32[]{:S(2)}) collective-permute-start(bf16[512,256]{1,0:T(8,128)(2,1)S(1)} %get-tuple-element.180), channel_id=1, source_target_pairs={{0,6},{2,0},{4,2},{6,4},{1,7},{3,1},{5,3},{7,5},{8,14},{10,8},{12,... | collective-permute-start | bytes 786440 | tf_op jit(solution)/shard_map/ppermute | solution.py:286
  99.6 9.3 %collective-permute-start.25 = (bf16[128,1024]{1,0:T(8,128)(2,1)S(1)}, bf16[128,1024]{1,0:T(8,128)(2,1)S(1)}, u32[]{:S(2)}, u32[]{:S(2)}) collective-permute-start(bf16[128,1024]{1,0:T(8,128)(2,1)S(1)} %get-tuple-element.184), channel_id=1, source_target_pairs={{0,8},{8,0},{16,24},{24,16},{1,9},{9,1},{17,25},{25,17},{2,10},{10... | collective-permute-start | bytes 786440 | tf_op jit(solution)/shard_map/ppermute | solution.py:283
  100.5 12.9 %collective-permute-start.26 = (bf16[128,1024]{1,0:T(8,128)(2,1)S(1)}, bf16[128,1024]{1,0:T(8,128)(2,1)S(1)}, u32[]{:S(2)}, u32[]{:S(2)}) collective-permute-start(bf16[128,1024]{1,0:T(8,128)(2,1)S(1)} %get-tuple-element.185), channel_id=1, source_target_pairs={{0,16},{8,24},{16,0},{24,8},{1,17},{9,25},{17,1},{25,9},{2,18},{10... | collective-permute-start | bytes 786440 | tf_op jit(solution)/shard_map/ppermute | solution.py:283
  101.5 11.9 %collective-permute-start.27 = (bf16[128,1024]{1,0:T(8,128)(2,1)S(1)}, bf16[128,1024]{1,0:T(8,128)(2,1)S(1)}, u32[]{:S(2)}, u32[]{:S(2)}) collective-permute-start(bf16[128,1024]{1,0:T(8,128)(2,1)S(1)} %get-tuple-element.186), channel_id=1, source_target_pairs={{0,24},{8,16},{16,8},{24,0},{1,25},{9,17},{17,9},{25,1},{2,26},{10... | collective-permute-start | bytes 786440 | tf_op jit(solution)/shard_map/ppermute | solution.py:283
  103.5 35.4 %collective-permute-start.23 = (bf16[1024,512]{1,0:T(8,128)(2,1)S(1)}, bf16[1024,512]{1,0:T(8,128)(2,1)S(1)}, u32[]{:S(2)}, u32[]{:S(2)}) collective-permute-start(bf16[1024,512]{1,0:T(8,128)(2,1)S(1)} %turn.2.refs_1_), channel_id=1, source_target_pairs={{0,1},{1,0},{2,3},{3,2},{4,5},{5,4},{6,7},{7,6},{8,9},{9,8},{10,11... | collective-permute-start | bytes 3145736 | tf_op jit(solution)/shard_map/ppermute | solution.py:280
  113.8 25.1 %collective-permute-start.28 = (bf16[1024,512]{1,0:T(8,128)(2,1)S(1)}, bf16[1024,512]{1,0:T(8,128)(2,1)S(1)}, u32[]{:S(2)}, u32[]{:S(2)}) collective-permute-start(bf16[1024,512]{1,0:T(8,128)(2,1)S(1)} %turn.3.refs_3_), channel_id=1, source_target_pairs={{0,1},{1,0},{2,3},{3,2},{4,5},{5,4},{6,7},{7,6},{8,9},{9,8},{10,11... | collective-permute-start | bytes 3145736 | tf_op jit(solution)/shard_map/ppermute | solution.py:280
  113.9 9.6 %collective-permute-start.20 = (bf16[512,256]{1,0:T(8,128)(2,1)S(1)}, bf16[512,256]{1,0:T(8,128)(2,1)S(1)}, u32[]{:S(2)}, u32[]{:S(2)}) collective-permute-start(bf16[512,256]{1,0:T(8,128)(2,1)S(1)} %get-tuple-element.171), channel_id=1, source_target_pairs={{0,6},{2,0},{4,2},{6,4},{1,7},{3,1},{5,3},{7,5},{8,14},{10,8},{12,... | collective-permute-start | bytes 786440 | tf_op jit(solution)/shard_map/ppermute | solution.py:286
  123.5 11.1 %collective-permute-start.21 = (bf16[512,256]{1,0:T(8,128)(2,1)S(1)}, bf16[512,256]{1,0:T(8,128)(2,1)S(1)}, u32[]{:S(2)}, u32[]{:S(2)}) collective-permute-start(bf16[512,256]{1,0:T(8,128)(2,1)S(1)} %pass.2), channel_id=1, source_target_pairs={{0,6},{2,0},{4,2},{6,4},{1,7},{3,1},{5,3},{7,5},{8,14},{10,8},{12,... | collective-permute-start | bytes 786440 | tf_op jit(solution)/shard_map/ppermute | solution.py:286
  127.9 6.7 %collective-permute-start.22 = (bf16[512,256]{1,0:T(8,128)(2,1)S(1)}, bf16[512,256]{1,0:T(8,128)(2,1)S(1)}, u32[]{:S(2)}, u32[]{:S(2)}) collective-permute-start(bf16[512,256]{1,0:T(8,128)(2,1)S(1)} %get-tuple-element.174), channel_id=1, source_target_pairs={{0,1},{1,0},{2,3},{3,2},{4,5},{5,4},{6,7},{7,6},{8,9},{9,8},{10,11... | collective-permute-start | bytes 786440 | tf_op jit(solution)/shard_map/ppermute | solution.py:280
  127.9 11.0 %collective-permute-start.29 = (bf16[512,256]{1,0:T(8,128)(2,1)S(1)}, bf16[512,256]{1,0:T(8,128)(2,1)S(1)}, u32[]{:S(2)}, u32[]{:S(2)}) collective-permute-start(bf16[512,256]{1,0:T(8,128)(2,1)S(1)} %pass.3), channel_id=1, source_target_pairs={{0,6},{2,0},{4,2},{6,4},{1,7},{3,1},{5,3},{7,5},{8,14},{10,8},{12,... | collective-permute-start | bytes 786440 | tf_op jit(solution)/shard_map/ppermute | solution.py:286
  140.7 6.4 %collective-permute-start.30 = (bf16[256,256]{1,0:T(8,128)(2,1)S(1)}, bf16[256,256]{1,0:T(8,128)(2,1)S(1)}, u32[]{:S(2)}, u32[]{:S(2)}) collective-permute-start(bf16[256,256]{1,0:T(8,128)(2,1)S(1)} %get-tuple-element.195), channel_id=1, source_target_pairs={{0,8},{8,0},{16,24},{24,16},{1,9},{9,1},{17,25},{25,17},{2,10},{10... | collective-permute-start | bytes 393224 | tf_op jit(solution)/shard_map/ppermute | solution.py:283
  142.1 7.2 %collective-permute-start.31 = (bf16[256,256]{1,0:T(8,128)(2,1)S(1)}, bf16[256,256]{1,0:T(8,128)(2,1)S(1)}, u32[]{:S(2)}, u32[]{:S(2)}) collective-permute-start(bf16[256,256]{1,0:T(8,128)(2,1)S(1)} %get-tuple-element.196), channel_id=1, source_target_pairs={{0,16},{8,24},{16,0},{24,8},{1,17},{9,25},{17,1},{25,9},{2,18},{10... | collective-permute-start | bytes 393224 | tf_op jit(solution)/shard_map/ppermute | solution.py:283
  143.0 6.3 %collective-permute-start.32 = (bf16[256,256]{1,0:T(8,128)(2,1)S(1)}, bf16[256,256]{1,0:T(8,128)(2,1)S(1)}, u32[]{:S(2)}, u32[]{:S(2)}) collective-permute-start(bf16[256,256]{1,0:T(8,128)(2,1)S(1)} %get-tuple-element.197), channel_id=1, source_target_pairs={{0,24},{8,16},{16,8},{24,0},{1,25},{9,17},{17,9},{25,1},{2,26},{10... | collective-permute-start | bytes 393224 | tf_op jit(solution)/shard_map/ppermute | solution.py:283
  149.4 5.0 %collective-permute-start.33 = (bf16[256,256]{1,0:T(8,128)(2,1)S(1)}, bf16[256,256]{1,0:T(8,128)(2,1)S(1)}, u32[]{:S(2)}, u32[]{:S(2)}) collective-permute-start(bf16[256,256]{1,0:T(8,128)(2,1)S(1)} %sum.3.refs_0_), channel_id=1, source_target_pairs={{0,2},{2,0},{4,6},{6,4},{1,3},{3,1},{5,7},{7,5},{8,10},{10,8},{12,... | collective-permute-start | bytes 393224 | tf_op jit(solution)/shard_map/ppermute | solution.py:460
  154.5 7.6 %collective-permute-start.34 = (bf16[256,256]{1,0:T(8,128)(2,1)S(1)}, bf16[256,256]{1,0:T(8,128)(2,1)S(1)}, u32[]{:S(2)}, u32[]{:S(2)}) collective-permute-start(bf16[256,256]{1,0:T(8,128)(2,1)S(1)} %sum.4.refs_0_), channel_id=1, source_target_pairs={{0,4},{2,6},{4,0},{6,2},{1,5},{3,7},{5,1},{7,3},{8,12},{10,14},{12... | collective-permute-start | bytes 393224 | tf_op jit(solution)/shard_map/ppermute | solution.py:460
  162.1 5.0 %collective-permute-start.35 = (bf16[256,256]{1,0:T(8,128)(2,1)S(1)}, bf16[256,256]{1,0:T(8,128)(2,1)S(1)}, u32[]{:S(2)}, u32[]{:S(2)}) collective-permute-start(bf16[256,256]{1,0:T(8,128)(2,1)S(1)} %sum.5.refs_1_), channel_id=1, source_target_pairs={{0,8},{8,0},{16,24},{24,16},{1,9},{9,1},{17,25},{25,17},{2,10},{10... | collective-permute-start | bytes 393224 | tf_op jit(solution)/shard_map/ppermute | solution.py:283
  162.8 5.0 %collective-permute-start.36 = (bf16[256,256]{1,0:T(8,128)(2,1)S(1)}, bf16[256,256]{1,0:T(8,128)(2,1)S(1)}, u32[]{:S(2)}, u32[]{:S(2)}) collective-permute-start(bf16[256,256]{1,0:T(8,128)(2,1)S(1)} %sum.5.refs_1_), channel_id=1, source_target_pairs={{0,16},{8,24},{16,0},{24,8},{1,17},{9,25},{17,1},{25,9},{2,18},{10... | collective-permute-start | bytes 393224 | tf_op jit(solution)/shard_map/ppermute | solution.py:283
  164.0 5.9 %collective-permute-start.37 = (bf16[256,256]{1,0:T(8,128)(2,1)S(1)}, bf16[256,256]{1,0:T(8,128)(2,1)S(1)}, u32[]{:S(2)}, u32[]{:S(2)}) collective-permute-start(bf16[256,256]{1,0:T(8,128)(2,1)S(1)} %sum.5.refs_1_), channel_id=1, source_target_pairs={{0,24},{8,16},{16,8},{24,0},{1,25},{9,17},{17,9},{25,1},{2,26},{10... | collective-permute-start | bytes 393224 | tf_op jit(solution)/shard_map/ppermute | solution.py:283
  165.6 5.1 %collective-permute-start.38 = (bf16[256,256]{1,0:T(8,128)(2,1)S(1)}, bf16[256,256]{1,0:T(8,128)(2,1)S(1)}, u32[]{:S(2)}, u32[]{:S(2)}) collective-permute-start(bf16[256,256]{1,0:T(8,128)(2,1)S(1)} %sum.5.refs_1_), channel_id=1, source_target_pairs={{0,1},{1,0},{2,3},{3,2},{4,5},{5,4},{6,7},{7,6},{8,9},{9,8},{10,11... | collective-permute-start | bytes 393224 | tf_op jit(solution)/shard_map/ppermute | solution.py:280
  167.1 3.6 %collective-permute-start.39 = (bf16[256,256]{1,0:T(8,128)(2,1)S(1)}, bf16[256,256]{1,0:T(8,128)(2,1)S(1)}, u32[]{:S(2)}, u32[]{:S(2)}) collective-permute-start(bf16[256,256]{1,0:T(8,128)(2,1)S(1)} %collective-permute-done.35.refs_2_), channel_id=1, source_target_pairs={{0,1},{1,0},{2,3},{3,2},{4,5},{5,4},{6,7},{7,6},{8,9},{9,8},{10,11... | collective-permute-start | bytes 393224 | tf_op jit(solution)/shard_map/ppermute | solution.py:280
  167.8 2.9 %collective-permute-start.40 = (bf16[256,256]{1,0:T(8,128)(2,1)S(1)}, bf16[256,256]{1,0:T(8,128)(2,1)S(1)}, u32[]{:S(2)}, u32[]{:S(2)}) collective-permute-start(bf16[256,256]{1,0:T(8,128)(2,1)S(1)} %collective-permute-done.36.refs_3_), channel_id=1, source_target_pairs={{0,1},{1,0},{2,3},{3,2},{4,5},{5,4},{6,7},{7,6},{8,9},{9,8},{10,11... | collective-permute-start | bytes 393224 | tf_op jit(solution)/shard_map/ppermute | solution.py:280
  169.8 1.3 collective-permute-start.41
  (8 other events, 11.3 us)

commit v7 on v6

--- a/solution.py
+++ b/solution.py
@@ -43,7 +43,7 @@
         out_specs=tuple(vmem for _ in outs),
         scratch_shapes=list(scratch),
         compiler_params=pltpu.CompilerParams(vmem_limit_bytes=size + (6 << 20)),
-        cost_estimate=pl.CostEstimate(flops=int(us * 2.5e8), bytes_accessed=0, transcendentals=0),
+        cost_estimate=pl.CostEstimate(flops=int(us * 2e7), bytes_accessed=0, transcendentals=0),
         name=name,
     )(*(value for _, value in ins))
 
@@ -56,7 +56,7 @@
         self.pair = rows // (self.grp * self.dom)
         self.piece = self.grp * self.pair
         self.per_grp = self.dom * self.pair
-        assert rows // 128 < 7 and self.pair <= 128
+        assert rows // 128 < 5 and self.pair <= 128
 
     def before(self, d):
         inner = d % self.dom
@@ -87,9 +87,9 @@
     want = (dot(owner, high) * 16.0 + dot(owner, low)).astype(I32)
     out_ref[...] = jnp.zeros_like(out_ref)
     for d in range(z.grp * z.dom):
-        out_ref[d, 0:1, 0:z.pair] = want[d:d + 1, :]
         near = z.before(d)
-        out_ref[d, 7:8, 0:z.pair] = want[near:near + 1, :]
+        for line, source in ((0, d), (5, d ^ 1), (6, near), (7, near ^ 1)):
+            out_ref[d, line:line + 1, 0:z.pair] = want[source:source + 1, :]
     across_grp = (source_r >> log2(z.dom)) ^ me_ref[0]
     inner = source_r & (z.dom - 1)
     slot = (inner * z.grp + across_grp) * z.pair + rank_r
@@ -98,49 +98,45 @@
         out_ref[:, 1 + i:2 + i, :] = jnp.broadcast_to(lanes[None], (z.grp * z.dom, 1, 128))
 
 
-def product_kernel(z, me_ref, weight_ref, *refs):
-    parts, outs = refs[:-2], refs[-2:]
-    half, size = outs[0].shape[1], parts[0].shape[0]
+def product_kernel(z, me_ref, features_ref, weight_ref, *outs):
+    half = outs[0].shape[1]
     for flip, out in enumerate(outs):
         at = pl.multiple_of((me_ref[2] ^ flip) * half, half)
-        for i, part in enumerate(parts):
-            product = dot(part[...], weight_ref[:, pl.ds(at, half)])
-            out[i * size:(i + 1) * size, :] = product.astype(BF16)
-
-
-def send_kernel(z, line, me_ref, message_ref, own_ref, other_ref, pick_ref, *outs):
+        out[...] = dot(features_ref[...], weight_ref[:, pl.ds(at, half)]).astype(BF16)
+
+
+def send_kernel(z, lines, me_ref, message_ref, own_ref, other_ref, pick_ref, *outs):
     devices, height, width = message_ref.shape
     message = message_ref[...].reshape(devices * height, width)
+    high_bits = (message >> 4).astype(F32).astype(BF16)
+    low_bits = (message & 15).astype(F32).astype(BF16)
     shape = (z.rows, devices * height)
     asker = (iota(shape, 0) >> log2(z.pair)) ^ (me_ref[0] * z.dom)
-    spread = one_hot(iota(shape, 1) == asker * height + line)
-    high = dot(spread, (message >> 4).astype(F32).astype(BF16))
-    low = dot(spread, (message & 15).astype(F32).astype(BF16))
     mine = iota((z.rows, width), 1) == (iota((z.rows, width), 0) & (z.pair - 1))
-    wanted = jnp.sum(jnp.where(mine, high * 16.0 + low, 0.0), axis=1, keepdims=True).astype(I32)
-    pick_ref[...] = one_hot(iota((z.rows, z.rows), 1) == wanted)
-    for flip, product in enumerate((own_ref, other_ref)):
-        got = dot(pick_ref[...], product[...]).astype(BF16)
+    for rel, (line, product) in enumerate(zip(lines, (own_ref, other_ref))):
+        spread = one_hot(iota(shape, 1) == asker * height + line)
+        asked = dot(spread, high_bits) * 16.0 + dot(spread, low_bits)
+        wanted = jnp.sum(jnp.where(mine, asked, 0.0), axis=1, keepdims=True).astype(I32)
+        pick = one_hot(iota((z.rows, z.rows), 1) == wanted)
+        if rel == 0:
+            pick_ref[...] = pick
+        got = dot(pick, product[...]).astype(BF16)
         for s in range(z.grp):
-            outs[s][flip] = got[s * z.per_grp:(s + 1) * z.per_grp, :]
-
-
-def rows_kernel(z, pick_ref, *refs):
-    parts, outs = refs[:-z.grp], refs[-z.grp:]
-    size = parts[0].shape[0]
+            outs[s][rel] = got[s * z.per_grp:(s + 1) * z.per_grp, :]
+
+
+def rows_kernel(z, pick_ref, features_ref, *outs):
     for s, out in enumerate(outs):
-        at = pl.ds(s * z.per_grp, z.per_grp)
-        rows = sum(
-            dot(pick_ref[at, i * size:(i + 1) * size], part[...]) for i, part in enumerate(parts)
-        )
-        out[...] = rows.astype(BF16)
+        pick = pick_ref[s * z.per_grp:(s + 1) * z.per_grp, :]
+        out[...] = dot(pick, features_ref[...]).astype(BF16)
 
 
 def pack_kernel(z, *refs):
-    ins, outs = refs[:z.grp], refs[z.grp:]
-    for flip in range(2):
+    ins, out = refs[:-1], refs[-1]
+    for rel in range(2):
         for s in range(z.grp):
-            outs[flip][s * z.per_grp:(s + 1) * z.per_grp, :] = ins[s][flip]
+            at = (rel * z.grp + s) * z.per_grp
+            out[at:at + z.per_grp, :] = ins[s][rel]
 
 
 def place_kernel(z, me_ref, message_ref, out_ref):
@@ -193,8 +189,7 @@
 
 def forward_kernel(z, first, last, *refs):
     turned, refs = refs[:2], refs[2:]
-    pieces, refs = refs[:2], refs[2:]
-    rows = jnp.concatenate([ref[...] for ref in pieces], axis=0)
+    rows, refs = refs[0][...], refs[1:]
     agg = [dot_rows(ref[...], rows) for ref in turned]
     if not first:
         agg = [part + ref[...] for part, ref in zip(agg, refs)]
@@ -203,38 +198,29 @@
         for ref, part in zip(refs, agg):
             ref[...] = part
         return
-    cots, ahead, hiddens, grads, parts = (refs[2 * i:2 * i + 2] for i in range(5))
+    cots, ahead, hiddens, grads = (refs[2 * i:2 * i + 2] for i in range(4))
     for part, cot, hidden, grad in zip(agg, cots, hiddens, grads):
         sig = jax.nn.sigmoid(part)
         hidden[...] = (part * sig).astype(BF16)
         grad[...] = (cot[...].astype(F32) * (sig * (1.0 + part * (1.0 - sig)))).astype(BF16)
-    back_into(parts, ahead, grads)
-
-
-def back_into(outs, turned, grads):
-    size = outs[0].shape[0]
-    for i, out in enumerate(outs):
-        rows = pl.ds(i * size, size)
-        value = dot(turned[0][rows, :], grads[0][...]) + dot(turned[1][rows, :], grads[1][...])
-        out[...] = value.astype(out.dtype)
-
-
-def back_kernel(turned_a, turned_b, grad_a, grad_b, *outs):
-    back_into(outs, (turned_a, turned_b), (grad_a, grad_b))
+    back_kernel(*ahead, *grads, refs[-1])
+
+
+def back_kernel(turned_a, turned_b, grad_a, grad_b, out):
+    value = dot(turned_a[...], grad_a[...]) + dot(turned_b[...], grad_b[...])
+    out[...] = value.astype(out.dtype)
 
 
 def pass_kernel(mine_ref, come_ref, out_ref):
     out_ref[...] = (mine_ref[...] + come_ref[...].astype(F32)).astype(BF16)
 
 
-def grad_kernel(z, me_ref, *refs):
-    own_left, near_left = refs[0:2], refs[2:4]
-    own, mine, come, outs, whole = refs[4:6], refs[6:8], refs[8:10], refs[10:-1], refs[-1]
-    total = 0.0
-    for left, part in zip(own_left, own):
-        total = total + dot(left[...], part[...].astype(BF16))
-    for left, part, moved in zip(near_left, mine, come):
-        total = total + dot(left[...], (part[...] + moved[...].astype(F32)).astype(BF16))
+def grad_kernel(z, me_ref, own_a, own_b, near_a, near_b, own_ref, mine_ref, come_ref, *refs):
+    outs, whole = refs[:-1], refs[-1]
+    own = own_ref[...].astype(BF16)
+    near = (mine_ref[...] + come_ref[...].astype(F32)).astype(BF16)
+    total = dot(own_a[...], own[:z.rows]) + dot(own_b[...], own[z.rows:])
+    total = total + dot(near_a[...], near[:z.rows]) + dot(near_b[...], near[z.rows:])
     whole[...] = total.astype(BF16)
     share = whole.shape[0] // z.grp
     for s in range(z.grp):
@@ -298,41 +284,56 @@
     )
     vals_b = to_core(block_vals)
 
-    def products_of(parts):
-        return call(
+    def products_of(part):
+        own, other = call(
             lambda *refs: product_kernel(z, *refs),
             [((rows, half), BF16)] * 2,
-            [("s", me), ("v", weight)] + [("v", part) for part in parts],
+            [("s", me), ("v", part), ("v", weight)],
             "product", 1.5,
         )
-
-    def send_of(line, products):
-        return call(
-            lambda *refs: send_kernel(z, line, *refs),
+        return own, to_core(other)
+
+    def send_of(lines, products):
+        return call(
+            lambda *refs: send_kernel(z, lines, *refs),
             [((rows, rows), BF16)] + [((2, z.per_grp, half), BF16)] * z.grp,
             [("s", me), ("v", message)] + [("v", part) for part in products],
             "send", 1.5,
         )
 
+    def across(parts):
+        return [to_grp(part, s) for s, part in enumerate(parts)]
+
     def pack(parts):
-        own, other = call(
+        return call(
             lambda *refs: pack_kernel(z, *refs),
-            [((rows, half), BF16)] * 2,
+            [((2 * rows, half), BF16)],
             [("v", part) for part in parts],
             "pack", 0.5,
-        )
-        return [own, to_core(other)]
-
-    near = [to_zz(first_half, 1)]
-    products = products_of([features])
-    products, later = lax.optimization_barrier((products, features[rows // 2:]))
-    near.append(to_zz(later, 1))
-    message, vals_b, near[0] = lax.optimization_barrier((message, vals_b, near[0]))
-    pick, *got = send_of(0, products)
-    got, message, cotangent, block_cols = lax.optimization_barrier(
-        (got, message, cotangent, block_cols)
-    )
-    came = [to_grp(got[s], s) for s in range(z.grp)]
+        )[0]
+
+    def rows_of(pick, part):
+        return call(
+            lambda *refs: rows_kernel(z, *refs),
+            [((z.per_grp, width_in), BF16)] * z.grp,
+            [("v", pick), ("v", part)],
+            "rows", 1,
+        )
+
+    def turned_of(parts):
+        (left,) = call(
+            turn_kernel, [((width_in, rows), BF16)], [("v", part) for part in parts], "turn", 0.5
+        )
+        return [left, to_core(left)]
+
+    products = products_of(features)
+    pick, *got = send_of((0, 5), products)
+    got, message, cotangent, block_cols, vals_b, late = lax.optimization_barrier(
+        (got, message, cotangent, block_cols, vals_b, features)
+    )
+    came = across(got)
+
+    near = to_zz(late, 1)
 
     live = iota((tiles, blocks), 1) < block_count[:, None]
     cols_a = jnp.where(live, block_cols, z.dom * tiles)
@@ -340,100 +341,82 @@
     cot_a = lax.dynamic_slice_in_dim(cotangent, core * half, half, axis=1)
     cot_b = to_core(lax.dynamic_slice_in_dim(cotangent, (1 - core) * half, half, axis=1))
 
-    wide = 2 * z.grp * z.per_grp
-
-    def arranged(cols, vals):
-        (dense,) = call(
+    (place,) = call(
+        lambda *refs: place_kernel(z, *refs),
+        [((z.dom, rows, rows), BF16)],
+        [("s", me), ("v", message)],
+        "place", 1.5,
+    )
+
+    def dense_of(cols, vals):
+        return call(
             dense_kernel,
             [((z.dom * rows, rows), BF16)],
             [("s", cols), ("v", vals)],
             "dense", 2.5,
             (pltpu.VMEM((z.dom * rows + tile, tile), F32),),
-        )
-        return arrange(z, place, dense, wide)
-
-    pick_near, *got = send_of(7, products_of(near))
-    came, got = lax.optimization_barrier((came, got))
-
-    def lefts_of(pick, parts):
-        picked = call(
-            lambda *refs: rows_kernel(z, *refs),
-            [((z.per_grp, width_in), BF16)] * z.grp,
-            [("v", pick)] + [("v", part) for part in parts],
-            "rows", 1,
-        )
-        return [to_grp(picked[s], s) for s in range(z.grp)]
-
-    def turned_of(parts):
-        (left,) = call(
-            turn_kernel, [((width_in, rows), BF16)], [("v", part) for part in parts], "turn", 0.5
-        )
-        return [left, to_core(left)]
-
+        )[0]
+
+    dense_a = dense_of(cols_a, block_vals)
+    came, dense_a, place, cols_b = lax.optimization_barrier((came, dense_a, place, cols_b))
+
+    wide = 2 * z.grp * z.per_grp
+    turned = [arrange(z, place, dense_a, wide), arrange(z, place, dense_of(cols_b, vals_b), wide)]
     ring = {0: pack(came)}
-    came = [to_grp(got[s], s) for s in range(z.grp)]
-    ring[0][1], pick, message = lax.optimization_barrier((ring[0][1], pick, message))
-    (place,) = call(
-        lambda *refs: place_kernel(z, *refs),
-        [((z.dom, rows, rows), BF16)],
-        [("s", me), ("v", message)],
-        "place", 1.5,
-    )
-    turned = [arranged(cols_a, block_vals)]
+    lefts = turned_of(across(rows_of(pick, features)))
+    near, turned[0][0] = lax.optimization_barrier((near, turned[0][0]))
     order = list(range(z.zz - 1, 1, -1))
     for k in order:
-        ring[k] = [to_zz(part, -1) for part in ring[(k + 1) % z.zz]]
+        ring[k] = to_zz(ring[(k + 1) % z.zz], -1)
         if k == order[0]:
-            ring[k][0], vals_b = lax.optimization_barrier((ring[k][0], vals_b))
-            turned.append(arranged(cols_b, vals_b))
-    came, left = lax.optimization_barrier((came, lefts_of(pick, [features])))
+            pick_near, *got = send_of((6, 7), products_of(near))
+            ring[k], turned, got, cot_a, cot_b, lefts = lax.optimization_barrier(
+                (ring[k], turned, got, cot_a, cot_b, lefts)
+            )
+            came = across(got)
+    came, pick_near = lax.optimization_barrier((came, pick_near))
     ring[1] = pack(came)
-    lefts = turned_of(left)
+    held_near = rows_of(pick_near, near)
 
     agg = []
-    order = [0, 1] + order
+    order = [0] + order[:-1] + [1] + order[-1:]
     for k in order:
-        ins = [("v", turned[0][k]), ("v", turned[1][k])] + [("v", part) for part in ring[k]]
-        ins += [("v", part) for part in agg]
+        last = k == order[-1]
+        if last:
+            agg, held_near = lax.optimization_barrier((agg, held_near))
+        ins = [("v", part) for part in (turned[0][k], turned[1][k], ring[k], *agg)]
         outs = [((rows, half), F32)] * 2
-        last = k == order[-1]
         if last:
             ahead = (turned[0][z.zz - 1], turned[1][z.zz - 1])
             ins += [("v", part) for part in (cot_a, cot_b, *ahead)]
-            outs = [((rows, half), BF16)] * 4 + [((wide // 2, half), BF16)] * 2
+            outs = [((rows, half), BF16)] * 4 + [((wide, half), BF16)]
         agg = call(
             lambda *refs, k=k, last=last: forward_kernel(z, k == 0, last, *refs),
             outs, ins, "forward", 3 if last else 1,
         )
-    hidden_a, hidden_b, grad_a, grad_b, *came = agg
+    hidden_a, hidden_b, grad_a, grad_b, came = agg
 
     def back(k):
         return call(
             back_kernel,
-            [((wide // 2, half), F32)] * 2,
+            [((wide, half), F32)],
             [("v", part) for part in (turned[0][k], turned[1][k], grad_a, grad_b)],
             "back", 1,
-        )
-
+        )[0]
+
+    held_near = across(held_near)
+    come = to_core(hidden_b)
     for k in range(z.zz - 2, 0, -1):
-        came = [to_zz(part, -1) for part in came]
-        if k == z.zz - 2:
-            came[0], pick_near = lax.optimization_barrier((came[0], pick_near))
-            lefts += turned_of(lefts_of(pick_near, near))
+        came = to_zz(came, -1)
         mine = back(k)
         if k == 1:
-            came[1], come = lax.optimization_barrier((came[1], come))
             break
-        came = [
-            call(
-                pass_kernel, [((wide // 2, half), BF16)], [("v", part), ("v", moved)],
-                "pass", 0.5,
-            )[0]
-            for part, moved in zip(mine, came)
-        ]
+        (came,) = call(
+            pass_kernel, [((wide, half), BF16)], [("v", mine), ("v", came)], "pass", 0.5
+        )
         if k == z.zz - 2:
-            came[1], hidden_b = lax.optimization_barrier((came[1], hidden_b))
-            come = to_core(hidden_b)
+            came, come, held_near = lax.optimization_barrier((came, come, held_near))
+    lefts += turned_of(held_near)
     first = core == 0
     hidden = jnp.concatenate(
         [jnp.where(first, hidden_a, come), jnp.where(first, come, hidden_a)], axis=1
@@ -443,7 +426,7 @@
     terms = call(
         lambda *refs: grad_kernel(z, *refs),
         [((share, half), BF16)] * z.grp,
-        [("s", me)] + [("v", part) for part in (*lefts, *back(0), *mine, *came)],
+        [("s", me)] + [("v", part) for part in (*lefts, back(0), mine, came)],
         "grad", 1.5,
         (pltpu.VMEM((width_in, half), BF16),),
     )

time: 174 us -> 159 us (0.914)
  starting transfers between devices: 43.6 us -> 32.5 us
  blocking collectives: 22.2 us -> 15.3 us
  Pallas kernels: 35.8 us -> 38.7 us
  local copies, waits for them, and re-layouts: 10.3 us -> 12.8 us
  waiting for transfers between devices: 59.2 us -> 57.1 us
    ppermute x10 -> x5, starting transfers between devices: 17.9 us -> 7.32 us  [to_zz(): lax.ppermute(x, 'zz', [(i, (i + k) % z.zz) for i in range(z.zz)])]
    all_to_all x1, blocking collectives: 22.2 us -> 15.3 us  [shards(): lax.all_to_all(message, ('grp', 'zz', 'core'), split_axis=0, concat_axis=...]
    unnamed x28, local copies, waits for them, and re-layouts: 7.23 us -> 12.8 us
    slice x2 -> x0, local copies, waits for them, and re-layouts: 3.03 us -> none  [the longest x1 1.87 us: shards(): first_half = features[:rows // 2]]
    pallas_call x30 -> x29, Pallas kernels: 35.8 us -> 38.7 us  [call(): pl.pallas_call(body, out_shape=tuple((jax.ShapeDtypeStruct(s, d) for s, d...]
    ppermute x10 -> x5, waiting for transfers between devices: 22.6 us -> 21.1 us  [to_zz(): lax.ppermute(x, 'zz', [(i, (i + k) % z.zz) for i in range(z.zz)])]
  transfers between devices with their start and end apart: 42 -> 37, of which waited for: 17 -> 15; matrix products, arithmetic and copies ran while one was open for 2% -> 1% of each run, Pallas kernels for 15% -> 18%
where the time goes in v7:
time: 159 us; the launch traced here: 158 us
  waiting for transfers between devices  57.1 us (36%)
  Pallas kernels  38.7 us (24%)
  starting transfers between devices  32.5 us (20%)
  blocking collectives  15.3 us (10%)
  local copies, waits for them, and re-layouts  12.8 us (8%)
    pallas_call x29, Pallas kernels, call(): pl.pallas_call(body, out_shape=tuple((jax.ShapeDtypeStruct(s, d) for s, d...  38.7 us
    ppermute x18, waiting for transfers between devices, to_grp(): lax.ppermute(x, 'grp', [(i, i ^ s) for i in range(z.grp)])  25.3 us
    ppermute x18, starting transfers between devices, to_grp(): lax.ppermute(x, 'grp', [(i, i ^ s) for i in range(z.grp)])  21.2 us
    ppermute x5, waiting for transfers between devices, to_zz(): lax.ppermute(x, 'zz', [(i, (i + k) % z.zz) for i in range(z.zz)])  21.1 us
    all_to_all x1, blocking collectives, shards(): lax.all_to_all(message, ('grp', 'zz', 'core'), split_axis=0, concat_axis=...  15.3 us
    unnamed x28, local copies, waits for them, and re-layouts  12.8 us
    ppermute x2, waiting for transfers between devices, shards(): lax.ppermute(mine, 'zz', [(i, i ^ step) for i in range(z.zz)])  10.2 us
    ppermute x5, starting transfers between devices, to_zz(): lax.ppermute(x, 'zz', [(i, (i + k) % z.zz) for i in range(z.zz)])  7.32 us
  transfers between devices with their start and end apart: 37, of which 15 were waited for; matrix products, arithmetic and copies ran while one was open for 1% of the time, Pallas kernels for 18%

profile of v7, /device:TPU:0, one launch (start us, length us, event | category | flops | bytes accessed | tf_op | source)
XLA Modules:
  0.0 158.4 jit_solution(5079953440816976408)
XLA Ops:
  5.5 1.3 product.2
  6.9 15.3 %all_to_all.5.refs_1_ = s32[32,8,128]{2,1,0:T(8,128)S(1)} all-to-all(s32[32,8,128]{2,1,0:T(8,128)S(1)} %index.1), channel_id=1, replica_groups=mesh['grp'=4,'zz'=4,'core'=2] {'grp','zz','core'}, dimensions={0} | all-to-all | bytes 262144 | tf_op jit(solution)/shard_map/all_to_all | solution.py:282
  22.2 1.7 %send.2 = (bf16[512,512]{1,0:T(8,128)(2,1)S(1)}, bf16[2,128,256]{2,1,0:T(8,128)(2,1)S(1)}, bf16[2,128,256]{2,1,0:T(8,128)(2,1)S(1)}, bf16[2,128,256]{2,1,0:T(8,128)(2,1)S(1)}, bf16[2,128,256]{2,1,0:T(8,128)(2,1)S(1)}) custom-call(s32[3]{0:T(128)S(1)} %pad_add_fusion.refs_0_, s32[32,8,128]{2,1,0:T(8,128)S(1)} %all_to_all.5.refs_1_, ...), custom_call_target="tpu_custom_call" | custom-call | flops 30000000 | tf_op jit(solution)/shard_map/send/pallas_call | solution.py:39
  24.5 1.3 copy-done.6
  27.7 2.3 %collective-permute-start.12 = (bf16[128,1024]{1,0:T(8,128)(2,1)S(1)}, bf16[128,1024]{1,0:T(8,128)(2,1)S(1)}, u32[]{:S(2)}, u32[]{:S(2)}) collective-permute-start(bf16[128,1024]{1,0:T(8,128)(2,1)S(1)} %get-tuple-element.145), channel_id=1, source_target_pairs={{0,24},{8,16},{16,8},{24,0},{1,25},{9,17},{17,9},{25,1},{2,26},{10... | collective-permute-start | bytes 786440 | tf_op jit(solution)/shard_map/ppermute | solution.py:269
  30.0 5.7 %collective-permute-done.10.refs_1_ = bf16[128,1024]{1,0:T(8,128)(2,1)S(1)} collective-permute-done((bf16[128,1024]{1,0:T(8,128)(2,1)S(1)}, bf16[128,1024]{1,0:T(8,128)(2,1)S(1)}, u32[]{:S(2)}, u32[]{:S(2)}) %collective-permute-start.10) | collective-permute-done | bytes 262176 | tf_op jit(solution)/shard_map/ppermute | solution.py:269
  35.7 4.9 %collective-permute-done.11.refs_2_ = bf16[128,1024]{1,0:T(8,128)(2,1)S(1)} collective-permute-done((bf16[128,1024]{1,0:T(8,128)(2,1)S(1)}, bf16[128,1024]{1,0:T(8,128)(2,1)S(1)}, u32[]{:S(2)}, u32[]{:S(2)}) %collective-permute-start.11) | collective-permute-done | bytes 262176 | tf_op jit(solution)/shard_map/ppermute | solution.py:269
  40.6 1.3 turn.2.refs_1_
  42.5 1.3 collective-permute-start.2
  44.5 1.4 collective-permute-start.4
  46.0 1.4 place.1.refs_0_
  47.4 2.0 %copy-done = bf16[8,512,512]{2,1,0:T(8,128)(2,1)} copy-done((bf16[8,512,512]{2,1,0:T(8,128)(2,1)}, bf16[8,512,512]{2,1,0:T(8,128)(2,1)S(1)}, u32[]{:S(2)}) %copy-start) | copy-done | bytes 4194328
  49.4 2.4 %dense.2.refs_1_ = bf16[4096,512]{1,0:T(8,128)(2,1)S(1)} custom-call(s32[4,16]{1,0:T(4,128)S(1)} %fusion.cols_ref, bf16[4,16,128,128]{3,2,1,0:T(8,128)(2,1)S(1)} %copy-done.9), custom_call_target="tpu_custom_call" | custom-call | flops 50000000 | tf_op jit(solution)/shard_map/dense/pallas_call | solution.py:39
  51.8 2.0 %copy-done.3 = bf16[4096,512]{1,0:T(8,128)(2,1)} copy-done((bf16[4096,512]{1,0:T(8,128)(2,1)}, bf16[4096,512]{1,0:T(8,128)(2,1)S(1)}, u32[]{:S(2)}) %copy-start.3) | copy-done | bytes 4194328
  54.6 3.1 %collective-permute-start.6 = (bf16[1024,256]{1,0:T(8,128)(2,1)}, bf16[1024,256]{1,0:T(8,128)(2,1)}, u32[]{:S(2)}, u32[]{:S(2)}) collective-permute-start(bf16[1024,256]{1,0:T(8,128)(2,1)} %pack.2.refs_2_), channel_id=1, source_target_pairs={{0,6},{2,0},{4,2},{6,4},{1,7},{3,1},{5,3},{7,5},{8,14},{10,8},{12,... | collective-permute-start | bytes 1572872 | tf_op jit(solution)/shard_map/ppermute | solution.py:272
  57.8 2.2 %copy-done.1 = bf16[8,512,512]{2,1,0:T(8,128)(2,1)S(1)} copy-done((bf16[8,512,512]{2,1,0:T(8,128)(2,1)S(1)}, bf16[8,512,512]{2,1,0:T(8,128)(2,1)}, u32[]{:S(2)}) %copy-start.1) | copy-done | bytes 4194328
  60.0 2.2 %copy-done.4 = bf16[4096,512]{1,0:T(8,128)(2,1)S(1)} copy-done((bf16[4096,512]{1,0:T(8,128)(2,1)S(1)}, bf16[4096,512]{1,0:T(8,128)(2,1)}, u32[]{:S(2)}) %copy-start.4) | copy-done | bytes 4194328
  62.1 3.5 %arrange.2 = (bf16[1024,512]{1,0:T(8,128)(2,1)S(1)}, bf16[1024,512]{1,0:T(8,128)(2,1)S(1)}, bf16[1024,512]{1,0:T(8,128)(2,1)S(1)}, bf16[1024,512]{1,0:T(8,128)(2,1)S(1)}) custom-call(bf16[8,512,512]{2,1,0:T(8,128)(2,1)S(1)} %copy-done.1, bf16[4096,512]{1,0:T(8,128)(2,1)S(1)} %copy-done.4), custom_call_target="tpu_custom_call" | custom-call | flops 80000000 | tf_op jit(solution)/shard_map/arrange/pallas_call | solution.py:39
  65.7 1.3 product.3
  67.6 3.8 %dense.3.refs_1_ = bf16[4096,512]{1,0:T(8,128)(2,1)S(1)} custom-call(s32[4,16]{1,0:T(4,128)S(1)} %collective-permute-done.5.cols_ref, bf16[4,16,128,128]{3,2,1,0:T(8,128)(2,1)} %collective-permute-done.1.vals_ref), custom_call_target="tpu_custom_call" | custom-call | flops 50000000 | tf_op jit(solution)/shard_map/dense/pallas_call | solution.py:39
  71.4 3.5 %arrange.3 = (bf16[1024,512]{1,0:T(8,128)(2,1)S(1)}, bf16[1024,512]{1,0:T(8,128)(2,1)S(1)}, bf16[1024,512]{1,0:T(8,128)(2,1)S(1)}, bf16[1024,512]{1,0:T(8,128)(2,1)S(1)}) custom-call(bf16[8,512,512]{2,1,0:T(8,128)(2,1)S(1)} %copy-done.2, bf16[4096,512]{1,0:T(8,128)(2,1)S(1)} %dense.3.refs_1_), custom_call_target="tpu_custom_call" | custom-call | flops 80000000 | tf_op jit(solution)/shard_map/arrange/pallas_call | solution.py:39
  75.0 1.7 %send.3 = (bf16[512,512]{1,0:T(8,128)(2,1)S(1)}, bf16[2,128,256]{2,1,0:T(8,128)(2,1)S(1)}, bf16[2,128,256]{2,1,0:T(8,128)(2,1)S(1)}, bf16[2,128,256]{2,1,0:T(8,128)(2,1)S(1)}, bf16[2,128,256]{2,1,0:T(8,128)(2,1)S(1)}) custom-call(s32[3]{0:T(128)S(1)} %pad_add_fusion.refs_0_, s32[32,8,128]{2,1,0:T(8,128)S(1)} %all_to_all.5.refs_1_, ...), custom_call_target="tpu_custom_call" | custom-call | flops 30000000 | tf_op jit(solution)/shard_map/send/pallas_call | solution.py:39
  76.9 1.7 %collective-permute-start.15 = (bf16[2,128,256]{2,1,0:T(8,128)(2,1)S(1)}, bf16[2,128,256]{2,1,0:T(8,128)(2,1)S(1)}, u32[]{:S(2)}, u32[]{:S(2)}) collective-permute-start(bf16[2,128,256]{2,1,0:T(8,128)(2,1)S(1)} %get-tuple-element.152), channel_id=1, source_target_pairs={{0,8},{8,0},{16,24},{24,16},{1,9},{9,1},{17,25},{25,17},{2,10},{10... | collective-permute-start | bytes 393224 | tf_op jit(solution)/shard_map/ppermute | solution.py:269
  79.2 1.3 collective-permute-start.17
  80.5 1.8 %forward.4 = (f32[512,256]{1,0:T(8,128)S(1)}, f32[512,256]{1,0:T(8,128)S(1)}) custom-call(bf16[1024,512]{1,0:T(8,128)(2,1)S(1)} %get-tuple-element.162.refs_0_.turned_a, bf16[1024,512]{1,0:T(8,128)(2,1)S(1)} %get-tuple-element.163.refs_1_.turned_b, bf16[1024,256]{1,0:T(8,128)(2,1)} %pack.2.refs_2_), custom_call_target="tpu_custom_call" | custom-call | flops 20000000 | tf_op jit(solution)/shard_map/forward/pallas_call | solution.py:39
  82.3 1.8 %forward.5 = (f32[512,256]{1,0:T(8,128)S(1)}, f32[512,256]{1,0:T(8,128)S(1)}) custom-call(bf16[1024,512]{1,0:T(8,128)(2,1)S(1)} %get-tuple-element.160.refs_0_.refs_7_, bf16[1024,512]{1,0:T(8,128)(2,1)S(1)} %get-tuple-element.161.refs_1_.refs_8_, bf16[1024,256]{1,0:T(8,128)(2,1)} %collective-permute-done.6.refs_2_, ...), custom_call_target="tpu_custom_call" | custom-call | flops 20000000 | tf_op jit(solution)/shard_map/forward/pallas_call | solution.py:39
  84.1 2.3 %collective-permute-done.16.refs_2_ = bf16[2,128,256]{2,1,0:T(8,128)(2,1)S(1)} collective-permute-done((bf16[2,128,256]{2,1,0:T(8,128)(2,1)S(1)}, bf16[2,128,256]{2,1,0:T(8,128)(2,1)S(1)}, u32[]{:S(2)}, u32[]{:S(2)}) %collective-permute-start.16) | collective-permute-done | bytes 131104 | tf_op jit(solution)/shard_map/ppermute | solution.py:269
  88.0 2.9 %collective-permute-done.14.refs_2_ = bf16[1024,256]{1,0:T(8,128)(2,1)S(1)} collective-permute-done((bf16[1024,256]{1,0:T(8,128)(2,1)}, bf16[1024,256]{1,0:T(8,128)(2,1)S(1)}, u32[]{:S(2)}, u32[]{:S(2)}) %collective-permute-start.14) | collective-permute-done | bytes 524320 | tf_op jit(solution)/shard_map/ppermute | solution.py:272
  90.8 1.6 %forward.7 = (bf16[512,256]{1,0:T(8,128)(2,1)S(1)}, bf16[512,256]{1,0:T(8,128)(2,1)S(1)}, bf16[512,256]{1,0:T(8,128)(2,1)S(1)}, bf16[512,256]{1,0:T(8,128)(2,1)S(1)}, bf16[1024,256]{1,0:T(8,128)(2,1)S(1)}) custom-call(bf16[1024,512]{1,0:T(8,128)(2,1)S(1)} %get-tuple-element.146.refs_0_.turned_a, bf16[1024,512]{1,0:T(8,128)(2,1)S(1)} %get-tuple-element.147.refs_1_.turned_b, ...), custom_call_target="tpu_custom_call" | custom-call | flops 60000000 | tf_op jit(solution)/shard_map/forward/pallas_call | solution.py:39
  92.4 2.1 %collective-permute-start.18 = (bf16[1024,256]{1,0:T(8,128)(2,1)S(1)}, bf16[1024,256]{1,0:T(8,128)(2,1)S(1)}, u32[]{:S(2)}, u32[]{:S(2)}) collective-permute-start(bf16[1024,256]{1,0:T(8,128)(2,1)S(1)} %get-tuple-element.182), channel_id=1, source_target_pairs={{0,6},{2,0},{4,2},{6,4},{1,7},{3,1},{5,3},{7,5},{8,14},{10,8},{12,... | collective-permute-start | bytes 1572872 | tf_op jit(solution)/shard_map/ppermute | solution.py:272
  94.6 1.5 collective-permute-start.20
  96.6 1.5 collective-permute-start.22
  98.8 6.5 %collective-permute-done.18.come_ref = bf16[1024,256]{1,0:T(8,128)(2,1)S(1)} collective-permute-done((bf16[1024,256]{1,0:T(8,128)(2,1)S(1)}, bf16[1024,256]{1,0:T(8,128)(2,1)S(1)}, u32[]{:S(2)}, u32[]{:S(2)}) %collective-permute-start.18) | collective-permute-done | bytes 524320 | tf_op jit(solution)/shard_map/ppermute | solution.py:272
  105.4 3.1 %collective-permute-done.22.refs_3_ = bf16[128,1024]{1,0:T(8,128)(2,1)S(1)} collective-permute-done((bf16[128,1024]{1,0:T(8,128)(2,1)S(1)}, bf16[128,1024]{1,0:T(8,128)(2,1)S(1)}, u32[]{:S(2)}, u32[]{:S(2)}) %collective-permute-start.22) | collective-permute-done | bytes 262176 | tf_op jit(solution)/shard_map/ppermute | solution.py:269
  111.6 11.7 %collective-permute-done.24.refs_7_ = bf16[1024,256]{1,0:T(8,128)(2,1)S(1)} collective-permute-done((bf16[1024,256]{1,0:T(8,128)(2,1)S(1)}, bf16[1024,256]{1,0:T(8,128)(2,1)S(1)}, u32[]{:S(2)}, u32[]{:S(2)}) %collective-permute-start.24) | collective-permute-done | bytes 524320 | tf_op jit(solution)/shard_map/ppermute | solution.py:272
  123.3 2.9 %grad.1 = (bf16[256,256]{1,0:T(8,128)(2,1)S(1)}, bf16[256,256]{1,0:T(8,128)(2,1)S(1)}, bf16[256,256]{1,0:T(8,128)(2,1)S(1)}, bf16[256,256]{1,0:T(8,128)(2,1)S(1)}) custom-call(s32[3]{0:T(128)S(1)} %pad_add_fusion.refs_0_, bf16[1024,512]{1,0:T(8,128)(2,1)} %turn.2.refs_1_, bf16[1024,512]{1,0:T(8,128)(2,1)} %collective-permute-done.13.refs_2_, ...), custom_call_target="tpu_custom_call" | custom-call | flops 30000000 | tf_op jit(solution)/shard_map/grad/pallas_call | solution.py:39
  126.9 1.6 %collective-permute-start.26 = (bf16[256,256]{1,0:T(8,128)(2,1)S(1)}, bf16[256,256]{1,0:T(8,128)(2,1)S(1)}, u32[]{:S(2)}, u32[]{:S(2)}) collective-permute-start(bf16[256,256]{1,0:T(8,128)(2,1)S(1)} %get-tuple-element.198), channel_id=1, source_target_pairs={{0,16},{8,24},{16,0},{24,8},{1,17},{9,25},{17,1},{25,9},{2,18},{10... | collective-permute-start | bytes 393224 | tf_op jit(solution)/shard_map/ppermute | solution.py:269
  129.7 2.8 %collective-permute-done.25.refs_1_ = bf16[256,256]{1,0:T(8,128)(2,1)S(1)} collective-permute-done((bf16[256,256]{1,0:T(8,128)(2,1)S(1)}, bf16[256,256]{1,0:T(8,128)(2,1)S(1)}, u32[]{:S(2)}, u32[]{:S(2)}) %collective-permute-start.25) | collective-permute-done | bytes 131104 | tf_op jit(solution)/shard_map/ppermute | solution.py:269
  132.5 2.2 %collective-permute-done.26.refs_2_ = bf16[256,256]{1,0:T(8,128)(2,1)S(1)} collective-permute-done((bf16[256,256]{1,0:T(8,128)(2,1)S(1)}, bf16[256,256]{1,0:T(8,128)(2,1)S(1)}, u32[]{:S(2)}, u32[]{:S(2)}) %collective-permute-start.26) | collective-permute-done | bytes 131104 | tf_op jit(solution)/shard_map/ppermute | solution.py:269
  134.8 5.0 %collective-permute-done.28.refs_1_ = bf16[256,256]{1,0:T(8,128)(2,1)S(1)} collective-permute-done((bf16[256,256]{1,0:T(8,128)(2,1)S(1)}, bf16[256,256]{1,0:T(8,128)(2,1)S(1)}, u32[]{:S(2)}, u32[]{:S(2)}) %collective-permute-start.28) | collective-permute-done | bytes 131104 | tf_op jit(solution)/shard_map/ppermute | solution.py:443
  139.8 2.1 %collective-permute-start.29 = (bf16[256,256]{1,0:T(8,128)(2,1)S(1)}, bf16[256,256]{1,0:T(8,128)(2,1)S(1)}, u32[]{:S(2)}, u32[]{:S(2)}) collective-permute-start(bf16[256,256]{1,0:T(8,128)(2,1)S(1)} %sum.4.refs_0_), channel_id=1, source_target_pairs={{0,4},{2,6},{4,0},{6,2},{1,5},{3,7},{5,1},{7,3},{8,12},{10,14},{12... | collective-permute-start | bytes 393224 | tf_op jit(solution)/shard_map/ppermute | solution.py:443
  141.9 5.2 %collective-permute-done.29.refs_1_ = bf16[256,256]{1,0:T(8,128)(2,1)S(1)} collective-permute-done((bf16[256,256]{1,0:T(8,128)(2,1)S(1)}, bf16[256,256]{1,0:T(8,128)(2,1)S(1)}, u32[]{:S(2)}, u32[]{:S(2)}) %collective-permute-start.29) | collective-permute-done | bytes 131104 | tf_op jit(solution)/shard_map/ppermute | solution.py:443
  147.2 1.4 collective-permute-start.30
  149.2 1.6 collective-permute-start.32
  150.7 1.5 collective-permute-done.30.refs_2_
  152.2 1.3 collective-permute-done.31.refs_3_
  153.5 1.5 collective-permute-done.32.refs_4_
  156.4 2.0 %last.1 = f32[1024,512]{1,0:T(8,128)} custom-call(s32[3]{0:T(128)S(1)} %pad_add_fusion.refs_0_, bf16[256,256]{1,0:T(8,128)(2,1)S(1)} %sum.5.refs_1_, bf16[256,256]{1,0:T(8,128)(2,1)S(1)} %collective-permute-done.30.refs_2_, bf16[256,256]{1,0:T(8,128)(2,1)S(1)} %collective-permute-done.31.refs_3_, bf16[256,256]{1,0:T(8,128)(2,1)S(1)} %collective-permute-done.32.refs_4_, ...), custom_call_target="tpu_custom_call" | custom-call | flops 40000000 | tf_op jit(solution)/shard_map/last/pallas_call | solution.py:39
  (89 shorter events, 21.1 us)
Async XLA Ops:
  0.6 41.3 %copy-start.12 = (s32[4,16]{1,0:T(4,128)S(1)}, s32[4,16]{1,0:T(4,128)}, u32[]{:S(2)}) copy-start(s32[4,16]{1,0:T(4,128)} %param.9) | copy-start | bytes 772
  0.6 41.3 %copy-start.13 = (s32[4]{0:T(128)S(1)}, s32[4]{0:T(128)}, u32[]{:S(2)}) copy-start(s32[4]{0:T(128)} %param.10) | copy-start | bytes 52
  0.6 23.2 %collective-permute-start.1 = (bf16[4,16,128,128]{3,2,1,0:T(8,128)(2,1)}, bf16[4,16,128,128]{3,2,1,0:T(8,128)(2,1)}, u32[]{:S(2)}, u32[]{:S(2)}) collective-permute-start(bf16[4,16,128,128]{3,2,1,0:T(8,128)(2,1)} %vals_ref.1), channel_id=1, source_target_pairs={{0,1},{1,0},{2,3},{3,2},{4,5},{5,4},{6,7},{7,6},{8,9},{9,8},{10,11... | collective-permute-start | bytes 6291464 | tf_op jit(solution)/shard_map/ppermute | solution.py:266
  5.5 43.9 %copy-start.9 = (bf16[4,16,128,128]{3,2,1,0:T(8,128)(2,1)S(1)}, bf16[4,16,128,128]{3,2,1,0:T(8,128)(2,1)}, u32[]{:S(2)}) copy-start(bf16[4,16,128,128]{3,2,1,0:T(8,128)(2,1)} %vals_ref.1) | copy-start | bytes 6291460
  6.8 15.4 %collective-permute-start = (bf16[512,256]{1,0:T(8,128)(2,1)S(1)}, bf16[512,256]{1,0:T(8,128)(2,1)S(1)}, u32[]{:S(2)}, u32[]{:S(2)}) collective-permute-start(bf16[512,256]{1,0:T(8,128)(2,1)S(1)} %get-tuple-element.104), channel_id=1, source_target_pairs={{0,1},{1,0},{2,3},{3,2},{4,5},{5,4},{6,7},{7,6},{8,9},{9,8},{10,11... | collective-permute-start | bytes 786440 | tf_op jit(solution)/shard_map/ppermute | solution.py:266
  23.9 41.8 %collective-permute-start.7 = (bf16[512,1024]{1,0:T(8,128)(2,1)}, bf16[512,1024]{1,0:T(8,128)(2,1)S(1)}, u32[]{:S(2)}, u32[]{:S(2)}) collective-permute-start(bf16[512,1024]{1,0:T(8,128)(2,1)} %refs_1_.1), channel_id=1, source_target_pairs={{0,2},{2,4},{4,6},{6,0},{1,3},{3,5},{5,7},{7,1},{8,10},{10,12},{12... | collective-permute-start | bytes 3145736 | tf_op jit(solution)/shard_map/ppermute | solution.py:272
  24.5 1.3 copy-start.6
  26.5 9.3 %collective-permute-start.10 = (bf16[128,1024]{1,0:T(8,128)(2,1)S(1)}, bf16[128,1024]{1,0:T(8,128)(2,1)S(1)}, u32[]{:S(2)}, u32[]{:S(2)}) collective-permute-start(bf16[128,1024]{1,0:T(8,128)(2,1)S(1)} %get-tuple-element.143), channel_id=1, source_target_pairs={{0,8},{8,0},{16,24},{24,16},{1,9},{9,1},{17,25},{25,17},{2,10},{10... | collective-permute-start | bytes 786440 | tf_op jit(solution)/shard_map/ppermute | solution.py:269
  27.0 13.6 %collective-permute-start.11 = (bf16[128,1024]{1,0:T(8,128)(2,1)S(1)}, bf16[128,1024]{1,0:T(8,128)(2,1)S(1)}, u32[]{:S(2)}, u32[]{:S(2)}) collective-permute-start(bf16[128,1024]{1,0:T(8,128)(2,1)S(1)} %get-tuple-element.144), channel_id=1, source_target_pairs={{0,16},{8,24},{16,0},{24,8},{1,17},{9,25},{17,1},{25,9},{2,18},{10... | collective-permute-start | bytes 786440 | tf_op jit(solution)/shard_map/ppermute | solution.py:269
  27.7 12.9 %collective-permute-start.12 = (bf16[128,1024]{1,0:T(8,128)(2,1)S(1)}, bf16[128,1024]{1,0:T(8,128)(2,1)S(1)}, u32[]{:S(2)}, u32[]{:S(2)}) collective-permute-start(bf16[128,1024]{1,0:T(8,128)(2,1)S(1)} %get-tuple-element.145), channel_id=1, source_target_pairs={{0,24},{8,16},{16,8},{24,0},{1,25},{9,17},{17,9},{25,1},{2,26},{10... | collective-permute-start | bytes 786440 | tf_op jit(solution)/shard_map/ppermute | solution.py:269
  41.9 34.7 %collective-permute-start.13 = (bf16[1024,512]{1,0:T(8,128)(2,1)}, bf16[1024,512]{1,0:T(8,128)(2,1)}, u32[]{:S(2)}, u32[]{:S(2)}) collective-permute-start(bf16[1024,512]{1,0:T(8,128)(2,1)} %turn.2.refs_1_), channel_id=1, source_target_pairs={{0,1},{1,0},{2,3},{3,2},{4,5},{5,4},{6,7},{7,6},{8,9},{9,8},{10,11... | collective-permute-start | bytes 3145736 | tf_op jit(solution)/shard_map/ppermute | solution.py:266
  42.0 2.6 %collective-permute-start.5 = (s32[4,16]{1,0:T(4,128)S(1)}, s32[4,16]{1,0:T(4,128)S(1)}, u32[]{:S(2)}, u32[]{:S(2)}) collective-permute-start(s32[4,16]{1,0:T(4,128)S(1)} %fusion.cols_ref), channel_id=1, source_target_pairs={{0,1},{1,0},{2,3},{3,2},{4,5},{5,4},{6,7},{7,6},{8,9},{9,8},{10,11... | collective-permute-start | bytes 776 | tf_op jit(solution)/shard_map/ppermute | solution.py:266
  42.5 11.3 %collective-permute-start.2 = (bf16[2,128,256]{2,1,0:T(8,128)(2,1)S(1)}, bf16[2,128,256]{2,1,0:T(8,128)(2,1)S(1)}, u32[]{:S(2)}, u32[]{:S(2)}) collective-permute-start(bf16[2,128,256]{2,1,0:T(8,128)(2,1)S(1)} %get-tuple-element.110), channel_id=1, source_target_pairs={{0,8},{8,0},{16,24},{24,16},{1,9},{9,1},{17,25},{25,17},{2,10},{10... | collective-permute-start | bytes 393224 | tf_op jit(solution)/shard_map/ppermute | solution.py:269
  43.8 10.0 %collective-permute-start.3 = (bf16[2,128,256]{2,1,0:T(8,128)(2,1)S(1)}, bf16[2,128,256]{2,1,0:T(8,128)(2,1)S(1)}, u32[]{:S(2)}, u32[]{:S(2)}) collective-permute-start(bf16[2,128,256]{2,1,0:T(8,128)(2,1)S(1)} %get-tuple-element.111), channel_id=1, source_target_pairs={{0,16},{8,24},{16,0},{24,8},{1,17},{9,25},{17,1},{25,9},{2,18},{10... | collective-permute-start | bytes 393224 | tf_op jit(solution)/shard_map/ppermute | solution.py:269
  44.5 9.3 %collective-permute-start.4 = (bf16[2,128,256]{2,1,0:T(8,128)(2,1)S(1)}, bf16[2,128,256]{2,1,0:T(8,128)(2,1)S(1)}, u32[]{:S(2)}, u32[]{:S(2)}) collective-permute-start(bf16[2,128,256]{2,1,0:T(8,128)(2,1)S(1)} %get-tuple-element.112), channel_id=1, source_target_pairs={{0,24},{8,16},{16,8},{24,0},{1,25},{9,17},{17,9},{25,1},{2,26},{10... | collective-permute-start | bytes 393224 | tf_op jit(solution)/shard_map/ppermute | solution.py:269
  47.4 2.0 %copy-start = (bf16[8,512,512]{2,1,0:T(8,128)(2,1)}, bf16[8,512,512]{2,1,0:T(8,128)(2,1)S(1)}, u32[]{:S(2)}) copy-start(bf16[8,512,512]{2,1,0:T(8,128)(2,1)S(1)} %place.1.refs_0_) | copy-start | bytes 12582916
  51.8 2.0 %copy-start.3 = (bf16[4096,512]{1,0:T(8,128)(2,1)}, bf16[4096,512]{1,0:T(8,128)(2,1)S(1)}, u32[]{:S(2)}) copy-start(bf16[4096,512]{1,0:T(8,128)(2,1)S(1)} %dense.2.refs_1_) | copy-start | bytes 12582916
  54.6 22.0 %collective-permute-start.6 = (bf16[1024,256]{1,0:T(8,128)(2,1)}, bf16[1024,256]{1,0:T(8,128)(2,1)}, u32[]{:S(2)}, u32[]{:S(2)}) collective-permute-start(bf16[1024,256]{1,0:T(8,128)(2,1)} %pack.2.refs_2_), channel_id=1, source_target_pairs={{0,6},{2,0},{4,2},{6,4},{1,7},{3,1},{5,3},{7,5},{8,14},{10,8},{12,... | collective-permute-start | bytes 1572872 | tf_op jit(solution)/shard_map/ppermute | solution.py:272
  57.8 2.2 %copy-start.1 = (bf16[8,512,512]{2,1,0:T(8,128)(2,1)S(1)}, bf16[8,512,512]{2,1,0:T(8,128)(2,1)}, u32[]{:S(2)}) copy-start(bf16[8,512,512]{2,1,0:T(8,128)(2,1)} %copy-done) | copy-start | bytes 12582916
  59.9 2.2 %copy-start.4 = (bf16[4096,512]{1,0:T(8,128)(2,1)S(1)}, bf16[4096,512]{1,0:T(8,128)(2,1)}, u32[]{:S(2)}) copy-start(bf16[4096,512]{1,0:T(8,128)(2,1)} %copy-done.3) | copy-start | bytes 12582916
  62.1 3.5 %copy-start.8 = (bf16[1024,512]{1,0:T(8,128)(2,1)S(1)}, bf16[1024,512]{1,0:T(8,128)(2,1)}, u32[]{:S(2)}) copy-start(bf16[1024,512]{1,0:T(8,128)(2,1)} %refs_2_.3) | copy-start | bytes 3145732
  62.1 4.9 %copy-start.11 = (bf16[512,512]{1,0:T(8,128)(2,1)S(1)}, bf16[512,512]{1,0:T(8,128)(2,1)}, u32[]{:S(2)}) copy-start(bf16[512,512]{1,0:T(8,128)(2,1)} %param.13) | copy-start | bytes 1572868
  66.9 4.5 %copy-start.2 = (bf16[8,512,512]{2,1,0:T(8,128)(2,1)S(1)}, bf16[8,512,512]{2,1,0:T(8,128)(2,1)}, u32[]{:S(2)}) copy-start(bf16[8,512,512]{2,1,0:T(8,128)(2,1)} %copy-done) | copy-start | bytes 12582916
  67.0 8.0 %collective-permute-start.8 = (bf16[512,256]{1,0:T(8,128)(2,1)S(1)}, bf16[512,256]{1,0:T(8,128)(2,1)S(1)}, u32[]{:S(2)}, u32[]{:S(2)}) collective-permute-start(bf16[512,256]{1,0:T(8,128)(2,1)S(1)} %get-tuple-element.135), channel_id=1, source_target_pairs={{0,1},{1,0},{2,3},{3,2},{4,5},{5,4},{6,7},{7,6},{8,9},{9,8},{10,11... | collective-permute-start | bytes 786440 | tf_op jit(solution)/shard_map/ppermute | solution.py:266
  67.1 9.6 %collective-permute-start.9 = (bf16[512,256]{1,0:T(8,128)(2,1)S(1)}, bf16[512,256]{1,0:T(8,128)(2,1)S(1)}, u32[]{:S(2)}, u32[]{:S(2)}) collective-permute-start(bf16[512,256]{1,0:T(8,128)(2,1)S(1)} %get-tuple-element.202), channel_id=1, source_target_pairs={{0,1},{1,0},{2,3},{3,2},{4,5},{5,4},{6,7},{7,6},{8,9},{9,8},{10,11... | collective-permute-start | bytes 786440 | tf_op jit(solution)/shard_map/ppermute | solution.py:266
  76.7 14.2 %collective-permute-start.14 = (bf16[1024,256]{1,0:T(8,128)(2,1)}, bf16[1024,256]{1,0:T(8,128)(2,1)S(1)}, u32[]{:S(2)}, u32[]{:S(2)}) collective-permute-start(bf16[1024,256]{1,0:T(8,128)(2,1)} %collective-permute-done.6.refs_2_), channel_id=1, source_target_pairs={{0,6},{2,0},{4,2},{6,4},{1,7},{3,1},{5,3},{7,5},{8,14},{10,8},{12,... | collective-permute-start | bytes 1572872 | tf_op jit(solution)/shard_map/ppermute | solution.py:272
  76.9 7.2 %collective-permute-start.15 = (bf16[2,128,256]{2,1,0:T(8,128)(2,1)S(1)}, bf16[2,128,256]{2,1,0:T(8,128)(2,1)S(1)}, u32[]{:S(2)}, u32[]{:S(2)}) collective-permute-start(bf16[2,128,256]{2,1,0:T(8,128)(2,1)S(1)} %get-tuple-element.152), channel_id=1, source_target_pairs={{0,8},{8,0},{16,24},{24,16},{1,9},{9,1},{17,25},{25,17},{2,10},{10... | collective-permute-start | bytes 393224 | tf_op jit(solution)/shard_map/ppermute | solution.py:269
  78.7 7.8 %collective-permute-start.16 = (bf16[2,128,256]{2,1,0:T(8,128)(2,1)S(1)}, bf16[2,128,256]{2,1,0:T(8,128)(2,1)S(1)}, u32[]{:S(2)}, u32[]{:S(2)}) collective-permute-start(bf16[2,128,256]{2,1,0:T(8,128)(2,1)S(1)} %get-tuple-element.153), channel_id=1, source_target_pairs={{0,16},{8,24},{16,0},{24,8},{1,17},{9,25},{17,1},{25,9},{2,18},{10... | collective-permute-start | bytes 393224 | tf_op jit(solution)/shard_map/ppermute | solution.py:269
  79.2 7.3 %collective-permute-start.17 = (bf16[2,128,256]{2,1,0:T(8,128)(2,1)S(1)}, bf16[2,128,256]{2,1,0:T(8,128)(2,1)S(1)}, u32[]{:S(2)}, u32[]{:S(2)}) collective-permute-start(bf16[2,128,256]{2,1,0:T(8,128)(2,1)S(1)} %get-tuple-element.154), channel_id=1, source_target_pairs={{0,24},{8,16},{16,8},{24,0},{1,25},{9,17},{17,9},{25,1},{2,26},{10... | collective-permute-start | bytes 393224 | tf_op jit(solution)/shard_map/ppermute | solution.py:269
  92.4 12.9 %collective-permute-start.18 = (bf16[1024,256]{1,0:T(8,128)(2,1)S(1)}, bf16[1024,256]{1,0:T(8,128)(2,1)S(1)}, u32[]{:S(2)}, u32[]{:S(2)}) collective-permute-start(bf16[1024,256]{1,0:T(8,128)(2,1)S(1)} %get-tuple-element.182), channel_id=1, source_target_pairs={{0,6},{2,0},{4,2},{6,4},{1,7},{3,1},{5,3},{7,5},{8,14},{10,8},{12,... | collective-permute-start | bytes 1572872 | tf_op jit(solution)/shard_map/ppermute | solution.py:272
  94.6 10.8 %collective-permute-start.20 = (bf16[128,1024]{1,0:T(8,128)(2,1)S(1)}, bf16[128,1024]{1,0:T(8,128)(2,1)S(1)}, u32[]{:S(2)}, u32[]{:S(2)}) collective-permute-start(bf16[128,1024]{1,0:T(8,128)(2,1)S(1)} %get-tuple-element.185), channel_id=1, source_target_pairs={{0,8},{8,0},{16,24},{24,16},{1,9},{9,1},{17,25},{25,17},{2,10},{10... | collective-permute-start | bytes 786440 | tf_op jit(solution)/shard_map/ppermute | solution.py:269
  96.1 9.4 %collective-permute-start.21 = (bf16[128,1024]{1,0:T(8,128)(2,1)S(1)}, bf16[128,1024]{1,0:T(8,128)(2,1)S(1)}, u32[]{:S(2)}, u32[]{:S(2)}) collective-permute-start(bf16[128,1024]{1,0:T(8,128)(2,1)S(1)} %get-tuple-element.186), channel_id=1, source_target_pairs={{0,16},{8,24},{16,0},{24,8},{1,17},{9,25},{17,1},{25,9},{2,18},{10... | collective-permute-start | bytes 786440 | tf_op jit(solution)/shard_map/ppermute | solution.py:269
  96.6 11.9 %collective-permute-start.22 = (bf16[128,1024]{1,0:T(8,128)(2,1)S(1)}, bf16[128,1024]{1,0:T(8,128)(2,1)S(1)}, u32[]{:S(2)}, u32[]{:S(2)}) collective-permute-start(bf16[128,1024]{1,0:T(8,128)(2,1)S(1)} %get-tuple-element.187), channel_id=1, source_target_pairs={{0,24},{8,16},{16,8},{24,0},{1,25},{9,17},{17,9},{25,1},{2,26},{10... | collective-permute-start | bytes 786440 | tf_op jit(solution)/shard_map/ppermute | solution.py:269
  98.1 10.5 %collective-permute-start.19 = (bf16[512,256]{1,0:T(8,128)(2,1)S(1)}, bf16[512,256]{1,0:T(8,128)(2,1)S(1)}, u32[]{:S(2)}, u32[]{:S(2)}) collective-permute-start(bf16[512,256]{1,0:T(8,128)(2,1)S(1)} %get-tuple-element.183), channel_id=1, source_target_pairs={{0,1},{1,0},{2,3},{3,2},{4,5},{5,4},{6,7},{7,6},{8,9},{9,8},{10,11... | collective-permute-start | bytes 786440 | tf_op jit(solution)/shard_map/ppermute | solution.py:266
  108.9 14.4 %collective-permute-start.23 = (bf16[1024,512]{1,0:T(8,128)(2,1)S(1)}, bf16[1024,512]{1,0:T(8,128)(2,1)S(1)}, u32[]{:S(2)}, u32[]{:S(2)}) collective-permute-start(bf16[1024,512]{1,0:T(8,128)(2,1)S(1)} %turn.3.refs_3_), channel_id=1, source_target_pairs={{0,1},{1,0},{2,3},{3,2},{4,5},{5,4},{6,7},{7,6},{8,9},{9,8},{10,11... | collective-permute-start | bytes 3145736 | tf_op jit(solution)/shard_map/ppermute | solution.py:266
  108.9 14.3 %collective-permute-start.24 = (bf16[1024,256]{1,0:T(8,128)(2,1)S(1)}, bf16[1024,256]{1,0:T(8,128)(2,1)S(1)}, u32[]{:S(2)}, u32[]{:S(2)}) collective-permute-start(bf16[1024,256]{1,0:T(8,128)(2,1)S(1)} %pass.1), channel_id=1, source_target_pairs={{0,6},{2,0},{4,2},{6,4},{1,7},{3,1},{5,3},{7,5},{8,14},{10,8},{12,... | collective-permute-start | bytes 1572872 | tf_op jit(solution)/shard_map/ppermute | solution.py:272
  126.1 6.4 %collective-permute-start.25 = (bf16[256,256]{1,0:T(8,128)(2,1)S(1)}, bf16[256,256]{1,0:T(8,128)(2,1)S(1)}, u32[]{:S(2)}, u32[]{:S(2)}) collective-permute-start(bf16[256,256]{1,0:T(8,128)(2,1)S(1)} %get-tuple-element.197), channel_id=1, source_target_pairs={{0,8},{8,0},{16,24},{24,16},{1,9},{9,1},{17,25},{25,17},{2,10},{10... | collective-permute-start | bytes 393224 | tf_op jit(solution)/shard_map/ppermute | solution.py:269
  126.9 7.8 %collective-permute-start.26 = (bf16[256,256]{1,0:T(8,128)(2,1)S(1)}, bf16[256,256]{1,0:T(8,128)(2,1)S(1)}, u32[]{:S(2)}, u32[]{:S(2)}) collective-permute-start(bf16[256,256]{1,0:T(8,128)(2,1)S(1)} %get-tuple-element.198), channel_id=1, source_target_pairs={{0,16},{8,24},{16,0},{24,8},{1,17},{9,25},{17,1},{25,9},{2,18},{10... | collective-permute-start | bytes 393224 | tf_op jit(solution)/shard_map/ppermute | solution.py:269
  128.5 6.1 %collective-permute-start.27 = (bf16[256,256]{1,0:T(8,128)(2,1)S(1)}, bf16[256,256]{1,0:T(8,128)(2,1)S(1)}, u32[]{:S(2)}, u32[]{:S(2)}) collective-permute-start(bf16[256,256]{1,0:T(8,128)(2,1)S(1)} %get-tuple-element.199), channel_id=1, source_target_pairs={{0,24},{8,16},{16,8},{24,0},{1,25},{9,17},{17,9},{25,1},{2,26},{10... | collective-permute-start | bytes 393224 | tf_op jit(solution)/shard_map/ppermute | solution.py:269
  134.7 5.0 %collective-permute-start.28 = (bf16[256,256]{1,0:T(8,128)(2,1)S(1)}, bf16[256,256]{1,0:T(8,128)(2,1)S(1)}, u32[]{:S(2)}, u32[]{:S(2)}) collective-permute-start(bf16[256,256]{1,0:T(8,128)(2,1)S(1)} %sum.3.refs_0_), channel_id=1, source_target_pairs={{0,2},{2,0},{4,6},{6,4},{1,3},{3,1},{5,7},{7,5},{8,10},{10,8},{12,... | collective-permute-start | bytes 393224 | tf_op jit(solution)/shard_map/ppermute | solution.py:443
  139.8 7.3 %collective-permute-start.29 = (bf16[256,256]{1,0:T(8,128)(2,1)S(1)}, bf16[256,256]{1,0:T(8,128)(2,1)S(1)}, u32[]{:S(2)}, u32[]{:S(2)}) collective-permute-start(bf16[256,256]{1,0:T(8,128)(2,1)S(1)} %sum.4.refs_0_), channel_id=1, source_target_pairs={{0,4},{2,6},{4,0},{6,2},{1,5},{3,7},{5,1},{7,3},{8,12},{10,14},{12... | collective-permute-start | bytes 393224 | tf_op jit(solution)/shard_map/ppermute | solution.py:443
  147.2 5.0 %collective-permute-start.30 = (bf16[256,256]{1,0:T(8,128)(2,1)S(1)}, bf16[256,256]{1,0:T(8,128)(2,1)S(1)}, u32[]{:S(2)}, u32[]{:S(2)}) collective-permute-start(bf16[256,256]{1,0:T(8,128)(2,1)S(1)} %sum.5.refs_1_), channel_id=1, source_target_pairs={{0,8},{8,0},{16,24},{24,16},{1,9},{9,1},{17,25},{25,17},{2,10},{10... | collective-permute-start | bytes 393224 | tf_op jit(solution)/shard_map/ppermute | solution.py:269
  148.5 5.0 %collective-permute-start.31 = (bf16[256,256]{1,0:T(8,128)(2,1)S(1)}, bf16[256,256]{1,0:T(8,128)(2,1)S(1)}, u32[]{:S(2)}, u32[]{:S(2)}) collective-permute-start(bf16[256,256]{1,0:T(8,128)(2,1)S(1)} %sum.5.refs_1_), channel_id=1, source_target_pairs={{0,16},{8,24},{16,0},{24,8},{1,17},{9,25},{17,1},{25,9},{2,18},{10... | collective-permute-start | bytes 393224 | tf_op jit(solution)/shard_map/ppermute | solution.py:269
  149.2 5.9 %collective-permute-start.32 = (bf16[256,256]{1,0:T(8,128)(2,1)S(1)}, bf16[256,256]{1,0:T(8,128)(2,1)S(1)}, u32[]{:S(2)}, u32[]{:S(2)}) collective-permute-start(bf16[256,256]{1,0:T(8,128)(2,1)S(1)} %sum.5.refs_1_), channel_id=1, source_target_pairs={{0,24},{8,16},{16,8},{24,0},{1,25},{9,17},{17,9},{25,1},{2,26},{10... | collective-permute-start | bytes 393224 | tf_op jit(solution)/shard_map/ppermute | solution.py:269
  150.7 5.2 %collective-permute-start.33 = (bf16[256,256]{1,0:T(8,128)(2,1)S(1)}, bf16[256,256]{1,0:T(8,128)(2,1)S(1)}, u32[]{:S(2)}, u32[]{:S(2)}) collective-permute-start(bf16[256,256]{1,0:T(8,128)(2,1)S(1)} %sum.5.refs_1_), channel_id=1, source_target_pairs={{0,1},{1,0},{2,3},{3,2},{4,5},{5,4},{6,7},{7,6},{8,9},{9,8},{10,11... | collective-permute-start | bytes 393224 | tf_op jit(solution)/shard_map/ppermute | solution.py:266
  152.2 3.7 %collective-permute-start.34 = (bf16[256,256]{1,0:T(8,128)(2,1)S(1)}, bf16[256,256]{1,0:T(8,128)(2,1)S(1)}, u32[]{:S(2)}, u32[]{:S(2)}) collective-permute-start(bf16[256,256]{1,0:T(8,128)(2,1)S(1)} %collective-permute-done.30.refs_2_), channel_id=1, source_target_pairs={{0,1},{1,0},{2,3},{3,2},{4,5},{5,4},{6,7},{7,6},{8,9},{9,8},{10,11... | collective-permute-start | bytes 393224 | tf_op jit(solution)/shard_map/ppermute | solution.py:266
  153.5 2.4 %collective-permute-start.35 = (bf16[256,256]{1,0:T(8,128)(2,1)S(1)}, bf16[256,256]{1,0:T(8,128)(2,1)S(1)}, u32[]{:S(2)}, u32[]{:S(2)}) collective-permute-start(bf16[256,256]{1,0:T(8,128)(2,1)S(1)} %collective-permute-done.31.refs_3_), channel_id=1, source_target_pairs={{0,1},{1,0},{2,3},{3,2},{4,5},{5,4},{6,7},{7,6},{8,9},{9,8},{10,11... | collective-permute-start | bytes 393224 | tf_op jit(solution)/shard_map/ppermute | solution.py:266
  155.0 1.3 collective-permute-start.36
  (3 other events, 3.1 us)

commit v8 on v7

--- a/solution.py
+++ b/solution.py
@@ -31,21 +31,35 @@
     return lax.dot_general(a, b, (((0,), (0,)), ((), ())), preferred_element_type=F32)
 
 
-def call(body, outs, ins, name, us, scratch=()):
+def call(body, outs, ins, name, us, scratch=(), after=(), token=False):
     smem = pl.BlockSpec(memory_space=pltpu.SMEM)
     vmem = pl.BlockSpec(memory_space=pltpu.VMEM)
+    count = len(ins)
+    ties = len(after)
+    if token:
+        outs = [*outs, ((8, 128), F32)]
+
+    def kernel(*refs):
+        refs = refs[:count] + refs[count + ties:]
+        if token:
+            at = count + len(outs) - 1
+            refs[at][...] = jnp.zeros((8, 128), F32)
+            refs = refs[:at] + refs[at + 1:]
+        body(*refs)
+
     arrays = [jax.ShapeDtypeStruct(s, d) for s, d in outs] + [value for _, value in ins]
     size = sum(a.size * a.dtype.itemsize for a in arrays + [m.get_array_aval() for m in scratch])
     return pl.pallas_call(
-        body,
+        kernel,
         out_shape=tuple(jax.ShapeDtypeStruct(s, d) for s, d in outs),
-        in_specs=[smem if where == "s" else vmem for where, _ in ins],
+        in_specs=[smem if where == "s" else vmem for where, _ in ins]
+        + [pl.BlockSpec(memory_space=pl.ANY)] * ties,
         out_specs=tuple(vmem for _ in outs),
         scratch_shapes=list(scratch),
         compiler_params=pltpu.CompilerParams(vmem_limit_bytes=size + (6 << 20)),
         cost_estimate=pl.CostEstimate(flops=int(us * 2e7), bytes_accessed=0, transcendentals=0),
         name=name,
-    )(*(value for _, value in ins))
+    )(*(value for _, value in ins), *after)
 
 
 class Sizes:
@@ -242,15 +256,15 @@
             out[pl.ds(at, share), pl.ds(left, half)] = pieces[rel * z.grp + s][...].astype(F32)
 
 
-def arrange(z, place, dense, wide):
+def arrange(z, place, dense, wide, after=()):
     inner = (wide, z.rows) if z.pair % 16 == 0 else (2 * z.grp, z.dom, z.pair, z.rows)
-    got = call(
+    *got, token = call(
         lambda *refs: arrange_kernel(z, *refs),
         [(inner, BF16)] * z.zz,
         [("v", place), ("v", dense)],
-        "arrange", 4,
-    )
-    return [part.reshape(wide, z.rows) for part in got]
+        "arrange", 4, after=after, token=True,
+    )
+    return [part.reshape(wide, z.rows) for part in got], token
 
 
 def shards(features, node_order, block_cols, block_count, block_vals, weight, cotangent):
@@ -284,12 +298,12 @@
     )
     vals_b = to_core(block_vals)
 
-    def products_of(part):
+    def products_of(part, after=()):
         own, other = call(
             lambda *refs: product_kernel(z, *refs),
             [((rows, half), BF16)] * 2,
             [("s", me), ("v", part), ("v", weight)],
-            "product", 1.5,
+            "product", 75, after=after,
         )
         return own, to_core(other)
 
@@ -298,38 +312,39 @@
             lambda *refs: send_kernel(z, lines, *refs),
             [((rows, rows), BF16)] + [((2, z.per_grp, half), BF16)] * z.grp,
             [("s", me), ("v", message)] + [("v", part) for part in products],
-            "send", 1.5,
+            "send", 1.5, token=True,
         )
 
     def across(parts):
         return [to_grp(part, s) for s, part in enumerate(parts)]
 
-    def pack(parts):
+    def pack(parts, after=()):
         return call(
             lambda *refs: pack_kernel(z, *refs),
             [((2 * rows, half), BF16)],
             [("v", part) for part in parts],
-            "pack", 0.5,
+            "pack", 0.5, after=after,
         )[0]
 
-    def rows_of(pick, part):
+    def rows_of(pick, part, after):
         return call(
             lambda *refs: rows_kernel(z, *refs),
             [((z.per_grp, width_in), BF16)] * z.grp,
             [("v", pick), ("v", part)],
-            "rows", 1,
+            "rows", 1, after=after,
         )
 
     def turned_of(parts):
-        (left,) = call(
-            turn_kernel, [((width_in, rows), BF16)], [("v", part) for part in parts], "turn", 0.5
-        )
-        return [left, to_core(left)]
+        left, token = call(
+            turn_kernel, [((width_in, rows), BF16)], [("v", part) for part in parts],
+            "turn", 0.5, token=True,
+        )
+        return [left, to_core(left)], token
 
     products = products_of(features)
-    pick, *got = send_of((0, 5), products)
-    got, message, cotangent, block_cols, vals_b, late = lax.optimization_barrier(
-        (got, message, cotangent, block_cols, vals_b, features)
+    pick, *got, token = send_of((0, 5), products)
+    token, cotangent, block_cols, late = lax.optimization_barrier(
+        (token, cotangent, block_cols, features)
     )
     came = across(got)
 
@@ -345,45 +360,40 @@
         lambda *refs: place_kernel(z, *refs),
         [((z.dom, rows, rows), BF16)],
         [("s", me), ("v", message)],
-        "place", 1.5,
-    )
-
-    def dense_of(cols, vals):
+        "place", 1.5, after=[token],
+    )
+
+    def dense_of(cols, vals, after=()):
         return call(
             dense_kernel,
             [((z.dom * rows, rows), BF16)],
             [("s", cols), ("v", vals)],
             "dense", 2.5,
-            (pltpu.VMEM((z.dom * rows + tile, tile), F32),),
+            (pltpu.VMEM((z.dom * rows + tile, tile), F32),), after=after,
         )[0]
 
-    dense_a = dense_of(cols_a, block_vals)
-    came, dense_a, place, cols_b = lax.optimization_barrier((came, dense_a, place, cols_b))
+    dense_a = dense_of(cols_a, block_vals, [vals_b])
 
     wide = 2 * z.grp * z.per_grp
-    turned = [arrange(z, place, dense_a, wide), arrange(z, place, dense_of(cols_b, vals_b), wide)]
-    ring = {0: pack(came)}
-    lefts = turned_of(across(rows_of(pick, features)))
-    near, turned[0][0] = lax.optimization_barrier((near, turned[0][0]))
+    ring = {0: pack(came, [place, dense_a, cols_b])}
+    turned_a, _ = arrange(z, place, dense_a, wide, [ring[0]])
+    turned_b, token_b = arrange(z, place, dense_of(cols_b, vals_b, [ring[0]]), wide)
+    turned = (turned_a, turned_b)
+    lefts, token_l = turned_of(across(rows_of(pick, features, [ring[0]])))
+    pick_near, *got, token_n = send_of((6, 7), products_of(near, [turned_a[0]]))
     order = list(range(z.zz - 1, 1, -1))
     for k in order:
         ring[k] = to_zz(ring[(k + 1) % z.zz], -1)
         if k == order[0]:
-            pick_near, *got = send_of((6, 7), products_of(near))
-            ring[k], turned, got, cot_a, cot_b, lefts = lax.optimization_barrier(
-                (ring[k], turned, got, cot_a, cot_b, lefts)
-            )
-            came = across(got)
-    came, pick_near = lax.optimization_barrier((came, pick_near))
+            ring[k], *tokens = lax.optimization_barrier((ring[k], token_b, token_l, token_n))
+    came = across(got)
     ring[1] = pack(came)
-    held_near = rows_of(pick_near, near)
+    held_near = rows_of(pick_near, near, came[1:])
 
     agg = []
     order = [0] + order[:-1] + [1] + order[-1:]
     for k in order:
         last = k == order[-1]
-        if last:
-            agg, held_near = lax.optimization_barrier((agg, held_near))
         ins = [("v", part) for part in (turned[0][k], turned[1][k], ring[k], *agg)]
         outs = [((rows, half), F32)] * 2
         if last:
@@ -393,6 +403,7 @@
         agg = call(
             lambda *refs, k=k, last=last: forward_kernel(z, k == 0, last, *refs),
             outs, ins, "forward", 3 if last else 1,
+            after=held_near if last else [cot_a, cot_b, *tokens] if k == order[1] else (),
         )
     hidden_a, hidden_b, grad_a, grad_b, came = agg
 
@@ -412,11 +423,10 @@
         if k == 1:
             break
         (came,) = call(
-            pass_kernel, [((wide, half), BF16)], [("v", mine), ("v", came)], "pass", 0.5
-        )
-        if k == z.zz - 2:
-            came, come, held_near = lax.optimization_barrier((came, come, held_near))
-    lefts += turned_of(held_near)
+            pass_kernel, [((wide, half), BF16)], [("v", mine), ("v", came)], "pass", 0.5,
+            after=[come, *held_near],
+        )
+    lefts += turned_of(held_near)[0]
     first = core == 0
     hidden = jnp.concatenate(
         [jnp.where(first, hidden_a, come), jnp.where(first, come, hidden_a)], axis=1

time: 159 us -> 151 us (0.950)
  waiting for transfers between devices: 57.1 us -> 52.1 us
  Pallas kernels: 38.7 us -> 34.6 us
    ppermute x18, waiting for transfers between devices: 25.3 us -> 17.4 us  [to_grp(): lax.ppermute(x, 'grp', [(i, i ^ s) for i in range(z.grp)])]
    pallas_call x29, Pallas kernels: 38.7 us -> 34.6 us  [call(): pl.pallas_call(kernel, out_shape=tuple((jax.ShapeDtypeStruct(s, d) for s,...]
    ppermute x5, waiting for transfers between devices: 21.1 us -> 24.7 us  [to_zz(): lax.ppermute(x, 'zz', [(i, (i + k) % z.zz) for i in range(z.zz)])]
    ppermute x2, starting transfers between devices: 2.17 us -> 4.78 us  [shards(): lax.ppermute(mine, 'zz', [(i, i ^ step) for i in range(z.zz)])]
    ppermute x2, waiting for transfers between devices: 10.2 us -> 7.67 us  [shards(): lax.ppermute(mine, 'zz', [(i, i ^ step) for i in range(z.zz)])]
    ppermute x12, waiting for transfers between devices: 0.49 us -> 2.3 us  [to_core(): return lax.ppermute(x, 'core', [(0, 1), (1, 0)])]
    unnamed x28 -> x58, local copies, waits for them, and re-layouts: 12.8 us -> 11.3 us
  transfers between devices with their start and end apart: 37 -> 37, of which waited for: 15 -> 17; matrix products, arithmetic and copies ran while one was open for 1% -> 1% of each run, Pallas kernels for 18% -> 18%
where the time goes in v8:
time: 151 us; the launch traced here: 150 us
  waiting for transfers between devices  52.1 us (35%)
  Pallas kernels  34.6 us (23%)
  starting transfers between devices  33.6 us (22%)
  blocking collectives  15.3 us (10%)
  local copies, waits for them, and re-layouts  12.4 us (8%)
    pallas_call x29, Pallas kernels, call(): pl.pallas_call(kernel, out_shape=tuple((jax.ShapeDtypeStruct(s, d) for s,...  34.6 us
    ppermute x5, waiting for transfers between devices, to_zz(): lax.ppermute(x, 'zz', [(i, (i + k) % z.zz) for i in range(z.zz)])  24.7 us
    ppermute x18, starting transfers between devices, to_grp(): lax.ppermute(x, 'grp', [(i, i ^ s) for i in range(z.grp)])  21.2 us
    ppermute x18, waiting for transfers between devices, to_grp(): lax.ppermute(x, 'grp', [(i, i ^ s) for i in range(z.grp)])  17.4 us
    all_to_all x1, blocking collectives, shards(): lax.all_to_all(message, ('grp', 'zz', 'core'), split_axis=0, concat_axis=...  15.3 us
    unnamed x58, local copies, waits for them, and re-layouts  11.3 us
    ppermute x2, waiting for transfers between devices, shards(): lax.ppermute(mine, 'zz', [(i, i ^ step) for i in range(z.zz)])  7.67 us
    ppermute x5, starting transfers between devices, to_zz(): lax.ppermute(x, 'zz', [(i, (i + k) % z.zz) for i in range(z.zz)])  6.12 us
  transfers between devices with their start and end apart: 37, of which 17 were waited for; matrix products, arithmetic and copies ran while one was open for 1% of the time, Pallas kernels for 18%

profile of v8, /device:TPU:0, one launch (start us, length us, event | category | flops | bytes accessed | tf_op | source)
XLA Modules:
  0.0 150.1 jit_solution(2268226948056165819)
XLA Ops:
  1.9 1.1 index.1
  3.0 1.2 copy-done.15
  4.3 1.2 copy-done.24
  5.5 1.2 product.2
  6.9 15.3 %all_to_all.5.refs_1_ = s32[32,8,128]{2,1,0:T(8,128)S(1)} all-to-all(s32[32,8,128]{2,1,0:T(8,128)S(1)} %index.1), channel_id=1, replica_groups=mesh['grp'=4,'zz'=4,'core'=2] {'grp','zz','core'}, dimensions={0} | all-to-all | bytes 262144 | tf_op jit(solution)/shard_map/all_to_all | solution.py:296
  22.2 1.7 %send.2 = (bf16[512,512]{1,0:T(8,128)(2,1)S(1)}, bf16[2,128,256]{2,1,0:T(8,128)(2,1)S(1)}, bf16[2,128,256]{2,1,0:T(8,128)(2,1)S(1)}, bf16[2,128,256]{2,1,0:T(8,1...) custom-call(s32[3]{0:T(128)S(1)} %pad_add_fusion.refs_0_, s32[32,8,128]{2,1,0:T(8,128)S(1)} %all_to_all.5.refs_1_, ...), custom_call_target="tpu_custom_call" | custom-call | flops 30000000 | tf_op jit(solution)/shard_map/send/pallas_call | solution.py:52
  25.7 2.3 %collective-permute-start.4 = (bf16[2,128,256]{2,1,0:T(8,128)(2,1)S(1)}, bf16[2,128,256]{2,1,0:T(8,128)(2,1)S(1)}, u32[]{:S(2)}, u32[]{:S(2)}) collective-permute-start(bf16[2,128,256]{2,1,0:T(8,128)(2,1)S(1)} %get-tuple-element.73), channel_id=1, source_target_pairs={{0,24},{8,16},{16,8},{24,0},{1,25},{9,17},{17,9},{25,1},{2,26},{10... | collective-permute-start | bytes 393224 | tf_op jit(solution)/shard_map/ppermute | solution.py:283
  28.0 1.4 place.1.refs_4_.refs_0_
  29.5 2.4 %dense.2.refs_5_.refs_1_ = bf16[4096,512]{1,0:T(8,128)(2,1)S(1)} custom-call(s32[4,16]{1,0:T(4,128)S(1)} %fusion.refs_0_, bf16[4,16,128,128]{3,2,1,0:T(8,128)(2,1)S(1)} %copy-done.14, bf16[4,16,128,128]{3,2,1,0:T(8,128)(2,1)S(1)} %collective-permute-done.1.refs_2_.refs_1_), custom_call_target="tpu_custom_call" | custom-call | flops 50000000 | tf_op jit(solution)/shard_map/dense/pallas_call | solution.py:52
  33.0 3.3 %collective-permute-start.6 = (bf16[1024,256]{1,0:T(8,128)(2,1)S(1)}, bf16[1024,256]{1,0:T(8,128)(2,1)}, u32[]{:S(2)}, u32[]{:S(2)}) collective-permute-start(bf16[1024,256]{1,0:T(8,128)(2,1)S(1)} %pack.2.refs_2_), channel_id=1, source_target_pairs={{0,6},{2,0},{4,2},{6,4},{1,7},{3,1},{5,3},{7,5},{8,14},{10,8},{12,... | collective-permute-start | bytes 1572872 | tf_op jit(solution)/shard_map/ppermute | solution.py:286
  37.0 1.6 %collective-permute-start.7 = (bf16[128,1024]{1,0:T(8,128)(2,1)S(1)}, bf16[128,1024]{1,0:T(8,128)(2,1)S(1)}, u32[]{:S(2)}, u32[]{:S(2)}) collective-permute-start(bf16[128,1024]{1,0:T(8,128)(2,1)S(1)} %get-tuple-element.79), channel_id=1, source_target_pairs={{0,8},{8,0},{16,24},{24,16},{1,9},{9,1},{17,25},{25,17},{2,10},{10... | collective-permute-start | bytes 786440 | tf_op jit(solution)/shard_map/ppermute | solution.py:283
  39.3 1.3 collective-permute-start.9
  40.6 4.1 %arrange.2 = (bf16[1024,512]{1,0:T(8,128)(2,1)S(1)}, bf16[1024,512]{1,0:T(8,128)(2,1)S(1)}, bf16[1024,512]{1,0:T(8,128)(2,1)S(1)}, bf16[1024,512]{1,0:T(8,128)(2,1)S(1)}, f32[8,128]{1,0:T(8,128)}) custom-call(bf16[8,512,512]{2,1,0:T(8,128)(2,1)S(1)} %place.1.refs_4_.refs_0_, bf16[4096,512]{1,0:T(8,128)(2,1)S(1)} %dense.2.refs_5_.refs_1_, ...), custom_call_target="tpu_custom_call" | custom-call | flops 80000000 | tf_op jit(solution)/shard_map/arrange/pallas_call | solution.py:52
  44.7 7.1 %collective-permute-done.10.refs_1_ = bf16[512,1024]{1,0:T(8,128)(2,1)S(1)} collective-permute-done((bf16[512,1024]{1,0:T(8,128)(2,1)S(1)}, bf16[512,1024]{1,0:T(8,128)(2,1)S(1)}, u32[]{:S(2)}, u32[]{:S(2)}) %collective-permute-start.10) | collective-permute-done | bytes 1048608 | tf_op jit(solution)/shard_map/ppermute | solution.py:286
  51.7 1.3 product.3
  53.1 2.4 %dense.3.refs_1_ = bf16[4096,512]{1,0:T(8,128)(2,1)S(1)} custom-call(s32[4,16]{1,0:T(4,128)S(1)} %collective-permute-done.5.refs_6_.refs_0_, bf16[4,16,128,128]{3,2,1,0:T(8,128)(2,1)S(1)} %collective-permute-done.1.refs_2_.refs_1_, bf16[1024,256]{1,0:T(8,128)(2,1)S(1)} %pack.2.refs_2_), custom_call_target="tpu_custom_call" | custom-call | flops 50000000 | tf_op jit(solution)/shard_map/dense/pallas_call | solution.py:52
  55.5 3.5 %arrange.3 = (bf16[1024,512]{1,0:T(8,128)(2,1)S(1)}, bf16[1024,512]{1,0:T(8,128)(2,1)S(1)}, bf16[1024,512]{1,0:T(8,128)(2,1)S(1)}, bf16[1024,512]{1,0:T(8,128)(2,1)S(1)}, f32[8,128]{1,0:T(8,128)S(1)}) custom-call(bf16[8,512,512]{2,1,0:T(8,128)(2,1)S(1)} %place.1.refs_4_.refs_0_, bf16[4096,512]{1,0:T(8,128)(2,1)S(1)} %dense.3.refs_1_), custom_call_target="tpu_custom_call" | custom-call | flops 80000000 | tf_op jit(solution)/shard_map/arrange/pallas_call | solution.py:52
  61.4 1.7 %send.3 = (bf16[512,512]{1,0:T(8,128)(2,1)S(1)}, bf16[2,128,256]{2,1,0:T(8,128)(2,1)S(1)}, bf16[2,128,256]{2,1,0:T(8,128)(2,1)S(1)}, bf16[2,128,256]{2,1,0:T(8,1...) custom-call(s32[3]{0:T(128)S(1)} %pad_add_fusion.refs_0_, s32[32,8,128]{2,1,0:T(8,128)S(1)} %all_to_all.5.refs_1_, ...), custom_call_target="tpu_custom_call" | custom-call | flops 30000000 | tf_op jit(solution)/shard_map/send/pallas_call | solution.py:52
  66.2 1.9 %collective-permute-start.15 = (bf16[2,128,256]{2,1,0:T(8,128)(2,1)S(1)}, bf16[2,128,256]{2,1,0:T(8,128)(2,1)S(1)}, u32[]{:S(2)}, u32[]{:S(2)}) collective-permute-start(bf16[2,128,256]{2,1,0:T(8,128)(2,1)S(1)} %get-tuple-element.94), channel_id=1, source_target_pairs={{0,24},{8,16},{16,8},{24,0},{1,25},{9,17},{17,9},{25,1},{2,26},{10... | collective-permute-start | bytes 393224 | tf_op jit(solution)/shard_map/ppermute | solution.py:283
  69.2 1.9 %collective-permute-done.13.refs_1_.refs_2_ = bf16[2,128,256]{2,1,0:T(8,128)(2,1)S(1)} collective-permute-done((bf16[2,128,256]{2,1,0:T(8,128)(2,1)}, bf16[2,128,256]{2,1,0:T(8,128)(2,1)S(1)}, u32[]{:S(2)}, u32[]{:S(2)}) %collective-permute-start.13) | collective-permute-done | bytes 131104 | tf_op jit(solution)/shard_map/ppermute | solution.py:283
  71.1 2.8 %collective-permute-done.14.refs_2_.refs_3_ = bf16[2,128,256]{2,1,0:T(8,128)(2,1)S(1)} collective-permute-done((bf16[2,128,256]{2,1,0:T(8,128)(2,1)S(1)}, bf16[2,128,256]{2,1,0:T(8,128)(2,1)S(1)}, u32[]{:S(2)}, u32[]{:S(2)}) %collective-permute-start.14) | collective-permute-done | bytes 131104 | tf_op jit(solution)/shard_map/ppermute | solution.py:283
  74.0 1.2 copy-done.18
  77.0 1.2 collective-permute-start.19
  79.0 1.5 %collective-permute-start.21 = (bf16[128,1024]{1,0:T(8,128)(2,1)S(1)}, bf16[128,1024]{1,0:T(8,128)(2,1)S(1)}, u32[]{:S(2)}, u32[]{:S(2)}) collective-permute-start(bf16[128,1024]{1,0:T(8,128)(2,1)S(1)} %get-tuple-element.112.refs_12_), channel_id=1, source_target_pairs={{0,24},{8,16},{16,8},{24,0},{1,25},{9,17},{17,9},{25,1},{2,26},{10... | collective-permute-start | bytes 786440 | tf_op jit(solution)/shard_map/ppermute | solution.py:283
  80.5 1.2 copy-done.9
  81.7 1.2 copy-done.12
  83.9 1.9 %forward.5 = (f32[512,256]{1,0:T(8,128)S(1)}, f32[512,256]{1,0:T(8,128)S(1)}) custom-call(bf16[1024,512]{1,0:T(8,128)(2,1)S(1)} %copy-done.5, bf16[1024,512]{1,0:T(8,128)(2,1)S(1)} %copy-done.7, bf16[1024,256]{1,0:T(8,128)(2,1)} %collective-permute-done.6.refs_2_, f32[512,256]{1,0:T(8,128)S(1)} %get-tuple-element.98.refs_3_, ...), custom_call_target="tpu_custom_call" | custom-call | flops 20000000 | tf_op jit(solution)/shard_map/forward/pallas_call | solution.py:52
  86.6 1.6 %forward.7 = (bf16[512,256]{1,0:T(8,128)(2,1)S(1)}, bf16[512,256]{1,0:T(8,128)(2,1)S(1)}, bf16[512,256]{1,0:T(8,128)(2,1)S(1)}, bf16[512,256]{1,0:T(8,128)(2,1)S(1)}, bf16[1024,256]{1,0:T(8,128)(2,1)S(1)}) custom-call(bf16[1024,512]{1,0:T(8,128)(2,1)S(1)} %copy-done.3, bf16[1024,512]{1,0:T(8,128)(2,1)S(1)} %get-tuple-element.75.refs_1_, ...), custom_call_target="tpu_custom_call" | custom-call | flops 60000000 | tf_op jit(solution)/shard_map/forward/pallas_call | solution.py:52
  88.3 1.5 collective-permute-done.20.refs_2_.refs_5_
  89.8 1.2 collective-permute-done.21.refs_3_.refs_6_
  93.1 1.8 %collective-permute-done.17.refs_2_ = bf16[512,256]{1,0:T(8,128)(2,1)S(1)} collective-permute-done((bf16[512,256]{1,0:T(8,128)(2,1)S(1)}, bf16[512,256]{1,0:T(8,128)(2,1)S(1)}, u32[]{:S(2)}, u32[]{:S(2)}) %collective-permute-start.17) | collective-permute-done | bytes 262176 | tf_op jit(solution)/shard_map/ppermute | solution.py:280
  94.9 7.6 %collective-permute-done.23.refs_1_ = bf16[1024,256]{1,0:T(8,128)(2,1)S(1)} collective-permute-done((bf16[1024,256]{1,0:T(8,128)(2,1)S(1)}, bf16[1024,256]{1,0:T(8,128)(2,1)S(1)}, u32[]{:S(2)}, u32[]{:S(2)}) %collective-permute-start.23) | collective-permute-done | bytes 524320 | tf_op jit(solution)/shard_map/ppermute | solution.py:286
  102.6 2.1 %collective-permute-start.24 = (bf16[1024,256]{1,0:T(8,128)(2,1)S(1)}, bf16[1024,256]{1,0:T(8,128)(2,1)S(1)}, u32[]{:S(2)}, u32[]{:S(2)}) collective-permute-start(bf16[1024,256]{1,0:T(8,128)(2,1)S(1)} %pass.1), channel_id=1, source_target_pairs={{0,6},{2,0},{4,2},{6,4},{1,7},{3,1},{5,3},{7,5},{8,14},{10,8},{12,... | collective-permute-start | bytes 1572872 | tf_op jit(solution)/shard_map/ppermute | solution.py:286
  106.2 9.9 %collective-permute-done.24.refs_7_ = bf16[1024,256]{1,0:T(8,128)(2,1)S(1)} collective-permute-done((bf16[1024,256]{1,0:T(8,128)(2,1)S(1)}, bf16[1024,256]{1,0:T(8,128)(2,1)S(1)}, u32[]{:S(2)}, u32[]{:S(2)}) %collective-permute-start.24) | collective-permute-done | bytes 524320 | tf_op jit(solution)/shard_map/ppermute | solution.py:286
  116.2 1.8 %grad.1 = (bf16[256,256]{1,0:T(8,128)(2,1)S(1)}, bf16[256,256]{1,0:T(8,128)(2,1)S(1)}, bf16[256,256]{1,0:T(8,128)(2,1)S(1)}, bf16[256,256]{1,0:T(8,128)(2,1)S(1)}) custom-call(s32[3]{0:T(128)S(1)} %pad_add_fusion.refs_0_, bf16[1024,512]{1,0:T(8,128)(2,1)S(1)} %copy-done.20, bf16[1024,512]{1,0:T(8,128)(2,1)S(1)} %collective-permute-done.18.refs_2_, ...), custom_call_target="tpu_custom_call" | custom-call | flops 30000000 | tf_op jit(solution)/shard_map/grad/pallas_call | solution.py:52
  118.0 1.2 collective-permute-start.25
  120.0 1.5 %collective-permute-start.27 = (bf16[256,256]{1,0:T(8,128)(2,1)S(1)}, bf16[256,256]{1,0:T(8,128)(2,1)S(1)}, u32[]{:S(2)}, u32[]{:S(2)}) collective-permute-start(bf16[256,256]{1,0:T(8,128)(2,1)S(1)} %get-tuple-element.123), channel_id=1, source_target_pairs={{0,24},{8,16},{16,8},{24,0},{1,25},{9,17},{17,9},{25,1},{2,26},{10... | collective-permute-start | bytes 393224 | tf_op jit(solution)/shard_map/ppermute | solution.py:283
  121.5 2.7 %collective-permute-done.25.refs_1_ = bf16[256,256]{1,0:T(8,128)(2,1)S(1)} collective-permute-done((bf16[256,256]{1,0:T(8,128)(2,1)S(1)}, bf16[256,256]{1,0:T(8,128)(2,1)S(1)}, u32[]{:S(2)}, u32[]{:S(2)}) %collective-permute-start.25) | collective-permute-done | bytes 131104 | tf_op jit(solution)/shard_map/ppermute | solution.py:283
  124.2 2.1 %collective-permute-done.26.refs_2_ = bf16[256,256]{1,0:T(8,128)(2,1)S(1)} collective-permute-done((bf16[256,256]{1,0:T(8,128)(2,1)S(1)}, bf16[256,256]{1,0:T(8,128)(2,1)S(1)}, u32[]{:S(2)}, u32[]{:S(2)}) %collective-permute-start.26) | collective-permute-done | bytes 131104 | tf_op jit(solution)/shard_map/ppermute | solution.py:283
  126.4 1.7 %collective-permute-start.28 = (bf16[256,256]{1,0:T(8,128)(2,1)S(1)}, bf16[256,256]{1,0:T(8,128)(2,1)S(1)}, u32[]{:S(2)}, u32[]{:S(2)}) collective-permute-start(bf16[256,256]{1,0:T(8,128)(2,1)S(1)} %sum.3.refs_0_), channel_id=1, source_target_pairs={{0,2},{2,0},{4,6},{6,4},{1,3},{3,1},{5,7},{7,5},{8,10},{10,8},{12,... | collective-permute-start | bytes 393224 | tf_op jit(solution)/shard_map/ppermute | solution.py:453
  128.1 3.3 %collective-permute-done.28.refs_1_ = bf16[256,256]{1,0:T(8,128)(2,1)S(1)} collective-permute-done((bf16[256,256]{1,0:T(8,128)(2,1)S(1)}, bf16[256,256]{1,0:T(8,128)(2,1)S(1)}, u32[]{:S(2)}, u32[]{:S(2)}) %collective-permute-start.28) | collective-permute-done | bytes 131104 | tf_op jit(solution)/shard_map/ppermute | solution.py:453
  131.4 3.1 %collective-permute-start.29 = (bf16[256,256]{1,0:T(8,128)(2,1)S(1)}, bf16[256,256]{1,0:T(8,128)(2,1)S(1)}, u32[]{:S(2)}, u32[]{:S(2)}) collective-permute-start(bf16[256,256]{1,0:T(8,128)(2,1)S(1)} %sum.4.refs_0_), channel_id=1, source_target_pairs={{0,4},{2,6},{4,0},{6,2},{1,5},{3,7},{5,1},{7,3},{8,12},{10,14},{12... | collective-permute-start | bytes 393224 | tf_op jit(solution)/shard_map/ppermute | solution.py:453
  134.5 4.4 %collective-permute-done.29.refs_1_ = bf16[256,256]{1,0:T(8,128)(2,1)S(1)} collective-permute-done((bf16[256,256]{1,0:T(8,128)(2,1)S(1)}, bf16[256,256]{1,0:T(8,128)(2,1)S(1)}, u32[]{:S(2)}, u32[]{:S(2)}) %collective-permute-start.29) | collective-permute-done | bytes 131104 | tf_op jit(solution)/shard_map/ppermute | solution.py:453
  139.0 1.9 %collective-permute-start.31 = (bf16[256,256]{1,0:T(8,128)(2,1)S(1)}, bf16[256,256]{1,0:T(8,128)(2,1)S(1)}, u32[]{:S(2)}, u32[]{:S(2)}) collective-permute-start(bf16[256,256]{1,0:T(8,128)(2,1)S(1)} %sum.5.refs_1_), channel_id=1, source_target_pairs={{0,16},{8,24},{16,0},{24,8},{1,17},{9,25},{17,1},{25,9},{2,18},{10... | collective-permute-start | bytes 393224 | tf_op jit(solution)/shard_map/ppermute | solution.py:283
  140.9 1.6 %collective-permute-start.32 = (bf16[256,256]{1,0:T(8,128)(2,1)S(1)}, bf16[256,256]{1,0:T(8,128)(2,1)S(1)}, u32[]{:S(2)}, u32[]{:S(2)}) collective-permute-start(bf16[256,256]{1,0:T(8,128)(2,1)S(1)} %sum.5.refs_1_), channel_id=1, source_target_pairs={{0,24},{8,16},{16,8},{24,0},{1,25},{9,17},{17,9},{25,1},{2,26},{10... | collective-permute-start | bytes 393224 | tf_op jit(solution)/shard_map/ppermute | solution.py:283
  142.4 1.5 collective-permute-done.30.refs_2_
  144.8 1.9 %collective-permute-done.32.refs_4_ = bf16[256,256]{1,0:T(8,128)(2,1)S(1)} collective-permute-done((bf16[256,256]{1,0:T(8,128)(2,1)S(1)}, bf16[256,256]{1,0:T(8,128)(2,1)S(1)}, u32[]{:S(2)}, u32[]{:S(2)}) %collective-permute-start.32) | collective-permute-done | bytes 131104 | tf_op jit(solution)/shard_map/ppermute | solution.py:283
  148.1 2.0 %last.1 = f32[1024,512]{1,0:T(8,128)} custom-call(s32[3]{0:T(128)S(1)} %pad_add_fusion.refs_0_, bf16[256,256]{1,0:T(8,128)(2,1)S(1)} %sum.5.refs_1_, bf16[256,256]{1,0:T(8,128)(2,1)S(1)} %collective-permute-done.30.refs_2_, bf16[256,256]{1,0:T(8,128)(2,1)S(1)} %collective-permute-done.31.refs_3_, bf16[256,256]{1,0:T(8,128)(2,1)S(1)} %collective-permute-done.32.refs_4_, ...), custom_call_target="tpu_custom_call" | custom-call | flops 40000000 | tf_op jit(solution)/shard_map/last/pallas_call | solution.py:52
  (119 shorter events, 23.5 us)
Async XLA Ops:
  0.6 28.9 %collective-permute-start.1 = (bf16[4,16,128,128]{3,2,1,0:T(8,128)(2,1)}, bf16[4,16,128,128]{3,2,1,0:T(8,128)(2,1)S(1)}, u32[]{:S(2)}, u32[]{:S(2)}) collective-permute-start(bf16[4,16,128,128]{3,2,1,0:T(8,128)(2,1)} %refs_1_.2), channel_id=1, source_target_pairs={{0,1},{1,0},{2,3},{3,2},{4,5},{5,4},{6,7},{7,6},{8,9},{9,8},{10,11... | collective-permute-start | bytes 6291464 | tf_op jit(solution)/shard_map/ppermute | solution.py:280
  5.5 18.4 %copy-start.16 = (bf16[512,1024]{1,0:T(8,128)(2,1)S(1)}, bf16[512,1024]{1,0:T(8,128)(2,1)}, u32[]{:S(2)}) copy-start(bf16[512,1024]{1,0:T(8,128)(2,1)} %refs_1_.3) | copy-start | bytes 3145732
  5.5 23.9 %copy-start.27 = (s32[4,16]{1,0:T(4,128)S(1)}, s32[4,16]{1,0:T(4,128)}, u32[]{:S(2)}) copy-start(s32[4,16]{1,0:T(4,128)} %param.9) | copy-start | bytes 772
  5.5 23.9 %copy-start.28 = (s32[4]{0:T(128)S(1)}, s32[4]{0:T(128)}, u32[]{:S(2)}) copy-start(s32[4]{0:T(128)} %param.10) | copy-start | bytes 52
  5.5 24.0 %copy-start.14 = (bf16[4,16,128,128]{3,2,1,0:T(8,128)(2,1)S(1)}, bf16[4,16,128,128]{3,2,1,0:T(8,128)(2,1)}, u32[]{:S(2)}) copy-start(bf16[4,16,128,128]{3,2,1,0:T(8,128)(2,1)} %refs_1_.2) | copy-start | bytes 6291460
  6.8 15.4 %collective-permute-start = (bf16[512,256]{1,0:T(8,128)(2,1)S(1)}, bf16[512,256]{1,0:T(8,128)(2,1)S(1)}, u32[]{:S(2)}, u32[]{:S(2)}) collective-permute-start(bf16[512,256]{1,0:T(8,128)(2,1)S(1)} %get-tuple-element.66), channel_id=1, source_target_pairs={{0,1},{1,0},{2,3},{3,2},{4,5},{5,4},{6,7},{7,6},{8,9},{9,8},{10,11... | collective-permute-start | bytes 786440 | tf_op jit(solution)/shard_map/ppermute | solution.py:280
  23.8 27.9 %collective-permute-start.10 = (bf16[512,1024]{1,0:T(8,128)(2,1)S(1)}, bf16[512,1024]{1,0:T(8,128)(2,1)S(1)}, u32[]{:S(2)}, u32[]{:S(2)}) collective-permute-start(bf16[512,1024]{1,0:T(8,128)(2,1)S(1)} %copy-done.16), channel_id=1, source_target_pairs={{0,2},{2,4},{4,6},{6,0},{1,3},{3,5},{5,7},{7,1},{8,10},{10,12},{12... | collective-permute-start | bytes 3145736 | tf_op jit(solution)/shard_map/ppermute | solution.py:286
  24.5 7.5 %collective-permute-start.2 = (bf16[2,128,256]{2,1,0:T(8,128)(2,1)S(1)}, bf16[2,128,256]{2,1,0:T(8,128)(2,1)S(1)}, u32[]{:S(2)}, u32[]{:S(2)}) collective-permute-start(bf16[2,128,256]{2,1,0:T(8,128)(2,1)S(1)} %get-tuple-element.71), channel_id=1, source_target_pairs={{0,8},{8,0},{16,24},{24,16},{1,9},{9,1},{17,25},{25,17},{2,10},{10... | collective-permute-start | bytes 393224 | tf_op jit(solution)/shard_map/ppermute | solution.py:283
  24.9 8.0 %collective-permute-start.3 = (bf16[2,128,256]{2,1,0:T(8,128)(2,1)S(1)}, bf16[2,128,256]{2,1,0:T(8,128)(2,1)S(1)}, u32[]{:S(2)}, u32[]{:S(2)}) collective-permute-start(bf16[2,128,256]{2,1,0:T(8,128)(2,1)S(1)} %get-tuple-element.72), channel_id=1, source_target_pairs={{0,16},{8,24},{16,0},{24,8},{1,17},{9,25},{17,1},{25,9},{2,18},{10... | collective-permute-start | bytes 393224 | tf_op jit(solution)/shard_map/ppermute | solution.py:283
  25.7 7.2 %collective-permute-start.4 = (bf16[2,128,256]{2,1,0:T(8,128)(2,1)S(1)}, bf16[2,128,256]{2,1,0:T(8,128)(2,1)S(1)}, u32[]{:S(2)}, u32[]{:S(2)}) collective-permute-start(bf16[2,128,256]{2,1,0:T(8,128)(2,1)S(1)} %get-tuple-element.73), channel_id=1, source_target_pairs={{0,24},{8,16},{16,8},{24,0},{1,25},{9,17},{17,9},{25,1},{2,26},{10... | collective-permute-start | bytes 393224 | tf_op jit(solution)/shard_map/ppermute | solution.py:283
  29.5 2.5 %collective-permute-start.5 = (s32[4,16]{1,0:T(4,128)S(1)}, s32[4,16]{1,0:T(4,128)S(1)}, u32[]{:S(2)}, u32[]{:S(2)}) collective-permute-start(s32[4,16]{1,0:T(4,128)S(1)} %fusion.refs_0_), channel_id=1, source_target_pairs={{0,1},{1,0},{2,3},{3,2},{4,5},{5,4},{6,7},{7,6},{8,9},{9,8},{10,11... | collective-permute-start | bytes 776 | tf_op jit(solution)/shard_map/ppermute | solution.py:280
  33.0 31.5 %collective-permute-start.6 = (bf16[1024,256]{1,0:T(8,128)(2,1)S(1)}, bf16[1024,256]{1,0:T(8,128)(2,1)}, u32[]{:S(2)}, u32[]{:S(2)}) collective-permute-start(bf16[1024,256]{1,0:T(8,128)(2,1)S(1)} %pack.2.refs_2_), channel_id=1, source_target_pairs={{0,6},{2,0},{4,2},{6,4},{1,7},{3,1},{5,3},{7,5},{8,14},{10,8},{12,... | collective-permute-start | bytes 1572872 | tf_op jit(solution)/shard_map/ppermute | solution.py:286
  37.0 23.0 %collective-permute-start.7 = (bf16[128,1024]{1,0:T(8,128)(2,1)S(1)}, bf16[128,1024]{1,0:T(8,128)(2,1)S(1)}, u32[]{:S(2)}, u32[]{:S(2)}) collective-permute-start(bf16[128,1024]{1,0:T(8,128)(2,1)S(1)} %get-tuple-element.79), channel_id=1, source_target_pairs={{0,8},{8,0},{16,24},{24,16},{1,9},{9,1},{17,25},{25,17},{2,10},{10... | collective-permute-start | bytes 786440 | tf_op jit(solution)/shard_map/ppermute | solution.py:283
  38.6 21.4 %collective-permute-start.8 = (bf16[128,1024]{1,0:T(8,128)(2,1)S(1)}, bf16[128,1024]{1,0:T(8,128)(2,1)S(1)}, u32[]{:S(2)}, u32[]{:S(2)}) collective-permute-start(bf16[128,1024]{1,0:T(8,128)(2,1)S(1)} %get-tuple-element.80), channel_id=1, source_target_pairs={{0,16},{8,24},{16,0},{24,8},{1,17},{9,25},{17,1},{25,9},{2,18},{10... | collective-permute-start | bytes 786440 | tf_op jit(solution)/shard_map/ppermute | solution.py:283
  39.2 12.5 %copy-start.25 = (bf16[1024,512]{1,0:T(8,128)(2,1)S(1)}, bf16[1024,512]{1,0:T(8,128)(2,1)}, u32[]{:S(2)}) copy-start(bf16[1024,512]{1,0:T(8,128)(2,1)} %refs_2_.3) | copy-start | bytes 3145732
  39.3 20.8 %collective-permute-start.9 = (bf16[128,1024]{1,0:T(8,128)(2,1)S(1)}, bf16[128,1024]{1,0:T(8,128)(2,1)S(1)}, u32[]{:S(2)}, u32[]{:S(2)}) collective-permute-start(bf16[128,1024]{1,0:T(8,128)(2,1)S(1)} %get-tuple-element.81), channel_id=1, source_target_pairs={{0,24},{8,16},{16,8},{24,0},{1,25},{9,17},{17,9},{25,1},{2,26},{10... | collective-permute-start | bytes 786440 | tf_op jit(solution)/shard_map/ppermute | solution.py:283
  53.0 8.4 %collective-permute-start.11 = (bf16[512,256]{1,0:T(8,128)(2,1)S(1)}, bf16[512,256]{1,0:T(8,128)(2,1)S(1)}, u32[]{:S(2)}, u32[]{:S(2)}) collective-permute-start(bf16[512,256]{1,0:T(8,128)(2,1)S(1)} %get-tuple-element.86), channel_id=1, source_target_pairs={{0,1},{1,0},{2,3},{3,2},{4,5},{5,4},{6,7},{7,6},{8,9},{9,8},{10,11... | collective-permute-start | bytes 786440 | tf_op jit(solution)/shard_map/ppermute | solution.py:280
  64.5 22.0 %collective-permute-start.12 = (bf16[1024,256]{1,0:T(8,128)(2,1)}, bf16[1024,256]{1,0:T(8,128)(2,1)S(1)}, u32[]{:S(2)}, u32[]{:S(2)}) collective-permute-start(bf16[1024,256]{1,0:T(8,128)(2,1)} %collective-permute-done.6.refs_2_), channel_id=1, source_target_pairs={{0,6},{2,0},{4,2},{6,4},{1,7},{3,1},{5,3},{7,5},{8,14},{10,8},{12,... | collective-permute-start | bytes 1572872 | tf_op jit(solution)/shard_map/ppermute | solution.py:286
  64.5 19.3 %copy-start.5 = (bf16[1024,512]{1,0:T(8,128)(2,1)S(1)}, bf16[1024,512]{1,0:T(8,128)(2,1)}, u32[]{:S(2)}) copy-start(bf16[1024,512]{1,0:T(8,128)(2,1)} %copy-done.4) | copy-start | bytes 3145732
  64.5 19.3 %copy-start.7 = (bf16[1024,512]{1,0:T(8,128)(2,1)S(1)}, bf16[1024,512]{1,0:T(8,128)(2,1)}, u32[]{:S(2)}) copy-start(bf16[1024,512]{1,0:T(8,128)(2,1)} %copy-done.6) | copy-start | bytes 3145732
  64.5 6.6 %collective-permute-start.13 = (bf16[2,128,256]{2,1,0:T(8,128)(2,1)}, bf16[2,128,256]{2,1,0:T(8,128)(2,1)S(1)}, u32[]{:S(2)}, u32[]{:S(2)}) collective-permute-start(bf16[2,128,256]{2,1,0:T(8,128)(2,1)} %copy-done.26), channel_id=1, source_target_pairs={{0,8},{8,0},{16,24},{24,16},{1,9},{9,1},{17,25},{25,17},{2,10},{10... | collective-permute-start | bytes 393224 | tf_op jit(solution)/shard_map/ppermute | solution.py:283
  65.6 8.4 %collective-permute-start.14 = (bf16[2,128,256]{2,1,0:T(8,128)(2,1)S(1)}, bf16[2,128,256]{2,1,0:T(8,128)(2,1)S(1)}, u32[]{:S(2)}, u32[]{:S(2)}) collective-permute-start(bf16[2,128,256]{2,1,0:T(8,128)(2,1)S(1)} %get-tuple-element.93), channel_id=1, source_target_pairs={{0,16},{8,24},{16,0},{24,8},{1,17},{9,25},{17,1},{25,9},{2,18},{10... | collective-permute-start | bytes 393224 | tf_op jit(solution)/shard_map/ppermute | solution.py:283
  66.2 7.8 %collective-permute-start.15 = (bf16[2,128,256]{2,1,0:T(8,128)(2,1)S(1)}, bf16[2,128,256]{2,1,0:T(8,128)(2,1)S(1)}, u32[]{:S(2)}, u32[]{:S(2)}) collective-permute-start(bf16[2,128,256]{2,1,0:T(8,128)(2,1)S(1)} %get-tuple-element.94), channel_id=1, source_target_pairs={{0,24},{8,16},{16,8},{24,0},{1,25},{9,17},{17,9},{25,1},{2,26},{10... | collective-permute-start | bytes 393224 | tf_op jit(solution)/shard_map/ppermute | solution.py:283
  69.2 14.6 %collective-permute-start.16 = (bf16[512,256]{1,0:T(8,128)(2,1)S(1)}, bf16[512,256]{1,0:T(8,128)(2,1)S(1)}, u32[]{:S(2)}, u32[]{:S(2)}) collective-permute-start(bf16[512,256]{1,0:T(8,128)(2,1)S(1)} %get-tuple-element.126), channel_id=1, source_target_pairs={{0,1},{1,0},{2,3},{3,2},{4,5},{5,4},{6,7},{7,6},{8,9},{9,8},{10,11... | collective-permute-start | bytes 786440 | tf_op jit(solution)/shard_map/ppermute | solution.py:280
  77.0 8.8 %copy-start.1 = (bf16[1024,512]{1,0:T(8,128)(2,1)S(1)}, bf16[1024,512]{1,0:T(8,128)(2,1)}, u32[]{:S(2)}) copy-start(bf16[1024,512]{1,0:T(8,128)(2,1)} %copy-done) | copy-start | bytes 3145732
  77.0 11.3 %collective-permute-start.19 = (bf16[128,1024]{1,0:T(8,128)(2,1)S(1)}, bf16[128,1024]{1,0:T(8,128)(2,1)S(1)}, u32[]{:S(2)}, u32[]{:S(2)}) collective-permute-start(bf16[128,1024]{1,0:T(8,128)(2,1)S(1)} %get-tuple-element.110.refs_10_), channel_id=1, source_target_pairs={{0,8},{8,0},{16,24},{24,16},{1,9},{9,1},{17,25},{25,17},{2,10},{10... | collective-permute-start | bytes 786440 | tf_op jit(solution)/shard_map/ppermute | solution.py:283
  78.1 11.6 %collective-permute-start.20 = (bf16[128,1024]{1,0:T(8,128)(2,1)S(1)}, bf16[128,1024]{1,0:T(8,128)(2,1)S(1)}, u32[]{:S(2)}, u32[]{:S(2)}) collective-permute-start(bf16[128,1024]{1,0:T(8,128)(2,1)S(1)} %get-tuple-element.111.refs_11_), channel_id=1, source_target_pairs={{0,16},{8,24},{16,0},{24,8},{1,17},{9,25},{17,1},{25,9},{2,18},{10... | collective-permute-start | bytes 786440 | tf_op jit(solution)/shard_map/ppermute | solution.py:283
  79.0 12.0 %collective-permute-start.21 = (bf16[128,1024]{1,0:T(8,128)(2,1)S(1)}, bf16[128,1024]{1,0:T(8,128)(2,1)S(1)}, u32[]{:S(2)}, u32[]{:S(2)}) collective-permute-start(bf16[128,1024]{1,0:T(8,128)(2,1)S(1)} %get-tuple-element.112.refs_12_), channel_id=1, source_target_pairs={{0,24},{8,16},{16,8},{24,0},{1,25},{9,17},{17,9},{25,1},{2,26},{10... | collective-permute-start | bytes 786440 | tf_op jit(solution)/shard_map/ppermute | solution.py:283
  83.8 22.4 %collective-permute-start.18 = (bf16[1024,512]{1,0:T(8,128)(2,1)}, bf16[1024,512]{1,0:T(8,128)(2,1)S(1)}, u32[]{:S(2)}, u32[]{:S(2)}) collective-permute-start(bf16[1024,512]{1,0:T(8,128)(2,1)} %copy-done.19), channel_id=1, source_target_pairs={{0,1},{1,0},{2,3},{3,2},{4,5},{5,4},{6,7},{7,6},{8,9},{9,8},{10,11... | collective-permute-start | bytes 3145736 | tf_op jit(solution)/shard_map/ppermute | solution.py:280
  88.2 16.6 %copy-start.10 = (bf16[1024,512]{1,0:T(8,128)(2,1)S(1)}, bf16[1024,512]{1,0:T(8,128)(2,1)}, u32[]{:S(2)}) copy-start(bf16[1024,512]{1,0:T(8,128)(2,1)} %copy-done.8) | copy-start | bytes 3145732
  88.2 16.5 %copy-start.13 = (bf16[1024,512]{1,0:T(8,128)(2,1)S(1)}, bf16[1024,512]{1,0:T(8,128)(2,1)}, u32[]{:S(2)}) copy-start(bf16[1024,512]{1,0:T(8,128)(2,1)} %copy-done.11) | copy-start | bytes 3145732
  88.2 14.3 %collective-permute-start.23 = (bf16[1024,256]{1,0:T(8,128)(2,1)S(1)}, bf16[1024,256]{1,0:T(8,128)(2,1)S(1)}, u32[]{:S(2)}, u32[]{:S(2)}) collective-permute-start(bf16[1024,256]{1,0:T(8,128)(2,1)S(1)} %get-tuple-element.119), channel_id=1, source_target_pairs={{0,6},{2,0},{4,2},{6,4},{1,7},{3,1},{5,3},{7,5},{8,14},{10,8},{12,... | collective-permute-start | bytes 1572872 | tf_op jit(solution)/shard_map/ppermute | solution.py:286
  91.9 14.3 %collective-permute-start.22 = (bf16[1024,512]{1,0:T(8,128)(2,1)S(1)}, bf16[1024,512]{1,0:T(8,128)(2,1)S(1)}, u32[]{:S(2)}, u32[]{:S(2)}) collective-permute-start(bf16[1024,512]{1,0:T(8,128)(2,1)S(1)} %get-tuple-element.116.refs_3_), channel_id=1, source_target_pairs={{0,1},{1,0},{2,3},{3,2},{4,5},{5,4},{6,7},{7,6},{8,9},{9,8},{10,11... | collective-permute-start | bytes 3145736 | tf_op jit(solution)/shard_map/ppermute | solution.py:280
  91.9 3.0 %collective-permute-start.17 = (bf16[512,256]{1,0:T(8,128)(2,1)S(1)}, bf16[512,256]{1,0:T(8,128)(2,1)S(1)}, u32[]{:S(2)}, u32[]{:S(2)}) collective-permute-start(bf16[512,256]{1,0:T(8,128)(2,1)S(1)} %get-tuple-element.114), channel_id=1, source_target_pairs={{0,1},{1,0},{2,3},{3,2},{4,5},{5,4},{6,7},{7,6},{8,9},{9,8},{10,11... | collective-permute-start | bytes 786440 | tf_op jit(solution)/shard_map/ppermute | solution.py:280
  102.6 13.5 %copy-start.20 = (bf16[1024,512]{1,0:T(8,128)(2,1)S(1)}, bf16[1024,512]{1,0:T(8,128)(2,1)}, u32[]{:S(2)}) copy-start(bf16[1024,512]{1,0:T(8,128)(2,1)} %copy-done.19) | copy-start | bytes 3145732
  102.6 13.5 %collective-permute-start.24 = (bf16[1024,256]{1,0:T(8,128)(2,1)S(1)}, bf16[1024,256]{1,0:T(8,128)(2,1)S(1)}, u32[]{:S(2)}, u32[]{:S(2)}) collective-permute-start(bf16[1024,256]{1,0:T(8,128)(2,1)S(1)} %pass.1), channel_id=1, source_target_pairs={{0,6},{2,0},{4,2},{6,4},{1,7},{3,1},{5,3},{7,5},{8,14},{10,8},{12,... | collective-permute-start | bytes 1572872 | tf_op jit(solution)/shard_map/ppermute | solution.py:286
  118.0 6.2 %collective-permute-start.25 = (bf16[256,256]{1,0:T(8,128)(2,1)S(1)}, bf16[256,256]{1,0:T(8,128)(2,1)S(1)}, u32[]{:S(2)}, u32[]{:S(2)}) collective-permute-start(bf16[256,256]{1,0:T(8,128)(2,1)S(1)} %get-tuple-element.121), channel_id=1, source_target_pairs={{0,8},{8,0},{16,24},{24,16},{1,9},{9,1},{17,25},{25,17},{2,10},{10... | collective-permute-start | bytes 393224 | tf_op jit(solution)/shard_map/ppermute | solution.py:283
  119.2 7.1 %collective-permute-start.26 = (bf16[256,256]{1,0:T(8,128)(2,1)S(1)}, bf16[256,256]{1,0:T(8,128)(2,1)S(1)}, u32[]{:S(2)}, u32[]{:S(2)}) collective-permute-start(bf16[256,256]{1,0:T(8,128)(2,1)S(1)} %get-tuple-element.122), channel_id=1, source_target_pairs={{0,16},{8,24},{16,0},{24,8},{1,17},{9,25},{17,1},{25,9},{2,18},{10... | collective-permute-start | bytes 393224 | tf_op jit(solution)/shard_map/ppermute | solution.py:283
  120.0 6.3 %collective-permute-start.27 = (bf16[256,256]{1,0:T(8,128)(2,1)S(1)}, bf16[256,256]{1,0:T(8,128)(2,1)S(1)}, u32[]{:S(2)}, u32[]{:S(2)}) collective-permute-start(bf16[256,256]{1,0:T(8,128)(2,1)S(1)} %get-tuple-element.123), channel_id=1, source_target_pairs={{0,24},{8,16},{16,8},{24,0},{1,25},{9,17},{17,9},{25,1},{2,26},{10... | collective-permute-start | bytes 393224 | tf_op jit(solution)/shard_map/ppermute | solution.py:283
  126.4 5.0 %collective-permute-start.28 = (bf16[256,256]{1,0:T(8,128)(2,1)S(1)}, bf16[256,256]{1,0:T(8,128)(2,1)S(1)}, u32[]{:S(2)}, u32[]{:S(2)}) collective-permute-start(bf16[256,256]{1,0:T(8,128)(2,1)S(1)} %sum.3.refs_0_), channel_id=1, source_target_pairs={{0,2},{2,0},{4,6},{6,4},{1,3},{3,1},{5,7},{7,5},{8,10},{10,8},{12,... | collective-permute-start | bytes 393224 | tf_op jit(solution)/shard_map/ppermute | solution.py:453
  131.4 7.4 %collective-permute-start.29 = (bf16[256,256]{1,0:T(8,128)(2,1)S(1)}, bf16[256,256]{1,0:T(8,128)(2,1)S(1)}, u32[]{:S(2)}, u32[]{:S(2)}) collective-permute-start(bf16[256,256]{1,0:T(8,128)(2,1)S(1)} %sum.4.refs_0_), channel_id=1, source_target_pairs={{0,4},{2,6},{4,0},{6,2},{1,5},{3,7},{5,1},{7,3},{8,12},{10,14},{12... | collective-permute-start | bytes 393224 | tf_op jit(solution)/shard_map/ppermute | solution.py:453
  138.9 5.0 %collective-permute-start.30 = (bf16[256,256]{1,0:T(8,128)(2,1)S(1)}, bf16[256,256]{1,0:T(8,128)(2,1)S(1)}, u32[]{:S(2)}, u32[]{:S(2)}) collective-permute-start(bf16[256,256]{1,0:T(8,128)(2,1)S(1)} %sum.5.refs_1_), channel_id=1, source_target_pairs={{0,8},{8,0},{16,24},{24,16},{1,9},{9,1},{17,25},{25,17},{2,10},{10... | collective-permute-start | bytes 393224 | tf_op jit(solution)/shard_map/ppermute | solution.py:283
  139.0 5.8 %collective-permute-start.31 = (bf16[256,256]{1,0:T(8,128)(2,1)S(1)}, bf16[256,256]{1,0:T(8,128)(2,1)S(1)}, u32[]{:S(2)}, u32[]{:S(2)}) collective-permute-start(bf16[256,256]{1,0:T(8,128)(2,1)S(1)} %sum.5.refs_1_), channel_id=1, source_target_pairs={{0,16},{8,24},{16,0},{24,8},{1,17},{9,25},{17,1},{25,9},{2,18},{10... | collective-permute-start | bytes 393224 | tf_op jit(solution)/shard_map/ppermute | solution.py:283
  140.9 5.9 %collective-permute-start.32 = (bf16[256,256]{1,0:T(8,128)(2,1)S(1)}, bf16[256,256]{1,0:T(8,128)(2,1)S(1)}, u32[]{:S(2)}, u32[]{:S(2)}) collective-permute-start(bf16[256,256]{1,0:T(8,128)(2,1)S(1)} %sum.5.refs_1_), channel_id=1, source_target_pairs={{0,24},{8,16},{16,8},{24,0},{1,25},{9,17},{17,9},{25,1},{2,26},{10... | collective-permute-start | bytes 393224 | tf_op jit(solution)/shard_map/ppermute | solution.py:283
  142.4 5.2 %collective-permute-start.33 = (bf16[256,256]{1,0:T(8,128)(2,1)S(1)}, bf16[256,256]{1,0:T(8,128)(2,1)S(1)}, u32[]{:S(2)}, u32[]{:S(2)}) collective-permute-start(bf16[256,256]{1,0:T(8,128)(2,1)S(1)} %sum.5.refs_1_), channel_id=1, source_target_pairs={{0,1},{1,0},{2,3},{3,2},{4,5},{5,4},{6,7},{7,6},{8,9},{9,8},{10,11... | collective-permute-start | bytes 393224 | tf_op jit(solution)/shard_map/ppermute | solution.py:280
  143.9 3.7 %collective-permute-start.34 = (bf16[256,256]{1,0:T(8,128)(2,1)S(1)}, bf16[256,256]{1,0:T(8,128)(2,1)S(1)}, u32[]{:S(2)}, u32[]{:S(2)}) collective-permute-start(bf16[256,256]{1,0:T(8,128)(2,1)S(1)} %collective-permute-done.30.refs_2_), channel_id=1, source_target_pairs={{0,1},{1,0},{2,3},{3,2},{4,5},{5,4},{6,7},{7,6},{8,9},{9,8},{10,11... | collective-permute-start | bytes 393224 | tf_op jit(solution)/shard_map/ppermute | solution.py:280
  144.8 2.8 %collective-permute-start.35 = (bf16[256,256]{1,0:T(8,128)(2,1)S(1)}, bf16[256,256]{1,0:T(8,128)(2,1)S(1)}, u32[]{:S(2)}, u32[]{:S(2)}) collective-permute-start(bf16[256,256]{1,0:T(8,128)(2,1)S(1)} %collective-permute-done.31.refs_3_), channel_id=1, source_target_pairs={{0,1},{1,0},{2,3},{3,2},{4,5},{5,4},{6,7},{7,6},{8,9},{9,8},{10,11... | collective-permute-start | bytes 393224 | tf_op jit(solution)/shard_map/ppermute | solution.py:280
  146.7 1.3 collective-permute-start.36
  (18 other events, 53.4 us)

commit v9 on v8

--- a/solution.py
+++ b/solution.py
@@ -53,10 +53,10 @@
         kernel,
         out_shape=tuple(jax.ShapeDtypeStruct(s, d) for s, d in outs),
         in_specs=[smem if where == "s" else vmem for where, _ in ins]
-        + [pl.BlockSpec(memory_space=pl.ANY)] * ties,
+        + [vmem] * ties,
         out_specs=tuple(vmem for _ in outs),
         scratch_shapes=list(scratch),
-        compiler_params=pltpu.CompilerParams(vmem_limit_bytes=size + (6 << 20)),
+        compiler_params=pltpu.CompilerParams(vmem_limit_bytes=size + (5 << 20)),
         cost_estimate=pl.CostEstimate(flops=int(us * 2e7), bytes_accessed=0, transcendentals=0),
         name=name,
     )(*(value for _, value in ins), *after)
@@ -307,12 +307,12 @@
         )
         return own, to_core(other)
 
-    def send_of(lines, products):
+    def send_of(lines, products, after=()):
         return call(
             lambda *refs: send_kernel(z, lines, *refs),
             [((rows, rows), BF16)] + [((2, z.per_grp, half), BF16)] * z.grp,
             [("s", me), ("v", message)] + [("v", part) for part in products],
-            "send", 1.5, token=True,
+            "send", 1.5, after=after, token=True,
         )
 
     def across(parts):
@@ -323,15 +323,15 @@
             lambda *refs: pack_kernel(z, *refs),
             [((2 * rows, half), BF16)],
             [("v", part) for part in parts],
-            "pack", 0.5, after=after,
-        )[0]
+            "pack", 0.5, after=after, token=True,
+        )
 
     def rows_of(pick, part, after):
         return call(
             lambda *refs: rows_kernel(z, *refs),
             [((z.per_grp, width_in), BF16)] * z.grp,
             [("v", pick), ("v", part)],
-            "rows", 1, after=after,
+            "rows", 1, after=after, token=True,
         )
 
     def turned_of(parts):
@@ -356,11 +356,11 @@
     cot_a = lax.dynamic_slice_in_dim(cotangent, core * half, half, axis=1)
     cot_b = to_core(lax.dynamic_slice_in_dim(cotangent, (1 - core) * half, half, axis=1))
 
-    (place,) = call(
+    place, token_p = call(
         lambda *refs: place_kernel(z, *refs),
         [((z.dom, rows, rows), BF16)],
         [("s", me), ("v", message)],
-        "place", 1.5, after=[token],
+        "place", 1.5, after=[token], token=True,
     )
 
     def dense_of(cols, vals, after=()):
@@ -369,26 +369,31 @@
             [((z.dom * rows, rows), BF16)],
             [("s", cols), ("v", vals)],
             "dense", 2.5,
-            (pltpu.VMEM((z.dom * rows + tile, tile), F32),), after=after,
-        )[0]
-
-    dense_a = dense_of(cols_a, block_vals, [vals_b])
+            (pltpu.VMEM((z.dom * rows + tile, tile), F32),), after=after, token=True,
+        )
+
+    dense_a, token_a = dense_of(cols_a, block_vals)
 
     wide = 2 * z.grp * z.per_grp
-    ring = {0: pack(came, [place, dense_a, cols_b])}
-    turned_a, _ = arrange(z, place, dense_a, wide, [ring[0]])
-    turned_b, token_b = arrange(z, place, dense_of(cols_b, vals_b, [ring[0]]), wide)
+    first, token = pack(came, [token_p, token_a])
+    ring = {0: first}
+    *picked, token_r = rows_of(pick, features, [token])
+    held = across(picked)
+    turned_a, token = arrange(z, place, dense_a, wide, [token_r])
+    dense_b, token = dense_of(cols_b, vals_b, [token])
+    turned_b, token = arrange(z, place, dense_b, wide)
     turned = (turned_a, turned_b)
-    lefts, token_l = turned_of(across(rows_of(pick, features, [ring[0]])))
-    pick_near, *got, token_n = send_of((6, 7), products_of(near, [turned_a[0]]))
+    lefts, token_l = turned_of(held)
+    products = products_of(near, [token, token_l])
     order = list(range(z.zz - 1, 1, -1))
     for k in order:
         ring[k] = to_zz(ring[(k + 1) % z.zz], -1)
         if k == order[0]:
-            ring[k], *tokens = lax.optimization_barrier((ring[k], token_b, token_l, token_n))
-    came = across(got)
-    ring[1] = pack(came)
-    held_near = rows_of(pick_near, near, came[1:])
+            ring[k], token = lax.optimization_barrier((ring[k], token))
+            pick_near, *got, _ = send_of((6, 7), products, [token])
+    ring[1], token_k = pack(across(got))
+    *picked, token_r = rows_of(pick_near, near, [token_k])
+    held_near = across(picked)
 
     agg = []
     order = [0] + order[:-1] + [1] + order[-1:]
@@ -403,7 +408,7 @@
         agg = call(
             lambda *refs, k=k, last=last: forward_kernel(z, k == 0, last, *refs),
             outs, ins, "forward", 3 if last else 1,
-            after=held_near if last else [cot_a, cot_b, *tokens] if k == order[1] else (),
+            after=[token_r] if last else [cot_a, cot_b] if k == order[1] else (),
         )
     hidden_a, hidden_b, grad_a, grad_b, came = agg
 
@@ -415,7 +420,6 @@
             "back", 1,
         )[0]
 
-    held_near = across(held_near)
     come = to_core(hidden_b)
     for k in range(z.zz - 2, 0, -1):
         came = to_zz(came, -1)
@@ -424,7 +428,7 @@
             break
         (came,) = call(
             pass_kernel, [((wide, half), BF16)], [("v", mine), ("v", came)], "pass", 0.5,
-            after=[come, *held_near],
+            after=[come],
         )
     lefts += turned_of(held_near)[0]
     first = core == 0

time: 151 us -> 154 us (1.020)
  Pallas kernels: 34.6 us -> 37.8 us
  waiting for transfers between devices: 52.1 us -> 54.1 us
    ppermute x18, waiting for transfers between devices: 17.4 us -> 25.4 us  [to_grp(): lax.ppermute(x, 'grp', [(i, i ^ s) for i in range(z.grp)])]
    ppermute x5, waiting for transfers between devices: 24.7 us -> 17 us  [to_zz(): lax.ppermute(x, 'zz', [(i, (i + k) % z.zz) for i in range(z.zz)])]
    pallas_call x29, Pallas kernels: 34.6 us -> 37.8 us  [call(): pl.pallas_call(kernel, out_shape=tuple((jax.ShapeDtypeStruct(s, d) for s,...]
    ppermute x2, starting transfers between devices: 4.78 us -> 2.95 us  [shards(): lax.ppermute(mine, 'zz', [(i, i ^ step) for i in range(z.zz)])]
    unnamed x58 -> x52, local copies, waits for them, and re-layouts: 11.3 us -> 11.4 us
  transfers between devices with their start and end apart: 37 -> 37, of which waited for: 17 -> 18; matrix products, arithmetic and copies ran while one was open for 1% -> 1% of each run, Pallas kernels for 18% -> 20%
where the time goes in v9:
time: 154 us
  waiting for transfers between devices  54.1 us (35%)
  Pallas kernels  37.8 us (25%)
  starting transfers between devices  32.2 us (21%)
  blocking collectives  15.2 us (10%)
  local copies, waits for them, and re-layouts  12.4 us (8%)
    pallas_call x29, Pallas kernels, call(): pl.pallas_call(kernel, out_shape=tuple((jax.ShapeDtypeStruct(s, d) for s,...  37.8 us
    ppermute x18, waiting for transfers between devices, to_grp(): lax.ppermute(x, 'grp', [(i, i ^ s) for i in range(z.grp)])  25.4 us
    ppermute x18, starting transfers between devices, to_grp(): lax.ppermute(x, 'grp', [(i, i ^ s) for i in range(z.grp)])  21.3 us
    ppermute x5, waiting for transfers between devices, to_zz(): lax.ppermute(x, 'zz', [(i, (i + k) % z.zz) for i in range(z.zz)])  17 us
    all_to_all x1, blocking collectives, shards(): lax.all_to_all(message, ('grp', 'zz', 'core'), split_axis=0, concat_axis=...  15.2 us
    unnamed x52, local copies, waits for them, and re-layouts  11.4 us
    ppermute x2, waiting for transfers between devices, shards(): lax.ppermute(mine, 'zz', [(i, i ^ step) for i in range(z.zz)])  8.02 us
    ppermute x5, starting transfers between devices, to_zz(): lax.ppermute(x, 'zz', [(i, (i + k) % z.zz) for i in range(z.zz)])  6.11 us
  transfers between devices with their start and end apart: 37, of which 18 were waited for; matrix products, arithmetic and copies ran while one was open for 1% of the time, Pallas kernels for 20%

profile of v9, /device:TPU:0, one launch (start us, length us, event | category | flops | bytes accessed | tf_op | source)
XLA Modules:
  0.0 153.8 jit_solution(7049037471522608035)
XLA Ops:
  3.1 1.2 copy-done.11
  4.3 1.2 copy-done.22
  5.5 1.3 product.2
  7.0 15.2 %all_to_all.5.refs_1_ = s32[32,8,128]{2,1,0:T(8,128)S(1)} all-to-all(s32[32,8,128]{2,1,0:T(8,128)S(1)} %index.1), channel_id=1, replica_groups=mesh['grp'=4,'zz'=4,'core'=2] {'grp','zz','core'}, dimensions={0} | all-to-all | bytes 262144 | tf_op jit(solution)/shard_map/all_to_all | solution.py:296
  22.2 1.7 %send.2 = (bf16[512,512]{1,0:T(8,128)(2,1)S(1)}, bf16[2,128,256]{2,1,0:T(8,128)(2,1)S(1)}, bf16[2,128,256]{2,1,0:T(8,128)(2,1)S(1)}, bf16[2,128,256]{2,1,0:T(8,1...) custom-call(s32[3]{0:T(128)S(1)} %pad_add_fusion.refs_0_, s32[32,8,128]{2,1,0:T(8,128)S(1)} %all_to_all.5.refs_1_, ...), custom_call_target="tpu_custom_call" | custom-call | flops 30000000 | tf_op jit(solution)/shard_map/send/pallas_call | solution.py:52
  25.7 2.3 %collective-permute-start.3 = (bf16[2,128,256]{2,1,0:T(8,128)(2,1)S(1)}, bf16[2,128,256]{2,1,0:T(8,128)(2,1)S(1)}, u32[]{:S(2)}, u32[]{:S(2)}) collective-permute-start(bf16[2,128,256]{2,1,0:T(8,128)(2,1)S(1)} %get-tuple-element.85), channel_id=1, source_target_pairs={{0,24},{8,16},{16,8},{24,0},{1,25},{9,17},{17,9},{25,1},{2,26},{10... | collective-permute-start | bytes 393224 | tf_op jit(solution)/shard_map/ppermute | solution.py:283
  28.0 1.4 place.1
  29.5 2.4 %dense.2 = (bf16[4096,512]{1,0:T(8,128)(2,1)S(1)}, f32[8,128]{1,0:T(8,128)S(1)}) custom-call(s32[4,16]{1,0:T(4,128)S(1)} %fusion.refs_0_, bf16[4,16,128,128]{3,2,1,0:T(8,128)(2,1)S(1)} %copy-done.10), custom_call_target="tpu_custom_call" | custom-call | flops 50000000 | tf_op jit(solution)/shard_map/dense/pallas_call | solution.py:52
  33.7 1.4 collective-permute-start.9
  35.8 1.4 collective-permute-start.11
  37.3 5.8 %collective-permute-done.9.refs_1_ = bf16[128,1024]{1,0:T(8,128)(2,1)S(1)} collective-permute-done((bf16[128,1024]{1,0:T(8,128)(2,1)S(1)}, bf16[128,1024]{1,0:T(8,128)(2,1)S(1)}, u32[]{:S(2)}, u32[]{:S(2)}) %collective-permute-start.9) | collective-permute-done | bytes 262176 | tf_op jit(solution)/shard_map/ppermute | solution.py:283
  43.0 3.3 %collective-permute-start.6 = (bf16[1024,256]{1,0:T(8,128)(2,1)S(1)}, bf16[1024,256]{1,0:T(8,128)(2,1)}, u32[]{:S(2)}, u32[]{:S(2)}) collective-permute-start(bf16[1024,256]{1,0:T(8,128)(2,1)S(1)} %get-tuple-element.94.refs_2_), channel_id=1, source_target_pairs={{0,6},{2,0},{4,2},{6,4},{1,7},{3,1},{5,3},{7,5},{8,14},{10,8},{12,... | collective-permute-start | bytes 1572872 | tf_op jit(solution)/shard_map/ppermute | solution.py:286
  46.3 3.5 %arrange.2 = (bf16[1024,512]{1,0:T(8,128)(2,1)S(1)}, bf16[1024,512]{1,0:T(8,128)(2,1)S(1)}, bf16[1024,512]{1,0:T(8,128)(2,1)S(1)}, bf16[1024,512]{1,0:T(8,128)(2,1)S(1)}, f32[8,128]{1,0:T(8,128)S(1)}) custom-call(bf16[8,512,512]{2,1,0:T(8,128)(2,1)S(1)} %get-tuple-element.78.refs_0_, bf16[4096,512]{1,0:T(8,128)(2,1)S(1)} %get-tuple-element.80.refs_1_, ...), custom_call_target="tpu_custom_call" | custom-call | flops 80000000 | tf_op jit(solution)/shard_map/arrange/pallas_call | solution.py:52
  52.1 3.8 %dense.3 = (bf16[4096,512]{1,0:T(8,128)(2,1)S(1)}, f32[8,128]{1,0:T(8,128)}) custom-call(s32[4,16]{1,0:T(4,128)S(1)} %collective-permute-done.4.refs_0_, bf16[4,16,128,128]{3,2,1,0:T(8,128)(2,1)} %collective-permute-done.5.refs_1_, f32[8,128]{1,0:T(8,128)S(1)} %get-tuple-element.91.refs_2_), custom_call_target="tpu_custom_call" | custom-call | flops 50000000 | tf_op jit(solution)/shard_map/dense/pallas_call | solution.py:52
  56.0 3.5 %arrange.3 = (bf16[1024,512]{1,0:T(8,128)(2,1)S(1)}, bf16[1024,512]{1,0:T(8,128)(2,1)S(1)}, bf16[1024,512]{1,0:T(8,128)(2,1)S(1)}, bf16[1024,512]{1,0:T(8,128)(2,1)S(1)}, f32[8,128]{1,0:T(8,128)S(1)}) custom-call(bf16[8,512,512]{2,1,0:T(8,128)(2,1)S(1)} %get-tuple-element.78.refs_0_, bf16[4096,512]{1,0:T(8,128)(2,1)S(1)} %get-tuple-element.92.refs_1_), custom_call_target="tpu_custom_call" | custom-call | flops 80000000 | tf_op jit(solution)/shard_map/arrange/pallas_call | solution.py:52
  62.5 2.0 %product.3 = (bf16[512,256]{1,0:T(8,128)(2,1)S(1)}, bf16[512,256]{1,0:T(8,128)(2,1)}) custom-call(s32[3]{0:T(128)S(1)} %pad_add_fusion.refs_0_, bf16[512,1024]{1,0:T(8,128)(2,1)S(1)} %collective-permute-done.8.refs_1_, bf16[1024,512]{1,0:T(8,128)(2,1)S(1)} %copy-done.23, f32[8,128]{1,0:T(8,128)S(1)} %get-tuple-element.107.refs_3_.refs_4_, ...), custom_call_target="tpu_custom_call" | custom-call | flops 1500000000 | tf_op jit(solution)/shard_map/product/pallas_call | solution.py:52
  65.9 1.5 collective-permute-done.12.refs_3_
  67.4 2.1 %send.3 = (bf16[512,512]{1,0:T(8,128)(2,1)S(1)}, bf16[2,128,256]{2,1,0:T(8,128)(2,1)S(1)}, bf16[2,128,256]{2,1,0:T(8,128)(2,1)S(1)}, bf16[2,128,256]{2,1,0:T(8,1...) custom-call(s32[3]{0:T(128)S(1)} %pad_add_fusion.refs_0_, s32[32,8,128]{2,1,0:T(8,128)S(1)} %all_to_all.5.refs_1_, ...), custom_call_target="tpu_custom_call" | custom-call | flops 30000000 | tf_op jit(solution)/shard_map/send/pallas_call | solution.py:52
  70.5 1.3 collective-permute-start.14
  71.7 1.3 collective-permute-start.15
  74.2 1.7 %collective-permute-done.13.refs_1_ = bf16[2,128,256]{2,1,0:T(8,128)(2,1)S(1)} collective-permute-done((bf16[2,128,256]{2,1,0:T(8,128)(2,1)S(1)}, bf16[2,128,256]{2,1,0:T(8,128)(2,1)S(1)}, u32[]{:S(2)}, u32[]{:S(2)}) %collective-permute-start.13) | collective-permute-done | bytes 131104 | tf_op jit(solution)/shard_map/ppermute | solution.py:283
  75.9 1.7 %collective-permute-done.14.refs_2_ = bf16[2,128,256]{2,1,0:T(8,128)(2,1)S(1)} collective-permute-done((bf16[2,128,256]{2,1,0:T(8,128)(2,1)S(1)}, bf16[2,128,256]{2,1,0:T(8,128)(2,1)S(1)}, u32[]{:S(2)}, u32[]{:S(2)}) %collective-permute-start.14) | collective-permute-done | bytes 131104 | tf_op jit(solution)/shard_map/ppermute | solution.py:283
  77.6 1.2 collective-permute-done.15.refs_3_
  78.9 1.2 copy-done.14
  80.9 1.1 collective-permute-start.19
  82.0 1.2 collective-permute-start.20
  83.2 1.2 collective-permute-start.21
  86.4 1.9 %forward.5 = (f32[512,256]{1,0:T(8,128)S(1)}, f32[512,256]{1,0:T(8,128)S(1)}) custom-call(bf16[1024,512]{1,0:T(8,128)(2,1)S(1)} %copy-done.7, bf16[1024,512]{1,0:T(8,128)(2,1)S(1)} %copy-done.9, bf16[1024,256]{1,0:T(8,128)(2,1)} %collective-permute-done.6.refs_2_, f32[512,256]{1,0:T(8,128)S(1)} %get-tuple-element.117.refs_3_, ...), custom_call_target="tpu_custom_call" | custom-call | flops 20000000 | tf_op jit(solution)/shard_map/forward/pallas_call | solution.py:52
  89.1 2.7 %forward.7 = (bf16[512,256]{1,0:T(8,128)(2,1)S(1)}, bf16[512,256]{1,0:T(8,128)(2,1)S(1)}, bf16[512,256]{1,0:T(8,128)(2,1)S(1)}, bf16[512,256]{1,0:T(8,128)(2,1)S(1)}, bf16[1024,256]{1,0:T(8,128)(2,1)S(1)}) custom-call(bf16[1024,512]{1,0:T(8,128)(2,1)S(1)} %copy-done.3, bf16[1024,512]{1,0:T(8,128)(2,1)S(1)} %copy-done.5, ...), custom_call_target="tpu_custom_call" | custom-call | flops 60000000 | tf_op jit(solution)/shard_map/forward/pallas_call | solution.py:52
  91.9 3.1 %collective-permute-done.20.refs_2_ = bf16[128,1024]{1,0:T(8,128)(2,1)S(1)} collective-permute-done((bf16[128,1024]{1,0:T(8,128)(2,1)S(1)}, bf16[128,1024]{1,0:T(8,128)(2,1)S(1)}, u32[]{:S(2)}, u32[]{:S(2)}) %collective-permute-start.20) | collective-permute-done | bytes 262176 | tf_op jit(solution)/shard_map/ppermute | solution.py:283
  97.1 1.8 %collective-permute-done.17.refs_2_ = bf16[512,256]{1,0:T(8,128)(2,1)S(1)} collective-permute-done((bf16[512,256]{1,0:T(8,128)(2,1)S(1)}, bf16[512,256]{1,0:T(8,128)(2,1)S(1)}, u32[]{:S(2)}, u32[]{:S(2)}) %collective-permute-start.17) | collective-permute-done | bytes 262176 | tf_op jit(solution)/shard_map/ppermute | solution.py:280
  98.9 7.1 %collective-permute-done.23.refs_1_ = bf16[1024,256]{1,0:T(8,128)(2,1)S(1)} collective-permute-done((bf16[1024,256]{1,0:T(8,128)(2,1)S(1)}, bf16[1024,256]{1,0:T(8,128)(2,1)S(1)}, u32[]{:S(2)}, u32[]{:S(2)}) %collective-permute-start.23) | collective-permute-done | bytes 524320 | tf_op jit(solution)/shard_map/ppermute | solution.py:286
  106.1 2.1 %collective-permute-start.24 = (bf16[1024,256]{1,0:T(8,128)(2,1)S(1)}, bf16[1024,256]{1,0:T(8,128)(2,1)S(1)}, u32[]{:S(2)}, u32[]{:S(2)}) collective-permute-start(bf16[1024,256]{1,0:T(8,128)(2,1)S(1)} %pass.1), channel_id=1, source_target_pairs={{0,6},{2,0},{4,2},{6,4},{1,7},{3,1},{5,3},{7,5},{8,14},{10,8},{12,... | collective-permute-start | bytes 1572872 | tf_op jit(solution)/shard_map/ppermute | solution.py:286
  109.7 9.8 %collective-permute-done.24.refs_7_ = bf16[1024,256]{1,0:T(8,128)(2,1)S(1)} collective-permute-done((bf16[1024,256]{1,0:T(8,128)(2,1)S(1)}, bf16[1024,256]{1,0:T(8,128)(2,1)S(1)}, u32[]{:S(2)}, u32[]{:S(2)}) %collective-permute-start.24) | collective-permute-done | bytes 524320 | tf_op jit(solution)/shard_map/ppermute | solution.py:286
  119.6 1.8 %grad.1 = (bf16[256,256]{1,0:T(8,128)(2,1)S(1)}, bf16[256,256]{1,0:T(8,128)(2,1)S(1)}, bf16[256,256]{1,0:T(8,128)(2,1)S(1)}, bf16[256,256]{1,0:T(8,128)(2,1)S(1)}) custom-call(s32[3]{0:T(128)S(1)} %pad_add_fusion.refs_0_, bf16[1024,512]{1,0:T(8,128)(2,1)S(1)} %copy-done.16, bf16[1024,512]{1,0:T(8,128)(2,1)S(1)} %collective-permute-done.18.refs_2_, ...), custom_call_target="tpu_custom_call" | custom-call | flops 30000000 | tf_op jit(solution)/shard_map/grad/pallas_call | solution.py:52
  121.4 1.1 collective-permute-start.25
  122.5 1.2 collective-permute-start.26
  123.8 1.2 collective-permute-start.27
  124.9 2.8 %collective-permute-done.25.refs_1_ = bf16[256,256]{1,0:T(8,128)(2,1)S(1)} collective-permute-done((bf16[256,256]{1,0:T(8,128)(2,1)S(1)}, bf16[256,256]{1,0:T(8,128)(2,1)S(1)}, u32[]{:S(2)}, u32[]{:S(2)}) %collective-permute-start.25) | collective-permute-done | bytes 131104 | tf_op jit(solution)/shard_map/ppermute | solution.py:283
  127.7 2.3 %collective-permute-done.26.refs_2_ = bf16[256,256]{1,0:T(8,128)(2,1)S(1)} collective-permute-done((bf16[256,256]{1,0:T(8,128)(2,1)S(1)}, bf16[256,256]{1,0:T(8,128)(2,1)S(1)}, u32[]{:S(2)}, u32[]{:S(2)}) %collective-permute-start.26) | collective-permute-done | bytes 131104 | tf_op jit(solution)/shard_map/ppermute | solution.py:283
  130.2 5.0 %collective-permute-done.28.refs_1_ = bf16[256,256]{1,0:T(8,128)(2,1)S(1)} collective-permute-done((bf16[256,256]{1,0:T(8,128)(2,1)S(1)}, bf16[256,256]{1,0:T(8,128)(2,1)S(1)}, u32[]{:S(2)}, u32[]{:S(2)}) %collective-permute-start.28) | collective-permute-done | bytes 131104 | tf_op jit(solution)/shard_map/ppermute | solution.py:457
  135.2 2.9 %collective-permute-start.29 = (bf16[256,256]{1,0:T(8,128)(2,1)S(1)}, bf16[256,256]{1,0:T(8,128)(2,1)S(1)}, u32[]{:S(2)}, u32[]{:S(2)}) collective-permute-start(bf16[256,256]{1,0:T(8,128)(2,1)S(1)} %sum.4.refs_0_), channel_id=1, source_target_pairs={{0,4},{2,6},{4,0},{6,2},{1,5},{3,7},{5,1},{7,3},{8,12},{10,14},{12... | collective-permute-start | bytes 393224 | tf_op jit(solution)/shard_map/ppermute | solution.py:457
  138.1 3.1 %collective-permute-done.29.refs_1_ = bf16[256,256]{1,0:T(8,128)(2,1)S(1)} collective-permute-done((bf16[256,256]{1,0:T(8,128)(2,1)S(1)}, bf16[256,256]{1,0:T(8,128)(2,1)S(1)}, u32[]{:S(2)}, u32[]{:S(2)}) %collective-permute-start.29) | collective-permute-done | bytes 131104 | tf_op jit(solution)/shard_map/ppermute | solution.py:457
  142.0 2.6 %collective-permute-start.31 = (bf16[256,256]{1,0:T(8,128)(2,1)S(1)}, bf16[256,256]{1,0:T(8,128)(2,1)S(1)}, u32[]{:S(2)}, u32[]{:S(2)}) collective-permute-start(bf16[256,256]{1,0:T(8,128)(2,1)S(1)} %sum.5.refs_1_), channel_id=1, source_target_pairs={{0,16},{8,24},{16,0},{24,8},{1,17},{9,25},{17,1},{25,9},{2,18},{10... | collective-permute-start | bytes 393224 | tf_op jit(solution)/shard_map/ppermute | solution.py:283
  144.7 1.5 collective-permute-done.30.refs_2_
  146.2 2.3 %collective-permute-done.31.refs_3_ = bf16[256,256]{1,0:T(8,128)(2,1)S(1)} collective-permute-done((bf16[256,256]{1,0:T(8,128)(2,1)S(1)}, bf16[256,256]{1,0:T(8,128)(2,1)S(1)}, u32[]{:S(2)}, u32[]{:S(2)}) %collective-permute-start.31) | collective-permute-done | bytes 131104 | tf_op jit(solution)/shard_map/ppermute | solution.py:283
  148.5 1.9 %collective-permute-done.32.refs_4_ = bf16[256,256]{1,0:T(8,128)(2,1)S(1)} collective-permute-done((bf16[256,256]{1,0:T(8,128)(2,1)S(1)}, bf16[256,256]{1,0:T(8,128)(2,1)S(1)}, u32[]{:S(2)}, u32[]{:S(2)}) %collective-permute-start.32) | collective-permute-done | bytes 131104 | tf_op jit(solution)/shard_map/ppermute | solution.py:283
  151.8 2.0 %last.1 = f32[1024,512]{1,0:T(8,128)} custom-call(s32[3]{0:T(128)S(1)} %pad_add_fusion.refs_0_, bf16[256,256]{1,0:T(8,128)(2,1)S(1)} %sum.5.refs_1_, bf16[256,256]{1,0:T(8,128)(2,1)S(1)} %collective-permute-done.30.refs_2_, bf16[256,256]{1,0:T(8,128)(2,1)S(1)} %collective-permute-done.31.refs_3_, bf16[256,256]{1,0:T(8,128)(2,1)S(1)} %collective-permute-done.32.refs_4_, ...), custom_call_target="tpu_custom_call" | custom-call | flops 40000000 | tf_op jit(solution)/shard_map/last/pallas_call | solution.py:52
  (113 shorter events, 25.5 us)
Async XLA Ops:
  0.6 28.9 %copy-start.10 = (bf16[4,16,128,128]{3,2,1,0:T(8,128)(2,1)S(1)}, bf16[4,16,128,128]{3,2,1,0:T(8,128)(2,1)}, u32[]{:S(2)}) copy-start(bf16[4,16,128,128]{3,2,1,0:T(8,128)(2,1)} %refs_1_.2) | copy-start | bytes 6291460
  0.6 51.5 %collective-permute-start.5 = (bf16[4,16,128,128]{3,2,1,0:T(8,128)(2,1)}, bf16[4,16,128,128]{3,2,1,0:T(8,128)(2,1)}, u32[]{:S(2)}, u32[]{:S(2)}) collective-permute-start(bf16[4,16,128,128]{3,2,1,0:T(8,128)(2,1)} %refs_1_.2), channel_id=1, source_target_pairs={{0,1},{1,0},{2,3},{3,2},{4,5},{5,4},{6,7},{7,6},{8,9},{9,8},{10,11... | collective-permute-start | bytes 6291464 | tf_op jit(solution)/shard_map/ppermute | solution.py:280
  5.5 18.3 %copy-start.12 = (bf16[512,1024]{1,0:T(8,128)(2,1)S(1)}, bf16[512,1024]{1,0:T(8,128)(2,1)}, u32[]{:S(2)}) copy-start(bf16[512,1024]{1,0:T(8,128)(2,1)} %refs_1_.3) | copy-start | bytes 3145732
  5.5 23.9 %copy-start.24 = (s32[4,16]{1,0:T(4,128)S(1)}, s32[4,16]{1,0:T(4,128)}, u32[]{:S(2)}) copy-start(s32[4,16]{1,0:T(4,128)} %param.9) | copy-start | bytes 772
  5.5 23.9 %copy-start.25 = (s32[4]{0:T(128)S(1)}, s32[4]{0:T(128)}, u32[]{:S(2)}) copy-start(s32[4]{0:T(128)} %param.10) | copy-start | bytes 52
  6.8 15.4 %collective-permute-start = (bf16[512,256]{1,0:T(8,128)(2,1)S(1)}, bf16[512,256]{1,0:T(8,128)(2,1)S(1)}, u32[]{:S(2)}, u32[]{:S(2)}) collective-permute-start(bf16[512,256]{1,0:T(8,128)(2,1)S(1)} %get-tuple-element.75), channel_id=1, source_target_pairs={{0,1},{1,0},{2,3},{3,2},{4,5},{5,4},{6,7},{7,6},{8,9},{9,8},{10,11... | collective-permute-start | bytes 786440 | tf_op jit(solution)/shard_map/ppermute | solution.py:280
  23.8 38.6 %collective-permute-start.8 = (bf16[512,1024]{1,0:T(8,128)(2,1)S(1)}, bf16[512,1024]{1,0:T(8,128)(2,1)S(1)}, u32[]{:S(2)}, u32[]{:S(2)}) collective-permute-start(bf16[512,1024]{1,0:T(8,128)(2,1)S(1)} %copy-done.12), channel_id=1, source_target_pairs={{0,2},{2,4},{4,6},{6,0},{1,3},{3,5},{5,7},{7,1},{8,10},{10,12},{12... | collective-permute-start | bytes 3145736 | tf_op jit(solution)/shard_map/ppermute | solution.py:286
  24.5 7.4 %collective-permute-start.1 = (bf16[2,128,256]{2,1,0:T(8,128)(2,1)S(1)}, bf16[2,128,256]{2,1,0:T(8,128)(2,1)S(1)}, u32[]{:S(2)}, u32[]{:S(2)}) collective-permute-start(bf16[2,128,256]{2,1,0:T(8,128)(2,1)S(1)} %get-tuple-element.83), channel_id=1, source_target_pairs={{0,8},{8,0},{16,24},{24,16},{1,9},{9,1},{17,25},{25,17},{2,10},{10... | collective-permute-start | bytes 393224 | tf_op jit(solution)/shard_map/ppermute | solution.py:283
  24.9 8.0 %collective-permute-start.2 = (bf16[2,128,256]{2,1,0:T(8,128)(2,1)S(1)}, bf16[2,128,256]{2,1,0:T(8,128)(2,1)S(1)}, u32[]{:S(2)}, u32[]{:S(2)}) collective-permute-start(bf16[2,128,256]{2,1,0:T(8,128)(2,1)S(1)} %get-tuple-element.84), channel_id=1, source_target_pairs={{0,16},{8,24},{16,0},{24,8},{1,17},{9,25},{17,1},{25,9},{2,18},{10... | collective-permute-start | bytes 393224 | tf_op jit(solution)/shard_map/ppermute | solution.py:283
  25.7 7.2 %collective-permute-start.3 = (bf16[2,128,256]{2,1,0:T(8,128)(2,1)S(1)}, bf16[2,128,256]{2,1,0:T(8,128)(2,1)S(1)}, u32[]{:S(2)}, u32[]{:S(2)}) collective-permute-start(bf16[2,128,256]{2,1,0:T(8,128)(2,1)S(1)} %get-tuple-element.85), channel_id=1, source_target_pairs={{0,24},{8,16},{16,8},{24,0},{1,25},{9,17},{17,9},{25,1},{2,26},{10... | collective-permute-start | bytes 393224 | tf_op jit(solution)/shard_map/ppermute | solution.py:283
  33.0 16.8 %copy-start.17 = (bf16[1024,256]{1,0:T(8,128)(2,1)}, bf16[1024,256]{1,0:T(8,128)(2,1)S(1)}, u32[]{:S(2)}) copy-start(bf16[1024,256]{1,0:T(8,128)(2,1)S(1)} %get-tuple-element.94.refs_2_) | copy-start | bytes 1572868
  33.7 9.3 %collective-permute-start.9 = (bf16[128,1024]{1,0:T(8,128)(2,1)S(1)}, bf16[128,1024]{1,0:T(8,128)(2,1)S(1)}, u32[]{:S(2)}, u32[]{:S(2)}) collective-permute-start(bf16[128,1024]{1,0:T(8,128)(2,1)S(1)} %get-tuple-element.101), channel_id=1, source_target_pairs={{0,8},{8,0},{16,24},{24,16},{1,9},{9,1},{17,25},{25,17},{2,10},{10... | collective-permute-start | bytes 786440 | tf_op jit(solution)/shard_map/ppermute | solution.py:283
  35.1 15.7 %collective-permute-start.10 = (bf16[128,1024]{1,0:T(8,128)(2,1)S(1)}, bf16[128,1024]{1,0:T(8,128)(2,1)S(1)}, u32[]{:S(2)}, u32[]{:S(2)}) collective-permute-start(bf16[128,1024]{1,0:T(8,128)(2,1)S(1)} %get-tuple-element.102), channel_id=1, source_target_pairs={{0,16},{8,24},{16,0},{24,8},{1,17},{9,25},{17,1},{25,9},{2,18},{10... | collective-permute-start | bytes 786440 | tf_op jit(solution)/shard_map/ppermute | solution.py:283
  35.8 15.0 %collective-permute-start.11 = (bf16[128,1024]{1,0:T(8,128)(2,1)S(1)}, bf16[128,1024]{1,0:T(8,128)(2,1)S(1)}, u32[]{:S(2)}, u32[]{:S(2)}) collective-permute-start(bf16[128,1024]{1,0:T(8,128)(2,1)S(1)} %get-tuple-element.103), channel_id=1, source_target_pairs={{0,24},{8,16},{16,8},{24,0},{1,25},{9,17},{17,9},{25,1},{2,26},{10... | collective-permute-start | bytes 786440 | tf_op jit(solution)/shard_map/ppermute | solution.py:283
  43.0 22.9 %collective-permute-start.6 = (bf16[1024,256]{1,0:T(8,128)(2,1)S(1)}, bf16[1024,256]{1,0:T(8,128)(2,1)}, u32[]{:S(2)}, u32[]{:S(2)}) collective-permute-start(bf16[1024,256]{1,0:T(8,128)(2,1)S(1)} %get-tuple-element.94.refs_2_), channel_id=1, source_target_pairs={{0,6},{2,0},{4,2},{6,4},{1,7},{3,1},{5,3},{7,5},{8,14},{10,8},{12,... | collective-permute-start | bytes 1572872 | tf_op jit(solution)/shard_map/ppermute | solution.py:286
  50.8 1.3 collective-permute-start.4
  56.0 6.5 %copy-start.23 = (bf16[1024,512]{1,0:T(8,128)(2,1)S(1)}, bf16[1024,512]{1,0:T(8,128)(2,1)}, u32[]{:S(2)}) copy-start(bf16[1024,512]{1,0:T(8,128)(2,1)} %refs_2_.3) | copy-start | bytes 3145732
  65.4 2.0 %collective-permute-start.12 = (bf16[512,256]{1,0:T(8,128)(2,1)}, bf16[512,256]{1,0:T(8,128)(2,1)}, u32[]{:S(2)}, u32[]{:S(2)}) collective-permute-start(bf16[512,256]{1,0:T(8,128)(2,1)} %get-tuple-element.106), channel_id=1, source_target_pairs={{0,1},{1,0},{2,3},{3,2},{4,5},{5,4},{6,7},{7,6},{8,9},{9,8},{10,11... | collective-permute-start | bytes 786440 | tf_op jit(solution)/shard_map/ppermute | solution.py:280
  65.9 23.1 %collective-permute-start.7 = (bf16[1024,256]{1,0:T(8,128)(2,1)}, bf16[1024,256]{1,0:T(8,128)(2,1)}, u32[]{:S(2)}, u32[]{:S(2)}) collective-permute-start(bf16[1024,256]{1,0:T(8,128)(2,1)} %collective-permute-done.6.refs_2_), channel_id=1, source_target_pairs={{0,6},{2,0},{4,2},{6,4},{1,7},{3,1},{5,3},{7,5},{8,14},{10,8},{12,... | collective-permute-start | bytes 1572872 | tf_op jit(solution)/shard_map/ppermute | solution.py:286
  65.9 18.5 %copy-start.1 = (bf16[1024,512]{1,0:T(8,128)(2,1)S(1)}, bf16[1024,512]{1,0:T(8,128)(2,1)}, u32[]{:S(2)}) copy-start(bf16[1024,512]{1,0:T(8,128)(2,1)} %copy-done) | copy-start | bytes 3145732
  65.9 20.4 %copy-start.7 = (bf16[1024,512]{1,0:T(8,128)(2,1)S(1)}, bf16[1024,512]{1,0:T(8,128)(2,1)}, u32[]{:S(2)}) copy-start(bf16[1024,512]{1,0:T(8,128)(2,1)} %copy-done.6) | copy-start | bytes 3145732
  65.9 20.4 %copy-start.9 = (bf16[1024,512]{1,0:T(8,128)(2,1)S(1)}, bf16[1024,512]{1,0:T(8,128)(2,1)}, u32[]{:S(2)}) copy-start(bf16[1024,512]{1,0:T(8,128)(2,1)} %copy-done.8) | copy-start | bytes 3145732
  69.5 6.4 %collective-permute-start.13 = (bf16[2,128,256]{2,1,0:T(8,128)(2,1)S(1)}, bf16[2,128,256]{2,1,0:T(8,128)(2,1)S(1)}, u32[]{:S(2)}, u32[]{:S(2)}) collective-permute-start(bf16[2,128,256]{2,1,0:T(8,128)(2,1)S(1)} %get-tuple-element.109), channel_id=1, source_target_pairs={{0,8},{8,0},{16,24},{24,16},{1,9},{9,1},{17,25},{25,17},{2,10},{10... | collective-permute-start | bytes 393224 | tf_op jit(solution)/shard_map/ppermute | solution.py:283
  70.5 7.1 %collective-permute-start.14 = (bf16[2,128,256]{2,1,0:T(8,128)(2,1)S(1)}, bf16[2,128,256]{2,1,0:T(8,128)(2,1)S(1)}, u32[]{:S(2)}, u32[]{:S(2)}) collective-permute-start(bf16[2,128,256]{2,1,0:T(8,128)(2,1)S(1)} %get-tuple-element.110), channel_id=1, source_target_pairs={{0,16},{8,24},{16,0},{24,8},{1,17},{9,25},{17,1},{25,9},{2,18},{10... | collective-permute-start | bytes 393224 | tf_op jit(solution)/shard_map/ppermute | solution.py:283
  71.7 7.1 %collective-permute-start.15 = (bf16[2,128,256]{2,1,0:T(8,128)(2,1)S(1)}, bf16[2,128,256]{2,1,0:T(8,128)(2,1)S(1)}, u32[]{:S(2)}, u32[]{:S(2)}) collective-permute-start(bf16[2,128,256]{2,1,0:T(8,128)(2,1)S(1)} %get-tuple-element.111), channel_id=1, source_target_pairs={{0,24},{8,16},{16,8},{24,0},{1,25},{9,17},{17,9},{25,1},{2,26},{10... | collective-permute-start | bytes 393224 | tf_op jit(solution)/shard_map/ppermute | solution.py:283
  74.1 12.1 %collective-permute-start.16 = (bf16[512,256]{1,0:T(8,128)(2,1)S(1)}, bf16[512,256]{1,0:T(8,128)(2,1)S(1)}, u32[]{:S(2)}, u32[]{:S(2)}) collective-permute-start(bf16[512,256]{1,0:T(8,128)(2,1)S(1)} %get-tuple-element.144), channel_id=1, source_target_pairs={{0,1},{1,0},{2,3},{3,2},{4,5},{5,4},{6,7},{7,6},{8,9},{9,8},{10,11... | collective-permute-start | bytes 786440 | tf_op jit(solution)/shard_map/ppermute | solution.py:280
  80.9 11.0 %collective-permute-start.19 = (bf16[128,1024]{1,0:T(8,128)(2,1)S(1)}, bf16[128,1024]{1,0:T(8,128)(2,1)S(1)}, u32[]{:S(2)}, u32[]{:S(2)}) collective-permute-start(bf16[128,1024]{1,0:T(8,128)(2,1)S(1)} %get-tuple-element.131), channel_id=1, source_target_pairs={{0,8},{8,0},{16,24},{24,16},{1,9},{9,1},{17,25},{25,17},{2,10},{10... | collective-permute-start | bytes 786440 | tf_op jit(solution)/shard_map/ppermute | solution.py:283
  82.0 13.0 %collective-permute-start.20 = (bf16[128,1024]{1,0:T(8,128)(2,1)S(1)}, bf16[128,1024]{1,0:T(8,128)(2,1)S(1)}, u32[]{:S(2)}, u32[]{:S(2)}) collective-permute-start(bf16[128,1024]{1,0:T(8,128)(2,1)S(1)} %get-tuple-element.132), channel_id=1, source_target_pairs={{0,16},{8,24},{16,0},{24,8},{1,17},{9,25},{17,1},{25,9},{2,18},{10... | collective-permute-start | bytes 786440 | tf_op jit(solution)/shard_map/ppermute | solution.py:283
  83.2 11.8 %collective-permute-start.21 = (bf16[128,1024]{1,0:T(8,128)(2,1)S(1)}, bf16[128,1024]{1,0:T(8,128)(2,1)S(1)}, u32[]{:S(2)}, u32[]{:S(2)}) collective-permute-start(bf16[128,1024]{1,0:T(8,128)(2,1)S(1)} %get-tuple-element.133), channel_id=1, source_target_pairs={{0,24},{8,16},{16,8},{24,0},{1,25},{9,17},{17,9},{25,1},{2,26},{10... | collective-permute-start | bytes 786440 | tf_op jit(solution)/shard_map/ppermute | solution.py:283
  86.3 23.4 %collective-permute-start.18 = (bf16[1024,512]{1,0:T(8,128)(2,1)S(1)}, bf16[1024,512]{1,0:T(8,128)(2,1)S(1)}, u32[]{:S(2)}, u32[]{:S(2)}) collective-permute-start(bf16[1024,512]{1,0:T(8,128)(2,1)S(1)} %copy-done.16), channel_id=1, source_target_pairs={{0,1},{1,0},{2,3},{3,2},{4,5},{5,4},{6,7},{7,6},{8,9},{9,8},{10,11... | collective-permute-start | bytes 3145736 | tf_op jit(solution)/shard_map/ppermute | solution.py:280
  91.8 17.2 %copy-start.19 = (bf16[512,256]{1,0:T(8,128)(2,1)}, bf16[512,256]{1,0:T(8,128)(2,1)S(1)}, u32[]{:S(2)}) copy-start(bf16[512,256]{1,0:T(8,128)(2,1)S(1)} %get-tuple-element.127) | copy-start | bytes 786436
  91.8 14.2 %collective-permute-start.23 = (bf16[1024,256]{1,0:T(8,128)(2,1)S(1)}, bf16[1024,256]{1,0:T(8,128)(2,1)S(1)}, u32[]{:S(2)}, u32[]{:S(2)}) collective-permute-start(bf16[1024,256]{1,0:T(8,128)(2,1)S(1)} %get-tuple-element.137), channel_id=1, source_target_pairs={{0,6},{2,0},{4,2},{6,4},{1,7},{3,1},{5,3},{7,5},{8,14},{10,8},{12,... | collective-permute-start | bytes 1572872 | tf_op jit(solution)/shard_map/ppermute | solution.py:286
  95.9 23.7 %collective-permute-start.22 = (bf16[1024,512]{1,0:T(8,128)(2,1)S(1)}, bf16[1024,512]{1,0:T(8,128)(2,1)S(1)}, u32[]{:S(2)}, u32[]{:S(2)}) collective-permute-start(bf16[1024,512]{1,0:T(8,128)(2,1)S(1)} %get-tuple-element.134.refs_3_), channel_id=1, source_target_pairs={{0,1},{1,0},{2,3},{3,2},{4,5},{5,4},{6,7},{7,6},{8,9},{9,8},{10,11... | collective-permute-start | bytes 3145736 | tf_op jit(solution)/shard_map/ppermute | solution.py:280
  95.9 3.0 %collective-permute-start.17 = (bf16[512,256]{1,0:T(8,128)(2,1)S(1)}, bf16[512,256]{1,0:T(8,128)(2,1)S(1)}, u32[]{:S(2)}, u32[]{:S(2)}) collective-permute-start(bf16[512,256]{1,0:T(8,128)(2,1)S(1)} %get-tuple-element.128), channel_id=1, source_target_pairs={{0,1},{1,0},{2,3},{3,2},{4,5},{5,4},{6,7},{7,6},{8,9},{9,8},{10,11... | collective-permute-start | bytes 786440 | tf_op jit(solution)/shard_map/ppermute | solution.py:280
  106.1 13.4 %collective-permute-start.24 = (bf16[1024,256]{1,0:T(8,128)(2,1)S(1)}, bf16[1024,256]{1,0:T(8,128)(2,1)S(1)}, u32[]{:S(2)}, u32[]{:S(2)}) collective-permute-start(bf16[1024,256]{1,0:T(8,128)(2,1)S(1)} %pass.1), channel_id=1, source_target_pairs={{0,6},{2,0},{4,2},{6,4},{1,7},{3,1},{5,3},{7,5},{8,14},{10,8},{12,... | collective-permute-start | bytes 1572872 | tf_op jit(solution)/shard_map/ppermute | solution.py:286
  109.7 40.8 %copy-start.20 = (bf16[512,256]{1,0:T(8,128)(2,1)S(1)}, bf16[512,256]{1,0:T(8,128)(2,1)}, u32[]{:S(2)}) copy-start(bf16[512,256]{1,0:T(8,128)(2,1)} %copy-done.19) | copy-start | bytes 786436
  121.4 6.4 %collective-permute-start.25 = (bf16[256,256]{1,0:T(8,128)(2,1)S(1)}, bf16[256,256]{1,0:T(8,128)(2,1)S(1)}, u32[]{:S(2)}, u32[]{:S(2)}) collective-permute-start(bf16[256,256]{1,0:T(8,128)(2,1)S(1)} %get-tuple-element.139), channel_id=1, source_target_pairs={{0,8},{8,0},{16,24},{24,16},{1,9},{9,1},{17,25},{25,17},{2,10},{10... | collective-permute-start | bytes 393224 | tf_op jit(solution)/shard_map/ppermute | solution.py:283
  122.5 7.5 %collective-permute-start.26 = (bf16[256,256]{1,0:T(8,128)(2,1)S(1)}, bf16[256,256]{1,0:T(8,128)(2,1)S(1)}, u32[]{:S(2)}, u32[]{:S(2)}) collective-permute-start(bf16[256,256]{1,0:T(8,128)(2,1)S(1)} %get-tuple-element.140), channel_id=1, source_target_pairs={{0,16},{8,24},{16,0},{24,8},{1,17},{9,25},{17,1},{25,9},{2,18},{10... | collective-permute-start | bytes 393224 | tf_op jit(solution)/shard_map/ppermute | solution.py:283
  123.8 6.3 %collective-permute-start.27 = (bf16[256,256]{1,0:T(8,128)(2,1)S(1)}, bf16[256,256]{1,0:T(8,128)(2,1)S(1)}, u32[]{:S(2)}, u32[]{:S(2)}) collective-permute-start(bf16[256,256]{1,0:T(8,128)(2,1)S(1)} %get-tuple-element.141), channel_id=1, source_target_pairs={{0,24},{8,16},{16,8},{24,0},{1,25},{9,17},{17,9},{25,1},{2,26},{10... | collective-permute-start | bytes 393224 | tf_op jit(solution)/shard_map/ppermute | solution.py:283
  130.1 5.0 %collective-permute-start.28 = (bf16[256,256]{1,0:T(8,128)(2,1)S(1)}, bf16[256,256]{1,0:T(8,128)(2,1)S(1)}, u32[]{:S(2)}, u32[]{:S(2)}) collective-permute-start(bf16[256,256]{1,0:T(8,128)(2,1)S(1)} %sum.3.refs_0_), channel_id=1, source_target_pairs={{0,2},{2,0},{4,6},{6,4},{1,3},{3,1},{5,7},{7,5},{8,10},{10,8},{12,... | collective-permute-start | bytes 393224 | tf_op jit(solution)/shard_map/ppermute | solution.py:457
  135.2 5.9 %collective-permute-start.29 = (bf16[256,256]{1,0:T(8,128)(2,1)S(1)}, bf16[256,256]{1,0:T(8,128)(2,1)S(1)}, u32[]{:S(2)}, u32[]{:S(2)}) collective-permute-start(bf16[256,256]{1,0:T(8,128)(2,1)S(1)} %sum.4.refs_0_), channel_id=1, source_target_pairs={{0,4},{2,6},{4,0},{6,2},{1,5},{3,7},{5,1},{7,3},{8,12},{10,14},{12... | collective-permute-start | bytes 393224 | tf_op jit(solution)/shard_map/ppermute | solution.py:457
  141.2 5.0 %collective-permute-start.30 = (bf16[256,256]{1,0:T(8,128)(2,1)S(1)}, bf16[256,256]{1,0:T(8,128)(2,1)S(1)}, u32[]{:S(2)}, u32[]{:S(2)}) collective-permute-start(bf16[256,256]{1,0:T(8,128)(2,1)S(1)} %sum.5.refs_1_), channel_id=1, source_target_pairs={{0,8},{8,0},{16,24},{24,16},{1,9},{9,1},{17,25},{25,17},{2,10},{10... | collective-permute-start | bytes 393224 | tf_op jit(solution)/shard_map/ppermute | solution.py:283
  142.0 6.5 %collective-permute-start.31 = (bf16[256,256]{1,0:T(8,128)(2,1)S(1)}, bf16[256,256]{1,0:T(8,128)(2,1)S(1)}, u32[]{:S(2)}, u32[]{:S(2)}) collective-permute-start(bf16[256,256]{1,0:T(8,128)(2,1)S(1)} %sum.5.refs_1_), channel_id=1, source_target_pairs={{0,16},{8,24},{16,0},{24,8},{1,17},{9,25},{17,1},{25,9},{2,18},{10... | collective-permute-start | bytes 393224 | tf_op jit(solution)/shard_map/ppermute | solution.py:283
  144.6 5.9 %collective-permute-start.32 = (bf16[256,256]{1,0:T(8,128)(2,1)S(1)}, bf16[256,256]{1,0:T(8,128)(2,1)S(1)}, u32[]{:S(2)}, u32[]{:S(2)}) collective-permute-start(bf16[256,256]{1,0:T(8,128)(2,1)S(1)} %sum.5.refs_1_), channel_id=1, source_target_pairs={{0,24},{8,16},{16,8},{24,0},{1,25},{9,17},{17,9},{25,1},{2,26},{10... | collective-permute-start | bytes 393224 | tf_op jit(solution)/shard_map/ppermute | solution.py:283
  144.7 6.6 %collective-permute-start.33 = (bf16[256,256]{1,0:T(8,128)(2,1)S(1)}, bf16[256,256]{1,0:T(8,128)(2,1)S(1)}, u32[]{:S(2)}, u32[]{:S(2)}) collective-permute-start(bf16[256,256]{1,0:T(8,128)(2,1)S(1)} %sum.5.refs_1_), channel_id=1, source_target_pairs={{0,1},{1,0},{2,3},{3,2},{4,5},{5,4},{6,7},{7,6},{8,9},{9,8},{10,11... | collective-permute-start | bytes 393224 | tf_op jit(solution)/shard_map/ppermute | solution.py:280
  146.2 5.1 %collective-permute-start.34 = (bf16[256,256]{1,0:T(8,128)(2,1)S(1)}, bf16[256,256]{1,0:T(8,128)(2,1)S(1)}, u32[]{:S(2)}, u32[]{:S(2)}) collective-permute-start(bf16[256,256]{1,0:T(8,128)(2,1)S(1)} %collective-permute-done.30.refs_2_), channel_id=1, source_target_pairs={{0,1},{1,0},{2,3},{3,2},{4,5},{5,4},{6,7},{7,6},{8,9},{9,8},{10,11... | collective-permute-start | bytes 393224 | tf_op jit(solution)/shard_map/ppermute | solution.py:280
  148.5 2.8 %collective-permute-start.35 = (bf16[256,256]{1,0:T(8,128)(2,1)S(1)}, bf16[256,256]{1,0:T(8,128)(2,1)S(1)}, u32[]{:S(2)}, u32[]{:S(2)}) collective-permute-start(bf16[256,256]{1,0:T(8,128)(2,1)S(1)} %collective-permute-done.31.refs_3_), channel_id=1, source_target_pairs={{0,1},{1,0},{2,3},{3,2},{4,5},{5,4},{6,7},{7,6},{8,9},{9,8},{10,11... | collective-permute-start | bytes 393224 | tf_op jit(solution)/shard_map/ppermute | solution.py:280
  150.4 1.3 collective-permute-start.36
  (15 other events, 28.4 us)

commit v10 on v9

--- a/solution.py
+++ b/solution.py
@@ -57,7 +57,7 @@
         out_specs=tuple(vmem for _ in outs),
         scratch_shapes=list(scratch),
         compiler_params=pltpu.CompilerParams(vmem_limit_bytes=size + (5 << 20)),
-        cost_estimate=pl.CostEstimate(flops=int(us * 2e7), bytes_accessed=0, transcendentals=0),
+        cost_estimate=pl.CostEstimate(flops=int(us * 1e8), bytes_accessed=0, transcendentals=0),
         name=name,
     )(*(value for _, value in ins), *after)
 
@@ -71,10 +71,6 @@
         self.piece = self.grp * self.pair
         self.per_grp = self.dom * self.pair
         assert rows // 128 < 5 and self.pair <= 128
-
-    def before(self, d):
-        inner = d % self.dom
-        return d - inner + (inner - 2) % self.dom
 
 
 def column(row):
@@ -101,8 +97,7 @@
     want = (dot(owner, high) * 16.0 + dot(owner, low)).astype(I32)
     out_ref[...] = jnp.zeros_like(out_ref)
     for d in range(z.grp * z.dom):
-        near = z.before(d)
-        for line, source in ((0, d), (5, d ^ 1), (6, near), (7, near ^ 1)):
+        for line, source in ((0, d), (5, d ^ 1)):
             out_ref[d, line:line + 1, 0:z.pair] = want[source:source + 1, :]
     across_grp = (source_r >> log2(z.dom)) ^ me_ref[0]
     inner = source_r & (z.dom - 1)
@@ -146,14 +141,25 @@
 
 
 def pack_kernel(z, *refs):
-    ins, out = refs[:-1], refs[-1]
-    for rel in range(2):
+    ins, outs = refs[:z.grp], refs[z.grp:]
+    for rel, out in enumerate(outs):
         for s in range(z.grp):
-            at = (rel * z.grp + s) * z.per_grp
-            out[at:at + z.per_grp, :] = ins[s][rel]
-
-
-def place_kernel(z, me_ref, message_ref, out_ref):
+            out[s * z.per_grp:(s + 1) * z.per_grp, :] = ins[s][rel]
+
+
+def prepare_kernel(z, me_ref, cols_ref, message_ref, vals_ref, *refs):
+    outs, (total, dense) = refs[:z.zz], refs[z.zz:]
+    tiles, blocks, tile, _ = vals_ref.shape
+
+    @pl.loop(0, tiles)
+    def _(t):
+        total[...] = jnp.zeros_like(total)
+        for k in range(blocks):
+            at = pl.multiple_of(cols_ref[t, k] * tile, tile)
+            total[pl.ds(at, tile), :] += vals_ref[t, k].T.astype(F32)
+        left = pl.multiple_of(t * tile, tile)
+        dense[:, pl.ds(left, tile)] = total[pl.ds(0, z.dom * z.rows), :].astype(BF16)
+
     @pl.loop(0, z.dom)
     def _(n):
         message = message_ref[me_ref[0] * z.dom + n]
@@ -162,28 +168,9 @@
         s, at = at & (z.grp - 1), at >> log2(z.grp)
         k, rel = (me_ref[1] - (at >> 1)) & (z.zz - 1), (at & 1) ^ me_ref[2]
         slot = ((k * 2 + rel) * z.grp + s) * z.pair + rank
-        out_ref[n] = one_hot(iota((z.rows, z.rows), 0) == slot)
-
-
-def dense_kernel(cols_ref, vals_ref, out_ref, total):
-    tiles, blocks, tile, _ = vals_ref.shape
-    count = out_ref.shape[0]
-
-    @pl.loop(0, tiles)
-    def _(t):
-        total[...] = jnp.zeros_like(total)
-        for k in range(blocks):
-            at = pl.multiple_of(cols_ref[t, k] * tile, tile)
-            total[pl.ds(at, tile), :] += vals_ref[t, k].T.astype(F32)
-        left = pl.multiple_of(t * tile, tile)
-        out_ref[:, pl.ds(left, tile)] = total[pl.ds(0, count), :].astype(BF16)
-
-
-def arrange_kernel(z, place_ref, dense_ref, *outs):
-    @pl.loop(0, z.dom)
-    def _(n):
+        place = one_hot(iota((z.rows, z.rows), 0) == slot)
         at = pl.multiple_of(n * z.rows, z.rows)
-        part = dot(place_ref[n], dense_ref[pl.ds(at, z.rows), :]).astype(BF16)
+        part = dot(place, dense[pl.ds(at, z.rows), :]).astype(BF16)
         for k in range(z.zz):
             for p in range(2 * z.grp):
                 first = (k * 2 * z.grp + p) * z.pair
@@ -203,7 +190,7 @@
 
 def forward_kernel(z, first, last, *refs):
     turned, refs = refs[:2], refs[2:]
-    rows, refs = refs[0][...], refs[1:]
+    rows, refs = jnp.concatenate([ref[...] for ref in refs[:2]], axis=0), refs[2:]
     agg = [dot_rows(ref[...], rows) for ref in turned]
     if not first:
         agg = [part + ref[...] for part, ref in zip(agg, refs)]
@@ -217,25 +204,28 @@
         sig = jax.nn.sigmoid(part)
         hidden[...] = (part * sig).astype(BF16)
         grad[...] = (cot[...].astype(F32) * (sig * (1.0 + part * (1.0 - sig)))).astype(BF16)
-    back_kernel(*ahead, *grads, refs[-1])
-
-
-def back_kernel(turned_a, turned_b, grad_a, grad_b, out):
-    value = dot(turned_a[...], grad_a[...]) + dot(turned_b[...], grad_b[...])
-    out[...] = value.astype(out.dtype)
+    back_kernel(*ahead, *grads, *refs[-2:])
+
+
+def back_kernel(turned_a, turned_b, grad_a, grad_b, *outs):
+    size = outs[0].shape[0]
+    for i, out in enumerate(outs):
+        rows = pl.ds(i * size, size)
+        value = dot(turned_a[rows, :], grad_a[...]) + dot(turned_b[rows, :], grad_b[...])
+        out[...] = value.astype(out.dtype)
 
 
 def pass_kernel(mine_ref, come_ref, out_ref):
     out_ref[...] = (mine_ref[...] + come_ref[...].astype(F32)).astype(BF16)
 
 
-def grad_kernel(z, me_ref, own_a, own_b, near_a, near_b, own_ref, mine_ref, come_ref, *refs):
+def grad_kernel(z, me_ref, left_a, left_b, mine_a, mine_b, come_a, come_b, *refs):
     outs, whole = refs[:-1], refs[-1]
-    own = own_ref[...].astype(BF16)
-    near = (mine_ref[...] + come_ref[...].astype(F32)).astype(BF16)
-    total = dot(own_a[...], own[:z.rows]) + dot(own_b[...], own[z.rows:])
-    total = total + dot(near_a[...], near[:z.rows]) + dot(near_b[...], near[z.rows:])
-    whole[...] = total.astype(BF16)
+    grads = [
+        (mine[...] + come[...].astype(F32)).astype(BF16)
+        for mine, come in ((mine_a, come_a), (mine_b, come_b))
+    ]
+    whole[...] = (dot(left_a[...], grads[0]) + dot(left_b[...], grads[1])).astype(BF16)
     share = whole.shape[0] // z.grp
     for s in range(z.grp):
         at = pl.multiple_of((me_ref[0] ^ s) * share, share)
@@ -256,17 +246,6 @@
             out[pl.ds(at, share), pl.ds(left, half)] = pieces[rel * z.grp + s][...].astype(F32)
 
 
-def arrange(z, place, dense, wide, after=()):
-    inner = (wide, z.rows) if z.pair % 16 == 0 else (2 * z.grp, z.dom, z.pair, z.rows)
-    *got, token = call(
-        lambda *refs: arrange_kernel(z, *refs),
-        [(inner, BF16)] * z.zz,
-        [("v", place), ("v", dense)],
-        "arrange", 4, after=after, token=True,
-    )
-    return [part.reshape(wide, z.rows) for part in got], token
-
-
 def shards(features, node_order, block_cols, block_count, block_vals, weight, cotangent):
     rows, width_in = features.shape
     hidden_units = weight.shape[1]
@@ -303,7 +282,7 @@
             lambda *refs: product_kernel(z, *refs),
             [((rows, half), BF16)] * 2,
             [("s", me), ("v", part), ("v", weight)],
-            "product", 75, after=after,
+            "product", 15, after=after,
         )
         return own, to_core(other)
 
@@ -321,7 +300,7 @@
     def pack(parts, after=()):
         return call(
             lambda *refs: pack_kernel(z, *refs),
-            [((2 * rows, half), BF16)],
+            [((rows, half), BF16)] * 2,
             [("v", part) for part in parts],
             "pack", 0.5, after=after, token=True,
         )
@@ -343,12 +322,9 @@
 
     products = products_of(features)
     pick, *got, token = send_of((0, 5), products)
-    token, cotangent, block_cols, late = lax.optimization_barrier(
-        (token, cotangent, block_cols, features)
-    )
-    came = across(got)
-
-    near = to_zz(late, 1)
+    token, cotangent = lax.optimization_barrier((token, cotangent))
+    *ring, token = pack(across(got), [token])
+    ring = [ring]
 
     live = iota((tiles, blocks), 1) < block_count[:, None]
     cols_a = jnp.where(live, block_cols, z.dom * tiles)
@@ -356,81 +332,71 @@
     cot_a = lax.dynamic_slice_in_dim(cotangent, core * half, half, axis=1)
     cot_b = to_core(lax.dynamic_slice_in_dim(cotangent, (1 - core) * half, half, axis=1))
 
-    place, token_p = call(
-        lambda *refs: place_kernel(z, *refs),
-        [((z.dom, rows, rows), BF16)],
-        [("s", me), ("v", message)],
-        "place", 1.5, after=[token], token=True,
-    )
-
-    def dense_of(cols, vals, after=()):
-        return call(
-            dense_kernel,
-            [((z.dom * rows, rows), BF16)],
-            [("s", cols), ("v", vals)],
-            "dense", 2.5,
-            (pltpu.VMEM((z.dom * rows + tile, tile), F32),), after=after, token=True,
-        )
-
-    dense_a, token_a = dense_of(cols_a, block_vals)
-
     wide = 2 * z.grp * z.per_grp
-    first, token = pack(came, [token_p, token_a])
-    ring = {0: first}
-    *picked, token_r = rows_of(pick, features, [token])
-    held = across(picked)
-    turned_a, token = arrange(z, place, dense_a, wide, [token_r])
-    dense_b, token = dense_of(cols_b, vals_b, [token])
-    turned_b, token = arrange(z, place, dense_b, wide)
-    turned = (turned_a, turned_b)
-    lefts, token_l = turned_of(held)
-    products = products_of(near, [token, token_l])
-    order = list(range(z.zz - 1, 1, -1))
-    for k in order:
-        ring[k] = to_zz(ring[(k + 1) % z.zz], -1)
-        if k == order[0]:
-            ring[k], token = lax.optimization_barrier((ring[k], token))
-            pick_near, *got, _ = send_of((6, 7), products, [token])
-    ring[1], token_k = pack(across(got))
-    *picked, token_r = rows_of(pick_near, near, [token_k])
-    held_near = across(picked)
+    inner = (wide, rows) if z.pair % 16 == 0 else (2 * z.grp, z.dom, z.pair, rows)
+
+    def prepared(cols, vals, token):
+        *got, token = call(
+            lambda *refs: prepare_kernel(z, *refs),
+            [(inner, BF16)] * z.zz,
+            [("s", me), ("s", cols), ("v", message), ("v", vals)],
+            "prepare", 7,
+            (
+                pltpu.VMEM((z.dom * rows + tile, tile), F32),
+                pltpu.VMEM((z.dom * rows, rows), BF16),
+            ),
+            after=[token], token=True,
+        )
+        return [part.reshape(wide, rows) for part in got], token
+
+    turned = []
+    for k in range(1, z.zz):
+        ring.append([to_zz(part, 1) for part in ring[-1]])
+        if k < 3:
+            got, token = prepared(*((cols_a, block_vals), (cols_b, vals_b))[k - 1], token)
+            turned.append(got)
+            ring[k][0], token = lax.optimization_barrier((ring[k][0], token))
 
     agg = []
-    order = [0] + order[:-1] + [1] + order[-1:]
-    for k in order:
-        last = k == order[-1]
-        ins = [("v", part) for part in (turned[0][k], turned[1][k], ring[k], *agg)]
+    for k in range(z.zz):
+        last = k == z.zz - 1
+        ins = [("v", part) for part in (turned[0][k], turned[1][k], *ring[k], *agg)]
         outs = [((rows, half), F32)] * 2
         if last:
-            ahead = (turned[0][z.zz - 1], turned[1][z.zz - 1])
+            ahead = (turned[0][k], turned[1][k])
             ins += [("v", part) for part in (cot_a, cot_b, *ahead)]
-            outs = [((rows, half), BF16)] * 4 + [((wide, half), BF16)]
+            outs = [((rows, half), BF16)] * 6
         agg = call(
             lambda *refs, k=k, last=last: forward_kernel(z, k == 0, last, *refs),
             outs, ins, "forward", 3 if last else 1,
-            after=[token_r] if last else [cot_a, cot_b] if k == order[1] else (),
-        )
-    hidden_a, hidden_b, grad_a, grad_b, came = agg
+            after=[cot_a, cot_b] if k == z.zz - 2 else (),
+        )
+    hidden_a, hidden_b, grad_a, grad_b, *came = agg
 
     def back(k):
         return call(
             back_kernel,
-            [((wide, half), F32)],
+            [((rows, half), F32)] * 2,
             [("v", part) for part in (turned[0][k], turned[1][k], grad_a, grad_b)],
             "back", 1,
-        )[0]
+        )
 
     come = to_core(hidden_b)
-    for k in range(z.zz - 2, 0, -1):
-        came = to_zz(came, -1)
+    for k in range(z.zz - 2, -1, -1):
+        came = [to_zz(part, -1) for part in came]
         mine = back(k)
-        if k == 1:
-            break
-        (came,) = call(
-            pass_kernel, [((wide, half), BF16)], [("v", mine), ("v", came)], "pass", 0.5,
-            after=[come],
-        )
-    lefts += turned_of(held_near)[0]
+        if k:
+            passed = [
+                call(
+                    pass_kernel, [((rows, half), BF16)], [("v", part), ("v", moved)], "pass", 0.5,
+                    after=[come] if i == 1 and k == 1 else (), token=True,
+                )
+                for i, (part, moved) in enumerate(zip(mine, came))
+            ]
+            came = [part for part, _ in passed]
+            if k == z.zz - 2:
+                *picked, _ = rows_of(pick, features, [passed[1][1]])
+                lefts, _ = turned_of(across(picked))
     first = core == 0
     hidden = jnp.concatenate(
         [jnp.where(first, hidden_a, come), jnp.where(first, come, hidden_a)], axis=1
@@ -440,7 +406,7 @@
     terms = call(
         lambda *refs: grad_kernel(z, *refs),
         [((share, half), BF16)] * z.grp,
-        [("s", me)] + [("v", part) for part in (*lefts, back(0), mine, came)],
+        [("s", me)] + [("v", part) for part in (*lefts, *mine, *came)],
         "grad", 1.5,
         (pltpu.VMEM((width_in, half), BF16),),
     )

time: 154 us -> 169 us (1.097)
  waiting for transfers between devices: 54.1 us -> 71 us
  starting transfers between devices: 32.2 us -> 41.7 us
  local copies, waits for them, and re-layouts: 12.4 us -> 6.05 us
  Pallas kernels: 37.8 us -> 33 us
    ppermute x5 -> x12, waiting for transfers between devices: 17 us -> 35.9 us  [to_zz(): lax.ppermute(x, 'zz', [(i, (i + k) % z.zz) for i in range(z.zz)])]
    ppermute x5 -> x12, starting transfers between devices: 6.11 us -> 22.5 us  [to_zz(): lax.ppermute(x, 'zz', [(i, (i + k) % z.zz) for i in range(z.zz)])]
    unnamed x52 -> x30, local copies, waits for them, and re-layouts: 11.4 us -> 4.93 us
    ppermute x18 -> x12, starting transfers between devices: 21.3 us -> 15.2 us  [to_grp(): lax.ppermute(x, 'grp', [(i, i ^ s) for i in range(z.grp)])]
    pallas_call x29 -> x24, Pallas kernels: 37.8 us -> 33 us  [call(): pl.pallas_call(kernel, out_shape=tuple((jax.ShapeDtypeStruct(s, d) for s,...]
    ppermute x12 -> x10, waiting for transfers between devices: 3.76 us -> 1.63 us  [to_core(): return lax.ppermute(x, 'core', [(0, 1), (1, 0)])]
    ppermute x18 -> x12, waiting for transfers between devices: 25.4 us -> 25.5 us  [to_grp(): lax.ppermute(x, 'grp', [(i, i ^ s) for i in range(z.grp)])]
  transfers between devices with their start and end apart: 37 -> 36, of which waited for: 18 -> 21; matrix products, arithmetic and copies ran while one was open for 1% -> 1% of each run, Pallas kernels for 20% -> 14%
where the time goes in v10:
time: 169 us
  waiting for transfers between devices  71 us (42%)
  starting transfers between devices  41.7 us (25%)
  Pallas kernels  33 us (20%)
  blocking collectives  15.3 us (9%)
  local copies, waits for them, and re-layouts  6.05 us (4%)
    ppermute x12, waiting for transfers between devices, to_zz(): lax.ppermute(x, 'zz', [(i, (i + k) % z.zz) for i in range(z.zz)])  35.9 us
    pallas_call x24, Pallas kernels, call(): pl.pallas_call(kernel, out_shape=tuple((jax.ShapeDtypeStruct(s, d) for s,...  33 us
    ppermute x12, waiting for transfers between devices, to_grp(): lax.ppermute(x, 'grp', [(i, i ^ s) for i in range(z.grp)])  25.5 us
    ppermute x12, starting transfers between devices, to_zz(): lax.ppermute(x, 'zz', [(i, (i + k) % z.zz) for i in range(z.zz)])  22.5 us
    all_to_all x1, blocking collectives, shards(): lax.all_to_all(message, ('grp', 'zz', 'core'), split_axis=0, concat_axis=...  15.3 us
    ppermute x12, starting transfers between devices, to_grp(): lax.ppermute(x, 'grp', [(i, i ^ s) for i in range(z.grp)])  15.2 us
    ppermute x2, waiting for transfers between devices, shards(): lax.ppermute(mine, 'zz', [(i, i ^ step) for i in range(z.zz)])  7.98 us
    unnamed x30, local copies, waits for them, and re-layouts  4.93 us
  transfers between devices with their start and end apart: 36, of which 21 were waited for; matrix products, arithmetic and copies ran while one was open for 1% of the time, Pallas kernels for 14%

profile of v10, /device:TPU:0, one launch (start us, length us, event | category | flops | bytes accessed | tf_op | source)
XLA Modules:
  0.0 169.0 jit_solution(1946935931603052076)
XLA Ops:
  1.9 1.1 index.1
  3.0 1.2 copy-done.2
  4.3 1.2 copy-done.11
  5.5 1.3 product.1
  6.9 15.3 %all_to_all.5.refs_1_.refs_2_ = s32[32,8,128]{2,1,0:T(8,128)S(1)} all-to-all(s32[32,8,128]{2,1,0:T(8,128)S(1)} %index.1), channel_id=1, replica_groups=mesh['grp'=4,'zz'=4,'core'=2] {'grp','zz','core'}, dimensions={0} | all-to-all | bytes 262144 | tf_op jit(solution)/shard_map/all_to_all | solution.py:275
  22.1 1.7 send.1
  26.1 2.0 %collective-permute-start.3 = (bf16[2,128,256]{2,1,0:T(8,128)(2,1)S(1)}, bf16[2,128,256]{2,1,0:T(8,128)(2,1)S(1)}, u32[]{:S(2)}, u32[]{:S(2)}) collective-permute-start(bf16[2,128,256]{2,1,0:T(8,128)(2,1)S(1)} %get-tuple-element.67), channel_id=1, source_target_pairs={{0,24},{8,16},{16,8},{24,0},{1,25},{9,17},{17,9},{25,1},{2,26},{10... | collective-permute-start | bytes 393224 | tf_op jit(solution)/shard_map/ppermute | solution.py:262
  28.1 2.8 %collective-permute-done.1.refs_1_ = bf16[2,128,256]{2,1,0:T(8,128)(2,1)S(1)} collective-permute-done((bf16[2,128,256]{2,1,0:T(8,128)(2,1)S(1)}, bf16[2,128,256]{2,1,0:T(8,128)(2,1)S(1)}, u32[]{:S(2)}, u32[]{:S(2)}) %collective-permute-start.1) | collective-permute-done | bytes 131104 | tf_op jit(solution)/shard_map/ppermute | solution.py:262
  30.9 2.3 %collective-permute-done.2.refs_2_ = bf16[2,128,256]{2,1,0:T(8,128)(2,1)S(1)} collective-permute-done((bf16[2,128,256]{2,1,0:T(8,128)(2,1)S(1)}, bf16[2,128,256]{2,1,0:T(8,128)(2,1)S(1)}, u32[]{:S(2)}, u32[]{:S(2)}) %collective-permute-start.2) | collective-permute-done | bytes 131104 | tf_op jit(solution)/shard_map/ppermute | solution.py:262
  34.7 5.9 %prepare.2 = (bf16[1024,512]{1,0:T(8,128)(2,1)S(1)}, bf16[1024,512]{1,0:T(8,128)(2,1)S(1)}, bf16[1024,512]{1,0:T(8,128)(2,1)S(1)}, bf16[1024,512]{1,0:T(8,128)(2,1)S(1)}, f32[8,128]{1,0:T(8,128)S(1)}) custom-call(s32[3]{0:T(128)S(1)} %pad_add_fusion.refs_0_, s32[4,16]{1,0:T(4,128)S(1)} %fusion.refs_1_, s32[32,8,128]{2,1,0:T(8,128)S(1)} %all_to_all.5.refs_1_.refs_2_, ...), custom_call_target="tpu_custom_call" | custom-call | flops 700000000 | tf_op jit(solution)/shard_map/prepare/pallas_call | solution.py:52
  41.5 2.8 %collective-permute-done.6.refs_2_ = bf16[512,256]{1,0:T(8,128)(2,1)S(1)} collective-permute-done((bf16[512,256]{1,0:T(8,128)(2,1)S(1)}, bf16[512,256]{1,0:T(8,128)(2,1)S(1)}, u32[]{:S(2)}, u32[]{:S(2)}) %collective-permute-start.6) | collective-permute-done | bytes 262176 | tf_op jit(solution)/shard_map/ppermute | solution.py:265
  44.4 5.7 %collective-permute-done.9.refs_3_ = bf16[512,256]{1,0:T(8,128)(2,1)} collective-permute-done((bf16[512,256]{1,0:T(8,128)(2,1)S(1)}, bf16[512,256]{1,0:T(8,128)(2,1)}, u32[]{:S(2)}, u32[]{:S(2)}) %collective-permute-start.9) | collective-permute-done | bytes 262176 | tf_op jit(solution)/shard_map/ppermute | solution.py:265
  50.1 1.1 constant_dynamic-slice_fusion
  51.3 4.4 %collective-permute-done.7.refs_2_ = bf16[512,256]{1,0:T(8,128)(2,1)} collective-permute-done((bf16[512,256]{1,0:T(8,128)(2,1)S(1)}, bf16[512,256]{1,0:T(8,128)(2,1)}, u32[]{:S(2)}, u32[]{:S(2)}) %collective-permute-start.7) | collective-permute-done | bytes 262176 | tf_op jit(solution)/shard_map/ppermute | solution.py:265
  55.7 5.7 %collective-permute-done.10.refs_3_ = bf16[512,256]{1,0:T(8,128)(2,1)} collective-permute-done((bf16[512,256]{1,0:T(8,128)(2,1)}, bf16[512,256]{1,0:T(8,128)(2,1)}, u32[]{:S(2)}, u32[]{:S(2)}) %collective-permute-start.10) | collective-permute-done | bytes 262176 | tf_op jit(solution)/shard_map/ppermute | solution.py:265
  61.5 1.2 collective-permute-done.4.refs_1_
  62.6 7.5 %prepare.3 = (bf16[1024,512]{1,0:T(8,128)(2,1)S(1)}, bf16[1024,512]{1,0:T(8,128)(2,1)S(1)}, bf16[1024,512]{1,0:T(8,128)(2,1)S(1)}, bf16[1024,512]{1,0:T(8,128)(2,1)S(1)}, f32[8,128]{1,0:T(8,128)}) custom-call(s32[3]{0:T(128)S(1)} %pad_add_fusion.refs_0_, s32[4,16]{1,0:T(4,128)S(1)} %collective-permute-done.4.refs_1_, ...), custom_call_target="tpu_custom_call" | custom-call | flops 700000000 | tf_op jit(solution)/shard_map/prepare/pallas_call | solution.py:52
  70.8 1.7 %forward.5 = (f32[512,256]{1,0:T(8,128)S(1)}, f32[512,256]{1,0:T(8,128)S(1)}) custom-call(bf16[1024,512]{1,0:T(8,128)(2,1)S(1)} %get-tuple-element.80.refs_0_, bf16[1024,512]{1,0:T(8,128)(2,1)S(1)} %get-tuple-element.81.refs_1_, bf16[512,256]{1,0:T(8,128)(2,1)S(1)} %collective-permute-done.6.refs_2_, bf16[512,256]{1,0:T(8,128)(2,1)} %collective-permute-done.9.refs_3_, ...), custom_call_target="tpu_custom_call" | custom-call | flops 100000000 | tf_op jit(solution)/shard_map/forward/pallas_call | solution.py:52
  72.6 1.9 %forward.6 = (f32[512,256]{1,0:T(8,128)S(1)}, f32[512,256]{1,0:T(8,128)S(1)}) custom-call(bf16[1024,512]{1,0:T(8,128)(2,1)S(1)} %get-tuple-element.78.refs_0_, bf16[1024,512]{1,0:T(8,128)(2,1)S(1)} %get-tuple-element.79.refs_1_, bf16[512,256]{1,0:T(8,128)(2,1)} %collective-permute-done.7.refs_2_, bf16[512,256]{1,0:T(8,128)(2,1)} %collective-permute-done.10.refs_3_, ...), custom_call_target="tpu_custom_call" | custom-call | flops 100000000 | tf_op jit(solution)/shard_map/forward/pallas_call | solution.py:52
  74.5 1.6 forward.7
  76.1 3.9 %collective-permute-start.14 = (bf16[512,256]{1,0:T(8,128)(2,1)S(1)}, bf16[512,256]{1,0:T(8,128)(2,1)S(1)}, u32[]{:S(2)}, u32[]{:S(2)}) collective-permute-start(bf16[512,256]{1,0:T(8,128)(2,1)S(1)} %get-tuple-element.97), channel_id=1, source_target_pairs={{0,6},{2,0},{4,2},{6,4},{1,7},{3,1},{5,3},{7,5},{8,14},{10,8},{12,... | collective-permute-start | bytes 786440 | tf_op jit(solution)/shard_map/ppermute | solution.py:265
  80.7 5.2 %collective-permute-done.14.refs_1_ = bf16[512,256]{1,0:T(8,128)(2,1)S(1)} collective-permute-done((bf16[512,256]{1,0:T(8,128)(2,1)S(1)}, bf16[512,256]{1,0:T(8,128)(2,1)S(1)}, u32[]{:S(2)}, u32[]{:S(2)}) %collective-permute-start.14) | collective-permute-done | bytes 262176 | tf_op jit(solution)/shard_map/ppermute | solution.py:265
  86.0 1.2 rows.1
  87.2 1.7 %collective-permute-start.15 = (bf16[128,1024]{1,0:T(8,128)(2,1)S(1)}, bf16[128,1024]{1,0:T(8,128)(2,1)S(1)}, u32[]{:S(2)}, u32[]{:S(2)}) collective-permute-start(bf16[128,1024]{1,0:T(8,128)(2,1)S(1)} %get-tuple-element.100), channel_id=1, source_target_pairs={{0,8},{8,0},{16,24},{24,16},{1,9},{9,1},{17,25},{25,17},{2,10},{10... | collective-permute-start | bytes 786440 | tf_op jit(solution)/shard_map/ppermute | solution.py:262
  88.9 1.8 %collective-permute-start.17 = (bf16[128,1024]{1,0:T(8,128)(2,1)S(1)}, bf16[128,1024]{1,0:T(8,128)(2,1)S(1)}, u32[]{:S(2)}, u32[]{:S(2)}) collective-permute-start(bf16[128,1024]{1,0:T(8,128)(2,1)S(1)} %get-tuple-element.102), channel_id=1, source_target_pairs={{0,24},{8,16},{16,8},{24,0},{1,25},{9,17},{17,9},{25,1},{2,26},{10... | collective-permute-start | bytes 786440 | tf_op jit(solution)/shard_map/ppermute | solution.py:262
  90.7 5.8 %collective-permute-done.15.refs_1_ = bf16[128,1024]{1,0:T(8,128)(2,1)S(1)} collective-permute-done((bf16[128,1024]{1,0:T(8,128)(2,1)S(1)}, bf16[128,1024]{1,0:T(8,128)(2,1)S(1)}, u32[]{:S(2)}, u32[]{:S(2)}) %collective-permute-start.15) | collective-permute-done | bytes 262176 | tf_op jit(solution)/shard_map/ppermute | solution.py:262
  96.4 5.4 %collective-permute-done.16.refs_2_ = bf16[128,1024]{1,0:T(8,128)(2,1)S(1)} collective-permute-done((bf16[128,1024]{1,0:T(8,128)(2,1)S(1)}, bf16[128,1024]{1,0:T(8,128)(2,1)S(1)}, u32[]{:S(2)}, u32[]{:S(2)}) %collective-permute-start.16) | collective-permute-done | bytes 262176 | tf_op jit(solution)/shard_map/ppermute | solution.py:262
  102.6 4.3 %collective-permute-start.19 = (bf16[512,256]{1,0:T(8,128)(2,1)S(1)}, bf16[512,256]{1,0:T(8,128)(2,1)S(1)}, u32[]{:S(2)}, u32[]{:S(2)}) collective-permute-start(bf16[512,256]{1,0:T(8,128)(2,1)S(1)} %get-tuple-element.108), channel_id=1, source_target_pairs={{0,6},{2,0},{4,2},{6,4},{1,7},{3,1},{5,3},{7,5},{8,14},{10,8},{12,... | collective-permute-start | bytes 786440 | tf_op jit(solution)/shard_map/ppermute | solution.py:265
  107.4 6.1 %collective-permute-done.19.refs_1_ = bf16[512,256]{1,0:T(8,128)(2,1)S(1)} collective-permute-done((bf16[512,256]{1,0:T(8,128)(2,1)S(1)}, bf16[512,256]{1,0:T(8,128)(2,1)S(1)}, u32[]{:S(2)}, u32[]{:S(2)}) %collective-permute-start.19) | collective-permute-done | bytes 262176 | tf_op jit(solution)/shard_map/ppermute | solution.py:265
  114.2 4.3 %collective-permute-start.20 = (bf16[512,256]{1,0:T(8,128)(2,1)S(1)}, bf16[512,256]{1,0:T(8,128)(2,1)S(1)}, u32[]{:S(2)}, u32[]{:S(2)}) collective-permute-start(bf16[512,256]{1,0:T(8,128)(2,1)S(1)} %get-tuple-element.109), channel_id=1, source_target_pairs={{0,6},{2,0},{4,2},{6,4},{1,7},{3,1},{5,3},{7,5},{8,14},{10,8},{12,... | collective-permute-start | bytes 786440 | tf_op jit(solution)/shard_map/ppermute | solution.py:265
  119.8 4.3 %collective-permute-start.23 = (bf16[512,256]{1,0:T(8,128)(2,1)S(1)}, bf16[512,256]{1,0:T(8,128)(2,1)S(1)}, u32[]{:S(2)}, u32[]{:S(2)}) collective-permute-start(bf16[512,256]{1,0:T(8,128)(2,1)S(1)} %get-tuple-element.113), channel_id=1, source_target_pairs={{0,6},{2,0},{4,2},{6,4},{1,7},{3,1},{5,3},{7,5},{8,14},{10,8},{12,... | collective-permute-start | bytes 786440 | tf_op jit(solution)/shard_map/ppermute | solution.py:265
  124.1 1.1 collective-permute-done.20.refs_1_
  125.8 4.3 %collective-permute-start.21 = (bf16[512,256]{1,0:T(8,128)(2,1)S(1)}, bf16[512,256]{1,0:T(8,128)(2,1)S(1)}, u32[]{:S(2)}, u32[]{:S(2)}) collective-permute-start(bf16[512,256]{1,0:T(8,128)(2,1)S(1)} %get-tuple-element.110), channel_id=1, source_target_pairs={{0,6},{2,0},{4,2},{6,4},{1,7},{3,1},{5,3},{7,5},{8,14},{10,8},{12,... | collective-permute-start | bytes 786440 | tf_op jit(solution)/shard_map/ppermute | solution.py:265
  130.8 4.8 %collective-permute-done.21.refs_5_ = bf16[512,256]{1,0:T(8,128)(2,1)S(1)} collective-permute-done((bf16[512,256]{1,0:T(8,128)(2,1)S(1)}, bf16[512,256]{1,0:T(8,128)(2,1)S(1)}, u32[]{:S(2)}, u32[]{:S(2)}) %collective-permute-start.21) | collective-permute-done | bytes 262176 | tf_op jit(solution)/shard_map/ppermute | solution.py:265
  135.6 1.3 grad.1
  137.3 1.4 collective-permute-start.25
  138.8 1.8 %collective-permute-start.26 = (bf16[256,256]{1,0:T(8,128)(2,1)S(1)}, bf16[256,256]{1,0:T(8,128)(2,1)S(1)}, u32[]{:S(2)}, u32[]{:S(2)}) collective-permute-start(bf16[256,256]{1,0:T(8,128)(2,1)S(1)} %get-tuple-element.117), channel_id=1, source_target_pairs={{0,24},{8,16},{16,8},{24,0},{1,25},{9,17},{17,9},{25,1},{2,26},{10... | collective-permute-start | bytes 393224 | tf_op jit(solution)/shard_map/ppermute | solution.py:262
  140.5 2.2 %collective-permute-done.24.refs_1_ = bf16[256,256]{1,0:T(8,128)(2,1)S(1)} collective-permute-done((bf16[256,256]{1,0:T(8,128)(2,1)S(1)}, bf16[256,256]{1,0:T(8,128)(2,1)S(1)}, u32[]{:S(2)}, u32[]{:S(2)}) %collective-permute-start.24) | collective-permute-done | bytes 131104 | tf_op jit(solution)/shard_map/ppermute | solution.py:262
  142.7 2.2 %collective-permute-done.25.refs_2_ = bf16[256,256]{1,0:T(8,128)(2,1)S(1)} collective-permute-done((bf16[256,256]{1,0:T(8,128)(2,1)S(1)}, bf16[256,256]{1,0:T(8,128)(2,1)S(1)}, u32[]{:S(2)}, u32[]{:S(2)}) %collective-permute-start.25) | collective-permute-done | bytes 131104 | tf_op jit(solution)/shard_map/ppermute | solution.py:262
  145.1 5.0 %collective-permute-done.27.refs_1_ = bf16[256,256]{1,0:T(8,128)(2,1)S(1)} collective-permute-done((bf16[256,256]{1,0:T(8,128)(2,1)S(1)}, bf16[256,256]{1,0:T(8,128)(2,1)S(1)}, u32[]{:S(2)}, u32[]{:S(2)}) %collective-permute-start.27) | collective-permute-done | bytes 131104 | tf_op jit(solution)/shard_map/ppermute | solution.py:423
  150.1 2.9 %collective-permute-start.28 = (bf16[256,256]{1,0:T(8,128)(2,1)S(1)}, bf16[256,256]{1,0:T(8,128)(2,1)S(1)}, u32[]{:S(2)}, u32[]{:S(2)}) collective-permute-start(bf16[256,256]{1,0:T(8,128)(2,1)S(1)} %sum.4.refs_0_), channel_id=1, source_target_pairs={{0,4},{2,6},{4,0},{6,2},{1,5},{3,7},{5,1},{7,3},{8,12},{10,14},{12... | collective-permute-start | bytes 393224 | tf_op jit(solution)/shard_map/ppermute | solution.py:423
  153.0 3.0 %collective-permute-done.28.refs_1_ = bf16[256,256]{1,0:T(8,128)(2,1)S(1)} collective-permute-done((bf16[256,256]{1,0:T(8,128)(2,1)S(1)}, bf16[256,256]{1,0:T(8,128)(2,1)S(1)}, u32[]{:S(2)}, u32[]{:S(2)}) %collective-permute-start.28) | collective-permute-done | bytes 131104 | tf_op jit(solution)/shard_map/ppermute | solution.py:423
  156.1 3.2 %collective-permute-start.29 = (bf16[256,256]{1,0:T(8,128)(2,1)S(1)}, bf16[256,256]{1,0:T(8,128)(2,1)S(1)}, u32[]{:S(2)}, u32[]{:S(2)}) collective-permute-start(bf16[256,256]{1,0:T(8,128)(2,1)S(1)} %sum.5.refs_1_), channel_id=1, source_target_pairs={{0,8},{8,0},{16,24},{24,16},{1,9},{9,1},{17,25},{25,17},{2,10},{10... | collective-permute-start | bytes 393224 | tf_op jit(solution)/shard_map/ppermute | solution.py:262
  159.8 1.0 collective-permute-start.31
  160.8 1.4 collective-permute-done.29.refs_2_
  162.2 2.0 %collective-permute-done.30.refs_3_ = bf16[256,256]{1,0:T(8,128)(2,1)S(1)} collective-permute-done((bf16[256,256]{1,0:T(8,128)(2,1)S(1)}, bf16[256,256]{1,0:T(8,128)(2,1)S(1)}, u32[]{:S(2)}, u32[]{:S(2)}) %collective-permute-start.30) | collective-permute-done | bytes 131104 | tf_op jit(solution)/shard_map/ppermute | solution.py:262
  164.2 1.4 collective-permute-done.31.refs_4_
  167.0 2.0 %last.1 = f32[1024,512]{1,0:T(8,128)} custom-call(s32[3]{0:T(128)S(1)} %pad_add_fusion.refs_0_, bf16[256,256]{1,0:T(8,128)(2,1)S(1)} %sum.5.refs_1_, bf16[256,256]{1,0:T(8,128)(2,1)S(1)} %collective-permute-done.29.refs_2_, bf16[256,256]{1,0:T(8,128)(2,1)S(1)} %collective-permute-done.30.refs_3_, bf16[256,256]{1,0:T(8,128)(2,1)S(1)} %collective-permute-done.31.refs_4_, ...), custom_call_target="tpu_custom_call" | custom-call | flops 200000000 | tf_op jit(solution)/shard_map/last/pallas_call | solution.py:52
  (84 shorter events, 14.9 us)
Async XLA Ops:
  0.6 62.0 %collective-permute-start.5 = (bf16[4,16,128,128]{3,2,1,0:T(8,128)(2,1)}, bf16[4,16,128,128]{3,2,1,0:T(8,128)(2,1)}, u32[]{:S(2)}, u32[]{:S(2)}) collective-permute-start(bf16[4,16,128,128]{3,2,1,0:T(8,128)(2,1)} %refs_3_.1), channel_id=1, source_target_pairs={{0,1},{1,0},{2,3},{3,2},{4,5},{5,4},{6,7},{7,6},{8,9},{9,8},{10,11... | collective-permute-start | bytes 6291464 | tf_op jit(solution)/shard_map/ppermute | solution.py:259
  3.0 1.2 copy-start.2
  4.2 1.2 copy-start.11
  5.5 29.1 %copy-start.13 = (s32[4,16]{1,0:T(4,128)S(1)}, s32[4,16]{1,0:T(4,128)}, u32[]{:S(2)}) copy-start(s32[4,16]{1,0:T(4,128)} %param.9) | copy-start | bytes 772
  5.5 29.1 %copy-start.14 = (s32[4]{0:T(128)S(1)}, s32[4]{0:T(128)}, u32[]{:S(2)}) copy-start(s32[4]{0:T(128)} %param.10) | copy-start | bytes 52
  5.5 29.2 %copy-start.10 = (bf16[4,16,128,128]{3,2,1,0:T(8,128)(2,1)S(1)}, bf16[4,16,128,128]{3,2,1,0:T(8,128)(2,1)}, u32[]{:S(2)}) copy-start(bf16[4,16,128,128]{3,2,1,0:T(8,128)(2,1)} %refs_3_.1) | copy-start | bytes 6291460
  6.7 15.4 %collective-permute-start = (bf16[512,256]{1,0:T(8,128)(2,1)S(1)}, bf16[512,256]{1,0:T(8,128)(2,1)S(1)}, u32[]{:S(2)}, u32[]{:S(2)}) collective-permute-start(bf16[512,256]{1,0:T(8,128)(2,1)S(1)} %get-tuple-element.63), channel_id=1, source_target_pairs={{0,1},{1,0},{2,3},{3,2},{4,5},{5,4},{6,7},{7,6},{8,9},{9,8},{10,11... | collective-permute-start | bytes 786440 | tf_op jit(solution)/shard_map/ppermute | solution.py:259
  24.6 6.3 %collective-permute-start.1 = (bf16[2,128,256]{2,1,0:T(8,128)(2,1)S(1)}, bf16[2,128,256]{2,1,0:T(8,128)(2,1)S(1)}, u32[]{:S(2)}, u32[]{:S(2)}) collective-permute-start(bf16[2,128,256]{2,1,0:T(8,128)(2,1)S(1)} %get-tuple-element.65), channel_id=1, source_target_pairs={{0,8},{8,0},{16,24},{24,16},{1,9},{9,1},{17,25},{25,17},{2,10},{10... | collective-permute-start | bytes 393224 | tf_op jit(solution)/shard_map/ppermute | solution.py:262
  25.4 7.8 %collective-permute-start.2 = (bf16[2,128,256]{2,1,0:T(8,128)(2,1)S(1)}, bf16[2,128,256]{2,1,0:T(8,128)(2,1)S(1)}, u32[]{:S(2)}, u32[]{:S(2)}) collective-permute-start(bf16[2,128,256]{2,1,0:T(8,128)(2,1)S(1)} %get-tuple-element.66), channel_id=1, source_target_pairs={{0,16},{8,24},{16,0},{24,8},{1,17},{9,25},{17,1},{25,9},{2,18},{10... | collective-permute-start | bytes 393224 | tf_op jit(solution)/shard_map/ppermute | solution.py:262
  26.1 7.1 %collective-permute-start.3 = (bf16[2,128,256]{2,1,0:T(8,128)(2,1)S(1)}, bf16[2,128,256]{2,1,0:T(8,128)(2,1)S(1)}, u32[]{:S(2)}, u32[]{:S(2)}) collective-permute-start(bf16[2,128,256]{2,1,0:T(8,128)(2,1)S(1)} %get-tuple-element.67), channel_id=1, source_target_pairs={{0,24},{8,16},{16,8},{24,0},{1,25},{9,17},{17,9},{25,1},{2,26},{10... | collective-permute-start | bytes 393224 | tf_op jit(solution)/shard_map/ppermute | solution.py:262
  33.2 11.1 %copy-start.6 = (bf16[512,256]{1,0:T(8,128)(2,1)}, bf16[512,256]{1,0:T(8,128)(2,1)S(1)}, u32[]{:S(2)}) copy-start(bf16[512,256]{1,0:T(8,128)(2,1)S(1)} %get-tuple-element.72.refs_2_) | copy-start | bytes 786436
  33.3 11.1 %copy-start.8 = (bf16[512,256]{1,0:T(8,128)(2,1)}, bf16[512,256]{1,0:T(8,128)(2,1)S(1)}, u32[]{:S(2)}) copy-start(bf16[512,256]{1,0:T(8,128)(2,1)S(1)} %get-tuple-element.77.refs_3_) | copy-start | bytes 786436
  33.3 11.1 %collective-permute-start.6 = (bf16[512,256]{1,0:T(8,128)(2,1)S(1)}, bf16[512,256]{1,0:T(8,128)(2,1)S(1)}, u32[]{:S(2)}, u32[]{:S(2)}) collective-permute-start(bf16[512,256]{1,0:T(8,128)(2,1)S(1)} %get-tuple-element.72.refs_2_), channel_id=1, source_target_pairs={{0,2},{2,4},{4,6},{6,0},{1,3},{3,5},{5,7},{7,1},{8,10},{10,12},{12... | collective-permute-start | bytes 786440 | tf_op jit(solution)/shard_map/ppermute | solution.py:265
  34.0 16.0 %collective-permute-start.9 = (bf16[512,256]{1,0:T(8,128)(2,1)S(1)}, bf16[512,256]{1,0:T(8,128)(2,1)}, u32[]{:S(2)}, u32[]{:S(2)}) collective-permute-start(bf16[512,256]{1,0:T(8,128)(2,1)S(1)} %get-tuple-element.77.refs_3_), channel_id=1, source_target_pairs={{0,2},{2,4},{4,6},{6,0},{1,3},{3,5},{5,7},{7,1},{8,10},{10,12},{12... | collective-permute-start | bytes 786440 | tf_op jit(solution)/shard_map/ppermute | solution.py:265
  44.4 11.3 %collective-permute-start.7 = (bf16[512,256]{1,0:T(8,128)(2,1)S(1)}, bf16[512,256]{1,0:T(8,128)(2,1)}, u32[]{:S(2)}, u32[]{:S(2)}) collective-permute-start(bf16[512,256]{1,0:T(8,128)(2,1)S(1)} %collective-permute-done.6.refs_2_), channel_id=1, source_target_pairs={{0,2},{2,4},{4,6},{6,0},{1,3},{3,5},{5,7},{7,1},{8,10},{10,12},{12... | collective-permute-start | bytes 786440 | tf_op jit(solution)/shard_map/ppermute | solution.py:265
  50.1 11.4 %collective-permute-start.10 = (bf16[512,256]{1,0:T(8,128)(2,1)}, bf16[512,256]{1,0:T(8,128)(2,1)}, u32[]{:S(2)}, u32[]{:S(2)}) collective-permute-start(bf16[512,256]{1,0:T(8,128)(2,1)} %collective-permute-done.9.refs_3_), channel_id=1, source_target_pairs={{0,2},{2,4},{4,6},{6,0},{1,3},{3,5},{5,7},{7,1},{8,10},{10,12},{12... | collective-permute-start | bytes 786440 | tf_op jit(solution)/shard_map/ppermute | solution.py:265
  50.1 20.0 %copy-start.7 = (bf16[512,256]{1,0:T(8,128)(2,1)S(1)}, bf16[512,256]{1,0:T(8,128)(2,1)}, u32[]{:S(2)}) copy-start(bf16[512,256]{1,0:T(8,128)(2,1)} %copy-done.6) | copy-start | bytes 786436
  50.1 20.0 %copy-start.9 = (bf16[512,256]{1,0:T(8,128)(2,1)S(1)}, bf16[512,256]{1,0:T(8,128)(2,1)}, u32[]{:S(2)}) copy-start(bf16[512,256]{1,0:T(8,128)(2,1)} %copy-done.8) | copy-start | bytes 786436
  51.2 21.3 %collective-permute-start.12 = (bf16[512,256]{1,0:T(8,128)(2,1)S(1)}, bf16[512,256]{1,0:T(8,128)(2,1)S(1)}, u32[]{:S(2)}, u32[]{:S(2)}) collective-permute-start(bf16[512,256]{1,0:T(8,128)(2,1)S(1)} %get-tuple-element.120), channel_id=1, source_target_pairs={{0,1},{1,0},{2,3},{3,2},{4,5},{5,4},{6,7},{7,6},{8,9},{9,8},{10,11... | collective-permute-start | bytes 786440 | tf_op jit(solution)/shard_map/ppermute | solution.py:259
  55.7 18.7 %collective-permute-start.8 = (bf16[512,256]{1,0:T(8,128)(2,1)}, bf16[512,256]{1,0:T(8,128)(2,1)S(1)}, u32[]{:S(2)}, u32[]{:S(2)}) collective-permute-start(bf16[512,256]{1,0:T(8,128)(2,1)} %collective-permute-done.7.refs_2_), channel_id=1, source_target_pairs={{0,2},{2,4},{4,6},{6,0},{1,3},{3,5},{5,7},{7,1},{8,10},{10,12},{12... | collective-permute-start | bytes 786440 | tf_op jit(solution)/shard_map/ppermute | solution.py:265
  61.4 13.0 %collective-permute-start.11 = (bf16[512,256]{1,0:T(8,128)(2,1)}, bf16[512,256]{1,0:T(8,128)(2,1)S(1)}, u32[]{:S(2)}, u32[]{:S(2)}) collective-permute-start(bf16[512,256]{1,0:T(8,128)(2,1)} %collective-permute-done.10.refs_3_), channel_id=1, source_target_pairs={{0,2},{2,4},{4,6},{6,0},{1,3},{3,5},{5,7},{7,1},{8,10},{10,12},{12... | collective-permute-start | bytes 786440 | tf_op jit(solution)/shard_map/ppermute | solution.py:265
  61.4 1.2 collective-permute-start.4
  72.6 1.9 %copy-start.1 = (bf16[1024,512]{1,0:T(8,128)(2,1)S(1)}, bf16[1024,512]{1,0:T(8,128)(2,1)}, u32[]{:S(2)}) copy-start(bf16[1024,512]{1,0:T(8,128)(2,1)} %copy-done) | copy-start | bytes 3145732
  76.1 9.8 %copy-start.3 = (bf16[512,1024]{1,0:T(8,128)(2,1)S(1)}, bf16[512,1024]{1,0:T(8,128)(2,1)}, u32[]{:S(2)}) copy-start(bf16[512,1024]{1,0:T(8,128)(2,1)} %refs_1_.1) | copy-start | bytes 3145732
  76.1 9.8 %copy-start.5 = (bf16[512,512]{1,0:T(8,128)(2,1)S(1)}, bf16[512,512]{1,0:T(8,128)(2,1)}, u32[]{:S(2)}) copy-start(bf16[512,512]{1,0:T(8,128)(2,1)} %copy-done.4) | copy-start | bytes 1572868
  76.1 9.7 %collective-permute-start.14 = (bf16[512,256]{1,0:T(8,128)(2,1)S(1)}, bf16[512,256]{1,0:T(8,128)(2,1)S(1)}, u32[]{:S(2)}, u32[]{:S(2)}) collective-permute-start(bf16[512,256]{1,0:T(8,128)(2,1)S(1)} %get-tuple-element.97), channel_id=1, source_target_pairs={{0,6},{2,0},{4,2},{6,4},{1,7},{3,1},{5,3},{7,5},{8,14},{10,8},{12,... | collective-permute-start | bytes 786440 | tf_op jit(solution)/shard_map/ppermute | solution.py:265
  87.2 9.2 %collective-permute-start.15 = (bf16[128,1024]{1,0:T(8,128)(2,1)S(1)}, bf16[128,1024]{1,0:T(8,128)(2,1)S(1)}, u32[]{:S(2)}, u32[]{:S(2)}) collective-permute-start(bf16[128,1024]{1,0:T(8,128)(2,1)S(1)} %get-tuple-element.100), channel_id=1, source_target_pairs={{0,8},{8,0},{16,24},{24,16},{1,9},{9,1},{17,25},{25,17},{2,10},{10... | collective-permute-start | bytes 786440 | tf_op jit(solution)/shard_map/ppermute | solution.py:262
  88.9 12.9 %collective-permute-start.16 = (bf16[128,1024]{1,0:T(8,128)(2,1)S(1)}, bf16[128,1024]{1,0:T(8,128)(2,1)S(1)}, u32[]{:S(2)}, u32[]{:S(2)}) collective-permute-start(bf16[128,1024]{1,0:T(8,128)(2,1)S(1)} %get-tuple-element.101), channel_id=1, source_target_pairs={{0,16},{8,24},{16,0},{24,8},{1,17},{9,25},{17,1},{25,9},{2,18},{10... | collective-permute-start | bytes 786440 | tf_op jit(solution)/shard_map/ppermute | solution.py:262
  88.9 12.9 %collective-permute-start.17 = (bf16[128,1024]{1,0:T(8,128)(2,1)S(1)}, bf16[128,1024]{1,0:T(8,128)(2,1)S(1)}, u32[]{:S(2)}, u32[]{:S(2)}) collective-permute-start(bf16[128,1024]{1,0:T(8,128)(2,1)S(1)} %get-tuple-element.102), channel_id=1, source_target_pairs={{0,24},{8,16},{16,8},{24,0},{1,25},{9,17},{17,9},{25,1},{2,26},{10... | collective-permute-start | bytes 786440 | tf_op jit(solution)/shard_map/ppermute | solution.py:262
  102.6 33.0 %collective-permute-start.18 = (bf16[1024,512]{1,0:T(8,128)(2,1)S(1)}, bf16[1024,512]{1,0:T(8,128)(2,1)S(1)}, u32[]{:S(2)}, u32[]{:S(2)}) collective-permute-start(bf16[1024,512]{1,0:T(8,128)(2,1)S(1)} %get-tuple-element.103.refs_1_), channel_id=1, source_target_pairs={{0,1},{1,0},{2,3},{3,2},{4,5},{5,4},{6,7},{7,6},{8,9},{9,8},{10,11... | collective-permute-start | bytes 3145736 | tf_op jit(solution)/shard_map/ppermute | solution.py:259
  102.6 10.9 %collective-permute-start.19 = (bf16[512,256]{1,0:T(8,128)(2,1)S(1)}, bf16[512,256]{1,0:T(8,128)(2,1)S(1)}, u32[]{:S(2)}, u32[]{:S(2)}) collective-permute-start(bf16[512,256]{1,0:T(8,128)(2,1)S(1)} %get-tuple-element.108), channel_id=1, source_target_pairs={{0,6},{2,0},{4,2},{6,4},{1,7},{3,1},{5,3},{7,5},{8,14},{10,8},{12,... | collective-permute-start | bytes 786440 | tf_op jit(solution)/shard_map/ppermute | solution.py:265
  106.9 12.2 %collective-permute-start.13 = (bf16[512,256]{1,0:T(8,128)(2,1)S(1)}, bf16[512,256]{1,0:T(8,128)(2,1)S(1)}, u32[]{:S(2)}, u32[]{:S(2)}) collective-permute-start(bf16[512,256]{1,0:T(8,128)(2,1)S(1)} %get-tuple-element.92), channel_id=1, source_target_pairs={{0,1},{1,0},{2,3},{3,2},{4,5},{5,4},{6,7},{7,6},{8,9},{9,8},{10,11... | collective-permute-start | bytes 786440 | tf_op jit(solution)/shard_map/ppermute | solution.py:259
  107.1 12.0 %collective-permute-start.22 = (bf16[512,256]{1,0:T(8,128)(2,1)S(1)}, bf16[512,256]{1,0:T(8,128)(2,1)S(1)}, u32[]{:S(2)}, u32[]{:S(2)}) collective-permute-start(bf16[512,256]{1,0:T(8,128)(2,1)S(1)} %get-tuple-element.112), channel_id=1, source_target_pairs={{0,6},{2,0},{4,2},{6,4},{1,7},{3,1},{5,3},{7,5},{8,14},{10,8},{12,... | collective-permute-start | bytes 786440 | tf_op jit(solution)/shard_map/ppermute | solution.py:265
  114.2 11.0 %collective-permute-start.20 = (bf16[512,256]{1,0:T(8,128)(2,1)S(1)}, bf16[512,256]{1,0:T(8,128)(2,1)S(1)}, u32[]{:S(2)}, u32[]{:S(2)}) collective-permute-start(bf16[512,256]{1,0:T(8,128)(2,1)S(1)} %get-tuple-element.109), channel_id=1, source_target_pairs={{0,6},{2,0},{4,2},{6,4},{1,7},{3,1},{5,3},{7,5},{8,14},{10,8},{12,... | collective-permute-start | bytes 786440 | tf_op jit(solution)/shard_map/ppermute | solution.py:265
  119.8 11.0 %collective-permute-start.23 = (bf16[512,256]{1,0:T(8,128)(2,1)S(1)}, bf16[512,256]{1,0:T(8,128)(2,1)S(1)}, u32[]{:S(2)}, u32[]{:S(2)}) collective-permute-start(bf16[512,256]{1,0:T(8,128)(2,1)S(1)} %get-tuple-element.113), channel_id=1, source_target_pairs={{0,6},{2,0},{4,2},{6,4},{1,7},{3,1},{5,3},{7,5},{8,14},{10,8},{12,... | collective-permute-start | bytes 786440 | tf_op jit(solution)/shard_map/ppermute | solution.py:265
  125.8 9.8 %collective-permute-start.21 = (bf16[512,256]{1,0:T(8,128)(2,1)S(1)}, bf16[512,256]{1,0:T(8,128)(2,1)S(1)}, u32[]{:S(2)}, u32[]{:S(2)}) collective-permute-start(bf16[512,256]{1,0:T(8,128)(2,1)S(1)} %get-tuple-element.110), channel_id=1, source_target_pairs={{0,6},{2,0},{4,2},{6,4},{1,7},{3,1},{5,3},{7,5},{8,14},{10,8},{12,... | collective-permute-start | bytes 786440 | tf_op jit(solution)/shard_map/ppermute | solution.py:265
  136.9 5.7 %collective-permute-start.24 = (bf16[256,256]{1,0:T(8,128)(2,1)S(1)}, bf16[256,256]{1,0:T(8,128)(2,1)S(1)}, u32[]{:S(2)}, u32[]{:S(2)}) collective-permute-start(bf16[256,256]{1,0:T(8,128)(2,1)S(1)} %get-tuple-element.115), channel_id=1, source_target_pairs={{0,8},{8,0},{16,24},{24,16},{1,9},{9,1},{17,25},{25,17},{2,10},{10... | collective-permute-start | bytes 393224 | tf_op jit(solution)/shard_map/ppermute | solution.py:262
  137.3 7.6 %collective-permute-start.25 = (bf16[256,256]{1,0:T(8,128)(2,1)S(1)}, bf16[256,256]{1,0:T(8,128)(2,1)S(1)}, u32[]{:S(2)}, u32[]{:S(2)}) collective-permute-start(bf16[256,256]{1,0:T(8,128)(2,1)S(1)} %get-tuple-element.116), channel_id=1, source_target_pairs={{0,16},{8,24},{16,0},{24,8},{1,17},{9,25},{17,1},{25,9},{2,18},{10... | collective-permute-start | bytes 393224 | tf_op jit(solution)/shard_map/ppermute | solution.py:262
  138.8 6.2 %collective-permute-start.26 = (bf16[256,256]{1,0:T(8,128)(2,1)S(1)}, bf16[256,256]{1,0:T(8,128)(2,1)S(1)}, u32[]{:S(2)}, u32[]{:S(2)}) collective-permute-start(bf16[256,256]{1,0:T(8,128)(2,1)S(1)} %get-tuple-element.117), channel_id=1, source_target_pairs={{0,24},{8,16},{16,8},{24,0},{1,25},{9,17},{17,9},{25,1},{2,26},{10... | collective-permute-start | bytes 393224 | tf_op jit(solution)/shard_map/ppermute | solution.py:262
  145.0 5.0 %collective-permute-start.27 = (bf16[256,256]{1,0:T(8,128)(2,1)S(1)}, bf16[256,256]{1,0:T(8,128)(2,1)S(1)}, u32[]{:S(2)}, u32[]{:S(2)}) collective-permute-start(bf16[256,256]{1,0:T(8,128)(2,1)S(1)} %sum.3.refs_0_), channel_id=1, source_target_pairs={{0,2},{2,0},{4,6},{6,4},{1,3},{3,1},{5,7},{7,5},{8,10},{10,8},{12,... | collective-permute-start | bytes 393224 | tf_op jit(solution)/shard_map/ppermute | solution.py:423
  150.1 5.9 %collective-permute-start.28 = (bf16[256,256]{1,0:T(8,128)(2,1)S(1)}, bf16[256,256]{1,0:T(8,128)(2,1)S(1)}, u32[]{:S(2)}, u32[]{:S(2)}) collective-permute-start(bf16[256,256]{1,0:T(8,128)(2,1)S(1)} %sum.4.refs_0_), channel_id=1, source_target_pairs={{0,4},{2,6},{4,0},{6,2},{1,5},{3,7},{5,1},{7,3},{8,12},{10,14},{12... | collective-permute-start | bytes 393224 | tf_op jit(solution)/shard_map/ppermute | solution.py:423
  156.1 6.1 %collective-permute-start.29 = (bf16[256,256]{1,0:T(8,128)(2,1)S(1)}, bf16[256,256]{1,0:T(8,128)(2,1)S(1)}, u32[]{:S(2)}, u32[]{:S(2)}) collective-permute-start(bf16[256,256]{1,0:T(8,128)(2,1)S(1)} %sum.5.refs_1_), channel_id=1, source_target_pairs={{0,8},{8,0},{16,24},{24,16},{1,9},{9,1},{17,25},{25,17},{2,10},{10... | collective-permute-start | bytes 393224 | tf_op jit(solution)/shard_map/ppermute | solution.py:262
  159.2 5.0 %collective-permute-start.30 = (bf16[256,256]{1,0:T(8,128)(2,1)S(1)}, bf16[256,256]{1,0:T(8,128)(2,1)S(1)}, u32[]{:S(2)}, u32[]{:S(2)}) collective-permute-start(bf16[256,256]{1,0:T(8,128)(2,1)S(1)} %sum.5.refs_1_), channel_id=1, source_target_pairs={{0,16},{8,24},{16,0},{24,8},{1,17},{9,25},{17,1},{25,9},{2,18},{10... | collective-permute-start | bytes 393224 | tf_op jit(solution)/shard_map/ppermute | solution.py:262
  159.8 5.9 %collective-permute-start.31 = (bf16[256,256]{1,0:T(8,128)(2,1)S(1)}, bf16[256,256]{1,0:T(8,128)(2,1)S(1)}, u32[]{:S(2)}, u32[]{:S(2)}) collective-permute-start(bf16[256,256]{1,0:T(8,128)(2,1)S(1)} %sum.5.refs_1_), channel_id=1, source_target_pairs={{0,24},{8,16},{16,8},{24,0},{1,25},{9,17},{17,9},{25,1},{2,26},{10... | collective-permute-start | bytes 393224 | tf_op jit(solution)/shard_map/ppermute | solution.py:262
  160.8 5.8 %collective-permute-start.32 = (bf16[256,256]{1,0:T(8,128)(2,1)S(1)}, bf16[256,256]{1,0:T(8,128)(2,1)S(1)}, u32[]{:S(2)}, u32[]{:S(2)}) collective-permute-start(bf16[256,256]{1,0:T(8,128)(2,1)S(1)} %sum.5.refs_1_), channel_id=1, source_target_pairs={{0,1},{1,0},{2,3},{3,2},{4,5},{5,4},{6,7},{7,6},{8,9},{9,8},{10,11... | collective-permute-start | bytes 393224 | tf_op jit(solution)/shard_map/ppermute | solution.py:259
  162.2 4.3 %collective-permute-start.33 = (bf16[256,256]{1,0:T(8,128)(2,1)S(1)}, bf16[256,256]{1,0:T(8,128)(2,1)S(1)}, u32[]{:S(2)}, u32[]{:S(2)}) collective-permute-start(bf16[256,256]{1,0:T(8,128)(2,1)S(1)} %collective-permute-done.29.refs_2_), channel_id=1, source_target_pairs={{0,1},{1,0},{2,3},{3,2},{4,5},{5,4},{6,7},{7,6},{8,9},{9,8},{10,11... | collective-permute-start | bytes 393224 | tf_op jit(solution)/shard_map/ppermute | solution.py:259
  164.2 2.3 %collective-permute-start.34 = (bf16[256,256]{1,0:T(8,128)(2,1)S(1)}, bf16[256,256]{1,0:T(8,128)(2,1)S(1)}, u32[]{:S(2)}, u32[]{:S(2)}) collective-permute-start(bf16[256,256]{1,0:T(8,128)(2,1)S(1)} %collective-permute-done.30.refs_3_), channel_id=1, source_target_pairs={{0,1},{1,0},{2,3},{3,2},{4,5},{5,4},{6,7},{7,6},{8,9},{9,8},{10,11... | collective-permute-start | bytes 393224 | tf_op jit(solution)/shard_map/ppermute | solution.py:259
  165.6 1.3 collective-permute-start.35
  (3 other events, 2.5 us)

commit v11 on v10

--- a/solution.py
+++ b/solution.py
@@ -349,13 +349,17 @@
         )
         return [part.reshape(wide, rows) for part in got], token
 
-    turned = []
     for k in range(1, z.zz):
         ring.append([to_zz(part, 1) for part in ring[-1]])
-        if k < 3:
-            got, token = prepared(*((cols_a, block_vals), (cols_b, vals_b))[k - 1], token)
-            turned.append(got)
-            ring[k][0], token = lax.optimization_barrier((ring[k][0], token))
+        if k == 1:
+            turned_a, token = prepared(cols_a, block_vals, token)
+            ring[1][0], token = lax.optimization_barrier((ring[1][0], token))
+            *picked, token = rows_of(pick, features, [token])
+            lefts, token_l = turned_of(across(picked))
+        if k == 2:
+            turned_b, token = prepared(cols_b, vals_b, token)
+            ring[2][0], token = lax.optimization_barrier((ring[2][0], token))
+    turned = (turned_a, turned_b)
 
     agg = []
     for k in range(z.zz):
@@ -369,7 +373,7 @@
         agg = call(
             lambda *refs, k=k, last=last: forward_kernel(z, k == 0, last, *refs),
             outs, ins, "forward", 3 if last else 1,
-            after=[cot_a, cot_b] if k == z.zz - 2 else (),
+            after=[cot_a, cot_b, token_l] if k == z.zz - 2 else [token] if k == 0 else (),
         )
     hidden_a, hidden_b, grad_a, grad_b, *came = agg
 
@@ -394,9 +398,6 @@
                 for i, (part, moved) in enumerate(zip(mine, came))
             ]
             came = [part for part, _ in passed]
-            if k == z.zz - 2:
-                *picked, _ = rows_of(pick, features, [passed[1][1]])
-                lefts, _ = turned_of(across(picked))
     first = core == 0
     hidden = jnp.concatenate(
         [jnp.where(first, hidden_a, come), jnp.where(first, come, hidden_a)], axis=1

time: 169 us -> 154 us (0.911)
  waiting for transfers between devices: 71 us -> 60.4 us
  starting transfers between devices: 41.7 us -> 35.3 us
    ppermute x12, waiting for transfers between devices: 25.5 us -> 17.7 us  [to_grp(): lax.ppermute(x, 'grp', [(i, i ^ s) for i in range(z.grp)])]
    ppermute x12, waiting for transfers between devices: 35.9 us -> 30.9 us  [to_zz(): lax.ppermute(x, 'zz', [(i, (i + k) % z.zz) for i in range(z.zz)])]
    ppermute x12, starting transfers between devices: 22.5 us -> 18 us  [to_zz(): lax.ppermute(x, 'zz', [(i, (i + k) % z.zz) for i in range(z.zz)])]
    ppermute x2, waiting for transfers between devices: 7.98 us -> 10.2 us  [shards(): lax.ppermute(mine, 'zz', [(i, i ^ step) for i in range(z.zz)])]
    unnamed x30 -> x38, local copies, waits for them, and re-layouts: 4.93 us -> 5.56 us
  transfers between devices with their start and end apart: 36 -> 36, of which waited for: 21 -> 22; matrix products, arithmetic and copies ran while one was open for 1% -> 1% of each run, Pallas kernels for 14% -> 19%
where the time goes in v11:
time: 154 us; the launch traced here: 153 us
  waiting for transfers between devices  60.4 us (39%)
  starting transfers between devices  35.3 us (23%)
  Pallas kernels  33.7 us (22%)
  blocking collectives  15.3 us (10%)
  local copies, waits for them, and re-layouts  6.71 us (4%)
    pallas_call x24, Pallas kernels, call(): pl.pallas_call(kernel, out_shape=tuple((jax.ShapeDtypeStruct(s, d) for s,...  33.7 us
    ppermute x12, waiting for transfers between devices, to_zz(): lax.ppermute(x, 'zz', [(i, (i + k) % z.zz) for i in range(z.zz)])  30.9 us
    ppermute x12, starting transfers between devices, to_zz(): lax.ppermute(x, 'zz', [(i, (i + k) % z.zz) for i in range(z.zz)])  18 us
    ppermute x12, waiting for transfers between devices, to_grp(): lax.ppermute(x, 'grp', [(i, i ^ s) for i in range(z.grp)])  17.7 us
    all_to_all x1, blocking collectives, shards(): lax.all_to_all(message, ('grp', 'zz', 'core'), split_axis=0, concat_axis=...  15.3 us
    ppermute x12, starting transfers between devices, to_grp(): lax.ppermute(x, 'grp', [(i, i ^ s) for i in range(z.grp)])  14.5 us
    ppermute x2, waiting for transfers between devices, shards(): lax.ppermute(mine, 'zz', [(i, i ^ step) for i in range(z.zz)])  10.2 us
    unnamed x38, local copies, waits for them, and re-layouts  5.56 us
  transfers between devices with their start and end apart: 36, of which 22 were waited for; matrix products, arithmetic and copies ran while one was open for 1% of the time, Pallas kernels for 19%

profile of v11, /device:TPU:0, one launch (start us, length us, event | category | flops | bytes accessed | tf_op | source)
XLA Modules:
  0.0 153.4 jit_solution(6882711961740429467)
XLA Ops:
  1.9 1.1 index.1
  3.0 1.2 copy-done.2
  4.3 1.2 copy-done.15
  5.5 1.3 product.1
  6.9 15.3 %all_to_all.5.refs_1_.refs_2_ = s32[32,8,128]{2,1,0:T(8,128)S(1)} all-to-all(s32[32,8,128]{2,1,0:T(8,128)S(1)} %index.1), channel_id=1, replica_groups=mesh['grp'=4,'zz'=4,'core'=2] {'grp','zz','core'}, dimensions={0} | all-to-all | bytes 262144 | tf_op jit(solution)/shard_map/all_to_all | solution.py:275
  22.2 1.7 %send.1 = (bf16[512,512]{1,0:T(8,128)(2,1)S(1)}, bf16[2,128,256]{2,1,0:T(8,128)(2,1)S(1)}, bf16[2,128,256]{2,1,0:T(8,128)(2,1)S(1)}, bf16[2,128,256]{2,1,0:T(8,1...) custom-call(s32[3]{0:T(128)S(1)} %pad_add_fusion.refs_0_, ...), custom_call_target="tpu_custom_call" | custom-call | flops 150000000 | tf_op jit(solution)/shard_map/send/pallas_call | solution.py:52
  25.4 2.0 %collective-permute-start.3 = (bf16[2,128,256]{2,1,0:T(8,128)(2,1)S(1)}, bf16[2,128,256]{2,1,0:T(8,128)(2,1)S(1)}, u32[]{:S(2)}, u32[]{:S(2)}) collective-permute-start(bf16[2,128,256]{2,1,0:T(8,128)(2,1)S(1)} %get-tuple-element.71), channel_id=1, source_target_pairs={{0,24},{8,16},{16,8},{24,0},{1,25},{9,17},{17,9},{25,1},{2,26},{10... | collective-permute-start | bytes 393224 | tf_op jit(solution)/shard_map/ppermute | solution.py:262
  27.4 2.8 %collective-permute-done.1.refs_1_ = bf16[2,128,256]{2,1,0:T(8,128)(2,1)S(1)} collective-permute-done((bf16[2,128,256]{2,1,0:T(8,128)(2,1)S(1)}, bf16[2,128,256]{2,1,0:T(8,128)(2,1)S(1)}, u32[]{:S(2)}, u32[]{:S(2)}) %collective-permute-start.1) | collective-permute-done | bytes 131104 | tf_op jit(solution)/shard_map/ppermute | solution.py:262
  30.2 2.3 %collective-permute-done.2.refs_2_ = bf16[2,128,256]{2,1,0:T(8,128)(2,1)S(1)} collective-permute-done((bf16[2,128,256]{2,1,0:T(8,128)(2,1)S(1)}, bf16[2,128,256]{2,1,0:T(8,128)(2,1)S(1)}, u32[]{:S(2)}, u32[]{:S(2)}) %collective-permute-start.2) | collective-permute-done | bytes 131104 | tf_op jit(solution)/shard_map/ppermute | solution.py:262
  33.9 5.9 %prepare.2 = (bf16[1024,512]{1,0:T(8,128)(2,1)S(1)}, bf16[1024,512]{1,0:T(8,128)(2,1)S(1)}, bf16[1024,512]{1,0:T(8,128)(2,1)S(1)}, bf16[1024,512]{1,0:T(8,128)(2,1)S(1)}, f32[8,128]{1,0:T(8,128)S(1)}) custom-call(s32[3]{0:T(128)S(1)} %pad_add_fusion.refs_0_, s32[4,16]{1,0:T(4,128)S(1)} %fusion.refs_1_, s32[32,8,128]{2,1,0:T(8,128)S(1)} %all_to_all.5.refs_1_.refs_2_, ...), custom_call_target="tpu_custom_call" | custom-call | flops 700000000 | tf_op jit(solution)/shard_map/prepare/pallas_call | solution.py:52
  39.9 1.0 copy-done
  40.8 2.8 %collective-permute-done.6.refs_2_ = bf16[512,256]{1,0:T(8,128)(2,1)S(1)} collective-permute-done((bf16[512,256]{1,0:T(8,128)(2,1)S(1)}, bf16[512,256]{1,0:T(8,128)(2,1)S(1)}, u32[]{:S(2)}, u32[]{:S(2)}) %collective-permute-start.6) | collective-permute-done | bytes 262176 | tf_op jit(solution)/shard_map/ppermute | solution.py:265
  43.7 5.7 %collective-permute-done.9.refs_3_ = bf16[512,256]{1,0:T(8,128)(2,1)} collective-permute-done((bf16[512,256]{1,0:T(8,128)(2,1)S(1)}, bf16[512,256]{1,0:T(8,128)(2,1)}, u32[]{:S(2)}, u32[]{:S(2)}) %collective-permute-start.9) | collective-permute-done | bytes 262176 | tf_op jit(solution)/shard_map/ppermute | solution.py:265
  49.4 1.4 rows.1
  51.5 1.7 %collective-permute-start.13 = (bf16[128,1024]{1,0:T(8,128)(2,1)}, bf16[128,1024]{1,0:T(8,128)(2,1)}, u32[]{:S(2)}, u32[]{:S(2)}) collective-permute-start(bf16[128,1024]{1,0:T(8,128)(2,1)} %get-tuple-element.99), channel_id=1, source_target_pairs={{0,8},{8,0},{16,24},{24,16},{1,9},{9,1},{17,25},{25,17},{2,10},{10... | collective-permute-start | bytes 786440 | tf_op jit(solution)/shard_map/ppermute | solution.py:262
  53.2 1.2 collective-permute-done.4.refs_1_
  55.6 1.6 %collective-permute-start.15 = (bf16[128,1024]{1,0:T(8,128)(2,1)}, bf16[128,1024]{1,0:T(8,128)(2,1)}, u32[]{:S(2)}, u32[]{:S(2)}) collective-permute-start(bf16[128,1024]{1,0:T(8,128)(2,1)} %get-tuple-element.101), channel_id=1, source_target_pairs={{0,24},{8,16},{16,8},{24,0},{1,25},{9,17},{17,9},{25,1},{2,26},{10... | collective-permute-start | bytes 786440 | tf_op jit(solution)/shard_map/ppermute | solution.py:262
  57.2 1.2 constant_dynamic-slice_fusion
  58.5 6.9 %prepare.3 = (bf16[1024,512]{1,0:T(8,128)(2,1)S(1)}, bf16[1024,512]{1,0:T(8,128)(2,1)S(1)}, bf16[1024,512]{1,0:T(8,128)(2,1)S(1)}, bf16[1024,512]{1,0:T(8,128)(2,1)S(1)}, f32[8,128]{1,0:T(8,128)S(1)}) custom-call(s32[3]{0:T(128)S(1)} %pad_add_fusion.refs_0_, s32[4,16]{1,0:T(4,128)S(1)} %collective-permute-done.4.refs_1_, ...), custom_call_target="tpu_custom_call" | custom-call | flops 700000000 | tf_op jit(solution)/shard_map/prepare/pallas_call | solution.py:52
  65.7 2.9 %collective-permute-done.14.refs_2_ = bf16[128,1024]{1,0:T(8,128)(2,1)} collective-permute-done((bf16[128,1024]{1,0:T(8,128)(2,1)}, bf16[128,1024]{1,0:T(8,128)(2,1)}, u32[]{:S(2)}, u32[]{:S(2)}) %collective-permute-start.14) | collective-permute-done | bytes 262176 | tf_op jit(solution)/shard_map/ppermute | solution.py:262
  68.7 1.4 turn.1
  71.0 1.7 %forward.5 = (f32[512,256]{1,0:T(8,128)S(1)}, f32[512,256]{1,0:T(8,128)S(1)}) custom-call(bf16[1024,512]{1,0:T(8,128)(2,1)S(1)} %get-tuple-element.88.refs_0_, bf16[1024,512]{1,0:T(8,128)(2,1)S(1)} %get-tuple-element.89.refs_1_, bf16[512,256]{1,0:T(8,128)(2,1)S(1)} %collective-permute-done.6.refs_2_, bf16[512,256]{1,0:T(8,128)(2,1)} %collective-permute-done.9.refs_3_, ...), custom_call_target="tpu_custom_call" | custom-call | flops 100000000 | tf_op jit(solution)/shard_map/forward/pallas_call | solution.py:52
  72.7 1.8 %forward.6 = (f32[512,256]{1,0:T(8,128)S(1)}, f32[512,256]{1,0:T(8,128)S(1)}) custom-call(bf16[1024,512]{1,0:T(8,128)(2,1)S(1)} %get-tuple-element.86.refs_0_, bf16[1024,512]{1,0:T(8,128)(2,1)S(1)} %get-tuple-element.87.refs_1_, bf16[512,256]{1,0:T(8,128)(2,1)S(1)} %copy-done.9, bf16[512,256]{1,0:T(8,128)(2,1)} %collective-permute-done.10.refs_3_, ...), custom_call_target="tpu_custom_call" | custom-call | flops 100000000 | tf_op jit(solution)/shard_map/forward/pallas_call | solution.py:52
  74.5 2.1 %collective-permute-done.11.refs_3_ = bf16[512,256]{1,0:T(8,128)(2,1)S(1)} collective-permute-done((bf16[512,256]{1,0:T(8,128)(2,1)}, bf16[512,256]{1,0:T(8,128)(2,1)S(1)}, u32[]{:S(2)}, u32[]{:S(2)}) %collective-permute-start.11) | collective-permute-done | bytes 262176 | tf_op jit(solution)/shard_map/ppermute | solution.py:265
  76.6 5.2 %collective-permute-done.8.refs_2_ = bf16[512,256]{1,0:T(8,128)(2,1)S(1)} collective-permute-done((bf16[512,256]{1,0:T(8,128)(2,1)S(1)}, bf16[512,256]{1,0:T(8,128)(2,1)S(1)}, u32[]{:S(2)}, u32[]{:S(2)}) %collective-permute-start.8) | collective-permute-done | bytes 262176 | tf_op jit(solution)/shard_map/ppermute | solution.py:265
  81.9 1.6 %forward.7 = (bf16[512,256]{1,0:T(8,128)(2,1)S(1)}, bf16[512,256]{1,0:T(8,128)(2,1)S(1)}, bf16[512,256]{1,0:T(8,128)(2,1)S(1)}, bf16[512,256]{1,0:T(8,128)(2,1)S...) custom-call(bf16[1024,512]{1,0:T(8,128)(2,1)S(1)} %copy-done.1, ...), custom_call_target="tpu_custom_call" | custom-call | flops 300000000 | tf_op jit(solution)/shard_map/forward/pallas_call | solution.py:52
  83.5 1.7 %collective-permute-start.21 = (bf16[512,256]{1,0:T(8,128)(2,1)S(1)}, bf16[512,256]{1,0:T(8,128)(2,1)S(1)}, u32[]{:S(2)}, u32[]{:S(2)}) collective-permute-start(bf16[512,256]{1,0:T(8,128)(2,1)S(1)} %get-tuple-element.119), channel_id=1, source_target_pairs={{0,6},{2,0},{4,2},{6,4},{1,7},{3,1},{5,3},{7,5},{8,14},{10,8},{12,... | collective-permute-start | bytes 786440 | tf_op jit(solution)/shard_map/ppermute | solution.py:265
  86.0 6.8 %collective-permute-done.21.refs_1_ = bf16[512,256]{1,0:T(8,128)(2,1)S(1)} collective-permute-done((bf16[512,256]{1,0:T(8,128)(2,1)S(1)}, bf16[512,256]{1,0:T(8,128)(2,1)S(1)}, u32[]{:S(2)}, u32[]{:S(2)}) %collective-permute-start.21) | collective-permute-done | bytes 262176 | tf_op jit(solution)/shard_map/ppermute | solution.py:265
  93.4 3.4 %collective-permute-start.22 = (bf16[512,256]{1,0:T(8,128)(2,1)S(1)}, bf16[512,256]{1,0:T(8,128)(2,1)S(1)}, u32[]{:S(2)}, u32[]{:S(2)}) collective-permute-start(bf16[512,256]{1,0:T(8,128)(2,1)S(1)} %get-tuple-element.120), channel_id=1, source_target_pairs={{0,6},{2,0},{4,2},{6,4},{1,7},{3,1},{5,3},{7,5},{8,14},{10,8},{12,... | collective-permute-start | bytes 786440 | tf_op jit(solution)/shard_map/ppermute | solution.py:265
  96.8 1.5 %collective-permute-done.18.refs_1_ = bf16[512,256]{1,0:T(8,128)(2,1)S(1)} collective-permute-done((bf16[512,256]{1,0:T(8,128)(2,1)S(1)}, bf16[512,256]{1,0:T(8,128)(2,1)S(1)}, u32[]{:S(2)}, u32[]{:S(2)}) %collective-permute-start.18) | collective-permute-done | bytes 262176 | tf_op jit(solution)/shard_map/ppermute | solution.py:265
  99.0 3.4 %collective-permute-start.19 = (bf16[512,256]{1,0:T(8,128)(2,1)S(1)}, bf16[512,256]{1,0:T(8,128)(2,1)S(1)}, u32[]{:S(2)}, u32[]{:S(2)}) collective-permute-start(bf16[512,256]{1,0:T(8,128)(2,1)S(1)} %get-tuple-element.115), channel_id=1, source_target_pairs={{0,6},{2,0},{4,2},{6,4},{1,7},{3,1},{5,3},{7,5},{8,14},{10,8},{12,... | collective-permute-start | bytes 786440 | tf_op jit(solution)/shard_map/ppermute | solution.py:265
  104.6 3.9 %collective-permute-start.23 = (bf16[512,256]{1,0:T(8,128)(2,1)S(1)}, bf16[512,256]{1,0:T(8,128)(2,1)S(1)}, u32[]{:S(2)}, u32[]{:S(2)}) collective-permute-start(bf16[512,256]{1,0:T(8,128)(2,1)S(1)} %get-tuple-element.121), channel_id=1, source_target_pairs={{0,6},{2,0},{4,2},{6,4},{1,7},{3,1},{5,3},{7,5},{8,14},{10,8},{12,... | collective-permute-start | bytes 786440 | tf_op jit(solution)/shard_map/ppermute | solution.py:265
  108.5 1.1 collective-permute-done.19.refs_1_
  110.2 3.9 %collective-permute-start.20 = (bf16[512,256]{1,0:T(8,128)(2,1)S(1)}, bf16[512,256]{1,0:T(8,128)(2,1)S(1)}, u32[]{:S(2)}, u32[]{:S(2)}) collective-permute-start(bf16[512,256]{1,0:T(8,128)(2,1)S(1)} %get-tuple-element.116), channel_id=1, source_target_pairs={{0,6},{2,0},{4,2},{6,4},{1,7},{3,1},{5,3},{7,5},{8,14},{10,8},{12,... | collective-permute-start | bytes 786440 | tf_op jit(solution)/shard_map/ppermute | solution.py:265
  115.3 4.3 %collective-permute-done.20.refs_5_ = bf16[512,256]{1,0:T(8,128)(2,1)S(1)} collective-permute-done((bf16[512,256]{1,0:T(8,128)(2,1)S(1)}, bf16[512,256]{1,0:T(8,128)(2,1)S(1)}, u32[]{:S(2)}, u32[]{:S(2)}) %collective-permute-start.20) | collective-permute-done | bytes 262176 | tf_op jit(solution)/shard_map/ppermute | solution.py:265
  119.6 1.3 grad.1
  120.9 1.8 %collective-permute-start.24 = (bf16[256,256]{1,0:T(8,128)(2,1)S(1)}, bf16[256,256]{1,0:T(8,128)(2,1)S(1)}, u32[]{:S(2)}, u32[]{:S(2)}) collective-permute-start(bf16[256,256]{1,0:T(8,128)(2,1)S(1)} %get-tuple-element.123), channel_id=1, source_target_pairs={{0,8},{8,0},{16,24},{24,16},{1,9},{9,1},{17,25},{25,17},{2,10},{10... | collective-permute-start | bytes 393224 | tf_op jit(solution)/shard_map/ppermute | solution.py:262
  123.2 1.2 collective-permute-start.26
  124.4 2.2 %collective-permute-done.24.refs_1_ = bf16[256,256]{1,0:T(8,128)(2,1)S(1)} collective-permute-done((bf16[256,256]{1,0:T(8,128)(2,1)S(1)}, bf16[256,256]{1,0:T(8,128)(2,1)S(1)}, u32[]{:S(2)}, u32[]{:S(2)}) %collective-permute-start.24) | collective-permute-done | bytes 131104 | tf_op jit(solution)/shard_map/ppermute | solution.py:262
  126.6 3.2 %collective-permute-done.25.refs_2_ = bf16[256,256]{1,0:T(8,128)(2,1)S(1)} collective-permute-done((bf16[256,256]{1,0:T(8,128)(2,1)S(1)}, bf16[256,256]{1,0:T(8,128)(2,1)S(1)}, u32[]{:S(2)}, u32[]{:S(2)}) %collective-permute-start.25) | collective-permute-done | bytes 131104 | tf_op jit(solution)/shard_map/ppermute | solution.py:262
  130.0 5.0 %collective-permute-done.27.refs_1_ = bf16[256,256]{1,0:T(8,128)(2,1)S(1)} collective-permute-done((bf16[256,256]{1,0:T(8,128)(2,1)S(1)}, bf16[256,256]{1,0:T(8,128)(2,1)S(1)}, u32[]{:S(2)}, u32[]{:S(2)}) %collective-permute-start.27) | collective-permute-done | bytes 131104 | tf_op jit(solution)/shard_map/ppermute | solution.py:424
  135.0 2.0 %collective-permute-start.28 = (bf16[256,256]{1,0:T(8,128)(2,1)S(1)}, bf16[256,256]{1,0:T(8,128)(2,1)S(1)}, u32[]{:S(2)}, u32[]{:S(2)}) collective-permute-start(bf16[256,256]{1,0:T(8,128)(2,1)S(1)} %sum.4.refs_0_), channel_id=1, source_target_pairs={{0,4},{2,6},{4,0},{6,2},{1,5},{3,7},{5,1},{7,3},{8,12},{10,14},{12... | collective-permute-start | bytes 393224 | tf_op jit(solution)/shard_map/ppermute | solution.py:424
  137.0 5.2 %collective-permute-done.28.refs_1_ = bf16[256,256]{1,0:T(8,128)(2,1)S(1)} collective-permute-done((bf16[256,256]{1,0:T(8,128)(2,1)S(1)}, bf16[256,256]{1,0:T(8,128)(2,1)S(1)}, u32[]{:S(2)}, u32[]{:S(2)}) %collective-permute-start.28) | collective-permute-done | bytes 131104 | tf_op jit(solution)/shard_map/ppermute | solution.py:424
  143.2 0.9 collective-permute-start.30
  144.1 1.7 %collective-permute-start.31 = (bf16[256,256]{1,0:T(8,128)(2,1)S(1)}, bf16[256,256]{1,0:T(8,128)(2,1)S(1)}, u32[]{:S(2)}, u32[]{:S(2)}) collective-permute-start(bf16[256,256]{1,0:T(8,128)(2,1)S(1)} %sum.5.refs_1_), channel_id=1, source_target_pairs={{0,24},{8,16},{16,8},{24,0},{1,25},{9,17},{17,9},{25,1},{2,26},{10... | collective-permute-start | bytes 393224 | tf_op jit(solution)/shard_map/ppermute | solution.py:262
  145.8 1.5 collective-permute-done.29.refs_2_
  148.2 1.8 %collective-permute-done.31.refs_4_ = bf16[256,256]{1,0:T(8,128)(2,1)S(1)} collective-permute-done((bf16[256,256]{1,0:T(8,128)(2,1)S(1)}, bf16[256,256]{1,0:T(8,128)(2,1)S(1)}, u32[]{:S(2)}, u32[]{:S(2)}) %collective-permute-start.31) | collective-permute-done | bytes 131104 | tf_op jit(solution)/shard_map/ppermute | solution.py:262
  151.3 2.0 %last.1 = f32[1024,512]{1,0:T(8,128)} custom-call(s32[3]{0:T(128)S(1)} %pad_add_fusion.refs_0_, bf16[256,256]{1,0:T(8,128)(2,1)S(1)} %sum.5.refs_1_, bf16[256,256]{1,0:T(8,128)(2,1)S(1)} %collective-permute-done.29.refs_2_, bf16[256,256]{1,0:T(8,128)(2,1)S(1)} %collective-permute-done.30.refs_3_, bf16[256,256]{1,0:T(8,128)(2,1)S(1)} %collective-permute-done.31.refs_4_, ...), custom_call_target="tpu_custom_call" | custom-call | flops 200000000 | tf_op jit(solution)/shard_map/last/pallas_call | solution.py:52
  (92 shorter events, 17.4 us)
Async XLA Ops:
  0.6 57.8 %collective-permute-start.5 = (bf16[4,16,128,128]{3,2,1,0:T(8,128)(2,1)}, bf16[4,16,128,128]{3,2,1,0:T(8,128)(2,1)}, u32[]{:S(2)}, u32[]{:S(2)}) collective-permute-start(bf16[4,16,128,128]{3,2,1,0:T(8,128)(2,1)} %refs_3_.1), channel_id=1, source_target_pairs={{0,1},{1,0},{2,3},{3,2},{4,5},{5,4},{6,7},{7,6},{8,9},{9,8},{10,11... | collective-permute-start | bytes 6291464 | tf_op jit(solution)/shard_map/ppermute | solution.py:259
  5.5 27.8 %copy-start.17 = (s32[4,16]{1,0:T(4,128)S(1)}, s32[4,16]{1,0:T(4,128)}, u32[]{:S(2)}) copy-start(s32[4,16]{1,0:T(4,128)} %param.9) | copy-start | bytes 772
  5.5 27.9 %copy-start.18 = (s32[4]{0:T(128)S(1)}, s32[4]{0:T(128)}, u32[]{:S(2)}) copy-start(s32[4]{0:T(128)} %param.10) | copy-start | bytes 52
  5.5 28.5 %copy-start.14 = (bf16[4,16,128,128]{3,2,1,0:T(8,128)(2,1)S(1)}, bf16[4,16,128,128]{3,2,1,0:T(8,128)(2,1)}, u32[]{:S(2)}) copy-start(bf16[4,16,128,128]{3,2,1,0:T(8,128)(2,1)} %refs_3_.1) | copy-start | bytes 6291460
  6.7 42.6 %copy-start.3 = (bf16[512,1024]{1,0:T(8,128)(2,1)S(1)}, bf16[512,1024]{1,0:T(8,128)(2,1)}, u32[]{:S(2)}) copy-start(bf16[512,1024]{1,0:T(8,128)(2,1)} %refs_1_.1) | copy-start | bytes 3145732
  6.8 15.4 %collective-permute-start = (bf16[512,256]{1,0:T(8,128)(2,1)S(1)}, bf16[512,256]{1,0:T(8,128)(2,1)S(1)}, u32[]{:S(2)}, u32[]{:S(2)}) collective-permute-start(bf16[512,256]{1,0:T(8,128)(2,1)S(1)} %get-tuple-element.67), channel_id=1, source_target_pairs={{0,1},{1,0},{2,3},{3,2},{4,5},{5,4},{6,7},{7,6},{8,9},{9,8},{10,11... | collective-permute-start | bytes 786440 | tf_op jit(solution)/shard_map/ppermute | solution.py:259
  23.8 6.4 %collective-permute-start.1 = (bf16[2,128,256]{2,1,0:T(8,128)(2,1)S(1)}, bf16[2,128,256]{2,1,0:T(8,128)(2,1)S(1)}, u32[]{:S(2)}, u32[]{:S(2)}) collective-permute-start(bf16[2,128,256]{2,1,0:T(8,128)(2,1)S(1)} %get-tuple-element.69), channel_id=1, source_target_pairs={{0,8},{8,0},{16,24},{24,16},{1,9},{9,1},{17,25},{25,17},{2,10},{10... | collective-permute-start | bytes 393224 | tf_op jit(solution)/shard_map/ppermute | solution.py:262
  24.7 7.8 %collective-permute-start.2 = (bf16[2,128,256]{2,1,0:T(8,128)(2,1)S(1)}, bf16[2,128,256]{2,1,0:T(8,128)(2,1)S(1)}, u32[]{:S(2)}, u32[]{:S(2)}) collective-permute-start(bf16[2,128,256]{2,1,0:T(8,128)(2,1)S(1)} %get-tuple-element.70), channel_id=1, source_target_pairs={{0,16},{8,24},{16,0},{24,8},{1,17},{9,25},{17,1},{25,9},{2,18},{10... | collective-permute-start | bytes 393224 | tf_op jit(solution)/shard_map/ppermute | solution.py:262
  25.4 7.1 %collective-permute-start.3 = (bf16[2,128,256]{2,1,0:T(8,128)(2,1)S(1)}, bf16[2,128,256]{2,1,0:T(8,128)(2,1)S(1)}, u32[]{:S(2)}, u32[]{:S(2)}) collective-permute-start(bf16[2,128,256]{2,1,0:T(8,128)(2,1)S(1)} %get-tuple-element.71), channel_id=1, source_target_pairs={{0,24},{8,16},{16,8},{24,0},{1,25},{9,17},{17,9},{25,1},{2,26},{10... | collective-permute-start | bytes 393224 | tf_op jit(solution)/shard_map/ppermute | solution.py:262
  32.5 22.4 %copy-start.4 = (bf16[512,256]{1,0:T(8,128)(2,1)}, bf16[512,256]{1,0:T(8,128)(2,1)S(1)}, u32[]{:S(2)}) copy-start(bf16[512,256]{1,0:T(8,128)(2,1)S(1)} %get-tuple-element.77.refs_2_) | copy-start | bytes 786436
  32.5 22.3 %copy-start.6 = (bf16[512,256]{1,0:T(8,128)(2,1)}, bf16[512,256]{1,0:T(8,128)(2,1)S(1)}, u32[]{:S(2)}) copy-start(bf16[512,256]{1,0:T(8,128)(2,1)S(1)} %get-tuple-element.85.refs_3_) | copy-start | bytes 786436
  32.6 11.1 %collective-permute-start.6 = (bf16[512,256]{1,0:T(8,128)(2,1)S(1)}, bf16[512,256]{1,0:T(8,128)(2,1)S(1)}, u32[]{:S(2)}, u32[]{:S(2)}) collective-permute-start(bf16[512,256]{1,0:T(8,128)(2,1)S(1)} %get-tuple-element.77.refs_2_), channel_id=1, source_target_pairs={{0,2},{2,4},{4,6},{6,0},{1,3},{3,5},{5,7},{7,1},{8,10},{10,12},{12... | collective-permute-start | bytes 786440 | tf_op jit(solution)/shard_map/ppermute | solution.py:265
  33.4 16.0 %collective-permute-start.9 = (bf16[512,256]{1,0:T(8,128)(2,1)S(1)}, bf16[512,256]{1,0:T(8,128)(2,1)}, u32[]{:S(2)}, u32[]{:S(2)}) collective-permute-start(bf16[512,256]{1,0:T(8,128)(2,1)S(1)} %get-tuple-element.85.refs_3_), channel_id=1, source_target_pairs={{0,2},{2,4},{4,6},{6,0},{1,3},{3,5},{5,7},{7,1},{8,10},{10,12},{12... | collective-permute-start | bytes 786440 | tf_op jit(solution)/shard_map/ppermute | solution.py:265
  43.7 11.2 %collective-permute-start.7 = (bf16[512,256]{1,0:T(8,128)(2,1)S(1)}, bf16[512,256]{1,0:T(8,128)(2,1)S(1)}, u32[]{:S(2)}, u32[]{:S(2)}) collective-permute-start(bf16[512,256]{1,0:T(8,128)(2,1)S(1)} %collective-permute-done.6.refs_2_), channel_id=1, source_target_pairs={{0,2},{2,4},{4,6},{6,0},{1,3},{3,5},{5,7},{7,1},{8,10},{10,12},{12... | collective-permute-start | bytes 786440 | tf_op jit(solution)/shard_map/ppermute | solution.py:265
  49.4 16.1 %collective-permute-start.10 = (bf16[512,256]{1,0:T(8,128)(2,1)}, bf16[512,256]{1,0:T(8,128)(2,1)}, u32[]{:S(2)}, u32[]{:S(2)}) collective-permute-start(bf16[512,256]{1,0:T(8,128)(2,1)} %collective-permute-done.9.refs_3_), channel_id=1, source_target_pairs={{0,2},{2,4},{4,6},{6,0},{1,3},{3,5},{5,7},{7,1},{8,10},{10,12},{12... | collective-permute-start | bytes 786440 | tf_op jit(solution)/shard_map/ppermute | solution.py:265
  51.5 14.0 %collective-permute-start.13 = (bf16[128,1024]{1,0:T(8,128)(2,1)}, bf16[128,1024]{1,0:T(8,128)(2,1)}, u32[]{:S(2)}, u32[]{:S(2)}) collective-permute-start(bf16[128,1024]{1,0:T(8,128)(2,1)} %get-tuple-element.99), channel_id=1, source_target_pairs={{0,8},{8,0},{16,24},{24,16},{1,9},{9,1},{17,25},{25,17},{2,10},{10... | collective-permute-start | bytes 786440 | tf_op jit(solution)/shard_map/ppermute | solution.py:262
  53.2 1.2 collective-permute-start.4
  54.3 14.3 %collective-permute-start.14 = (bf16[128,1024]{1,0:T(8,128)(2,1)}, bf16[128,1024]{1,0:T(8,128)(2,1)}, u32[]{:S(2)}, u32[]{:S(2)}) collective-permute-start(bf16[128,1024]{1,0:T(8,128)(2,1)} %get-tuple-element.100), channel_id=1, source_target_pairs={{0,16},{8,24},{16,0},{24,8},{1,17},{9,25},{17,1},{25,9},{2,18},{10... | collective-permute-start | bytes 786440 | tf_op jit(solution)/shard_map/ppermute | solution.py:262
  55.6 13.1 %collective-permute-start.15 = (bf16[128,1024]{1,0:T(8,128)(2,1)}, bf16[128,1024]{1,0:T(8,128)(2,1)}, u32[]{:S(2)}, u32[]{:S(2)}) collective-permute-start(bf16[128,1024]{1,0:T(8,128)(2,1)} %get-tuple-element.101), channel_id=1, source_target_pairs={{0,24},{8,16},{16,8},{24,0},{1,25},{9,17},{17,9},{25,1},{2,26},{10... | collective-permute-start | bytes 786440 | tf_op jit(solution)/shard_map/ppermute | solution.py:262
  57.2 11.4 %copy-start.13 = (bf16[128,1024]{1,0:T(8,128)(2,1)S(1)}, bf16[128,1024]{1,0:T(8,128)(2,1)}, u32[]{:S(2)}) copy-start(bf16[128,1024]{1,0:T(8,128)(2,1)} %copy-done.12) | copy-start | bytes 786436
  57.2 12.9 %copy-start.5 = (bf16[512,256]{1,0:T(8,128)(2,1)S(1)}, bf16[512,256]{1,0:T(8,128)(2,1)}, u32[]{:S(2)}) copy-start(bf16[512,256]{1,0:T(8,128)(2,1)} %copy-done.4) | copy-start | bytes 786436
  57.2 13.0 %copy-start.7 = (bf16[512,256]{1,0:T(8,128)(2,1)S(1)}, bf16[512,256]{1,0:T(8,128)(2,1)}, u32[]{:S(2)}) copy-start(bf16[512,256]{1,0:T(8,128)(2,1)} %copy-done.6) | copy-start | bytes 786436
  58.4 14.3 %collective-permute-start.12 = (bf16[512,256]{1,0:T(8,128)(2,1)S(1)}, bf16[512,256]{1,0:T(8,128)(2,1)S(1)}, u32[]{:S(2)}, u32[]{:S(2)}) collective-permute-start(bf16[512,256]{1,0:T(8,128)(2,1)S(1)} %get-tuple-element.128), channel_id=1, source_target_pairs={{0,1},{1,0},{2,3},{3,2},{4,5},{5,4},{6,7},{7,6},{8,9},{9,8},{10,11... | collective-permute-start | bytes 786440 | tf_op jit(solution)/shard_map/ppermute | solution.py:259
  65.5 11.2 %collective-permute-start.11 = (bf16[512,256]{1,0:T(8,128)(2,1)}, bf16[512,256]{1,0:T(8,128)(2,1)S(1)}, u32[]{:S(2)}, u32[]{:S(2)}) collective-permute-start(bf16[512,256]{1,0:T(8,128)(2,1)} %collective-permute-done.10.refs_3_), channel_id=1, source_target_pairs={{0,2},{2,4},{4,6},{6,0},{1,3},{3,5},{5,7},{7,1},{8,10},{10,12},{12... | collective-permute-start | bytes 786440 | tf_op jit(solution)/shard_map/ppermute | solution.py:265
  65.5 16.3 %collective-permute-start.8 = (bf16[512,256]{1,0:T(8,128)(2,1)S(1)}, bf16[512,256]{1,0:T(8,128)(2,1)S(1)}, u32[]{:S(2)}, u32[]{:S(2)}) collective-permute-start(bf16[512,256]{1,0:T(8,128)(2,1)S(1)} %copy-done.9), channel_id=1, source_target_pairs={{0,2},{2,4},{4,6},{6,0},{1,3},{3,5},{5,7},{7,1},{8,10},{10,12},{12... | collective-permute-start | bytes 786440 | tf_op jit(solution)/shard_map/ppermute | solution.py:265
  70.1 44.7 %collective-permute-start.17 = (bf16[1024,512]{1,0:T(8,128)(2,1)S(1)}, bf16[1024,512]{1,0:T(8,128)(2,1)S(1)}, u32[]{:S(2)}, u32[]{:S(2)}) collective-permute-start(bf16[1024,512]{1,0:T(8,128)(2,1)S(1)} %get-tuple-element.107.refs_1_), channel_id=1, source_target_pairs={{0,1},{1,0},{2,3},{3,2},{4,5},{5,4},{6,7},{7,6},{8,9},{9,8},{10,11... | collective-permute-start | bytes 3145736 | tf_op jit(solution)/shard_map/ppermute | solution.py:259
  72.7 9.2 %copy-start.1 = (bf16[1024,512]{1,0:T(8,128)(2,1)S(1)}, bf16[1024,512]{1,0:T(8,128)(2,1)}, u32[]{:S(2)}) copy-start(bf16[1024,512]{1,0:T(8,128)(2,1)} %copy-done) | copy-start | bytes 3145732
  83.5 15.5 %copy-start.10 = (bf16[512,256]{1,0:T(8,128)(2,1)}, bf16[512,256]{1,0:T(8,128)(2,1)S(1)}, u32[]{:S(2)}) copy-start(bf16[512,256]{1,0:T(8,128)(2,1)S(1)} %get-tuple-element.105) | copy-start | bytes 786436
  83.5 9.3 %collective-permute-start.21 = (bf16[512,256]{1,0:T(8,128)(2,1)S(1)}, bf16[512,256]{1,0:T(8,128)(2,1)S(1)}, u32[]{:S(2)}, u32[]{:S(2)}) collective-permute-start(bf16[512,256]{1,0:T(8,128)(2,1)S(1)} %get-tuple-element.119), channel_id=1, source_target_pairs={{0,6},{2,0},{4,2},{6,4},{1,7},{3,1},{5,3},{7,5},{8,14},{10,8},{12,... | collective-permute-start | bytes 786440 | tf_op jit(solution)/shard_map/ppermute | solution.py:265
  85.2 13.2 %collective-permute-start.18 = (bf16[512,256]{1,0:T(8,128)(2,1)S(1)}, bf16[512,256]{1,0:T(8,128)(2,1)S(1)}, u32[]{:S(2)}, u32[]{:S(2)}) collective-permute-start(bf16[512,256]{1,0:T(8,128)(2,1)S(1)} %get-tuple-element.114), channel_id=1, source_target_pairs={{0,6},{2,0},{4,2},{6,4},{1,7},{3,1},{5,3},{7,5},{8,14},{10,8},{12,... | collective-permute-start | bytes 786440 | tf_op jit(solution)/shard_map/ppermute | solution.py:265
  85.3 17.9 %collective-permute-start.16 = (bf16[512,256]{1,0:T(8,128)(2,1)S(1)}, bf16[512,256]{1,0:T(8,128)(2,1)S(1)}, u32[]{:S(2)}, u32[]{:S(2)}) collective-permute-start(bf16[512,256]{1,0:T(8,128)(2,1)S(1)} %get-tuple-element.106), channel_id=1, source_target_pairs={{0,1},{1,0},{2,3},{3,2},{4,5},{5,4},{6,7},{7,6},{8,9},{9,8},{10,11... | collective-permute-start | bytes 786440 | tf_op jit(solution)/shard_map/ppermute | solution.py:259
  93.4 10.6 %collective-permute-start.22 = (bf16[512,256]{1,0:T(8,128)(2,1)S(1)}, bf16[512,256]{1,0:T(8,128)(2,1)S(1)}, u32[]{:S(2)}, u32[]{:S(2)}) collective-permute-start(bf16[512,256]{1,0:T(8,128)(2,1)S(1)} %get-tuple-element.120), channel_id=1, source_target_pairs={{0,6},{2,0},{4,2},{6,4},{1,7},{3,1},{5,3},{7,5},{8,14},{10,8},{12,... | collective-permute-start | bytes 786440 | tf_op jit(solution)/shard_map/ppermute | solution.py:265
  99.0 10.6 %collective-permute-start.19 = (bf16[512,256]{1,0:T(8,128)(2,1)S(1)}, bf16[512,256]{1,0:T(8,128)(2,1)S(1)}, u32[]{:S(2)}, u32[]{:S(2)}) collective-permute-start(bf16[512,256]{1,0:T(8,128)(2,1)S(1)} %get-tuple-element.115), channel_id=1, source_target_pairs={{0,6},{2,0},{4,2},{6,4},{1,7},{3,1},{5,3},{7,5},{8,14},{10,8},{12,... | collective-permute-start | bytes 786440 | tf_op jit(solution)/shard_map/ppermute | solution.py:265
  104.6 10.6 %collective-permute-start.23 = (bf16[512,256]{1,0:T(8,128)(2,1)S(1)}, bf16[512,256]{1,0:T(8,128)(2,1)S(1)}, u32[]{:S(2)}, u32[]{:S(2)}) collective-permute-start(bf16[512,256]{1,0:T(8,128)(2,1)S(1)} %get-tuple-element.121), channel_id=1, source_target_pairs={{0,6},{2,0},{4,2},{6,4},{1,7},{3,1},{5,3},{7,5},{8,14},{10,8},{12,... | collective-permute-start | bytes 786440 | tf_op jit(solution)/shard_map/ppermute | solution.py:265
  110.2 9.3 %collective-permute-start.20 = (bf16[512,256]{1,0:T(8,128)(2,1)S(1)}, bf16[512,256]{1,0:T(8,128)(2,1)S(1)}, u32[]{:S(2)}, u32[]{:S(2)}) collective-permute-start(bf16[512,256]{1,0:T(8,128)(2,1)S(1)} %get-tuple-element.116), channel_id=1, source_target_pairs={{0,6},{2,0},{4,2},{6,4},{1,7},{3,1},{5,3},{7,5},{8,14},{10,8},{12,... | collective-permute-start | bytes 786440 | tf_op jit(solution)/shard_map/ppermute | solution.py:265
  119.6 30.4 %copy-start.11 = (bf16[512,256]{1,0:T(8,128)(2,1)S(1)}, bf16[512,256]{1,0:T(8,128)(2,1)}, u32[]{:S(2)}) copy-start(bf16[512,256]{1,0:T(8,128)(2,1)} %copy-done.10) | copy-start | bytes 786436
  120.9 5.7 %collective-permute-start.24 = (bf16[256,256]{1,0:T(8,128)(2,1)S(1)}, bf16[256,256]{1,0:T(8,128)(2,1)S(1)}, u32[]{:S(2)}, u32[]{:S(2)}) collective-permute-start(bf16[256,256]{1,0:T(8,128)(2,1)S(1)} %get-tuple-element.123), channel_id=1, source_target_pairs={{0,8},{8,0},{16,24},{24,16},{1,9},{9,1},{17,25},{25,17},{2,10},{10... | collective-permute-start | bytes 393224 | tf_op jit(solution)/shard_map/ppermute | solution.py:262
  122.7 7.1 %collective-permute-start.25 = (bf16[256,256]{1,0:T(8,128)(2,1)S(1)}, bf16[256,256]{1,0:T(8,128)(2,1)S(1)}, u32[]{:S(2)}, u32[]{:S(2)}) collective-permute-start(bf16[256,256]{1,0:T(8,128)(2,1)S(1)} %get-tuple-element.124), channel_id=1, source_target_pairs={{0,16},{8,24},{16,0},{24,8},{1,17},{9,25},{17,1},{25,9},{2,18},{10... | collective-permute-start | bytes 393224 | tf_op jit(solution)/shard_map/ppermute | solution.py:262
  123.2 6.6 %collective-permute-start.26 = (bf16[256,256]{1,0:T(8,128)(2,1)S(1)}, bf16[256,256]{1,0:T(8,128)(2,1)S(1)}, u32[]{:S(2)}, u32[]{:S(2)}) collective-permute-start(bf16[256,256]{1,0:T(8,128)(2,1)S(1)} %get-tuple-element.125), channel_id=1, source_target_pairs={{0,24},{8,16},{16,8},{24,0},{1,25},{9,17},{17,9},{25,1},{2,26},{10... | collective-permute-start | bytes 393224 | tf_op jit(solution)/shard_map/ppermute | solution.py:262
  129.9 5.0 %collective-permute-start.27 = (bf16[256,256]{1,0:T(8,128)(2,1)S(1)}, bf16[256,256]{1,0:T(8,128)(2,1)S(1)}, u32[]{:S(2)}, u32[]{:S(2)}) collective-permute-start(bf16[256,256]{1,0:T(8,128)(2,1)S(1)} %sum.3.refs_0_), channel_id=1, source_target_pairs={{0,2},{2,0},{4,6},{6,4},{1,3},{3,1},{5,7},{7,5},{8,10},{10,8},{12,... | collective-permute-start | bytes 393224 | tf_op jit(solution)/shard_map/ppermute | solution.py:424
  135.0 7.2 %collective-permute-start.28 = (bf16[256,256]{1,0:T(8,128)(2,1)S(1)}, bf16[256,256]{1,0:T(8,128)(2,1)S(1)}, u32[]{:S(2)}, u32[]{:S(2)}) collective-permute-start(bf16[256,256]{1,0:T(8,128)(2,1)S(1)} %sum.4.refs_0_), channel_id=1, source_target_pairs={{0,4},{2,6},{4,0},{6,2},{1,5},{3,7},{5,1},{7,3},{8,12},{10,14},{12... | collective-permute-start | bytes 393224 | tf_op jit(solution)/shard_map/ppermute | solution.py:424
  142.2 5.0 %collective-permute-start.29 = (bf16[256,256]{1,0:T(8,128)(2,1)S(1)}, bf16[256,256]{1,0:T(8,128)(2,1)S(1)}, u32[]{:S(2)}, u32[]{:S(2)}) collective-permute-start(bf16[256,256]{1,0:T(8,128)(2,1)S(1)} %sum.5.refs_1_), channel_id=1, source_target_pairs={{0,8},{8,0},{16,24},{24,16},{1,9},{9,1},{17,25},{25,17},{2,10},{10... | collective-permute-start | bytes 393224 | tf_op jit(solution)/shard_map/ppermute | solution.py:262
  143.2 5.0 %collective-permute-start.30 = (bf16[256,256]{1,0:T(8,128)(2,1)S(1)}, bf16[256,256]{1,0:T(8,128)(2,1)S(1)}, u32[]{:S(2)}, u32[]{:S(2)}) collective-permute-start(bf16[256,256]{1,0:T(8,128)(2,1)S(1)} %sum.5.refs_1_), channel_id=1, source_target_pairs={{0,16},{8,24},{16,0},{24,8},{1,17},{9,25},{17,1},{25,9},{2,18},{10... | collective-permute-start | bytes 393224 | tf_op jit(solution)/shard_map/ppermute | solution.py:262
  144.1 5.9 %collective-permute-start.31 = (bf16[256,256]{1,0:T(8,128)(2,1)S(1)}, bf16[256,256]{1,0:T(8,128)(2,1)S(1)}, u32[]{:S(2)}, u32[]{:S(2)}) collective-permute-start(bf16[256,256]{1,0:T(8,128)(2,1)S(1)} %sum.5.refs_1_), channel_id=1, source_target_pairs={{0,24},{8,16},{16,8},{24,0},{1,25},{9,17},{17,9},{25,1},{2,26},{10... | collective-permute-start | bytes 393224 | tf_op jit(solution)/shard_map/ppermute | solution.py:262
  145.8 5.1 %collective-permute-start.32 = (bf16[256,256]{1,0:T(8,128)(2,1)S(1)}, bf16[256,256]{1,0:T(8,128)(2,1)S(1)}, u32[]{:S(2)}, u32[]{:S(2)}) collective-permute-start(bf16[256,256]{1,0:T(8,128)(2,1)S(1)} %sum.5.refs_1_), channel_id=1, source_target_pairs={{0,1},{1,0},{2,3},{3,2},{4,5},{5,4},{6,7},{7,6},{8,9},{9,8},{10,11... | collective-permute-start | bytes 393224 | tf_op jit(solution)/shard_map/ppermute | solution.py:259
  147.3 3.6 %collective-permute-start.33 = (bf16[256,256]{1,0:T(8,128)(2,1)S(1)}, bf16[256,256]{1,0:T(8,128)(2,1)S(1)}, u32[]{:S(2)}, u32[]{:S(2)}) collective-permute-start(bf16[256,256]{1,0:T(8,128)(2,1)S(1)} %collective-permute-done.29.refs_2_), channel_id=1, source_target_pairs={{0,1},{1,0},{2,3},{3,2},{4,5},{5,4},{6,7},{7,6},{8,9},{9,8},{10,11... | collective-permute-start | bytes 393224 | tf_op jit(solution)/shard_map/ppermute | solution.py:259
  148.1 2.7 %collective-permute-start.34 = (bf16[256,256]{1,0:T(8,128)(2,1)S(1)}, bf16[256,256]{1,0:T(8,128)(2,1)S(1)}, u32[]{:S(2)}, u32[]{:S(2)}) collective-permute-start(bf16[256,256]{1,0:T(8,128)(2,1)S(1)} %collective-permute-done.30.refs_3_), channel_id=1, source_target_pairs={{0,1},{1,0},{2,3},{3,2},{4,5},{5,4},{6,7},{7,6},{8,9},{9,8},{10,11... | collective-permute-start | bytes 393224 | tf_op jit(solution)/shard_map/ppermute | solution.py:259
  150.0 1.3 collective-permute-start.35
  (7 other events, 13.8 us)

commit v12 on v11

--- a/solution.py
+++ b/solution.py
@@ -97,8 +97,7 @@
     want = (dot(owner, high) * 16.0 + dot(owner, low)).astype(I32)
     out_ref[...] = jnp.zeros_like(out_ref)
     for d in range(z.grp * z.dom):
-        for line, source in ((0, d), (5, d ^ 1)):
-            out_ref[d, line:line + 1, 0:z.pair] = want[source:source + 1, :]
+        out_ref[d, 0:1, 0:z.pair] = want[d:d + 1, :]
     across_grp = (source_r >> log2(z.dom)) ^ me_ref[0]
     inner = source_r & (z.dom - 1)
     slot = (inner * z.grp + across_grp) * z.pair + rank_r
@@ -114,24 +113,21 @@
         out[...] = dot(features_ref[...], weight_ref[:, pl.ds(at, half)]).astype(BF16)
 
 
-def send_kernel(z, lines, me_ref, message_ref, own_ref, other_ref, pick_ref, *outs):
+def send_kernel(z, me_ref, message_ref, own_ref, other_ref, pick_ref, *outs):
     devices, height, width = message_ref.shape
     message = message_ref[...].reshape(devices * height, width)
-    high_bits = (message >> 4).astype(F32).astype(BF16)
-    low_bits = (message & 15).astype(F32).astype(BF16)
     shape = (z.rows, devices * height)
     asker = (iota(shape, 0) >> log2(z.pair)) ^ (me_ref[0] * z.dom)
+    spread = one_hot(iota(shape, 1) == asker * height)
+    high = dot(spread, (message >> 4).astype(F32).astype(BF16))
+    low = dot(spread, (message & 15).astype(F32).astype(BF16))
     mine = iota((z.rows, width), 1) == (iota((z.rows, width), 0) & (z.pair - 1))
-    for rel, (line, product) in enumerate(zip(lines, (own_ref, other_ref))):
-        spread = one_hot(iota(shape, 1) == asker * height + line)
-        asked = dot(spread, high_bits) * 16.0 + dot(spread, low_bits)
-        wanted = jnp.sum(jnp.where(mine, asked, 0.0), axis=1, keepdims=True).astype(I32)
-        pick = one_hot(iota((z.rows, z.rows), 1) == wanted)
-        if rel == 0:
-            pick_ref[...] = pick
-        got = dot(pick, product[...]).astype(BF16)
+    wanted = jnp.sum(jnp.where(mine, high * 16.0 + low, 0.0), axis=1, keepdims=True).astype(I32)
+    pick_ref[...] = one_hot(iota((z.rows, z.rows), 1) == wanted)
+    for flip, product in enumerate((own_ref, other_ref)):
+        got = dot(pick_ref[...], product[...]).astype(BF16)
         for s in range(z.grp):
-            outs[s][rel] = got[s * z.per_grp:(s + 1) * z.per_grp, :]
+            outs[s][flip] = got[s * z.per_grp:(s + 1) * z.per_grp, :]
 
 
 def rows_kernel(z, pick_ref, features_ref, *outs):
@@ -277,23 +273,6 @@
     )
     vals_b = to_core(block_vals)
 
-    def products_of(part, after=()):
-        own, other = call(
-            lambda *refs: product_kernel(z, *refs),
-            [((rows, half), BF16)] * 2,
-            [("s", me), ("v", part), ("v", weight)],
-            "product", 15, after=after,
-        )
-        return own, to_core(other)
-
-    def send_of(lines, products, after=()):
-        return call(
-            lambda *refs: send_kernel(z, lines, *refs),
-            [((rows, rows), BF16)] + [((2, z.per_grp, half), BF16)] * z.grp,
-            [("s", me), ("v", message)] + [("v", part) for part in products],
-            "send", 1.5, after=after, token=True,
-        )
-
     def across(parts):
         return [to_grp(part, s) for s, part in enumerate(parts)]
 
@@ -320,11 +299,21 @@
         )
         return [left, to_core(left)], token
 
-    products = products_of(features)
-    pick, *got, token = send_of((0, 5), products)
-    token, cotangent = lax.optimization_barrier((token, cotangent))
-    *ring, token = pack(across(got), [token])
-    ring = [ring]
+    products = call(
+        lambda *refs: product_kernel(z, *refs),
+        [((rows, half), BF16)] * 2,
+        [("s", me), ("v", features), ("v", weight)],
+        "product", 15,
+    )
+    pick, *got, token = call(
+        lambda *refs: send_kernel(z, *refs),
+        [((rows, rows), BF16)] + [((2, z.per_grp, half), BF16)] * z.grp,
+        [("s", me), ("v", message)] + [("v", part) for part in products],
+        "send", 1.5, token=True,
+    )
+    token, cotangent, block_cols = lax.optimization_barrier((token, cotangent, block_cols))
+    own, other, token = pack(across(got), [token])
+    ring = [[own, to_core(other)]]
 
     live = iota((tiles, blocks), 1) < block_count[:, None]
     cols_a = jnp.where(live, block_cols, z.dom * tiles)
@@ -345,17 +334,17 @@
                 pltpu.VMEM((z.dom * rows + tile, tile), F32),
                 pltpu.VMEM((z.dom * rows, rows), BF16),
             ),
-            after=[token], token=True,
+            after=[token, cols_b], token=True,
         )
         return [part.reshape(wide, rows) for part in got], token
 
     for k in range(1, z.zz):
         ring.append([to_zz(part, 1) for part in ring[-1]])
         if k == 1:
+            *picked, token = rows_of(pick, features, [token, cot_a, cot_b])
+            lefts, token_l = turned_of(across(picked))
             turned_a, token = prepared(cols_a, block_vals, token)
             ring[1][0], token = lax.optimization_barrier((ring[1][0], token))
-            *picked, token = rows_of(pick, features, [token])
-            lefts, token_l = turned_of(across(picked))
         if k == 2:
             turned_b, token = prepared(cols_b, vals_b, token)
             ring[2][0], token = lax.optimization_barrier((ring[2][0], token))
@@ -373,7 +362,7 @@
         agg = call(
             lambda *refs, k=k, last=last: forward_kernel(z, k == 0, last, *refs),
             outs, ins, "forward", 3 if last else 1,
-            after=[cot_a, cot_b, token_l] if k == z.zz - 2 else [token] if k == 0 else (),
+            after=[token_l] if k == z.zz - 2 else [token] if k == 0 else (),
         )
     hidden_a, hidden_b, grad_a, grad_b, *came = agg
 

time: 154 us -> 141 us (0.916)
  blocking collectives: 15.3 us -> 0 us
  starting transfers between devices: 35.3 us -> 47.5 us
  Pallas kernels: 33.7 us -> 30.1 us
  local copies, waits for them, and re-layouts: 6.71 us -> 3.19 us
  waiting for transfers between devices: 60.4 us -> 57.7 us
    all_to_all x1 -> x0, blocking collectives: 15.3 us -> none  [shards(): lax.all_to_all(message, ('grp', 'zz', 'core'), split_axis=0, concat_axis=...]
    all_to_all x0 -> x1, starting transfers between devices: none -> 6.96 us  [shards(): lax.all_to_all(message, ('grp', 'zz', 'core'), split_axis=0, concat_axis=...]
    all_to_all x0 -> x1, waiting for transfers between devices: none -> 4.43 us  [shards(): lax.all_to_all(message, ('grp', 'zz', 'core'), split_axis=0, concat_axis=...]
    ppermute x12, waiting for transfers between devices: 17.7 us -> 13.4 us  [to_grp(): lax.ppermute(x, 'grp', [(i, i ^ s) for i in range(z.grp)])]
    ppermute x12, starting transfers between devices: 18 us -> 22.1 us  [to_zz(): lax.ppermute(x, 'zz', [(i, (i + k) % z.zz) for i in range(z.zz)])]
    pallas_call x24, Pallas kernels: 33.7 us -> 30.1 us  [call(): pl.pallas_call(kernel, out_shape=tuple((jax.ShapeDtypeStruct(s, d) for s,...]
    ppermute x12, waiting for transfers between devices: 30.9 us -> 27.5 us  [to_zz(): lax.ppermute(x, 'zz', [(i, (i + k) % z.zz) for i in range(z.zz)])]
    unnamed x38 -> x16, local copies, waits for them, and re-layouts: 5.56 us -> 3.15 us
  transfers between devices with their start and end apart: 36 -> 37, of which waited for: 22 -> 22; matrix products, arithmetic and copies ran while one was open for 1% -> 1% of each run, Pallas kernels for 19% -> 18%
where the time goes in v12:
time: 141 us; the launch traced here: 140 us
  waiting for transfers between devices  57.7 us (41%)
  starting transfers between devices  47.5 us (34%)
  Pallas kernels  30.1 us (21%)
  local copies, waits for them, and re-layouts  3.19 us (2%)
    pallas_call x24, Pallas kernels, call(): pl.pallas_call(kernel, out_shape=tuple((jax.ShapeDtypeStruct(s, d) for s,...  30.1 us
    ppermute x12, waiting for transfers between devices, to_zz(): lax.ppermute(x, 'zz', [(i, (i + k) % z.zz) for i in range(z.zz)])  27.5 us
    ppermute x12, starting transfers between devices, to_zz(): lax.ppermute(x, 'zz', [(i, (i + k) % z.zz) for i in range(z.zz)])  22.1 us
    ppermute x12, starting transfers between devices, to_grp(): lax.ppermute(x, 'grp', [(i, i ^ s) for i in range(z.grp)])  14.7 us
    ppermute x12, waiting for transfers between devices, to_grp(): lax.ppermute(x, 'grp', [(i, i ^ s) for i in range(z.grp)])  13.4 us
    ppermute x2, waiting for transfers between devices, shards(): lax.ppermute(mine, 'zz', [(i, i ^ step) for i in range(z.zz)])  10 us
    all_to_all x1, starting transfers between devices, shards(): lax.all_to_all(message, ('grp', 'zz', 'core'), split_axis=0, concat_axis=...  6.96 us
    all_to_all x1, waiting for transfers between devices, shards(): lax.all_to_all(message, ('grp', 'zz', 'core'), split_axis=0, concat_axis=...  4.43 us
  transfers between devices with their start and end apart: 37, of which 22 were waited for; matrix products, arithmetic and copies ran while one was open for 1% of the time, Pallas kernels for 18%

profile of v12, /device:TPU:0, one launch (start us, length us, event | category | flops | bytes accessed | tf_op | source)
XLA Modules:
  0.0 140.5 jit_solution(10283775478350613404)
XLA Ops:
  1.9 1.8 %index.1 = s32[32,8,128]{2,1,0:T(8,128)} custom-call(s32[3]{0:T(128)S(1)} %pad_add_fusion.refs_0_, s32[1,512]{1,0:T(1,128)S(1)} %bitcast.4), custom_call_target="tpu_custom_call" | custom-call | flops 100000000 | tf_op jit(solution)/shard_map/index/pallas_call | solution.py:52
  3.7 7.0 %all-to-all-start = ((s32[32,8,128]{2,1,0:T(8,128)}), s32[32,8,128]{2,1,0:T(8,128)S(1)}, u32[]{:S(2)}, u32[]{:S(2)}) async-start(s32[32,8,128]{2,1,0:T(8,128)} %index.1), calls=%async_computation | async-start | bytes 262144 | tf_op jit(solution)/shard_map/all_to_all | solution.py:271
  10.6 1.2 copy-done
  11.9 1.2 copy-done.3
  13.1 1.2 product.1
  14.4 4.4 %all-to-all-done.refs_1_.refs_2_ = s32[32,8,128]{2,1,0:T(8,128)S(1)} async-done(((s32[32,8,128]{2,1,0:T(8,128)}), s32[32,8,128]{2,1,0:T(8,128)S(1)}, u32[]{:S(2)}, u32[]{:S(2)}) %all-to-all-start) | async-done | bytes 131104 | tf_op jit(solution)/shard_map/all_to_all | solution.py:271
  18.8 1.2 send.1
  20.0 0.9 collective-permute-start
  21.6 2.0 %collective-permute-start.2 = (bf16[2,128,256]{2,1,0:T(8,128)(2,1)S(1)}, bf16[2,128,256]{2,1,0:T(8,128)(2,1)S(1)}, u32[]{:S(2)}, u32[]{:S(2)}) collective-permute-start(bf16[2,128,256]{2,1,0:T(8,128)(2,1)S(1)} %get-tuple-element.75), channel_id=1, source_target_pairs={{0,24},{8,16},{16,8},{24,0},{1,25},{9,17},{17,9},{25,1},{2,26},{10... | collective-permute-start | bytes 393224 | tf_op jit(solution)/shard_map/ppermute | solution.py:258
  23.6 2.8 %collective-permute-done.refs_1_ = bf16[2,128,256]{2,1,0:T(8,128)(2,1)S(1)} collective-permute-done((bf16[2,128,256]{2,1,0:T(8,128)(2,1)S(1)}, bf16[2,128,256]{2,1,0:T(8,128)(2,1)S(1)}, u32[]{:S(2)}, u32[]{:S(2)}) %collective-permute-start) | collective-permute-done | bytes 131104 | tf_op jit(solution)/shard_map/ppermute | solution.py:258
  26.4 2.3 %collective-permute-done.1.refs_2_ = bf16[2,128,256]{2,1,0:T(8,128)(2,1)S(1)} collective-permute-done((bf16[2,128,256]{2,1,0:T(8,128)(2,1)S(1)}, bf16[2,128,256]{2,1,0:T(8,128)(2,1)S(1)}, u32[]{:S(2)}, u32[]{:S(2)}) %collective-permute-start.1) | collective-permute-done | bytes 131104 | tf_op jit(solution)/shard_map/ppermute | solution.py:258
  28.8 1.5 %collective-permute-done.9.refs_3_ = bf16[512,256]{1,0:T(8,128)(2,1)S(1)} collective-permute-done((bf16[512,256]{1,0:T(8,128)(2,1)S(1)}, bf16[512,256]{1,0:T(8,128)(2,1)S(1)}, u32[]{:S(2)}, u32[]{:S(2)}) %collective-permute-start.9) | collective-permute-done | bytes 262176 | tf_op jit(solution)/shard_map/ppermute | solution.py:255
  31.8 9.5 %collective-permute-done.10.refs_3_ = bf16[512,256]{1,0:T(8,128)(2,1)S(1)} collective-permute-done((bf16[512,256]{1,0:T(8,128)(2,1)S(1)}, bf16[512,256]{1,0:T(8,128)(2,1)S(1)}, u32[]{:S(2)}, u32[]{:S(2)}) %collective-permute-start.10) | collective-permute-done | bytes 262176 | tf_op jit(solution)/shard_map/ppermute | solution.py:261
  42.5 5.9 %prepare.2 = (bf16[1024,512]{1,0:T(8,128)(2,1)S(1)}, bf16[1024,512]{1,0:T(8,128)(2,1)S(1)}, bf16[1024,512]{1,0:T(8,128)(2,1)S(1)}, bf16[1024,512]{1,0:T(8,128)(2,1)S(1)}, f32[8,128]{1,0:T(8,128)S(1)}) custom-call(s32[3]{0:T(128)S(1)} %pad_add_fusion.refs_0_, s32[4,16]{1,0:T(4,128)S(1)} %fusion.refs_1_, s32[32,8,128]{2,1,0:T(8,128)S(1)} %all-to-all-done.refs_1_.refs_2_, ...), custom_call_target="tpu_custom_call" | custom-call | flops 700000000 | tf_op jit(solution)/shard_map/prepare/pallas_call | solution.py:52
  48.5 1.7 %collective-permute-start.13 = (bf16[128,1024]{1,0:T(8,128)(2,1)S(1)}, bf16[128,1024]{1,0:T(8,128)(2,1)S(1)}, u32[]{:S(2)}, u32[]{:S(2)}) collective-permute-start(bf16[128,1024]{1,0:T(8,128)(2,1)S(1)} %get-tuple-element.101), channel_id=1, source_target_pairs={{0,8},{8,0},{16,24},{24,16},{1,9},{9,1},{17,25},{25,17},{2,10},{10... | collective-permute-start | bytes 786440 | tf_op jit(solution)/shard_map/ppermute | solution.py:258
  50.8 0.9 collective-permute-done.11.refs_3_
  51.7 1.6 %collective-permute-start.15 = (bf16[128,1024]{1,0:T(8,128)(2,1)S(1)}, bf16[128,1024]{1,0:T(8,128)(2,1)S(1)}, u32[]{:S(2)}, u32[]{:S(2)}) collective-permute-start(bf16[128,1024]{1,0:T(8,128)(2,1)S(1)} %get-tuple-element.103), channel_id=1, source_target_pairs={{0,24},{8,16},{16,8},{24,0},{1,25},{9,17},{17,9},{25,1},{2,26},{10... | collective-permute-start | bytes 786440 | tf_op jit(solution)/shard_map/ppermute | solution.py:258
  53.4 6.9 %prepare.3 = (bf16[1024,512]{1,0:T(8,128)(2,1)S(1)}, bf16[1024,512]{1,0:T(8,128)(2,1)S(1)}, bf16[1024,512]{1,0:T(8,128)(2,1)S(1)}, bf16[1024,512]{1,0:T(8,128)(2,1)S(1)}, f32[8,128]{1,0:T(8,128)S(1)}) custom-call(s32[3]{0:T(128)S(1)} %pad_add_fusion.refs_0_, s32[4,16]{1,0:T(4,128)S(1)} %collective-permute-done.4.refs_5_.refs_1_, ...), custom_call_target="tpu_custom_call" | custom-call | flops 700000000 | tf_op jit(solution)/shard_map/prepare/pallas_call | solution.py:52
  60.3 3.6 %collective-permute-start.8 = (bf16[512,256]{1,0:T(8,128)(2,1)S(1)}, bf16[512,256]{1,0:T(8,128)(2,1)S(1)}, u32[]{:S(2)}, u32[]{:S(2)}) collective-permute-start(bf16[512,256]{1,0:T(8,128)(2,1)S(1)} %collective-permute-done.7.refs_2_), channel_id=1, source_target_pairs={{0,2},{2,4},{4,6},{6,0},{1,3},{3,5},{5,7},{7,1},{8,10},{10,12},{12... | collective-permute-start | bytes 786440 | tf_op jit(solution)/shard_map/ppermute | solution.py:261
  64.4 0.8 forward.4
  65.2 0.8 forward.5
  65.9 0.8 forward.6
  66.7 3.5 %collective-permute-done.8.refs_2_ = bf16[512,256]{1,0:T(8,128)(2,1)S(1)} collective-permute-done((bf16[512,256]{1,0:T(8,128)(2,1)S(1)}, bf16[512,256]{1,0:T(8,128)(2,1)S(1)}, u32[]{:S(2)}, u32[]{:S(2)}) %collective-permute-start.8) | collective-permute-done | bytes 262176 | tf_op jit(solution)/shard_map/ppermute | solution.py:261
  70.2 1.6 %forward.7 = (bf16[512,256]{1,0:T(8,128)(2,1)S(1)}, bf16[512,256]{1,0:T(8,128)(2,1)S(1)}, bf16[512,256]{1,0:T(8,128)(2,1)S(1)}, bf16[512,256]{1,0:T(8,128)(2,1)S...) custom-call(bf16[1024,512]{1,0:T(8,128)(2,1)S(1)} %get-tuple-element.80.refs_0_.refs_8_, ...), custom_call_target="tpu_custom_call" | custom-call | flops 300000000 | tf_op jit(solution)/shard_map/forward/pallas_call | solution.py:52
  71.8 1.8 %collective-permute-start.21 = (bf16[512,256]{1,0:T(8,128)(2,1)S(1)}, bf16[512,256]{1,0:T(8,128)(2,1)S(1)}, u32[]{:S(2)}, u32[]{:S(2)}) collective-permute-start(bf16[512,256]{1,0:T(8,128)(2,1)S(1)} %get-tuple-element.121), channel_id=1, source_target_pairs={{0,6},{2,0},{4,2},{6,4},{1,7},{3,1},{5,3},{7,5},{8,14},{10,8},{12,... | collective-permute-start | bytes 786440 | tf_op jit(solution)/shard_map/ppermute | solution.py:261
  74.6 6.5 %collective-permute-done.21.refs_1_ = bf16[512,256]{1,0:T(8,128)(2,1)S(1)} collective-permute-done((bf16[512,256]{1,0:T(8,128)(2,1)S(1)}, bf16[512,256]{1,0:T(8,128)(2,1)S(1)}, u32[]{:S(2)}, u32[]{:S(2)}) %collective-permute-start.21) | collective-permute-done | bytes 262176 | tf_op jit(solution)/shard_map/ppermute | solution.py:261
  81.8 3.5 %collective-permute-start.22 = (bf16[512,256]{1,0:T(8,128)(2,1)S(1)}, bf16[512,256]{1,0:T(8,128)(2,1)S(1)}, u32[]{:S(2)}, u32[]{:S(2)}) collective-permute-start(bf16[512,256]{1,0:T(8,128)(2,1)S(1)} %get-tuple-element.122), channel_id=1, source_target_pairs={{0,6},{2,0},{4,2},{6,4},{1,7},{3,1},{5,3},{7,5},{8,14},{10,8},{12,... | collective-permute-start | bytes 786440 | tf_op jit(solution)/shard_map/ppermute | solution.py:261
  85.3 1.4 %collective-permute-done.18.refs_1_ = bf16[512,256]{1,0:T(8,128)(2,1)S(1)} collective-permute-done((bf16[512,256]{1,0:T(8,128)(2,1)S(1)}, bf16[512,256]{1,0:T(8,128)(2,1)S(1)}, u32[]{:S(2)}, u32[]{:S(2)}) %collective-permute-start.18) | collective-permute-done | bytes 262176 | tf_op jit(solution)/shard_map/ppermute | solution.py:261
  87.4 3.5 %collective-permute-start.19 = (bf16[512,256]{1,0:T(8,128)(2,1)S(1)}, bf16[512,256]{1,0:T(8,128)(2,1)S(1)}, u32[]{:S(2)}, u32[]{:S(2)}) collective-permute-start(bf16[512,256]{1,0:T(8,128)(2,1)S(1)} %get-tuple-element.117), channel_id=1, source_target_pairs={{0,6},{2,0},{4,2},{6,4},{1,7},{3,1},{5,3},{7,5},{8,14},{10,8},{12,... | collective-permute-start | bytes 786440 | tf_op jit(solution)/shard_map/ppermute | solution.py:261
  91.6 0.7 collective-permute-done.22.refs_1_
  93.0 4.0 %collective-permute-start.23 = (bf16[512,256]{1,0:T(8,128)(2,1)S(1)}, bf16[512,256]{1,0:T(8,128)(2,1)S(1)}, u32[]{:S(2)}, u32[]{:S(2)}) collective-permute-start(bf16[512,256]{1,0:T(8,128)(2,1)S(1)} %get-tuple-element.123), channel_id=1, source_target_pairs={{0,6},{2,0},{4,2},{6,4},{1,7},{3,1},{5,3},{7,5},{8,14},{10,8},{12,... | collective-permute-start | bytes 786440 | tf_op jit(solution)/shard_map/ppermute | solution.py:261
  97.0 1.0 collective-permute-done.19.refs_1_
  98.6 4.0 %collective-permute-start.20 = (bf16[512,256]{1,0:T(8,128)(2,1)S(1)}, bf16[512,256]{1,0:T(8,128)(2,1)S(1)}, u32[]{:S(2)}, u32[]{:S(2)}) collective-permute-start(bf16[512,256]{1,0:T(8,128)(2,1)S(1)} %get-tuple-element.118), channel_id=1, source_target_pairs={{0,6},{2,0},{4,2},{6,4},{1,7},{3,1},{5,3},{7,5},{8,14},{10,8},{12,... | collective-permute-start | bytes 786440 | tf_op jit(solution)/shard_map/ppermute | solution.py:261
  103.7 3.4 %collective-permute-done.20.refs_5_ = bf16[512,256]{1,0:T(8,128)(2,1)S(1)} collective-permute-done((bf16[512,256]{1,0:T(8,128)(2,1)S(1)}, bf16[512,256]{1,0:T(8,128)(2,1)S(1)}, u32[]{:S(2)}, u32[]{:S(2)}) %collective-permute-start.20) | collective-permute-done | bytes 262176 | tf_op jit(solution)/shard_map/ppermute | solution.py:261
  107.1 1.3 grad.1
  108.4 2.2 %collective-permute-start.24 = (bf16[256,256]{1,0:T(8,128)(2,1)S(1)}, bf16[256,256]{1,0:T(8,128)(2,1)S(1)}, u32[]{:S(2)}, u32[]{:S(2)}) collective-permute-start(bf16[256,256]{1,0:T(8,128)(2,1)S(1)} %get-tuple-element.125), channel_id=1, source_target_pairs={{0,8},{8,0},{16,24},{24,16},{1,9},{9,1},{17,25},{25,17},{2,10},{10... | collective-permute-start | bytes 393224 | tf_op jit(solution)/shard_map/ppermute | solution.py:258
  111.0 1.1 collective-permute-start.26
  112.1 2.5 %collective-permute-done.24.refs_1_ = bf16[256,256]{1,0:T(8,128)(2,1)S(1)} collective-permute-done((bf16[256,256]{1,0:T(8,128)(2,1)S(1)}, bf16[256,256]{1,0:T(8,128)(2,1)S(1)}, u32[]{:S(2)}, u32[]{:S(2)}) %collective-permute-start.24) | collective-permute-done | bytes 131104 | tf_op jit(solution)/shard_map/ppermute | solution.py:258
  114.6 2.6 %collective-permute-done.25.refs_2_ = bf16[256,256]{1,0:T(8,128)(2,1)S(1)} collective-permute-done((bf16[256,256]{1,0:T(8,128)(2,1)S(1)}, bf16[256,256]{1,0:T(8,128)(2,1)S(1)}, u32[]{:S(2)}, u32[]{:S(2)}) %collective-permute-start.25) | collective-permute-done | bytes 131104 | tf_op jit(solution)/shard_map/ppermute | solution.py:258
  117.4 5.3 %collective-permute-done.27.refs_1_ = bf16[256,256]{1,0:T(8,128)(2,1)S(1)} collective-permute-done((bf16[256,256]{1,0:T(8,128)(2,1)S(1)}, bf16[256,256]{1,0:T(8,128)(2,1)S(1)}, u32[]{:S(2)}, u32[]{:S(2)}) %collective-permute-start.27) | collective-permute-done | bytes 131104 | tf_op jit(solution)/shard_map/ppermute | solution.py:413
  122.7 2.6 %collective-permute-start.28 = (bf16[256,256]{1,0:T(8,128)(2,1)S(1)}, bf16[256,256]{1,0:T(8,128)(2,1)S(1)}, u32[]{:S(2)}, u32[]{:S(2)}) collective-permute-start(bf16[256,256]{1,0:T(8,128)(2,1)S(1)} %sum.4.refs_0_), channel_id=1, source_target_pairs={{0,4},{2,6},{4,0},{6,2},{1,5},{3,7},{5,1},{7,3},{8,12},{10,14},{12... | collective-permute-start | bytes 393224 | tf_op jit(solution)/shard_map/ppermute | solution.py:413
  125.2 4.8 %collective-permute-done.28.refs_1_ = bf16[256,256]{1,0:T(8,128)(2,1)S(1)} collective-permute-done((bf16[256,256]{1,0:T(8,128)(2,1)S(1)}, bf16[256,256]{1,0:T(8,128)(2,1)S(1)}, u32[]{:S(2)}, u32[]{:S(2)}) %collective-permute-start.28) | collective-permute-done | bytes 131104 | tf_op jit(solution)/shard_map/ppermute | solution.py:413
  130.3 1.0 collective-permute-start.30
  131.2 2.3 %collective-permute-start.31 = (bf16[256,256]{1,0:T(8,128)(2,1)S(1)}, bf16[256,256]{1,0:T(8,128)(2,1)S(1)}, u32[]{:S(2)}, u32[]{:S(2)}) collective-permute-start(bf16[256,256]{1,0:T(8,128)(2,1)S(1)} %sum.5.refs_1_), channel_id=1, source_target_pairs={{0,24},{8,16},{16,8},{24,0},{1,25},{9,17},{17,9},{25,1},{2,26},{10... | collective-permute-start | bytes 393224 | tf_op jit(solution)/shard_map/ppermute | solution.py:258
  133.6 1.5 %collective-permute-done.29.refs_2_ = bf16[256,256]{1,0:T(8,128)(2,1)S(1)} collective-permute-done((bf16[256,256]{1,0:T(8,128)(2,1)S(1)}, bf16[256,256]{1,0:T(8,128)(2,1)S(1)}, u32[]{:S(2)}, u32[]{:S(2)}) %collective-permute-start.29) | collective-permute-done | bytes 131104 | tf_op jit(solution)/shard_map/ppermute | solution.py:258
  135.6 1.5 %collective-permute-done.31.refs_4_ = bf16[256,256]{1,0:T(8,128)(2,1)S(1)} collective-permute-done((bf16[256,256]{1,0:T(8,128)(2,1)S(1)}, bf16[256,256]{1,0:T(8,128)(2,1)S(1)}, u32[]{:S(2)}, u32[]{:S(2)}) %collective-permute-start.31) | collective-permute-done | bytes 131104 | tf_op jit(solution)/shard_map/ppermute | solution.py:258
  137.1 0.8 pad_maximum_fusion
  138.4 2.0 %last.1 = f32[1024,512]{1,0:T(8,128)} custom-call(s32[3]{0:T(128)S(1)} %pad_add_fusion.refs_0_, bf16[256,256]{1,0:T(8,128)(2,1)S(1)} %sum.5.refs_1_, bf16[256,256]{1,0:T(8,128)(2,1)S(1)} %collective-permute-done.29.refs_2_, bf16[256,256]{1,0:T(8,128)(2,1)S(1)} %collective-permute-done.30.refs_3_, bf16[256,256]{1,0:T(8,128)(2,1)S(1)} %collective-permute-done.31.refs_4_, ...), custom_call_target="tpu_custom_call" | custom-call | flops 200000000 | tf_op jit(solution)/shard_map/last/pallas_call | solution.py:52
  (71 shorter events, 12.9 us)
Async XLA Ops:
  0.6 52.7 %collective-permute-start.5 = (bf16[4,16,128,128]{3,2,1,0:T(8,128)(2,1)}, bf16[4,16,128,128]{3,2,1,0:T(8,128)(2,1)}, u32[]{:S(2)}, u32[]{:S(2)}) collective-permute-start(bf16[4,16,128,128]{3,2,1,0:T(8,128)(2,1)} %refs_3_.1), channel_id=1, source_target_pairs={{0,1},{1,0},{2,3},{3,2},{4,5},{5,4},{6,7},{7,6},{8,9},{9,8},{10,11... | collective-permute-start | bytes 6291464 | tf_op jit(solution)/shard_map/ppermute | solution.py:255
  1.2 0.7 copy-start.4
  3.7 15.1 %all-to-all-start = ((s32[32,8,128]{2,1,0:T(8,128)}), s32[32,8,128]{2,1,0:T(8,128)S(1)}, u32[]{:S(2)}, u32[]{:S(2)}) async-start(s32[32,8,128]{2,1,0:T(8,128)} %index.1), calls=%async_computation | async-start | bytes 262144 | tf_op jit(solution)/shard_map/all_to_all | solution.py:271
  10.6 1.2 copy-start
  11.9 1.2 copy-start.3
  13.1 18.0 %copy-start.5 = (bf16[512,512]{1,0:T(8,128)(2,1)S(1)}, bf16[512,512]{1,0:T(8,128)(2,1)}, u32[]{:S(2)}) copy-start(bf16[512,512]{1,0:T(8,128)(2,1)} %param.13) | copy-start | bytes 1572868
  14.3 27.0 %copy-start.6 = (s32[4,16]{1,0:T(4,128)S(1)}, s32[4,16]{1,0:T(4,128)}, u32[]{:S(2)}) copy-start(s32[4,16]{1,0:T(4,128)} %param.9) | copy-start | bytes 772
  14.4 26.9 %copy-start.7 = (s32[4]{0:T(128)S(1)}, s32[4]{0:T(128)}, u32[]{:S(2)}) copy-start(s32[4]{0:T(128)} %param.10) | copy-start | bytes 52
  14.4 27.0 %copy-start.1 = (bf16[512,1024]{1,0:T(8,128)(2,1)S(1)}, bf16[512,1024]{1,0:T(8,128)(2,1)}, u32[]{:S(2)}) copy-start(bf16[512,1024]{1,0:T(8,128)(2,1)} %refs_1_.1) | copy-start | bytes 3145732
  20.0 6.4 %collective-permute-start = (bf16[2,128,256]{2,1,0:T(8,128)(2,1)S(1)}, bf16[2,128,256]{2,1,0:T(8,128)(2,1)S(1)}, u32[]{:S(2)}, u32[]{:S(2)}) collective-permute-start(bf16[2,128,256]{2,1,0:T(8,128)(2,1)S(1)} %get-tuple-element.73), channel_id=1, source_target_pairs={{0,8},{8,0},{16,24},{24,16},{1,9},{9,1},{17,25},{25,17},{2,10},{10... | collective-permute-start | bytes 393224 | tf_op jit(solution)/shard_map/ppermute | solution.py:258
  20.9 7.8 %collective-permute-start.1 = (bf16[2,128,256]{2,1,0:T(8,128)(2,1)S(1)}, bf16[2,128,256]{2,1,0:T(8,128)(2,1)S(1)}, u32[]{:S(2)}, u32[]{:S(2)}) collective-permute-start(bf16[2,128,256]{2,1,0:T(8,128)(2,1)S(1)} %get-tuple-element.74), channel_id=1, source_target_pairs={{0,16},{8,24},{16,0},{24,8},{1,17},{9,25},{17,1},{25,9},{2,18},{10... | collective-permute-start | bytes 393224 | tf_op jit(solution)/shard_map/ppermute | solution.py:258
  21.6 7.1 %collective-permute-start.2 = (bf16[2,128,256]{2,1,0:T(8,128)(2,1)S(1)}, bf16[2,128,256]{2,1,0:T(8,128)(2,1)S(1)}, u32[]{:S(2)}, u32[]{:S(2)}) collective-permute-start(bf16[2,128,256]{2,1,0:T(8,128)(2,1)S(1)} %get-tuple-element.75), channel_id=1, source_target_pairs={{0,24},{8,16},{16,8},{24,0},{1,25},{9,17},{17,9},{25,1},{2,26},{10... | collective-permute-start | bytes 393224 | tf_op jit(solution)/shard_map/ppermute | solution.py:258
  28.7 1.6 %collective-permute-start.9 = (bf16[512,256]{1,0:T(8,128)(2,1)S(1)}, bf16[512,256]{1,0:T(8,128)(2,1)S(1)}, u32[]{:S(2)}, u32[]{:S(2)}) collective-permute-start(bf16[512,256]{1,0:T(8,128)(2,1)S(1)} %get-tuple-element.88), channel_id=1, source_target_pairs={{0,1},{1,0},{2,3},{3,2},{4,5},{5,4},{6,7},{7,6},{8,9},{9,8},{10,11... | collective-permute-start | bytes 786440 | tf_op jit(solution)/shard_map/ppermute | solution.py:255
  30.3 10.9 %collective-permute-start.10 = (bf16[512,256]{1,0:T(8,128)(2,1)S(1)}, bf16[512,256]{1,0:T(8,128)(2,1)S(1)}, u32[]{:S(2)}, u32[]{:S(2)}) collective-permute-start(bf16[512,256]{1,0:T(8,128)(2,1)S(1)} %collective-permute-done.9.refs_3_), channel_id=1, source_target_pairs={{0,2},{2,4},{4,6},{6,0},{1,3},{3,5},{5,7},{7,1},{8,10},{10,12},{12... | collective-permute-start | bytes 786440 | tf_op jit(solution)/shard_map/ppermute | solution.py:261
  31.0 11.5 %copy-start.2 = (bf16[4,16,128,128]{3,2,1,0:T(8,128)(2,1)S(1)}, bf16[4,16,128,128]{3,2,1,0:T(8,128)(2,1)}, u32[]{:S(2)}) copy-start(bf16[4,16,128,128]{3,2,1,0:T(8,128)(2,1)} %refs_3_.1) | copy-start | bytes 6291460
  31.1 10.3 %collective-permute-start.3 = (bf16[512,256]{1,0:T(8,128)(2,1)S(1)}, bf16[512,256]{1,0:T(8,128)(2,1)S(1)}, u32[]{:S(2)}, u32[]{:S(2)}) collective-permute-start(bf16[512,256]{1,0:T(8,128)(2,1)S(1)} %get-tuple-element.130), channel_id=1, source_target_pairs={{0,1},{1,0},{2,3},{3,2},{4,5},{5,4},{6,7},{7,6},{8,9},{9,8},{10,11... | collective-permute-start | bytes 786440 | tf_op jit(solution)/shard_map/ppermute | solution.py:255
  31.2 17.3 %collective-permute-start.6 = (bf16[512,256]{1,0:T(8,128)(2,1)S(1)}, bf16[512,256]{1,0:T(8,128)(2,1)S(1)}, u32[]{:S(2)}, u32[]{:S(2)}) collective-permute-start(bf16[512,256]{1,0:T(8,128)(2,1)S(1)} %get-tuple-element.81.refs_2_), channel_id=1, source_target_pairs={{0,2},{2,4},{4,6},{6,0},{1,3},{3,5},{5,7},{7,1},{8,10},{10,12},{12... | collective-permute-start | bytes 786440 | tf_op jit(solution)/shard_map/ppermute | solution.py:261
  41.3 10.4 %collective-permute-start.11 = (bf16[512,256]{1,0:T(8,128)(2,1)S(1)}, bf16[512,256]{1,0:T(8,128)(2,1)S(1)}, u32[]{:S(2)}, u32[]{:S(2)}) collective-permute-start(bf16[512,256]{1,0:T(8,128)(2,1)S(1)} %collective-permute-done.10.refs_3_), channel_id=1, source_target_pairs={{0,2},{2,4},{4,6},{6,0},{1,3},{3,5},{5,7},{7,1},{8,10},{10,12},{12... | collective-permute-start | bytes 786440 | tf_op jit(solution)/shard_map/ppermute | solution.py:261
  41.4 1.2 collective-permute-start.4
  48.5 11.8 %collective-permute-start.7 = (bf16[512,256]{1,0:T(8,128)(2,1)S(1)}, bf16[512,256]{1,0:T(8,128)(2,1)S(1)}, u32[]{:S(2)}, u32[]{:S(2)}) collective-permute-start(bf16[512,256]{1,0:T(8,128)(2,1)S(1)} %collective-permute-done.6.refs_2_), channel_id=1, source_target_pairs={{0,2},{2,4},{4,6},{6,0},{1,3},{3,5},{5,7},{7,1},{8,10},{10,12},{12... | collective-permute-start | bytes 786440 | tf_op jit(solution)/shard_map/ppermute | solution.py:261
  48.5 15.4 %collective-permute-start.13 = (bf16[128,1024]{1,0:T(8,128)(2,1)S(1)}, bf16[128,1024]{1,0:T(8,128)(2,1)S(1)}, u32[]{:S(2)}, u32[]{:S(2)}) collective-permute-start(bf16[128,1024]{1,0:T(8,128)(2,1)S(1)} %get-tuple-element.101), channel_id=1, source_target_pairs={{0,8},{8,0},{16,24},{24,16},{1,9},{9,1},{17,25},{25,17},{2,10},{10... | collective-permute-start | bytes 786440 | tf_op jit(solution)/shard_map/ppermute | solution.py:258
  50.3 13.7 %collective-permute-start.14 = (bf16[128,1024]{1,0:T(8,128)(2,1)S(1)}, bf16[128,1024]{1,0:T(8,128)(2,1)S(1)}, u32[]{:S(2)}, u32[]{:S(2)}) collective-permute-start(bf16[128,1024]{1,0:T(8,128)(2,1)S(1)} %get-tuple-element.102), channel_id=1, source_target_pairs={{0,16},{8,24},{16,0},{24,8},{1,17},{9,25},{17,1},{25,9},{2,18},{10... | collective-permute-start | bytes 786440 | tf_op jit(solution)/shard_map/ppermute | solution.py:258
  51.7 12.3 %collective-permute-start.15 = (bf16[128,1024]{1,0:T(8,128)(2,1)S(1)}, bf16[128,1024]{1,0:T(8,128)(2,1)S(1)}, u32[]{:S(2)}, u32[]{:S(2)}) collective-permute-start(bf16[128,1024]{1,0:T(8,128)(2,1)S(1)} %get-tuple-element.103), channel_id=1, source_target_pairs={{0,24},{8,16},{16,8},{24,0},{1,25},{9,17},{17,9},{25,1},{2,26},{10... | collective-permute-start | bytes 786440 | tf_op jit(solution)/shard_map/ppermute | solution.py:258
  53.4 13.3 %collective-permute-start.12 = (bf16[512,256]{1,0:T(8,128)(2,1)S(1)}, bf16[512,256]{1,0:T(8,128)(2,1)S(1)}, u32[]{:S(2)}, u32[]{:S(2)}) collective-permute-start(bf16[512,256]{1,0:T(8,128)(2,1)S(1)} %collective-permute-done.11.refs_3_), channel_id=1, source_target_pairs={{0,2},{2,4},{4,6},{6,0},{1,3},{3,5},{5,7},{7,1},{8,10},{10,12},{12... | collective-permute-start | bytes 786440 | tf_op jit(solution)/shard_map/ppermute | solution.py:261
  60.3 9.9 %collective-permute-start.8 = (bf16[512,256]{1,0:T(8,128)(2,1)S(1)}, bf16[512,256]{1,0:T(8,128)(2,1)S(1)}, u32[]{:S(2)}, u32[]{:S(2)}) collective-permute-start(bf16[512,256]{1,0:T(8,128)(2,1)S(1)} %collective-permute-done.7.refs_2_), channel_id=1, source_target_pairs={{0,2},{2,4},{4,6},{6,0},{1,3},{3,5},{5,7},{7,1},{8,10},{10,12},{12... | collective-permute-start | bytes 786440 | tf_op jit(solution)/shard_map/ppermute | solution.py:261
  64.3 39.0 %collective-permute-start.17 = (bf16[1024,512]{1,0:T(8,128)(2,1)S(1)}, bf16[1024,512]{1,0:T(8,128)(2,1)S(1)}, u32[]{:S(2)}, u32[]{:S(2)}) collective-permute-start(bf16[1024,512]{1,0:T(8,128)(2,1)S(1)} %get-tuple-element.109.refs_1_), channel_id=1, source_target_pairs={{0,1},{1,0},{2,3},{3,2},{4,5},{5,4},{6,7},{7,6},{8,9},{9,8},{10,11... | collective-permute-start | bytes 3145736 | tf_op jit(solution)/shard_map/ppermute | solution.py:255
  71.8 9.3 %collective-permute-start.21 = (bf16[512,256]{1,0:T(8,128)(2,1)S(1)}, bf16[512,256]{1,0:T(8,128)(2,1)S(1)}, u32[]{:S(2)}, u32[]{:S(2)}) collective-permute-start(bf16[512,256]{1,0:T(8,128)(2,1)S(1)} %get-tuple-element.121), channel_id=1, source_target_pairs={{0,6},{2,0},{4,2},{6,4},{1,7},{3,1},{5,3},{7,5},{8,14},{10,8},{12,... | collective-permute-start | bytes 786440 | tf_op jit(solution)/shard_map/ppermute | solution.py:261
  73.6 13.1 %collective-permute-start.18 = (bf16[512,256]{1,0:T(8,128)(2,1)S(1)}, bf16[512,256]{1,0:T(8,128)(2,1)S(1)}, u32[]{:S(2)}, u32[]{:S(2)}) collective-permute-start(bf16[512,256]{1,0:T(8,128)(2,1)S(1)} %get-tuple-element.116), channel_id=1, source_target_pairs={{0,6},{2,0},{4,2},{6,4},{1,7},{3,1},{5,3},{7,5},{8,14},{10,8},{12,... | collective-permute-start | bytes 786440 | tf_op jit(solution)/shard_map/ppermute | solution.py:261
  73.9 17.7 %collective-permute-start.16 = (bf16[512,256]{1,0:T(8,128)(2,1)S(1)}, bf16[512,256]{1,0:T(8,128)(2,1)S(1)}, u32[]{:S(2)}, u32[]{:S(2)}) collective-permute-start(bf16[512,256]{1,0:T(8,128)(2,1)S(1)} %get-tuple-element.108), channel_id=1, source_target_pairs={{0,1},{1,0},{2,3},{3,2},{4,5},{5,4},{6,7},{7,6},{8,9},{9,8},{10,11... | collective-permute-start | bytes 786440 | tf_op jit(solution)/shard_map/ppermute | solution.py:255
  81.8 10.6 %collective-permute-start.22 = (bf16[512,256]{1,0:T(8,128)(2,1)S(1)}, bf16[512,256]{1,0:T(8,128)(2,1)S(1)}, u32[]{:S(2)}, u32[]{:S(2)}) collective-permute-start(bf16[512,256]{1,0:T(8,128)(2,1)S(1)} %get-tuple-element.122), channel_id=1, source_target_pairs={{0,6},{2,0},{4,2},{6,4},{1,7},{3,1},{5,3},{7,5},{8,14},{10,8},{12,... | collective-permute-start | bytes 786440 | tf_op jit(solution)/shard_map/ppermute | solution.py:261
  87.4 10.6 %collective-permute-start.19 = (bf16[512,256]{1,0:T(8,128)(2,1)S(1)}, bf16[512,256]{1,0:T(8,128)(2,1)S(1)}, u32[]{:S(2)}, u32[]{:S(2)}) collective-permute-start(bf16[512,256]{1,0:T(8,128)(2,1)S(1)} %get-tuple-element.117), channel_id=1, source_target_pairs={{0,6},{2,0},{4,2},{6,4},{1,7},{3,1},{5,3},{7,5},{8,14},{10,8},{12,... | collective-permute-start | bytes 786440 | tf_op jit(solution)/shard_map/ppermute | solution.py:261
  93.0 10.7 %collective-permute-start.23 = (bf16[512,256]{1,0:T(8,128)(2,1)S(1)}, bf16[512,256]{1,0:T(8,128)(2,1)S(1)}, u32[]{:S(2)}, u32[]{:S(2)}) collective-permute-start(bf16[512,256]{1,0:T(8,128)(2,1)S(1)} %get-tuple-element.123), channel_id=1, source_target_pairs={{0,6},{2,0},{4,2},{6,4},{1,7},{3,1},{5,3},{7,5},{8,14},{10,8},{12,... | collective-permute-start | bytes 786440 | tf_op jit(solution)/shard_map/ppermute | solution.py:261
  98.6 8.5 %collective-permute-start.20 = (bf16[512,256]{1,0:T(8,128)(2,1)S(1)}, bf16[512,256]{1,0:T(8,128)(2,1)S(1)}, u32[]{:S(2)}, u32[]{:S(2)}) collective-permute-start(bf16[512,256]{1,0:T(8,128)(2,1)S(1)} %get-tuple-element.118), channel_id=1, source_target_pairs={{0,6},{2,0},{4,2},{6,4},{1,7},{3,1},{5,3},{7,5},{8,14},{10,8},{12,... | collective-permute-start | bytes 786440 | tf_op jit(solution)/shard_map/ppermute | solution.py:261
  108.4 6.2 %collective-permute-start.24 = (bf16[256,256]{1,0:T(8,128)(2,1)S(1)}, bf16[256,256]{1,0:T(8,128)(2,1)S(1)}, u32[]{:S(2)}, u32[]{:S(2)}) collective-permute-start(bf16[256,256]{1,0:T(8,128)(2,1)S(1)} %get-tuple-element.125), channel_id=1, source_target_pairs={{0,8},{8,0},{16,24},{24,16},{1,9},{9,1},{17,25},{25,17},{2,10},{10... | collective-permute-start | bytes 393224 | tf_op jit(solution)/shard_map/ppermute | solution.py:258
  110.6 6.6 %collective-permute-start.25 = (bf16[256,256]{1,0:T(8,128)(2,1)S(1)}, bf16[256,256]{1,0:T(8,128)(2,1)S(1)}, u32[]{:S(2)}, u32[]{:S(2)}) collective-permute-start(bf16[256,256]{1,0:T(8,128)(2,1)S(1)} %get-tuple-element.126), channel_id=1, source_target_pairs={{0,16},{8,24},{16,0},{24,8},{1,17},{9,25},{17,1},{25,9},{2,18},{10... | collective-permute-start | bytes 393224 | tf_op jit(solution)/shard_map/ppermute | solution.py:258
  111.0 6.2 %collective-permute-start.26 = (bf16[256,256]{1,0:T(8,128)(2,1)S(1)}, bf16[256,256]{1,0:T(8,128)(2,1)S(1)}, u32[]{:S(2)}, u32[]{:S(2)}) collective-permute-start(bf16[256,256]{1,0:T(8,128)(2,1)S(1)} %get-tuple-element.127), channel_id=1, source_target_pairs={{0,24},{8,16},{16,8},{24,0},{1,25},{9,17},{17,9},{25,1},{2,26},{10... | collective-permute-start | bytes 393224 | tf_op jit(solution)/shard_map/ppermute | solution.py:258
  117.3 5.3 %collective-permute-start.27 = (bf16[256,256]{1,0:T(8,128)(2,1)S(1)}, bf16[256,256]{1,0:T(8,128)(2,1)S(1)}, u32[]{:S(2)}, u32[]{:S(2)}) collective-permute-start(bf16[256,256]{1,0:T(8,128)(2,1)S(1)} %sum.3.refs_0_), channel_id=1, source_target_pairs={{0,2},{2,0},{4,6},{6,4},{1,3},{3,1},{5,7},{7,5},{8,10},{10,8},{12,... | collective-permute-start | bytes 393224 | tf_op jit(solution)/shard_map/ppermute | solution.py:413
  122.7 7.3 %collective-permute-start.28 = (bf16[256,256]{1,0:T(8,128)(2,1)S(1)}, bf16[256,256]{1,0:T(8,128)(2,1)S(1)}, u32[]{:S(2)}, u32[]{:S(2)}) collective-permute-start(bf16[256,256]{1,0:T(8,128)(2,1)S(1)} %sum.4.refs_0_), channel_id=1, source_target_pairs={{0,4},{2,6},{4,0},{6,2},{1,5},{3,7},{5,1},{7,3},{8,12},{10,14},{12... | collective-permute-start | bytes 393224 | tf_op jit(solution)/shard_map/ppermute | solution.py:413
  130.0 5.0 %collective-permute-start.29 = (bf16[256,256]{1,0:T(8,128)(2,1)S(1)}, bf16[256,256]{1,0:T(8,128)(2,1)S(1)}, u32[]{:S(2)}, u32[]{:S(2)}) collective-permute-start(bf16[256,256]{1,0:T(8,128)(2,1)S(1)} %sum.5.refs_1_), channel_id=1, source_target_pairs={{0,8},{8,0},{16,24},{24,16},{1,9},{9,1},{17,25},{25,17},{2,10},{10... | collective-permute-start | bytes 393224 | tf_op jit(solution)/shard_map/ppermute | solution.py:258
  130.3 5.0 %collective-permute-start.30 = (bf16[256,256]{1,0:T(8,128)(2,1)S(1)}, bf16[256,256]{1,0:T(8,128)(2,1)S(1)}, u32[]{:S(2)}, u32[]{:S(2)}) collective-permute-start(bf16[256,256]{1,0:T(8,128)(2,1)S(1)} %sum.5.refs_1_), channel_id=1, source_target_pairs={{0,16},{8,24},{16,0},{24,8},{1,17},{9,25},{17,1},{25,9},{2,18},{10... | collective-permute-start | bytes 393224 | tf_op jit(solution)/shard_map/ppermute | solution.py:258
  131.2 5.9 %collective-permute-start.31 = (bf16[256,256]{1,0:T(8,128)(2,1)S(1)}, bf16[256,256]{1,0:T(8,128)(2,1)S(1)}, u32[]{:S(2)}, u32[]{:S(2)}) collective-permute-start(bf16[256,256]{1,0:T(8,128)(2,1)S(1)} %sum.5.refs_1_), channel_id=1, source_target_pairs={{0,24},{8,16},{16,8},{24,0},{1,25},{9,17},{17,9},{25,1},{2,26},{10... | collective-permute-start | bytes 393224 | tf_op jit(solution)/shard_map/ppermute | solution.py:258
  133.6 4.4 %collective-permute-start.32 = (bf16[256,256]{1,0:T(8,128)(2,1)S(1)}, bf16[256,256]{1,0:T(8,128)(2,1)S(1)}, u32[]{:S(2)}, u32[]{:S(2)}) collective-permute-start(bf16[256,256]{1,0:T(8,128)(2,1)S(1)} %sum.5.refs_1_), channel_id=1, source_target_pairs={{0,1},{1,0},{2,3},{3,2},{4,5},{5,4},{6,7},{7,6},{8,9},{9,8},{10,11... | collective-permute-start | bytes 393224 | tf_op jit(solution)/shard_map/ppermute | solution.py:255
  135.1 2.9 %collective-permute-start.33 = (bf16[256,256]{1,0:T(8,128)(2,1)S(1)}, bf16[256,256]{1,0:T(8,128)(2,1)S(1)}, u32[]{:S(2)}, u32[]{:S(2)}) collective-permute-start(bf16[256,256]{1,0:T(8,128)(2,1)S(1)} %collective-permute-done.29.refs_2_), channel_id=1, source_target_pairs={{0,1},{1,0},{2,3},{3,2},{4,5},{5,4},{6,7},{7,6},{8,9},{9,8},{10,11... | collective-permute-start | bytes 393224 | tf_op jit(solution)/shard_map/ppermute | solution.py:255
  135.2 2.8 %collective-permute-start.34 = (bf16[256,256]{1,0:T(8,128)(2,1)S(1)}, bf16[256,256]{1,0:T(8,128)(2,1)S(1)}, u32[]{:S(2)}, u32[]{:S(2)}) collective-permute-start(bf16[256,256]{1,0:T(8,128)(2,1)S(1)} %collective-permute-done.30.refs_3_), channel_id=1, source_target_pairs={{0,1},{1,0},{2,3},{3,2},{4,5},{5,4},{6,7},{7,6},{8,9},{9,8},{10,11... | collective-permute-start | bytes 393224 | tf_op jit(solution)/shard_map/ppermute | solution.py:255
  137.1 1.3 collective-permute-start.35

commit v13 on v12

--- a/solution.py
+++ b/solution.py
@@ -344,10 +344,11 @@
             *picked, token = rows_of(pick, features, [token, cot_a, cot_b])
             lefts, token_l = turned_of(across(picked))
             turned_a, token = prepared(cols_a, block_vals, token)
-            ring[1][0], token = lax.optimization_barrier((ring[1][0], token))
+            for part in range(2):
+                ring[1][part], token = lax.optimization_barrier((ring[1][part], token))
         if k == 2:
             turned_b, token = prepared(cols_b, vals_b, token)
-            ring[2][0], token = lax.optimization_barrier((ring[2][0], token))
+            ring[2][1], token = lax.optimization_barrier((ring[2][1], token))
     turned = (turned_a, turned_b)
 
     agg = []

time: 141 us -> 140 us (level)
  starting transfers between devices: 47.5 us -> 42.3 us
  waiting for transfers between devices: 57.7 us -> 61.8 us
    ppermute x12, starting transfers between devices: 22.1 us -> 18.3 us  [to_zz(): lax.ppermute(x, 'zz', [(i, (i + k) % z.zz) for i in range(z.zz)])]
    ppermute x12, waiting for transfers between devices: 27.5 us -> 30.9 us  [to_zz(): lax.ppermute(x, 'zz', [(i, (i + k) % z.zz) for i in range(z.zz)])]
    ppermute x2, waiting for transfers between devices: 10 us -> 12.1 us  [shards(): lax.ppermute(mine, 'zz', [(i, i ^ step) for i in range(z.zz)])]
    ppermute x10, waiting for transfers between devices: 2.4 us -> 0.48 us  [to_core(): return lax.ppermute(x, 'core', [(0, 1), (1, 0)])]
  transfers between devices with their start and end apart: 37 -> 37, of which waited for: 22 -> 23; matrix products, arithmetic and copies ran while one was open for 1% -> 1% of each run, Pallas kernels for 18% -> 18%
where the time goes in v13:
time: 140 us; the launch traced here: 139 us
  waiting for transfers between devices  61.8 us (44%)
  starting transfers between devices  42.3 us (30%)
  Pallas kernels  30.1 us (22%)
  local copies, waits for them, and re-layouts  3.19 us (2%)
    ppermute x12, waiting for transfers between devices, to_zz(): lax.ppermute(x, 'zz', [(i, (i + k) % z.zz) for i in range(z.zz)])  30.9 us
    pallas_call x24, Pallas kernels, call(): pl.pallas_call(kernel, out_shape=tuple((jax.ShapeDtypeStruct(s, d) for s,...  30.1 us
    ppermute x12, starting transfers between devices, to_zz(): lax.ppermute(x, 'zz', [(i, (i + k) % z.zz) for i in range(z.zz)])  18.3 us
    ppermute x12, starting transfers between devices, to_grp(): lax.ppermute(x, 'grp', [(i, i ^ s) for i in range(z.grp)])  14.5 us
    ppermute x12, waiting for transfers between devices, to_grp(): lax.ppermute(x, 'grp', [(i, i ^ s) for i in range(z.grp)])  14 us
    ppermute x2, waiting for transfers between devices, shards(): lax.ppermute(mine, 'zz', [(i, i ^ step) for i in range(z.zz)])  12.1 us
    all_to_all x1, starting transfers between devices, shards(): lax.all_to_all(message, ('grp', 'zz', 'core'), split_axis=0, concat_axis=...  6.96 us
    all_to_all x1, waiting for transfers between devices, shards(): lax.all_to_all(message, ('grp', 'zz', 'core'), split_axis=0, concat_axis=...  4.43 us
  transfers between devices with their start and end apart: 37, of which 23 were waited for; matrix products, arithmetic and copies ran while one was open for 1% of the time, Pallas kernels for 18%

profile of v13, /device:TPU:0, one launch (start us, length us, event | category | flops | bytes accessed | tf_op | source)
XLA Modules:
  0.0 139.3 jit_solution(11825534148578694021)
XLA Ops:
  1.9 1.8 %index.1 = s32[32,8,128]{2,1,0:T(8,128)} custom-call(s32[3]{0:T(128)S(1)} %pad_add_fusion.refs_0_, s32[1,512]{1,0:T(1,128)S(1)} %bitcast.4), custom_call_target="tpu_custom_call" | custom-call | flops 100000000 | tf_op jit(solution)/shard_map/index/pallas_call | solution.py:52
  3.7 7.0 %all-to-all-start = ((s32[32,8,128]{2,1,0:T(8,128)}), s32[32,8,128]{2,1,0:T(8,128)S(1)}, u32[]{:S(2)}, u32[]{:S(2)}) async-start(s32[32,8,128]{2,1,0:T(8,128)} %index.1), calls=%async_computation | async-start | bytes 262144 | tf_op jit(solution)/shard_map/all_to_all | solution.py:271
  10.6 1.2 copy-done
  11.9 1.2 copy-done.3
  13.1 1.2 product.1
  14.4 4.4 %all-to-all-done.refs_1_.refs_2_ = s32[32,8,128]{2,1,0:T(8,128)S(1)} async-done(((s32[32,8,128]{2,1,0:T(8,128)}), s32[32,8,128]{2,1,0:T(8,128)S(1)}, u32[]{:S(2)}, u32[]{:S(2)}) %all-to-all-start) | async-done | bytes 131104 | tf_op jit(solution)/shard_map/all_to_all | solution.py:271
  18.8 1.2 send.1
  20.0 0.9 collective-permute-start
  21.6 2.0 %collective-permute-start.2 = (bf16[2,128,256]{2,1,0:T(8,128)(2,1)S(1)}, bf16[2,128,256]{2,1,0:T(8,128)(2,1)S(1)}, u32[]{:S(2)}, u32[]{:S(2)}) collective-permute-start(bf16[2,128,256]{2,1,0:T(8,128)(2,1)S(1)} %get-tuple-element.77), channel_id=1, source_target_pairs={{0,24},{8,16},{16,8},{24,0},{1,25},{9,17},{17,9},{25,1},{2,26},{10... | collective-permute-start | bytes 393224 | tf_op jit(solution)/shard_map/ppermute | solution.py:258
  23.7 2.7 %collective-permute-done.refs_1_ = bf16[2,128,256]{2,1,0:T(8,128)(2,1)S(1)} collective-permute-done((bf16[2,128,256]{2,1,0:T(8,128)(2,1)S(1)}, bf16[2,128,256]{2,1,0:T(8,128)(2,1)S(1)}, u32[]{:S(2)}, u32[]{:S(2)}) %collective-permute-start) | collective-permute-done | bytes 131104 | tf_op jit(solution)/shard_map/ppermute | solution.py:258
  26.4 2.3 %collective-permute-done.1.refs_2_ = bf16[2,128,256]{2,1,0:T(8,128)(2,1)S(1)} collective-permute-done((bf16[2,128,256]{2,1,0:T(8,128)(2,1)S(1)}, bf16[2,128,256]{2,1,0:T(8,128)(2,1)S(1)}, u32[]{:S(2)}, u32[]{:S(2)}) %collective-permute-start.1) | collective-permute-done | bytes 131104 | tf_op jit(solution)/shard_map/ppermute | solution.py:258
  31.2 5.9 %prepare.2 = (bf16[1024,512]{1,0:T(8,128)(2,1)S(1)}, bf16[1024,512]{1,0:T(8,128)(2,1)S(1)}, bf16[1024,512]{1,0:T(8,128)(2,1)S(1)}, bf16[1024,512]{1,0:T(8,128)(2,1)S(1)}, f32[8,128]{1,0:T(8,128)S(1)}) custom-call(s32[3]{0:T(128)S(1)} %pad_add_fusion.refs_0_, s32[4,16]{1,0:T(4,128)S(1)} %fusion.refs_1_, s32[32,8,128]{2,1,0:T(8,128)S(1)} %all-to-all-done.refs_1_.refs_2_, ...), custom_call_target="tpu_custom_call" | custom-call | flops 700000000 | tf_op jit(solution)/shard_map/prepare/pallas_call | solution.py:52
  37.1 2.7 %collective-permute-done.8.refs_2_ = bf16[512,256]{1,0:T(8,128)(2,1)S(1)} collective-permute-done((bf16[512,256]{1,0:T(8,128)(2,1)S(1)}, bf16[512,256]{1,0:T(8,128)(2,1)S(1)}, u32[]{:S(2)}, u32[]{:S(2)}) %collective-permute-start.8) | collective-permute-done | bytes 262176 | tf_op jit(solution)/shard_map/ppermute | solution.py:261
  39.8 5.6 %collective-permute-done.7.refs_3_ = bf16[512,256]{1,0:T(8,128)(2,1)S(1)} collective-permute-done((bf16[512,256]{1,0:T(8,128)(2,1)S(1)}, bf16[512,256]{1,0:T(8,128)(2,1)S(1)}, u32[]{:S(2)}, u32[]{:S(2)}) %collective-permute-start.7) | collective-permute-done | bytes 262176 | tf_op jit(solution)/shard_map/ppermute | solution.py:261
  45.4 1.7 %collective-permute-start.13 = (bf16[128,1024]{1,0:T(8,128)(2,1)S(1)}, bf16[128,1024]{1,0:T(8,128)(2,1)S(1)}, u32[]{:S(2)}, u32[]{:S(2)}) collective-permute-start(bf16[128,1024]{1,0:T(8,128)(2,1)S(1)} %get-tuple-element.105), channel_id=1, source_target_pairs={{0,8},{8,0},{16,24},{24,16},{1,9},{9,1},{17,25},{25,17},{2,10},{10... | collective-permute-start | bytes 786440 | tf_op jit(solution)/shard_map/ppermute | solution.py:258
  47.6 3.4 %collective-permute-done.9.refs_2_ = bf16[512,256]{1,0:T(8,128)(2,1)S(1)} collective-permute-done((bf16[512,256]{1,0:T(8,128)(2,1)S(1)}, bf16[512,256]{1,0:T(8,128)(2,1)S(1)}, u32[]{:S(2)}, u32[]{:S(2)}) %collective-permute-start.9) | collective-permute-done | bytes 262176 | tf_op jit(solution)/shard_map/ppermute | solution.py:261
  51.0 1.6 %collective-permute-start.15 = (bf16[128,1024]{1,0:T(8,128)(2,1)S(1)}, bf16[128,1024]{1,0:T(8,128)(2,1)S(1)}, u32[]{:S(2)}, u32[]{:S(2)}) collective-permute-start(bf16[128,1024]{1,0:T(8,128)(2,1)S(1)} %get-tuple-element.107), channel_id=1, source_target_pairs={{0,24},{8,16},{16,8},{24,0},{1,25},{9,17},{17,9},{25,1},{2,26},{10... | collective-permute-start | bytes 786440 | tf_op jit(solution)/shard_map/ppermute | solution.py:258
  52.7 6.9 %prepare.3 = (bf16[1024,512]{1,0:T(8,128)(2,1)S(1)}, bf16[1024,512]{1,0:T(8,128)(2,1)S(1)}, bf16[1024,512]{1,0:T(8,128)(2,1)S(1)}, bf16[1024,512]{1,0:T(8,128)(2,1)S(1)}, f32[8,128]{1,0:T(8,128)S(1)}) custom-call(s32[3]{0:T(128)S(1)} %pad_add_fusion.refs_0_, s32[4,16]{1,0:T(4,128)S(1)} %collective-permute-done.4.refs_5_.refs_1_, ...), custom_call_target="tpu_custom_call" | custom-call | flops 700000000 | tf_op jit(solution)/shard_map/prepare/pallas_call | solution.py:52
  60.2 0.8 forward.4
  61.0 0.8 forward.5
  61.8 0.8 forward.6
  62.5 6.1 %collective-permute-done.12.refs_3_ = bf16[512,256]{1,0:T(8,128)(2,1)S(1)} collective-permute-done((bf16[512,256]{1,0:T(8,128)(2,1)S(1)}, bf16[512,256]{1,0:T(8,128)(2,1)S(1)}, u32[]{:S(2)}, u32[]{:S(2)}) %collective-permute-start.12) | collective-permute-done | bytes 262176 | tf_op jit(solution)/shard_map/ppermute | solution.py:261
  68.6 1.6 %forward.7 = (bf16[512,256]{1,0:T(8,128)(2,1)S(1)}, bf16[512,256]{1,0:T(8,128)(2,1)S(1)}, bf16[512,256]{1,0:T(8,128)(2,1)S(1)}, bf16[512,256]{1,0:T(8,128)(2,1)S...) custom-call(bf16[1024,512]{1,0:T(8,128)(2,1)S(1)} %get-tuple-element.82.refs_0_.refs_8_, ...), custom_call_target="tpu_custom_call" | custom-call | flops 300000000 | tf_op jit(solution)/shard_map/forward/pallas_call | solution.py:52
  70.2 1.8 %collective-permute-start.21 = (bf16[512,256]{1,0:T(8,128)(2,1)S(1)}, bf16[512,256]{1,0:T(8,128)(2,1)S(1)}, u32[]{:S(2)}, u32[]{:S(2)}) collective-permute-start(bf16[512,256]{1,0:T(8,128)(2,1)S(1)} %get-tuple-element.125), channel_id=1, source_target_pairs={{0,6},{2,0},{4,2},{6,4},{1,7},{3,1},{5,3},{7,5},{8,14},{10,8},{12,... | collective-permute-start | bytes 786440 | tf_op jit(solution)/shard_map/ppermute | solution.py:261
  72.8 6.7 %collective-permute-done.21.refs_1_ = bf16[512,256]{1,0:T(8,128)(2,1)S(1)} collective-permute-done((bf16[512,256]{1,0:T(8,128)(2,1)S(1)}, bf16[512,256]{1,0:T(8,128)(2,1)S(1)}, u32[]{:S(2)}, u32[]{:S(2)}) %collective-permute-start.21) | collective-permute-done | bytes 262176 | tf_op jit(solution)/shard_map/ppermute | solution.py:261
  80.1 3.5 %collective-permute-start.22 = (bf16[512,256]{1,0:T(8,128)(2,1)S(1)}, bf16[512,256]{1,0:T(8,128)(2,1)S(1)}, u32[]{:S(2)}, u32[]{:S(2)}) collective-permute-start(bf16[512,256]{1,0:T(8,128)(2,1)S(1)} %get-tuple-element.126), channel_id=1, source_target_pairs={{0,6},{2,0},{4,2},{6,4},{1,7},{3,1},{5,3},{7,5},{8,14},{10,8},{12,... | collective-permute-start | bytes 786440 | tf_op jit(solution)/shard_map/ppermute | solution.py:261
  83.7 1.4 %collective-permute-done.18.refs_1_ = bf16[512,256]{1,0:T(8,128)(2,1)S(1)} collective-permute-done((bf16[512,256]{1,0:T(8,128)(2,1)S(1)}, bf16[512,256]{1,0:T(8,128)(2,1)S(1)}, u32[]{:S(2)}, u32[]{:S(2)}) %collective-permute-start.18) | collective-permute-done | bytes 262176 | tf_op jit(solution)/shard_map/ppermute | solution.py:261
  85.8 3.5 %collective-permute-start.19 = (bf16[512,256]{1,0:T(8,128)(2,1)S(1)}, bf16[512,256]{1,0:T(8,128)(2,1)S(1)}, u32[]{:S(2)}, u32[]{:S(2)}) collective-permute-start(bf16[512,256]{1,0:T(8,128)(2,1)S(1)} %get-tuple-element.121), channel_id=1, source_target_pairs={{0,6},{2,0},{4,2},{6,4},{1,7},{3,1},{5,3},{7,5},{8,14},{10,8},{12,... | collective-permute-start | bytes 786440 | tf_op jit(solution)/shard_map/ppermute | solution.py:261
  91.4 4.0 %collective-permute-start.23 = (bf16[512,256]{1,0:T(8,128)(2,1)S(1)}, bf16[512,256]{1,0:T(8,128)(2,1)S(1)}, u32[]{:S(2)}, u32[]{:S(2)}) collective-permute-start(bf16[512,256]{1,0:T(8,128)(2,1)S(1)} %get-tuple-element.127), channel_id=1, source_target_pairs={{0,6},{2,0},{4,2},{6,4},{1,7},{3,1},{5,3},{7,5},{8,14},{10,8},{12,... | collective-permute-start | bytes 786440 | tf_op jit(solution)/shard_map/ppermute | solution.py:261
  95.4 1.0 collective-permute-done.19.refs_1_
  97.0 4.0 %collective-permute-start.20 = (bf16[512,256]{1,0:T(8,128)(2,1)S(1)}, bf16[512,256]{1,0:T(8,128)(2,1)S(1)}, u32[]{:S(2)}, u32[]{:S(2)}) collective-permute-start(bf16[512,256]{1,0:T(8,128)(2,1)S(1)} %get-tuple-element.122), channel_id=1, source_target_pairs={{0,6},{2,0},{4,2},{6,4},{1,7},{3,1},{5,3},{7,5},{8,14},{10,8},{12,... | collective-permute-start | bytes 786440 | tf_op jit(solution)/shard_map/ppermute | solution.py:261
  101.8 3.1 %collective-permute-done.20.refs_5_ = bf16[512,256]{1,0:T(8,128)(2,1)S(1)} collective-permute-done((bf16[512,256]{1,0:T(8,128)(2,1)S(1)}, bf16[512,256]{1,0:T(8,128)(2,1)S(1)}, u32[]{:S(2)}, u32[]{:S(2)}) %collective-permute-start.20) | collective-permute-done | bytes 262176 | tf_op jit(solution)/shard_map/ppermute | solution.py:261
  104.9 1.3 grad.1
  106.2 1.3 collective-permute-start.24
  108.1 1.6 %collective-permute-start.26 = (bf16[256,256]{1,0:T(8,128)(2,1)S(1)}, bf16[256,256]{1,0:T(8,128)(2,1)S(1)}, u32[]{:S(2)}, u32[]{:S(2)}) collective-permute-start(bf16[256,256]{1,0:T(8,128)(2,1)S(1)} %get-tuple-element.131), channel_id=1, source_target_pairs={{0,24},{8,16},{16,8},{24,0},{1,25},{9,17},{17,9},{25,1},{2,26},{10... | collective-permute-start | bytes 393224 | tf_op jit(solution)/shard_map/ppermute | solution.py:258
  109.7 1.5 %collective-permute-done.24.refs_1_ = bf16[256,256]{1,0:T(8,128)(2,1)S(1)} collective-permute-done((bf16[256,256]{1,0:T(8,128)(2,1)S(1)}, bf16[256,256]{1,0:T(8,128)(2,1)S(1)}, u32[]{:S(2)}, u32[]{:S(2)}) %collective-permute-start.24) | collective-permute-done | bytes 131104 | tf_op jit(solution)/shard_map/ppermute | solution.py:258
  111.2 1.2 collective-permute-done.25.refs_2_
  112.4 1.5 %collective-permute-done.26.refs_3_ = bf16[256,256]{1,0:T(8,128)(2,1)S(1)} collective-permute-done((bf16[256,256]{1,0:T(8,128)(2,1)S(1)}, bf16[256,256]{1,0:T(8,128)(2,1)S(1)}, u32[]{:S(2)}, u32[]{:S(2)}) %collective-permute-start.26) | collective-permute-done | bytes 131104 | tf_op jit(solution)/shard_map/ppermute | solution.py:258
  114.1 6.3 %collective-permute-done.27.refs_1_ = bf16[256,256]{1,0:T(8,128)(2,1)S(1)} collective-permute-done((bf16[256,256]{1,0:T(8,128)(2,1)S(1)}, bf16[256,256]{1,0:T(8,128)(2,1)S(1)}, u32[]{:S(2)}, u32[]{:S(2)}) %collective-permute-start.27) | collective-permute-done | bytes 131104 | tf_op jit(solution)/shard_map/ppermute | solution.py:414
  120.4 1.5 %collective-permute-start.28 = (bf16[256,256]{1,0:T(8,128)(2,1)S(1)}, bf16[256,256]{1,0:T(8,128)(2,1)S(1)}, u32[]{:S(2)}, u32[]{:S(2)}) collective-permute-start(bf16[256,256]{1,0:T(8,128)(2,1)S(1)} %sum.4.refs_0_), channel_id=1, source_target_pairs={{0,4},{2,6},{4,0},{6,2},{1,5},{3,7},{5,1},{7,3},{8,12},{10,14},{12... | collective-permute-start | bytes 393224 | tf_op jit(solution)/shard_map/ppermute | solution.py:414
  122.0 5.8 %collective-permute-done.28.refs_1_ = bf16[256,256]{1,0:T(8,128)(2,1)S(1)} collective-permute-done((bf16[256,256]{1,0:T(8,128)(2,1)S(1)}, bf16[256,256]{1,0:T(8,128)(2,1)S(1)}, u32[]{:S(2)}, u32[]{:S(2)}) %collective-permute-start.28) | collective-permute-done | bytes 131104 | tf_op jit(solution)/shard_map/ppermute | solution.py:414
  128.3 1.8 %collective-permute-start.30 = (bf16[256,256]{1,0:T(8,128)(2,1)S(1)}, bf16[256,256]{1,0:T(8,128)(2,1)S(1)}, u32[]{:S(2)}, u32[]{:S(2)}) collective-permute-start(bf16[256,256]{1,0:T(8,128)(2,1)S(1)} %sum.5.refs_1_), channel_id=1, source_target_pairs={{0,16},{8,24},{16,0},{24,8},{1,17},{9,25},{17,1},{25,9},{2,18},{10... | collective-permute-start | bytes 393224 | tf_op jit(solution)/shard_map/ppermute | solution.py:258
  130.1 1.3 collective-permute-start.31
  131.4 1.5 %collective-permute-done.29.refs_2_ = bf16[256,256]{1,0:T(8,128)(2,1)S(1)} collective-permute-done((bf16[256,256]{1,0:T(8,128)(2,1)S(1)}, bf16[256,256]{1,0:T(8,128)(2,1)S(1)}, u32[]{:S(2)}, u32[]{:S(2)}) %collective-permute-start.29) | collective-permute-done | bytes 131104 | tf_op jit(solution)/shard_map/ppermute | solution.py:258
  132.9 1.2 collective-permute-done.30.refs_3_
  134.0 1.9 %collective-permute-done.31.refs_4_ = bf16[256,256]{1,0:T(8,128)(2,1)S(1)} collective-permute-done((bf16[256,256]{1,0:T(8,128)(2,1)S(1)}, bf16[256,256]{1,0:T(8,128)(2,1)S(1)}, u32[]{:S(2)}, u32[]{:S(2)}) %collective-permute-start.31) | collective-permute-done | bytes 131104 | tf_op jit(solution)/shard_map/ppermute | solution.py:258
  136.0 0.8 pad_maximum_fusion
  137.3 2.0 %last.1 = f32[1024,512]{1,0:T(8,128)} custom-call(s32[3]{0:T(128)S(1)} %pad_add_fusion.refs_0_, bf16[256,256]{1,0:T(8,128)(2,1)S(1)} %sum.5.refs_1_, bf16[256,256]{1,0:T(8,128)(2,1)S(1)} %collective-permute-done.29.refs_2_, bf16[256,256]{1,0:T(8,128)(2,1)S(1)} %collective-permute-done.30.refs_3_, bf16[256,256]{1,0:T(8,128)(2,1)S(1)} %collective-permute-done.31.refs_4_, ...), custom_call_target="tpu_custom_call" | custom-call | flops 200000000 | tf_op jit(solution)/shard_map/last/pallas_call | solution.py:52
  (71 shorter events, 13.0 us)
Async XLA Ops:
  0.6 52.0 %collective-permute-start.5 = (bf16[4,16,128,128]{3,2,1,0:T(8,128)(2,1)}, bf16[4,16,128,128]{3,2,1,0:T(8,128)(2,1)}, u32[]{:S(2)}, u32[]{:S(2)}) collective-permute-start(bf16[4,16,128,128]{3,2,1,0:T(8,128)(2,1)} %refs_3_.1), channel_id=1, source_target_pairs={{0,1},{1,0},{2,3},{3,2},{4,5},{5,4},{6,7},{7,6},{8,9},{9,8},{10,11... | collective-permute-start | bytes 6291464 | tf_op jit(solution)/shard_map/ppermute | solution.py:255
  1.2 0.7 copy-start.4
  3.7 15.1 %all-to-all-start = ((s32[32,8,128]{2,1,0:T(8,128)}), s32[32,8,128]{2,1,0:T(8,128)S(1)}, u32[]{:S(2)}, u32[]{:S(2)}) async-start(s32[32,8,128]{2,1,0:T(8,128)} %index.1), calls=%async_computation | async-start | bytes 262144 | tf_op jit(solution)/shard_map/all_to_all | solution.py:271
  10.6 1.2 copy-start
  11.9 1.2 copy-start.3
  13.1 10.5 %copy-start.5 = (bf16[512,512]{1,0:T(8,128)(2,1)S(1)}, bf16[512,512]{1,0:T(8,128)(2,1)}, u32[]{:S(2)}) copy-start(bf16[512,512]{1,0:T(8,128)(2,1)} %param.13) | copy-start | bytes 1572868
  14.3 15.2 %copy-start.6 = (s32[4,16]{1,0:T(4,128)S(1)}, s32[4,16]{1,0:T(4,128)}, u32[]{:S(2)}) copy-start(s32[4,16]{1,0:T(4,128)} %param.9) | copy-start | bytes 772
  14.4 15.2 %copy-start.7 = (s32[4]{0:T(128)S(1)}, s32[4]{0:T(128)}, u32[]{:S(2)}) copy-start(s32[4]{0:T(128)} %param.10) | copy-start | bytes 52
  14.4 15.5 %copy-start.1 = (bf16[512,1024]{1,0:T(8,128)(2,1)S(1)}, bf16[512,1024]{1,0:T(8,128)(2,1)}, u32[]{:S(2)}) copy-start(bf16[512,1024]{1,0:T(8,128)(2,1)} %refs_1_.1) | copy-start | bytes 3145732
  20.0 6.4 %collective-permute-start = (bf16[2,128,256]{2,1,0:T(8,128)(2,1)S(1)}, bf16[2,128,256]{2,1,0:T(8,128)(2,1)S(1)}, u32[]{:S(2)}, u32[]{:S(2)}) collective-permute-start(bf16[2,128,256]{2,1,0:T(8,128)(2,1)S(1)} %get-tuple-element.75), channel_id=1, source_target_pairs={{0,8},{8,0},{16,24},{24,16},{1,9},{9,1},{17,25},{25,17},{2,10},{10... | collective-permute-start | bytes 393224 | tf_op jit(solution)/shard_map/ppermute | solution.py:258
  20.9 7.8 %collective-permute-start.1 = (bf16[2,128,256]{2,1,0:T(8,128)(2,1)S(1)}, bf16[2,128,256]{2,1,0:T(8,128)(2,1)S(1)}, u32[]{:S(2)}, u32[]{:S(2)}) collective-permute-start(bf16[2,128,256]{2,1,0:T(8,128)(2,1)S(1)} %get-tuple-element.76), channel_id=1, source_target_pairs={{0,16},{8,24},{16,0},{24,8},{1,17},{9,25},{17,1},{25,9},{2,18},{10... | collective-permute-start | bytes 393224 | tf_op jit(solution)/shard_map/ppermute | solution.py:258
  21.6 7.1 %collective-permute-start.2 = (bf16[2,128,256]{2,1,0:T(8,128)(2,1)S(1)}, bf16[2,128,256]{2,1,0:T(8,128)(2,1)S(1)}, u32[]{:S(2)}, u32[]{:S(2)}) collective-permute-start(bf16[2,128,256]{2,1,0:T(8,128)(2,1)S(1)} %get-tuple-element.77), channel_id=1, source_target_pairs={{0,24},{8,16},{16,8},{24,0},{1,25},{9,17},{17,9},{25,1},{2,26},{10... | collective-permute-start | bytes 393224 | tf_op jit(solution)/shard_map/ppermute | solution.py:258
  23.6 7.6 %copy-start.2 = (bf16[4,16,128,128]{3,2,1,0:T(8,128)(2,1)S(1)}, bf16[4,16,128,128]{3,2,1,0:T(8,128)(2,1)}, u32[]{:S(2)}) copy-start(bf16[4,16,128,128]{3,2,1,0:T(8,128)(2,1)} %refs_3_.1) | copy-start | bytes 6291460
  23.6 6.2 %collective-permute-start.3 = (bf16[512,256]{1,0:T(8,128)(2,1)S(1)}, bf16[512,256]{1,0:T(8,128)(2,1)S(1)}, u32[]{:S(2)}, u32[]{:S(2)}) collective-permute-start(bf16[512,256]{1,0:T(8,128)(2,1)S(1)} %get-tuple-element.134), channel_id=1, source_target_pairs={{0,1},{1,0},{2,3},{3,2},{4,5},{5,4},{6,7},{7,6},{8,9},{9,8},{10,11... | collective-permute-start | bytes 786440 | tf_op jit(solution)/shard_map/ppermute | solution.py:255
  28.7 1.8 %collective-permute-start.6 = (bf16[512,256]{1,0:T(8,128)(2,1)S(1)}, bf16[512,256]{1,0:T(8,128)(2,1)S(1)}, u32[]{:S(2)}, u32[]{:S(2)}) collective-permute-start(bf16[512,256]{1,0:T(8,128)(2,1)S(1)} %get-tuple-element.83), channel_id=1, source_target_pairs={{0,1},{1,0},{2,3},{3,2},{4,5},{5,4},{6,7},{7,6},{8,9},{9,8},{10,11... | collective-permute-start | bytes 786440 | tf_op jit(solution)/shard_map/ppermute | solution.py:255
  28.8 11.0 %collective-permute-start.8 = (bf16[512,256]{1,0:T(8,128)(2,1)S(1)}, bf16[512,256]{1,0:T(8,128)(2,1)S(1)}, u32[]{:S(2)}, u32[]{:S(2)}) collective-permute-start(bf16[512,256]{1,0:T(8,128)(2,1)S(1)} %get-tuple-element.84.refs_2_), channel_id=1, source_target_pairs={{0,2},{2,4},{4,6},{6,0},{1,3},{3,5},{5,7},{7,1},{8,10},{10,12},{12... | collective-permute-start | bytes 786440 | tf_op jit(solution)/shard_map/ppermute | solution.py:261
  29.6 1.5 %collective-permute-start.4 = (s32[4,16]{1,0:T(4,128)S(1)}, s32[4,16]{1,0:T(4,128)S(1)}, u32[]{:S(2)}, u32[]{:S(2)}) collective-permute-start(s32[4,16]{1,0:T(4,128)S(1)} %fusion.refs_1_), channel_id=1, source_target_pairs={{0,1},{1,0},{2,3},{3,2},{4,5},{5,4},{6,7},{7,6},{8,9},{9,8},{10,11... | collective-permute-start | bytes 776 | tf_op jit(solution)/shard_map/ppermute | solution.py:255
  30.6 14.8 %collective-permute-start.7 = (bf16[512,256]{1,0:T(8,128)(2,1)S(1)}, bf16[512,256]{1,0:T(8,128)(2,1)S(1)}, u32[]{:S(2)}, u32[]{:S(2)}) collective-permute-start(bf16[512,256]{1,0:T(8,128)(2,1)S(1)} %collective-permute-done.6.refs_3_), channel_id=1, source_target_pairs={{0,2},{2,4},{4,6},{6,0},{1,3},{3,5},{5,7},{7,1},{8,10},{10,12},{12... | collective-permute-start | bytes 786440 | tf_op jit(solution)/shard_map/ppermute | solution.py:261
  39.8 11.2 %collective-permute-start.9 = (bf16[512,256]{1,0:T(8,128)(2,1)S(1)}, bf16[512,256]{1,0:T(8,128)(2,1)S(1)}, u32[]{:S(2)}, u32[]{:S(2)}) collective-permute-start(bf16[512,256]{1,0:T(8,128)(2,1)S(1)} %collective-permute-done.8.refs_2_), channel_id=1, source_target_pairs={{0,2},{2,4},{4,6},{6,0},{1,3},{3,5},{5,7},{7,1},{8,10},{10,12},{12... | collective-permute-start | bytes 786440 | tf_op jit(solution)/shard_map/ppermute | solution.py:261
  45.4 14.2 %collective-permute-start.11 = (bf16[512,256]{1,0:T(8,128)(2,1)S(1)}, bf16[512,256]{1,0:T(8,128)(2,1)S(1)}, u32[]{:S(2)}, u32[]{:S(2)}) collective-permute-start(bf16[512,256]{1,0:T(8,128)(2,1)S(1)} %collective-permute-done.7.refs_3_), channel_id=1, source_target_pairs={{0,2},{2,4},{4,6},{6,0},{1,3},{3,5},{5,7},{7,1},{8,10},{10,12},{12... | collective-permute-start | bytes 786440 | tf_op jit(solution)/shard_map/ppermute | solution.py:261
  45.4 14.3 %collective-permute-start.13 = (bf16[128,1024]{1,0:T(8,128)(2,1)S(1)}, bf16[128,1024]{1,0:T(8,128)(2,1)S(1)}, u32[]{:S(2)}, u32[]{:S(2)}) collective-permute-start(bf16[128,1024]{1,0:T(8,128)(2,1)S(1)} %get-tuple-element.105), channel_id=1, source_target_pairs={{0,8},{8,0},{16,24},{24,16},{1,9},{9,1},{17,25},{25,17},{2,10},{10... | collective-permute-start | bytes 786440 | tf_op jit(solution)/shard_map/ppermute | solution.py:258
  47.1 12.8 %collective-permute-start.14 = (bf16[128,1024]{1,0:T(8,128)(2,1)S(1)}, bf16[128,1024]{1,0:T(8,128)(2,1)S(1)}, u32[]{:S(2)}, u32[]{:S(2)}) collective-permute-start(bf16[128,1024]{1,0:T(8,128)(2,1)S(1)} %get-tuple-element.106), channel_id=1, source_target_pairs={{0,16},{8,24},{16,0},{24,8},{1,17},{9,25},{17,1},{25,9},{2,18},{10... | collective-permute-start | bytes 786440 | tf_op jit(solution)/shard_map/ppermute | solution.py:258
  51.0 8.8 %collective-permute-start.15 = (bf16[128,1024]{1,0:T(8,128)(2,1)S(1)}, bf16[128,1024]{1,0:T(8,128)(2,1)S(1)}, u32[]{:S(2)}, u32[]{:S(2)}) collective-permute-start(bf16[128,1024]{1,0:T(8,128)(2,1)S(1)} %get-tuple-element.107), channel_id=1, source_target_pairs={{0,24},{8,16},{16,8},{24,0},{1,25},{9,17},{17,9},{25,1},{2,26},{10... | collective-permute-start | bytes 786440 | tf_op jit(solution)/shard_map/ppermute | solution.py:258
  52.6 9.9 %collective-permute-start.10 = (bf16[512,256]{1,0:T(8,128)(2,1)S(1)}, bf16[512,256]{1,0:T(8,128)(2,1)S(1)}, u32[]{:S(2)}, u32[]{:S(2)}) collective-permute-start(bf16[512,256]{1,0:T(8,128)(2,1)S(1)} %collective-permute-done.9.refs_2_), channel_id=1, source_target_pairs={{0,2},{2,4},{4,6},{6,0},{1,3},{3,5},{5,7},{7,1},{8,10},{10,12},{12... | collective-permute-start | bytes 786440 | tf_op jit(solution)/shard_map/ppermute | solution.py:261
  59.6 9.0 %collective-permute-start.12 = (bf16[512,256]{1,0:T(8,128)(2,1)S(1)}, bf16[512,256]{1,0:T(8,128)(2,1)S(1)}, u32[]{:S(2)}, u32[]{:S(2)}) collective-permute-start(bf16[512,256]{1,0:T(8,128)(2,1)S(1)} %collective-permute-done.11.refs_3_), channel_id=1, source_target_pairs={{0,2},{2,4},{4,6},{6,0},{1,3},{3,5},{5,7},{7,1},{8,10},{10,12},{12... | collective-permute-start | bytes 786440 | tf_op jit(solution)/shard_map/ppermute | solution.py:261
  60.2 41.5 %collective-permute-start.17 = (bf16[1024,512]{1,0:T(8,128)(2,1)S(1)}, bf16[1024,512]{1,0:T(8,128)(2,1)S(1)}, u32[]{:S(2)}, u32[]{:S(2)}) collective-permute-start(bf16[1024,512]{1,0:T(8,128)(2,1)S(1)} %get-tuple-element.113.refs_1_), channel_id=1, source_target_pairs={{0,1},{1,0},{2,3},{3,2},{4,5},{5,4},{6,7},{7,6},{8,9},{9,8},{10,11... | collective-permute-start | bytes 3145736 | tf_op jit(solution)/shard_map/ppermute | solution.py:255
  70.2 9.3 %collective-permute-start.21 = (bf16[512,256]{1,0:T(8,128)(2,1)S(1)}, bf16[512,256]{1,0:T(8,128)(2,1)S(1)}, u32[]{:S(2)}, u32[]{:S(2)}) collective-permute-start(bf16[512,256]{1,0:T(8,128)(2,1)S(1)} %get-tuple-element.125), channel_id=1, source_target_pairs={{0,6},{2,0},{4,2},{6,4},{1,7},{3,1},{5,3},{7,5},{8,14},{10,8},{12,... | collective-permute-start | bytes 786440 | tf_op jit(solution)/shard_map/ppermute | solution.py:261
  72.0 13.1 %collective-permute-start.18 = (bf16[512,256]{1,0:T(8,128)(2,1)S(1)}, bf16[512,256]{1,0:T(8,128)(2,1)S(1)}, u32[]{:S(2)}, u32[]{:S(2)}) collective-permute-start(bf16[512,256]{1,0:T(8,128)(2,1)S(1)} %get-tuple-element.120), channel_id=1, source_target_pairs={{0,6},{2,0},{4,2},{6,4},{1,7},{3,1},{5,3},{7,5},{8,14},{10,8},{12,... | collective-permute-start | bytes 786440 | tf_op jit(solution)/shard_map/ppermute | solution.py:261
  72.1 17.9 %collective-permute-start.16 = (bf16[512,256]{1,0:T(8,128)(2,1)S(1)}, bf16[512,256]{1,0:T(8,128)(2,1)S(1)}, u32[]{:S(2)}, u32[]{:S(2)}) collective-permute-start(bf16[512,256]{1,0:T(8,128)(2,1)S(1)} %get-tuple-element.112), channel_id=1, source_target_pairs={{0,1},{1,0},{2,3},{3,2},{4,5},{5,4},{6,7},{7,6},{8,9},{9,8},{10,11... | collective-permute-start | bytes 786440 | tf_op jit(solution)/shard_map/ppermute | solution.py:255
  80.1 10.6 %collective-permute-start.22 = (bf16[512,256]{1,0:T(8,128)(2,1)S(1)}, bf16[512,256]{1,0:T(8,128)(2,1)S(1)}, u32[]{:S(2)}, u32[]{:S(2)}) collective-permute-start(bf16[512,256]{1,0:T(8,128)(2,1)S(1)} %get-tuple-element.126), channel_id=1, source_target_pairs={{0,6},{2,0},{4,2},{6,4},{1,7},{3,1},{5,3},{7,5},{8,14},{10,8},{12,... | collective-permute-start | bytes 786440 | tf_op jit(solution)/shard_map/ppermute | solution.py:261
  85.8 10.6 %collective-permute-start.19 = (bf16[512,256]{1,0:T(8,128)(2,1)S(1)}, bf16[512,256]{1,0:T(8,128)(2,1)S(1)}, u32[]{:S(2)}, u32[]{:S(2)}) collective-permute-start(bf16[512,256]{1,0:T(8,128)(2,1)S(1)} %get-tuple-element.121), channel_id=1, source_target_pairs={{0,6},{2,0},{4,2},{6,4},{1,7},{3,1},{5,3},{7,5},{8,14},{10,8},{12,... | collective-permute-start | bytes 786440 | tf_op jit(solution)/shard_map/ppermute | solution.py:261
  91.4 10.4 %collective-permute-start.23 = (bf16[512,256]{1,0:T(8,128)(2,1)S(1)}, bf16[512,256]{1,0:T(8,128)(2,1)S(1)}, u32[]{:S(2)}, u32[]{:S(2)}) collective-permute-start(bf16[512,256]{1,0:T(8,128)(2,1)S(1)} %get-tuple-element.127), channel_id=1, source_target_pairs={{0,6},{2,0},{4,2},{6,4},{1,7},{3,1},{5,3},{7,5},{8,14},{10,8},{12,... | collective-permute-start | bytes 786440 | tf_op jit(solution)/shard_map/ppermute | solution.py:261
  97.0 7.9 %collective-permute-start.20 = (bf16[512,256]{1,0:T(8,128)(2,1)S(1)}, bf16[512,256]{1,0:T(8,128)(2,1)S(1)}, u32[]{:S(2)}, u32[]{:S(2)}) collective-permute-start(bf16[512,256]{1,0:T(8,128)(2,1)S(1)} %get-tuple-element.122), channel_id=1, source_target_pairs={{0,6},{2,0},{4,2},{6,4},{1,7},{3,1},{5,3},{7,5},{8,14},{10,8},{12,... | collective-permute-start | bytes 786440 | tf_op jit(solution)/shard_map/ppermute | solution.py:261
  106.2 5.0 %collective-permute-start.24 = (bf16[256,256]{1,0:T(8,128)(2,1)S(1)}, bf16[256,256]{1,0:T(8,128)(2,1)S(1)}, u32[]{:S(2)}, u32[]{:S(2)}) collective-permute-start(bf16[256,256]{1,0:T(8,128)(2,1)S(1)} %get-tuple-element.129), channel_id=1, source_target_pairs={{0,8},{8,0},{16,24},{24,16},{1,9},{9,1},{17,25},{25,17},{2,10},{10... | collective-permute-start | bytes 393224 | tf_op jit(solution)/shard_map/ppermute | solution.py:258
  107.5 5.0 %collective-permute-start.25 = (bf16[256,256]{1,0:T(8,128)(2,1)S(1)}, bf16[256,256]{1,0:T(8,128)(2,1)S(1)}, u32[]{:S(2)}, u32[]{:S(2)}) collective-permute-start(bf16[256,256]{1,0:T(8,128)(2,1)S(1)} %get-tuple-element.130), channel_id=1, source_target_pairs={{0,16},{8,24},{16,0},{24,8},{1,17},{9,25},{17,1},{25,9},{2,18},{10... | collective-permute-start | bytes 393224 | tf_op jit(solution)/shard_map/ppermute | solution.py:258
  108.1 5.9 %collective-permute-start.26 = (bf16[256,256]{1,0:T(8,128)(2,1)S(1)}, bf16[256,256]{1,0:T(8,128)(2,1)S(1)}, u32[]{:S(2)}, u32[]{:S(2)}) collective-permute-start(bf16[256,256]{1,0:T(8,128)(2,1)S(1)} %get-tuple-element.131), channel_id=1, source_target_pairs={{0,24},{8,16},{16,8},{24,0},{1,25},{9,17},{17,9},{25,1},{2,26},{10... | collective-permute-start | bytes 393224 | tf_op jit(solution)/shard_map/ppermute | solution.py:258
  114.0 6.4 %collective-permute-start.27 = (bf16[256,256]{1,0:T(8,128)(2,1)S(1)}, bf16[256,256]{1,0:T(8,128)(2,1)S(1)}, u32[]{:S(2)}, u32[]{:S(2)}) collective-permute-start(bf16[256,256]{1,0:T(8,128)(2,1)S(1)} %sum.3.refs_0_), channel_id=1, source_target_pairs={{0,2},{2,0},{4,6},{6,4},{1,3},{3,1},{5,7},{7,5},{8,10},{10,8},{12,... | collective-permute-start | bytes 393224 | tf_op jit(solution)/shard_map/ppermute | solution.py:414
  120.4 7.3 %collective-permute-start.28 = (bf16[256,256]{1,0:T(8,128)(2,1)S(1)}, bf16[256,256]{1,0:T(8,128)(2,1)S(1)}, u32[]{:S(2)}, u32[]{:S(2)}) collective-permute-start(bf16[256,256]{1,0:T(8,128)(2,1)S(1)} %sum.4.refs_0_), channel_id=1, source_target_pairs={{0,4},{2,6},{4,0},{6,2},{1,5},{3,7},{5,1},{7,3},{8,12},{10,14},{12... | collective-permute-start | bytes 393224 | tf_op jit(solution)/shard_map/ppermute | solution.py:414
  127.8 5.0 %collective-permute-start.29 = (bf16[256,256]{1,0:T(8,128)(2,1)S(1)}, bf16[256,256]{1,0:T(8,128)(2,1)S(1)}, u32[]{:S(2)}, u32[]{:S(2)}) collective-permute-start(bf16[256,256]{1,0:T(8,128)(2,1)S(1)} %sum.5.refs_1_), channel_id=1, source_target_pairs={{0,8},{8,0},{16,24},{24,16},{1,9},{9,1},{17,25},{25,17},{2,10},{10... | collective-permute-start | bytes 393224 | tf_op jit(solution)/shard_map/ppermute | solution.py:258
  128.3 5.7 %collective-permute-start.30 = (bf16[256,256]{1,0:T(8,128)(2,1)S(1)}, bf16[256,256]{1,0:T(8,128)(2,1)S(1)}, u32[]{:S(2)}, u32[]{:S(2)}) collective-permute-start(bf16[256,256]{1,0:T(8,128)(2,1)S(1)} %sum.5.refs_1_), channel_id=1, source_target_pairs={{0,16},{8,24},{16,0},{24,8},{1,17},{9,25},{17,1},{25,9},{2,18},{10... | collective-permute-start | bytes 393224 | tf_op jit(solution)/shard_map/ppermute | solution.py:258
  130.1 5.9 %collective-permute-start.31 = (bf16[256,256]{1,0:T(8,128)(2,1)S(1)}, bf16[256,256]{1,0:T(8,128)(2,1)S(1)}, u32[]{:S(2)}, u32[]{:S(2)}) collective-permute-start(bf16[256,256]{1,0:T(8,128)(2,1)S(1)} %sum.5.refs_1_), channel_id=1, source_target_pairs={{0,24},{8,16},{16,8},{24,0},{1,25},{9,17},{17,9},{25,1},{2,26},{10... | collective-permute-start | bytes 393224 | tf_op jit(solution)/shard_map/ppermute | solution.py:258
  131.4 5.5 %collective-permute-start.32 = (bf16[256,256]{1,0:T(8,128)(2,1)S(1)}, bf16[256,256]{1,0:T(8,128)(2,1)S(1)}, u32[]{:S(2)}, u32[]{:S(2)}) collective-permute-start(bf16[256,256]{1,0:T(8,128)(2,1)S(1)} %sum.5.refs_1_), channel_id=1, source_target_pairs={{0,1},{1,0},{2,3},{3,2},{4,5},{5,4},{6,7},{7,6},{8,9},{9,8},{10,11... | collective-permute-start | bytes 393224 | tf_op jit(solution)/shard_map/ppermute | solution.py:255
  132.9 4.0 %collective-permute-start.33 = (bf16[256,256]{1,0:T(8,128)(2,1)S(1)}, bf16[256,256]{1,0:T(8,128)(2,1)S(1)}, u32[]{:S(2)}, u32[]{:S(2)}) collective-permute-start(bf16[256,256]{1,0:T(8,128)(2,1)S(1)} %collective-permute-done.29.refs_2_), channel_id=1, source_target_pairs={{0,1},{1,0},{2,3},{3,2},{4,5},{5,4},{6,7},{7,6},{8,9},{9,8},{10,11... | collective-permute-start | bytes 393224 | tf_op jit(solution)/shard_map/ppermute | solution.py:255
  134.0 2.8 %collective-permute-start.34 = (bf16[256,256]{1,0:T(8,128)(2,1)S(1)}, bf16[256,256]{1,0:T(8,128)(2,1)S(1)}, u32[]{:S(2)}, u32[]{:S(2)}) collective-permute-start(bf16[256,256]{1,0:T(8,128)(2,1)S(1)} %collective-permute-done.30.refs_3_), channel_id=1, source_target_pairs={{0,1},{1,0},{2,3},{3,2},{4,5},{5,4},{6,7},{7,6},{8,9},{9,8},{10,11... | collective-permute-start | bytes 393224 | tf_op jit(solution)/shard_map/ppermute | solution.py:255
  136.0 1.3 collective-permute-start.35

commit v14 on v13

--- a/solution.py
+++ b/solution.py
@@ -31,7 +31,7 @@
     return lax.dot_general(a, b, (((0,), (0,)), ((), ())), preferred_element_type=F32)
 
 
-def call(body, outs, ins, name, us, scratch=(), after=(), token=False):
+def call(body, outs, ins, name, us, scratch=(), after=(), token=False, where=pltpu.VMEM):
     smem = pl.BlockSpec(memory_space=pltpu.SMEM)
     vmem = pl.BlockSpec(memory_space=pltpu.VMEM)
     count = len(ins)
@@ -48,13 +48,13 @@
         body(*refs)
 
     arrays = [jax.ShapeDtypeStruct(s, d) for s, d in outs] + [value for _, value in ins]
-    size = sum(a.size * a.dtype.itemsize for a in arrays + [m.get_array_aval() for m in scratch])
+    size = sum(a.size * a.dtype.itemsize for a in arrays + [m.get_array_aval() for m in scratch if m.memory_space == pltpu.VMEM])
     return pl.pallas_call(
         kernel,
         out_shape=tuple(jax.ShapeDtypeStruct(s, d) for s, d in outs),
-        in_specs=[smem if where == "s" else vmem for where, _ in ins]
+        in_specs=[smem if kind == "s" else vmem for kind, _ in ins]
         + [vmem] * ties,
-        out_specs=tuple(vmem for _ in outs),
+        out_specs=tuple(pl.BlockSpec(memory_space=where) for _ in outs),
         scratch_shapes=list(scratch),
         compiler_params=pltpu.CompilerParams(vmem_limit_bytes=size + (5 << 20)),
         cost_estimate=pl.CostEstimate(flops=int(us * 1e8), bytes_accessed=0, transcendentals=0),
@@ -204,10 +204,10 @@
 
 
 def back_kernel(turned_a, turned_b, grad_a, grad_b, *outs):
-    size = outs[0].shape[0]
+    size = outs[0].shape[1]
     for i, out in enumerate(outs):
-        rows = pl.ds(i * size, size)
-        value = dot(turned_a[rows, :], grad_a[...]) + dot(turned_b[rows, :], grad_b[...])
+        cols = pl.ds(i * size, size)
+        value = dot(turned_a[...], grad_a[:, cols]) + dot(turned_b[...], grad_b[:, cols])
         out[...] = value.astype(out.dtype)
 
 
@@ -215,31 +215,45 @@
     out_ref[...] = (mine_ref[...] + come_ref[...].astype(F32)).astype(BF16)
 
 
-def grad_kernel(z, me_ref, left_a, left_b, mine_a, mine_b, come_a, come_b, *refs):
+def grad_kernel(z, me_ref, left_a, left_b, mine_ref, come_ref, *refs):
     outs, whole = refs[:-1], refs[-1]
-    grads = [
-        (mine[...] + come[...].astype(F32)).astype(BF16)
-        for mine, come in ((mine_a, come_a), (mine_b, come_b))
-    ]
-    whole[...] = (dot(left_a[...], grads[0]) + dot(left_b[...], grads[1])).astype(BF16)
+    grad = (mine_ref[...] + come_ref[...].astype(F32)).astype(BF16)
+    total = dot(left_a[...], grad[:z.rows]) + dot(left_b[...], grad[z.rows:])
+    whole[...] = total.astype(BF16)
     share = whole.shape[0] // z.grp
     for s in range(z.grp):
         at = pl.multiple_of((me_ref[0] ^ s) * share, share)
         outs[s][...] = whole[pl.ds(at, share), :]
 
 
+def merge_kernel(*refs):
+    terms, out = refs[:-1], refs[-1]
+    count, width = len(terms) // 2, terms[0].shape[1]
+    for i in range(2):
+        value = sum(term[...].astype(F32) for term in terms[i * count:(i + 1) * count])
+        out[:, i * width:(i + 1) * width] = value.astype(BF16)
+
+
 def sum_kernel(*refs):
     refs[-1][...] = sum(term[...].astype(F32) for term in refs[:-1]).astype(BF16)
 
 
 def last_kernel(z, me_ref, *refs):
-    pieces, out = refs[:-1], refs[-1]
+    pieces, (out, whole, sems) = refs[:-3], refs[-3:]
     share, half = pieces[0].shape
-    for rel in range(2):
-        left = pl.multiple_of((me_ref[2] ^ rel) * half, half)
-        for s in range(z.grp):
-            at = pl.multiple_of((me_ref[0] ^ s) * share, share)
-            out[pl.ds(at, share), pl.ds(left, half)] = pieces[rel * z.grp + s][...].astype(F32)
+    copies = []
+    for s in range(z.grp):
+        rows = pl.ds(s * share, share)
+        for rel in range(2):
+            left = pl.multiple_of((me_ref[2] ^ rel) * half, half)
+            whole[rows, pl.ds(left, half)] = pieces[rel * z.grp + s][...].astype(F32)
+        at = pl.multiple_of((me_ref[0] ^ s) * share, share)
+        copies.append(
+            pltpu.make_async_copy(whole.at[rows], out.at[pl.ds(at, share)], sems.at[s])
+        )
+        copies[-1].start()
+    for copy in copies:
+        copy.wait()
 
 
 def shards(features, node_order, block_cols, block_count, block_vals, weight, cotangent):
@@ -312,19 +326,22 @@
         "send", 1.5, token=True,
     )
     token, cotangent, block_cols = lax.optimization_barrier((token, cotangent, block_cols))
-    own, other, token = pack(across(got), [token])
-    ring = [[own, to_core(other)]]
-
     live = iota((tiles, blocks), 1) < block_count[:, None]
     cols_a = jnp.where(live, block_cols, z.dom * tiles)
     cols_b = to_core(cols_a)
     cot_a = lax.dynamic_slice_in_dim(cotangent, core * half, half, axis=1)
     cot_b = to_core(lax.dynamic_slice_in_dim(cotangent, (1 - core) * half, half, axis=1))
 
+    came = across(got)
+    *picked, token_r = rows_of(pick, features, [token, cot_a, cot_b])
+    own, other, token = pack(came, [token_r])
+    ring = [[own, to_core(other)]]
+    lefts, token_l = turned_of(across(picked))
+
     wide = 2 * z.grp * z.per_grp
     inner = (wide, rows) if z.pair % 16 == 0 else (2 * z.grp, z.dom, z.pair, rows)
 
-    def prepared(cols, vals, token):
+    def prepared(cols, vals, token, after=()):
         *got, token = call(
             lambda *refs: prepare_kernel(z, *refs),
             [(inner, BF16)] * z.zz,
@@ -334,21 +351,20 @@
                 pltpu.VMEM((z.dom * rows + tile, tile), F32),
                 pltpu.VMEM((z.dom * rows, rows), BF16),
             ),
-            after=[token, cols_b], token=True,
+            after=[token, cols_b, *after], token=True,
         )
         return [part.reshape(wide, rows) for part in got], token
 
     for k in range(1, z.zz):
         ring.append([to_zz(part, 1) for part in ring[-1]])
         if k == 1:
-            *picked, token = rows_of(pick, features, [token, cot_a, cot_b])
-            lefts, token_l = turned_of(across(picked))
-            turned_a, token = prepared(cols_a, block_vals, token)
+            turned_a, token = prepared(cols_a, block_vals, token, [vals_b])
             for part in range(2):
                 ring[1][part], token = lax.optimization_barrier((ring[1][part], token))
         if k == 2:
-            turned_b, token = prepared(cols_b, vals_b, token)
-            ring[2][1], token = lax.optimization_barrier((ring[2][1], token))
+            turned_b, token = prepared(cols_b, vals_b, token, [token_l])
+            for part in range(2):
+                ring[2][part], token = lax.optimization_barrier((ring[2][part], token))
     turned = (turned_a, turned_b)
 
     agg = []
@@ -359,18 +375,18 @@
         if last:
             ahead = (turned[0][k], turned[1][k])
             ins += [("v", part) for part in (cot_a, cot_b, *ahead)]
-            outs = [((rows, half), BF16)] * 6
+            outs = [((rows, half), BF16)] * 4 + [((wide, half // 2), BF16)] * 2
         agg = call(
             lambda *refs, k=k, last=last: forward_kernel(z, k == 0, last, *refs),
             outs, ins, "forward", 3 if last else 1,
-            after=[token_l] if k == z.zz - 2 else [token] if k == 0 else (),
+            after=[token] if k == 0 else (),
         )
     hidden_a, hidden_b, grad_a, grad_b, *came = agg
 
     def back(k):
         return call(
             back_kernel,
-            [((rows, half), F32)] * 2,
+            [((wide, half // 2), F32)] * 2,
             [("v", part) for part in (turned[0][k], turned[1][k], grad_a, grad_b)],
             "back", 1,
         )
@@ -382,7 +398,8 @@
         if k:
             passed = [
                 call(
-                    pass_kernel, [((rows, half), BF16)], [("v", part), ("v", moved)], "pass", 0.5,
+                    pass_kernel, [((wide, half // 2), BF16)], [("v", part), ("v", moved)],
+                    "pass", 0.5,
                     after=[come] if i == 1 and k == 1 else (), token=True,
                 )
                 for i, (part, moved) in enumerate(zip(mine, came))
@@ -394,20 +411,25 @@
     )
 
     share = width_in // z.grp
-    terms = call(
-        lambda *refs: grad_kernel(z, *refs),
-        [((share, half), BF16)] * z.grp,
-        [("s", me)] + [("v", part) for part in (*lefts, *mine, *came)],
-        "grad", 1.5,
-        (pltpu.VMEM((width_in, half), BF16),),
-    )
+    terms = []
+    for part, moved in zip(mine, came):
+        got = call(
+            lambda *refs: grad_kernel(z, *refs),
+            [((share, half // 2), BF16)] * z.grp,
+            [("s", me)] + [("v", value) for value in (*lefts, part, moved)],
+            "grad", 1.5,
+            (pltpu.VMEM((width_in, half // 2), BF16),),
+        )
+        terms += across(got)
 
     def total_of(parts):
         return call(
             sum_kernel, [((share, half), BF16)], [("v", part) for part in parts], "sum", 0.5
         )[0]
 
-    mine = total_of([to_grp(terms[s], s) for s in range(z.grp)])
+    (mine,) = call(
+        merge_kernel, [((share, half), BF16)], [("v", term) for term in terms], "merge", 0.5
+    )
     step = 1
     while step < z.zz:
         mine = total_of(
@@ -420,6 +442,8 @@
         [((width_in, hidden_units), F32)],
         [("s", me)] + [("v", part) for part in mine + [to_core(part) for part in mine]],
         "last", 2,
+        (pltpu.VMEM((width_in, hidden_units), F32), pltpu.SemaphoreType.DMA((z.grp,))),
+        where=pl.ANY,
     )
     return hidden, grad_weight
 

time: 140 us -> 145 us (1.036)
  starting transfers between devices: 42.3 us -> 36.3 us
  waiting for transfers between devices: 61.8 us -> 67.6 us
  local copies, waits for them, and re-layouts: 3.19 us -> 5.86 us
  Pallas kernels: 30.1 us -> 32.3 us
    ppermute x12, starting transfers between devices: 18.3 us -> 9.86 us  [to_zz(): lax.ppermute(x, 'zz', [(i, (i + k) % z.zz) for i in range(z.zz)])]
    ppermute x12, waiting for transfers between devices: 30.9 us -> 36.7 us  [to_zz(): lax.ppermute(x, 'zz', [(i, (i + k) % z.zz) for i in range(z.zz)])]
    ppermute x12 -> x15, starting transfers between devices: 14.5 us -> 18.1 us  [to_grp(): lax.ppermute(x, 'grp', [(i, i ^ s) for i in range(z.grp)])]
    pallas_call x24 -> x25, Pallas kernels: 30.1 us -> 32.3 us  [call(): pl.pallas_call(kernel, out_shape=tuple((jax.ShapeDtypeStruct(s, d) for s,...]
    unnamed x16 -> x18, local copies, waits for them, and re-layouts: 3.15 us -> 4.79 us
    ppermute x12 -> x15, waiting for transfers between devices: 14 us -> 14.1 us  [to_grp(): lax.ppermute(x, 'grp', [(i, i ^ s) for i in range(z.grp)])]
  transfers between devices with their start and end apart: 37 -> 40, of which waited for: 23 -> 23; matrix products, arithmetic and copies ran while one was open for 1% -> 1% of each run, Pallas kernels for 18% -> 20%
where the time goes in v14:
time: 145 us; the launch traced here: 144 us
  waiting for transfers between devices  67.6 us (47%)
  starting transfers between devices  36.3 us (25%)
  Pallas kernels  32.3 us (22%)
  local copies, waits for them, and re-layouts  5.86 us (4%)
    ppermute x12, waiting for transfers between devices, to_zz(): lax.ppermute(x, 'zz', [(i, (i + k) % z.zz) for i in range(z.zz)])  36.7 us
    pallas_call x25, Pallas kernels, call(): pl.pallas_call(kernel, out_shape=tuple((jax.ShapeDtypeStruct(s, d) for s,...  32.3 us
    ppermute x15, starting transfers between devices, to_grp(): lax.ppermute(x, 'grp', [(i, i ^ s) for i in range(z.grp)])  18.1 us
    ppermute x15, waiting for transfers between devices, to_grp(): lax.ppermute(x, 'grp', [(i, i ^ s) for i in range(z.grp)])  14.1 us
    ppermute x2, waiting for transfers between devices, shards(): lax.ppermute(mine, 'zz', [(i, i ^ step) for i in range(z.zz)])  11.4 us
    ppermute x12, starting transfers between devices, to_zz(): lax.ppermute(x, 'zz', [(i, (i + k) % z.zz) for i in range(z.zz)])  9.86 us
    all_to_all x1, starting transfers between devices, shards(): lax.all_to_all(message, ('grp', 'zz', 'core'), split_axis=0, concat_axis=...  6.96 us
    unnamed x18, local copies, waits for them, and re-layouts  4.79 us
  transfers between devices with their start and end apart: 40, of which 23 were waited for; matrix products, arithmetic and copies ran while one was open for 1% of the time, Pallas kernels for 20%

profile of v14, /device:TPU:0, one launch (start us, length us, event | category | flops | bytes accessed | tf_op | source)
XLA Modules:
  0.0 144.3 jit_solution(2272243344643813319)
XLA Ops:
  1.9 1.8 %index.1 = s32[32,8,128]{2,1,0:T(8,128)} custom-call(s32[3]{0:T(128)S(1)} %pad_add_fusion.refs_0_, s32[1,512]{1,0:T(1,128)S(1)} %bitcast.4), custom_call_target="tpu_custom_call" | custom-call | flops 100000000 | tf_op jit(solution)/shard_map/index/pallas_call | solution.py:52
  3.7 7.0 %all-to-all-start = ((s32[32,8,128]{2,1,0:T(8,128)}), s32[32,8,128]{2,1,0:T(8,128)S(1)}, u32[]{:S(2)}, u32[]{:S(2)}) async-start(s32[32,8,128]{2,1,0:T(8,128)} %index.1), calls=%async_computation | async-start | bytes 262144 | tf_op jit(solution)/shard_map/all_to_all | solution.py:285
  10.6 1.2 copy-done.1
  11.9 1.2 copy-done.5
  13.1 1.3 product.1
  15.1 3.7 %all-to-all-done.refs_1_.refs_2_ = s32[32,8,128]{2,1,0:T(8,128)S(1)} async-done(((s32[32,8,128]{2,1,0:T(8,128)}), s32[32,8,128]{2,1,0:T(8,128)S(1)}, u32[]{:S(2)}, u32[]{:S(2)}) %all-to-all-start) | async-done | bytes 131104 | tf_op jit(solution)/shard_map/all_to_all | solution.py:285
  19.8 1.2 send.1
  23.8 2.2 %collective-permute-start.2 = (bf16[2,128,256]{2,1,0:T(8,128)(2,1)S(1)}, bf16[2,128,256]{2,1,0:T(8,128)(2,1)S(1)}, u32[]{:S(2)}, u32[]{:S(2)}) collective-permute-start(bf16[2,128,256]{2,1,0:T(8,128)(2,1)S(1)} %get-tuple-element.82), channel_id=1, source_target_pairs={{0,24},{8,16},{16,8},{24,0},{1,25},{9,17},{17,9},{25,1},{2,26},{10... | collective-permute-start | bytes 393224 | tf_op jit(solution)/shard_map/ppermute | solution.py:272
  26.7 2.1 %collective-permute-done.refs_1_ = bf16[2,128,256]{2,1,0:T(8,128)(2,1)S(1)} collective-permute-done((bf16[2,128,256]{2,1,0:T(8,128)(2,1)S(1)}, bf16[2,128,256]{2,1,0:T(8,128)(2,1)S(1)}, u32[]{:S(2)}, u32[]{:S(2)}) %collective-permute-start) | collective-permute-done | bytes 131104 | tf_op jit(solution)/shard_map/ppermute | solution.py:272
  28.8 2.6 %collective-permute-done.1.refs_2_ = bf16[2,128,256]{2,1,0:T(8,128)(2,1)S(1)} collective-permute-done((bf16[2,128,256]{2,1,0:T(8,128)(2,1)S(1)}, bf16[2,128,256]{2,1,0:T(8,128)(2,1)S(1)}, u32[]{:S(2)}, u32[]{:S(2)}) %collective-permute-start.1) | collective-permute-done | bytes 131104 | tf_op jit(solution)/shard_map/ppermute | solution.py:272
  31.8 1.3 collective-permute-done.6.refs_3_
  33.3 1.4 collective-permute-start.10
  34.7 1.8 %collective-permute-start.11 = (bf16[128,1024]{1,0:T(8,128)(2,1)S(1)}, bf16[128,1024]{1,0:T(8,128)(2,1)S(1)}, u32[]{:S(2)}, u32[]{:S(2)}) collective-permute-start(bf16[128,1024]{1,0:T(8,128)(2,1)S(1)} %get-tuple-element.97), channel_id=1, source_target_pairs={{0,24},{8,16},{16,8},{24,0},{1,25},{9,17},{17,9},{25,1},{2,26},{10... | collective-permute-start | bytes 786440 | tf_op jit(solution)/shard_map/ppermute | solution.py:272
  37.2 5.9 %prepare.2 = (bf16[1024,512]{1,0:T(8,128)(2,1)S(1)}, bf16[1024,512]{1,0:T(8,128)(2,1)S(1)}, bf16[1024,512]{1,0:T(8,128)(2,1)S(1)}, bf16[1024,512]{1,0:T(8,128)(2,1)S(1)}, f32[8,128]{1,0:T(8,128)S(1)}) custom-call(s32[3]{0:T(128)S(1)} %pad_add_fusion.refs_0_, s32[4,16]{1,0:T(4,128)S(1)} %fusion.refs_1_, s32[32,8,128]{2,1,0:T(8,128)S(1)} %all-to-all-done.refs_1_.refs_2_, ...), custom_call_target="tpu_custom_call" | custom-call | flops 700000000 | tf_op jit(solution)/shard_map/prepare/pallas_call | solution.py:52
  43.7 4.3 %collective-permute-done.7.refs_3_ = bf16[512,256]{1,0:T(8,128)(2,1)S(1)} collective-permute-done((bf16[512,256]{1,0:T(8,128)(2,1)S(1)}, bf16[512,256]{1,0:T(8,128)(2,1)S(1)}, u32[]{:S(2)}, u32[]{:S(2)}) %collective-permute-start.7) | collective-permute-done | bytes 262176 | tf_op jit(solution)/shard_map/ppermute | solution.py:275
  48.0 1.2 collective-permute-done.9.refs_1_
  49.6 5.9 %prepare.3 = (bf16[1024,512]{1,0:T(8,128)(2,1)S(1)}, bf16[1024,512]{1,0:T(8,128)(2,1)S(1)}, bf16[1024,512]{1,0:T(8,128)(2,1)S(1)}, bf16[1024,512]{1,0:T(8,128)(2,1)S(1)}, f32[8,128]{1,0:T(8,128)S(1)}) custom-call(s32[3]{0:T(128)S(1)} %pad_add_fusion.refs_0_, s32[4,16]{1,0:T(4,128)S(1)} %collective-permute-done.4.refs_5_.refs_1_, ...), custom_call_target="tpu_custom_call" | custom-call | flops 700000000 | tf_op jit(solution)/shard_map/prepare/pallas_call | solution.py:52
  55.5 3.4 %collective-permute-done.14.refs_3_ = bf16[512,256]{1,0:T(8,128)(2,1)S(1)} collective-permute-done((bf16[512,256]{1,0:T(8,128)(2,1)S(1)}, bf16[512,256]{1,0:T(8,128)(2,1)S(1)}, u32[]{:S(2)}, u32[]{:S(2)}) %collective-permute-start.14) | collective-permute-done | bytes 262176 | tf_op jit(solution)/shard_map/ppermute | solution.py:275
  61.9 8.0 %collective-permute-done.15.refs_3_ = bf16[512,256]{1,0:T(8,128)(2,1)S(1)} collective-permute-done((bf16[512,256]{1,0:T(8,128)(2,1)S(1)}, bf16[512,256]{1,0:T(8,128)(2,1)S(1)}, u32[]{:S(2)}, u32[]{:S(2)}) %collective-permute-start.15) | collective-permute-done | bytes 262176 | tf_op jit(solution)/shard_map/ppermute | solution.py:275
  69.9 3.7 %collective-permute-done.13.refs_2_ = bf16[512,256]{1,0:T(8,128)(2,1)S(1)} collective-permute-done((bf16[512,256]{1,0:T(8,128)(2,1)S(1)}, bf16[512,256]{1,0:T(8,128)(2,1)S(1)}, u32[]{:S(2)}, u32[]{:S(2)}) %collective-permute-start.13) | collective-permute-done | bytes 262176 | tf_op jit(solution)/shard_map/ppermute | solution.py:275
  73.7 2.1 %forward.7 = (bf16[512,256]{1,0:T(8,128)(2,1)S(1)}, bf16[512,256]{1,0:T(8,128)(2,1)S(1)}, bf16[512,256]{1,0:T(8,128)(2,1)S(1)}, bf16[512,256]{1,0:T(8,128)(2,1)S...) custom-call(bf16[1024,512]{1,0:T(8,128)(2,1)S(1)} %get-tuple-element.88.refs_0_.refs_8_, ...), custom_call_target="tpu_custom_call" | custom-call | flops 300000000 | tf_op jit(solution)/shard_map/forward/pallas_call | solution.py:52
  76.0 1.2 back.5
  77.2 7.8 %collective-permute-done.24.refs_1_ = bf16[1024,128]{1,0:T(8,128)(2,1)S(1)} collective-permute-done((bf16[1024,128]{1,0:T(8,128)(2,1)S(1)}, bf16[1024,128]{1,0:T(8,128)(2,1)S(1)}, u32[]{:S(2)}, u32[]{:S(2)}) %collective-permute-start.24) | collective-permute-done | bytes 262176 | tf_op jit(solution)/shard_map/ppermute | solution.py:275
  85.7 1.8 %collective-permute-start.25 = (bf16[1024,128]{1,0:T(8,128)(2,1)S(1)}, bf16[1024,128]{1,0:T(8,128)(2,1)S(1)}, u32[]{:S(2)}, u32[]{:S(2)}) collective-permute-start(bf16[1024,128]{1,0:T(8,128)(2,1)S(1)} %get-tuple-element.138), channel_id=1, source_target_pairs={{0,6},{2,0},{4,2},{6,4},{1,7},{3,1},{5,3},{7,5},{8,14},{10,8},{12,... | collective-permute-start | bytes 786440 | tf_op jit(solution)/shard_map/ppermute | solution.py:275
  87.5 3.2 %collective-permute-done.18.refs_1_ = bf16[1024,128]{1,0:T(8,128)(2,1)S(1)} collective-permute-done((bf16[1024,128]{1,0:T(8,128)(2,1)S(1)}, bf16[1024,128]{1,0:T(8,128)(2,1)S(1)}, u32[]{:S(2)}, u32[]{:S(2)}) %collective-permute-start.18) | collective-permute-done | bytes 262176 | tf_op jit(solution)/shard_map/ppermute | solution.py:275
  91.3 1.8 %collective-permute-start.19 = (bf16[1024,128]{1,0:T(8,128)(2,1)S(1)}, bf16[1024,128]{1,0:T(8,128)(2,1)S(1)}, u32[]{:S(2)}, u32[]{:S(2)}) collective-permute-start(bf16[1024,128]{1,0:T(8,128)(2,1)S(1)} %get-tuple-element.128), channel_id=1, source_target_pairs={{0,6},{2,0},{4,2},{6,4},{1,7},{3,1},{5,3},{7,5},{8,14},{10,8},{12,... | collective-permute-start | bytes 786440 | tf_op jit(solution)/shard_map/ppermute | solution.py:275
  93.1 1.2 back.4
  94.4 1.9 %collective-permute-done.25.refs_1_ = bf16[1024,128]{1,0:T(8,128)(2,1)S(1)} collective-permute-done((bf16[1024,128]{1,0:T(8,128)(2,1)S(1)}, bf16[1024,128]{1,0:T(8,128)(2,1)S(1)}, u32[]{:S(2)}, u32[]{:S(2)}) %collective-permute-start.25) | collective-permute-done | bytes 262176 | tf_op jit(solution)/shard_map/ppermute | solution.py:275
  96.9 2.2 %collective-permute-start.26 = (bf16[1024,128]{1,0:T(8,128)(2,1)S(1)}, bf16[1024,128]{1,0:T(8,128)(2,1)S(1)}, u32[]{:S(2)}, u32[]{:S(2)}) collective-permute-start(bf16[1024,128]{1,0:T(8,128)(2,1)S(1)} %get-tuple-element.139), channel_id=1, source_target_pairs={{0,6},{2,0},{4,2},{6,4},{1,7},{3,1},{5,3},{7,5},{8,14},{10,8},{12,... | collective-permute-start | bytes 786440 | tf_op jit(solution)/shard_map/ppermute | solution.py:275
  99.2 2.8 %collective-permute-done.19.refs_1_ = bf16[1024,128]{1,0:T(8,128)(2,1)S(1)} collective-permute-done((bf16[1024,128]{1,0:T(8,128)(2,1)S(1)}, bf16[1024,128]{1,0:T(8,128)(2,1)S(1)}, u32[]{:S(2)}, u32[]{:S(2)}) %collective-permute-start.19) | collective-permute-done | bytes 262176 | tf_op jit(solution)/shard_map/ppermute | solution.py:275
  102.6 2.2 %collective-permute-start.20 = (bf16[1024,128]{1,0:T(8,128)(2,1)S(1)}, bf16[1024,128]{1,0:T(8,128)(2,1)S(1)}, u32[]{:S(2)}, u32[]{:S(2)}) collective-permute-start(bf16[1024,128]{1,0:T(8,128)(2,1)S(1)} %get-tuple-element.129), channel_id=1, source_target_pairs={{0,6},{2,0},{4,2},{6,4},{1,7},{3,1},{5,3},{7,5},{8,14},{10,8},{12,... | collective-permute-start | bytes 786440 | tf_op jit(solution)/shard_map/ppermute | solution.py:275
  104.8 1.2 back.3
  106.0 1.5 %collective-permute-done.26.refs_4_ = bf16[1024,128]{1,0:T(8,128)(2,1)S(1)} collective-permute-done((bf16[1024,128]{1,0:T(8,128)(2,1)S(1)}, bf16[1024,128]{1,0:T(8,128)(2,1)S(1)}, u32[]{:S(2)}, u32[]{:S(2)}) %collective-permute-start.26) | collective-permute-done | bytes 262176 | tf_op jit(solution)/shard_map/ppermute | solution.py:275
  107.5 1.3 grad.3
  108.8 1.2 collective-permute-start.27
  110.4 2.0 %collective-permute-start.29 = (bf16[256,128]{1,0:T(8,128)(2,1)S(1)}, bf16[256,128]{1,0:T(8,128)(2,1)S(1)}, u32[]{:S(2)}, u32[]{:S(2)}) collective-permute-start(bf16[256,128]{1,0:T(8,128)(2,1)S(1)} %get-tuple-element.143), channel_id=1, source_target_pairs={{0,24},{8,16},{16,8},{24,0},{1,25},{9,17},{17,9},{25,1},{2,26},{10... | collective-permute-start | bytes 196616 | tf_op jit(solution)/shard_map/ppermute | solution.py:272
  112.4 1.3 grad.2
  113.7 1.2 collective-permute-start.21
  115.2 2.0 %collective-permute-start.23 = (bf16[256,128]{1,0:T(8,128)(2,1)S(1)}, bf16[256,128]{1,0:T(8,128)(2,1)S(1)}, u32[]{:S(2)}, u32[]{:S(2)}) collective-permute-start(bf16[256,128]{1,0:T(8,128)(2,1)S(1)} %get-tuple-element.133), channel_id=1, source_target_pairs={{0,24},{8,16},{16,8},{24,0},{1,25},{9,17},{17,9},{25,1},{2,26},{10... | collective-permute-start | bytes 196616 | tf_op jit(solution)/shard_map/ppermute | solution.py:272
  119.1 1.3 collective-permute-done.23.refs_3_
  120.6 5.3 %collective-permute-done.30.refs_1_ = bf16[256,256]{1,0:T(8,128)(2,1)S(1)} collective-permute-done((bf16[256,256]{1,0:T(8,128)(2,1)S(1)}, bf16[256,256]{1,0:T(8,128)(2,1)S(1)}, u32[]{:S(2)}, u32[]{:S(2)}) %collective-permute-start.30) | collective-permute-done | bytes 131104 | tf_op jit(solution)/shard_map/ppermute | solution.py:436
  126.2 6.1 %collective-permute-done.31.refs_1_ = bf16[256,256]{1,0:T(8,128)(2,1)S(1)} collective-permute-done((bf16[256,256]{1,0:T(8,128)(2,1)S(1)}, bf16[256,256]{1,0:T(8,128)(2,1)S(1)}, u32[]{:S(2)}, u32[]{:S(2)}) %collective-permute-start.31) | collective-permute-done | bytes 131104 | tf_op jit(solution)/shard_map/ppermute | solution.py:436
  132.4 1.4 collective-permute-start.32
  133.8 1.2 collective-permute-start.33
  135.9 1.5 %collective-permute-done.32.refs_2_ = bf16[256,256]{1,0:T(8,128)(2,1)S(1)} collective-permute-done((bf16[256,256]{1,0:T(8,128)(2,1)S(1)}, bf16[256,256]{1,0:T(8,128)(2,1)S(1)}, u32[]{:S(2)}, u32[]{:S(2)}) %collective-permute-start.32) | collective-permute-done | bytes 131104 | tf_op jit(solution)/shard_map/ppermute | solution.py:272
  137.4 1.4 collective-permute-done.33.refs_3_
  138.8 2.1 %collective-permute-done.34.refs_4_ = bf16[256,256]{1,0:T(8,128)(2,1)S(1)} collective-permute-done((bf16[256,256]{1,0:T(8,128)(2,1)S(1)}, bf16[256,256]{1,0:T(8,128)(2,1)S(1)}, u32[]{:S(2)}, u32[]{:S(2)}) %collective-permute-start.34) | collective-permute-done | bytes 131104 | tf_op jit(solution)/shard_map/ppermute | solution.py:272
  142.2 1.9 %last.1 = f32[1024,512]{1,0:T(8,128)} custom-call(s32[3]{0:T(128)S(1)} %pad_add_fusion.refs_0_, bf16[256,256]{1,0:T(8,128)(2,1)S(1)} %sum.3.refs_1_, bf16[256,256]{1,0:T(8,128)(2,1)S(1)} %collective-permute-done.32.refs_2_, bf16[256,256]{1,0:T(8,128)(2,1)S(1)} %collective-permute-done.33.refs_3_, bf16[256,256]{1,0:T(8,128)(2,1)S(1)} %collective-permute-done.34.refs_4_, ...), custom_call_target="tpu_custom_call" | custom-call | flops 200000000 | tf_op jit(solution)/shard_map/last/pallas_call | solution.py:52
  (80 shorter events, 19.9 us)
Async XLA Ops:
  0.6 35.8 %collective-permute-start.5 = (bf16[4,16,128,128]{3,2,1,0:T(8,128)(2,1)}, bf16[4,16,128,128]{3,2,1,0:T(8,128)(2,1)S(1)}, u32[]{:S(2)}, u32[]{:S(2)}) collective-permute-start(bf16[4,16,128,128]{3,2,1,0:T(8,128)(2,1)} %refs_3_.1), channel_id=1, source_target_pairs={{0,1},{1,0},{2,3},{3,2},{4,5},{5,4},{6,7},{7,6},{8,9},{9,8},{10,11... | collective-permute-start | bytes 6291464 | tf_op jit(solution)/shard_map/ppermute | solution.py:269
  3.7 15.1 %all-to-all-start = ((s32[32,8,128]{2,1,0:T(8,128)}), s32[32,8,128]{2,1,0:T(8,128)S(1)}, u32[]{:S(2)}, u32[]{:S(2)}) async-start(s32[32,8,128]{2,1,0:T(8,128)} %index.1), calls=%async_computation | async-start | bytes 262144 | tf_op jit(solution)/shard_map/all_to_all | solution.py:285
  10.6 1.2 copy-start.1
  11.9 1.2 copy-start.5
  14.4 0.7 copy-start.3
  15.1 10.9 %copy-start.2 = (bf16[512,1024]{1,0:T(8,128)(2,1)S(1)}, bf16[512,1024]{1,0:T(8,128)(2,1)}, u32[]{:S(2)}) copy-start(bf16[512,1024]{1,0:T(8,128)(2,1)} %refs_1_.1) | copy-start | bytes 3145732
  18.8 1.0 copy-start.4
  19.8 13.5 %copy-start.7 = (s32[4,16]{1,0:T(4,128)S(1)}, s32[4,16]{1,0:T(4,128)}, u32[]{:S(2)}) copy-start(s32[4,16]{1,0:T(4,128)} %param.9) | copy-start | bytes 772
  19.8 13.5 %copy-start.8 = (s32[4]{0:T(128)S(1)}, s32[4]{0:T(128)}, u32[]{:S(2)}) copy-start(s32[4]{0:T(128)} %param.10) | copy-start | bytes 52
  19.8 17.5 %copy-start = (bf16[4,16,128,128]{3,2,1,0:T(8,128)(2,1)S(1)}, bf16[4,16,128,128]{3,2,1,0:T(8,128)(2,1)}, u32[]{:S(2)}) copy-start(bf16[4,16,128,128]{3,2,1,0:T(8,128)(2,1)} %refs_3_.1) | copy-start | bytes 6291460
  22.1 3.9 %collective-permute-start.3 = (bf16[512,256]{1,0:T(8,128)(2,1)S(1)}, bf16[512,256]{1,0:T(8,128)(2,1)S(1)}, u32[]{:S(2)}, u32[]{:S(2)}) collective-permute-start(bf16[512,256]{1,0:T(8,128)(2,1)S(1)} %get-tuple-element.146), channel_id=1, source_target_pairs={{0,1},{1,0},{2,3},{3,2},{4,5},{5,4},{6,7},{7,6},{8,9},{9,8},{10,11... | collective-permute-start | bytes 786440 | tf_op jit(solution)/shard_map/ppermute | solution.py:269
  22.4 6.3 %collective-permute-start = (bf16[2,128,256]{2,1,0:T(8,128)(2,1)S(1)}, bf16[2,128,256]{2,1,0:T(8,128)(2,1)S(1)}, u32[]{:S(2)}, u32[]{:S(2)}) collective-permute-start(bf16[2,128,256]{2,1,0:T(8,128)(2,1)S(1)} %get-tuple-element.80), channel_id=1, source_target_pairs={{0,8},{8,0},{16,24},{24,16},{1,9},{9,1},{17,25},{25,17},{2,10},{10... | collective-permute-start | bytes 393224 | tf_op jit(solution)/shard_map/ppermute | solution.py:272
  23.0 8.4 %collective-permute-start.1 = (bf16[2,128,256]{2,1,0:T(8,128)(2,1)S(1)}, bf16[2,128,256]{2,1,0:T(8,128)(2,1)S(1)}, u32[]{:S(2)}, u32[]{:S(2)}) collective-permute-start(bf16[2,128,256]{2,1,0:T(8,128)(2,1)S(1)} %get-tuple-element.81), channel_id=1, source_target_pairs={{0,16},{8,24},{16,0},{24,8},{1,17},{9,25},{17,1},{25,9},{2,18},{10... | collective-permute-start | bytes 393224 | tf_op jit(solution)/shard_map/ppermute | solution.py:272
  23.8 7.7 %collective-permute-start.2 = (bf16[2,128,256]{2,1,0:T(8,128)(2,1)S(1)}, bf16[2,128,256]{2,1,0:T(8,128)(2,1)S(1)}, u32[]{:S(2)}, u32[]{:S(2)}) collective-permute-start(bf16[2,128,256]{2,1,0:T(8,128)(2,1)S(1)} %get-tuple-element.82), channel_id=1, source_target_pairs={{0,24},{8,16},{16,8},{24,0},{1,25},{9,17},{17,9},{25,1},{2,26},{10... | collective-permute-start | bytes 393224 | tf_op jit(solution)/shard_map/ppermute | solution.py:272
  31.4 1.6 %collective-permute-start.6 = (bf16[512,256]{1,0:T(8,128)(2,1)S(1)}, bf16[512,256]{1,0:T(8,128)(2,1)S(1)}, u32[]{:S(2)}, u32[]{:S(2)}) collective-permute-start(bf16[512,256]{1,0:T(8,128)(2,1)S(1)} %get-tuple-element.89), channel_id=1, source_target_pairs={{0,1},{1,0},{2,3},{3,2},{4,5},{5,4},{6,7},{7,6},{8,9},{9,8},{10,11... | collective-permute-start | bytes 786440 | tf_op jit(solution)/shard_map/ppermute | solution.py:269
  31.5 11.6 %collective-permute-start.8 = (bf16[512,256]{1,0:T(8,128)(2,1)S(1)}, bf16[512,256]{1,0:T(8,128)(2,1)S(1)}, u32[]{:S(2)}, u32[]{:S(2)}) collective-permute-start(bf16[512,256]{1,0:T(8,128)(2,1)S(1)} %get-tuple-element.90.refs_2_), channel_id=1, source_target_pairs={{0,2},{2,4},{4,6},{6,0},{1,3},{3,5},{5,7},{7,1},{8,10},{10,12},{12... | collective-permute-start | bytes 786440 | tf_op jit(solution)/shard_map/ppermute | solution.py:275
  33.1 15.0 %collective-permute-start.7 = (bf16[512,256]{1,0:T(8,128)(2,1)S(1)}, bf16[512,256]{1,0:T(8,128)(2,1)S(1)}, u32[]{:S(2)}, u32[]{:S(2)}) collective-permute-start(bf16[512,256]{1,0:T(8,128)(2,1)S(1)} %collective-permute-done.6.refs_3_), channel_id=1, source_target_pairs={{0,2},{2,4},{4,6},{6,0},{1,3},{3,5},{5,7},{7,1},{8,10},{10,12},{12... | collective-permute-start | bytes 786440 | tf_op jit(solution)/shard_map/ppermute | solution.py:275
  33.3 1.4 collective-permute-start.4
  33.3 14.7 %collective-permute-start.10 = (bf16[128,1024]{1,0:T(8,128)(2,1)S(1)}, bf16[128,1024]{1,0:T(8,128)(2,1)S(1)}, u32[]{:S(2)}, u32[]{:S(2)}) collective-permute-start(bf16[128,1024]{1,0:T(8,128)(2,1)S(1)} %get-tuple-element.96), channel_id=1, source_target_pairs={{0,16},{8,24},{16,0},{24,8},{1,17},{9,25},{17,1},{25,9},{2,18},{10... | collective-permute-start | bytes 786440 | tf_op jit(solution)/shard_map/ppermute | solution.py:272
  34.7 13.3 %collective-permute-start.11 = (bf16[128,1024]{1,0:T(8,128)(2,1)S(1)}, bf16[128,1024]{1,0:T(8,128)(2,1)S(1)}, u32[]{:S(2)}, u32[]{:S(2)}) collective-permute-start(bf16[128,1024]{1,0:T(8,128)(2,1)S(1)} %get-tuple-element.97), channel_id=1, source_target_pairs={{0,24},{8,16},{16,8},{24,0},{1,25},{9,17},{17,9},{25,1},{2,26},{10... | collective-permute-start | bytes 786440 | tf_op jit(solution)/shard_map/ppermute | solution.py:272
  36.4 12.8 %collective-permute-start.9 = (bf16[128,1024]{1,0:T(8,128)(2,1)S(1)}, bf16[128,1024]{1,0:T(8,128)(2,1)S(1)}, u32[]{:S(2)}, u32[]{:S(2)}) collective-permute-start(bf16[128,1024]{1,0:T(8,128)(2,1)S(1)} %get-tuple-element.95), channel_id=1, source_target_pairs={{0,8},{8,0},{16,24},{24,16},{1,9},{9,1},{17,25},{25,17},{2,10},{10... | collective-permute-start | bytes 786440 | tf_op jit(solution)/shard_map/ppermute | solution.py:272
  43.2 12.3 %collective-permute-start.12 = (bf16[512,256]{1,0:T(8,128)(2,1)S(1)}, bf16[512,256]{1,0:T(8,128)(2,1)S(1)}, u32[]{:S(2)}, u32[]{:S(2)}) collective-permute-start(bf16[512,256]{1,0:T(8,128)(2,1)S(1)} %collective-permute-done.8.refs_2_), channel_id=1, source_target_pairs={{0,2},{2,4},{4,6},{6,0},{1,3},{3,5},{5,7},{7,1},{8,10},{10,12},{12... | collective-permute-start | bytes 786440 | tf_op jit(solution)/shard_map/ppermute | solution.py:275
  48.0 10.9 %collective-permute-start.14 = (bf16[512,256]{1,0:T(8,128)(2,1)S(1)}, bf16[512,256]{1,0:T(8,128)(2,1)S(1)}, u32[]{:S(2)}, u32[]{:S(2)}) collective-permute-start(bf16[512,256]{1,0:T(8,128)(2,1)S(1)} %collective-permute-done.7.refs_3_), channel_id=1, source_target_pairs={{0,2},{2,4},{4,6},{6,0},{1,3},{3,5},{5,7},{7,1},{8,10},{10,12},{12... | collective-permute-start | bytes 786440 | tf_op jit(solution)/shard_map/ppermute | solution.py:275
  58.9 11.0 %collective-permute-start.15 = (bf16[512,256]{1,0:T(8,128)(2,1)S(1)}, bf16[512,256]{1,0:T(8,128)(2,1)S(1)}, u32[]{:S(2)}, u32[]{:S(2)}) collective-permute-start(bf16[512,256]{1,0:T(8,128)(2,1)S(1)} %collective-permute-done.14.refs_3_), channel_id=1, source_target_pairs={{0,2},{2,4},{4,6},{6,0},{1,3},{3,5},{5,7},{7,1},{8,10},{10,12},{12... | collective-permute-start | bytes 786440 | tf_op jit(solution)/shard_map/ppermute | solution.py:275
  58.9 14.8 %collective-permute-start.13 = (bf16[512,256]{1,0:T(8,128)(2,1)S(1)}, bf16[512,256]{1,0:T(8,128)(2,1)S(1)}, u32[]{:S(2)}, u32[]{:S(2)}) collective-permute-start(bf16[512,256]{1,0:T(8,128)(2,1)S(1)} %collective-permute-done.12.refs_2_), channel_id=1, source_target_pairs={{0,2},{2,4},{4,6},{6,0},{1,3},{3,5},{5,7},{7,1},{8,10},{10,12},{12... | collective-permute-start | bytes 786440 | tf_op jit(solution)/shard_map/ppermute | solution.py:275
  59.6 46.4 %collective-permute-start.17 = (bf16[1024,512]{1,0:T(8,128)(2,1)S(1)}, bf16[1024,512]{1,0:T(8,128)(2,1)S(1)}, u32[]{:S(2)}, u32[]{:S(2)}) collective-permute-start(bf16[1024,512]{1,0:T(8,128)(2,1)S(1)} %get-tuple-element.121.refs_1_), channel_id=1, source_target_pairs={{0,1},{1,0},{2,3},{3,2},{4,5},{5,4},{6,7},{7,6},{8,9},{9,8},{10,11... | collective-permute-start | bytes 3145736 | tf_op jit(solution)/shard_map/ppermute | solution.py:269
  75.8 9.3 %collective-permute-start.24 = (bf16[1024,128]{1,0:T(8,128)(2,1)S(1)}, bf16[1024,128]{1,0:T(8,128)(2,1)S(1)}, u32[]{:S(2)}, u32[]{:S(2)}) collective-permute-start(bf16[1024,128]{1,0:T(8,128)(2,1)S(1)} %get-tuple-element.137), channel_id=1, source_target_pairs={{0,6},{2,0},{4,2},{6,4},{1,7},{3,1},{5,3},{7,5},{8,14},{10,8},{12,... | collective-permute-start | bytes 786440 | tf_op jit(solution)/shard_map/ppermute | solution.py:275
  75.9 14.8 %collective-permute-start.18 = (bf16[1024,128]{1,0:T(8,128)(2,1)S(1)}, bf16[1024,128]{1,0:T(8,128)(2,1)S(1)}, u32[]{:S(2)}, u32[]{:S(2)}) collective-permute-start(bf16[1024,128]{1,0:T(8,128)(2,1)S(1)} %get-tuple-element.127), channel_id=1, source_target_pairs={{0,6},{2,0},{4,2},{6,4},{1,7},{3,1},{5,3},{7,5},{8,14},{10,8},{12,... | collective-permute-start | bytes 786440 | tf_op jit(solution)/shard_map/ppermute | solution.py:275
  75.9 18.5 %collective-permute-start.16 = (bf16[512,256]{1,0:T(8,128)(2,1)S(1)}, bf16[512,256]{1,0:T(8,128)(2,1)S(1)}, u32[]{:S(2)}, u32[]{:S(2)}) collective-permute-start(bf16[512,256]{1,0:T(8,128)(2,1)S(1)} %get-tuple-element.120), channel_id=1, source_target_pairs={{0,1},{1,0},{2,3},{3,2},{4,5},{5,4},{6,7},{7,6},{8,9},{9,8},{10,11... | collective-permute-start | bytes 786440 | tf_op jit(solution)/shard_map/ppermute | solution.py:269
  85.7 10.6 %collective-permute-start.25 = (bf16[1024,128]{1,0:T(8,128)(2,1)S(1)}, bf16[1024,128]{1,0:T(8,128)(2,1)S(1)}, u32[]{:S(2)}, u32[]{:S(2)}) collective-permute-start(bf16[1024,128]{1,0:T(8,128)(2,1)S(1)} %get-tuple-element.138), channel_id=1, source_target_pairs={{0,6},{2,0},{4,2},{6,4},{1,7},{3,1},{5,3},{7,5},{8,14},{10,8},{12,... | collective-permute-start | bytes 786440 | tf_op jit(solution)/shard_map/ppermute | solution.py:275
  91.3 10.6 %collective-permute-start.19 = (bf16[1024,128]{1,0:T(8,128)(2,1)S(1)}, bf16[1024,128]{1,0:T(8,128)(2,1)S(1)}, u32[]{:S(2)}, u32[]{:S(2)}) collective-permute-start(bf16[1024,128]{1,0:T(8,128)(2,1)S(1)} %get-tuple-element.128), channel_id=1, source_target_pairs={{0,6},{2,0},{4,2},{6,4},{1,7},{3,1},{5,3},{7,5},{8,14},{10,8},{12,... | collective-permute-start | bytes 786440 | tf_op jit(solution)/shard_map/ppermute | solution.py:275
  96.9 10.6 %collective-permute-start.26 = (bf16[1024,128]{1,0:T(8,128)(2,1)S(1)}, bf16[1024,128]{1,0:T(8,128)(2,1)S(1)}, u32[]{:S(2)}, u32[]{:S(2)}) collective-permute-start(bf16[1024,128]{1,0:T(8,128)(2,1)S(1)} %get-tuple-element.139), channel_id=1, source_target_pairs={{0,6},{2,0},{4,2},{6,4},{1,7},{3,1},{5,3},{7,5},{8,14},{10,8},{12,... | collective-permute-start | bytes 786440 | tf_op jit(solution)/shard_map/ppermute | solution.py:275
  102.6 9.8 %collective-permute-start.20 = (bf16[1024,128]{1,0:T(8,128)(2,1)S(1)}, bf16[1024,128]{1,0:T(8,128)(2,1)S(1)}, u32[]{:S(2)}, u32[]{:S(2)}) collective-permute-start(bf16[1024,128]{1,0:T(8,128)(2,1)S(1)} %get-tuple-element.129), channel_id=1, source_target_pairs={{0,6},{2,0},{4,2},{6,4},{1,7},{3,1},{5,3},{7,5},{8,14},{10,8},{12,... | collective-permute-start | bytes 786440 | tf_op jit(solution)/shard_map/ppermute | solution.py:275
  108.8 6.4 %collective-permute-start.27 = (bf16[256,128]{1,0:T(8,128)(2,1)S(1)}, bf16[256,128]{1,0:T(8,128)(2,1)S(1)}, u32[]{:S(2)}, u32[]{:S(2)}) collective-permute-start(bf16[256,128]{1,0:T(8,128)(2,1)S(1)} %get-tuple-element.141), channel_id=1, source_target_pairs={{0,8},{8,0},{16,24},{24,16},{1,9},{9,1},{17,25},{25,17},{2,10},{10... | collective-permute-start | bytes 196616 | tf_op jit(solution)/shard_map/ppermute | solution.py:272
  110.0 7.2 %collective-permute-start.28 = (bf16[256,128]{1,0:T(8,128)(2,1)S(1)}, bf16[256,128]{1,0:T(8,128)(2,1)S(1)}, u32[]{:S(2)}, u32[]{:S(2)}) collective-permute-start(bf16[256,128]{1,0:T(8,128)(2,1)S(1)} %get-tuple-element.142), channel_id=1, source_target_pairs={{0,16},{8,24},{16,0},{24,8},{1,17},{9,25},{17,1},{25,9},{2,18},{10... | collective-permute-start | bytes 196616 | tf_op jit(solution)/shard_map/ppermute | solution.py:272
  110.4 6.8 %collective-permute-start.29 = (bf16[256,128]{1,0:T(8,128)(2,1)S(1)}, bf16[256,128]{1,0:T(8,128)(2,1)S(1)}, u32[]{:S(2)}, u32[]{:S(2)}) collective-permute-start(bf16[256,128]{1,0:T(8,128)(2,1)S(1)} %get-tuple-element.143), channel_id=1, source_target_pairs={{0,24},{8,16},{16,8},{24,0},{1,25},{9,17},{17,9},{25,1},{2,26},{10... | collective-permute-start | bytes 196616 | tf_op jit(solution)/shard_map/ppermute | solution.py:272
  113.7 4.3 %collective-permute-start.21 = (bf16[256,128]{1,0:T(8,128)(2,1)S(1)}, bf16[256,128]{1,0:T(8,128)(2,1)S(1)}, u32[]{:S(2)}, u32[]{:S(2)}) collective-permute-start(bf16[256,128]{1,0:T(8,128)(2,1)S(1)} %get-tuple-element.131), channel_id=1, source_target_pairs={{0,8},{8,0},{16,24},{24,16},{1,9},{9,1},{17,25},{25,17},{2,10},{10... | collective-permute-start | bytes 196616 | tf_op jit(solution)/shard_map/ppermute | solution.py:272
  114.8 4.3 %collective-permute-start.22 = (bf16[256,128]{1,0:T(8,128)(2,1)S(1)}, bf16[256,128]{1,0:T(8,128)(2,1)S(1)}, u32[]{:S(2)}, u32[]{:S(2)}) collective-permute-start(bf16[256,128]{1,0:T(8,128)(2,1)S(1)} %get-tuple-element.132), channel_id=1, source_target_pairs={{0,16},{8,24},{16,0},{24,8},{1,17},{9,25},{17,1},{25,9},{2,18},{10... | collective-permute-start | bytes 196616 | tf_op jit(solution)/shard_map/ppermute | solution.py:272
  115.2 5.2 %collective-permute-start.23 = (bf16[256,128]{1,0:T(8,128)(2,1)S(1)}, bf16[256,128]{1,0:T(8,128)(2,1)S(1)}, u32[]{:S(2)}, u32[]{:S(2)}) collective-permute-start(bf16[256,128]{1,0:T(8,128)(2,1)S(1)} %get-tuple-element.133), channel_id=1, source_target_pairs={{0,24},{8,16},{16,8},{24,0},{1,25},{9,17},{17,9},{25,1},{2,26},{10... | collective-permute-start | bytes 196616 | tf_op jit(solution)/shard_map/ppermute | solution.py:272
  120.5 5.4 %collective-permute-start.30 = (bf16[256,256]{1,0:T(8,128)(2,1)S(1)}, bf16[256,256]{1,0:T(8,128)(2,1)S(1)}, u32[]{:S(2)}, u32[]{:S(2)}) collective-permute-start(bf16[256,256]{1,0:T(8,128)(2,1)S(1)} %merge.1.refs_0_), channel_id=1, source_target_pairs={{0,2},{2,0},{4,6},{6,4},{1,3},{3,1},{5,7},{7,5},{8,10},{10,8},{12,... | collective-permute-start | bytes 393224 | tf_op jit(solution)/shard_map/ppermute | solution.py:436
  125.9 6.4 %collective-permute-start.31 = (bf16[256,256]{1,0:T(8,128)(2,1)S(1)}, bf16[256,256]{1,0:T(8,128)(2,1)S(1)}, u32[]{:S(2)}, u32[]{:S(2)}) collective-permute-start(bf16[256,256]{1,0:T(8,128)(2,1)S(1)} %sum.2.refs_0_), channel_id=1, source_target_pairs={{0,4},{2,6},{4,0},{6,2},{1,5},{3,7},{5,1},{7,3},{8,12},{10,14},{12... | collective-permute-start | bytes 393224 | tf_op jit(solution)/shard_map/ppermute | solution.py:436
  132.4 5.0 %collective-permute-start.32 = (bf16[256,256]{1,0:T(8,128)(2,1)S(1)}, bf16[256,256]{1,0:T(8,128)(2,1)S(1)}, u32[]{:S(2)}, u32[]{:S(2)}) collective-permute-start(bf16[256,256]{1,0:T(8,128)(2,1)S(1)} %sum.3.refs_1_), channel_id=1, source_target_pairs={{0,8},{8,0},{16,24},{24,16},{1,9},{9,1},{17,25},{25,17},{2,10},{10... | collective-permute-start | bytes 393224 | tf_op jit(solution)/shard_map/ppermute | solution.py:272
  133.8 5.0 %collective-permute-start.33 = (bf16[256,256]{1,0:T(8,128)(2,1)S(1)}, bf16[256,256]{1,0:T(8,128)(2,1)S(1)}, u32[]{:S(2)}, u32[]{:S(2)}) collective-permute-start(bf16[256,256]{1,0:T(8,128)(2,1)S(1)} %sum.3.refs_1_), channel_id=1, source_target_pairs={{0,16},{8,24},{16,0},{24,8},{1,17},{9,25},{17,1},{25,9},{2,18},{10... | collective-permute-start | bytes 393224 | tf_op jit(solution)/shard_map/ppermute | solution.py:272
  135.0 5.9 %collective-permute-start.34 = (bf16[256,256]{1,0:T(8,128)(2,1)S(1)}, bf16[256,256]{1,0:T(8,128)(2,1)S(1)}, u32[]{:S(2)}, u32[]{:S(2)}) collective-permute-start(bf16[256,256]{1,0:T(8,128)(2,1)S(1)} %sum.3.refs_1_), channel_id=1, source_target_pairs={{0,24},{8,16},{16,8},{24,0},{1,25},{9,17},{17,9},{25,1},{2,26},{10... | collective-permute-start | bytes 393224 | tf_op jit(solution)/shard_map/ppermute | solution.py:272
  135.9 5.8 %collective-permute-start.35 = (bf16[256,256]{1,0:T(8,128)(2,1)S(1)}, bf16[256,256]{1,0:T(8,128)(2,1)S(1)}, u32[]{:S(2)}, u32[]{:S(2)}) collective-permute-start(bf16[256,256]{1,0:T(8,128)(2,1)S(1)} %sum.3.refs_1_), channel_id=1, source_target_pairs={{0,1},{1,0},{2,3},{3,2},{4,5},{5,4},{6,7},{7,6},{8,9},{9,8},{10,11... | collective-permute-start | bytes 393224 | tf_op jit(solution)/shard_map/ppermute | solution.py:269
  137.4 4.3 %collective-permute-start.36 = (bf16[256,256]{1,0:T(8,128)(2,1)S(1)}, bf16[256,256]{1,0:T(8,128)(2,1)S(1)}, u32[]{:S(2)}, u32[]{:S(2)}) collective-permute-start(bf16[256,256]{1,0:T(8,128)(2,1)S(1)} %collective-permute-done.32.refs_2_), channel_id=1, source_target_pairs={{0,1},{1,0},{2,3},{3,2},{4,5},{5,4},{6,7},{7,6},{8,9},{9,8},{10,11... | collective-permute-start | bytes 393224 | tf_op jit(solution)/shard_map/ppermute | solution.py:269
  138.8 3.0 %collective-permute-start.37 = (bf16[256,256]{1,0:T(8,128)(2,1)S(1)}, bf16[256,256]{1,0:T(8,128)(2,1)S(1)}, u32[]{:S(2)}, u32[]{:S(2)}) collective-permute-start(bf16[256,256]{1,0:T(8,128)(2,1)S(1)} %collective-permute-done.33.refs_3_), channel_id=1, source_target_pairs={{0,1},{1,0},{2,3},{3,2},{4,5},{5,4},{6,7},{7,6},{8,9},{9,8},{10,11... | collective-permute-start | bytes 393224 | tf_op jit(solution)/shard_map/ppermute | solution.py:269
  140.8 1.3 collective-permute-start.38
  (1 other events, 0.7 us)

commit v15 on v13

--- a/solution.py
+++ b/solution.py
@@ -13,6 +13,13 @@
 def log2(n):
     assert n & (n - 1) == 0
     return n.bit_length() - 1
+
+
+def place_of(at, count):
+    place = at
+    for shift in range(1, log2(count)):
+        place = place ^ (at >> shift)
+    return place
 
 
 def iota(shape, dim):
@@ -162,7 +169,8 @@
         slot = jnp.concatenate([message[1 + i:2 + i, :] for i in range(z.rows // 128)], axis=1)
         rank, at = slot & (z.pair - 1), slot >> log2(z.pair)
         s, at = at & (z.grp - 1), at >> log2(z.grp)
-        k, rel = (me_ref[1] - (at >> 1)) & (z.zz - 1), (at & 1) ^ me_ref[2]
+        k = (place_of(me_ref[1], z.zz) - place_of(at >> 1, z.zz)) & (z.zz - 1)
+        rel = (at & 1) ^ me_ref[2]
         slot = ((k * 2 + rel) * z.grp + s) * z.pair + rank
         place = one_hot(iota((z.rows, z.rows), 0) == slot)
         at = pl.multiple_of(n * z.rows, z.rows)
@@ -258,7 +266,8 @@
         return lax.ppermute(x, "grp", [(i, i ^ s) for i in range(z.grp)]) if s else x
 
     def to_zz(x, k):
-        return lax.ppermute(x, "zz", [(i, (i + k) % z.zz) for i in range(z.zz)]) if k else x
+        order = [i ^ (i >> 1) for i in range(z.zz)]
+        return lax.ppermute(x, "zz", [(order[i], order[(i + k) % z.zz]) for i in range(z.zz)])
 
     first_half = features[:rows // 2]
     (message,) = call(

time: 140 us -> 138 us (0.986)
  waiting for transfers between devices: 61.8 us -> 57.7 us
  starting transfers between devices: 42.3 us -> 44.3 us
    ppermute x2, waiting for transfers between devices: 12.1 us -> 7.75 us  [shards(): lax.ppermute(mine, 'zz', [(i, i ^ step) for i in range(z.zz)])]
    ppermute x12, starting transfers between devices: 18.3 us -> 16.1 us  [to_zz(): lax.ppermute(x, 'zz', [(order[i], order[(i + k) % z.zz]) for i in range(z...]
    ppermute x12, starting transfers between devices: 14.5 us -> 16.5 us  [to_grp(): lax.ppermute(x, 'grp', [(i, i ^ s) for i in range(z.grp)])]
    ppermute x2, starting transfers between devices: 1.62 us -> 3.33 us  [shards(): lax.ppermute(mine, 'zz', [(i, i ^ step) for i in range(z.zz)])]
  transfers between devices with their start and end apart: 37 -> 37, of which waited for: 23 -> 21; matrix products, arithmetic and copies ran while one was open for 1% -> 1% of each run, Pallas kernels for 18% -> 19%
where the time goes in v15:
time: 138 us; the launch traced here: 137 us
  waiting for transfers between devices  57.7 us (42%)
  starting transfers between devices  44.3 us (32%)
  Pallas kernels  30.1 us (22%)
  local copies, waits for them, and re-layouts  3.19 us (2%)
    ppermute x12, waiting for transfers between devices, to_zz(): lax.ppermute(x, 'zz', [(order[i], order[(i + k) % z.zz]) for i in range(z...  31.2 us
    pallas_call x24, Pallas kernels, call(): pl.pallas_call(kernel, out_shape=tuple((jax.ShapeDtypeStruct(s, d) for s,...  30.1 us
    ppermute x12, starting transfers between devices, to_grp(): lax.ppermute(x, 'grp', [(i, i ^ s) for i in range(z.grp)])  16.5 us
    ppermute x12, starting transfers between devices, to_zz(): lax.ppermute(x, 'zz', [(order[i], order[(i + k) % z.zz]) for i in range(z...  16.1 us
    ppermute x12, waiting for transfers between devices, to_grp(): lax.ppermute(x, 'grp', [(i, i ^ s) for i in range(z.grp)])  14.2 us
    ppermute x2, waiting for transfers between devices, shards(): lax.ppermute(mine, 'zz', [(i, i ^ step) for i in range(z.zz)])  7.75 us
    all_to_all x1, starting transfers between devices, shards(): lax.all_to_all(message, ('grp', 'zz', 'core'), split_axis=0, concat_axis=...  6.96 us
    all_to_all x1, waiting for transfers between devices, shards(): lax.all_to_all(message, ('grp', 'zz', 'core'), split_axis=0, concat_axis=...  4.43 us
  transfers between devices with their start and end apart: 37, of which 21 were waited for; matrix products, arithmetic and copies ran while one was open for 1% of the time, Pallas kernels for 19%

profile of v15, /device:TPU:0, one launch (start us, length us, event | category | flops | bytes accessed | tf_op | source)
XLA Modules:
  0.0 137.2 jit_solution(9841347470181174277)
XLA Ops:
  1.9 1.8 %index.1 = s32[32,8,128]{2,1,0:T(8,128)} custom-call(s32[3]{0:T(128)S(1)} %pad_add_fusion.refs_0_, s32[1,512]{1,0:T(1,128)S(1)} %bitcast.4), custom_call_target="tpu_custom_call" | custom-call | flops 100000000 | tf_op jit(solution)/shard_map/index/pallas_call | solution.py:59
  3.7 7.0 %all-to-all-start = ((s32[32,8,128]{2,1,0:T(8,128)}), s32[32,8,128]{2,1,0:T(8,128)S(1)}, u32[]{:S(2)}, u32[]{:S(2)}) async-start(s32[32,8,128]{2,1,0:T(8,128)} %index.1), calls=%async_computation | async-start | bytes 262144 | tf_op jit(solution)/shard_map/all_to_all | solution.py:280
  10.6 1.2 copy-done
  11.9 1.2 copy-done.3
  13.1 1.2 product.1
  14.4 4.4 %all-to-all-done.refs_1_.refs_2_ = s32[32,8,128]{2,1,0:T(8,128)S(1)} async-done(((s32[32,8,128]{2,1,0:T(8,128)}), s32[32,8,128]{2,1,0:T(8,128)S(1)}, u32[]{:S(2)}, u32[]{:S(2)}) %all-to-all-start) | async-done | bytes 131104 | tf_op jit(solution)/shard_map/all_to_all | solution.py:280
  18.8 1.2 send.1
  20.0 0.9 collective-permute-start
  21.6 2.0 %collective-permute-start.2 = (bf16[2,128,256]{2,1,0:T(8,128)(2,1)S(1)}, bf16[2,128,256]{2,1,0:T(8,128)(2,1)S(1)}, u32[]{:S(2)}, u32[]{:S(2)}) collective-permute-start(bf16[2,128,256]{2,1,0:T(8,128)(2,1)S(1)} %get-tuple-element.77), channel_id=1, source_target_pairs={{0,24},{8,16},{16,8},{24,0},{1,25},{9,17},{17,9},{25,1},{2,26},{10... | collective-permute-start | bytes 393224 | tf_op jit(solution)/shard_map/ppermute | solution.py:266
  23.7 2.7 %collective-permute-done.refs_1_ = bf16[2,128,256]{2,1,0:T(8,128)(2,1)S(1)} collective-permute-done((bf16[2,128,256]{2,1,0:T(8,128)(2,1)S(1)}, bf16[2,128,256]{2,1,0:T(8,128)(2,1)S(1)}, u32[]{:S(2)}, u32[]{:S(2)}) %collective-permute-start) | collective-permute-done | bytes 131104 | tf_op jit(solution)/shard_map/ppermute | solution.py:266
  26.4 2.3 %collective-permute-done.1.refs_2_ = bf16[2,128,256]{2,1,0:T(8,128)(2,1)S(1)} collective-permute-done((bf16[2,128,256]{2,1,0:T(8,128)(2,1)S(1)}, bf16[2,128,256]{2,1,0:T(8,128)(2,1)S(1)}, u32[]{:S(2)}, u32[]{:S(2)}) %collective-permute-start.1) | collective-permute-done | bytes 131104 | tf_op jit(solution)/shard_map/ppermute | solution.py:266
  30.6 1.3 collective-permute-start.7
  31.8 5.9 %prepare.2 = (bf16[1024,512]{1,0:T(8,128)(2,1)S(1)}, bf16[1024,512]{1,0:T(8,128)(2,1)S(1)}, bf16[1024,512]{1,0:T(8,128)(2,1)S(1)}, bf16[1024,512]{1,0:T(8,128)(2,1)S(1)}, f32[8,128]{1,0:T(8,128)S(1)}) custom-call(s32[3]{0:T(128)S(1)} %pad_add_fusion.refs_0_, s32[4,16]{1,0:T(4,128)S(1)} %fusion.refs_1_, s32[32,8,128]{2,1,0:T(8,128)S(1)} %all-to-all-done.refs_1_.refs_2_, ...), custom_call_target="tpu_custom_call" | custom-call | flops 700000000 | tf_op jit(solution)/shard_map/prepare/pallas_call | solution.py:59
  37.7 1.2 collective-permute-done.8.refs_2_
  38.9 5.6 %collective-permute-done.7.refs_3_ = bf16[512,256]{1,0:T(8,128)(2,1)S(1)} collective-permute-done((bf16[512,256]{1,0:T(8,128)(2,1)S(1)}, bf16[512,256]{1,0:T(8,128)(2,1)S(1)}, u32[]{:S(2)}, u32[]{:S(2)}) %collective-permute-start.7) | collective-permute-done | bytes 262176 | tf_op jit(solution)/shard_map/ppermute | solution.py:270
  44.5 1.7 %collective-permute-start.13 = (bf16[128,1024]{1,0:T(8,128)(2,1)S(1)}, bf16[128,1024]{1,0:T(8,128)(2,1)S(1)}, u32[]{:S(2)}, u32[]{:S(2)}) collective-permute-start(bf16[128,1024]{1,0:T(8,128)(2,1)S(1)} %get-tuple-element.105), channel_id=1, source_target_pairs={{0,8},{8,0},{16,24},{24,16},{1,9},{9,1},{17,25},{25,17},{2,10},{10... | collective-permute-start | bytes 786440 | tf_op jit(solution)/shard_map/ppermute | solution.py:266
  46.7 3.4 %collective-permute-done.9.refs_2_ = bf16[512,256]{1,0:T(8,128)(2,1)S(1)} collective-permute-done((bf16[512,256]{1,0:T(8,128)(2,1)S(1)}, bf16[512,256]{1,0:T(8,128)(2,1)S(1)}, u32[]{:S(2)}, u32[]{:S(2)}) %collective-permute-start.9) | collective-permute-done | bytes 262176 | tf_op jit(solution)/shard_map/ppermute | solution.py:270
  50.1 1.6 %collective-permute-start.15 = (bf16[128,1024]{1,0:T(8,128)(2,1)S(1)}, bf16[128,1024]{1,0:T(8,128)(2,1)S(1)}, u32[]{:S(2)}, u32[]{:S(2)}) collective-permute-start(bf16[128,1024]{1,0:T(8,128)(2,1)S(1)} %get-tuple-element.107), channel_id=1, source_target_pairs={{0,24},{8,16},{16,8},{24,0},{1,25},{9,17},{17,9},{25,1},{2,26},{10... | collective-permute-start | bytes 786440 | tf_op jit(solution)/shard_map/ppermute | solution.py:266
  51.8 6.9 %prepare.3 = (bf16[1024,512]{1,0:T(8,128)(2,1)S(1)}, bf16[1024,512]{1,0:T(8,128)(2,1)S(1)}, bf16[1024,512]{1,0:T(8,128)(2,1)S(1)}, bf16[1024,512]{1,0:T(8,128)(2,1)S(1)}, f32[8,128]{1,0:T(8,128)S(1)}) custom-call(s32[3]{0:T(128)S(1)} %pad_add_fusion.refs_0_, s32[4,16]{1,0:T(4,128)S(1)} %collective-permute-done.4.refs_5_.refs_1_, ...), custom_call_target="tpu_custom_call" | custom-call | flops 700000000 | tf_op jit(solution)/shard_map/prepare/pallas_call | solution.py:59
  58.7 1.7 %collective-permute-start.12 = (bf16[512,256]{1,0:T(8,128)(2,1)S(1)}, bf16[512,256]{1,0:T(8,128)(2,1)S(1)}, u32[]{:S(2)}, u32[]{:S(2)}) collective-permute-start(bf16[512,256]{1,0:T(8,128)(2,1)S(1)} %collective-permute-done.11.refs_3_), channel_id=1, source_target_pairs={{0,2},{2,6},{6,4},{4,0},{1,3},{3,7},{7,5},{5,1},{8,10},{10,14},{14... | collective-permute-start | bytes 786440 | tf_op jit(solution)/shard_map/ppermute | solution.py:270
  63.1 3.7 %collective-permute-done.12.refs_3_ = bf16[512,256]{1,0:T(8,128)(2,1)S(1)} collective-permute-done((bf16[512,256]{1,0:T(8,128)(2,1)S(1)}, bf16[512,256]{1,0:T(8,128)(2,1)S(1)}, u32[]{:S(2)}, u32[]{:S(2)}) %collective-permute-start.12) | collective-permute-done | bytes 262176 | tf_op jit(solution)/shard_map/ppermute | solution.py:270
  66.8 1.6 %forward.7 = (bf16[512,256]{1,0:T(8,128)(2,1)S(1)}, bf16[512,256]{1,0:T(8,128)(2,1)S(1)}, bf16[512,256]{1,0:T(8,128)(2,1)S(1)}, bf16[512,256]{1,0:T(8,128)(2,1)S...) custom-call(bf16[1024,512]{1,0:T(8,128)(2,1)S(1)} %get-tuple-element.82.refs_0_.refs_8_, ...), custom_call_target="tpu_custom_call" | custom-call | flops 300000000 | tf_op jit(solution)/shard_map/forward/pallas_call | solution.py:59
  68.4 1.8 %collective-permute-start.21 = (bf16[512,256]{1,0:T(8,128)(2,1)S(1)}, bf16[512,256]{1,0:T(8,128)(2,1)S(1)}, u32[]{:S(2)}, u32[]{:S(2)}) collective-permute-start(bf16[512,256]{1,0:T(8,128)(2,1)S(1)} %get-tuple-element.125), channel_id=1, source_target_pairs={{0,4},{2,0},{6,2},{4,6},{1,5},{3,1},{7,3},{5,7},{8,12},{10,8},{14,... | collective-permute-start | bytes 786440 | tf_op jit(solution)/shard_map/ppermute | solution.py:270
  71.0 6.7 %collective-permute-done.21.refs_1_ = bf16[512,256]{1,0:T(8,128)(2,1)S(1)} collective-permute-done((bf16[512,256]{1,0:T(8,128)(2,1)S(1)}, bf16[512,256]{1,0:T(8,128)(2,1)S(1)}, u32[]{:S(2)}, u32[]{:S(2)}) %collective-permute-start.21) | collective-permute-done | bytes 262176 | tf_op jit(solution)/shard_map/ppermute | solution.py:270
  78.3 2.6 %collective-permute-start.22 = (bf16[512,256]{1,0:T(8,128)(2,1)S(1)}, bf16[512,256]{1,0:T(8,128)(2,1)S(1)}, u32[]{:S(2)}, u32[]{:S(2)}) collective-permute-start(bf16[512,256]{1,0:T(8,128)(2,1)S(1)} %get-tuple-element.126), channel_id=1, source_target_pairs={{0,4},{2,0},{6,2},{4,6},{1,5},{3,1},{7,3},{5,7},{8,12},{10,8},{14,... | collective-permute-start | bytes 786440 | tf_op jit(solution)/shard_map/ppermute | solution.py:270
  81.0 2.3 %collective-permute-done.18.refs_1_ = bf16[512,256]{1,0:T(8,128)(2,1)S(1)} collective-permute-done((bf16[512,256]{1,0:T(8,128)(2,1)S(1)}, bf16[512,256]{1,0:T(8,128)(2,1)S(1)}, u32[]{:S(2)}, u32[]{:S(2)}) %collective-permute-start.18) | collective-permute-done | bytes 262176 | tf_op jit(solution)/shard_map/ppermute | solution.py:270
  84.0 2.6 %collective-permute-start.19 = (bf16[512,256]{1,0:T(8,128)(2,1)S(1)}, bf16[512,256]{1,0:T(8,128)(2,1)S(1)}, u32[]{:S(2)}, u32[]{:S(2)}) collective-permute-start(bf16[512,256]{1,0:T(8,128)(2,1)S(1)} %get-tuple-element.121), channel_id=1, source_target_pairs={{0,4},{2,0},{6,2},{4,6},{1,5},{3,1},{7,3},{5,7},{8,12},{10,8},{14,... | collective-permute-start | bytes 786440 | tf_op jit(solution)/shard_map/ppermute | solution.py:270
  87.3 1.6 %collective-permute-done.22.refs_1_ = bf16[512,256]{1,0:T(8,128)(2,1)S(1)} collective-permute-done((bf16[512,256]{1,0:T(8,128)(2,1)S(1)}, bf16[512,256]{1,0:T(8,128)(2,1)S(1)}, u32[]{:S(2)}, u32[]{:S(2)}) %collective-permute-start.22) | collective-permute-done | bytes 262176 | tf_op jit(solution)/shard_map/ppermute | solution.py:270
  89.6 2.6 %collective-permute-start.23 = (bf16[512,256]{1,0:T(8,128)(2,1)S(1)}, bf16[512,256]{1,0:T(8,128)(2,1)S(1)}, u32[]{:S(2)}, u32[]{:S(2)}) collective-permute-start(bf16[512,256]{1,0:T(8,128)(2,1)S(1)} %get-tuple-element.127), channel_id=1, source_target_pairs={{0,4},{2,0},{6,2},{4,6},{1,5},{3,1},{7,3},{5,7},{8,12},{10,8},{14,... | collective-permute-start | bytes 786440 | tf_op jit(solution)/shard_map/ppermute | solution.py:270
  92.2 2.3 %collective-permute-done.19.refs_1_ = bf16[512,256]{1,0:T(8,128)(2,1)S(1)} collective-permute-done((bf16[512,256]{1,0:T(8,128)(2,1)S(1)}, bf16[512,256]{1,0:T(8,128)(2,1)S(1)}, u32[]{:S(2)}, u32[]{:S(2)}) %collective-permute-start.19) | collective-permute-done | bytes 262176 | tf_op jit(solution)/shard_map/ppermute | solution.py:270
  95.2 2.6 %collective-permute-start.20 = (bf16[512,256]{1,0:T(8,128)(2,1)S(1)}, bf16[512,256]{1,0:T(8,128)(2,1)S(1)}, u32[]{:S(2)}, u32[]{:S(2)}) collective-permute-start(bf16[512,256]{1,0:T(8,128)(2,1)S(1)} %get-tuple-element.122), channel_id=1, source_target_pairs={{0,4},{2,0},{6,2},{4,6},{1,5},{3,1},{7,3},{5,7},{8,12},{10,8},{14,... | collective-permute-start | bytes 786440 | tf_op jit(solution)/shard_map/ppermute | solution.py:270
  98.5 1.4 %collective-permute-done.23.refs_6_ = bf16[512,256]{1,0:T(8,128)(2,1)S(1)} collective-permute-done((bf16[512,256]{1,0:T(8,128)(2,1)S(1)}, bf16[512,256]{1,0:T(8,128)(2,1)S(1)}, u32[]{:S(2)}, u32[]{:S(2)}) %collective-permute-start.23) | collective-permute-done | bytes 262176 | tf_op jit(solution)/shard_map/ppermute | solution.py:270
  100.0 2.8 %collective-permute-done.20.refs_5_ = bf16[512,256]{1,0:T(8,128)(2,1)S(1)} collective-permute-done((bf16[512,256]{1,0:T(8,128)(2,1)S(1)}, bf16[512,256]{1,0:T(8,128)(2,1)S(1)}, u32[]{:S(2)}, u32[]{:S(2)}) %collective-permute-start.20) | collective-permute-done | bytes 262176 | tf_op jit(solution)/shard_map/ppermute | solution.py:270
  102.8 1.3 grad.1
  104.1 1.6 %collective-permute-start.24 = (bf16[256,256]{1,0:T(8,128)(2,1)S(1)}, bf16[256,256]{1,0:T(8,128)(2,1)S(1)}, u32[]{:S(2)}, u32[]{:S(2)}) collective-permute-start(bf16[256,256]{1,0:T(8,128)(2,1)S(1)} %get-tuple-element.129), channel_id=1, source_target_pairs={{0,8},{8,0},{16,24},{24,16},{1,9},{9,1},{17,25},{25,17},{2,10},{10... | collective-permute-start | bytes 393224 | tf_op jit(solution)/shard_map/ppermute | solution.py:266
  106.1 1.5 %collective-permute-start.26 = (bf16[256,256]{1,0:T(8,128)(2,1)S(1)}, bf16[256,256]{1,0:T(8,128)(2,1)S(1)}, u32[]{:S(2)}, u32[]{:S(2)}) collective-permute-start(bf16[256,256]{1,0:T(8,128)(2,1)S(1)} %get-tuple-element.131), channel_id=1, source_target_pairs={{0,24},{8,16},{16,8},{24,0},{1,25},{9,17},{17,9},{25,1},{2,26},{10... | collective-permute-start | bytes 393224 | tf_op jit(solution)/shard_map/ppermute | solution.py:266
  107.7 1.6 %collective-permute-done.24.refs_1_ = bf16[256,256]{1,0:T(8,128)(2,1)S(1)} collective-permute-done((bf16[256,256]{1,0:T(8,128)(2,1)S(1)}, bf16[256,256]{1,0:T(8,128)(2,1)S(1)}, u32[]{:S(2)}, u32[]{:S(2)}) %collective-permute-start.24) | collective-permute-done | bytes 131104 | tf_op jit(solution)/shard_map/ppermute | solution.py:266
  109.3 1.4 %collective-permute-done.25.refs_2_ = bf16[256,256]{1,0:T(8,128)(2,1)S(1)} collective-permute-done((bf16[256,256]{1,0:T(8,128)(2,1)S(1)}, bf16[256,256]{1,0:T(8,128)(2,1)S(1)}, u32[]{:S(2)}, u32[]{:S(2)}) %collective-permute-start.25) | collective-permute-done | bytes 131104 | tf_op jit(solution)/shard_map/ppermute | solution.py:266
  110.7 1.4 %collective-permute-done.26.refs_3_ = bf16[256,256]{1,0:T(8,128)(2,1)S(1)} collective-permute-done((bf16[256,256]{1,0:T(8,128)(2,1)S(1)}, bf16[256,256]{1,0:T(8,128)(2,1)S(1)}, u32[]{:S(2)}, u32[]{:S(2)}) %collective-permute-start.26) | collective-permute-done | bytes 131104 | tf_op jit(solution)/shard_map/ppermute | solution.py:266
  112.2 1.2 collective-permute-start.27
  113.3 3.9 %collective-permute-done.27.refs_1_ = bf16[256,256]{1,0:T(8,128)(2,1)S(1)} collective-permute-done((bf16[256,256]{1,0:T(8,128)(2,1)S(1)}, bf16[256,256]{1,0:T(8,128)(2,1)S(1)}, u32[]{:S(2)}, u32[]{:S(2)}) %collective-permute-start.27) | collective-permute-done | bytes 131104 | tf_op jit(solution)/shard_map/ppermute | solution.py:423
  117.3 2.1 %collective-permute-start.28 = (bf16[256,256]{1,0:T(8,128)(2,1)S(1)}, bf16[256,256]{1,0:T(8,128)(2,1)S(1)}, u32[]{:S(2)}, u32[]{:S(2)}) collective-permute-start(bf16[256,256]{1,0:T(8,128)(2,1)S(1)} %sum.4.refs_0_), channel_id=1, source_target_pairs={{0,4},{2,6},{4,0},{6,2},{1,5},{3,7},{5,1},{7,3},{8,12},{10,14},{12... | collective-permute-start | bytes 393224 | tf_op jit(solution)/shard_map/ppermute | solution.py:423
  119.5 3.8 %collective-permute-done.28.refs_1_ = bf16[256,256]{1,0:T(8,128)(2,1)S(1)} collective-permute-done((bf16[256,256]{1,0:T(8,128)(2,1)S(1)}, bf16[256,256]{1,0:T(8,128)(2,1)S(1)}, u32[]{:S(2)}, u32[]{:S(2)}) %collective-permute-start.28) | collective-permute-done | bytes 131104 | tf_op jit(solution)/shard_map/ppermute | solution.py:423
  123.3 4.0 %collective-permute-start.29 = (bf16[256,256]{1,0:T(8,128)(2,1)S(1)}, bf16[256,256]{1,0:T(8,128)(2,1)S(1)}, u32[]{:S(2)}, u32[]{:S(2)}) collective-permute-start(bf16[256,256]{1,0:T(8,128)(2,1)S(1)} %sum.5.refs_1_), channel_id=1, source_target_pairs={{0,8},{8,0},{16,24},{24,16},{1,9},{9,1},{17,25},{25,17},{2,10},{10... | collective-permute-start | bytes 393224 | tf_op jit(solution)/shard_map/ppermute | solution.py:266
  127.5 1.4 %collective-permute-start.31 = (bf16[256,256]{1,0:T(8,128)(2,1)S(1)}, bf16[256,256]{1,0:T(8,128)(2,1)S(1)}, u32[]{:S(2)}, u32[]{:S(2)}) collective-permute-start(bf16[256,256]{1,0:T(8,128)(2,1)S(1)} %sum.5.refs_1_), channel_id=1, source_target_pairs={{0,24},{8,16},{16,8},{24,0},{1,25},{9,17},{17,9},{25,1},{2,26},{10... | collective-permute-start | bytes 393224 | tf_op jit(solution)/shard_map/ppermute | solution.py:266
  128.9 1.4 %collective-permute-done.29.refs_2_ = bf16[256,256]{1,0:T(8,128)(2,1)S(1)} collective-permute-done((bf16[256,256]{1,0:T(8,128)(2,1)S(1)}, bf16[256,256]{1,0:T(8,128)(2,1)S(1)}, u32[]{:S(2)}, u32[]{:S(2)}) %collective-permute-start.29) | collective-permute-done | bytes 131104 | tf_op jit(solution)/shard_map/ppermute | solution.py:266
  130.2 3.4 %collective-permute-done.30.refs_3_ = bf16[256,256]{1,0:T(8,128)(2,1)S(1)} collective-permute-done((bf16[256,256]{1,0:T(8,128)(2,1)S(1)}, bf16[256,256]{1,0:T(8,128)(2,1)S(1)}, u32[]{:S(2)}, u32[]{:S(2)}) %collective-permute-start.30) | collective-permute-done | bytes 131104 | tf_op jit(solution)/shard_map/ppermute | solution.py:266
  135.2 2.0 %last.1 = f32[1024,512]{1,0:T(8,128)} custom-call(s32[3]{0:T(128)S(1)} %pad_add_fusion.refs_0_, bf16[256,256]{1,0:T(8,128)(2,1)S(1)} %sum.5.refs_1_, bf16[256,256]{1,0:T(8,128)(2,1)S(1)} %collective-permute-done.29.refs_2_, bf16[256,256]{1,0:T(8,128)(2,1)S(1)} %collective-permute-done.30.refs_3_, bf16[256,256]{1,0:T(8,128)(2,1)S(1)} %collective-permute-done.31.refs_4_, ...), custom_call_target="tpu_custom_call" | custom-call | flops 200000000 | tf_op jit(solution)/shard_map/last/pallas_call | solution.py:59
  (71 shorter events, 14.1 us)
Async XLA Ops:
  0.6 51.1 %collective-permute-start.5 = (bf16[4,16,128,128]{3,2,1,0:T(8,128)(2,1)}, bf16[4,16,128,128]{3,2,1,0:T(8,128)(2,1)}, u32[]{:S(2)}, u32[]{:S(2)}) collective-permute-start(bf16[4,16,128,128]{3,2,1,0:T(8,128)(2,1)} %refs_3_.1), channel_id=1, source_target_pairs={{0,1},{1,0},{2,3},{3,2},{4,5},{5,4},{6,7},{7,6},{8,9},{9,8},{10,11... | collective-permute-start | bytes 6291464 | tf_op jit(solution)/shard_map/ppermute | solution.py:263
  1.2 0.7 copy-start.4
  3.7 15.1 %all-to-all-start = ((s32[32,8,128]{2,1,0:T(8,128)}), s32[32,8,128]{2,1,0:T(8,128)S(1)}, u32[]{:S(2)}, u32[]{:S(2)}) async-start(s32[32,8,128]{2,1,0:T(8,128)} %index.1), calls=%async_computation | async-start | bytes 262144 | tf_op jit(solution)/shard_map/all_to_all | solution.py:280
  10.6 1.2 copy-start
  11.9 1.2 copy-start.3
  13.1 10.5 %copy-start.5 = (bf16[512,512]{1,0:T(8,128)(2,1)S(1)}, bf16[512,512]{1,0:T(8,128)(2,1)}, u32[]{:S(2)}) copy-start(bf16[512,512]{1,0:T(8,128)(2,1)} %param.13) | copy-start | bytes 1572868
  14.3 15.2 %copy-start.6 = (s32[4,16]{1,0:T(4,128)S(1)}, s32[4,16]{1,0:T(4,128)}, u32[]{:S(2)}) copy-start(s32[4,16]{1,0:T(4,128)} %param.9) | copy-start | bytes 772
  14.4 15.2 %copy-start.7 = (s32[4]{0:T(128)S(1)}, s32[4]{0:T(128)}, u32[]{:S(2)}) copy-start(s32[4]{0:T(128)} %param.10) | copy-start | bytes 52
  14.4 15.5 %copy-start.1 = (bf16[512,1024]{1,0:T(8,128)(2,1)S(1)}, bf16[512,1024]{1,0:T(8,128)(2,1)}, u32[]{:S(2)}) copy-start(bf16[512,1024]{1,0:T(8,128)(2,1)} %refs_1_.1) | copy-start | bytes 3145732
  20.0 6.4 %collective-permute-start = (bf16[2,128,256]{2,1,0:T(8,128)(2,1)S(1)}, bf16[2,128,256]{2,1,0:T(8,128)(2,1)S(1)}, u32[]{:S(2)}, u32[]{:S(2)}) collective-permute-start(bf16[2,128,256]{2,1,0:T(8,128)(2,1)S(1)} %get-tuple-element.75), channel_id=1, source_target_pairs={{0,8},{8,0},{16,24},{24,16},{1,9},{9,1},{17,25},{25,17},{2,10},{10... | collective-permute-start | bytes 393224 | tf_op jit(solution)/shard_map/ppermute | solution.py:266
  20.9 7.8 %collective-permute-start.1 = (bf16[2,128,256]{2,1,0:T(8,128)(2,1)S(1)}, bf16[2,128,256]{2,1,0:T(8,128)(2,1)S(1)}, u32[]{:S(2)}, u32[]{:S(2)}) collective-permute-start(bf16[2,128,256]{2,1,0:T(8,128)(2,1)S(1)} %get-tuple-element.76), channel_id=1, source_target_pairs={{0,16},{8,24},{16,0},{24,8},{1,17},{9,25},{17,1},{25,9},{2,18},{10... | collective-permute-start | bytes 393224 | tf_op jit(solution)/shard_map/ppermute | solution.py:266
  21.6 7.1 %collective-permute-start.2 = (bf16[2,128,256]{2,1,0:T(8,128)(2,1)S(1)}, bf16[2,128,256]{2,1,0:T(8,128)(2,1)S(1)}, u32[]{:S(2)}, u32[]{:S(2)}) collective-permute-start(bf16[2,128,256]{2,1,0:T(8,128)(2,1)S(1)} %get-tuple-element.77), channel_id=1, source_target_pairs={{0,24},{8,16},{16,8},{24,0},{1,25},{9,17},{17,9},{25,1},{2,26},{10... | collective-permute-start | bytes 393224 | tf_op jit(solution)/shard_map/ppermute | solution.py:266
  23.6 8.2 %copy-start.2 = (bf16[4,16,128,128]{3,2,1,0:T(8,128)(2,1)S(1)}, bf16[4,16,128,128]{3,2,1,0:T(8,128)(2,1)}, u32[]{:S(2)}) copy-start(bf16[4,16,128,128]{3,2,1,0:T(8,128)(2,1)} %refs_3_.1) | copy-start | bytes 6291460
  23.6 6.2 %collective-permute-start.3 = (bf16[512,256]{1,0:T(8,128)(2,1)S(1)}, bf16[512,256]{1,0:T(8,128)(2,1)S(1)}, u32[]{:S(2)}, u32[]{:S(2)}) collective-permute-start(bf16[512,256]{1,0:T(8,128)(2,1)S(1)} %get-tuple-element.134), channel_id=1, source_target_pairs={{0,1},{1,0},{2,3},{3,2},{4,5},{5,4},{6,7},{7,6},{8,9},{9,8},{10,11... | collective-permute-start | bytes 786440 | tf_op jit(solution)/shard_map/ppermute | solution.py:263
  28.7 1.8 %collective-permute-start.6 = (bf16[512,256]{1,0:T(8,128)(2,1)S(1)}, bf16[512,256]{1,0:T(8,128)(2,1)S(1)}, u32[]{:S(2)}, u32[]{:S(2)}) collective-permute-start(bf16[512,256]{1,0:T(8,128)(2,1)S(1)} %get-tuple-element.83), channel_id=1, source_target_pairs={{0,1},{1,0},{2,3},{3,2},{4,5},{5,4},{6,7},{7,6},{8,9},{9,8},{10,11... | collective-permute-start | bytes 786440 | tf_op jit(solution)/shard_map/ppermute | solution.py:263
  28.8 10.1 %collective-permute-start.8 = (bf16[512,256]{1,0:T(8,128)(2,1)S(1)}, bf16[512,256]{1,0:T(8,128)(2,1)S(1)}, u32[]{:S(2)}, u32[]{:S(2)}) collective-permute-start(bf16[512,256]{1,0:T(8,128)(2,1)S(1)} %get-tuple-element.84.refs_2_), channel_id=1, source_target_pairs={{0,2},{2,6},{6,4},{4,0},{1,3},{3,7},{7,5},{5,1},{8,10},{10,14},{14... | collective-permute-start | bytes 786440 | tf_op jit(solution)/shard_map/ppermute | solution.py:270
  29.6 2.2 %collective-permute-start.4 = (s32[4,16]{1,0:T(4,128)S(1)}, s32[4,16]{1,0:T(4,128)S(1)}, u32[]{:S(2)}, u32[]{:S(2)}) collective-permute-start(s32[4,16]{1,0:T(4,128)S(1)} %fusion.refs_1_), channel_id=1, source_target_pairs={{0,1},{1,0},{2,3},{3,2},{4,5},{5,4},{6,7},{7,6},{8,9},{9,8},{10,11... | collective-permute-start | bytes 776 | tf_op jit(solution)/shard_map/ppermute | solution.py:263
  30.6 13.9 %collective-permute-start.7 = (bf16[512,256]{1,0:T(8,128)(2,1)S(1)}, bf16[512,256]{1,0:T(8,128)(2,1)S(1)}, u32[]{:S(2)}, u32[]{:S(2)}) collective-permute-start(bf16[512,256]{1,0:T(8,128)(2,1)S(1)} %collective-permute-done.6.refs_3_), channel_id=1, source_target_pairs={{0,2},{2,6},{6,4},{4,0},{1,3},{3,7},{7,5},{5,1},{8,10},{10,14},{14... | collective-permute-start | bytes 786440 | tf_op jit(solution)/shard_map/ppermute | solution.py:270
  38.9 11.2 %collective-permute-start.9 = (bf16[512,256]{1,0:T(8,128)(2,1)S(1)}, bf16[512,256]{1,0:T(8,128)(2,1)S(1)}, u32[]{:S(2)}, u32[]{:S(2)}) collective-permute-start(bf16[512,256]{1,0:T(8,128)(2,1)S(1)} %collective-permute-done.8.refs_2_), channel_id=1, source_target_pairs={{0,2},{2,6},{6,4},{4,0},{1,3},{3,7},{7,5},{5,1},{8,10},{10,14},{14... | collective-permute-start | bytes 786440 | tf_op jit(solution)/shard_map/ppermute | solution.py:270
  44.5 14.2 %collective-permute-start.11 = (bf16[512,256]{1,0:T(8,128)(2,1)S(1)}, bf16[512,256]{1,0:T(8,128)(2,1)S(1)}, u32[]{:S(2)}, u32[]{:S(2)}) collective-permute-start(bf16[512,256]{1,0:T(8,128)(2,1)S(1)} %collective-permute-done.7.refs_3_), channel_id=1, source_target_pairs={{0,2},{2,6},{6,4},{4,0},{1,3},{3,7},{7,5},{5,1},{8,10},{10,14},{14... | collective-permute-start | bytes 786440 | tf_op jit(solution)/shard_map/ppermute | solution.py:270
  44.5 15.9 %collective-permute-start.13 = (bf16[128,1024]{1,0:T(8,128)(2,1)S(1)}, bf16[128,1024]{1,0:T(8,128)(2,1)S(1)}, u32[]{:S(2)}, u32[]{:S(2)}) collective-permute-start(bf16[128,1024]{1,0:T(8,128)(2,1)S(1)} %get-tuple-element.105), channel_id=1, source_target_pairs={{0,8},{8,0},{16,24},{24,16},{1,9},{9,1},{17,25},{25,17},{2,10},{10... | collective-permute-start | bytes 786440 | tf_op jit(solution)/shard_map/ppermute | solution.py:266
  46.2 14.2 %collective-permute-start.14 = (bf16[128,1024]{1,0:T(8,128)(2,1)S(1)}, bf16[128,1024]{1,0:T(8,128)(2,1)S(1)}, u32[]{:S(2)}, u32[]{:S(2)}) collective-permute-start(bf16[128,1024]{1,0:T(8,128)(2,1)S(1)} %get-tuple-element.106), channel_id=1, source_target_pairs={{0,16},{8,24},{16,0},{24,8},{1,17},{9,25},{17,1},{25,9},{2,18},{10... | collective-permute-start | bytes 786440 | tf_op jit(solution)/shard_map/ppermute | solution.py:266
  50.1 10.3 %collective-permute-start.15 = (bf16[128,1024]{1,0:T(8,128)(2,1)S(1)}, bf16[128,1024]{1,0:T(8,128)(2,1)S(1)}, u32[]{:S(2)}, u32[]{:S(2)}) collective-permute-start(bf16[128,1024]{1,0:T(8,128)(2,1)S(1)} %get-tuple-element.107), channel_id=1, source_target_pairs={{0,24},{8,16},{16,8},{24,0},{1,25},{9,17},{17,9},{25,1},{2,26},{10... | collective-permute-start | bytes 786440 | tf_op jit(solution)/shard_map/ppermute | solution.py:266
  51.7 11.4 %collective-permute-start.10 = (bf16[512,256]{1,0:T(8,128)(2,1)S(1)}, bf16[512,256]{1,0:T(8,128)(2,1)S(1)}, u32[]{:S(2)}, u32[]{:S(2)}) collective-permute-start(bf16[512,256]{1,0:T(8,128)(2,1)S(1)} %collective-permute-done.9.refs_2_), channel_id=1, source_target_pairs={{0,2},{2,6},{6,4},{4,0},{1,3},{3,7},{7,5},{5,1},{8,10},{10,14},{14... | collective-permute-start | bytes 786440 | tf_op jit(solution)/shard_map/ppermute | solution.py:270
  58.7 8.1 %collective-permute-start.12 = (bf16[512,256]{1,0:T(8,128)(2,1)S(1)}, bf16[512,256]{1,0:T(8,128)(2,1)S(1)}, u32[]{:S(2)}, u32[]{:S(2)}) collective-permute-start(bf16[512,256]{1,0:T(8,128)(2,1)S(1)} %collective-permute-done.11.refs_3_), channel_id=1, source_target_pairs={{0,2},{2,6},{6,4},{4,0},{1,3},{3,7},{7,5},{5,1},{8,10},{10,14},{14... | collective-permute-start | bytes 786440 | tf_op jit(solution)/shard_map/ppermute | solution.py:270
  60.7 37.8 %collective-permute-start.17 = (bf16[1024,512]{1,0:T(8,128)(2,1)S(1)}, bf16[1024,512]{1,0:T(8,128)(2,1)S(1)}, u32[]{:S(2)}, u32[]{:S(2)}) collective-permute-start(bf16[1024,512]{1,0:T(8,128)(2,1)S(1)} %get-tuple-element.113.refs_1_), channel_id=1, source_target_pairs={{0,1},{1,0},{2,3},{3,2},{4,5},{5,4},{6,7},{7,6},{8,9},{9,8},{10,11... | collective-permute-start | bytes 3145736 | tf_op jit(solution)/shard_map/ppermute | solution.py:263
  68.4 9.3 %collective-permute-start.21 = (bf16[512,256]{1,0:T(8,128)(2,1)S(1)}, bf16[512,256]{1,0:T(8,128)(2,1)S(1)}, u32[]{:S(2)}, u32[]{:S(2)}) collective-permute-start(bf16[512,256]{1,0:T(8,128)(2,1)S(1)} %get-tuple-element.125), channel_id=1, source_target_pairs={{0,4},{2,0},{6,2},{4,6},{1,5},{3,1},{7,3},{5,7},{8,12},{10,8},{14,... | collective-permute-start | bytes 786440 | tf_op jit(solution)/shard_map/ppermute | solution.py:270
  70.2 13.1 %collective-permute-start.18 = (bf16[512,256]{1,0:T(8,128)(2,1)S(1)}, bf16[512,256]{1,0:T(8,128)(2,1)S(1)}, u32[]{:S(2)}, u32[]{:S(2)}) collective-permute-start(bf16[512,256]{1,0:T(8,128)(2,1)S(1)} %get-tuple-element.120), channel_id=1, source_target_pairs={{0,4},{2,0},{6,2},{4,6},{1,5},{3,1},{7,3},{5,7},{8,12},{10,8},{14,... | collective-permute-start | bytes 786440 | tf_op jit(solution)/shard_map/ppermute | solution.py:270
  70.3 17.0 %collective-permute-start.16 = (bf16[512,256]{1,0:T(8,128)(2,1)S(1)}, bf16[512,256]{1,0:T(8,128)(2,1)S(1)}, u32[]{:S(2)}, u32[]{:S(2)}) collective-permute-start(bf16[512,256]{1,0:T(8,128)(2,1)S(1)} %get-tuple-element.112), channel_id=1, source_target_pairs={{0,1},{1,0},{2,3},{3,2},{4,5},{5,4},{6,7},{7,6},{8,9},{9,8},{10,11... | collective-permute-start | bytes 786440 | tf_op jit(solution)/shard_map/ppermute | solution.py:263
  78.3 10.6 %collective-permute-start.22 = (bf16[512,256]{1,0:T(8,128)(2,1)S(1)}, bf16[512,256]{1,0:T(8,128)(2,1)S(1)}, u32[]{:S(2)}, u32[]{:S(2)}) collective-permute-start(bf16[512,256]{1,0:T(8,128)(2,1)S(1)} %get-tuple-element.126), channel_id=1, source_target_pairs={{0,4},{2,0},{6,2},{4,6},{1,5},{3,1},{7,3},{5,7},{8,12},{10,8},{14,... | collective-permute-start | bytes 786440 | tf_op jit(solution)/shard_map/ppermute | solution.py:270
  84.0 10.6 %collective-permute-start.19 = (bf16[512,256]{1,0:T(8,128)(2,1)S(1)}, bf16[512,256]{1,0:T(8,128)(2,1)S(1)}, u32[]{:S(2)}, u32[]{:S(2)}) collective-permute-start(bf16[512,256]{1,0:T(8,128)(2,1)S(1)} %get-tuple-element.121), channel_id=1, source_target_pairs={{0,4},{2,0},{6,2},{4,6},{1,5},{3,1},{7,3},{5,7},{8,12},{10,8},{14,... | collective-permute-start | bytes 786440 | tf_op jit(solution)/shard_map/ppermute | solution.py:270
  89.6 10.4 %collective-permute-start.23 = (bf16[512,256]{1,0:T(8,128)(2,1)S(1)}, bf16[512,256]{1,0:T(8,128)(2,1)S(1)}, u32[]{:S(2)}, u32[]{:S(2)}) collective-permute-start(bf16[512,256]{1,0:T(8,128)(2,1)S(1)} %get-tuple-element.127), channel_id=1, source_target_pairs={{0,4},{2,0},{6,2},{4,6},{1,5},{3,1},{7,3},{5,7},{8,12},{10,8},{14,... | collective-permute-start | bytes 786440 | tf_op jit(solution)/shard_map/ppermute | solution.py:270
  95.2 7.6 %collective-permute-start.20 = (bf16[512,256]{1,0:T(8,128)(2,1)S(1)}, bf16[512,256]{1,0:T(8,128)(2,1)S(1)}, u32[]{:S(2)}, u32[]{:S(2)}) collective-permute-start(bf16[512,256]{1,0:T(8,128)(2,1)S(1)} %get-tuple-element.122), channel_id=1, source_target_pairs={{0,4},{2,0},{6,2},{4,6},{1,5},{3,1},{7,3},{5,7},{8,12},{10,8},{14,... | collective-permute-start | bytes 786440 | tf_op jit(solution)/shard_map/ppermute | solution.py:270
  104.1 5.2 %collective-permute-start.24 = (bf16[256,256]{1,0:T(8,128)(2,1)S(1)}, bf16[256,256]{1,0:T(8,128)(2,1)S(1)}, u32[]{:S(2)}, u32[]{:S(2)}) collective-permute-start(bf16[256,256]{1,0:T(8,128)(2,1)S(1)} %get-tuple-element.129), channel_id=1, source_target_pairs={{0,8},{8,0},{16,24},{24,16},{1,9},{9,1},{17,25},{25,17},{2,10},{10... | collective-permute-start | bytes 393224 | tf_op jit(solution)/shard_map/ppermute | solution.py:266
  105.7 5.0 %collective-permute-start.25 = (bf16[256,256]{1,0:T(8,128)(2,1)S(1)}, bf16[256,256]{1,0:T(8,128)(2,1)S(1)}, u32[]{:S(2)}, u32[]{:S(2)}) collective-permute-start(bf16[256,256]{1,0:T(8,128)(2,1)S(1)} %get-tuple-element.130), channel_id=1, source_target_pairs={{0,16},{8,24},{16,0},{24,8},{1,17},{9,25},{17,1},{25,9},{2,18},{10... | collective-permute-start | bytes 393224 | tf_op jit(solution)/shard_map/ppermute | solution.py:266
  106.1 6.0 %collective-permute-start.26 = (bf16[256,256]{1,0:T(8,128)(2,1)S(1)}, bf16[256,256]{1,0:T(8,128)(2,1)S(1)}, u32[]{:S(2)}, u32[]{:S(2)}) collective-permute-start(bf16[256,256]{1,0:T(8,128)(2,1)S(1)} %get-tuple-element.131), channel_id=1, source_target_pairs={{0,24},{8,16},{16,8},{24,0},{1,25},{9,17},{17,9},{25,1},{2,26},{10... | collective-permute-start | bytes 393224 | tf_op jit(solution)/shard_map/ppermute | solution.py:266
  112.2 5.1 %collective-permute-start.27 = (bf16[256,256]{1,0:T(8,128)(2,1)S(1)}, bf16[256,256]{1,0:T(8,128)(2,1)S(1)}, u32[]{:S(2)}, u32[]{:S(2)}) collective-permute-start(bf16[256,256]{1,0:T(8,128)(2,1)S(1)} %sum.3.refs_0_), channel_id=1, source_target_pairs={{0,2},{2,0},{4,6},{6,4},{1,3},{3,1},{5,7},{7,5},{8,10},{10,8},{12,... | collective-permute-start | bytes 393224 | tf_op jit(solution)/shard_map/ppermute | solution.py:423
  117.3 5.9 %collective-permute-start.28 = (bf16[256,256]{1,0:T(8,128)(2,1)S(1)}, bf16[256,256]{1,0:T(8,128)(2,1)S(1)}, u32[]{:S(2)}, u32[]{:S(2)}) collective-permute-start(bf16[256,256]{1,0:T(8,128)(2,1)S(1)} %sum.4.refs_0_), channel_id=1, source_target_pairs={{0,4},{2,6},{4,0},{6,2},{1,5},{3,7},{5,1},{7,3},{8,12},{10,14},{12... | collective-permute-start | bytes 393224 | tf_op jit(solution)/shard_map/ppermute | solution.py:423
  123.3 6.9 %collective-permute-start.29 = (bf16[256,256]{1,0:T(8,128)(2,1)S(1)}, bf16[256,256]{1,0:T(8,128)(2,1)S(1)}, u32[]{:S(2)}, u32[]{:S(2)}) collective-permute-start(bf16[256,256]{1,0:T(8,128)(2,1)S(1)} %sum.5.refs_1_), channel_id=1, source_target_pairs={{0,8},{8,0},{16,24},{24,16},{1,9},{9,1},{17,25},{25,17},{2,10},{10... | collective-permute-start | bytes 393224 | tf_op jit(solution)/shard_map/ppermute | solution.py:266
  127.3 6.4 %collective-permute-start.30 = (bf16[256,256]{1,0:T(8,128)(2,1)S(1)}, bf16[256,256]{1,0:T(8,128)(2,1)S(1)}, u32[]{:S(2)}, u32[]{:S(2)}) collective-permute-start(bf16[256,256]{1,0:T(8,128)(2,1)S(1)} %sum.5.refs_1_), channel_id=1, source_target_pairs={{0,16},{8,24},{16,0},{24,8},{1,17},{9,25},{17,1},{25,9},{2,18},{10... | collective-permute-start | bytes 393224 | tf_op jit(solution)/shard_map/ppermute | solution.py:266
  127.5 6.2 %collective-permute-start.31 = (bf16[256,256]{1,0:T(8,128)(2,1)S(1)}, bf16[256,256]{1,0:T(8,128)(2,1)S(1)}, u32[]{:S(2)}, u32[]{:S(2)}) collective-permute-start(bf16[256,256]{1,0:T(8,128)(2,1)S(1)} %sum.5.refs_1_), channel_id=1, source_target_pairs={{0,24},{8,16},{16,8},{24,0},{1,25},{9,17},{17,9},{25,1},{2,26},{10... | collective-permute-start | bytes 393224 | tf_op jit(solution)/shard_map/ppermute | solution.py:266
  128.8 6.2 %collective-permute-start.32 = (bf16[256,256]{1,0:T(8,128)(2,1)S(1)}, bf16[256,256]{1,0:T(8,128)(2,1)S(1)}, u32[]{:S(2)}, u32[]{:S(2)}) collective-permute-start(bf16[256,256]{1,0:T(8,128)(2,1)S(1)} %sum.5.refs_1_), channel_id=1, source_target_pairs={{0,1},{1,0},{2,3},{3,2},{4,5},{5,4},{6,7},{7,6},{8,9},{9,8},{10,11... | collective-permute-start | bytes 393224 | tf_op jit(solution)/shard_map/ppermute | solution.py:263
  130.2 4.8 %collective-permute-start.33 = (bf16[256,256]{1,0:T(8,128)(2,1)S(1)}, bf16[256,256]{1,0:T(8,128)(2,1)S(1)}, u32[]{:S(2)}, u32[]{:S(2)}) collective-permute-start(bf16[256,256]{1,0:T(8,128)(2,1)S(1)} %collective-permute-done.29.refs_2_), channel_id=1, source_target_pairs={{0,1},{1,0},{2,3},{3,2},{4,5},{5,4},{6,7},{7,6},{8,9},{9,8},{10,11... | collective-permute-start | bytes 393224 | tf_op jit(solution)/shard_map/ppermute | solution.py:263
  133.7 1.4 %collective-permute-start.34 = (bf16[256,256]{1,0:T(8,128)(2,1)S(1)}, bf16[256,256]{1,0:T(8,128)(2,1)S(1)}, u32[]{:S(2)}, u32[]{:S(2)}) collective-permute-start(bf16[256,256]{1,0:T(8,128)(2,1)S(1)} %collective-permute-done.30.refs_3_), channel_id=1, source_target_pairs={{0,1},{1,0},{2,3},{3,2},{4,5},{5,4},{6,7},{7,6},{8,9},{9,8},{10,11... | collective-permute-start | bytes 393224 | tf_op jit(solution)/shard_map/ppermute | solution.py:263
  133.7 1.5 %collective-permute-start.35 = (bf16[256,256]{1,0:T(8,128)(2,1)S(1)}, bf16[256,256]{1,0:T(8,128)(2,1)S(1)}, u32[]{:S(2)}, u32[]{:S(2)}) collective-permute-start(bf16[256,256]{1,0:T(8,128)(2,1)S(1)} %collective-permute-done.31.refs_4_), channel_id=1, source_target_pairs={{0,1},{1,0},{2,3},{3,2},{4,5},{5,4},{6,7},{7,6},{8,9},{9,8},{10,11... | collective-permute-start | bytes 393224 | tf_op jit(solution)/shard_map/ppermute | solution.py:263

commit v16 on v15

--- a/solution.py
+++ b/solution.py
@@ -144,7 +144,7 @@
 
 
 def pack_kernel(z, *refs):
-    ins, outs = refs[:z.grp], refs[z.grp:]
+    ins, outs = refs[:z.grp][::-1], refs[z.grp:]
     for rel, out in enumerate(outs):
         for s in range(z.grp):
             out[s * z.per_grp:(s + 1) * z.per_grp, :] = ins[s][rel]
@@ -223,13 +223,15 @@
     out_ref[...] = (mine_ref[...] + come_ref[...].astype(F32)).astype(BF16)
 
 
-def grad_kernel(z, me_ref, left_a, left_b, mine_a, mine_b, come_a, come_b, *refs):
+def part_kernel(left_ref, mine_ref, come_ref, out_ref):
+    grad = (mine_ref[...] + come_ref[...].astype(F32)).astype(BF16)
+    out_ref[...] = dot(left_ref[...], grad)
+
+
+def grad_kernel(z, me_ref, left_ref, mine_ref, come_ref, part_ref, *refs):
     outs, whole = refs[:-1], refs[-1]
-    grads = [
-        (mine[...] + come[...].astype(F32)).astype(BF16)
-        for mine, come in ((mine_a, come_a), (mine_b, come_b))
-    ]
-    whole[...] = (dot(left_a[...], grads[0]) + dot(left_b[...], grads[1])).astype(BF16)
+    grad = (mine_ref[...] + come_ref[...].astype(F32)).astype(BF16)
+    whole[...] = (part_ref[...] + dot(left_ref[...], grad)).astype(BF16)
     share = whole.shape[0] // z.grp
     for s in range(z.grp):
         at = pl.multiple_of((me_ref[0] ^ s) * share, share)
@@ -289,7 +291,7 @@
         return call(
             lambda *refs: pack_kernel(z, *refs),
             [((rows, half), BF16)] * 2,
-            [("v", part) for part in parts],
+            [("v", part) for part in parts[::-1]],
             "pack", 0.5, after=after, token=True,
         )
 
@@ -403,10 +405,14 @@
     )
 
     share = width_in // z.grp
+    (part,) = call(
+        part_kernel, [((width_in, half), F32)],
+        [("v", value) for value in (lefts[0], mine[0], came[0])], "part", 1,
+    )
     terms = call(
         lambda *refs: grad_kernel(z, *refs),
         [((share, half), BF16)] * z.grp,
-        [("s", me)] + [("v", part) for part in (*lefts, *mine, *came)],
+        [("s", me)] + [("v", value) for value in (lefts[1], mine[1], came[1], part)],
         "grad", 1.5,
         (pltpu.VMEM((width_in, half), BF16),),
     )
@@ -416,14 +422,14 @@
             sum_kernel, [((share, half), BF16)], [("v", part) for part in parts], "sum", 0.5
         )[0]
 
-    mine = total_of([to_grp(terms[s], s) for s in range(z.grp)])
+    mine = total_of(across(terms)[::-1])
     step = 1
     while step < z.zz:
         mine = total_of(
             [mine, lax.ppermute(mine, "zz", [(i, i ^ step) for i in range(z.zz)])]
         )
         step *= 2
-    mine = [to_grp(mine, s) for s in range(z.grp)]
+    mine = across([mine] * z.grp)
     (grad_weight,) = call(
         lambda *refs: last_kernel(z, *refs),
         [((width_in, hidden_units), F32)],

time: 138 us -> 136 us (0.986)
  starting transfers between devices: 44.3 us -> 40.6 us
  waiting for transfers between devices: 57.7 us -> 59.6 us
    ppermute x12, starting transfers between devices: 16.5 us -> 13.6 us  [to_grp(): lax.ppermute(x, 'grp', [(i, i ^ s) for i in range(z.grp)])]
    pallas_call x24 -> x25, Pallas kernels: 30.1 us -> 30.3 us  [call(): pl.pallas_call(kernel, out_shape=tuple((jax.ShapeDtypeStruct(s, d) for s,...]
  transfers between devices with their start and end apart: 37 -> 37, of which waited for: 21 -> 22; matrix products, arithmetic and copies ran while one was open for 1% -> 1% of each run, Pallas kernels for 19% -> 19%
where the time goes in v16:
time: 136 us
  waiting for transfers between devices  59.6 us (44%)
  starting transfers between devices  40.6 us (30%)
  Pallas kernels  30.3 us (22%)
  local copies, waits for them, and re-layouts  3.19 us (2%)
    ppermute x12, waiting for transfers between devices, to_zz(): lax.ppermute(x, 'zz', [(order[i], order[(i + k) % z.zz]) for i in range(z...  32.1 us
    pallas_call x25, Pallas kernels, call(): pl.pallas_call(kernel, out_shape=tuple((jax.ShapeDtypeStruct(s, d) for s,...  30.3 us
    ppermute x12, starting transfers between devices, to_zz(): lax.ppermute(x, 'zz', [(order[i], order[(i + k) % z.zz]) for i in range(z...  15.4 us
    ppermute x12, waiting for transfers between devices, to_grp(): lax.ppermute(x, 'grp', [(i, i ^ s) for i in range(z.grp)])  13.9 us
    ppermute x12, starting transfers between devices, to_grp(): lax.ppermute(x, 'grp', [(i, i ^ s) for i in range(z.grp)])  13.6 us
    ppermute x2, waiting for transfers between devices, shards(): lax.ppermute(mine, 'zz', [(i, i ^ step) for i in range(z.zz)])  8.6 us
    all_to_all x1, starting transfers between devices, shards(): lax.all_to_all(message, ('grp', 'zz', 'core'), split_axis=0, concat_axis=...  6.96 us
    all_to_all x1, waiting for transfers between devices, shards(): lax.all_to_all(message, ('grp', 'zz', 'core'), split_axis=0, concat_axis=...  4.42 us
  transfers between devices with their start and end apart: 37, of which 22 were waited for; matrix products, arithmetic and copies ran while one was open for 1% of the time, Pallas kernels for 19%

profile of v16, /device:TPU:0, one launch (start us, length us, event | category | flops | bytes accessed | tf_op | source)
XLA Modules:
  0.0 135.6 jit_solution(339044359772423635)
XLA Ops:
  1.9 1.8 %index.1 = s32[32,8,128]{2,1,0:T(8,128)} custom-call(s32[3]{0:T(128)S(1)} %pad_add_fusion.refs_0_, s32[1,512]{1,0:T(1,128)S(1)} %bitcast.4), custom_call_target="tpu_custom_call" | custom-call | flops 100000000 | tf_op jit(solution)/shard_map/index/pallas_call | solution.py:59
  3.7 7.0 %all-to-all-start = ((s32[32,8,128]{2,1,0:T(8,128)}), s32[32,8,128]{2,1,0:T(8,128)S(1)}, u32[]{:S(2)}, u32[]{:S(2)}) async-start(s32[32,8,128]{2,1,0:T(8,128)} %index.1), calls=%async_computation | async-start | bytes 262144 | tf_op jit(solution)/shard_map/all_to_all | solution.py:282
  10.6 1.2 copy-done
  11.9 1.2 copy-done.3
  13.1 1.3 product.1
  14.4 4.4 %all-to-all-done.refs_1_.refs_2_ = s32[32,8,128]{2,1,0:T(8,128)S(1)} async-done(((s32[32,8,128]{2,1,0:T(8,128)}), s32[32,8,128]{2,1,0:T(8,128)S(1)}, u32[]{:S(2)}, u32[]{:S(2)}) %all-to-all-start) | async-done | bytes 131104 | tf_op jit(solution)/shard_map/all_to_all | solution.py:282
  18.8 1.2 send.1
  20.0 1.0 collective-permute-start
  21.1 1.3 collective-permute-start.1
  22.4 1.2 collective-permute-start.2
  23.7 3.7 %collective-permute-done.refs_0_ = bf16[2,128,256]{2,1,0:T(8,128)(2,1)S(1)} collective-permute-done((bf16[2,128,256]{2,1,0:T(8,128)(2,1)S(1)}, bf16[2,128,256]{2,1,0:T(8,128)(2,1)S(1)}, u32[]{:S(2)}, u32[]{:S(2)}) %collective-permute-start) | collective-permute-done | bytes 131104 | tf_op jit(solution)/shard_map/ppermute | solution.py:268
  27.4 1.6 %collective-permute-done.1.refs_1_ = bf16[2,128,256]{2,1,0:T(8,128)(2,1)S(1)} collective-permute-done((bf16[2,128,256]{2,1,0:T(8,128)(2,1)S(1)}, bf16[2,128,256]{2,1,0:T(8,128)(2,1)S(1)}, u32[]{:S(2)}, u32[]{:S(2)}) %collective-permute-start.1) | collective-permute-done | bytes 131104 | tf_op jit(solution)/shard_map/ppermute | solution.py:268
  30.6 1.2 collective-permute-start.7
  31.8 5.9 %prepare.2 = (bf16[1024,512]{1,0:T(8,128)(2,1)S(1)}, bf16[1024,512]{1,0:T(8,128)(2,1)S(1)}, bf16[1024,512]{1,0:T(8,128)(2,1)S(1)}, bf16[1024,512]{1,0:T(8,128)(2,1)S(1)}, f32[8,128]{1,0:T(8,128)S(1)}) custom-call(s32[3]{0:T(128)S(1)} %pad_add_fusion.refs_0_, s32[4,16]{1,0:T(4,128)S(1)} %fusion.refs_1_, s32[32,8,128]{2,1,0:T(8,128)S(1)} %all-to-all-done.refs_1_.refs_2_, ...), custom_call_target="tpu_custom_call" | custom-call | flops 700000000 | tf_op jit(solution)/shard_map/prepare/pallas_call | solution.py:59
  37.7 1.4 %collective-permute-done.8.refs_2_ = bf16[512,256]{1,0:T(8,128)(2,1)S(1)} collective-permute-done((bf16[512,256]{1,0:T(8,128)(2,1)S(1)}, bf16[512,256]{1,0:T(8,128)(2,1)S(1)}, u32[]{:S(2)}, u32[]{:S(2)}) %collective-permute-start.8) | collective-permute-done | bytes 262176 | tf_op jit(solution)/shard_map/ppermute | solution.py:272
  39.1 5.6 %collective-permute-done.7.refs_3_ = bf16[512,256]{1,0:T(8,128)(2,1)S(1)} collective-permute-done((bf16[512,256]{1,0:T(8,128)(2,1)S(1)}, bf16[512,256]{1,0:T(8,128)(2,1)S(1)}, u32[]{:S(2)}, u32[]{:S(2)}) %collective-permute-start.7) | collective-permute-done | bytes 262176 | tf_op jit(solution)/shard_map/ppermute | solution.py:272
  45.5 1.0 collective-permute-start.14
  46.5 3.9 %collective-permute-done.9.refs_2_ = bf16[512,256]{1,0:T(8,128)(2,1)S(1)} collective-permute-done((bf16[512,256]{1,0:T(8,128)(2,1)S(1)}, bf16[512,256]{1,0:T(8,128)(2,1)S(1)}, u32[]{:S(2)}, u32[]{:S(2)}) %collective-permute-start.9) | collective-permute-done | bytes 262176 | tf_op jit(solution)/shard_map/ppermute | solution.py:272
  50.4 1.2 collective-permute-start.15
  51.5 6.9 %prepare.3 = (bf16[1024,512]{1,0:T(8,128)(2,1)S(1)}, bf16[1024,512]{1,0:T(8,128)(2,1)S(1)}, bf16[1024,512]{1,0:T(8,128)(2,1)S(1)}, bf16[1024,512]{1,0:T(8,128)(2,1)S(1)}, f32[8,128]{1,0:T(8,128)S(1)}) custom-call(s32[3]{0:T(128)S(1)} %pad_add_fusion.refs_0_, s32[4,16]{1,0:T(4,128)S(1)} %collective-permute-done.4.refs_5_.refs_1_, ...), custom_call_target="tpu_custom_call" | custom-call | flops 700000000 | tf_op jit(solution)/shard_map/prepare/pallas_call | solution.py:59
  58.5 1.7 %collective-permute-start.12 = (bf16[512,256]{1,0:T(8,128)(2,1)S(1)}, bf16[512,256]{1,0:T(8,128)(2,1)S(1)}, u32[]{:S(2)}, u32[]{:S(2)}) collective-permute-start(bf16[512,256]{1,0:T(8,128)(2,1)S(1)} %collective-permute-done.11.refs_3_), channel_id=1, source_target_pairs={{0,2},{2,6},{6,4},{4,0},{1,3},{3,7},{7,5},{5,1},{8,10},{10,14},{14... | collective-permute-start | bytes 786440 | tf_op jit(solution)/shard_map/ppermute | solution.py:272
  63.0 3.8 %collective-permute-done.12.refs_3_ = bf16[512,256]{1,0:T(8,128)(2,1)S(1)} collective-permute-done((bf16[512,256]{1,0:T(8,128)(2,1)S(1)}, bf16[512,256]{1,0:T(8,128)(2,1)S(1)}, u32[]{:S(2)}, u32[]{:S(2)}) %collective-permute-start.12) | collective-permute-done | bytes 262176 | tf_op jit(solution)/shard_map/ppermute | solution.py:272
  66.8 1.6 %forward.7 = (bf16[512,256]{1,0:T(8,128)(2,1)S(1)}, bf16[512,256]{1,0:T(8,128)(2,1)S(1)}, bf16[512,256]{1,0:T(8,128)(2,1)S(1)}, bf16[512,256]{1,0:T(8,128)(2,1)S...) custom-call(bf16[1024,512]{1,0:T(8,128)(2,1)S(1)} %get-tuple-element.82.refs_0_.refs_8_, ...), custom_call_target="tpu_custom_call" | custom-call | flops 300000000 | tf_op jit(solution)/shard_map/forward/pallas_call | solution.py:59
  68.4 1.6 %collective-permute-start.21 = (bf16[512,256]{1,0:T(8,128)(2,1)S(1)}, bf16[512,256]{1,0:T(8,128)(2,1)S(1)}, u32[]{:S(2)}, u32[]{:S(2)}) collective-permute-start(bf16[512,256]{1,0:T(8,128)(2,1)S(1)} %get-tuple-element.125), channel_id=1, source_target_pairs={{0,4},{2,0},{6,2},{4,6},{1,5},{3,1},{7,3},{5,7},{8,12},{10,8},{14,... | collective-permute-start | bytes 786440 | tf_op jit(solution)/shard_map/ppermute | solution.py:272
  70.8 6.9 %collective-permute-done.21.refs_1_ = bf16[512,256]{1,0:T(8,128)(2,1)S(1)} collective-permute-done((bf16[512,256]{1,0:T(8,128)(2,1)S(1)}, bf16[512,256]{1,0:T(8,128)(2,1)S(1)}, u32[]{:S(2)}, u32[]{:S(2)}) %collective-permute-start.21) | collective-permute-done | bytes 262176 | tf_op jit(solution)/shard_map/ppermute | solution.py:272
  78.3 2.5 %collective-permute-start.22 = (bf16[512,256]{1,0:T(8,128)(2,1)S(1)}, bf16[512,256]{1,0:T(8,128)(2,1)S(1)}, u32[]{:S(2)}, u32[]{:S(2)}) collective-permute-start(bf16[512,256]{1,0:T(8,128)(2,1)S(1)} %get-tuple-element.126), channel_id=1, source_target_pairs={{0,4},{2,0},{6,2},{4,6},{1,5},{3,1},{7,3},{5,7},{8,12},{10,8},{14,... | collective-permute-start | bytes 786440 | tf_op jit(solution)/shard_map/ppermute | solution.py:272
  80.8 2.5 %collective-permute-done.18.refs_1_ = bf16[512,256]{1,0:T(8,128)(2,1)S(1)} collective-permute-done((bf16[512,256]{1,0:T(8,128)(2,1)S(1)}, bf16[512,256]{1,0:T(8,128)(2,1)S(1)}, u32[]{:S(2)}, u32[]{:S(2)}) %collective-permute-start.18) | collective-permute-done | bytes 262176 | tf_op jit(solution)/shard_map/ppermute | solution.py:272
  83.9 2.0 %collective-permute-start.19 = (bf16[512,256]{1,0:T(8,128)(2,1)S(1)}, bf16[512,256]{1,0:T(8,128)(2,1)S(1)}, u32[]{:S(2)}, u32[]{:S(2)}) collective-permute-start(bf16[512,256]{1,0:T(8,128)(2,1)S(1)} %get-tuple-element.120), channel_id=1, source_target_pairs={{0,4},{2,0},{6,2},{4,6},{1,5},{3,1},{7,3},{5,7},{8,12},{10,8},{14,... | collective-permute-start | bytes 786440 | tf_op jit(solution)/shard_map/ppermute | solution.py:272
  88.2 2.9 %collective-permute-start.23 = (bf16[512,256]{1,0:T(8,128)(2,1)S(1)}, bf16[512,256]{1,0:T(8,128)(2,1)S(1)}, u32[]{:S(2)}, u32[]{:S(2)}) collective-permute-start(bf16[512,256]{1,0:T(8,128)(2,1)S(1)} %get-tuple-element.127), channel_id=1, source_target_pairs={{0,4},{2,0},{6,2},{4,6},{1,5},{3,1},{7,3},{5,7},{8,12},{10,8},{14,... | collective-permute-start | bytes 786440 | tf_op jit(solution)/shard_map/ppermute | solution.py:272
  91.0 2.1 %collective-permute-done.19.refs_1_ = bf16[512,256]{1,0:T(8,128)(2,1)S(1)} collective-permute-done((bf16[512,256]{1,0:T(8,128)(2,1)S(1)}, bf16[512,256]{1,0:T(8,128)(2,1)S(1)}, u32[]{:S(2)}, u32[]{:S(2)}) %collective-permute-start.19) | collective-permute-done | bytes 262176 | tf_op jit(solution)/shard_map/ppermute | solution.py:272
  93.8 2.9 %collective-permute-start.20 = (bf16[512,256]{1,0:T(8,128)(2,1)S(1)}, bf16[512,256]{1,0:T(8,128)(2,1)S(1)}, u32[]{:S(2)}, u32[]{:S(2)}) collective-permute-start(bf16[512,256]{1,0:T(8,128)(2,1)S(1)} %get-tuple-element.121), channel_id=1, source_target_pairs={{0,4},{2,0},{6,2},{4,6},{1,5},{3,1},{7,3},{5,7},{8,12},{10,8},{14,... | collective-permute-start | bytes 786440 | tf_op jit(solution)/shard_map/ppermute | solution.py:272
  97.4 1.4 %collective-permute-done.23.refs_2_ = bf16[512,256]{1,0:T(8,128)(2,1)S(1)} collective-permute-done((bf16[512,256]{1,0:T(8,128)(2,1)S(1)}, bf16[512,256]{1,0:T(8,128)(2,1)S(1)}, u32[]{:S(2)}, u32[]{:S(2)}) %collective-permute-start.23) | collective-permute-done | bytes 262176 | tf_op jit(solution)/shard_map/ppermute | solution.py:272
  99.2 3.7 %collective-permute-done.20.refs_3_ = bf16[512,256]{1,0:T(8,128)(2,1)S(1)} collective-permute-done((bf16[512,256]{1,0:T(8,128)(2,1)S(1)}, bf16[512,256]{1,0:T(8,128)(2,1)S(1)}, u32[]{:S(2)}, u32[]{:S(2)}) %collective-permute-start.20) | collective-permute-done | bytes 262176 | tf_op jit(solution)/shard_map/ppermute | solution.py:272
  102.9 1.0 grad.1
  103.9 1.5 %collective-permute-start.24 = (bf16[256,256]{1,0:T(8,128)(2,1)S(1)}, bf16[256,256]{1,0:T(8,128)(2,1)S(1)}, u32[]{:S(2)}, u32[]{:S(2)}) collective-permute-start(bf16[256,256]{1,0:T(8,128)(2,1)S(1)} %get-tuple-element.128), channel_id=1, source_target_pairs={{0,24},{8,16},{16,8},{24,0},{1,25},{9,17},{17,9},{25,1},{2,26},{10... | collective-permute-start | bytes 393224 | tf_op jit(solution)/shard_map/ppermute | solution.py:268
  105.4 1.2 collective-permute-start.25
  107.5 3.0 %collective-permute-done.24.refs_0_ = bf16[256,256]{1,0:T(8,128)(2,1)S(1)} collective-permute-done((bf16[256,256]{1,0:T(8,128)(2,1)S(1)}, bf16[256,256]{1,0:T(8,128)(2,1)S(1)}, u32[]{:S(2)}, u32[]{:S(2)}) %collective-permute-start.24) | collective-permute-done | bytes 131104 | tf_op jit(solution)/shard_map/ppermute | solution.py:268
  110.4 1.3 collective-permute-done.25.refs_1_
  111.8 0.9 collective-permute-start.27
  112.7 4.1 %collective-permute-done.27.refs_1_ = bf16[256,256]{1,0:T(8,128)(2,1)S(1)} collective-permute-done((bf16[256,256]{1,0:T(8,128)(2,1)S(1)}, bf16[256,256]{1,0:T(8,128)(2,1)S(1)}, u32[]{:S(2)}, u32[]{:S(2)}) %collective-permute-start.27) | collective-permute-done | bytes 131104 | tf_op jit(solution)/shard_map/ppermute | solution.py:429
  116.9 2.9 %collective-permute-start.28 = (bf16[256,256]{1,0:T(8,128)(2,1)S(1)}, bf16[256,256]{1,0:T(8,128)(2,1)S(1)}, u32[]{:S(2)}, u32[]{:S(2)}) collective-permute-start(bf16[256,256]{1,0:T(8,128)(2,1)S(1)} %sum.4.refs_0_), channel_id=1, source_target_pairs={{0,4},{2,6},{4,0},{6,2},{1,5},{3,7},{5,1},{7,3},{8,12},{10,14},{12... | collective-permute-start | bytes 393224 | tf_op jit(solution)/shard_map/ppermute | solution.py:429
  119.7 4.5 %collective-permute-done.28.refs_1_ = bf16[256,256]{1,0:T(8,128)(2,1)S(1)} collective-permute-done((bf16[256,256]{1,0:T(8,128)(2,1)S(1)}, bf16[256,256]{1,0:T(8,128)(2,1)S(1)}, u32[]{:S(2)}, u32[]{:S(2)}) %collective-permute-start.28) | collective-permute-done | bytes 131104 | tf_op jit(solution)/shard_map/ppermute | solution.py:429
  124.3 1.4 %collective-permute-start.29 = (bf16[256,256]{1,0:T(8,128)(2,1)S(1)}, bf16[256,256]{1,0:T(8,128)(2,1)S(1)}, u32[]{:S(2)}, u32[]{:S(2)}) collective-permute-start(bf16[256,256]{1,0:T(8,128)(2,1)S(1)} %sum.5.refs_1_), channel_id=1, source_target_pairs={{0,8},{8,0},{16,24},{24,16},{1,9},{9,1},{17,25},{25,17},{2,10},{10... | collective-permute-start | bytes 393224 | tf_op jit(solution)/shard_map/ppermute | solution.py:268
  126.4 1.4 %collective-permute-start.31 = (bf16[256,256]{1,0:T(8,128)(2,1)S(1)}, bf16[256,256]{1,0:T(8,128)(2,1)S(1)}, u32[]{:S(2)}, u32[]{:S(2)}) collective-permute-start(bf16[256,256]{1,0:T(8,128)(2,1)S(1)} %sum.5.refs_1_), channel_id=1, source_target_pairs={{0,24},{8,16},{16,8},{24,0},{1,25},{9,17},{17,9},{25,1},{2,26},{10... | collective-permute-start | bytes 393224 | tf_op jit(solution)/shard_map/ppermute | solution.py:268
  127.8 1.5 %collective-permute-done.29.refs_2_ = bf16[256,256]{1,0:T(8,128)(2,1)S(1)} collective-permute-done((bf16[256,256]{1,0:T(8,128)(2,1)S(1)}, bf16[256,256]{1,0:T(8,128)(2,1)S(1)}, u32[]{:S(2)}, u32[]{:S(2)}) %collective-permute-start.29) | collective-permute-done | bytes 131104 | tf_op jit(solution)/shard_map/ppermute | solution.py:268
  129.3 1.4 %collective-permute-done.30.refs_3_ = bf16[256,256]{1,0:T(8,128)(2,1)S(1)} collective-permute-done((bf16[256,256]{1,0:T(8,128)(2,1)S(1)}, bf16[256,256]{1,0:T(8,128)(2,1)S(1)}, u32[]{:S(2)}, u32[]{:S(2)}) %collective-permute-start.30) | collective-permute-done | bytes 131104 | tf_op jit(solution)/shard_map/ppermute | solution.py:268
  130.7 1.6 %collective-permute-done.31.refs_4_ = bf16[256,256]{1,0:T(8,128)(2,1)S(1)} collective-permute-done((bf16[256,256]{1,0:T(8,128)(2,1)S(1)}, bf16[256,256]{1,0:T(8,128)(2,1)S(1)}, u32[]{:S(2)}, u32[]{:S(2)}) %collective-permute-start.31) | collective-permute-done | bytes 131104 | tf_op jit(solution)/shard_map/ppermute | solution.py:268
  133.6 2.0 %last.1 = f32[1024,512]{1,0:T(8,128)} custom-call(s32[3]{0:T(128)S(1)} %pad_add_fusion.refs_0_, bf16[256,256]{1,0:T(8,128)(2,1)S(1)} %sum.5.refs_1_, bf16[256,256]{1,0:T(8,128)(2,1)S(1)} %collective-permute-done.29.refs_2_, bf16[256,256]{1,0:T(8,128)(2,1)S(1)} %collective-permute-done.30.refs_3_, bf16[256,256]{1,0:T(8,128)(2,1)S(1)} %collective-permute-done.31.refs_4_, ...), custom_call_target="tpu_custom_call" | custom-call | flops 200000000 | tf_op jit(solution)/shard_map/last/pallas_call | solution.py:59
  (72 shorter events, 15.6 us)
Async XLA Ops:
  0.6 50.9 %collective-permute-start.5 = (bf16[4,16,128,128]{3,2,1,0:T(8,128)(2,1)}, bf16[4,16,128,128]{3,2,1,0:T(8,128)(2,1)}, u32[]{:S(2)}, u32[]{:S(2)}) collective-permute-start(bf16[4,16,128,128]{3,2,1,0:T(8,128)(2,1)} %refs_3_.1), channel_id=1, source_target_pairs={{0,1},{1,0},{2,3},{3,2},{4,5},{5,4},{6,7},{7,6},{8,9},{9,8},{10,11... | collective-permute-start | bytes 6291464 | tf_op jit(solution)/shard_map/ppermute | solution.py:265
  1.2 0.7 copy-start.4
  3.7 15.1 %all-to-all-start = ((s32[32,8,128]{2,1,0:T(8,128)}), s32[32,8,128]{2,1,0:T(8,128)S(1)}, u32[]{:S(2)}, u32[]{:S(2)}) async-start(s32[32,8,128]{2,1,0:T(8,128)} %index.1), calls=%async_computation | async-start | bytes 262144 | tf_op jit(solution)/shard_map/all_to_all | solution.py:282
  10.6 1.2 copy-start
  11.9 1.2 copy-start.3
  13.1 10.5 %copy-start.5 = (bf16[512,512]{1,0:T(8,128)(2,1)S(1)}, bf16[512,512]{1,0:T(8,128)(2,1)}, u32[]{:S(2)}) copy-start(bf16[512,512]{1,0:T(8,128)(2,1)} %param.13) | copy-start | bytes 1572868
  14.4 15.2 %copy-start.6 = (s32[4,16]{1,0:T(4,128)S(1)}, s32[4,16]{1,0:T(4,128)}, u32[]{:S(2)}) copy-start(s32[4,16]{1,0:T(4,128)} %param.9) | copy-start | bytes 772
  14.4 15.2 %copy-start.7 = (s32[4]{0:T(128)S(1)}, s32[4]{0:T(128)}, u32[]{:S(2)}) copy-start(s32[4]{0:T(128)} %param.10) | copy-start | bytes 52
  14.4 15.4 %copy-start.1 = (bf16[512,1024]{1,0:T(8,128)(2,1)S(1)}, bf16[512,1024]{1,0:T(8,128)(2,1)}, u32[]{:S(2)}) copy-start(bf16[512,1024]{1,0:T(8,128)(2,1)} %refs_1_.1) | copy-start | bytes 3145732
  20.0 7.3 %collective-permute-start = (bf16[2,128,256]{2,1,0:T(8,128)(2,1)S(1)}, bf16[2,128,256]{2,1,0:T(8,128)(2,1)S(1)}, u32[]{:S(2)}, u32[]{:S(2)}) collective-permute-start(bf16[2,128,256]{2,1,0:T(8,128)(2,1)S(1)} %get-tuple-element.74), channel_id=1, source_target_pairs={{0,24},{8,16},{16,8},{24,0},{1,25},{9,17},{17,9},{25,1},{2,26},{10... | collective-permute-start | bytes 393224 | tf_op jit(solution)/shard_map/ppermute | solution.py:268
  21.1 7.9 %collective-permute-start.1 = (bf16[2,128,256]{2,1,0:T(8,128)(2,1)S(1)}, bf16[2,128,256]{2,1,0:T(8,128)(2,1)S(1)}, u32[]{:S(2)}, u32[]{:S(2)}) collective-permute-start(bf16[2,128,256]{2,1,0:T(8,128)(2,1)S(1)} %get-tuple-element.75), channel_id=1, source_target_pairs={{0,16},{8,24},{16,0},{24,8},{1,17},{9,25},{17,1},{25,9},{2,18},{10... | collective-permute-start | bytes 393224 | tf_op jit(solution)/shard_map/ppermute | solution.py:268
  22.4 6.6 %collective-permute-start.2 = (bf16[2,128,256]{2,1,0:T(8,128)(2,1)S(1)}, bf16[2,128,256]{2,1,0:T(8,128)(2,1)S(1)}, u32[]{:S(2)}, u32[]{:S(2)}) collective-permute-start(bf16[2,128,256]{2,1,0:T(8,128)(2,1)S(1)} %get-tuple-element.76), channel_id=1, source_target_pairs={{0,8},{8,0},{16,24},{24,16},{1,9},{9,1},{17,25},{25,17},{2,10},{10... | collective-permute-start | bytes 393224 | tf_op jit(solution)/shard_map/ppermute | solution.py:268
  23.6 8.2 %copy-start.2 = (bf16[4,16,128,128]{3,2,1,0:T(8,128)(2,1)S(1)}, bf16[4,16,128,128]{3,2,1,0:T(8,128)(2,1)}, u32[]{:S(2)}) copy-start(bf16[4,16,128,128]{3,2,1,0:T(8,128)(2,1)} %refs_3_.1) | copy-start | bytes 6291460
  23.6 6.2 %collective-permute-start.3 = (bf16[512,256]{1,0:T(8,128)(2,1)S(1)}, bf16[512,256]{1,0:T(8,128)(2,1)S(1)}, u32[]{:S(2)}, u32[]{:S(2)}) collective-permute-start(bf16[512,256]{1,0:T(8,128)(2,1)S(1)} %get-tuple-element.134), channel_id=1, source_target_pairs={{0,1},{1,0},{2,3},{3,2},{4,5},{5,4},{6,7},{7,6},{8,9},{9,8},{10,11... | collective-permute-start | bytes 786440 | tf_op jit(solution)/shard_map/ppermute | solution.py:265
  29.0 1.6 %collective-permute-start.6 = (bf16[512,256]{1,0:T(8,128)(2,1)S(1)}, bf16[512,256]{1,0:T(8,128)(2,1)S(1)}, u32[]{:S(2)}, u32[]{:S(2)}) collective-permute-start(bf16[512,256]{1,0:T(8,128)(2,1)S(1)} %get-tuple-element.83), channel_id=1, source_target_pairs={{0,1},{1,0},{2,3},{3,2},{4,5},{5,4},{6,7},{7,6},{8,9},{9,8},{10,11... | collective-permute-start | bytes 786440 | tf_op jit(solution)/shard_map/ppermute | solution.py:265
  29.1 10.1 %collective-permute-start.8 = (bf16[512,256]{1,0:T(8,128)(2,1)S(1)}, bf16[512,256]{1,0:T(8,128)(2,1)S(1)}, u32[]{:S(2)}, u32[]{:S(2)}) collective-permute-start(bf16[512,256]{1,0:T(8,128)(2,1)S(1)} %get-tuple-element.84.refs_2_), channel_id=1, source_target_pairs={{0,2},{2,6},{6,4},{4,0},{1,3},{3,7},{7,5},{5,1},{8,10},{10,14},{14... | collective-permute-start | bytes 786440 | tf_op jit(solution)/shard_map/ppermute | solution.py:272
  29.6 2.2 %collective-permute-start.4 = (s32[4,16]{1,0:T(4,128)S(1)}, s32[4,16]{1,0:T(4,128)S(1)}, u32[]{:S(2)}, u32[]{:S(2)}) collective-permute-start(s32[4,16]{1,0:T(4,128)S(1)} %fusion.refs_1_), channel_id=1, source_target_pairs={{0,1},{1,0},{2,3},{3,2},{4,5},{5,4},{6,7},{7,6},{8,9},{9,8},{10,11... | collective-permute-start | bytes 776 | tf_op jit(solution)/shard_map/ppermute | solution.py:265
  30.6 14.2 %collective-permute-start.7 = (bf16[512,256]{1,0:T(8,128)(2,1)S(1)}, bf16[512,256]{1,0:T(8,128)(2,1)S(1)}, u32[]{:S(2)}, u32[]{:S(2)}) collective-permute-start(bf16[512,256]{1,0:T(8,128)(2,1)S(1)} %collective-permute-done.6.refs_3_), channel_id=1, source_target_pairs={{0,2},{2,6},{6,4},{4,0},{1,3},{3,7},{7,5},{5,1},{8,10},{10,14},{14... | collective-permute-start | bytes 786440 | tf_op jit(solution)/shard_map/ppermute | solution.py:272
  39.1 11.2 %collective-permute-start.9 = (bf16[512,256]{1,0:T(8,128)(2,1)S(1)}, bf16[512,256]{1,0:T(8,128)(2,1)S(1)}, u32[]{:S(2)}, u32[]{:S(2)}) collective-permute-start(bf16[512,256]{1,0:T(8,128)(2,1)S(1)} %collective-permute-done.8.refs_2_), channel_id=1, source_target_pairs={{0,2},{2,6},{6,4},{4,0},{1,3},{3,7},{7,5},{5,1},{8,10},{10,14},{14... | collective-permute-start | bytes 786440 | tf_op jit(solution)/shard_map/ppermute | solution.py:272
  44.7 13.8 %collective-permute-start.11 = (bf16[512,256]{1,0:T(8,128)(2,1)S(1)}, bf16[512,256]{1,0:T(8,128)(2,1)S(1)}, u32[]{:S(2)}, u32[]{:S(2)}) collective-permute-start(bf16[512,256]{1,0:T(8,128)(2,1)S(1)} %collective-permute-done.7.refs_3_), channel_id=1, source_target_pairs={{0,2},{2,6},{6,4},{4,0},{1,3},{3,7},{7,5},{5,1},{8,10},{10,14},{14... | collective-permute-start | bytes 786440 | tf_op jit(solution)/shard_map/ppermute | solution.py:272
  44.7 15.5 %collective-permute-start.13 = (bf16[128,1024]{1,0:T(8,128)(2,1)S(1)}, bf16[128,1024]{1,0:T(8,128)(2,1)S(1)}, u32[]{:S(2)}, u32[]{:S(2)}) collective-permute-start(bf16[128,1024]{1,0:T(8,128)(2,1)S(1)} %get-tuple-element.105), channel_id=1, source_target_pairs={{0,8},{8,0},{16,24},{24,16},{1,9},{9,1},{17,25},{25,17},{2,10},{10... | collective-permute-start | bytes 786440 | tf_op jit(solution)/shard_map/ppermute | solution.py:268
  45.5 14.8 %collective-permute-start.14 = (bf16[128,1024]{1,0:T(8,128)(2,1)S(1)}, bf16[128,1024]{1,0:T(8,128)(2,1)S(1)}, u32[]{:S(2)}, u32[]{:S(2)}) collective-permute-start(bf16[128,1024]{1,0:T(8,128)(2,1)S(1)} %get-tuple-element.106), channel_id=1, source_target_pairs={{0,16},{8,24},{16,0},{24,8},{1,17},{9,25},{17,1},{25,9},{2,18},{10... | collective-permute-start | bytes 786440 | tf_op jit(solution)/shard_map/ppermute | solution.py:268
  50.4 9.9 %collective-permute-start.15 = (bf16[128,1024]{1,0:T(8,128)(2,1)S(1)}, bf16[128,1024]{1,0:T(8,128)(2,1)S(1)}, u32[]{:S(2)}, u32[]{:S(2)}) collective-permute-start(bf16[128,1024]{1,0:T(8,128)(2,1)S(1)} %get-tuple-element.107), channel_id=1, source_target_pairs={{0,24},{8,16},{16,8},{24,0},{1,25},{9,17},{17,9},{25,1},{2,26},{10... | collective-permute-start | bytes 786440 | tf_op jit(solution)/shard_map/ppermute | solution.py:268
  51.5 11.4 %collective-permute-start.10 = (bf16[512,256]{1,0:T(8,128)(2,1)S(1)}, bf16[512,256]{1,0:T(8,128)(2,1)S(1)}, u32[]{:S(2)}, u32[]{:S(2)}) collective-permute-start(bf16[512,256]{1,0:T(8,128)(2,1)S(1)} %collective-permute-done.9.refs_2_), channel_id=1, source_target_pairs={{0,2},{2,6},{6,4},{4,0},{1,3},{3,7},{7,5},{5,1},{8,10},{10,14},{14... | collective-permute-start | bytes 786440 | tf_op jit(solution)/shard_map/ppermute | solution.py:272
  58.5 8.3 %collective-permute-start.12 = (bf16[512,256]{1,0:T(8,128)(2,1)S(1)}, bf16[512,256]{1,0:T(8,128)(2,1)S(1)}, u32[]{:S(2)}, u32[]{:S(2)}) collective-permute-start(bf16[512,256]{1,0:T(8,128)(2,1)S(1)} %collective-permute-done.11.refs_3_), channel_id=1, source_target_pairs={{0,2},{2,6},{6,4},{4,0},{1,3},{3,7},{7,5},{5,1},{8,10},{10,14},{14... | collective-permute-start | bytes 786440 | tf_op jit(solution)/shard_map/ppermute | solution.py:272
  60.6 38.6 %collective-permute-start.17 = (bf16[1024,512]{1,0:T(8,128)(2,1)S(1)}, bf16[1024,512]{1,0:T(8,128)(2,1)S(1)}, u32[]{:S(2)}, u32[]{:S(2)}) collective-permute-start(bf16[1024,512]{1,0:T(8,128)(2,1)S(1)} %get-tuple-element.113.refs_0_), channel_id=1, source_target_pairs={{0,1},{1,0},{2,3},{3,2},{4,5},{5,4},{6,7},{7,6},{8,9},{9,8},{10,11... | collective-permute-start | bytes 3145736 | tf_op jit(solution)/shard_map/ppermute | solution.py:265
  68.4 9.3 %collective-permute-start.21 = (bf16[512,256]{1,0:T(8,128)(2,1)S(1)}, bf16[512,256]{1,0:T(8,128)(2,1)S(1)}, u32[]{:S(2)}, u32[]{:S(2)}) collective-permute-start(bf16[512,256]{1,0:T(8,128)(2,1)S(1)} %get-tuple-element.125), channel_id=1, source_target_pairs={{0,4},{2,0},{6,2},{4,6},{1,5},{3,1},{7,3},{5,7},{8,12},{10,8},{14,... | collective-permute-start | bytes 786440 | tf_op jit(solution)/shard_map/ppermute | solution.py:272
  70.0 13.2 %collective-permute-start.18 = (bf16[512,256]{1,0:T(8,128)(2,1)S(1)}, bf16[512,256]{1,0:T(8,128)(2,1)S(1)}, u32[]{:S(2)}, u32[]{:S(2)}) collective-permute-start(bf16[512,256]{1,0:T(8,128)(2,1)S(1)} %get-tuple-element.119), channel_id=1, source_target_pairs={{0,4},{2,0},{6,2},{4,6},{1,5},{3,1},{7,3},{5,7},{8,12},{10,8},{14,... | collective-permute-start | bytes 786440 | tf_op jit(solution)/shard_map/ppermute | solution.py:272
  78.3 9.2 %collective-permute-start.22 = (bf16[512,256]{1,0:T(8,128)(2,1)S(1)}, bf16[512,256]{1,0:T(8,128)(2,1)S(1)}, u32[]{:S(2)}, u32[]{:S(2)}) collective-permute-start(bf16[512,256]{1,0:T(8,128)(2,1)S(1)} %get-tuple-element.126), channel_id=1, source_target_pairs={{0,4},{2,0},{6,2},{4,6},{1,5},{3,1},{7,3},{5,7},{8,12},{10,8},{14,... | collective-permute-start | bytes 786440 | tf_op jit(solution)/shard_map/ppermute | solution.py:272
  80.8 10.3 %collective-permute-start.16 = (bf16[512,256]{1,0:T(8,128)(2,1)S(1)}, bf16[512,256]{1,0:T(8,128)(2,1)S(1)}, u32[]{:S(2)}, u32[]{:S(2)}) collective-permute-start(bf16[512,256]{1,0:T(8,128)(2,1)S(1)} %get-tuple-element.112), channel_id=1, source_target_pairs={{0,1},{1,0},{2,3},{3,2},{4,5},{5,4},{6,7},{7,6},{8,9},{9,8},{10,11... | collective-permute-start | bytes 786440 | tf_op jit(solution)/shard_map/ppermute | solution.py:265
  83.9 9.3 %collective-permute-start.19 = (bf16[512,256]{1,0:T(8,128)(2,1)S(1)}, bf16[512,256]{1,0:T(8,128)(2,1)S(1)}, u32[]{:S(2)}, u32[]{:S(2)}) collective-permute-start(bf16[512,256]{1,0:T(8,128)(2,1)S(1)} %get-tuple-element.120), channel_id=1, source_target_pairs={{0,4},{2,0},{6,2},{4,6},{1,5},{3,1},{7,3},{5,7},{8,12},{10,8},{14,... | collective-permute-start | bytes 786440 | tf_op jit(solution)/shard_map/ppermute | solution.py:272
  88.2 10.6 %collective-permute-start.23 = (bf16[512,256]{1,0:T(8,128)(2,1)S(1)}, bf16[512,256]{1,0:T(8,128)(2,1)S(1)}, u32[]{:S(2)}, u32[]{:S(2)}) collective-permute-start(bf16[512,256]{1,0:T(8,128)(2,1)S(1)} %get-tuple-element.127), channel_id=1, source_target_pairs={{0,4},{2,0},{6,2},{4,6},{1,5},{3,1},{7,3},{5,7},{8,12},{10,8},{14,... | collective-permute-start | bytes 786440 | tf_op jit(solution)/shard_map/ppermute | solution.py:272
  93.8 9.1 %collective-permute-start.20 = (bf16[512,256]{1,0:T(8,128)(2,1)S(1)}, bf16[512,256]{1,0:T(8,128)(2,1)S(1)}, u32[]{:S(2)}, u32[]{:S(2)}) collective-permute-start(bf16[512,256]{1,0:T(8,128)(2,1)S(1)} %get-tuple-element.121), channel_id=1, source_target_pairs={{0,4},{2,0},{6,2},{4,6},{1,5},{3,1},{7,3},{5,7},{8,12},{10,8},{14,... | collective-permute-start | bytes 786440 | tf_op jit(solution)/shard_map/ppermute | solution.py:272
  103.9 6.5 %collective-permute-start.24 = (bf16[256,256]{1,0:T(8,128)(2,1)S(1)}, bf16[256,256]{1,0:T(8,128)(2,1)S(1)}, u32[]{:S(2)}, u32[]{:S(2)}) collective-permute-start(bf16[256,256]{1,0:T(8,128)(2,1)S(1)} %get-tuple-element.128), channel_id=1, source_target_pairs={{0,24},{8,16},{16,8},{24,0},{1,25},{9,17},{17,9},{25,1},{2,26},{10... | collective-permute-start | bytes 393224 | tf_op jit(solution)/shard_map/ppermute | solution.py:268
  105.4 6.3 %collective-permute-start.25 = (bf16[256,256]{1,0:T(8,128)(2,1)S(1)}, bf16[256,256]{1,0:T(8,128)(2,1)S(1)}, u32[]{:S(2)}, u32[]{:S(2)}) collective-permute-start(bf16[256,256]{1,0:T(8,128)(2,1)S(1)} %get-tuple-element.129), channel_id=1, source_target_pairs={{0,16},{8,24},{16,0},{24,8},{1,17},{9,25},{17,1},{25,9},{2,18},{10... | collective-permute-start | bytes 393224 | tf_op jit(solution)/shard_map/ppermute | solution.py:268
  106.6 5.1 %collective-permute-start.26 = (bf16[256,256]{1,0:T(8,128)(2,1)S(1)}, bf16[256,256]{1,0:T(8,128)(2,1)S(1)}, u32[]{:S(2)}, u32[]{:S(2)}) collective-permute-start(bf16[256,256]{1,0:T(8,128)(2,1)S(1)} %get-tuple-element.130), channel_id=1, source_target_pairs={{0,8},{8,0},{16,24},{24,16},{1,9},{9,1},{17,25},{25,17},{2,10},{10... | collective-permute-start | bytes 393224 | tf_op jit(solution)/shard_map/ppermute | solution.py:268
  111.8 5.0 %collective-permute-start.27 = (bf16[256,256]{1,0:T(8,128)(2,1)S(1)}, bf16[256,256]{1,0:T(8,128)(2,1)S(1)}, u32[]{:S(2)}, u32[]{:S(2)}) collective-permute-start(bf16[256,256]{1,0:T(8,128)(2,1)S(1)} %sum.3.refs_0_), channel_id=1, source_target_pairs={{0,2},{2,0},{4,6},{6,4},{1,3},{3,1},{5,7},{7,5},{8,10},{10,8},{12,... | collective-permute-start | bytes 393224 | tf_op jit(solution)/shard_map/ppermute | solution.py:429
  116.9 7.3 %collective-permute-start.28 = (bf16[256,256]{1,0:T(8,128)(2,1)S(1)}, bf16[256,256]{1,0:T(8,128)(2,1)S(1)}, u32[]{:S(2)}, u32[]{:S(2)}) collective-permute-start(bf16[256,256]{1,0:T(8,128)(2,1)S(1)} %sum.4.refs_0_), channel_id=1, source_target_pairs={{0,4},{2,6},{4,0},{6,2},{1,5},{3,7},{5,1},{7,3},{8,12},{10,14},{12... | collective-permute-start | bytes 393224 | tf_op jit(solution)/shard_map/ppermute | solution.py:429
  124.3 5.0 %collective-permute-start.29 = (bf16[256,256]{1,0:T(8,128)(2,1)S(1)}, bf16[256,256]{1,0:T(8,128)(2,1)S(1)}, u32[]{:S(2)}, u32[]{:S(2)}) collective-permute-start(bf16[256,256]{1,0:T(8,128)(2,1)S(1)} %sum.5.refs_1_), channel_id=1, source_target_pairs={{0,8},{8,0},{16,24},{24,16},{1,9},{9,1},{17,25},{25,17},{2,10},{10... | collective-permute-start | bytes 393224 | tf_op jit(solution)/shard_map/ppermute | solution.py:268
  125.7 5.0 %collective-permute-start.30 = (bf16[256,256]{1,0:T(8,128)(2,1)S(1)}, bf16[256,256]{1,0:T(8,128)(2,1)S(1)}, u32[]{:S(2)}, u32[]{:S(2)}) collective-permute-start(bf16[256,256]{1,0:T(8,128)(2,1)S(1)} %sum.5.refs_1_), channel_id=1, source_target_pairs={{0,16},{8,24},{16,0},{24,8},{1,17},{9,25},{17,1},{25,9},{2,18},{10... | collective-permute-start | bytes 393224 | tf_op jit(solution)/shard_map/ppermute | solution.py:268
  126.4 5.9 %collective-permute-start.31 = (bf16[256,256]{1,0:T(8,128)(2,1)S(1)}, bf16[256,256]{1,0:T(8,128)(2,1)S(1)}, u32[]{:S(2)}, u32[]{:S(2)}) collective-permute-start(bf16[256,256]{1,0:T(8,128)(2,1)S(1)} %sum.5.refs_1_), channel_id=1, source_target_pairs={{0,24},{8,16},{16,8},{24,0},{1,25},{9,17},{17,9},{25,1},{2,26},{10... | collective-permute-start | bytes 393224 | tf_op jit(solution)/shard_map/ppermute | solution.py:268
  127.8 5.3 %collective-permute-start.32 = (bf16[256,256]{1,0:T(8,128)(2,1)S(1)}, bf16[256,256]{1,0:T(8,128)(2,1)S(1)}, u32[]{:S(2)}, u32[]{:S(2)}) collective-permute-start(bf16[256,256]{1,0:T(8,128)(2,1)S(1)} %sum.5.refs_1_), channel_id=1, source_target_pairs={{0,1},{1,0},{2,3},{3,2},{4,5},{5,4},{6,7},{7,6},{8,9},{9,8},{10,11... | collective-permute-start | bytes 393224 | tf_op jit(solution)/shard_map/ppermute | solution.py:265
  129.3 3.9 %collective-permute-start.33 = (bf16[256,256]{1,0:T(8,128)(2,1)S(1)}, bf16[256,256]{1,0:T(8,128)(2,1)S(1)}, u32[]{:S(2)}, u32[]{:S(2)}) collective-permute-start(bf16[256,256]{1,0:T(8,128)(2,1)S(1)} %collective-permute-done.29.refs_2_), channel_id=1, source_target_pairs={{0,1},{1,0},{2,3},{3,2},{4,5},{5,4},{6,7},{7,6},{8,9},{9,8},{10,11... | collective-permute-start | bytes 393224 | tf_op jit(solution)/shard_map/ppermute | solution.py:265
  130.7 2.5 %collective-permute-start.34 = (bf16[256,256]{1,0:T(8,128)(2,1)S(1)}, bf16[256,256]{1,0:T(8,128)(2,1)S(1)}, u32[]{:S(2)}, u32[]{:S(2)}) collective-permute-start(bf16[256,256]{1,0:T(8,128)(2,1)S(1)} %collective-permute-done.30.refs_3_), channel_id=1, source_target_pairs={{0,1},{1,0},{2,3},{3,2},{4,5},{5,4},{6,7},{7,6},{8,9},{9,8},{10,11... | collective-permute-start | bytes 393224 | tf_op jit(solution)/shard_map/ppermute | solution.py:265
  132.3 1.3 collective-permute-start.35

commit v17 on v16

--- a/solution.py
+++ b/solution.py
@@ -394,7 +394,7 @@
             passed = [
                 call(
                     pass_kernel, [((rows, half), BF16)], [("v", part), ("v", moved)], "pass", 0.5,
-                    after=[come] if i == 1 and k == 1 else (), token=True,
+                    after=[come] if i == 1 and k == z.zz - 2 else (), token=True,
                 )
                 for i, (part, moved) in enumerate(zip(mine, came))
             ]

time: 136 us -> 137 us (level)
  starting transfers between devices: 40.6 us -> 45.7 us
  waiting for transfers between devices: 59.6 us -> 55.5 us
    ppermute x12, starting transfers between devices: 15.4 us -> 18.7 us  [to_zz(): lax.ppermute(x, 'zz', [(order[i], order[(i + k) % z.zz]) for i in range(z...]
    ppermute x12, waiting for transfers between devices: 32.1 us -> 28.8 us  [to_zz(): lax.ppermute(x, 'zz', [(order[i], order[(i + k) % z.zz]) for i in range(z...]
where the time goes in v17:
time: 137 us
  waiting for transfers between devices  55.5 us (41%)
  starting transfers between devices  45.7 us (33%)
  Pallas kernels  30.3 us (22%)
  local copies, waits for them, and re-layouts  3.19 us (2%)
    pallas_call x25, Pallas kernels, call(): pl.pallas_call(kernel, out_shape=tuple((jax.ShapeDtypeStruct(s, d) for s,...  30.3 us
    ppermute x12, waiting for transfers between devices, to_zz(): lax.ppermute(x, 'zz', [(order[i], order[(i + k) % z.zz]) for i in range(z...  28.8 us
    ppermute x12, starting transfers between devices, to_zz(): lax.ppermute(x, 'zz', [(order[i], order[(i + k) % z.zz]) for i in range(z...  18.7 us
    ppermute x12, waiting for transfers between devices, to_grp(): lax.ppermute(x, 'grp', [(i, i ^ s) for i in range(z.grp)])  14 us
    ppermute x12, starting transfers between devices, to_grp(): lax.ppermute(x, 'grp', [(i, i ^ s) for i in range(z.grp)])  13.6 us
    ppermute x2, waiting for transfers between devices, shards(): lax.ppermute(mine, 'zz', [(i, i ^ step) for i in range(z.zz)])  8.06 us
    all_to_all x1, starting transfers between devices, shards(): lax.all_to_all(message, ('grp', 'zz', 'core'), split_axis=0, concat_axis=...  6.96 us
    ppermute x2, starting transfers between devices, shards(): lax.ppermute(mine, 'zz', [(i, i ^ step) for i in range(z.zz)])  4.98 us
  transfers between devices with their start and end apart: 37, of which 22 were waited for; matrix products, arithmetic and copies ran while one was open for 1% of the time, Pallas kernels for 19%

profile of v17, /device:TPU:0, one launch (start us, length us, event | category | flops | bytes accessed | tf_op | source)
XLA Modules:
  0.0 136.6 jit_solution(17924845115736883021)
XLA Ops:
  1.9 1.8 %index.1 = s32[32,8,128]{2,1,0:T(8,128)} custom-call(s32[3]{0:T(128)S(1)} %pad_add_fusion.refs_0_, s32[1,512]{1,0:T(1,128)S(1)} %bitcast.4), custom_call_target="tpu_custom_call" | custom-call | flops 100000000 | tf_op jit(solution)/shard_map/index/pallas_call | solution.py:59
  3.7 7.0 %all-to-all-start = ((s32[32,8,128]{2,1,0:T(8,128)}), s32[32,8,128]{2,1,0:T(8,128)S(1)}, u32[]{:S(2)}, u32[]{:S(2)}) async-start(s32[32,8,128]{2,1,0:T(8,128)} %index.1), calls=%async_computation | async-start | bytes 262144 | tf_op jit(solution)/shard_map/all_to_all | solution.py:282
  10.6 1.2 copy-done
  11.9 1.2 copy-done.3
  13.1 1.3 product.1
  14.4 4.4 %all-to-all-done.refs_1_.refs_2_ = s32[32,8,128]{2,1,0:T(8,128)S(1)} async-done(((s32[32,8,128]{2,1,0:T(8,128)}), s32[32,8,128]{2,1,0:T(8,128)S(1)}, u32[]{:S(2)}, u32[]{:S(2)}) %all-to-all-start) | async-done | bytes 131104 | tf_op jit(solution)/shard_map/all_to_all | solution.py:282
  18.8 1.2 send.1
  20.0 1.0 collective-permute-start
  21.1 1.3 collective-permute-start.1
  22.4 1.2 collective-permute-start.2
  23.7 3.7 %collective-permute-done.refs_0_ = bf16[2,128,256]{2,1,0:T(8,128)(2,1)S(1)} collective-permute-done((bf16[2,128,256]{2,1,0:T(8,128)(2,1)S(1)}, bf16[2,128,256]{2,1,0:T(8,128)(2,1)S(1)}, u32[]{:S(2)}, u32[]{:S(2)}) %collective-permute-start) | collective-permute-done | bytes 131104 | tf_op jit(solution)/shard_map/ppermute | solution.py:268
  27.4 1.6 %collective-permute-done.1.refs_1_ = bf16[2,128,256]{2,1,0:T(8,128)(2,1)S(1)} collective-permute-done((bf16[2,128,256]{2,1,0:T(8,128)(2,1)S(1)}, bf16[2,128,256]{2,1,0:T(8,128)(2,1)S(1)}, u32[]{:S(2)}, u32[]{:S(2)}) %collective-permute-start.1) | collective-permute-done | bytes 131104 | tf_op jit(solution)/shard_map/ppermute | solution.py:268
  30.6 1.2 collective-permute-start.7
  31.8 5.9 %prepare.2 = (bf16[1024,512]{1,0:T(8,128)(2,1)S(1)}, bf16[1024,512]{1,0:T(8,128)(2,1)S(1)}, bf16[1024,512]{1,0:T(8,128)(2,1)S(1)}, bf16[1024,512]{1,0:T(8,128)(2,1)S(1)}, f32[8,128]{1,0:T(8,128)S(1)}) custom-call(s32[3]{0:T(128)S(1)} %pad_add_fusion.refs_0_, s32[4,16]{1,0:T(4,128)S(1)} %fusion.refs_1_, s32[32,8,128]{2,1,0:T(8,128)S(1)} %all-to-all-done.refs_1_.refs_2_, ...), custom_call_target="tpu_custom_call" | custom-call | flops 700000000 | tf_op jit(solution)/shard_map/prepare/pallas_call | solution.py:59
  37.7 1.4 %collective-permute-done.8.refs_2_ = bf16[512,256]{1,0:T(8,128)(2,1)S(1)} collective-permute-done((bf16[512,256]{1,0:T(8,128)(2,1)S(1)}, bf16[512,256]{1,0:T(8,128)(2,1)S(1)}, u32[]{:S(2)}, u32[]{:S(2)}) %collective-permute-start.8) | collective-permute-done | bytes 262176 | tf_op jit(solution)/shard_map/ppermute | solution.py:272
  39.1 5.6 %collective-permute-done.7.refs_3_ = bf16[512,256]{1,0:T(8,128)(2,1)S(1)} collective-permute-done((bf16[512,256]{1,0:T(8,128)(2,1)S(1)}, bf16[512,256]{1,0:T(8,128)(2,1)S(1)}, u32[]{:S(2)}, u32[]{:S(2)}) %collective-permute-start.7) | collective-permute-done | bytes 262176 | tf_op jit(solution)/shard_map/ppermute | solution.py:272
  45.5 1.0 collective-permute-start.14
  46.5 3.9 %collective-permute-done.9.refs_2_ = bf16[512,256]{1,0:T(8,128)(2,1)S(1)} collective-permute-done((bf16[512,256]{1,0:T(8,128)(2,1)S(1)}, bf16[512,256]{1,0:T(8,128)(2,1)S(1)}, u32[]{:S(2)}, u32[]{:S(2)}) %collective-permute-start.9) | collective-permute-done | bytes 262176 | tf_op jit(solution)/shard_map/ppermute | solution.py:272
  50.4 1.2 collective-permute-start.15
  51.5 6.9 %prepare.3 = (bf16[1024,512]{1,0:T(8,128)(2,1)S(1)}, bf16[1024,512]{1,0:T(8,128)(2,1)S(1)}, bf16[1024,512]{1,0:T(8,128)(2,1)S(1)}, bf16[1024,512]{1,0:T(8,128)(2,1)S(1)}, f32[8,128]{1,0:T(8,128)S(1)}) custom-call(s32[3]{0:T(128)S(1)} %pad_add_fusion.refs_0_, s32[4,16]{1,0:T(4,128)S(1)} %collective-permute-done.4.refs_5_.refs_1_, ...), custom_call_target="tpu_custom_call" | custom-call | flops 700000000 | tf_op jit(solution)/shard_map/prepare/pallas_call | solution.py:59
  58.5 1.7 %collective-permute-start.12 = (bf16[512,256]{1,0:T(8,128)(2,1)S(1)}, bf16[512,256]{1,0:T(8,128)(2,1)S(1)}, u32[]{:S(2)}, u32[]{:S(2)}) collective-permute-start(bf16[512,256]{1,0:T(8,128)(2,1)S(1)} %collective-permute-done.11.refs_3_), channel_id=1, source_target_pairs={{0,2},{2,6},{6,4},{4,0},{1,3},{3,7},{7,5},{5,1},{8,10},{10,14},{14... | collective-permute-start | bytes 786440 | tf_op jit(solution)/shard_map/ppermute | solution.py:272
  63.0 3.8 %collective-permute-done.12.refs_3_ = bf16[512,256]{1,0:T(8,128)(2,1)S(1)} collective-permute-done((bf16[512,256]{1,0:T(8,128)(2,1)S(1)}, bf16[512,256]{1,0:T(8,128)(2,1)S(1)}, u32[]{:S(2)}, u32[]{:S(2)}) %collective-permute-start.12) | collective-permute-done | bytes 262176 | tf_op jit(solution)/shard_map/ppermute | solution.py:272
  66.8 1.6 %forward.7 = (bf16[512,256]{1,0:T(8,128)(2,1)S(1)}, bf16[512,256]{1,0:T(8,128)(2,1)S(1)}, bf16[512,256]{1,0:T(8,128)(2,1)S(1)}, bf16[512,256]{1,0:T(8,128)(2,1)S...) custom-call(bf16[1024,512]{1,0:T(8,128)(2,1)S(1)} %get-tuple-element.82.refs_0_.refs_8_, ...), custom_call_target="tpu_custom_call" | custom-call | flops 300000000 | tf_op jit(solution)/shard_map/forward/pallas_call | solution.py:59
  68.4 1.6 %collective-permute-start.21 = (bf16[512,256]{1,0:T(8,128)(2,1)S(1)}, bf16[512,256]{1,0:T(8,128)(2,1)S(1)}, u32[]{:S(2)}, u32[]{:S(2)}) collective-permute-start(bf16[512,256]{1,0:T(8,128)(2,1)S(1)} %get-tuple-element.125), channel_id=1, source_target_pairs={{0,4},{2,0},{6,2},{4,6},{1,5},{3,1},{7,3},{5,7},{8,12},{10,8},{14,... | collective-permute-start | bytes 786440 | tf_op jit(solution)/shard_map/ppermute | solution.py:272
  70.8 5.8 %collective-permute-done.21.refs_1_ = bf16[512,256]{1,0:T(8,128)(2,1)S(1)} collective-permute-done((bf16[512,256]{1,0:T(8,128)(2,1)S(1)}, bf16[512,256]{1,0:T(8,128)(2,1)S(1)}, u32[]{:S(2)}, u32[]{:S(2)}) %collective-permute-start.21) | collective-permute-done | bytes 262176 | tf_op jit(solution)/shard_map/ppermute | solution.py:272
  77.3 3.4 %collective-permute-start.22 = (bf16[512,256]{1,0:T(8,128)(2,1)S(1)}, bf16[512,256]{1,0:T(8,128)(2,1)S(1)}, u32[]{:S(2)}, u32[]{:S(2)}) collective-permute-start(bf16[512,256]{1,0:T(8,128)(2,1)S(1)} %get-tuple-element.126), channel_id=1, source_target_pairs={{0,4},{2,0},{6,2},{4,6},{1,5},{3,1},{7,3},{5,7},{8,12},{10,8},{14,... | collective-permute-start | bytes 786440 | tf_op jit(solution)/shard_map/ppermute | solution.py:272
  80.7 1.6 %collective-permute-done.18.refs_1_ = bf16[512,256]{1,0:T(8,128)(2,1)S(1)} collective-permute-done((bf16[512,256]{1,0:T(8,128)(2,1)S(1)}, bf16[512,256]{1,0:T(8,128)(2,1)S(1)}, u32[]{:S(2)}, u32[]{:S(2)}) %collective-permute-start.18) | collective-permute-done | bytes 262176 | tf_op jit(solution)/shard_map/ppermute | solution.py:272
  82.9 3.4 %collective-permute-start.19 = (bf16[512,256]{1,0:T(8,128)(2,1)S(1)}, bf16[512,256]{1,0:T(8,128)(2,1)S(1)}, u32[]{:S(2)}, u32[]{:S(2)}) collective-permute-start(bf16[512,256]{1,0:T(8,128)(2,1)S(1)} %get-tuple-element.120), channel_id=1, source_target_pairs={{0,4},{2,0},{6,2},{4,6},{1,5},{3,1},{7,3},{5,7},{8,12},{10,8},{14,... | collective-permute-start | bytes 786440 | tf_op jit(solution)/shard_map/ppermute | solution.py:272
  87.0 0.9 collective-permute-done.22.refs_1_
  88.6 3.4 %collective-permute-start.23 = (bf16[512,256]{1,0:T(8,128)(2,1)S(1)}, bf16[512,256]{1,0:T(8,128)(2,1)S(1)}, u32[]{:S(2)}, u32[]{:S(2)}) collective-permute-start(bf16[512,256]{1,0:T(8,128)(2,1)S(1)} %get-tuple-element.127), channel_id=1, source_target_pairs={{0,4},{2,0},{6,2},{4,6},{1,5},{3,1},{7,3},{5,7},{8,12},{10,8},{14,... | collective-permute-start | bytes 786440 | tf_op jit(solution)/shard_map/ppermute | solution.py:272
  91.9 1.6 %collective-permute-done.19.refs_1_ = bf16[512,256]{1,0:T(8,128)(2,1)S(1)} collective-permute-done((bf16[512,256]{1,0:T(8,128)(2,1)S(1)}, bf16[512,256]{1,0:T(8,128)(2,1)S(1)}, u32[]{:S(2)}, u32[]{:S(2)}) %collective-permute-start.19) | collective-permute-done | bytes 262176 | tf_op jit(solution)/shard_map/ppermute | solution.py:272
  94.2 3.4 %collective-permute-start.20 = (bf16[512,256]{1,0:T(8,128)(2,1)S(1)}, bf16[512,256]{1,0:T(8,128)(2,1)S(1)}, u32[]{:S(2)}, u32[]{:S(2)}) collective-permute-start(bf16[512,256]{1,0:T(8,128)(2,1)S(1)} %get-tuple-element.121), channel_id=1, source_target_pairs={{0,4},{2,0},{6,2},{4,6},{1,5},{3,1},{7,3},{5,7},{8,12},{10,8},{14,... | collective-permute-start | bytes 786440 | tf_op jit(solution)/shard_map/ppermute | solution.py:272
  99.5 3.4 %collective-permute-done.20.refs_3_ = bf16[512,256]{1,0:T(8,128)(2,1)S(1)} collective-permute-done((bf16[512,256]{1,0:T(8,128)(2,1)S(1)}, bf16[512,256]{1,0:T(8,128)(2,1)S(1)}, u32[]{:S(2)}, u32[]{:S(2)}) %collective-permute-start.20) | collective-permute-done | bytes 262176 | tf_op jit(solution)/shard_map/ppermute | solution.py:272
  102.9 1.0 grad.1
  103.9 1.6 %collective-permute-start.24 = (bf16[256,256]{1,0:T(8,128)(2,1)S(1)}, bf16[256,256]{1,0:T(8,128)(2,1)S(1)}, u32[]{:S(2)}, u32[]{:S(2)}) collective-permute-start(bf16[256,256]{1,0:T(8,128)(2,1)S(1)} %get-tuple-element.128), channel_id=1, source_target_pairs={{0,24},{8,16},{16,8},{24,0},{1,25},{9,17},{17,9},{25,1},{2,26},{10... | collective-permute-start | bytes 393224 | tf_op jit(solution)/shard_map/ppermute | solution.py:268
  105.6 1.2 collective-permute-start.25
  107.5 3.1 %collective-permute-done.24.refs_0_ = bf16[256,256]{1,0:T(8,128)(2,1)S(1)} collective-permute-done((bf16[256,256]{1,0:T(8,128)(2,1)S(1)}, bf16[256,256]{1,0:T(8,128)(2,1)S(1)}, u32[]{:S(2)}, u32[]{:S(2)}) %collective-permute-start.24) | collective-permute-done | bytes 131104 | tf_op jit(solution)/shard_map/ppermute | solution.py:268
  110.5 1.0 collective-permute-done.25.refs_1_
  111.8 1.4 %collective-permute-start.27 = (bf16[256,256]{1,0:T(8,128)(2,1)S(1)}, bf16[256,256]{1,0:T(8,128)(2,1)S(1)}, u32[]{:S(2)}, u32[]{:S(2)}) collective-permute-start(bf16[256,256]{1,0:T(8,128)(2,1)S(1)} %sum.3.refs_0_), channel_id=1, source_target_pairs={{0,2},{2,0},{4,6},{6,4},{1,3},{3,1},{5,7},{7,5},{8,10},{10,8},{12,... | collective-permute-start | bytes 393224 | tf_op jit(solution)/shard_map/ppermute | solution.py:429
  113.2 3.7 %collective-permute-done.27.refs_1_ = bf16[256,256]{1,0:T(8,128)(2,1)S(1)} collective-permute-done((bf16[256,256]{1,0:T(8,128)(2,1)S(1)}, bf16[256,256]{1,0:T(8,128)(2,1)S(1)}, u32[]{:S(2)}, u32[]{:S(2)}) %collective-permute-start.27) | collective-permute-done | bytes 131104 | tf_op jit(solution)/shard_map/ppermute | solution.py:429
  116.9 3.6 %collective-permute-start.28 = (bf16[256,256]{1,0:T(8,128)(2,1)S(1)}, bf16[256,256]{1,0:T(8,128)(2,1)S(1)}, u32[]{:S(2)}, u32[]{:S(2)}) collective-permute-start(bf16[256,256]{1,0:T(8,128)(2,1)S(1)} %sum.4.refs_0_), channel_id=1, source_target_pairs={{0,4},{2,6},{4,0},{6,2},{1,5},{3,7},{5,1},{7,3},{8,12},{10,14},{12... | collective-permute-start | bytes 393224 | tf_op jit(solution)/shard_map/ppermute | solution.py:429
  120.5 4.4 %collective-permute-done.28.refs_1_ = bf16[256,256]{1,0:T(8,128)(2,1)S(1)} collective-permute-done((bf16[256,256]{1,0:T(8,128)(2,1)S(1)}, bf16[256,256]{1,0:T(8,128)(2,1)S(1)}, u32[]{:S(2)}, u32[]{:S(2)}) %collective-permute-start.28) | collective-permute-done | bytes 131104 | tf_op jit(solution)/shard_map/ppermute | solution.py:429
  124.9 1.7 %collective-permute-start.29 = (bf16[256,256]{1,0:T(8,128)(2,1)S(1)}, bf16[256,256]{1,0:T(8,128)(2,1)S(1)}, u32[]{:S(2)}, u32[]{:S(2)}) collective-permute-start(bf16[256,256]{1,0:T(8,128)(2,1)S(1)} %sum.5.refs_1_), channel_id=1, source_target_pairs={{0,8},{8,0},{16,24},{24,16},{1,9},{9,1},{17,25},{25,17},{2,10},{10... | collective-permute-start | bytes 393224 | tf_op jit(solution)/shard_map/ppermute | solution.py:268
  126.6 1.8 %collective-permute-start.31 = (bf16[256,256]{1,0:T(8,128)(2,1)S(1)}, bf16[256,256]{1,0:T(8,128)(2,1)S(1)}, u32[]{:S(2)}, u32[]{:S(2)}) collective-permute-start(bf16[256,256]{1,0:T(8,128)(2,1)S(1)} %sum.5.refs_1_), channel_id=1, source_target_pairs={{0,24},{8,16},{16,8},{24,0},{1,25},{9,17},{17,9},{25,1},{2,26},{10... | collective-permute-start | bytes 393224 | tf_op jit(solution)/shard_map/ppermute | solution.py:268
  128.5 1.5 %collective-permute-done.29.refs_2_ = bf16[256,256]{1,0:T(8,128)(2,1)S(1)} collective-permute-done((bf16[256,256]{1,0:T(8,128)(2,1)S(1)}, bf16[256,256]{1,0:T(8,128)(2,1)S(1)}, u32[]{:S(2)}, u32[]{:S(2)}) %collective-permute-start.29) | collective-permute-done | bytes 131104 | tf_op jit(solution)/shard_map/ppermute | solution.py:268
  129.9 3.1 %collective-permute-done.30.refs_3_ = bf16[256,256]{1,0:T(8,128)(2,1)S(1)} collective-permute-done((bf16[256,256]{1,0:T(8,128)(2,1)S(1)}, bf16[256,256]{1,0:T(8,128)(2,1)S(1)}, u32[]{:S(2)}, u32[]{:S(2)}) %collective-permute-start.30) | collective-permute-done | bytes 131104 | tf_op jit(solution)/shard_map/ppermute | solution.py:268
  133.6 0.8 pad_maximum_fusion
  134.5 2.0 %last.1 = f32[1024,512]{1,0:T(8,128)} custom-call(s32[3]{0:T(128)S(1)} %pad_add_fusion.refs_0_, bf16[256,256]{1,0:T(8,128)(2,1)S(1)} %sum.5.refs_1_, bf16[256,256]{1,0:T(8,128)(2,1)S(1)} %collective-permute-done.29.refs_2_, bf16[256,256]{1,0:T(8,128)(2,1)S(1)} %collective-permute-done.30.refs_3_, bf16[256,256]{1,0:T(8,128)(2,1)S(1)} %collective-permute-done.31.refs_4_, ...), custom_call_target="tpu_custom_call" | custom-call | flops 200000000 | tf_op jit(solution)/shard_map/last/pallas_call | solution.py:59
  (72 shorter events, 14.1 us)
Async XLA Ops:
  0.6 50.9 %collective-permute-start.5 = (bf16[4,16,128,128]{3,2,1,0:T(8,128)(2,1)}, bf16[4,16,128,128]{3,2,1,0:T(8,128)(2,1)}, u32[]{:S(2)}, u32[]{:S(2)}) collective-permute-start(bf16[4,16,128,128]{3,2,1,0:T(8,128)(2,1)} %refs_3_.1), channel_id=1, source_target_pairs={{0,1},{1,0},{2,3},{3,2},{4,5},{5,4},{6,7},{7,6},{8,9},{9,8},{10,11... | collective-permute-start | bytes 6291464 | tf_op jit(solution)/shard_map/ppermute | solution.py:265
  1.2 0.7 copy-start.4
  3.7 15.1 %all-to-all-start = ((s32[32,8,128]{2,1,0:T(8,128)}), s32[32,8,128]{2,1,0:T(8,128)S(1)}, u32[]{:S(2)}, u32[]{:S(2)}) async-start(s32[32,8,128]{2,1,0:T(8,128)} %index.1), calls=%async_computation | async-start | bytes 262144 | tf_op jit(solution)/shard_map/all_to_all | solution.py:282
  10.6 1.2 copy-start
  11.9 1.2 copy-start.3
  13.1 10.5 %copy-start.5 = (bf16[512,512]{1,0:T(8,128)(2,1)S(1)}, bf16[512,512]{1,0:T(8,128)(2,1)}, u32[]{:S(2)}) copy-start(bf16[512,512]{1,0:T(8,128)(2,1)} %param.13) | copy-start | bytes 1572868
  14.4 15.2 %copy-start.6 = (s32[4,16]{1,0:T(4,128)S(1)}, s32[4,16]{1,0:T(4,128)}, u32[]{:S(2)}) copy-start(s32[4,16]{1,0:T(4,128)} %param.9) | copy-start | bytes 772
  14.4 15.2 %copy-start.7 = (s32[4]{0:T(128)S(1)}, s32[4]{0:T(128)}, u32[]{:S(2)}) copy-start(s32[4]{0:T(128)} %param.10) | copy-start | bytes 52
  14.4 15.4 %copy-start.1 = (bf16[512,1024]{1,0:T(8,128)(2,1)S(1)}, bf16[512,1024]{1,0:T(8,128)(2,1)}, u32[]{:S(2)}) copy-start(bf16[512,1024]{1,0:T(8,128)(2,1)} %refs_1_.1) | copy-start | bytes 3145732
  20.0 7.3 %collective-permute-start = (bf16[2,128,256]{2,1,0:T(8,128)(2,1)S(1)}, bf16[2,128,256]{2,1,0:T(8,128)(2,1)S(1)}, u32[]{:S(2)}, u32[]{:S(2)}) collective-permute-start(bf16[2,128,256]{2,1,0:T(8,128)(2,1)S(1)} %get-tuple-element.74), channel_id=1, source_target_pairs={{0,24},{8,16},{16,8},{24,0},{1,25},{9,17},{17,9},{25,1},{2,26},{10... | collective-permute-start | bytes 393224 | tf_op jit(solution)/shard_map/ppermute | solution.py:268
  21.1 7.9 %collective-permute-start.1 = (bf16[2,128,256]{2,1,0:T(8,128)(2,1)S(1)}, bf16[2,128,256]{2,1,0:T(8,128)(2,1)S(1)}, u32[]{:S(2)}, u32[]{:S(2)}) collective-permute-start(bf16[2,128,256]{2,1,0:T(8,128)(2,1)S(1)} %get-tuple-element.75), channel_id=1, source_target_pairs={{0,16},{8,24},{16,0},{24,8},{1,17},{9,25},{17,1},{25,9},{2,18},{10... | collective-permute-start | bytes 393224 | tf_op jit(solution)/shard_map/ppermute | solution.py:268
  22.4 6.6 %collective-permute-start.2 = (bf16[2,128,256]{2,1,0:T(8,128)(2,1)S(1)}, bf16[2,128,256]{2,1,0:T(8,128)(2,1)S(1)}, u32[]{:S(2)}, u32[]{:S(2)}) collective-permute-start(bf16[2,128,256]{2,1,0:T(8,128)(2,1)S(1)} %get-tuple-element.76), channel_id=1, source_target_pairs={{0,8},{8,0},{16,24},{24,16},{1,9},{9,1},{17,25},{25,17},{2,10},{10... | collective-permute-start | bytes 393224 | tf_op jit(solution)/shard_map/ppermute | solution.py:268
  23.6 8.2 %copy-start.2 = (bf16[4,16,128,128]{3,2,1,0:T(8,128)(2,1)S(1)}, bf16[4,16,128,128]{3,2,1,0:T(8,128)(2,1)}, u32[]{:S(2)}) copy-start(bf16[4,16,128,128]{3,2,1,0:T(8,128)(2,1)} %refs_3_.1) | copy-start | bytes 6291460
  23.6 6.2 %collective-permute-start.3 = (bf16[512,256]{1,0:T(8,128)(2,1)S(1)}, bf16[512,256]{1,0:T(8,128)(2,1)S(1)}, u32[]{:S(2)}, u32[]{:S(2)}) collective-permute-start(bf16[512,256]{1,0:T(8,128)(2,1)S(1)} %get-tuple-element.134), channel_id=1, source_target_pairs={{0,1},{1,0},{2,3},{3,2},{4,5},{5,4},{6,7},{7,6},{8,9},{9,8},{10,11... | collective-permute-start | bytes 786440 | tf_op jit(solution)/shard_map/ppermute | solution.py:265
  29.0 1.6 %collective-permute-start.6 = (bf16[512,256]{1,0:T(8,128)(2,1)S(1)}, bf16[512,256]{1,0:T(8,128)(2,1)S(1)}, u32[]{:S(2)}, u32[]{:S(2)}) collective-permute-start(bf16[512,256]{1,0:T(8,128)(2,1)S(1)} %get-tuple-element.83), channel_id=1, source_target_pairs={{0,1},{1,0},{2,3},{3,2},{4,5},{5,4},{6,7},{7,6},{8,9},{9,8},{10,11... | collective-permute-start | bytes 786440 | tf_op jit(solution)/shard_map/ppermute | solution.py:265
  29.1 10.1 %collective-permute-start.8 = (bf16[512,256]{1,0:T(8,128)(2,1)S(1)}, bf16[512,256]{1,0:T(8,128)(2,1)S(1)}, u32[]{:S(2)}, u32[]{:S(2)}) collective-permute-start(bf16[512,256]{1,0:T(8,128)(2,1)S(1)} %get-tuple-element.84.refs_2_), channel_id=1, source_target_pairs={{0,2},{2,6},{6,4},{4,0},{1,3},{3,7},{7,5},{5,1},{8,10},{10,14},{14... | collective-permute-start | bytes 786440 | tf_op jit(solution)/shard_map/ppermute | solution.py:272
  29.6 2.2 %collective-permute-start.4 = (s32[4,16]{1,0:T(4,128)S(1)}, s32[4,16]{1,0:T(4,128)S(1)}, u32[]{:S(2)}, u32[]{:S(2)}) collective-permute-start(s32[4,16]{1,0:T(4,128)S(1)} %fusion.refs_1_), channel_id=1, source_target_pairs={{0,1},{1,0},{2,3},{3,2},{4,5},{5,4},{6,7},{7,6},{8,9},{9,8},{10,11... | collective-permute-start | bytes 776 | tf_op jit(solution)/shard_map/ppermute | solution.py:265
  30.6 14.2 %collective-permute-start.7 = (bf16[512,256]{1,0:T(8,128)(2,1)S(1)}, bf16[512,256]{1,0:T(8,128)(2,1)S(1)}, u32[]{:S(2)}, u32[]{:S(2)}) collective-permute-start(bf16[512,256]{1,0:T(8,128)(2,1)S(1)} %collective-permute-done.6.refs_3_), channel_id=1, source_target_pairs={{0,2},{2,6},{6,4},{4,0},{1,3},{3,7},{7,5},{5,1},{8,10},{10,14},{14... | collective-permute-start | bytes 786440 | tf_op jit(solution)/shard_map/ppermute | solution.py:272
  39.1 11.2 %collective-permute-start.9 = (bf16[512,256]{1,0:T(8,128)(2,1)S(1)}, bf16[512,256]{1,0:T(8,128)(2,1)S(1)}, u32[]{:S(2)}, u32[]{:S(2)}) collective-permute-start(bf16[512,256]{1,0:T(8,128)(2,1)S(1)} %collective-permute-done.8.refs_2_), channel_id=1, source_target_pairs={{0,2},{2,6},{6,4},{4,0},{1,3},{3,7},{7,5},{5,1},{8,10},{10,14},{14... | collective-permute-start | bytes 786440 | tf_op jit(solution)/shard_map/ppermute | solution.py:272
  44.7 13.8 %collective-permute-start.11 = (bf16[512,256]{1,0:T(8,128)(2,1)S(1)}, bf16[512,256]{1,0:T(8,128)(2,1)S(1)}, u32[]{:S(2)}, u32[]{:S(2)}) collective-permute-start(bf16[512,256]{1,0:T(8,128)(2,1)S(1)} %collective-permute-done.7.refs_3_), channel_id=1, source_target_pairs={{0,2},{2,6},{6,4},{4,0},{1,3},{3,7},{7,5},{5,1},{8,10},{10,14},{14... | collective-permute-start | bytes 786440 | tf_op jit(solution)/shard_map/ppermute | solution.py:272
  44.7 15.5 %collective-permute-start.13 = (bf16[128,1024]{1,0:T(8,128)(2,1)S(1)}, bf16[128,1024]{1,0:T(8,128)(2,1)S(1)}, u32[]{:S(2)}, u32[]{:S(2)}) collective-permute-start(bf16[128,1024]{1,0:T(8,128)(2,1)S(1)} %get-tuple-element.105), channel_id=1, source_target_pairs={{0,8},{8,0},{16,24},{24,16},{1,9},{9,1},{17,25},{25,17},{2,10},{10... | collective-permute-start | bytes 786440 | tf_op jit(solution)/shard_map/ppermute | solution.py:268
  45.5 14.8 %collective-permute-start.14 = (bf16[128,1024]{1,0:T(8,128)(2,1)S(1)}, bf16[128,1024]{1,0:T(8,128)(2,1)S(1)}, u32[]{:S(2)}, u32[]{:S(2)}) collective-permute-start(bf16[128,1024]{1,0:T(8,128)(2,1)S(1)} %get-tuple-element.106), channel_id=1, source_target_pairs={{0,16},{8,24},{16,0},{24,8},{1,17},{9,25},{17,1},{25,9},{2,18},{10... | collective-permute-start | bytes 786440 | tf_op jit(solution)/shard_map/ppermute | solution.py:268
  50.4 9.9 %collective-permute-start.15 = (bf16[128,1024]{1,0:T(8,128)(2,1)S(1)}, bf16[128,1024]{1,0:T(8,128)(2,1)S(1)}, u32[]{:S(2)}, u32[]{:S(2)}) collective-permute-start(bf16[128,1024]{1,0:T(8,128)(2,1)S(1)} %get-tuple-element.107), channel_id=1, source_target_pairs={{0,24},{8,16},{16,8},{24,0},{1,25},{9,17},{17,9},{25,1},{2,26},{10... | collective-permute-start | bytes 786440 | tf_op jit(solution)/shard_map/ppermute | solution.py:268
  51.5 11.4 %collective-permute-start.10 = (bf16[512,256]{1,0:T(8,128)(2,1)S(1)}, bf16[512,256]{1,0:T(8,128)(2,1)S(1)}, u32[]{:S(2)}, u32[]{:S(2)}) collective-permute-start(bf16[512,256]{1,0:T(8,128)(2,1)S(1)} %collective-permute-done.9.refs_2_), channel_id=1, source_target_pairs={{0,2},{2,6},{6,4},{4,0},{1,3},{3,7},{7,5},{5,1},{8,10},{10,14},{14... | collective-permute-start | bytes 786440 | tf_op jit(solution)/shard_map/ppermute | solution.py:272
  58.5 8.3 %collective-permute-start.12 = (bf16[512,256]{1,0:T(8,128)(2,1)S(1)}, bf16[512,256]{1,0:T(8,128)(2,1)S(1)}, u32[]{:S(2)}, u32[]{:S(2)}) collective-permute-start(bf16[512,256]{1,0:T(8,128)(2,1)S(1)} %collective-permute-done.11.refs_3_), channel_id=1, source_target_pairs={{0,2},{2,6},{6,4},{4,0},{1,3},{3,7},{7,5},{5,1},{8,10},{10,14},{14... | collective-permute-start | bytes 786440 | tf_op jit(solution)/shard_map/ppermute | solution.py:272
  60.6 38.9 %collective-permute-start.17 = (bf16[1024,512]{1,0:T(8,128)(2,1)S(1)}, bf16[1024,512]{1,0:T(8,128)(2,1)S(1)}, u32[]{:S(2)}, u32[]{:S(2)}) collective-permute-start(bf16[1024,512]{1,0:T(8,128)(2,1)S(1)} %get-tuple-element.113.refs_0_), channel_id=1, source_target_pairs={{0,1},{1,0},{2,3},{3,2},{4,5},{5,4},{6,7},{7,6},{8,9},{9,8},{10,11... | collective-permute-start | bytes 3145736 | tf_op jit(solution)/shard_map/ppermute | solution.py:265
  68.4 8.3 %collective-permute-start.21 = (bf16[512,256]{1,0:T(8,128)(2,1)S(1)}, bf16[512,256]{1,0:T(8,128)(2,1)S(1)}, u32[]{:S(2)}, u32[]{:S(2)}) collective-permute-start(bf16[512,256]{1,0:T(8,128)(2,1)S(1)} %get-tuple-element.125), channel_id=1, source_target_pairs={{0,4},{2,0},{6,2},{4,6},{1,5},{3,1},{7,3},{5,7},{8,12},{10,8},{14,... | collective-permute-start | bytes 786440 | tf_op jit(solution)/shard_map/ppermute | solution.py:272
  70.0 10.7 %collective-permute-start.16 = (bf16[512,256]{1,0:T(8,128)(2,1)S(1)}, bf16[512,256]{1,0:T(8,128)(2,1)S(1)}, u32[]{:S(2)}, u32[]{:S(2)}) collective-permute-start(bf16[512,256]{1,0:T(8,128)(2,1)S(1)} %get-tuple-element.112), channel_id=1, source_target_pairs={{0,1},{1,0},{2,3},{3,2},{4,5},{5,4},{6,7},{7,6},{8,9},{9,8},{10,11... | collective-permute-start | bytes 786440 | tf_op jit(solution)/shard_map/ppermute | solution.py:265
  70.0 12.3 %collective-permute-start.18 = (bf16[512,256]{1,0:T(8,128)(2,1)S(1)}, bf16[512,256]{1,0:T(8,128)(2,1)S(1)}, u32[]{:S(2)}, u32[]{:S(2)}) collective-permute-start(bf16[512,256]{1,0:T(8,128)(2,1)S(1)} %get-tuple-element.119), channel_id=1, source_target_pairs={{0,4},{2,0},{6,2},{4,6},{1,5},{3,1},{7,3},{5,7},{8,12},{10,8},{14,... | collective-permute-start | bytes 786440 | tf_op jit(solution)/shard_map/ppermute | solution.py:272
  77.3 10.6 %collective-permute-start.22 = (bf16[512,256]{1,0:T(8,128)(2,1)S(1)}, bf16[512,256]{1,0:T(8,128)(2,1)S(1)}, u32[]{:S(2)}, u32[]{:S(2)}) collective-permute-start(bf16[512,256]{1,0:T(8,128)(2,1)S(1)} %get-tuple-element.126), channel_id=1, source_target_pairs={{0,4},{2,0},{6,2},{4,6},{1,5},{3,1},{7,3},{5,7},{8,12},{10,8},{14,... | collective-permute-start | bytes 786440 | tf_op jit(solution)/shard_map/ppermute | solution.py:272
  82.9 10.6 %collective-permute-start.19 = (bf16[512,256]{1,0:T(8,128)(2,1)S(1)}, bf16[512,256]{1,0:T(8,128)(2,1)S(1)}, u32[]{:S(2)}, u32[]{:S(2)}) collective-permute-start(bf16[512,256]{1,0:T(8,128)(2,1)S(1)} %get-tuple-element.120), channel_id=1, source_target_pairs={{0,4},{2,0},{6,2},{4,6},{1,5},{3,1},{7,3},{5,7},{8,12},{10,8},{14,... | collective-permute-start | bytes 786440 | tf_op jit(solution)/shard_map/ppermute | solution.py:272
  88.6 10.4 %collective-permute-start.23 = (bf16[512,256]{1,0:T(8,128)(2,1)S(1)}, bf16[512,256]{1,0:T(8,128)(2,1)S(1)}, u32[]{:S(2)}, u32[]{:S(2)}) collective-permute-start(bf16[512,256]{1,0:T(8,128)(2,1)S(1)} %get-tuple-element.127), channel_id=1, source_target_pairs={{0,4},{2,0},{6,2},{4,6},{1,5},{3,1},{7,3},{5,7},{8,12},{10,8},{14,... | collective-permute-start | bytes 786440 | tf_op jit(solution)/shard_map/ppermute | solution.py:272
  94.2 8.7 %collective-permute-start.20 = (bf16[512,256]{1,0:T(8,128)(2,1)S(1)}, bf16[512,256]{1,0:T(8,128)(2,1)S(1)}, u32[]{:S(2)}, u32[]{:S(2)}) collective-permute-start(bf16[512,256]{1,0:T(8,128)(2,1)S(1)} %get-tuple-element.121), channel_id=1, source_target_pairs={{0,4},{2,0},{6,2},{4,6},{1,5},{3,1},{7,3},{5,7},{8,12},{10,8},{14,... | collective-permute-start | bytes 786440 | tf_op jit(solution)/shard_map/ppermute | solution.py:272
  103.9 6.6 %collective-permute-start.24 = (bf16[256,256]{1,0:T(8,128)(2,1)S(1)}, bf16[256,256]{1,0:T(8,128)(2,1)S(1)}, u32[]{:S(2)}, u32[]{:S(2)}) collective-permute-start(bf16[256,256]{1,0:T(8,128)(2,1)S(1)} %get-tuple-element.128), channel_id=1, source_target_pairs={{0,24},{8,16},{16,8},{24,0},{1,25},{9,17},{17,9},{25,1},{2,26},{10... | collective-permute-start | bytes 393224 | tf_op jit(solution)/shard_map/ppermute | solution.py:268
  105.6 6.0 %collective-permute-start.25 = (bf16[256,256]{1,0:T(8,128)(2,1)S(1)}, bf16[256,256]{1,0:T(8,128)(2,1)S(1)}, u32[]{:S(2)}, u32[]{:S(2)}) collective-permute-start(bf16[256,256]{1,0:T(8,128)(2,1)S(1)} %get-tuple-element.129), channel_id=1, source_target_pairs={{0,16},{8,24},{16,0},{24,8},{1,17},{9,25},{17,1},{25,9},{2,18},{10... | collective-permute-start | bytes 393224 | tf_op jit(solution)/shard_map/ppermute | solution.py:268
  106.8 5.0 %collective-permute-start.26 = (bf16[256,256]{1,0:T(8,128)(2,1)S(1)}, bf16[256,256]{1,0:T(8,128)(2,1)S(1)}, u32[]{:S(2)}, u32[]{:S(2)}) collective-permute-start(bf16[256,256]{1,0:T(8,128)(2,1)S(1)} %get-tuple-element.130), channel_id=1, source_target_pairs={{0,8},{8,0},{16,24},{24,16},{1,9},{9,1},{17,25},{25,17},{2,10},{10... | collective-permute-start | bytes 393224 | tf_op jit(solution)/shard_map/ppermute | solution.py:268
  111.8 5.1 %collective-permute-start.27 = (bf16[256,256]{1,0:T(8,128)(2,1)S(1)}, bf16[256,256]{1,0:T(8,128)(2,1)S(1)}, u32[]{:S(2)}, u32[]{:S(2)}) collective-permute-start(bf16[256,256]{1,0:T(8,128)(2,1)S(1)} %sum.3.refs_0_), channel_id=1, source_target_pairs={{0,2},{2,0},{4,6},{6,4},{1,3},{3,1},{5,7},{7,5},{8,10},{10,8},{12,... | collective-permute-start | bytes 393224 | tf_op jit(solution)/shard_map/ppermute | solution.py:429
  116.9 8.0 %collective-permute-start.28 = (bf16[256,256]{1,0:T(8,128)(2,1)S(1)}, bf16[256,256]{1,0:T(8,128)(2,1)S(1)}, u32[]{:S(2)}, u32[]{:S(2)}) collective-permute-start(bf16[256,256]{1,0:T(8,128)(2,1)S(1)} %sum.4.refs_0_), channel_id=1, source_target_pairs={{0,4},{2,6},{4,0},{6,2},{1,5},{3,7},{5,1},{7,3},{8,12},{10,14},{12... | collective-permute-start | bytes 393224 | tf_op jit(solution)/shard_map/ppermute | solution.py:429
  124.9 5.0 %collective-permute-start.29 = (bf16[256,256]{1,0:T(8,128)(2,1)S(1)}, bf16[256,256]{1,0:T(8,128)(2,1)S(1)}, u32[]{:S(2)}, u32[]{:S(2)}) collective-permute-start(bf16[256,256]{1,0:T(8,128)(2,1)S(1)} %sum.5.refs_1_), channel_id=1, source_target_pairs={{0,8},{8,0},{16,24},{24,16},{1,9},{9,1},{17,25},{25,17},{2,10},{10... | collective-permute-start | bytes 393224 | tf_op jit(solution)/shard_map/ppermute | solution.py:268
  126.6 6.4 %collective-permute-start.30 = (bf16[256,256]{1,0:T(8,128)(2,1)S(1)}, bf16[256,256]{1,0:T(8,128)(2,1)S(1)}, u32[]{:S(2)}, u32[]{:S(2)}) collective-permute-start(bf16[256,256]{1,0:T(8,128)(2,1)S(1)} %sum.5.refs_1_), channel_id=1, source_target_pairs={{0,16},{8,24},{16,0},{24,8},{1,17},{9,25},{17,1},{25,9},{2,18},{10... | collective-permute-start | bytes 393224 | tf_op jit(solution)/shard_map/ppermute | solution.py:268
  126.6 6.4 %collective-permute-start.31 = (bf16[256,256]{1,0:T(8,128)(2,1)S(1)}, bf16[256,256]{1,0:T(8,128)(2,1)S(1)}, u32[]{:S(2)}, u32[]{:S(2)}) collective-permute-start(bf16[256,256]{1,0:T(8,128)(2,1)S(1)} %sum.5.refs_1_), channel_id=1, source_target_pairs={{0,24},{8,16},{16,8},{24,0},{1,25},{9,17},{17,9},{25,1},{2,26},{10... | collective-permute-start | bytes 393224 | tf_op jit(solution)/shard_map/ppermute | solution.py:268
  128.5 5.9 %collective-permute-start.32 = (bf16[256,256]{1,0:T(8,128)(2,1)S(1)}, bf16[256,256]{1,0:T(8,128)(2,1)S(1)}, u32[]{:S(2)}, u32[]{:S(2)}) collective-permute-start(bf16[256,256]{1,0:T(8,128)(2,1)S(1)} %sum.5.refs_1_), channel_id=1, source_target_pairs={{0,1},{1,0},{2,3},{3,2},{4,5},{5,4},{6,7},{7,6},{8,9},{9,8},{10,11... | collective-permute-start | bytes 393224 | tf_op jit(solution)/shard_map/ppermute | solution.py:265
  129.9 4.5 %collective-permute-start.33 = (bf16[256,256]{1,0:T(8,128)(2,1)S(1)}, bf16[256,256]{1,0:T(8,128)(2,1)S(1)}, u32[]{:S(2)}, u32[]{:S(2)}) collective-permute-start(bf16[256,256]{1,0:T(8,128)(2,1)S(1)} %collective-permute-done.29.refs_2_), channel_id=1, source_target_pairs={{0,1},{1,0},{2,3},{3,2},{4,5},{5,4},{6,7},{7,6},{8,9},{9,8},{10,11... | collective-permute-start | bytes 393224 | tf_op jit(solution)/shard_map/ppermute | solution.py:265
  133.0 1.4 %collective-permute-start.34 = (bf16[256,256]{1,0:T(8,128)(2,1)S(1)}, bf16[256,256]{1,0:T(8,128)(2,1)S(1)}, u32[]{:S(2)}, u32[]{:S(2)}) collective-permute-start(bf16[256,256]{1,0:T(8,128)(2,1)S(1)} %collective-permute-done.30.refs_3_), channel_id=1, source_target_pairs={{0,1},{1,0},{2,3},{3,2},{4,5},{5,4},{6,7},{7,6},{8,9},{9,8},{10,11... | collective-permute-start | bytes 393224 | tf_op jit(solution)/shard_map/ppermute | solution.py:265
  133.0 1.5 %collective-permute-start.35 = (bf16[256,256]{1,0:T(8,128)(2,1)S(1)}, bf16[256,256]{1,0:T(8,128)(2,1)S(1)}, u32[]{:S(2)}, u32[]{:S(2)}) collective-permute-start(bf16[256,256]{1,0:T(8,128)(2,1)S(1)} %collective-permute-done.31.refs_4_), channel_id=1, source_target_pairs={{0,1},{1,0},{2,3},{3,2},{4,5},{5,4},{6,7},{7,6},{8,9},{9,8},{10,11... | collective-permute-start | bytes 393224 | tf_op jit(solution)/shard_map/ppermute | solution.py:265

commit v18 on v17

--- a/solution.py
+++ b/solution.py
@@ -386,7 +386,6 @@
             "back", 1,
         )
 
-    come = to_core(hidden_b)
     for k in range(z.zz - 2, -1, -1):
         came = [to_zz(part, -1) for part in came]
         mine = back(k)
@@ -394,11 +393,14 @@
             passed = [
                 call(
                     pass_kernel, [((rows, half), BF16)], [("v", part), ("v", moved)], "pass", 0.5,
-                    after=[come] if i == 1 and k == z.zz - 2 else (), token=True,
+                    token=True,
                 )
                 for i, (part, moved) in enumerate(zip(mine, came))
             ]
             came = [part for part, _ in passed]
+            if k == 1:
+                hidden_b, token = lax.optimization_barrier((hidden_b, passed[1][1]))
+                come = to_core(hidden_b)
     first = core == 0
     hidden = jnp.concatenate(
         [jnp.where(first, hidden_a, come), jnp.where(first, come, hidden_a)], axis=1
@@ -408,6 +410,7 @@
     (part,) = call(
         part_kernel, [((width_in, half), F32)],
         [("v", value) for value in (lefts[0], mine[0], came[0])], "part", 1,
+        after=[come, token],
     )
     terms = call(
         lambda *refs: grad_kernel(z, *refs),

time: 137 us -> 139 us (1.015)
  waiting for transfers between devices: 55.5 us -> 62.6 us
  starting transfers between devices: 45.7 us -> 41.6 us
    ppermute x12, waiting for transfers between devices: 28.8 us -> 33.6 us  [to_zz(): lax.ppermute(x, 'zz', [(order[i], order[(i + k) % z.zz]) for i in range(z...]
    ppermute x12, starting transfers between devices: 18.7 us -> 14.8 us  [to_zz(): lax.ppermute(x, 'zz', [(order[i], order[(i + k) % z.zz]) for i in range(z...]
    ppermute x12, waiting for transfers between devices: 14 us -> 16 us  [to_grp(): lax.ppermute(x, 'grp', [(i, i ^ s) for i in range(z.grp)])]
  transfers between devices with their start and end apart: 37 -> 37, of which waited for: 22 -> 20; matrix products, arithmetic and copies ran while one was open for 1% -> 1% of each run, Pallas kernels for 19% -> 18%
where the time goes in v18:
time: 139 us
  waiting for transfers between devices  62.6 us (45%)
  starting transfers between devices  41.6 us (30%)
  Pallas kernels  29.7 us (21%)
  local copies, waits for them, and re-layouts  3.19 us (2%)
    ppermute x12, waiting for transfers between devices, to_zz(): lax.ppermute(x, 'zz', [(order[i], order[(i + k) % z.zz]) for i in range(z...  33.6 us
    pallas_call x25, Pallas kernels, call(): pl.pallas_call(kernel, out_shape=tuple((jax.ShapeDtypeStruct(s, d) for s,...  29.7 us
    ppermute x12, waiting for transfers between devices, to_grp(): lax.ppermute(x, 'grp', [(i, i ^ s) for i in range(z.grp)])  16 us
    ppermute x12, starting transfers between devices, to_zz(): lax.ppermute(x, 'zz', [(order[i], order[(i + k) % z.zz]) for i in range(z...  14.8 us
    ppermute x12, starting transfers between devices, to_grp(): lax.ppermute(x, 'grp', [(i, i ^ s) for i in range(z.grp)])  13.6 us
    ppermute x2, waiting for transfers between devices, shards(): lax.ppermute(mine, 'zz', [(i, i ^ step) for i in range(z.zz)])  8.37 us
    all_to_all x1, starting transfers between devices, shards(): lax.all_to_all(message, ('grp', 'zz', 'core'), split_axis=0, concat_axis=...  6.96 us
    ppermute x2, starting transfers between devices, shards(): lax.ppermute(mine, 'zz', [(i, i ^ step) for i in range(z.zz)])  4.72 us
  transfers between devices with their start and end apart: 37, of which 20 were waited for; matrix products, arithmetic and copies ran while one was open for 1% of the time, Pallas kernels for 18%

profile of v18, /device:TPU:0, one launch (start us, length us, event | category | flops | bytes accessed | tf_op | source)
XLA Modules:
  0.0 138.9 jit_solution(10260327228689575192)
XLA Ops:
  1.9 1.8 %index.1 = s32[32,8,128]{2,1,0:T(8,128)} custom-call(s32[3]{0:T(128)S(1)} %pad_add_fusion.refs_0_, s32[1,512]{1,0:T(1,128)S(1)} %bitcast.4), custom_call_target="tpu_custom_call" | custom-call | flops 100000000 | tf_op jit(solution)/shard_map/index/pallas_call | solution.py:59
  3.7 7.0 %all-to-all-start = ((s32[32,8,128]{2,1,0:T(8,128)}), s32[32,8,128]{2,1,0:T(8,128)S(1)}, u32[]{:S(2)}, u32[]{:S(2)}) async-start(s32[32,8,128]{2,1,0:T(8,128)} %index.1), calls=%async_computation | async-start | bytes 262144 | tf_op jit(solution)/shard_map/all_to_all | solution.py:282
  10.6 1.2 copy-done
  11.9 1.2 copy-done.3
  13.1 1.3 product.1
  14.4 4.4 %all-to-all-done.refs_1_.refs_2_ = s32[32,8,128]{2,1,0:T(8,128)S(1)} async-done(((s32[32,8,128]{2,1,0:T(8,128)}), s32[32,8,128]{2,1,0:T(8,128)S(1)}, u32[]{:S(2)}, u32[]{:S(2)}) %all-to-all-start) | async-done | bytes 131104 | tf_op jit(solution)/shard_map/all_to_all | solution.py:282
  18.8 1.2 send.1
  20.0 1.0 collective-permute-start
  21.1 1.3 collective-permute-start.1
  22.4 1.2 collective-permute-start.2
  23.7 3.7 %collective-permute-done.refs_0_ = bf16[2,128,256]{2,1,0:T(8,128)(2,1)S(1)} collective-permute-done((bf16[2,128,256]{2,1,0:T(8,128)(2,1)S(1)}, bf16[2,128,256]{2,1,0:T(8,128)(2,1)S(1)}, u32[]{:S(2)}, u32[]{:S(2)}) %collective-permute-start) | collective-permute-done | bytes 131104 | tf_op jit(solution)/shard_map/ppermute | solution.py:268
  27.4 1.6 %collective-permute-done.1.refs_1_ = bf16[2,128,256]{2,1,0:T(8,128)(2,1)S(1)} collective-permute-done((bf16[2,128,256]{2,1,0:T(8,128)(2,1)S(1)}, bf16[2,128,256]{2,1,0:T(8,128)(2,1)S(1)}, u32[]{:S(2)}, u32[]{:S(2)}) %collective-permute-start.1) | collective-permute-done | bytes 131104 | tf_op jit(solution)/shard_map/ppermute | solution.py:268
  30.6 1.2 collective-permute-start.7
  31.8 5.9 %prepare.2 = (bf16[1024,512]{1,0:T(8,128)(2,1)S(1)}, bf16[1024,512]{1,0:T(8,128)(2,1)S(1)}, bf16[1024,512]{1,0:T(8,128)(2,1)S(1)}, bf16[1024,512]{1,0:T(8,128)(2,1)S(1)}, f32[8,128]{1,0:T(8,128)S(1)}) custom-call(s32[3]{0:T(128)S(1)} %pad_add_fusion.refs_0_, s32[4,16]{1,0:T(4,128)S(1)} %fusion.refs_1_, s32[32,8,128]{2,1,0:T(8,128)S(1)} %all-to-all-done.refs_1_.refs_2_, ...), custom_call_target="tpu_custom_call" | custom-call | flops 700000000 | tf_op jit(solution)/shard_map/prepare/pallas_call | solution.py:59
  37.7 1.4 %collective-permute-done.8.refs_2_ = bf16[512,256]{1,0:T(8,128)(2,1)S(1)} collective-permute-done((bf16[512,256]{1,0:T(8,128)(2,1)S(1)}, bf16[512,256]{1,0:T(8,128)(2,1)S(1)}, u32[]{:S(2)}, u32[]{:S(2)}) %collective-permute-start.8) | collective-permute-done | bytes 262176 | tf_op jit(solution)/shard_map/ppermute | solution.py:272
  39.1 5.6 %collective-permute-done.7.refs_3_ = bf16[512,256]{1,0:T(8,128)(2,1)S(1)} collective-permute-done((bf16[512,256]{1,0:T(8,128)(2,1)S(1)}, bf16[512,256]{1,0:T(8,128)(2,1)S(1)}, u32[]{:S(2)}, u32[]{:S(2)}) %collective-permute-start.7) | collective-permute-done | bytes 262176 | tf_op jit(solution)/shard_map/ppermute | solution.py:272
  45.5 1.0 collective-permute-start.14
  46.5 3.9 %collective-permute-done.9.refs_2_ = bf16[512,256]{1,0:T(8,128)(2,1)S(1)} collective-permute-done((bf16[512,256]{1,0:T(8,128)(2,1)S(1)}, bf16[512,256]{1,0:T(8,128)(2,1)S(1)}, u32[]{:S(2)}, u32[]{:S(2)}) %collective-permute-start.9) | collective-permute-done | bytes 262176 | tf_op jit(solution)/shard_map/ppermute | solution.py:272
  50.4 1.2 collective-permute-start.15
  51.5 6.9 %prepare.3 = (bf16[1024,512]{1,0:T(8,128)(2,1)S(1)}, bf16[1024,512]{1,0:T(8,128)(2,1)S(1)}, bf16[1024,512]{1,0:T(8,128)(2,1)S(1)}, bf16[1024,512]{1,0:T(8,128)(2,1)S(1)}, f32[8,128]{1,0:T(8,128)S(1)}) custom-call(s32[3]{0:T(128)S(1)} %pad_add_fusion.refs_0_, s32[4,16]{1,0:T(4,128)S(1)} %collective-permute-done.4.refs_5_.refs_1_, ...), custom_call_target="tpu_custom_call" | custom-call | flops 700000000 | tf_op jit(solution)/shard_map/prepare/pallas_call | solution.py:59
  58.5 1.7 %collective-permute-start.12 = (bf16[512,256]{1,0:T(8,128)(2,1)S(1)}, bf16[512,256]{1,0:T(8,128)(2,1)S(1)}, u32[]{:S(2)}, u32[]{:S(2)}) collective-permute-start(bf16[512,256]{1,0:T(8,128)(2,1)S(1)} %collective-permute-done.11.refs_3_), channel_id=1, source_target_pairs={{0,2},{2,6},{6,4},{4,0},{1,3},{3,7},{7,5},{5,1},{8,10},{10,14},{14... | collective-permute-start | bytes 786440 | tf_op jit(solution)/shard_map/ppermute | solution.py:272
  63.0 3.8 %collective-permute-done.12.refs_3_ = bf16[512,256]{1,0:T(8,128)(2,1)S(1)} collective-permute-done((bf16[512,256]{1,0:T(8,128)(2,1)S(1)}, bf16[512,256]{1,0:T(8,128)(2,1)S(1)}, u32[]{:S(2)}, u32[]{:S(2)}) %collective-permute-start.12) | collective-permute-done | bytes 262176 | tf_op jit(solution)/shard_map/ppermute | solution.py:272
  66.8 1.6 %forward.7 = (bf16[512,256]{1,0:T(8,128)(2,1)S(1)}, bf16[512,256]{1,0:T(8,128)(2,1)S(1)}, bf16[512,256]{1,0:T(8,128)(2,1)S(1)}, bf16[512,256]{1,0:T(8,128)(2,1)S...) custom-call(bf16[1024,512]{1,0:T(8,128)(2,1)S(1)} %get-tuple-element.85.refs_0_.refs_8_, ...), custom_call_target="tpu_custom_call" | custom-call | flops 300000000 | tf_op jit(solution)/shard_map/forward/pallas_call | solution.py:59
  68.4 1.6 %collective-permute-start.21 = (bf16[512,256]{1,0:T(8,128)(2,1)S(1)}, bf16[512,256]{1,0:T(8,128)(2,1)S(1)}, u32[]{:S(2)}, u32[]{:S(2)}) collective-permute-start(bf16[512,256]{1,0:T(8,128)(2,1)S(1)} %get-tuple-element.130), channel_id=1, source_target_pairs={{0,4},{2,0},{6,2},{4,6},{1,5},{3,1},{7,3},{5,7},{8,12},{10,8},{14,... | collective-permute-start | bytes 786440 | tf_op jit(solution)/shard_map/ppermute | solution.py:272
  70.8 6.9 %collective-permute-done.21.refs_1_ = bf16[512,256]{1,0:T(8,128)(2,1)S(1)} collective-permute-done((bf16[512,256]{1,0:T(8,128)(2,1)S(1)}, bf16[512,256]{1,0:T(8,128)(2,1)S(1)}, u32[]{:S(2)}, u32[]{:S(2)}) %collective-permute-start.21) | collective-permute-done | bytes 262176 | tf_op jit(solution)/shard_map/ppermute | solution.py:272
  78.3 2.5 %collective-permute-start.22 = (bf16[512,256]{1,0:T(8,128)(2,1)S(1)}, bf16[512,256]{1,0:T(8,128)(2,1)S(1)}, u32[]{:S(2)}, u32[]{:S(2)}) collective-permute-start(bf16[512,256]{1,0:T(8,128)(2,1)S(1)} %get-tuple-element.131), channel_id=1, source_target_pairs={{0,4},{2,0},{6,2},{4,6},{1,5},{3,1},{7,3},{5,7},{8,12},{10,8},{14,... | collective-permute-start | bytes 786440 | tf_op jit(solution)/shard_map/ppermute | solution.py:272
  80.8 2.5 %collective-permute-done.16.refs_1_ = bf16[512,256]{1,0:T(8,128)(2,1)S(1)} collective-permute-done((bf16[512,256]{1,0:T(8,128)(2,1)S(1)}, bf16[512,256]{1,0:T(8,128)(2,1)S(1)}, u32[]{:S(2)}, u32[]{:S(2)}) %collective-permute-start.16) | collective-permute-done | bytes 262176 | tf_op jit(solution)/shard_map/ppermute | solution.py:272
  83.9 2.5 %collective-permute-start.17 = (bf16[512,256]{1,0:T(8,128)(2,1)S(1)}, bf16[512,256]{1,0:T(8,128)(2,1)S(1)}, u32[]{:S(2)}, u32[]{:S(2)}) collective-permute-start(bf16[512,256]{1,0:T(8,128)(2,1)S(1)} %get-tuple-element.121), channel_id=1, source_target_pairs={{0,4},{2,0},{6,2},{4,6},{1,5},{3,1},{7,3},{5,7},{8,12},{10,8},{14,... | collective-permute-start | bytes 786440 | tf_op jit(solution)/shard_map/ppermute | solution.py:272
  87.1 1.8 %collective-permute-done.22.refs_1_ = bf16[512,256]{1,0:T(8,128)(2,1)S(1)} collective-permute-done((bf16[512,256]{1,0:T(8,128)(2,1)S(1)}, bf16[512,256]{1,0:T(8,128)(2,1)S(1)}, u32[]{:S(2)}, u32[]{:S(2)}) %collective-permute-start.22) | collective-permute-done | bytes 262176 | tf_op jit(solution)/shard_map/ppermute | solution.py:272
  89.5 2.5 %collective-permute-start.23 = (bf16[512,256]{1,0:T(8,128)(2,1)S(1)}, bf16[512,256]{1,0:T(8,128)(2,1)S(1)}, u32[]{:S(2)}, u32[]{:S(2)}) collective-permute-start(bf16[512,256]{1,0:T(8,128)(2,1)S(1)} %get-tuple-element.132), channel_id=1, source_target_pairs={{0,4},{2,0},{6,2},{4,6},{1,5},{3,1},{7,3},{5,7},{8,12},{10,8},{14,... | collective-permute-start | bytes 786440 | tf_op jit(solution)/shard_map/ppermute | solution.py:272
  92.0 2.5 %collective-permute-done.17.refs_1_ = bf16[512,256]{1,0:T(8,128)(2,1)S(1)} collective-permute-done((bf16[512,256]{1,0:T(8,128)(2,1)S(1)}, bf16[512,256]{1,0:T(8,128)(2,1)S(1)}, u32[]{:S(2)}, u32[]{:S(2)}) %collective-permute-start.17) | collective-permute-done | bytes 262176 | tf_op jit(solution)/shard_map/ppermute | solution.py:272
  94.6 2.3 %collective-permute-start.20 = (bf16[512,256]{1,0:T(8,128)(2,1)S(1)}, bf16[512,256]{1,0:T(8,128)(2,1)S(1)}, u32[]{:S(2)}, u32[]{:S(2)}) collective-permute-start(bf16[512,256]{1,0:T(8,128)(2,1)S(1)} %get-tuple-element.126), channel_id=1, source_target_pairs={{0,4},{2,0},{6,2},{4,6},{1,5},{3,1},{7,3},{5,7},{8,12},{10,8},{14,... | collective-permute-start | bytes 786440 | tf_op jit(solution)/shard_map/ppermute | solution.py:272
  98.1 5.2 %collective-permute-done.20.refs_3_ = bf16[512,256]{1,0:T(8,128)(2,1)S(1)} collective-permute-done((bf16[512,256]{1,0:T(8,128)(2,1)S(1)}, bf16[512,256]{1,0:T(8,128)(2,1)S(1)}, u32[]{:S(2)}, u32[]{:S(2)}) %collective-permute-start.20) | collective-permute-done | bytes 262176 | tf_op jit(solution)/shard_map/ppermute | solution.py:272
  103.3 1.0 grad.1
  104.3 1.5 %collective-permute-start.24 = (bf16[256,256]{1,0:T(8,128)(2,1)S(1)}, bf16[256,256]{1,0:T(8,128)(2,1)S(1)}, u32[]{:S(2)}, u32[]{:S(2)}) collective-permute-start(bf16[256,256]{1,0:T(8,128)(2,1)S(1)} %get-tuple-element.134), channel_id=1, source_target_pairs={{0,24},{8,16},{16,8},{24,0},{1,25},{9,17},{17,9},{25,1},{2,26},{10... | collective-permute-start | bytes 393224 | tf_op jit(solution)/shard_map/ppermute | solution.py:268
  105.8 1.2 collective-permute-start.25
  107.0 0.9 collective-permute-start.26
  107.9 3.7 %collective-permute-done.24.refs_0_ = bf16[256,256]{1,0:T(8,128)(2,1)S(1)} collective-permute-done((bf16[256,256]{1,0:T(8,128)(2,1)S(1)}, bf16[256,256]{1,0:T(8,128)(2,1)S(1)}, u32[]{:S(2)}, u32[]{:S(2)}) %collective-permute-start.24) | collective-permute-done | bytes 131104 | tf_op jit(solution)/shard_map/ppermute | solution.py:268
  111.6 1.4 collective-permute-done.25.refs_1_
  113.0 1.8 %collective-permute-start.27 = (bf16[256,256]{1,0:T(8,128)(2,1)S(1)}, bf16[256,256]{1,0:T(8,128)(2,1)S(1)}, u32[]{:S(2)}, u32[]{:S(2)}) collective-permute-start(bf16[256,256]{1,0:T(8,128)(2,1)S(1)} %sum.3.refs_0_), channel_id=1, source_target_pairs={{0,2},{2,0},{4,6},{6,4},{1,3},{3,1},{5,7},{7,5},{8,10},{10,8},{12,... | collective-permute-start | bytes 393224 | tf_op jit(solution)/shard_map/ppermute | solution.py:432
  114.8 3.4 %collective-permute-done.27.refs_1_ = bf16[256,256]{1,0:T(8,128)(2,1)S(1)} collective-permute-done((bf16[256,256]{1,0:T(8,128)(2,1)S(1)}, bf16[256,256]{1,0:T(8,128)(2,1)S(1)}, u32[]{:S(2)}, u32[]{:S(2)}) %collective-permute-start.27) | collective-permute-done | bytes 131104 | tf_op jit(solution)/shard_map/ppermute | solution.py:432
  118.2 2.9 %collective-permute-start.28 = (bf16[256,256]{1,0:T(8,128)(2,1)S(1)}, bf16[256,256]{1,0:T(8,128)(2,1)S(1)}, u32[]{:S(2)}, u32[]{:S(2)}) collective-permute-start(bf16[256,256]{1,0:T(8,128)(2,1)S(1)} %sum.4.refs_0_), channel_id=1, source_target_pairs={{0,4},{2,6},{4,0},{6,2},{1,5},{3,7},{5,1},{7,3},{8,12},{10,14},{12... | collective-permute-start | bytes 393224 | tf_op jit(solution)/shard_map/ppermute | solution.py:432
  121.2 5.0 %collective-permute-done.28.refs_1_ = bf16[256,256]{1,0:T(8,128)(2,1)S(1)} collective-permute-done((bf16[256,256]{1,0:T(8,128)(2,1)S(1)}, bf16[256,256]{1,0:T(8,128)(2,1)S(1)}, u32[]{:S(2)}, u32[]{:S(2)}) %collective-permute-start.28) | collective-permute-done | bytes 131104 | tf_op jit(solution)/shard_map/ppermute | solution.py:432
  126.2 1.5 %collective-permute-start.29 = (bf16[256,256]{1,0:T(8,128)(2,1)S(1)}, bf16[256,256]{1,0:T(8,128)(2,1)S(1)}, u32[]{:S(2)}, u32[]{:S(2)}) collective-permute-start(bf16[256,256]{1,0:T(8,128)(2,1)S(1)} %sum.5.refs_1_), channel_id=1, source_target_pairs={{0,8},{8,0},{16,24},{24,16},{1,9},{9,1},{17,25},{25,17},{2,10},{10... | collective-permute-start | bytes 393224 | tf_op jit(solution)/shard_map/ppermute | solution.py:268
  127.7 1.5 %collective-permute-start.30 = (bf16[256,256]{1,0:T(8,128)(2,1)S(1)}, bf16[256,256]{1,0:T(8,128)(2,1)S(1)}, u32[]{:S(2)}, u32[]{:S(2)}) collective-permute-start(bf16[256,256]{1,0:T(8,128)(2,1)S(1)} %sum.5.refs_1_), channel_id=1, source_target_pairs={{0,16},{8,24},{16,0},{24,8},{1,17},{9,25},{17,1},{25,9},{2,18},{10... | collective-permute-start | bytes 393224 | tf_op jit(solution)/shard_map/ppermute | solution.py:268
  129.8 2.7 %collective-permute-done.29.refs_2_ = bf16[256,256]{1,0:T(8,128)(2,1)S(1)} collective-permute-done((bf16[256,256]{1,0:T(8,128)(2,1)S(1)}, bf16[256,256]{1,0:T(8,128)(2,1)S(1)}, u32[]{:S(2)}, u32[]{:S(2)}) %collective-permute-start.29) | collective-permute-done | bytes 131104 | tf_op jit(solution)/shard_map/ppermute | solution.py:268
  132.4 3.0 %collective-permute-done.30.refs_3_ = bf16[256,256]{1,0:T(8,128)(2,1)S(1)} collective-permute-done((bf16[256,256]{1,0:T(8,128)(2,1)S(1)}, bf16[256,256]{1,0:T(8,128)(2,1)S(1)}, u32[]{:S(2)}, u32[]{:S(2)}) %collective-permute-start.30) | collective-permute-done | bytes 131104 | tf_op jit(solution)/shard_map/ppermute | solution.py:268
  136.9 2.0 %last.1 = f32[1024,512]{1,0:T(8,128)} custom-call(s32[3]{0:T(128)S(1)} %pad_add_fusion.refs_0_, bf16[256,256]{1,0:T(8,128)(2,1)S(1)} %sum.5.refs_1_, bf16[256,256]{1,0:T(8,128)(2,1)S(1)} %collective-permute-done.29.refs_2_, bf16[256,256]{1,0:T(8,128)(2,1)S(1)} %collective-permute-done.30.refs_3_, bf16[256,256]{1,0:T(8,128)(2,1)S(1)} %collective-permute-done.31.refs_4_, ...), custom_call_target="tpu_custom_call" | custom-call | flops 200000000 | tf_op jit(solution)/shard_map/last/pallas_call | solution.py:59
  (72 shorter events, 13.4 us)
Async XLA Ops:
  0.6 50.9 %collective-permute-start.5 = (bf16[4,16,128,128]{3,2,1,0:T(8,128)(2,1)}, bf16[4,16,128,128]{3,2,1,0:T(8,128)(2,1)}, u32[]{:S(2)}, u32[]{:S(2)}) collective-permute-start(bf16[4,16,128,128]{3,2,1,0:T(8,128)(2,1)} %refs_3_.1), channel_id=1, source_target_pairs={{0,1},{1,0},{2,3},{3,2},{4,5},{5,4},{6,7},{7,6},{8,9},{9,8},{10,11... | collective-permute-start | bytes 6291464 | tf_op jit(solution)/shard_map/ppermute | solution.py:265
  1.2 0.7 copy-start.4
  3.7 15.1 %all-to-all-start = ((s32[32,8,128]{2,1,0:T(8,128)}), s32[32,8,128]{2,1,0:T(8,128)S(1)}, u32[]{:S(2)}, u32[]{:S(2)}) async-start(s32[32,8,128]{2,1,0:T(8,128)} %index.1), calls=%async_computation | async-start | bytes 262144 | tf_op jit(solution)/shard_map/all_to_all | solution.py:282
  10.6 1.2 copy-start
  11.9 1.2 copy-start.3
  13.1 10.5 %copy-start.5 = (bf16[512,512]{1,0:T(8,128)(2,1)S(1)}, bf16[512,512]{1,0:T(8,128)(2,1)}, u32[]{:S(2)}) copy-start(bf16[512,512]{1,0:T(8,128)(2,1)} %param.13) | copy-start | bytes 1572868
  14.4 15.2 %copy-start.6 = (s32[4,16]{1,0:T(4,128)S(1)}, s32[4,16]{1,0:T(4,128)}, u32[]{:S(2)}) copy-start(s32[4,16]{1,0:T(4,128)} %param.9) | copy-start | bytes 772
  14.4 15.2 %copy-start.7 = (s32[4]{0:T(128)S(1)}, s32[4]{0:T(128)}, u32[]{:S(2)}) copy-start(s32[4]{0:T(128)} %param.10) | copy-start | bytes 52
  14.4 15.4 %copy-start.1 = (bf16[512,1024]{1,0:T(8,128)(2,1)S(1)}, bf16[512,1024]{1,0:T(8,128)(2,1)}, u32[]{:S(2)}) copy-start(bf16[512,1024]{1,0:T(8,128)(2,1)} %refs_1_.1) | copy-start | bytes 3145732
  20.0 7.3 %collective-permute-start = (bf16[2,128,256]{2,1,0:T(8,128)(2,1)S(1)}, bf16[2,128,256]{2,1,0:T(8,128)(2,1)S(1)}, u32[]{:S(2)}, u32[]{:S(2)}) collective-permute-start(bf16[2,128,256]{2,1,0:T(8,128)(2,1)S(1)} %get-tuple-element.77), channel_id=1, source_target_pairs={{0,24},{8,16},{16,8},{24,0},{1,25},{9,17},{17,9},{25,1},{2,26},{10... | collective-permute-start | bytes 393224 | tf_op jit(solution)/shard_map/ppermute | solution.py:268
  21.1 7.9 %collective-permute-start.1 = (bf16[2,128,256]{2,1,0:T(8,128)(2,1)S(1)}, bf16[2,128,256]{2,1,0:T(8,128)(2,1)S(1)}, u32[]{:S(2)}, u32[]{:S(2)}) collective-permute-start(bf16[2,128,256]{2,1,0:T(8,128)(2,1)S(1)} %get-tuple-element.78), channel_id=1, source_target_pairs={{0,16},{8,24},{16,0},{24,8},{1,17},{9,25},{17,1},{25,9},{2,18},{10... | collective-permute-start | bytes 393224 | tf_op jit(solution)/shard_map/ppermute | solution.py:268
  22.4 6.6 %collective-permute-start.2 = (bf16[2,128,256]{2,1,0:T(8,128)(2,1)S(1)}, bf16[2,128,256]{2,1,0:T(8,128)(2,1)S(1)}, u32[]{:S(2)}, u32[]{:S(2)}) collective-permute-start(bf16[2,128,256]{2,1,0:T(8,128)(2,1)S(1)} %get-tuple-element.79), channel_id=1, source_target_pairs={{0,8},{8,0},{16,24},{24,16},{1,9},{9,1},{17,25},{25,17},{2,10},{10... | collective-permute-start | bytes 393224 | tf_op jit(solution)/shard_map/ppermute | solution.py:268
  23.6 8.2 %copy-start.2 = (bf16[4,16,128,128]{3,2,1,0:T(8,128)(2,1)S(1)}, bf16[4,16,128,128]{3,2,1,0:T(8,128)(2,1)}, u32[]{:S(2)}) copy-start(bf16[4,16,128,128]{3,2,1,0:T(8,128)(2,1)} %refs_3_.1) | copy-start | bytes 6291460
  23.6 6.2 %collective-permute-start.3 = (bf16[512,256]{1,0:T(8,128)(2,1)S(1)}, bf16[512,256]{1,0:T(8,128)(2,1)S(1)}, u32[]{:S(2)}, u32[]{:S(2)}) collective-permute-start(bf16[512,256]{1,0:T(8,128)(2,1)S(1)} %get-tuple-element.140), channel_id=1, source_target_pairs={{0,1},{1,0},{2,3},{3,2},{4,5},{5,4},{6,7},{7,6},{8,9},{9,8},{10,11... | collective-permute-start | bytes 786440 | tf_op jit(solution)/shard_map/ppermute | solution.py:265
  29.0 1.6 %collective-permute-start.6 = (bf16[512,256]{1,0:T(8,128)(2,1)S(1)}, bf16[512,256]{1,0:T(8,128)(2,1)S(1)}, u32[]{:S(2)}, u32[]{:S(2)}) collective-permute-start(bf16[512,256]{1,0:T(8,128)(2,1)S(1)} %get-tuple-element.86), channel_id=1, source_target_pairs={{0,1},{1,0},{2,3},{3,2},{4,5},{5,4},{6,7},{7,6},{8,9},{9,8},{10,11... | collective-permute-start | bytes 786440 | tf_op jit(solution)/shard_map/ppermute | solution.py:265
  29.1 10.1 %collective-permute-start.8 = (bf16[512,256]{1,0:T(8,128)(2,1)S(1)}, bf16[512,256]{1,0:T(8,128)(2,1)S(1)}, u32[]{:S(2)}, u32[]{:S(2)}) collective-permute-start(bf16[512,256]{1,0:T(8,128)(2,1)S(1)} %get-tuple-element.87.refs_2_), channel_id=1, source_target_pairs={{0,2},{2,6},{6,4},{4,0},{1,3},{3,7},{7,5},{5,1},{8,10},{10,14},{14... | collective-permute-start | bytes 786440 | tf_op jit(solution)/shard_map/ppermute | solution.py:272
  29.6 2.2 %collective-permute-start.4 = (s32[4,16]{1,0:T(4,128)S(1)}, s32[4,16]{1,0:T(4,128)S(1)}, u32[]{:S(2)}, u32[]{:S(2)}) collective-permute-start(s32[4,16]{1,0:T(4,128)S(1)} %fusion.refs_1_), channel_id=1, source_target_pairs={{0,1},{1,0},{2,3},{3,2},{4,5},{5,4},{6,7},{7,6},{8,9},{9,8},{10,11... | collective-permute-start | bytes 776 | tf_op jit(solution)/shard_map/ppermute | solution.py:265
  30.6 14.2 %collective-permute-start.7 = (bf16[512,256]{1,0:T(8,128)(2,1)S(1)}, bf16[512,256]{1,0:T(8,128)(2,1)S(1)}, u32[]{:S(2)}, u32[]{:S(2)}) collective-permute-start(bf16[512,256]{1,0:T(8,128)(2,1)S(1)} %collective-permute-done.6.refs_3_), channel_id=1, source_target_pairs={{0,2},{2,6},{6,4},{4,0},{1,3},{3,7},{7,5},{5,1},{8,10},{10,14},{14... | collective-permute-start | bytes 786440 | tf_op jit(solution)/shard_map/ppermute | solution.py:272
  39.1 11.2 %collective-permute-start.9 = (bf16[512,256]{1,0:T(8,128)(2,1)S(1)}, bf16[512,256]{1,0:T(8,128)(2,1)S(1)}, u32[]{:S(2)}, u32[]{:S(2)}) collective-permute-start(bf16[512,256]{1,0:T(8,128)(2,1)S(1)} %collective-permute-done.8.refs_2_), channel_id=1, source_target_pairs={{0,2},{2,6},{6,4},{4,0},{1,3},{3,7},{7,5},{5,1},{8,10},{10,14},{14... | collective-permute-start | bytes 786440 | tf_op jit(solution)/shard_map/ppermute | solution.py:272
  44.7 13.8 %collective-permute-start.11 = (bf16[512,256]{1,0:T(8,128)(2,1)S(1)}, bf16[512,256]{1,0:T(8,128)(2,1)S(1)}, u32[]{:S(2)}, u32[]{:S(2)}) collective-permute-start(bf16[512,256]{1,0:T(8,128)(2,1)S(1)} %collective-permute-done.7.refs_3_), channel_id=1, source_target_pairs={{0,2},{2,6},{6,4},{4,0},{1,3},{3,7},{7,5},{5,1},{8,10},{10,14},{14... | collective-permute-start | bytes 786440 | tf_op jit(solution)/shard_map/ppermute | solution.py:272
  44.7 15.5 %collective-permute-start.13 = (bf16[128,1024]{1,0:T(8,128)(2,1)S(1)}, bf16[128,1024]{1,0:T(8,128)(2,1)S(1)}, u32[]{:S(2)}, u32[]{:S(2)}) collective-permute-start(bf16[128,1024]{1,0:T(8,128)(2,1)S(1)} %get-tuple-element.108), channel_id=1, source_target_pairs={{0,8},{8,0},{16,24},{24,16},{1,9},{9,1},{17,25},{25,17},{2,10},{10... | collective-permute-start | bytes 786440 | tf_op jit(solution)/shard_map/ppermute | solution.py:268
  45.5 14.8 %collective-permute-start.14 = (bf16[128,1024]{1,0:T(8,128)(2,1)S(1)}, bf16[128,1024]{1,0:T(8,128)(2,1)S(1)}, u32[]{:S(2)}, u32[]{:S(2)}) collective-permute-start(bf16[128,1024]{1,0:T(8,128)(2,1)S(1)} %get-tuple-element.109), channel_id=1, source_target_pairs={{0,16},{8,24},{16,0},{24,8},{1,17},{9,25},{17,1},{25,9},{2,18},{10... | collective-permute-start | bytes 786440 | tf_op jit(solution)/shard_map/ppermute | solution.py:268
  50.4 9.9 %collective-permute-start.15 = (bf16[128,1024]{1,0:T(8,128)(2,1)S(1)}, bf16[128,1024]{1,0:T(8,128)(2,1)S(1)}, u32[]{:S(2)}, u32[]{:S(2)}) collective-permute-start(bf16[128,1024]{1,0:T(8,128)(2,1)S(1)} %get-tuple-element.110), channel_id=1, source_target_pairs={{0,24},{8,16},{16,8},{24,0},{1,25},{9,17},{17,9},{25,1},{2,26},{10... | collective-permute-start | bytes 786440 | tf_op jit(solution)/shard_map/ppermute | solution.py:268
  51.5 11.4 %collective-permute-start.10 = (bf16[512,256]{1,0:T(8,128)(2,1)S(1)}, bf16[512,256]{1,0:T(8,128)(2,1)S(1)}, u32[]{:S(2)}, u32[]{:S(2)}) collective-permute-start(bf16[512,256]{1,0:T(8,128)(2,1)S(1)} %collective-permute-done.9.refs_2_), channel_id=1, source_target_pairs={{0,2},{2,6},{6,4},{4,0},{1,3},{3,7},{7,5},{5,1},{8,10},{10,14},{14... | collective-permute-start | bytes 786440 | tf_op jit(solution)/shard_map/ppermute | solution.py:272
  58.5 8.3 %collective-permute-start.12 = (bf16[512,256]{1,0:T(8,128)(2,1)S(1)}, bf16[512,256]{1,0:T(8,128)(2,1)S(1)}, u32[]{:S(2)}, u32[]{:S(2)}) collective-permute-start(bf16[512,256]{1,0:T(8,128)(2,1)S(1)} %collective-permute-done.11.refs_3_), channel_id=1, source_target_pairs={{0,2},{2,6},{6,4},{4,0},{1,3},{3,7},{7,5},{5,1},{8,10},{10,14},{14... | collective-permute-start | bytes 786440 | tf_op jit(solution)/shard_map/ppermute | solution.py:272
  60.6 37.5 %collective-permute-start.19 = (bf16[1024,512]{1,0:T(8,128)(2,1)S(1)}, bf16[1024,512]{1,0:T(8,128)(2,1)S(1)}, u32[]{:S(2)}, u32[]{:S(2)}) collective-permute-start(bf16[1024,512]{1,0:T(8,128)(2,1)S(1)} %get-tuple-element.124.refs_0_), channel_id=1, source_target_pairs={{0,1},{1,0},{2,3},{3,2},{4,5},{5,4},{6,7},{7,6},{8,9},{9,8},{10,11... | collective-permute-start | bytes 3145736 | tf_op jit(solution)/shard_map/ppermute | solution.py:265
  68.4 9.3 %collective-permute-start.21 = (bf16[512,256]{1,0:T(8,128)(2,1)S(1)}, bf16[512,256]{1,0:T(8,128)(2,1)S(1)}, u32[]{:S(2)}, u32[]{:S(2)}) collective-permute-start(bf16[512,256]{1,0:T(8,128)(2,1)S(1)} %get-tuple-element.130), channel_id=1, source_target_pairs={{0,4},{2,0},{6,2},{4,6},{1,5},{3,1},{7,3},{5,7},{8,12},{10,8},{14,... | collective-permute-start | bytes 786440 | tf_op jit(solution)/shard_map/ppermute | solution.py:272
  70.0 13.3 %collective-permute-start.16 = (bf16[512,256]{1,0:T(8,128)(2,1)S(1)}, bf16[512,256]{1,0:T(8,128)(2,1)S(1)}, u32[]{:S(2)}, u32[]{:S(2)}) collective-permute-start(bf16[512,256]{1,0:T(8,128)(2,1)S(1)} %get-tuple-element.120), channel_id=1, source_target_pairs={{0,4},{2,0},{6,2},{4,6},{1,5},{3,1},{7,3},{5,7},{8,12},{10,8},{14,... | collective-permute-start | bytes 786440 | tf_op jit(solution)/shard_map/ppermute | solution.py:272
  78.3 10.6 %collective-permute-start.22 = (bf16[512,256]{1,0:T(8,128)(2,1)S(1)}, bf16[512,256]{1,0:T(8,128)(2,1)S(1)}, u32[]{:S(2)}, u32[]{:S(2)}) collective-permute-start(bf16[512,256]{1,0:T(8,128)(2,1)S(1)} %get-tuple-element.131), channel_id=1, source_target_pairs={{0,4},{2,0},{6,2},{4,6},{1,5},{3,1},{7,3},{5,7},{8,12},{10,8},{14,... | collective-permute-start | bytes 786440 | tf_op jit(solution)/shard_map/ppermute | solution.py:272
  83.9 10.6 %collective-permute-start.17 = (bf16[512,256]{1,0:T(8,128)(2,1)S(1)}, bf16[512,256]{1,0:T(8,128)(2,1)S(1)}, u32[]{:S(2)}, u32[]{:S(2)}) collective-permute-start(bf16[512,256]{1,0:T(8,128)(2,1)S(1)} %get-tuple-element.121), channel_id=1, source_target_pairs={{0,4},{2,0},{6,2},{4,6},{1,5},{3,1},{7,3},{5,7},{8,12},{10,8},{14,... | collective-permute-start | bytes 786440 | tf_op jit(solution)/shard_map/ppermute | solution.py:272
  89.5 8.0 %collective-permute-start.23 = (bf16[512,256]{1,0:T(8,128)(2,1)S(1)}, bf16[512,256]{1,0:T(8,128)(2,1)S(1)}, u32[]{:S(2)}, u32[]{:S(2)}) collective-permute-start(bf16[512,256]{1,0:T(8,128)(2,1)S(1)} %get-tuple-element.132), channel_id=1, source_target_pairs={{0,4},{2,0},{6,2},{4,6},{1,5},{3,1},{7,3},{5,7},{8,12},{10,8},{14,... | collective-permute-start | bytes 786440 | tf_op jit(solution)/shard_map/ppermute | solution.py:272
  94.5 3.1 %collective-permute-start.18 = (bf16[512,256]{1,0:T(8,128)(2,1)S(1)}, bf16[512,256]{1,0:T(8,128)(2,1)S(1)}, u32[]{:S(2)}, u32[]{:S(2)}) collective-permute-start(bf16[512,256]{1,0:T(8,128)(2,1)S(1)} %get-tuple-element.123), channel_id=1, source_target_pairs={{0,1},{1,0},{2,3},{3,2},{4,5},{5,4},{6,7},{7,6},{8,9},{9,8},{10,11... | collective-permute-start | bytes 786440 | tf_op jit(solution)/shard_map/ppermute | solution.py:265
  94.6 8.7 %collective-permute-start.20 = (bf16[512,256]{1,0:T(8,128)(2,1)S(1)}, bf16[512,256]{1,0:T(8,128)(2,1)S(1)}, u32[]{:S(2)}, u32[]{:S(2)}) collective-permute-start(bf16[512,256]{1,0:T(8,128)(2,1)S(1)} %get-tuple-element.126), channel_id=1, source_target_pairs={{0,4},{2,0},{6,2},{4,6},{1,5},{3,1},{7,3},{5,7},{8,12},{10,8},{14,... | collective-permute-start | bytes 786440 | tf_op jit(solution)/shard_map/ppermute | solution.py:272
  104.3 7.2 %collective-permute-start.24 = (bf16[256,256]{1,0:T(8,128)(2,1)S(1)}, bf16[256,256]{1,0:T(8,128)(2,1)S(1)}, u32[]{:S(2)}, u32[]{:S(2)}) collective-permute-start(bf16[256,256]{1,0:T(8,128)(2,1)S(1)} %get-tuple-element.134), channel_id=1, source_target_pairs={{0,24},{8,16},{16,8},{24,0},{1,25},{9,17},{17,9},{25,1},{2,26},{10... | collective-permute-start | bytes 393224 | tf_op jit(solution)/shard_map/ppermute | solution.py:268
  105.8 7.1 %collective-permute-start.25 = (bf16[256,256]{1,0:T(8,128)(2,1)S(1)}, bf16[256,256]{1,0:T(8,128)(2,1)S(1)}, u32[]{:S(2)}, u32[]{:S(2)}) collective-permute-start(bf16[256,256]{1,0:T(8,128)(2,1)S(1)} %get-tuple-element.135), channel_id=1, source_target_pairs={{0,16},{8,24},{16,0},{24,8},{1,17},{9,25},{17,1},{25,9},{2,18},{10... | collective-permute-start | bytes 393224 | tf_op jit(solution)/shard_map/ppermute | solution.py:268
  107.0 5.9 %collective-permute-start.26 = (bf16[256,256]{1,0:T(8,128)(2,1)S(1)}, bf16[256,256]{1,0:T(8,128)(2,1)S(1)}, u32[]{:S(2)}, u32[]{:S(2)}) collective-permute-start(bf16[256,256]{1,0:T(8,128)(2,1)S(1)} %get-tuple-element.136), channel_id=1, source_target_pairs={{0,8},{8,0},{16,24},{24,16},{1,9},{9,1},{17,25},{25,17},{2,10},{10... | collective-permute-start | bytes 393224 | tf_op jit(solution)/shard_map/ppermute | solution.py:268
  113.0 5.1 %collective-permute-start.27 = (bf16[256,256]{1,0:T(8,128)(2,1)S(1)}, bf16[256,256]{1,0:T(8,128)(2,1)S(1)}, u32[]{:S(2)}, u32[]{:S(2)}) collective-permute-start(bf16[256,256]{1,0:T(8,128)(2,1)S(1)} %sum.3.refs_0_), channel_id=1, source_target_pairs={{0,2},{2,0},{4,6},{6,4},{1,3},{3,1},{5,7},{7,5},{8,10},{10,8},{12,... | collective-permute-start | bytes 393224 | tf_op jit(solution)/shard_map/ppermute | solution.py:432
  118.2 8.0 %collective-permute-start.28 = (bf16[256,256]{1,0:T(8,128)(2,1)S(1)}, bf16[256,256]{1,0:T(8,128)(2,1)S(1)}, u32[]{:S(2)}, u32[]{:S(2)}) collective-permute-start(bf16[256,256]{1,0:T(8,128)(2,1)S(1)} %sum.4.refs_0_), channel_id=1, source_target_pairs={{0,4},{2,6},{4,0},{6,2},{1,5},{3,7},{5,1},{7,3},{8,12},{10,14},{12... | collective-permute-start | bytes 393224 | tf_op jit(solution)/shard_map/ppermute | solution.py:432
  126.2 6.3 %collective-permute-start.29 = (bf16[256,256]{1,0:T(8,128)(2,1)S(1)}, bf16[256,256]{1,0:T(8,128)(2,1)S(1)}, u32[]{:S(2)}, u32[]{:S(2)}) collective-permute-start(bf16[256,256]{1,0:T(8,128)(2,1)S(1)} %sum.5.refs_1_), channel_id=1, source_target_pairs={{0,8},{8,0},{16,24},{24,16},{1,9},{9,1},{17,25},{25,17},{2,10},{10... | collective-permute-start | bytes 393224 | tf_op jit(solution)/shard_map/ppermute | solution.py:268
  127.7 7.7 %collective-permute-start.30 = (bf16[256,256]{1,0:T(8,128)(2,1)S(1)}, bf16[256,256]{1,0:T(8,128)(2,1)S(1)}, u32[]{:S(2)}, u32[]{:S(2)}) collective-permute-start(bf16[256,256]{1,0:T(8,128)(2,1)S(1)} %sum.5.refs_1_), channel_id=1, source_target_pairs={{0,16},{8,24},{16,0},{24,8},{1,17},{9,25},{17,1},{25,9},{2,18},{10... | collective-permute-start | bytes 393224 | tf_op jit(solution)/shard_map/ppermute | solution.py:268
  129.1 6.3 %collective-permute-start.31 = (bf16[256,256]{1,0:T(8,128)(2,1)S(1)}, bf16[256,256]{1,0:T(8,128)(2,1)S(1)}, u32[]{:S(2)}, u32[]{:S(2)}) collective-permute-start(bf16[256,256]{1,0:T(8,128)(2,1)S(1)} %sum.5.refs_1_), channel_id=1, source_target_pairs={{0,24},{8,16},{16,8},{24,0},{1,25},{9,17},{17,9},{25,1},{2,26},{10... | collective-permute-start | bytes 393224 | tf_op jit(solution)/shard_map/ppermute | solution.py:268
  129.7 7.0 %collective-permute-start.32 = (bf16[256,256]{1,0:T(8,128)(2,1)S(1)}, bf16[256,256]{1,0:T(8,128)(2,1)S(1)}, u32[]{:S(2)}, u32[]{:S(2)}) collective-permute-start(bf16[256,256]{1,0:T(8,128)(2,1)S(1)} %sum.5.refs_1_), channel_id=1, source_target_pairs={{0,1},{1,0},{2,3},{3,2},{4,5},{5,4},{6,7},{7,6},{8,9},{9,8},{10,11... | collective-permute-start | bytes 393224 | tf_op jit(solution)/shard_map/ppermute | solution.py:265
  132.4 4.4 %collective-permute-start.33 = (bf16[256,256]{1,0:T(8,128)(2,1)S(1)}, bf16[256,256]{1,0:T(8,128)(2,1)S(1)}, u32[]{:S(2)}, u32[]{:S(2)}) collective-permute-start(bf16[256,256]{1,0:T(8,128)(2,1)S(1)} %collective-permute-done.29.refs_2_), channel_id=1, source_target_pairs={{0,1},{1,0},{2,3},{3,2},{4,5},{5,4},{6,7},{7,6},{8,9},{9,8},{10,11... | collective-permute-start | bytes 393224 | tf_op jit(solution)/shard_map/ppermute | solution.py:265
  135.4 1.4 %collective-permute-start.34 = (bf16[256,256]{1,0:T(8,128)(2,1)S(1)}, bf16[256,256]{1,0:T(8,128)(2,1)S(1)}, u32[]{:S(2)}, u32[]{:S(2)}) collective-permute-start(bf16[256,256]{1,0:T(8,128)(2,1)S(1)} %collective-permute-done.30.refs_3_), channel_id=1, source_target_pairs={{0,1},{1,0},{2,3},{3,2},{4,5},{5,4},{6,7},{7,6},{8,9},{9,8},{10,11... | collective-permute-start | bytes 393224 | tf_op jit(solution)/shard_map/ppermute | solution.py:265
  135.4 1.5 %collective-permute-start.35 = (bf16[256,256]{1,0:T(8,128)(2,1)S(1)}, bf16[256,256]{1,0:T(8,128)(2,1)S(1)}, u32[]{:S(2)}, u32[]{:S(2)}) collective-permute-start(bf16[256,256]{1,0:T(8,128)(2,1)S(1)} %collective-permute-done.31.refs_4_), channel_id=1, source_target_pairs={{0,1},{1,0},{2,3},{3,2},{4,5},{5,4},{6,7},{7,6},{8,9},{9,8},{10,11... | collective-permute-start | bytes 393224 | tf_op jit(solution)/shard_map/ppermute | solution.py:265

commit v19 on v16

--- a/solution.py
+++ b/solution.py
@@ -243,7 +243,8 @@
 
 
 def last_kernel(z, me_ref, *refs):
-    pieces, out = refs[:-1], refs[-1]
+    first, *rest, out = refs
+    pieces = [*rest[:z.grp], first, *rest[z.grp:]]
     share, half = pieces[0].shape
     for rel in range(2):
         left = pl.multiple_of((me_ref[2] ^ rel) * half, half)
@@ -429,11 +430,14 @@
             [mine, lax.ppermute(mine, "zz", [(i, i ^ step) for i in range(z.zz)])]
         )
         step *= 2
+    come = [to_core(mine)]
+    mine, come[0] = lax.optimization_barrier((mine, come[0]))
     mine = across([mine] * z.grp)
+    come += [to_core(part) for part in mine[1:]]
     (grad_weight,) = call(
         lambda *refs: last_kernel(z, *refs),
         [((width_in, hidden_units), F32)],
-        [("s", me)] + [("v", part) for part in mine + [to_core(part) for part in mine]],
+        [("s", me)] + [("v", part) for part in [come[0], *mine, *come[1:]]],
         "last", 2,
     )
     return hidden, grad_weight

time: 136 us -> 139 us (1.022)
  waiting for transfers between devices: 59.6 us -> 62.2 us
    ppermute x12, waiting for transfers between devices: 13.9 us -> 15.5 us  [to_grp(): lax.ppermute(x, 'grp', [(i, i ^ s) for i in range(z.grp)])]
where the time goes in v19:
time: 139 us
  waiting for transfers between devices  62.2 us (45%)
  starting transfers between devices  41.1 us (30%)
  Pallas kernels  30.3 us (22%)
  local copies, waits for them, and re-layouts  3.19 us (2%)
    ppermute x12, waiting for transfers between devices, to_zz(): lax.ppermute(x, 'zz', [(order[i], order[(i + k) % z.zz]) for i in range(z...  32.1 us
    pallas_call x25, Pallas kernels, call(): pl.pallas_call(kernel, out_shape=tuple((jax.ShapeDtypeStruct(s, d) for s,...  30.3 us
    ppermute x12, waiting for transfers between devices, to_grp(): lax.ppermute(x, 'grp', [(i, i ^ s) for i in range(z.grp)])  15.5 us
    ppermute x12, starting transfers between devices, to_zz(): lax.ppermute(x, 'zz', [(order[i], order[(i + k) % z.zz]) for i in range(z...  15.4 us
    ppermute x12, starting transfers between devices, to_grp(): lax.ppermute(x, 'grp', [(i, i ^ s) for i in range(z.grp)])  13.5 us
    ppermute x2, waiting for transfers between devices, shards(): lax.ppermute(mine, 'zz', [(i, i ^ step) for i in range(z.zz)])  8.6 us
    all_to_all x1, starting transfers between devices, shards(): lax.all_to_all(message, ('grp', 'zz', 'core'), split_axis=0, concat_axis=...  6.96 us
    all_to_all x1, waiting for transfers between devices, shards(): lax.all_to_all(message, ('grp', 'zz', 'core'), split_axis=0, concat_axis=...  4.42 us
  transfers between devices with their start and end apart: 37, of which 22 were waited for; matrix products, arithmetic and copies ran while one was open for 1% of the time, Pallas kernels for 19%

profile of v19, /device:TPU:0, one launch (start us, length us, event | category | flops | bytes accessed | tf_op | source)
XLA Modules:
  0.0 138.7 jit_solution(8280643910860936990)
XLA Ops:
  1.9 1.8 %index.1 = s32[32,8,128]{2,1,0:T(8,128)} custom-call(s32[3]{0:T(128)S(1)} %pad_add_fusion.refs_0_, s32[1,512]{1,0:T(1,128)S(1)} %bitcast.4), custom_call_target="tpu_custom_call" | custom-call | flops 100000000 | tf_op jit(solution)/shard_map/index/pallas_call | solution.py:59
  3.7 7.0 %all-to-all-start = ((s32[32,8,128]{2,1,0:T(8,128)}), s32[32,8,128]{2,1,0:T(8,128)S(1)}, u32[]{:S(2)}, u32[]{:S(2)}) async-start(s32[32,8,128]{2,1,0:T(8,128)} %index.1), calls=%async_computation | async-start | bytes 262144 | tf_op jit(solution)/shard_map/all_to_all | solution.py:283
  10.6 1.2 copy-done
  11.9 1.2 copy-done.3
  13.1 1.3 product.1
  14.4 4.4 %all-to-all-done.refs_1_.refs_2_ = s32[32,8,128]{2,1,0:T(8,128)S(1)} async-done(((s32[32,8,128]{2,1,0:T(8,128)}), s32[32,8,128]{2,1,0:T(8,128)S(1)}, u32[]{:S(2)}, u32[]{:S(2)}) %all-to-all-start) | async-done | bytes 131104 | tf_op jit(solution)/shard_map/all_to_all | solution.py:283
  18.8 1.2 send.1
  20.0 1.0 collective-permute-start
  21.1 1.3 collective-permute-start.1
  22.4 1.2 collective-permute-start.2
  23.7 3.7 %collective-permute-done.refs_0_ = bf16[2,128,256]{2,1,0:T(8,128)(2,1)S(1)} collective-permute-done((bf16[2,128,256]{2,1,0:T(8,128)(2,1)S(1)}, bf16[2,128,256]{2,1,0:T(8,128)(2,1)S(1)}, u32[]{:S(2)}, u32[]{:S(2)}) %collective-permute-start) | collective-permute-done | bytes 131104 | tf_op jit(solution)/shard_map/ppermute | solution.py:269
  27.4 1.6 %collective-permute-done.1.refs_1_ = bf16[2,128,256]{2,1,0:T(8,128)(2,1)S(1)} collective-permute-done((bf16[2,128,256]{2,1,0:T(8,128)(2,1)S(1)}, bf16[2,128,256]{2,1,0:T(8,128)(2,1)S(1)}, u32[]{:S(2)}, u32[]{:S(2)}) %collective-permute-start.1) | collective-permute-done | bytes 131104 | tf_op jit(solution)/shard_map/ppermute | solution.py:269
  30.6 1.2 collective-permute-start.7
  31.8 5.9 %prepare.2 = (bf16[1024,512]{1,0:T(8,128)(2,1)S(1)}, bf16[1024,512]{1,0:T(8,128)(2,1)S(1)}, bf16[1024,512]{1,0:T(8,128)(2,1)S(1)}, bf16[1024,512]{1,0:T(8,128)(2,1)S(1)}, f32[8,128]{1,0:T(8,128)S(1)}) custom-call(s32[3]{0:T(128)S(1)} %pad_add_fusion.refs_0_, s32[4,16]{1,0:T(4,128)S(1)} %fusion.refs_1_, s32[32,8,128]{2,1,0:T(8,128)S(1)} %all-to-all-done.refs_1_.refs_2_, ...), custom_call_target="tpu_custom_call" | custom-call | flops 700000000 | tf_op jit(solution)/shard_map/prepare/pallas_call | solution.py:59
  37.7 1.4 %collective-permute-done.8.refs_2_ = bf16[512,256]{1,0:T(8,128)(2,1)S(1)} collective-permute-done((bf16[512,256]{1,0:T(8,128)(2,1)S(1)}, bf16[512,256]{1,0:T(8,128)(2,1)S(1)}, u32[]{:S(2)}, u32[]{:S(2)}) %collective-permute-start.8) | collective-permute-done | bytes 262176 | tf_op jit(solution)/shard_map/ppermute | solution.py:273
  39.1 5.6 %collective-permute-done.7.refs_3_ = bf16[512,256]{1,0:T(8,128)(2,1)S(1)} collective-permute-done((bf16[512,256]{1,0:T(8,128)(2,1)S(1)}, bf16[512,256]{1,0:T(8,128)(2,1)S(1)}, u32[]{:S(2)}, u32[]{:S(2)}) %collective-permute-start.7) | collective-permute-done | bytes 262176 | tf_op jit(solution)/shard_map/ppermute | solution.py:273
  45.5 1.0 collective-permute-start.14
  46.5 3.9 %collective-permute-done.9.refs_2_ = bf16[512,256]{1,0:T(8,128)(2,1)S(1)} collective-permute-done((bf16[512,256]{1,0:T(8,128)(2,1)S(1)}, bf16[512,256]{1,0:T(8,128)(2,1)S(1)}, u32[]{:S(2)}, u32[]{:S(2)}) %collective-permute-start.9) | collective-permute-done | bytes 262176 | tf_op jit(solution)/shard_map/ppermute | solution.py:273
  50.4 1.2 collective-permute-start.15
  51.5 6.9 %prepare.3 = (bf16[1024,512]{1,0:T(8,128)(2,1)S(1)}, bf16[1024,512]{1,0:T(8,128)(2,1)S(1)}, bf16[1024,512]{1,0:T(8,128)(2,1)S(1)}, bf16[1024,512]{1,0:T(8,128)(2,1)S(1)}, f32[8,128]{1,0:T(8,128)S(1)}) custom-call(s32[3]{0:T(128)S(1)} %pad_add_fusion.refs_0_, s32[4,16]{1,0:T(4,128)S(1)} %collective-permute-done.4.refs_5_.refs_1_, ...), custom_call_target="tpu_custom_call" | custom-call | flops 700000000 | tf_op jit(solution)/shard_map/prepare/pallas_call | solution.py:59
  58.5 1.7 %collective-permute-start.12 = (bf16[512,256]{1,0:T(8,128)(2,1)S(1)}, bf16[512,256]{1,0:T(8,128)(2,1)S(1)}, u32[]{:S(2)}, u32[]{:S(2)}) collective-permute-start(bf16[512,256]{1,0:T(8,128)(2,1)S(1)} %collective-permute-done.11.refs_3_), channel_id=1, source_target_pairs={{0,2},{2,6},{6,4},{4,0},{1,3},{3,7},{7,5},{5,1},{8,10},{10,14},{14... | collective-permute-start | bytes 786440 | tf_op jit(solution)/shard_map/ppermute | solution.py:273
  63.0 3.8 %collective-permute-done.12.refs_3_ = bf16[512,256]{1,0:T(8,128)(2,1)S(1)} collective-permute-done((bf16[512,256]{1,0:T(8,128)(2,1)S(1)}, bf16[512,256]{1,0:T(8,128)(2,1)S(1)}, u32[]{:S(2)}, u32[]{:S(2)}) %collective-permute-start.12) | collective-permute-done | bytes 262176 | tf_op jit(solution)/shard_map/ppermute | solution.py:273
  66.8 1.6 %forward.7 = (bf16[512,256]{1,0:T(8,128)(2,1)S(1)}, bf16[512,256]{1,0:T(8,128)(2,1)S(1)}, bf16[512,256]{1,0:T(8,128)(2,1)S(1)}, bf16[512,256]{1,0:T(8,128)(2,1)S...) custom-call(bf16[1024,512]{1,0:T(8,128)(2,1)S(1)} %get-tuple-element.84.refs_0_.refs_8_, ...), custom_call_target="tpu_custom_call" | custom-call | flops 300000000 | tf_op jit(solution)/shard_map/forward/pallas_call | solution.py:59
  68.4 1.6 %collective-permute-start.21 = (bf16[512,256]{1,0:T(8,128)(2,1)S(1)}, bf16[512,256]{1,0:T(8,128)(2,1)S(1)}, u32[]{:S(2)}, u32[]{:S(2)}) collective-permute-start(bf16[512,256]{1,0:T(8,128)(2,1)S(1)} %get-tuple-element.127), channel_id=1, source_target_pairs={{0,4},{2,0},{6,2},{4,6},{1,5},{3,1},{7,3},{5,7},{8,12},{10,8},{14,... | collective-permute-start | bytes 786440 | tf_op jit(solution)/shard_map/ppermute | solution.py:273
  70.8 6.9 %collective-permute-done.21.refs_1_ = bf16[512,256]{1,0:T(8,128)(2,1)S(1)} collective-permute-done((bf16[512,256]{1,0:T(8,128)(2,1)S(1)}, bf16[512,256]{1,0:T(8,128)(2,1)S(1)}, u32[]{:S(2)}, u32[]{:S(2)}) %collective-permute-start.21) | collective-permute-done | bytes 262176 | tf_op jit(solution)/shard_map/ppermute | solution.py:273
  78.3 2.5 %collective-permute-start.22 = (bf16[512,256]{1,0:T(8,128)(2,1)S(1)}, bf16[512,256]{1,0:T(8,128)(2,1)S(1)}, u32[]{:S(2)}, u32[]{:S(2)}) collective-permute-start(bf16[512,256]{1,0:T(8,128)(2,1)S(1)} %get-tuple-element.128), channel_id=1, source_target_pairs={{0,4},{2,0},{6,2},{4,6},{1,5},{3,1},{7,3},{5,7},{8,12},{10,8},{14,... | collective-permute-start | bytes 786440 | tf_op jit(solution)/shard_map/ppermute | solution.py:273
  80.8 2.5 %collective-permute-done.18.refs_1_ = bf16[512,256]{1,0:T(8,128)(2,1)S(1)} collective-permute-done((bf16[512,256]{1,0:T(8,128)(2,1)S(1)}, bf16[512,256]{1,0:T(8,128)(2,1)S(1)}, u32[]{:S(2)}, u32[]{:S(2)}) %collective-permute-start.18) | collective-permute-done | bytes 262176 | tf_op jit(solution)/shard_map/ppermute | solution.py:273
  83.9 2.0 %collective-permute-start.19 = (bf16[512,256]{1,0:T(8,128)(2,1)S(1)}, bf16[512,256]{1,0:T(8,128)(2,1)S(1)}, u32[]{:S(2)}, u32[]{:S(2)}) collective-permute-start(bf16[512,256]{1,0:T(8,128)(2,1)S(1)} %get-tuple-element.122), channel_id=1, source_target_pairs={{0,4},{2,0},{6,2},{4,6},{1,5},{3,1},{7,3},{5,7},{8,12},{10,8},{14,... | collective-permute-start | bytes 786440 | tf_op jit(solution)/shard_map/ppermute | solution.py:273
  86.6 0.9 collective-permute-done.22.refs_1_
  88.2 2.9 %collective-permute-start.23 = (bf16[512,256]{1,0:T(8,128)(2,1)S(1)}, bf16[512,256]{1,0:T(8,128)(2,1)S(1)}, u32[]{:S(2)}, u32[]{:S(2)}) collective-permute-start(bf16[512,256]{1,0:T(8,128)(2,1)S(1)} %get-tuple-element.129), channel_id=1, source_target_pairs={{0,4},{2,0},{6,2},{4,6},{1,5},{3,1},{7,3},{5,7},{8,12},{10,8},{14,... | collective-permute-start | bytes 786440 | tf_op jit(solution)/shard_map/ppermute | solution.py:273
  91.0 2.1 %collective-permute-done.19.refs_1_ = bf16[512,256]{1,0:T(8,128)(2,1)S(1)} collective-permute-done((bf16[512,256]{1,0:T(8,128)(2,1)S(1)}, bf16[512,256]{1,0:T(8,128)(2,1)S(1)}, u32[]{:S(2)}, u32[]{:S(2)}) %collective-permute-start.19) | collective-permute-done | bytes 262176 | tf_op jit(solution)/shard_map/ppermute | solution.py:273
  93.8 2.9 %collective-permute-start.20 = (bf16[512,256]{1,0:T(8,128)(2,1)S(1)}, bf16[512,256]{1,0:T(8,128)(2,1)S(1)}, u32[]{:S(2)}, u32[]{:S(2)}) collective-permute-start(bf16[512,256]{1,0:T(8,128)(2,1)S(1)} %get-tuple-element.123), channel_id=1, source_target_pairs={{0,4},{2,0},{6,2},{4,6},{1,5},{3,1},{7,3},{5,7},{8,12},{10,8},{14,... | collective-permute-start | bytes 786440 | tf_op jit(solution)/shard_map/ppermute | solution.py:273
  97.4 1.4 %collective-permute-done.23.refs_2_ = bf16[512,256]{1,0:T(8,128)(2,1)S(1)} collective-permute-done((bf16[512,256]{1,0:T(8,128)(2,1)S(1)}, bf16[512,256]{1,0:T(8,128)(2,1)S(1)}, u32[]{:S(2)}, u32[]{:S(2)}) %collective-permute-start.23) | collective-permute-done | bytes 262176 | tf_op jit(solution)/shard_map/ppermute | solution.py:273
  99.2 3.7 %collective-permute-done.20.refs_3_ = bf16[512,256]{1,0:T(8,128)(2,1)S(1)} collective-permute-done((bf16[512,256]{1,0:T(8,128)(2,1)S(1)}, bf16[512,256]{1,0:T(8,128)(2,1)S(1)}, u32[]{:S(2)}, u32[]{:S(2)}) %collective-permute-start.20) | collective-permute-done | bytes 262176 | tf_op jit(solution)/shard_map/ppermute | solution.py:273
  102.9 1.0 grad.1
  103.9 1.5 %collective-permute-start.24 = (bf16[256,256]{1,0:T(8,128)(2,1)S(1)}, bf16[256,256]{1,0:T(8,128)(2,1)S(1)}, u32[]{:S(2)}, u32[]{:S(2)}) collective-permute-start(bf16[256,256]{1,0:T(8,128)(2,1)S(1)} %get-tuple-element.130), channel_id=1, source_target_pairs={{0,24},{8,16},{16,8},{24,0},{1,25},{9,17},{17,9},{25,1},{2,26},{10... | collective-permute-start | bytes 393224 | tf_op jit(solution)/shard_map/ppermute | solution.py:269
  105.4 1.2 collective-permute-start.25
  107.5 3.0 %collective-permute-done.24.refs_0_ = bf16[256,256]{1,0:T(8,128)(2,1)S(1)} collective-permute-done((bf16[256,256]{1,0:T(8,128)(2,1)S(1)}, bf16[256,256]{1,0:T(8,128)(2,1)S(1)}, u32[]{:S(2)}, u32[]{:S(2)}) %collective-permute-start.24) | collective-permute-done | bytes 131104 | tf_op jit(solution)/shard_map/ppermute | solution.py:269
  110.4 1.3 collective-permute-done.25.refs_1_
  112.7 4.1 %collective-permute-done.27.refs_1_ = bf16[256,256]{1,0:T(8,128)(2,1)S(1)} collective-permute-done((bf16[256,256]{1,0:T(8,128)(2,1)S(1)}, bf16[256,256]{1,0:T(8,128)(2,1)S(1)}, u32[]{:S(2)}, u32[]{:S(2)}) %collective-permute-start.27) | collective-permute-done | bytes 131104 | tf_op jit(solution)/shard_map/ppermute | solution.py:430
  116.9 2.9 %collective-permute-start.28 = (bf16[256,256]{1,0:T(8,128)(2,1)S(1)}, bf16[256,256]{1,0:T(8,128)(2,1)S(1)}, u32[]{:S(2)}, u32[]{:S(2)}) collective-permute-start(bf16[256,256]{1,0:T(8,128)(2,1)S(1)} %sum.4.refs_0_), channel_id=1, source_target_pairs={{0,4},{2,6},{4,0},{6,2},{1,5},{3,7},{5,1},{7,3},{8,12},{10,14},{12... | collective-permute-start | bytes 393224 | tf_op jit(solution)/shard_map/ppermute | solution.py:430
  119.7 4.5 %collective-permute-done.28.refs_1_ = bf16[256,256]{1,0:T(8,128)(2,1)S(1)} collective-permute-done((bf16[256,256]{1,0:T(8,128)(2,1)S(1)}, bf16[256,256]{1,0:T(8,128)(2,1)S(1)}, u32[]{:S(2)}, u32[]{:S(2)}) %collective-permute-start.28) | collective-permute-done | bytes 131104 | tf_op jit(solution)/shard_map/ppermute | solution.py:430
  124.3 1.3 collective-permute-done.29.refs_1_
  125.7 1.4 collective-permute-start.30
  127.7 1.4 %collective-permute-start.32 = (bf16[256,256]{1,0:T(8,128)(2,1)S(1)}, bf16[256,256]{1,0:T(8,128)(2,1)S(1)}, u32[]{:S(2)}, u32[]{:S(2)}) collective-permute-start(bf16[256,256]{1,0:T(8,128)(2,1)S(1)} %sum.5.refs_2_), channel_id=1, source_target_pairs={{0,24},{8,16},{16,8},{24,0},{1,25},{9,17},{17,9},{25,1},{2,26},{10... | collective-permute-start | bytes 393224 | tf_op jit(solution)/shard_map/ppermute | solution.py:269
  129.2 2.5 %collective-permute-done.30.refs_3_ = bf16[256,256]{1,0:T(8,128)(2,1)S(1)} collective-permute-done((bf16[256,256]{1,0:T(8,128)(2,1)S(1)}, bf16[256,256]{1,0:T(8,128)(2,1)S(1)}, u32[]{:S(2)}, u32[]{:S(2)}) %collective-permute-start.30) | collective-permute-done | bytes 131104 | tf_op jit(solution)/shard_map/ppermute | solution.py:269
  131.7 3.4 %collective-permute-done.31.refs_4_ = bf16[256,256]{1,0:T(8,128)(2,1)S(1)} collective-permute-done((bf16[256,256]{1,0:T(8,128)(2,1)S(1)}, bf16[256,256]{1,0:T(8,128)(2,1)S(1)}, u32[]{:S(2)}, u32[]{:S(2)}) %collective-permute-start.31) | collective-permute-done | bytes 131104 | tf_op jit(solution)/shard_map/ppermute | solution.py:269
  136.7 2.0 %last.1 = f32[1024,512]{1,0:T(8,128)} custom-call(s32[3]{0:T(128)S(1)} %pad_add_fusion.refs_0_, bf16[256,256]{1,0:T(8,128)(2,1)S(1)} %collective-permute-done.29.refs_1_, bf16[256,256]{1,0:T(8,128)(2,1)S(1)} %sum.5.refs_2_, bf16[256,256]{1,0:T(8,128)(2,1)S(1)} %collective-permute-done.30.refs_3_, bf16[256,256]{1,0:T(8,128)(2,1)S(1)} %collective-permute-done.31.refs_4_, ...), custom_call_target="tpu_custom_call" | custom-call | flops 200000000 | tf_op jit(solution)/shard_map/last/pallas_call | solution.py:59
  (72 shorter events, 15.8 us)
Async XLA Ops:
  0.6 50.9 %collective-permute-start.5 = (bf16[4,16,128,128]{3,2,1,0:T(8,128)(2,1)}, bf16[4,16,128,128]{3,2,1,0:T(8,128)(2,1)}, u32[]{:S(2)}, u32[]{:S(2)}) collective-permute-start(bf16[4,16,128,128]{3,2,1,0:T(8,128)(2,1)} %refs_3_.1), channel_id=1, source_target_pairs={{0,1},{1,0},{2,3},{3,2},{4,5},{5,4},{6,7},{7,6},{8,9},{9,8},{10,11... | collective-permute-start | bytes 6291464 | tf_op jit(solution)/shard_map/ppermute | solution.py:266
  1.2 0.7 copy-start.4
  3.7 15.1 %all-to-all-start = ((s32[32,8,128]{2,1,0:T(8,128)}), s32[32,8,128]{2,1,0:T(8,128)S(1)}, u32[]{:S(2)}, u32[]{:S(2)}) async-start(s32[32,8,128]{2,1,0:T(8,128)} %index.1), calls=%async_computation | async-start | bytes 262144 | tf_op jit(solution)/shard_map/all_to_all | solution.py:283
  10.6 1.2 copy-start
  11.9 1.2 copy-start.3
  13.1 10.5 %copy-start.5 = (bf16[512,512]{1,0:T(8,128)(2,1)S(1)}, bf16[512,512]{1,0:T(8,128)(2,1)}, u32[]{:S(2)}) copy-start(bf16[512,512]{1,0:T(8,128)(2,1)} %param.13) | copy-start | bytes 1572868
  14.4 15.2 %copy-start.6 = (s32[4,16]{1,0:T(4,128)S(1)}, s32[4,16]{1,0:T(4,128)}, u32[]{:S(2)}) copy-start(s32[4,16]{1,0:T(4,128)} %param.9) | copy-start | bytes 772
  14.4 15.2 %copy-start.7 = (s32[4]{0:T(128)S(1)}, s32[4]{0:T(128)}, u32[]{:S(2)}) copy-start(s32[4]{0:T(128)} %param.10) | copy-start | bytes 52
  14.4 15.4 %copy-start.1 = (bf16[512,1024]{1,0:T(8,128)(2,1)S(1)}, bf16[512,1024]{1,0:T(8,128)(2,1)}, u32[]{:S(2)}) copy-start(bf16[512,1024]{1,0:T(8,128)(2,1)} %refs_1_.1) | copy-start | bytes 3145732
  20.0 7.3 %collective-permute-start = (bf16[2,128,256]{2,1,0:T(8,128)(2,1)S(1)}, bf16[2,128,256]{2,1,0:T(8,128)(2,1)S(1)}, u32[]{:S(2)}, u32[]{:S(2)}) collective-permute-start(bf16[2,128,256]{2,1,0:T(8,128)(2,1)S(1)} %get-tuple-element.76), channel_id=1, source_target_pairs={{0,24},{8,16},{16,8},{24,0},{1,25},{9,17},{17,9},{25,1},{2,26},{10... | collective-permute-start | bytes 393224 | tf_op jit(solution)/shard_map/ppermute | solution.py:269
  21.1 7.9 %collective-permute-start.1 = (bf16[2,128,256]{2,1,0:T(8,128)(2,1)S(1)}, bf16[2,128,256]{2,1,0:T(8,128)(2,1)S(1)}, u32[]{:S(2)}, u32[]{:S(2)}) collective-permute-start(bf16[2,128,256]{2,1,0:T(8,128)(2,1)S(1)} %get-tuple-element.77), channel_id=1, source_target_pairs={{0,16},{8,24},{16,0},{24,8},{1,17},{9,25},{17,1},{25,9},{2,18},{10... | collective-permute-start | bytes 393224 | tf_op jit(solution)/shard_map/ppermute | solution.py:269
  22.4 6.6 %collective-permute-start.2 = (bf16[2,128,256]{2,1,0:T(8,128)(2,1)S(1)}, bf16[2,128,256]{2,1,0:T(8,128)(2,1)S(1)}, u32[]{:S(2)}, u32[]{:S(2)}) collective-permute-start(bf16[2,128,256]{2,1,0:T(8,128)(2,1)S(1)} %get-tuple-element.78), channel_id=1, source_target_pairs={{0,8},{8,0},{16,24},{24,16},{1,9},{9,1},{17,25},{25,17},{2,10},{10... | collective-permute-start | bytes 393224 | tf_op jit(solution)/shard_map/ppermute | solution.py:269
  23.6 8.2 %copy-start.2 = (bf16[4,16,128,128]{3,2,1,0:T(8,128)(2,1)S(1)}, bf16[4,16,128,128]{3,2,1,0:T(8,128)(2,1)}, u32[]{:S(2)}) copy-start(bf16[4,16,128,128]{3,2,1,0:T(8,128)(2,1)} %refs_3_.1) | copy-start | bytes 6291460
  23.6 6.2 %collective-permute-start.3 = (bf16[512,256]{1,0:T(8,128)(2,1)S(1)}, bf16[512,256]{1,0:T(8,128)(2,1)S(1)}, u32[]{:S(2)}, u32[]{:S(2)}) collective-permute-start(bf16[512,256]{1,0:T(8,128)(2,1)S(1)} %get-tuple-element.138), channel_id=1, source_target_pairs={{0,1},{1,0},{2,3},{3,2},{4,5},{5,4},{6,7},{7,6},{8,9},{9,8},{10,11... | collective-permute-start | bytes 786440 | tf_op jit(solution)/shard_map/ppermute | solution.py:266
  29.0 1.6 %collective-permute-start.6 = (bf16[512,256]{1,0:T(8,128)(2,1)S(1)}, bf16[512,256]{1,0:T(8,128)(2,1)S(1)}, u32[]{:S(2)}, u32[]{:S(2)}) collective-permute-start(bf16[512,256]{1,0:T(8,128)(2,1)S(1)} %get-tuple-element.85), channel_id=1, source_target_pairs={{0,1},{1,0},{2,3},{3,2},{4,5},{5,4},{6,7},{7,6},{8,9},{9,8},{10,11... | collective-permute-start | bytes 786440 | tf_op jit(solution)/shard_map/ppermute | solution.py:266
  29.1 10.1 %collective-permute-start.8 = (bf16[512,256]{1,0:T(8,128)(2,1)S(1)}, bf16[512,256]{1,0:T(8,128)(2,1)S(1)}, u32[]{:S(2)}, u32[]{:S(2)}) collective-permute-start(bf16[512,256]{1,0:T(8,128)(2,1)S(1)} %get-tuple-element.86.refs_2_), channel_id=1, source_target_pairs={{0,2},{2,6},{6,4},{4,0},{1,3},{3,7},{7,5},{5,1},{8,10},{10,14},{14... | collective-permute-start | bytes 786440 | tf_op jit(solution)/shard_map/ppermute | solution.py:273
  29.6 2.2 %collective-permute-start.4 = (s32[4,16]{1,0:T(4,128)S(1)}, s32[4,16]{1,0:T(4,128)S(1)}, u32[]{:S(2)}, u32[]{:S(2)}) collective-permute-start(s32[4,16]{1,0:T(4,128)S(1)} %fusion.refs_1_), channel_id=1, source_target_pairs={{0,1},{1,0},{2,3},{3,2},{4,5},{5,4},{6,7},{7,6},{8,9},{9,8},{10,11... | collective-permute-start | bytes 776 | tf_op jit(solution)/shard_map/ppermute | solution.py:266
  30.6 14.2 %collective-permute-start.7 = (bf16[512,256]{1,0:T(8,128)(2,1)S(1)}, bf16[512,256]{1,0:T(8,128)(2,1)S(1)}, u32[]{:S(2)}, u32[]{:S(2)}) collective-permute-start(bf16[512,256]{1,0:T(8,128)(2,1)S(1)} %collective-permute-done.6.refs_3_), channel_id=1, source_target_pairs={{0,2},{2,6},{6,4},{4,0},{1,3},{3,7},{7,5},{5,1},{8,10},{10,14},{14... | collective-permute-start | bytes 786440 | tf_op jit(solution)/shard_map/ppermute | solution.py:273
  39.1 11.2 %collective-permute-start.9 = (bf16[512,256]{1,0:T(8,128)(2,1)S(1)}, bf16[512,256]{1,0:T(8,128)(2,1)S(1)}, u32[]{:S(2)}, u32[]{:S(2)}) collective-permute-start(bf16[512,256]{1,0:T(8,128)(2,1)S(1)} %collective-permute-done.8.refs_2_), channel_id=1, source_target_pairs={{0,2},{2,6},{6,4},{4,0},{1,3},{3,7},{7,5},{5,1},{8,10},{10,14},{14... | collective-permute-start | bytes 786440 | tf_op jit(solution)/shard_map/ppermute | solution.py:273
  44.7 13.8 %collective-permute-start.11 = (bf16[512,256]{1,0:T(8,128)(2,1)S(1)}, bf16[512,256]{1,0:T(8,128)(2,1)S(1)}, u32[]{:S(2)}, u32[]{:S(2)}) collective-permute-start(bf16[512,256]{1,0:T(8,128)(2,1)S(1)} %collective-permute-done.7.refs_3_), channel_id=1, source_target_pairs={{0,2},{2,6},{6,4},{4,0},{1,3},{3,7},{7,5},{5,1},{8,10},{10,14},{14... | collective-permute-start | bytes 786440 | tf_op jit(solution)/shard_map/ppermute | solution.py:273
  44.7 15.5 %collective-permute-start.13 = (bf16[128,1024]{1,0:T(8,128)(2,1)S(1)}, bf16[128,1024]{1,0:T(8,128)(2,1)S(1)}, u32[]{:S(2)}, u32[]{:S(2)}) collective-permute-start(bf16[128,1024]{1,0:T(8,128)(2,1)S(1)} %get-tuple-element.107), channel_id=1, source_target_pairs={{0,8},{8,0},{16,24},{24,16},{1,9},{9,1},{17,25},{25,17},{2,10},{10... | collective-permute-start | bytes 786440 | tf_op jit(solution)/shard_map/ppermute | solution.py:269
  45.5 14.8 %collective-permute-start.14 = (bf16[128,1024]{1,0:T(8,128)(2,1)S(1)}, bf16[128,1024]{1,0:T(8,128)(2,1)S(1)}, u32[]{:S(2)}, u32[]{:S(2)}) collective-permute-start(bf16[128,1024]{1,0:T(8,128)(2,1)S(1)} %get-tuple-element.108), channel_id=1, source_target_pairs={{0,16},{8,24},{16,0},{24,8},{1,17},{9,25},{17,1},{25,9},{2,18},{10... | collective-permute-start | bytes 786440 | tf_op jit(solution)/shard_map/ppermute | solution.py:269
  50.4 9.9 %collective-permute-start.15 = (bf16[128,1024]{1,0:T(8,128)(2,1)S(1)}, bf16[128,1024]{1,0:T(8,128)(2,1)S(1)}, u32[]{:S(2)}, u32[]{:S(2)}) collective-permute-start(bf16[128,1024]{1,0:T(8,128)(2,1)S(1)} %get-tuple-element.109), channel_id=1, source_target_pairs={{0,24},{8,16},{16,8},{24,0},{1,25},{9,17},{17,9},{25,1},{2,26},{10... | collective-permute-start | bytes 786440 | tf_op jit(solution)/shard_map/ppermute | solution.py:269
  51.5 11.4 %collective-permute-start.10 = (bf16[512,256]{1,0:T(8,128)(2,1)S(1)}, bf16[512,256]{1,0:T(8,128)(2,1)S(1)}, u32[]{:S(2)}, u32[]{:S(2)}) collective-permute-start(bf16[512,256]{1,0:T(8,128)(2,1)S(1)} %collective-permute-done.9.refs_2_), channel_id=1, source_target_pairs={{0,2},{2,6},{6,4},{4,0},{1,3},{3,7},{7,5},{5,1},{8,10},{10,14},{14... | collective-permute-start | bytes 786440 | tf_op jit(solution)/shard_map/ppermute | solution.py:273
  58.5 8.3 %collective-permute-start.12 = (bf16[512,256]{1,0:T(8,128)(2,1)S(1)}, bf16[512,256]{1,0:T(8,128)(2,1)S(1)}, u32[]{:S(2)}, u32[]{:S(2)}) collective-permute-start(bf16[512,256]{1,0:T(8,128)(2,1)S(1)} %collective-permute-done.11.refs_3_), channel_id=1, source_target_pairs={{0,2},{2,6},{6,4},{4,0},{1,3},{3,7},{7,5},{5,1},{8,10},{10,14},{14... | collective-permute-start | bytes 786440 | tf_op jit(solution)/shard_map/ppermute | solution.py:273
  60.6 38.6 %collective-permute-start.17 = (bf16[1024,512]{1,0:T(8,128)(2,1)S(1)}, bf16[1024,512]{1,0:T(8,128)(2,1)S(1)}, u32[]{:S(2)}, u32[]{:S(2)}) collective-permute-start(bf16[1024,512]{1,0:T(8,128)(2,1)S(1)} %get-tuple-element.115.refs_0_), channel_id=1, source_target_pairs={{0,1},{1,0},{2,3},{3,2},{4,5},{5,4},{6,7},{7,6},{8,9},{9,8},{10,11... | collective-permute-start | bytes 3145736 | tf_op jit(solution)/shard_map/ppermute | solution.py:266
  68.4 9.3 %collective-permute-start.21 = (bf16[512,256]{1,0:T(8,128)(2,1)S(1)}, bf16[512,256]{1,0:T(8,128)(2,1)S(1)}, u32[]{:S(2)}, u32[]{:S(2)}) collective-permute-start(bf16[512,256]{1,0:T(8,128)(2,1)S(1)} %get-tuple-element.127), channel_id=1, source_target_pairs={{0,4},{2,0},{6,2},{4,6},{1,5},{3,1},{7,3},{5,7},{8,12},{10,8},{14,... | collective-permute-start | bytes 786440 | tf_op jit(solution)/shard_map/ppermute | solution.py:273
  70.0 13.2 %collective-permute-start.18 = (bf16[512,256]{1,0:T(8,128)(2,1)S(1)}, bf16[512,256]{1,0:T(8,128)(2,1)S(1)}, u32[]{:S(2)}, u32[]{:S(2)}) collective-permute-start(bf16[512,256]{1,0:T(8,128)(2,1)S(1)} %get-tuple-element.121), channel_id=1, source_target_pairs={{0,4},{2,0},{6,2},{4,6},{1,5},{3,1},{7,3},{5,7},{8,12},{10,8},{14,... | collective-permute-start | bytes 786440 | tf_op jit(solution)/shard_map/ppermute | solution.py:273
  78.3 9.2 %collective-permute-start.22 = (bf16[512,256]{1,0:T(8,128)(2,1)S(1)}, bf16[512,256]{1,0:T(8,128)(2,1)S(1)}, u32[]{:S(2)}, u32[]{:S(2)}) collective-permute-start(bf16[512,256]{1,0:T(8,128)(2,1)S(1)} %get-tuple-element.128), channel_id=1, source_target_pairs={{0,4},{2,0},{6,2},{4,6},{1,5},{3,1},{7,3},{5,7},{8,12},{10,8},{14,... | collective-permute-start | bytes 786440 | tf_op jit(solution)/shard_map/ppermute | solution.py:273
  80.8 10.3 %collective-permute-start.16 = (bf16[512,256]{1,0:T(8,128)(2,1)S(1)}, bf16[512,256]{1,0:T(8,128)(2,1)S(1)}, u32[]{:S(2)}, u32[]{:S(2)}) collective-permute-start(bf16[512,256]{1,0:T(8,128)(2,1)S(1)} %get-tuple-element.114), channel_id=1, source_target_pairs={{0,1},{1,0},{2,3},{3,2},{4,5},{5,4},{6,7},{7,6},{8,9},{9,8},{10,11... | collective-permute-start | bytes 786440 | tf_op jit(solution)/shard_map/ppermute | solution.py:266
  83.9 9.3 %collective-permute-start.19 = (bf16[512,256]{1,0:T(8,128)(2,1)S(1)}, bf16[512,256]{1,0:T(8,128)(2,1)S(1)}, u32[]{:S(2)}, u32[]{:S(2)}) collective-permute-start(bf16[512,256]{1,0:T(8,128)(2,1)S(1)} %get-tuple-element.122), channel_id=1, source_target_pairs={{0,4},{2,0},{6,2},{4,6},{1,5},{3,1},{7,3},{5,7},{8,12},{10,8},{14,... | collective-permute-start | bytes 786440 | tf_op jit(solution)/shard_map/ppermute | solution.py:273
  88.2 10.6 %collective-permute-start.23 = (bf16[512,256]{1,0:T(8,128)(2,1)S(1)}, bf16[512,256]{1,0:T(8,128)(2,1)S(1)}, u32[]{:S(2)}, u32[]{:S(2)}) collective-permute-start(bf16[512,256]{1,0:T(8,128)(2,1)S(1)} %get-tuple-element.129), channel_id=1, source_target_pairs={{0,4},{2,0},{6,2},{4,6},{1,5},{3,1},{7,3},{5,7},{8,12},{10,8},{14,... | collective-permute-start | bytes 786440 | tf_op jit(solution)/shard_map/ppermute | solution.py:273
  93.8 9.1 %collective-permute-start.20 = (bf16[512,256]{1,0:T(8,128)(2,1)S(1)}, bf16[512,256]{1,0:T(8,128)(2,1)S(1)}, u32[]{:S(2)}, u32[]{:S(2)}) collective-permute-start(bf16[512,256]{1,0:T(8,128)(2,1)S(1)} %get-tuple-element.123), channel_id=1, source_target_pairs={{0,4},{2,0},{6,2},{4,6},{1,5},{3,1},{7,3},{5,7},{8,12},{10,8},{14,... | collective-permute-start | bytes 786440 | tf_op jit(solution)/shard_map/ppermute | solution.py:273
  103.9 6.5 %collective-permute-start.24 = (bf16[256,256]{1,0:T(8,128)(2,1)S(1)}, bf16[256,256]{1,0:T(8,128)(2,1)S(1)}, u32[]{:S(2)}, u32[]{:S(2)}) collective-permute-start(bf16[256,256]{1,0:T(8,128)(2,1)S(1)} %get-tuple-element.130), channel_id=1, source_target_pairs={{0,24},{8,16},{16,8},{24,0},{1,25},{9,17},{17,9},{25,1},{2,26},{10... | collective-permute-start | bytes 393224 | tf_op jit(solution)/shard_map/ppermute | solution.py:269
  105.4 6.3 %collective-permute-start.25 = (bf16[256,256]{1,0:T(8,128)(2,1)S(1)}, bf16[256,256]{1,0:T(8,128)(2,1)S(1)}, u32[]{:S(2)}, u32[]{:S(2)}) collective-permute-start(bf16[256,256]{1,0:T(8,128)(2,1)S(1)} %get-tuple-element.131), channel_id=1, source_target_pairs={{0,16},{8,24},{16,0},{24,8},{1,17},{9,25},{17,1},{25,9},{2,18},{10... | collective-permute-start | bytes 393224 | tf_op jit(solution)/shard_map/ppermute | solution.py:269
  106.6 5.1 %collective-permute-start.26 = (bf16[256,256]{1,0:T(8,128)(2,1)S(1)}, bf16[256,256]{1,0:T(8,128)(2,1)S(1)}, u32[]{:S(2)}, u32[]{:S(2)}) collective-permute-start(bf16[256,256]{1,0:T(8,128)(2,1)S(1)} %get-tuple-element.132), channel_id=1, source_target_pairs={{0,8},{8,0},{16,24},{24,16},{1,9},{9,1},{17,25},{25,17},{2,10},{10... | collective-permute-start | bytes 393224 | tf_op jit(solution)/shard_map/ppermute | solution.py:269
  111.8 5.0 %collective-permute-start.27 = (bf16[256,256]{1,0:T(8,128)(2,1)S(1)}, bf16[256,256]{1,0:T(8,128)(2,1)S(1)}, u32[]{:S(2)}, u32[]{:S(2)}) collective-permute-start(bf16[256,256]{1,0:T(8,128)(2,1)S(1)} %sum.3.refs_0_), channel_id=1, source_target_pairs={{0,2},{2,0},{4,6},{6,4},{1,3},{3,1},{5,7},{7,5},{8,10},{10,8},{12,... | collective-permute-start | bytes 393224 | tf_op jit(solution)/shard_map/ppermute | solution.py:430
  116.9 7.3 %collective-permute-start.28 = (bf16[256,256]{1,0:T(8,128)(2,1)S(1)}, bf16[256,256]{1,0:T(8,128)(2,1)S(1)}, u32[]{:S(2)}, u32[]{:S(2)}) collective-permute-start(bf16[256,256]{1,0:T(8,128)(2,1)S(1)} %sum.4.refs_0_), channel_id=1, source_target_pairs={{0,4},{2,6},{4,0},{6,2},{1,5},{3,7},{5,1},{7,3},{8,12},{10,14},{12... | collective-permute-start | bytes 393224 | tf_op jit(solution)/shard_map/ppermute | solution.py:430
  124.3 1.4 %collective-permute-start.29 = (bf16[256,256]{1,0:T(8,128)(2,1)S(1)}, bf16[256,256]{1,0:T(8,128)(2,1)S(1)}, u32[]{:S(2)}, u32[]{:S(2)}) collective-permute-start(bf16[256,256]{1,0:T(8,128)(2,1)S(1)} %sum.5.refs_2_), channel_id=1, source_target_pairs={{0,1},{1,0},{2,3},{3,2},{4,5},{5,4},{6,7},{7,6},{8,9},{9,8},{10,11... | collective-permute-start | bytes 393224 | tf_op jit(solution)/shard_map/ppermute | solution.py:266
  125.7 6.0 %collective-permute-start.30 = (bf16[256,256]{1,0:T(8,128)(2,1)S(1)}, bf16[256,256]{1,0:T(8,128)(2,1)S(1)}, u32[]{:S(2)}, u32[]{:S(2)}) collective-permute-start(bf16[256,256]{1,0:T(8,128)(2,1)S(1)} %sum.5.refs_2_), channel_id=1, source_target_pairs={{0,8},{8,0},{16,24},{24,16},{1,9},{9,1},{17,25},{25,17},{2,10},{10... | collective-permute-start | bytes 393224 | tf_op jit(solution)/shard_map/ppermute | solution.py:269
  127.0 8.1 %collective-permute-start.31 = (bf16[256,256]{1,0:T(8,128)(2,1)S(1)}, bf16[256,256]{1,0:T(8,128)(2,1)S(1)}, u32[]{:S(2)}, u32[]{:S(2)}) collective-permute-start(bf16[256,256]{1,0:T(8,128)(2,1)S(1)} %sum.5.refs_2_), channel_id=1, source_target_pairs={{0,16},{8,24},{16,0},{24,8},{1,17},{9,25},{17,1},{25,9},{2,18},{10... | collective-permute-start | bytes 393224 | tf_op jit(solution)/shard_map/ppermute | solution.py:269
  127.7 7.4 %collective-permute-start.32 = (bf16[256,256]{1,0:T(8,128)(2,1)S(1)}, bf16[256,256]{1,0:T(8,128)(2,1)S(1)}, u32[]{:S(2)}, u32[]{:S(2)}) collective-permute-start(bf16[256,256]{1,0:T(8,128)(2,1)S(1)} %sum.5.refs_2_), channel_id=1, source_target_pairs={{0,24},{8,16},{16,8},{24,0},{1,25},{9,17},{17,9},{25,1},{2,26},{10... | collective-permute-start | bytes 393224 | tf_op jit(solution)/shard_map/ppermute | solution.py:269
  131.7 4.8 %collective-permute-start.33 = (bf16[256,256]{1,0:T(8,128)(2,1)S(1)}, bf16[256,256]{1,0:T(8,128)(2,1)S(1)}, u32[]{:S(2)}, u32[]{:S(2)}) collective-permute-start(bf16[256,256]{1,0:T(8,128)(2,1)S(1)} %collective-permute-done.30.refs_3_), channel_id=1, source_target_pairs={{0,1},{1,0},{2,3},{3,2},{4,5},{5,4},{6,7},{7,6},{8,9},{9,8},{10,11... | collective-permute-start | bytes 393224 | tf_op jit(solution)/shard_map/ppermute | solution.py:266
  135.1 1.4 %collective-permute-start.34 = (bf16[256,256]{1,0:T(8,128)(2,1)S(1)}, bf16[256,256]{1,0:T(8,128)(2,1)S(1)}, u32[]{:S(2)}, u32[]{:S(2)}) collective-permute-start(bf16[256,256]{1,0:T(8,128)(2,1)S(1)} %collective-permute-done.31.refs_4_), channel_id=1, source_target_pairs={{0,1},{1,0},{2,3},{3,2},{4,5},{5,4},{6,7},{7,6},{8,9},{9,8},{10,11... | collective-permute-start | bytes 393224 | tf_op jit(solution)/shard_map/ppermute | solution.py:266
  135.1 1.5 %collective-permute-start.35 = (bf16[256,256]{1,0:T(8,128)(2,1)S(1)}, bf16[256,256]{1,0:T(8,128)(2,1)S(1)}, u32[]{:S(2)}, u32[]{:S(2)}) collective-permute-start(bf16[256,256]{1,0:T(8,128)(2,1)S(1)} %collective-permute-done.32.refs_5_), channel_id=1, source_target_pairs={{0,1},{1,0},{2,3},{3,2},{4,5},{5,4},{6,7},{7,6},{8,9},{9,8},{10,11... | collective-permute-start | bytes 393224 | tf_op jit(solution)/shard_map/ppermute | solution.py:266

commit v20 on v16

--- a/solution.py
+++ b/solution.py
@@ -423,12 +423,12 @@
         )[0]
 
     mine = total_of(across(terms)[::-1])
-    step = 1
-    while step < z.zz:
+    step = z.zz // 2
+    while step:
         mine = total_of(
             [mine, lax.ppermute(mine, "zz", [(i, i ^ step) for i in range(z.zz)])]
         )
-        step *= 2
+        step //= 2
     mine = across([mine] * z.grp)
     (grad_weight,) = call(
         lambda *refs: last_kernel(z, *refs),

time: 136 us -> 136 us (level)
  waiting for transfers between devices: 59.6 us -> 61.2 us
  starting transfers between devices: 40.6 us -> 39.1 us
    ppermute x2, waiting for transfers between devices: 8.6 us -> 10.1 us  [shards(): lax.ppermute(mine, 'zz', [(i, i ^ step) for i in range(z.zz)])]
    ppermute x2, starting transfers between devices: 3.77 us -> 2.32 us  [shards(): lax.ppermute(mine, 'zz', [(i, i ^ step) for i in range(z.zz)])]
where the time goes in v20:
time: 136 us
  waiting for transfers between devices  61.2 us (45%)
  starting transfers between devices  39.1 us (29%)
  Pallas kernels  30.3 us (22%)
  local copies, waits for them, and re-layouts  3.19 us (2%)
    ppermute x12, waiting for transfers between devices, to_zz(): lax.ppermute(x, 'zz', [(order[i], order[(i + k) % z.zz]) for i in range(z...  32.2 us
    pallas_call x25, Pallas kernels, call(): pl.pallas_call(kernel, out_shape=tuple((jax.ShapeDtypeStruct(s, d) for s,...  30.3 us
    ppermute x12, starting transfers between devices, to_zz(): lax.ppermute(x, 'zz', [(order[i], order[(i + k) % z.zz]) for i in range(z...  15.4 us
    ppermute x12, waiting for transfers between devices, to_grp(): lax.ppermute(x, 'grp', [(i, i ^ s) for i in range(z.grp)])  13.9 us
    ppermute x12, starting transfers between devices, to_grp(): lax.ppermute(x, 'grp', [(i, i ^ s) for i in range(z.grp)])  13.6 us
    ppermute x2, waiting for transfers between devices, shards(): lax.ppermute(mine, 'zz', [(i, i ^ step) for i in range(z.zz)])  10.1 us
    all_to_all x1, starting transfers between devices, shards(): lax.all_to_all(message, ('grp', 'zz', 'core'), split_axis=0, concat_axis=...  6.96 us
    all_to_all x1, waiting for transfers between devices, shards(): lax.all_to_all(message, ('grp', 'zz', 'core'), split_axis=0, concat_axis=...  4.42 us
  transfers between devices with their start and end apart: 37, of which 22 were waited for; matrix products, arithmetic and copies ran while one was open for 1% of the time, Pallas kernels for 19%

profile of v20, /device:TPU:0, one launch (start us, length us, event | category | flops | bytes accessed | tf_op | source)
XLA Modules:
  0.0 135.7 jit_solution(2603778363109437135)
XLA Ops:
  1.9 1.8 %index.1 = s32[32,8,128]{2,1,0:T(8,128)} custom-call(s32[3]{0:T(128)S(1)} %pad_add_fusion.refs_0_, s32[1,512]{1,0:T(1,128)S(1)} %bitcast.4), custom_call_target="tpu_custom_call" | custom-call | flops 100000000 | tf_op jit(solution)/shard_map/index/pallas_call | solution.py:59
  3.7 7.0 %all-to-all-start = ((s32[32,8,128]{2,1,0:T(8,128)}), s32[32,8,128]{2,1,0:T(8,128)S(1)}, u32[]{:S(2)}, u32[]{:S(2)}) async-start(s32[32,8,128]{2,1,0:T(8,128)} %index.1), calls=%async_computation | async-start | bytes 262144 | tf_op jit(solution)/shard_map/all_to_all | solution.py:282
  10.6 1.2 copy-done
  11.9 1.2 copy-done.3
  13.1 1.3 product.1
  14.4 4.4 %all-to-all-done.refs_1_.refs_2_ = s32[32,8,128]{2,1,0:T(8,128)S(1)} async-done(((s32[32,8,128]{2,1,0:T(8,128)}), s32[32,8,128]{2,1,0:T(8,128)S(1)}, u32[]{:S(2)}, u32[]{:S(2)}) %all-to-all-start) | async-done | bytes 131104 | tf_op jit(solution)/shard_map/all_to_all | solution.py:282
  18.8 1.2 send.1
  20.0 1.0 collective-permute-start
  21.1 1.3 collective-permute-start.1
  22.4 1.2 collective-permute-start.2
  23.7 3.7 %collective-permute-done.refs_0_ = bf16[2,128,256]{2,1,0:T(8,128)(2,1)S(1)} collective-permute-done((bf16[2,128,256]{2,1,0:T(8,128)(2,1)S(1)}, bf16[2,128,256]{2,1,0:T(8,128)(2,1)S(1)}, u32[]{:S(2)}, u32[]{:S(2)}) %collective-permute-start) | collective-permute-done | bytes 131104 | tf_op jit(solution)/shard_map/ppermute | solution.py:268
  27.4 1.6 %collective-permute-done.1.refs_1_ = bf16[2,128,256]{2,1,0:T(8,128)(2,1)S(1)} collective-permute-done((bf16[2,128,256]{2,1,0:T(8,128)(2,1)S(1)}, bf16[2,128,256]{2,1,0:T(8,128)(2,1)S(1)}, u32[]{:S(2)}, u32[]{:S(2)}) %collective-permute-start.1) | collective-permute-done | bytes 131104 | tf_op jit(solution)/shard_map/ppermute | solution.py:268
  30.6 1.2 collective-permute-start.7
  31.8 5.9 %prepare.2 = (bf16[1024,512]{1,0:T(8,128)(2,1)S(1)}, bf16[1024,512]{1,0:T(8,128)(2,1)S(1)}, bf16[1024,512]{1,0:T(8,128)(2,1)S(1)}, bf16[1024,512]{1,0:T(8,128)(2,1)S(1)}, f32[8,128]{1,0:T(8,128)S(1)}) custom-call(s32[3]{0:T(128)S(1)} %pad_add_fusion.refs_0_, s32[4,16]{1,0:T(4,128)S(1)} %fusion.refs_1_, s32[32,8,128]{2,1,0:T(8,128)S(1)} %all-to-all-done.refs_1_.refs_2_, ...), custom_call_target="tpu_custom_call" | custom-call | flops 700000000 | tf_op jit(solution)/shard_map/prepare/pallas_call | solution.py:59
  37.7 1.4 %collective-permute-done.8.refs_2_ = bf16[512,256]{1,0:T(8,128)(2,1)S(1)} collective-permute-done((bf16[512,256]{1,0:T(8,128)(2,1)S(1)}, bf16[512,256]{1,0:T(8,128)(2,1)S(1)}, u32[]{:S(2)}, u32[]{:S(2)}) %collective-permute-start.8) | collective-permute-done | bytes 262176 | tf_op jit(solution)/shard_map/ppermute | solution.py:272
  39.1 5.6 %collective-permute-done.7.refs_3_ = bf16[512,256]{1,0:T(8,128)(2,1)S(1)} collective-permute-done((bf16[512,256]{1,0:T(8,128)(2,1)S(1)}, bf16[512,256]{1,0:T(8,128)(2,1)S(1)}, u32[]{:S(2)}, u32[]{:S(2)}) %collective-permute-start.7) | collective-permute-done | bytes 262176 | tf_op jit(solution)/shard_map/ppermute | solution.py:272
  45.5 1.0 collective-permute-start.14
  46.5 3.9 %collective-permute-done.9.refs_2_ = bf16[512,256]{1,0:T(8,128)(2,1)S(1)} collective-permute-done((bf16[512,256]{1,0:T(8,128)(2,1)S(1)}, bf16[512,256]{1,0:T(8,128)(2,1)S(1)}, u32[]{:S(2)}, u32[]{:S(2)}) %collective-permute-start.9) | collective-permute-done | bytes 262176 | tf_op jit(solution)/shard_map/ppermute | solution.py:272
  50.4 1.2 collective-permute-start.15
  51.5 6.9 %prepare.3 = (bf16[1024,512]{1,0:T(8,128)(2,1)S(1)}, bf16[1024,512]{1,0:T(8,128)(2,1)S(1)}, bf16[1024,512]{1,0:T(8,128)(2,1)S(1)}, bf16[1024,512]{1,0:T(8,128)(2,1)S(1)}, f32[8,128]{1,0:T(8,128)S(1)}) custom-call(s32[3]{0:T(128)S(1)} %pad_add_fusion.refs_0_, s32[4,16]{1,0:T(4,128)S(1)} %collective-permute-done.4.refs_5_.refs_1_, ...), custom_call_target="tpu_custom_call" | custom-call | flops 700000000 | tf_op jit(solution)/shard_map/prepare/pallas_call | solution.py:59
  58.5 1.7 %collective-permute-start.12 = (bf16[512,256]{1,0:T(8,128)(2,1)S(1)}, bf16[512,256]{1,0:T(8,128)(2,1)S(1)}, u32[]{:S(2)}, u32[]{:S(2)}) collective-permute-start(bf16[512,256]{1,0:T(8,128)(2,1)S(1)} %collective-permute-done.11.refs_3_), channel_id=1, source_target_pairs={{0,2},{2,6},{6,4},{4,0},{1,3},{3,7},{7,5},{5,1},{8,10},{10,14},{14... | collective-permute-start | bytes 786440 | tf_op jit(solution)/shard_map/ppermute | solution.py:272
  63.0 3.8 %collective-permute-done.12.refs_3_ = bf16[512,256]{1,0:T(8,128)(2,1)S(1)} collective-permute-done((bf16[512,256]{1,0:T(8,128)(2,1)S(1)}, bf16[512,256]{1,0:T(8,128)(2,1)S(1)}, u32[]{:S(2)}, u32[]{:S(2)}) %collective-permute-start.12) | collective-permute-done | bytes 262176 | tf_op jit(solution)/shard_map/ppermute | solution.py:272
  66.8 1.6 %forward.7 = (bf16[512,256]{1,0:T(8,128)(2,1)S(1)}, bf16[512,256]{1,0:T(8,128)(2,1)S(1)}, bf16[512,256]{1,0:T(8,128)(2,1)S(1)}, bf16[512,256]{1,0:T(8,128)(2,1)S...) custom-call(bf16[1024,512]{1,0:T(8,128)(2,1)S(1)} %get-tuple-element.82.refs_0_.refs_8_, ...), custom_call_target="tpu_custom_call" | custom-call | flops 300000000 | tf_op jit(solution)/shard_map/forward/pallas_call | solution.py:59
  68.4 1.6 %collective-permute-start.21 = (bf16[512,256]{1,0:T(8,128)(2,1)S(1)}, bf16[512,256]{1,0:T(8,128)(2,1)S(1)}, u32[]{:S(2)}, u32[]{:S(2)}) collective-permute-start(bf16[512,256]{1,0:T(8,128)(2,1)S(1)} %get-tuple-element.125), channel_id=1, source_target_pairs={{0,4},{2,0},{6,2},{4,6},{1,5},{3,1},{7,3},{5,7},{8,12},{10,8},{14,... | collective-permute-start | bytes 786440 | tf_op jit(solution)/shard_map/ppermute | solution.py:272
  70.8 6.9 %collective-permute-done.21.refs_1_ = bf16[512,256]{1,0:T(8,128)(2,1)S(1)} collective-permute-done((bf16[512,256]{1,0:T(8,128)(2,1)S(1)}, bf16[512,256]{1,0:T(8,128)(2,1)S(1)}, u32[]{:S(2)}, u32[]{:S(2)}) %collective-permute-start.21) | collective-permute-done | bytes 262176 | tf_op jit(solution)/shard_map/ppermute | solution.py:272
  78.3 2.5 %collective-permute-start.22 = (bf16[512,256]{1,0:T(8,128)(2,1)S(1)}, bf16[512,256]{1,0:T(8,128)(2,1)S(1)}, u32[]{:S(2)}, u32[]{:S(2)}) collective-permute-start(bf16[512,256]{1,0:T(8,128)(2,1)S(1)} %get-tuple-element.126), channel_id=1, source_target_pairs={{0,4},{2,0},{6,2},{4,6},{1,5},{3,1},{7,3},{5,7},{8,12},{10,8},{14,... | collective-permute-start | bytes 786440 | tf_op jit(solution)/shard_map/ppermute | solution.py:272
  80.8 2.5 %collective-permute-done.18.refs_1_ = bf16[512,256]{1,0:T(8,128)(2,1)S(1)} collective-permute-done((bf16[512,256]{1,0:T(8,128)(2,1)S(1)}, bf16[512,256]{1,0:T(8,128)(2,1)S(1)}, u32[]{:S(2)}, u32[]{:S(2)}) %collective-permute-start.18) | collective-permute-done | bytes 262176 | tf_op jit(solution)/shard_map/ppermute | solution.py:272
  83.9 2.0 %collective-permute-start.19 = (bf16[512,256]{1,0:T(8,128)(2,1)S(1)}, bf16[512,256]{1,0:T(8,128)(2,1)S(1)}, u32[]{:S(2)}, u32[]{:S(2)}) collective-permute-start(bf16[512,256]{1,0:T(8,128)(2,1)S(1)} %get-tuple-element.120), channel_id=1, source_target_pairs={{0,4},{2,0},{6,2},{4,6},{1,5},{3,1},{7,3},{5,7},{8,12},{10,8},{14,... | collective-permute-start | bytes 786440 | tf_op jit(solution)/shard_map/ppermute | solution.py:272
  88.2 2.9 %collective-permute-start.23 = (bf16[512,256]{1,0:T(8,128)(2,1)S(1)}, bf16[512,256]{1,0:T(8,128)(2,1)S(1)}, u32[]{:S(2)}, u32[]{:S(2)}) collective-permute-start(bf16[512,256]{1,0:T(8,128)(2,1)S(1)} %get-tuple-element.127), channel_id=1, source_target_pairs={{0,4},{2,0},{6,2},{4,6},{1,5},{3,1},{7,3},{5,7},{8,12},{10,8},{14,... | collective-permute-start | bytes 786440 | tf_op jit(solution)/shard_map/ppermute | solution.py:272
  91.0 2.1 %collective-permute-done.19.refs_1_ = bf16[512,256]{1,0:T(8,128)(2,1)S(1)} collective-permute-done((bf16[512,256]{1,0:T(8,128)(2,1)S(1)}, bf16[512,256]{1,0:T(8,128)(2,1)S(1)}, u32[]{:S(2)}, u32[]{:S(2)}) %collective-permute-start.19) | collective-permute-done | bytes 262176 | tf_op jit(solution)/shard_map/ppermute | solution.py:272
  93.8 2.9 %collective-permute-start.20 = (bf16[512,256]{1,0:T(8,128)(2,1)S(1)}, bf16[512,256]{1,0:T(8,128)(2,1)S(1)}, u32[]{:S(2)}, u32[]{:S(2)}) collective-permute-start(bf16[512,256]{1,0:T(8,128)(2,1)S(1)} %get-tuple-element.121), channel_id=1, source_target_pairs={{0,4},{2,0},{6,2},{4,6},{1,5},{3,1},{7,3},{5,7},{8,12},{10,8},{14,... | collective-permute-start | bytes 786440 | tf_op jit(solution)/shard_map/ppermute | solution.py:272
  97.3 1.4 %collective-permute-done.23.refs_2_ = bf16[512,256]{1,0:T(8,128)(2,1)S(1)} collective-permute-done((bf16[512,256]{1,0:T(8,128)(2,1)S(1)}, bf16[512,256]{1,0:T(8,128)(2,1)S(1)}, u32[]{:S(2)}, u32[]{:S(2)}) %collective-permute-start.23) | collective-permute-done | bytes 262176 | tf_op jit(solution)/shard_map/ppermute | solution.py:272
  99.2 3.7 %collective-permute-done.20.refs_3_ = bf16[512,256]{1,0:T(8,128)(2,1)S(1)} collective-permute-done((bf16[512,256]{1,0:T(8,128)(2,1)S(1)}, bf16[512,256]{1,0:T(8,128)(2,1)S(1)}, u32[]{:S(2)}, u32[]{:S(2)}) %collective-permute-start.20) | collective-permute-done | bytes 262176 | tf_op jit(solution)/shard_map/ppermute | solution.py:272
  102.9 1.0 grad.1
  103.9 1.5 %collective-permute-start.24 = (bf16[256,256]{1,0:T(8,128)(2,1)S(1)}, bf16[256,256]{1,0:T(8,128)(2,1)S(1)}, u32[]{:S(2)}, u32[]{:S(2)}) collective-permute-start(bf16[256,256]{1,0:T(8,128)(2,1)S(1)} %get-tuple-element.128), channel_id=1, source_target_pairs={{0,24},{8,16},{16,8},{24,0},{1,25},{9,17},{17,9},{25,1},{2,26},{10... | collective-permute-start | bytes 393224 | tf_op jit(solution)/shard_map/ppermute | solution.py:268
  105.4 1.2 collective-permute-start.25
  107.5 3.0 %collective-permute-done.24.refs_0_ = bf16[256,256]{1,0:T(8,128)(2,1)S(1)} collective-permute-done((bf16[256,256]{1,0:T(8,128)(2,1)S(1)}, bf16[256,256]{1,0:T(8,128)(2,1)S(1)}, u32[]{:S(2)}, u32[]{:S(2)}) %collective-permute-start.24) | collective-permute-done | bytes 131104 | tf_op jit(solution)/shard_map/ppermute | solution.py:268
  110.4 1.3 collective-permute-done.25.refs_1_
  111.8 2.2 %collective-permute-start.27 = (bf16[256,256]{1,0:T(8,128)(2,1)S(1)}, bf16[256,256]{1,0:T(8,128)(2,1)S(1)}, u32[]{:S(2)}, u32[]{:S(2)}) collective-permute-start(bf16[256,256]{1,0:T(8,128)(2,1)S(1)} %sum.3.refs_0_), channel_id=1, source_target_pairs={{0,4},{2,6},{4,0},{6,2},{1,5},{3,7},{5,1},{7,3},{8,12},{10,14},{12... | collective-permute-start | bytes 393224 | tf_op jit(solution)/shard_map/ppermute | solution.py:429
  114.1 5.2 %collective-permute-done.27.refs_1_ = bf16[256,256]{1,0:T(8,128)(2,1)S(1)} collective-permute-done((bf16[256,256]{1,0:T(8,128)(2,1)S(1)}, bf16[256,256]{1,0:T(8,128)(2,1)S(1)}, u32[]{:S(2)}, u32[]{:S(2)}) %collective-permute-start.27) | collective-permute-done | bytes 131104 | tf_op jit(solution)/shard_map/ppermute | solution.py:429
  119.4 5.0 %collective-permute-done.28.refs_1_ = bf16[256,256]{1,0:T(8,128)(2,1)S(1)} collective-permute-done((bf16[256,256]{1,0:T(8,128)(2,1)S(1)}, bf16[256,256]{1,0:T(8,128)(2,1)S(1)}, u32[]{:S(2)}, u32[]{:S(2)}) %collective-permute-start.28) | collective-permute-done | bytes 131104 | tf_op jit(solution)/shard_map/ppermute | solution.py:429
  124.4 1.2 collective-permute-start.29
  125.5 1.0 collective-permute-start.30
  126.5 1.4 %collective-permute-start.31 = (bf16[256,256]{1,0:T(8,128)(2,1)S(1)}, bf16[256,256]{1,0:T(8,128)(2,1)S(1)}, u32[]{:S(2)}, u32[]{:S(2)}) collective-permute-start(bf16[256,256]{1,0:T(8,128)(2,1)S(1)} %sum.5.refs_1_), channel_id=1, source_target_pairs={{0,24},{8,16},{16,8},{24,0},{1,25},{9,17},{17,9},{25,1},{2,26},{10... | collective-permute-start | bytes 393224 | tf_op jit(solution)/shard_map/ppermute | solution.py:268
  127.9 1.5 %collective-permute-done.29.refs_2_ = bf16[256,256]{1,0:T(8,128)(2,1)S(1)} collective-permute-done((bf16[256,256]{1,0:T(8,128)(2,1)S(1)}, bf16[256,256]{1,0:T(8,128)(2,1)S(1)}, u32[]{:S(2)}, u32[]{:S(2)}) %collective-permute-start.29) | collective-permute-done | bytes 131104 | tf_op jit(solution)/shard_map/ppermute | solution.py:268
  129.4 1.1 collective-permute-done.30.refs_3_
  130.5 1.9 %collective-permute-done.31.refs_4_ = bf16[256,256]{1,0:T(8,128)(2,1)S(1)} collective-permute-done((bf16[256,256]{1,0:T(8,128)(2,1)S(1)}, bf16[256,256]{1,0:T(8,128)(2,1)S(1)}, u32[]{:S(2)}, u32[]{:S(2)}) %collective-permute-start.31) | collective-permute-done | bytes 131104 | tf_op jit(solution)/shard_map/ppermute | solution.py:268
  133.7 2.0 %last.1 = f32[1024,512]{1,0:T(8,128)} custom-call(s32[3]{0:T(128)S(1)} %pad_add_fusion.refs_0_, bf16[256,256]{1,0:T(8,128)(2,1)S(1)} %sum.5.refs_1_, bf16[256,256]{1,0:T(8,128)(2,1)S(1)} %collective-permute-done.29.refs_2_, bf16[256,256]{1,0:T(8,128)(2,1)S(1)} %collective-permute-done.30.refs_3_, bf16[256,256]{1,0:T(8,128)(2,1)S(1)} %collective-permute-done.31.refs_4_, ...), custom_call_target="tpu_custom_call" | custom-call | flops 200000000 | tf_op jit(solution)/shard_map/last/pallas_call | solution.py:59
  (72 shorter events, 15.0 us)
Async XLA Ops:
  0.6 50.9 %collective-permute-start.5 = (bf16[4,16,128,128]{3,2,1,0:T(8,128)(2,1)}, bf16[4,16,128,128]{3,2,1,0:T(8,128)(2,1)}, u32[]{:S(2)}, u32[]{:S(2)}) collective-permute-start(bf16[4,16,128,128]{3,2,1,0:T(8,128)(2,1)} %refs_3_.1), channel_id=1, source_target_pairs={{0,1},{1,0},{2,3},{3,2},{4,5},{5,4},{6,7},{7,6},{8,9},{9,8},{10,11... | collective-permute-start | bytes 6291464 | tf_op jit(solution)/shard_map/ppermute | solution.py:265
  1.2 0.7 copy-start.4
  3.7 15.1 %all-to-all-start = ((s32[32,8,128]{2,1,0:T(8,128)}), s32[32,8,128]{2,1,0:T(8,128)S(1)}, u32[]{:S(2)}, u32[]{:S(2)}) async-start(s32[32,8,128]{2,1,0:T(8,128)} %index.1), calls=%async_computation | async-start | bytes 262144 | tf_op jit(solution)/shard_map/all_to_all | solution.py:282
  10.6 1.2 copy-start
  11.9 1.2 copy-start.3
  13.1 10.5 %copy-start.5 = (bf16[512,512]{1,0:T(8,128)(2,1)S(1)}, bf16[512,512]{1,0:T(8,128)(2,1)}, u32[]{:S(2)}) copy-start(bf16[512,512]{1,0:T(8,128)(2,1)} %param.13) | copy-start | bytes 1572868
  14.4 15.2 %copy-start.6 = (s32[4,16]{1,0:T(4,128)S(1)}, s32[4,16]{1,0:T(4,128)}, u32[]{:S(2)}) copy-start(s32[4,16]{1,0:T(4,128)} %param.9) | copy-start | bytes 772
  14.4 15.2 %copy-start.7 = (s32[4]{0:T(128)S(1)}, s32[4]{0:T(128)}, u32[]{:S(2)}) copy-start(s32[4]{0:T(128)} %param.10) | copy-start | bytes 52
  14.4 15.4 %copy-start.1 = (bf16[512,1024]{1,0:T(8,128)(2,1)S(1)}, bf16[512,1024]{1,0:T(8,128)(2,1)}, u32[]{:S(2)}) copy-start(bf16[512,1024]{1,0:T(8,128)(2,1)} %refs_1_.1) | copy-start | bytes 3145732
  20.0 7.3 %collective-permute-start = (bf16[2,128,256]{2,1,0:T(8,128)(2,1)S(1)}, bf16[2,128,256]{2,1,0:T(8,128)(2,1)S(1)}, u32[]{:S(2)}, u32[]{:S(2)}) collective-permute-start(bf16[2,128,256]{2,1,0:T(8,128)(2,1)S(1)} %get-tuple-element.74), channel_id=1, source_target_pairs={{0,24},{8,16},{16,8},{24,0},{1,25},{9,17},{17,9},{25,1},{2,26},{10... | collective-permute-start | bytes 393224 | tf_op jit(solution)/shard_map/ppermute | solution.py:268
  21.1 7.9 %collective-permute-start.1 = (bf16[2,128,256]{2,1,0:T(8,128)(2,1)S(1)}, bf16[2,128,256]{2,1,0:T(8,128)(2,1)S(1)}, u32[]{:S(2)}, u32[]{:S(2)}) collective-permute-start(bf16[2,128,256]{2,1,0:T(8,128)(2,1)S(1)} %get-tuple-element.75), channel_id=1, source_target_pairs={{0,16},{8,24},{16,0},{24,8},{1,17},{9,25},{17,1},{25,9},{2,18},{10... | collective-permute-start | bytes 393224 | tf_op jit(solution)/shard_map/ppermute | solution.py:268
  22.4 6.6 %collective-permute-start.2 = (bf16[2,128,256]{2,1,0:T(8,128)(2,1)S(1)}, bf16[2,128,256]{2,1,0:T(8,128)(2,1)S(1)}, u32[]{:S(2)}, u32[]{:S(2)}) collective-permute-start(bf16[2,128,256]{2,1,0:T(8,128)(2,1)S(1)} %get-tuple-element.76), channel_id=1, source_target_pairs={{0,8},{8,0},{16,24},{24,16},{1,9},{9,1},{17,25},{25,17},{2,10},{10... | collective-permute-start | bytes 393224 | tf_op jit(solution)/shard_map/ppermute | solution.py:268
  23.6 8.2 %copy-start.2 = (bf16[4,16,128,128]{3,2,1,0:T(8,128)(2,1)S(1)}, bf16[4,16,128,128]{3,2,1,0:T(8,128)(2,1)}, u32[]{:S(2)}) copy-start(bf16[4,16,128,128]{3,2,1,0:T(8,128)(2,1)} %refs_3_.1) | copy-start | bytes 6291460
  23.6 6.2 %collective-permute-start.3 = (bf16[512,256]{1,0:T(8,128)(2,1)S(1)}, bf16[512,256]{1,0:T(8,128)(2,1)S(1)}, u32[]{:S(2)}, u32[]{:S(2)}) collective-permute-start(bf16[512,256]{1,0:T(8,128)(2,1)S(1)} %get-tuple-element.134), channel_id=1, source_target_pairs={{0,1},{1,0},{2,3},{3,2},{4,5},{5,4},{6,7},{7,6},{8,9},{9,8},{10,11... | collective-permute-start | bytes 786440 | tf_op jit(solution)/shard_map/ppermute | solution.py:265
  29.0 1.6 %collective-permute-start.6 = (bf16[512,256]{1,0:T(8,128)(2,1)S(1)}, bf16[512,256]{1,0:T(8,128)(2,1)S(1)}, u32[]{:S(2)}, u32[]{:S(2)}) collective-permute-start(bf16[512,256]{1,0:T(8,128)(2,1)S(1)} %get-tuple-element.83), channel_id=1, source_target_pairs={{0,1},{1,0},{2,3},{3,2},{4,5},{5,4},{6,7},{7,6},{8,9},{9,8},{10,11... | collective-permute-start | bytes 786440 | tf_op jit(solution)/shard_map/ppermute | solution.py:265
  29.1 10.1 %collective-permute-start.8 = (bf16[512,256]{1,0:T(8,128)(2,1)S(1)}, bf16[512,256]{1,0:T(8,128)(2,1)S(1)}, u32[]{:S(2)}, u32[]{:S(2)}) collective-permute-start(bf16[512,256]{1,0:T(8,128)(2,1)S(1)} %get-tuple-element.84.refs_2_), channel_id=1, source_target_pairs={{0,2},{2,6},{6,4},{4,0},{1,3},{3,7},{7,5},{5,1},{8,10},{10,14},{14... | collective-permute-start | bytes 786440 | tf_op jit(solution)/shard_map/ppermute | solution.py:272
  29.6 2.2 %collective-permute-start.4 = (s32[4,16]{1,0:T(4,128)S(1)}, s32[4,16]{1,0:T(4,128)S(1)}, u32[]{:S(2)}, u32[]{:S(2)}) collective-permute-start(s32[4,16]{1,0:T(4,128)S(1)} %fusion.refs_1_), channel_id=1, source_target_pairs={{0,1},{1,0},{2,3},{3,2},{4,5},{5,4},{6,7},{7,6},{8,9},{9,8},{10,11... | collective-permute-start | bytes 776 | tf_op jit(solution)/shard_map/ppermute | solution.py:265
  30.6 14.2 %collective-permute-start.7 = (bf16[512,256]{1,0:T(8,128)(2,1)S(1)}, bf16[512,256]{1,0:T(8,128)(2,1)S(1)}, u32[]{:S(2)}, u32[]{:S(2)}) collective-permute-start(bf16[512,256]{1,0:T(8,128)(2,1)S(1)} %collective-permute-done.6.refs_3_), channel_id=1, source_target_pairs={{0,2},{2,6},{6,4},{4,0},{1,3},{3,7},{7,5},{5,1},{8,10},{10,14},{14... | collective-permute-start | bytes 786440 | tf_op jit(solution)/shard_map/ppermute | solution.py:272
  39.1 11.2 %collective-permute-start.9 = (bf16[512,256]{1,0:T(8,128)(2,1)S(1)}, bf16[512,256]{1,0:T(8,128)(2,1)S(1)}, u32[]{:S(2)}, u32[]{:S(2)}) collective-permute-start(bf16[512,256]{1,0:T(8,128)(2,1)S(1)} %collective-permute-done.8.refs_2_), channel_id=1, source_target_pairs={{0,2},{2,6},{6,4},{4,0},{1,3},{3,7},{7,5},{5,1},{8,10},{10,14},{14... | collective-permute-start | bytes 786440 | tf_op jit(solution)/shard_map/ppermute | solution.py:272
  44.7 13.8 %collective-permute-start.11 = (bf16[512,256]{1,0:T(8,128)(2,1)S(1)}, bf16[512,256]{1,0:T(8,128)(2,1)S(1)}, u32[]{:S(2)}, u32[]{:S(2)}) collective-permute-start(bf16[512,256]{1,0:T(8,128)(2,1)S(1)} %collective-permute-done.7.refs_3_), channel_id=1, source_target_pairs={{0,2},{2,6},{6,4},{4,0},{1,3},{3,7},{7,5},{5,1},{8,10},{10,14},{14... | collective-permute-start | bytes 786440 | tf_op jit(solution)/shard_map/ppermute | solution.py:272
  44.7 15.5 %collective-permute-start.13 = (bf16[128,1024]{1,0:T(8,128)(2,1)S(1)}, bf16[128,1024]{1,0:T(8,128)(2,1)S(1)}, u32[]{:S(2)}, u32[]{:S(2)}) collective-permute-start(bf16[128,1024]{1,0:T(8,128)(2,1)S(1)} %get-tuple-element.105), channel_id=1, source_target_pairs={{0,8},{8,0},{16,24},{24,16},{1,9},{9,1},{17,25},{25,17},{2,10},{10... | collective-permute-start | bytes 786440 | tf_op jit(solution)/shard_map/ppermute | solution.py:268
  45.5 14.8 %collective-permute-start.14 = (bf16[128,1024]{1,0:T(8,128)(2,1)S(1)}, bf16[128,1024]{1,0:T(8,128)(2,1)S(1)}, u32[]{:S(2)}, u32[]{:S(2)}) collective-permute-start(bf16[128,1024]{1,0:T(8,128)(2,1)S(1)} %get-tuple-element.106), channel_id=1, source_target_pairs={{0,16},{8,24},{16,0},{24,8},{1,17},{9,25},{17,1},{25,9},{2,18},{10... | collective-permute-start | bytes 786440 | tf_op jit(solution)/shard_map/ppermute | solution.py:268
  50.4 9.9 %collective-permute-start.15 = (bf16[128,1024]{1,0:T(8,128)(2,1)S(1)}, bf16[128,1024]{1,0:T(8,128)(2,1)S(1)}, u32[]{:S(2)}, u32[]{:S(2)}) collective-permute-start(bf16[128,1024]{1,0:T(8,128)(2,1)S(1)} %get-tuple-element.107), channel_id=1, source_target_pairs={{0,24},{8,16},{16,8},{24,0},{1,25},{9,17},{17,9},{25,1},{2,26},{10... | collective-permute-start | bytes 786440 | tf_op jit(solution)/shard_map/ppermute | solution.py:268
  51.5 11.4 %collective-permute-start.10 = (bf16[512,256]{1,0:T(8,128)(2,1)S(1)}, bf16[512,256]{1,0:T(8,128)(2,1)S(1)}, u32[]{:S(2)}, u32[]{:S(2)}) collective-permute-start(bf16[512,256]{1,0:T(8,128)(2,1)S(1)} %collective-permute-done.9.refs_2_), channel_id=1, source_target_pairs={{0,2},{2,6},{6,4},{4,0},{1,3},{3,7},{7,5},{5,1},{8,10},{10,14},{14... | collective-permute-start | bytes 786440 | tf_op jit(solution)/shard_map/ppermute | solution.py:272
  58.5 8.3 %collective-permute-start.12 = (bf16[512,256]{1,0:T(8,128)(2,1)S(1)}, bf16[512,256]{1,0:T(8,128)(2,1)S(1)}, u32[]{:S(2)}, u32[]{:S(2)}) collective-permute-start(bf16[512,256]{1,0:T(8,128)(2,1)S(1)} %collective-permute-done.11.refs_3_), channel_id=1, source_target_pairs={{0,2},{2,6},{6,4},{4,0},{1,3},{3,7},{7,5},{5,1},{8,10},{10,14},{14... | collective-permute-start | bytes 786440 | tf_op jit(solution)/shard_map/ppermute | solution.py:272
  60.6 38.6 %collective-permute-start.17 = (bf16[1024,512]{1,0:T(8,128)(2,1)S(1)}, bf16[1024,512]{1,0:T(8,128)(2,1)S(1)}, u32[]{:S(2)}, u32[]{:S(2)}) collective-permute-start(bf16[1024,512]{1,0:T(8,128)(2,1)S(1)} %get-tuple-element.113.refs_0_), channel_id=1, source_target_pairs={{0,1},{1,0},{2,3},{3,2},{4,5},{5,4},{6,7},{7,6},{8,9},{9,8},{10,11... | collective-permute-start | bytes 3145736 | tf_op jit(solution)/shard_map/ppermute | solution.py:265
  68.4 9.3 %collective-permute-start.21 = (bf16[512,256]{1,0:T(8,128)(2,1)S(1)}, bf16[512,256]{1,0:T(8,128)(2,1)S(1)}, u32[]{:S(2)}, u32[]{:S(2)}) collective-permute-start(bf16[512,256]{1,0:T(8,128)(2,1)S(1)} %get-tuple-element.125), channel_id=1, source_target_pairs={{0,4},{2,0},{6,2},{4,6},{1,5},{3,1},{7,3},{5,7},{8,12},{10,8},{14,... | collective-permute-start | bytes 786440 | tf_op jit(solution)/shard_map/ppermute | solution.py:272
  70.0 13.2 %collective-permute-start.18 = (bf16[512,256]{1,0:T(8,128)(2,1)S(1)}, bf16[512,256]{1,0:T(8,128)(2,1)S(1)}, u32[]{:S(2)}, u32[]{:S(2)}) collective-permute-start(bf16[512,256]{1,0:T(8,128)(2,1)S(1)} %get-tuple-element.119), channel_id=1, source_target_pairs={{0,4},{2,0},{6,2},{4,6},{1,5},{3,1},{7,3},{5,7},{8,12},{10,8},{14,... | collective-permute-start | bytes 786440 | tf_op jit(solution)/shard_map/ppermute | solution.py:272
  78.3 9.2 %collective-permute-start.22 = (bf16[512,256]{1,0:T(8,128)(2,1)S(1)}, bf16[512,256]{1,0:T(8,128)(2,1)S(1)}, u32[]{:S(2)}, u32[]{:S(2)}) collective-permute-start(bf16[512,256]{1,0:T(8,128)(2,1)S(1)} %get-tuple-element.126), channel_id=1, source_target_pairs={{0,4},{2,0},{6,2},{4,6},{1,5},{3,1},{7,3},{5,7},{8,12},{10,8},{14,... | collective-permute-start | bytes 786440 | tf_op jit(solution)/shard_map/ppermute | solution.py:272
  80.8 10.3 %collective-permute-start.16 = (bf16[512,256]{1,0:T(8,128)(2,1)S(1)}, bf16[512,256]{1,0:T(8,128)(2,1)S(1)}, u32[]{:S(2)}, u32[]{:S(2)}) collective-permute-start(bf16[512,256]{1,0:T(8,128)(2,1)S(1)} %get-tuple-element.112), channel_id=1, source_target_pairs={{0,1},{1,0},{2,3},{3,2},{4,5},{5,4},{6,7},{7,6},{8,9},{9,8},{10,11... | collective-permute-start | bytes 786440 | tf_op jit(solution)/shard_map/ppermute | solution.py:265
  83.9 9.3 %collective-permute-start.19 = (bf16[512,256]{1,0:T(8,128)(2,1)S(1)}, bf16[512,256]{1,0:T(8,128)(2,1)S(1)}, u32[]{:S(2)}, u32[]{:S(2)}) collective-permute-start(bf16[512,256]{1,0:T(8,128)(2,1)S(1)} %get-tuple-element.120), channel_id=1, source_target_pairs={{0,4},{2,0},{6,2},{4,6},{1,5},{3,1},{7,3},{5,7},{8,12},{10,8},{14,... | collective-permute-start | bytes 786440 | tf_op jit(solution)/shard_map/ppermute | solution.py:272
  88.2 10.6 %collective-permute-start.23 = (bf16[512,256]{1,0:T(8,128)(2,1)S(1)}, bf16[512,256]{1,0:T(8,128)(2,1)S(1)}, u32[]{:S(2)}, u32[]{:S(2)}) collective-permute-start(bf16[512,256]{1,0:T(8,128)(2,1)S(1)} %get-tuple-element.127), channel_id=1, source_target_pairs={{0,4},{2,0},{6,2},{4,6},{1,5},{3,1},{7,3},{5,7},{8,12},{10,8},{14,... | collective-permute-start | bytes 786440 | tf_op jit(solution)/shard_map/ppermute | solution.py:272
  93.8 9.1 %collective-permute-start.20 = (bf16[512,256]{1,0:T(8,128)(2,1)S(1)}, bf16[512,256]{1,0:T(8,128)(2,1)S(1)}, u32[]{:S(2)}, u32[]{:S(2)}) collective-permute-start(bf16[512,256]{1,0:T(8,128)(2,1)S(1)} %get-tuple-element.121), channel_id=1, source_target_pairs={{0,4},{2,0},{6,2},{4,6},{1,5},{3,1},{7,3},{5,7},{8,12},{10,8},{14,... | collective-permute-start | bytes 786440 | tf_op jit(solution)/shard_map/ppermute | solution.py:272
  103.9 6.5 %collective-permute-start.24 = (bf16[256,256]{1,0:T(8,128)(2,1)S(1)}, bf16[256,256]{1,0:T(8,128)(2,1)S(1)}, u32[]{:S(2)}, u32[]{:S(2)}) collective-permute-start(bf16[256,256]{1,0:T(8,128)(2,1)S(1)} %get-tuple-element.128), channel_id=1, source_target_pairs={{0,24},{8,16},{16,8},{24,0},{1,25},{9,17},{17,9},{25,1},{2,26},{10... | collective-permute-start | bytes 393224 | tf_op jit(solution)/shard_map/ppermute | solution.py:268
  105.4 6.3 %collective-permute-start.25 = (bf16[256,256]{1,0:T(8,128)(2,1)S(1)}, bf16[256,256]{1,0:T(8,128)(2,1)S(1)}, u32[]{:S(2)}, u32[]{:S(2)}) collective-permute-start(bf16[256,256]{1,0:T(8,128)(2,1)S(1)} %get-tuple-element.129), channel_id=1, source_target_pairs={{0,16},{8,24},{16,0},{24,8},{1,17},{9,25},{17,1},{25,9},{2,18},{10... | collective-permute-start | bytes 393224 | tf_op jit(solution)/shard_map/ppermute | solution.py:268
  106.6 5.1 %collective-permute-start.26 = (bf16[256,256]{1,0:T(8,128)(2,1)S(1)}, bf16[256,256]{1,0:T(8,128)(2,1)S(1)}, u32[]{:S(2)}, u32[]{:S(2)}) collective-permute-start(bf16[256,256]{1,0:T(8,128)(2,1)S(1)} %get-tuple-element.130), channel_id=1, source_target_pairs={{0,8},{8,0},{16,24},{24,16},{1,9},{9,1},{17,25},{25,17},{2,10},{10... | collective-permute-start | bytes 393224 | tf_op jit(solution)/shard_map/ppermute | solution.py:268
  111.8 7.4 %collective-permute-start.27 = (bf16[256,256]{1,0:T(8,128)(2,1)S(1)}, bf16[256,256]{1,0:T(8,128)(2,1)S(1)}, u32[]{:S(2)}, u32[]{:S(2)}) collective-permute-start(bf16[256,256]{1,0:T(8,128)(2,1)S(1)} %sum.3.refs_0_), channel_id=1, source_target_pairs={{0,4},{2,6},{4,0},{6,2},{1,5},{3,7},{5,1},{7,3},{8,12},{10,14},{12... | collective-permute-start | bytes 393224 | tf_op jit(solution)/shard_map/ppermute | solution.py:429
  119.3 5.0 %collective-permute-start.28 = (bf16[256,256]{1,0:T(8,128)(2,1)S(1)}, bf16[256,256]{1,0:T(8,128)(2,1)S(1)}, u32[]{:S(2)}, u32[]{:S(2)}) collective-permute-start(bf16[256,256]{1,0:T(8,128)(2,1)S(1)} %sum.4.refs_0_), channel_id=1, source_target_pairs={{0,2},{2,0},{4,6},{6,4},{1,3},{3,1},{5,7},{7,5},{8,10},{10,8},{12,... | collective-permute-start | bytes 393224 | tf_op jit(solution)/shard_map/ppermute | solution.py:429
  124.4 5.0 %collective-permute-start.29 = (bf16[256,256]{1,0:T(8,128)(2,1)S(1)}, bf16[256,256]{1,0:T(8,128)(2,1)S(1)}, u32[]{:S(2)}, u32[]{:S(2)}) collective-permute-start(bf16[256,256]{1,0:T(8,128)(2,1)S(1)} %sum.5.refs_1_), channel_id=1, source_target_pairs={{0,8},{8,0},{16,24},{24,16},{1,9},{9,1},{17,25},{25,17},{2,10},{10... | collective-permute-start | bytes 393224 | tf_op jit(solution)/shard_map/ppermute | solution.py:268
  125.5 5.0 %collective-permute-start.30 = (bf16[256,256]{1,0:T(8,128)(2,1)S(1)}, bf16[256,256]{1,0:T(8,128)(2,1)S(1)}, u32[]{:S(2)}, u32[]{:S(2)}) collective-permute-start(bf16[256,256]{1,0:T(8,128)(2,1)S(1)} %sum.5.refs_1_), channel_id=1, source_target_pairs={{0,16},{8,24},{16,0},{24,8},{1,17},{9,25},{17,1},{25,9},{2,18},{10... | collective-permute-start | bytes 393224 | tf_op jit(solution)/shard_map/ppermute | solution.py:268
  126.5 5.9 %collective-permute-start.31 = (bf16[256,256]{1,0:T(8,128)(2,1)S(1)}, bf16[256,256]{1,0:T(8,128)(2,1)S(1)}, u32[]{:S(2)}, u32[]{:S(2)}) collective-permute-start(bf16[256,256]{1,0:T(8,128)(2,1)S(1)} %sum.5.refs_1_), channel_id=1, source_target_pairs={{0,24},{8,16},{16,8},{24,0},{1,25},{9,17},{17,9},{25,1},{2,26},{10... | collective-permute-start | bytes 393224 | tf_op jit(solution)/shard_map/ppermute | solution.py:268
  127.9 5.3 %collective-permute-start.32 = (bf16[256,256]{1,0:T(8,128)(2,1)S(1)}, bf16[256,256]{1,0:T(8,128)(2,1)S(1)}, u32[]{:S(2)}, u32[]{:S(2)}) collective-permute-start(bf16[256,256]{1,0:T(8,128)(2,1)S(1)} %sum.5.refs_1_), channel_id=1, source_target_pairs={{0,1},{1,0},{2,3},{3,2},{4,5},{5,4},{6,7},{7,6},{8,9},{9,8},{10,11... | collective-permute-start | bytes 393224 | tf_op jit(solution)/shard_map/ppermute | solution.py:265
  129.4 3.9 %collective-permute-start.33 = (bf16[256,256]{1,0:T(8,128)(2,1)S(1)}, bf16[256,256]{1,0:T(8,128)(2,1)S(1)}, u32[]{:S(2)}, u32[]{:S(2)}) collective-permute-start(bf16[256,256]{1,0:T(8,128)(2,1)S(1)} %collective-permute-done.29.refs_2_), channel_id=1, source_target_pairs={{0,1},{1,0},{2,3},{3,2},{4,5},{5,4},{6,7},{7,6},{8,9},{9,8},{10,11... | collective-permute-start | bytes 393224 | tf_op jit(solution)/shard_map/ppermute | solution.py:265
  130.5 2.8 %collective-permute-start.34 = (bf16[256,256]{1,0:T(8,128)(2,1)S(1)}, bf16[256,256]{1,0:T(8,128)(2,1)S(1)}, u32[]{:S(2)}, u32[]{:S(2)}) collective-permute-start(bf16[256,256]{1,0:T(8,128)(2,1)S(1)} %collective-permute-done.30.refs_3_), channel_id=1, source_target_pairs={{0,1},{1,0},{2,3},{3,2},{4,5},{5,4},{6,7},{7,6},{8,9},{9,8},{10,11... | collective-permute-start | bytes 393224 | tf_op jit(solution)/shard_map/ppermute | solution.py:265
  132.4 1.3 collective-permute-start.35
